TPU v7x, 32 devices: a whole 2x2x4 slice. The times are simulated.
32 devices in a mesh: parts: 2 (over y), blk: 4 (over z), reader: 4 (over x, core), sub: 1.
Axes of the slice: x: 2, y: 2, z: 4, core: 2. Of those that a mesh axis runs over, the one named last changes fastest.
Arguments:
- images: bfloat16 [3072, 8192], P(('parts', 'blk', 'reader'), 'sub'), parts along dimension 0, may hold values from -40 to 40
- routes: int32 [3072, 2], P(('parts', 'blk', 'reader')), parts along dimension 0, may hold values from 0 to 3, all different within a row; in each aligned block of 96 rows (0 to 95, 96 to 191, ...) at most 96 rows name the same one
- projections: bfloat16 [8, 128, 8192], P(('parts', 'reader'), 'blk', 'sub'), parts along dimension 0, may hold values from -8 to 8
- noise_weights: float32 [16384], P(('parts', 'sub')), parts along dimension 0, may hold values from 0.3 to 3
Outputs:
- weighted_sums: float32 [8, 128, 8192], P(('parts', 'reader'), 'blk', 'sub'), parts along dimension 0
- normalizer: float32 [3072], P(('parts', 'blk', 'reader')), parts along dimension 0
There are 2 independent parts, one for each index of `parts`. A program takes and returns all parts, laid end to end along the dimension named above; each array names one. Nothing has to cross between parts.
Inputs may be any that keep to these rules, and one draw needn't show every extreme that they name: `routes`: each row names 2 different class groups. In the rows of one device (aligned blocks of 96 rows) no group is named by more than 96 rows, a bound that some block reaches.
All inputs are finite; a program needn't handle non-finite values.
Results may differ from a plain program's by a relative error of at most 0.019.
Values may be sent and summed in bfloat16 or wider, within the bound.
No kernel may reach another device: no remote copies, remote signals or barrier semaphores. Data moves between devices by JAX's collectives and lax.ppermute only.
A program may use at most 64 MiB of HBM per device.

v0:
```python
from functools import partial

import jax
import jax.numpy as jnp
from jax import lax
from jax.sharding import PartitionSpec as P


def from_behind(block, axis, distance):
    devices = range(lax.axis_size(axis))
    route = [((i - distance) % len(devices), i) for i in devices]
    return lax.ppermute(block, axis, route)


def slot_positions(route_block, groups):
    flat_routes = route_block.reshape(-1)
    onehot = (flat_routes[:, None] == jnp.arange(groups, dtype=jnp.int32)[None, :]).astype(
        jnp.int32
    )
    before = jnp.cumsum(onehot, axis=0) - onehot
    return jnp.sum(before * onehot, axis=1).reshape(route_block.shape)


def combine_stats(row_peaks, row_totals):
    highest = jnp.max(row_peaks, axis=-1)
    spread = row_totals * jnp.exp(row_peaks - highest[..., None])
    return highest + jnp.log(jnp.sum(spread, axis=-1))


def on_device(images, routes, projections, noise_weights):
    groups = lax.axis_size("reader")
    cycle_size = lax.axis_size("blk")
    my_group = lax.axis_index("reader")
    my_member = lax.axis_index("blk")
    per_device, top_count = routes.shape
    half_width = images.shape[1]
    capacity = min(per_device, 2 * per_device * top_count // groups)
    slot_count = groups * capacity
    ref_count = projections.shape[1]
    all_refs = ref_count * cycle_size
    anchor = jnp.zeros((), jnp.int32)
    own_index = slot_positions(routes, groups)
    own_target = routes * capacity + own_index
    sources = jnp.broadcast_to(jnp.arange(per_device, dtype=jnp.int32)[:, None], routes.shape)
    picker = (
        jnp.full((slot_count,), per_device, jnp.int32)
        .at[own_target.reshape(-1)]
        .set(sources.reshape(-1))
    )
    padded = jnp.concatenate([images, jnp.zeros((1, half_width), images.dtype)], axis=0)
    outgoing = padded[picker].reshape(groups, capacity, half_width)
    received = lax.all_to_all(outgoing, "reader", split_axis=0, concat_axis=0, tiled=True).reshape(
        slot_count, half_width
    )
    every_route = lax.all_gather(routes, "reader", axis=0, tiled=True).reshape(
        groups, per_device, top_count
    )
    every_index = jax.vmap(partial(slot_positions, groups=groups))(every_route)
    senders = jnp.arange(groups, dtype=jnp.int32)[:, None, None]
    landing = jnp.where(every_route == my_group, senders * capacity + every_index, slot_count)
    live_slot = jnp.zeros((slot_count,), jnp.int32).at[landing.reshape(-1)].set(1, mode="drop") > 0

    def score_block(ref_block):
        scaled = ref_block.astype(jnp.float32) * noise_weights[None, :]
        weighted = scaled.astype(jnp.bfloat16)
        penalty = 0.5 * jnp.sum(scaled * ref_block.astype(jnp.float32), axis=1)
        partial_scores = lax.dot_general(
            weighted, received, (((1,), (1,)), ((), ())), preferred_element_type=jnp.float32
        )
        partial_scores = partial_scores - penalty[:, None]
        return partial_scores

    def cycle_turn(rotation, carry):
        ref_block, score_table = carry
        position = (my_member - rotation) % cycle_size
        score_table = lax.dynamic_update_slice(
            score_table, score_block(ref_block)[None], (position, anchor, anchor)
        )
        ref_block = from_behind(ref_block, "blk", 1)
        return (ref_block, score_table)

    empty_table = jnp.zeros((cycle_size, ref_count, slot_count), jnp.float32)
    ref_block, score_table = lax.fori_loop(
        0, cycle_size - 1, cycle_turn, (projections[0], empty_table)
    )
    position = (my_member + 1) % cycle_size
    score_table = lax.dynamic_update_slice(
        score_table, score_block(ref_block)[None], (position, anchor, anchor)
    )
    score_table = lax.psum(score_table, "sub")
    scores = score_table.reshape(all_refs, slot_count)
    row_peak = jnp.max(scores, axis=0)
    row_total = jnp.sum(jnp.exp(scores - row_peak[None, :]), axis=0)
    back_peak, back_total = (
        lax.all_to_all(
            row_peak.reshape(groups, capacity), "reader", split_axis=0, concat_axis=0, tiled=True
        ),
        lax.all_to_all(
            row_total.reshape(groups, capacity), "reader", split_axis=0, concat_axis=0, tiled=True
        ),
    )
    normalizer = combine_stats(
        back_peak.reshape(-1)[own_target], back_total.reshape(-1)[own_target]
    )
    outgoing_norm = (
        jnp.zeros((slot_count,), jnp.float32)
        .at[own_target.reshape(-1)]
        .set(jnp.repeat(normalizer, top_count))
    )
    slot_norm = lax.all_to_all(
        outgoing_norm.reshape(groups, capacity), "reader", split_axis=0, concat_axis=0, tiled=True
    ).reshape(slot_count)
    exponent = jnp.where(live_slot[None, :], scores - slot_norm[None, :], -jnp.inf)
    posterior = jnp.exp(exponent).astype(jnp.bfloat16)
    summed = lax.psum_scatter(
        jnp.dot(posterior, received, preferred_element_type=jnp.float32).astype(jnp.bfloat16),
        "blk",
        scatter_dimension=0,
        tiled=True,
    ).astype(jnp.float32)
    return (summed[None], normalizer)


def solution(mesh):
    return jax.shard_map(
        on_device,
        mesh=mesh,
        in_specs=(
            P(("parts", "blk", "reader"), "sub"),
            P(("parts", "blk", "reader"), None),
            P(("parts", "reader"), "blk", "sub"),
            P(("parts", "sub")),
        ),
        out_specs=(P(("parts", "reader"), "blk", "sub"), P(("parts", "blk", "reader"))),
        check_vma=False,
    )
```

profile of v0, /device:TPU:0, one launch (start us, length us, event | category | flops | bytes accessed | tf_op | source)
XLA Modules:
  0.0 242.1 jit_solution(12317410076920263179)
XLA Ops:
  13.9 7.2 %gather_fusion = bf16[384,8192]{1,0:T(8,128)(2,1)} fusion(bf16[97,8192]{1,0:T(8,128)(2,1)S(1)} %concatenate.3, s32[1024]{0:T(1024)S(1)} %pad_clamp_fusion.1), kind=kCustom, calls=%fused_computation | custom fusion | bytes 12584448 | tf_op jit(solution)/shard_map/gather | solution.py:51
  21.1 5.4 %all-to-all-start = ((bf16[4,96,8192]{2,1,0:T(8,128)(2,1)}), bf16[4,96,8192]{2,1,0:T(8,128)(2,1)}, u32[]{:S(2)}, u32[]{:S(2)}) async-start(bf16[4,96,8192]{2,1,0:T(8,128)(2,1)} %bitcast.40), calls=%async_computation | async-start | bytes 12582912 | tf_op jit(solution)/shard_map/all_to_all | solution.py:52
  26.5 72.1 %all-gather = s32[4,96,2]{1,2,0:T(2,128)S(1)} all-gather(s32[1,96,2]{1,2,0:T(2,128)S(1)} %bitcast.45), channel_id=1, replica_groups=mesh['parts'=2,'blk'=4,'reader'=4,'sub'=1] {'reader'}, dimensions={0}, use_global_device_ids=true | all-gather | bytes 3840 | tf_op jit(solution)/shard_map/all_gather | solution.py:55
  98.9 4.8 %reduce-window.14 = s32[4,4,2,128]{3,2,1,0:T(2,128)S(1)} reduce-window(s32[4,4,2,128]{3,2,1,0:T(2,128)S(1)} %reshape.195, s32[]{:T(128)} %constant.106.clone.1), window={size=1x1x1x128 pad=0_0x0_0x0_0x127_0}, to_apply=%region_0.0 | reduce-window | flops 520192 | bytes 32772 | tf_op jit(solution)/shard_map/reduce-window
  105.0 47.2 %while.17 = (s32[]{:T(128)}, bf16[32,8192]{1,0:T(8,128)(2,1)S(1)}, f32[4,32,384]{2,1,0:T(8,128)S(1)}, f32[8192]{0:T(1024)S(1)}, bf16[384,8192]{1,0:T(8,128)(2,1)...) while((s32[]{:T(128)}, bf16[32,8192]{1,0:T(8,128)(2,1)S(1)}, ...), condition=%wide.region_10.11_spmd, body=%wide.region_8.10_spmd.sunk | while | flops 203173904 | bytes 10601644 | solution.py:83
  105.0 2.5 %collective-permute-start = (bf16[32,8192]{1,0:T(8,128)(2,1)S(1)}, bf16[32,8192]{1,0:T(8,128)(2,1)S(1)}, u32[]{:S(2)}, u32[]{:S(2)}) collective-permute-start(bf16[32,8192]{1,0:T(8,128)(2,1)S(1)} %copy.54), channel_id=1, source_target_pairs={{12,0},{0,4},{4,8},{8,12},{13,1},{1,5},{5,9},{9,13},{14,2},{2,6},{... | collective-permute-start | bytes 1572872 | tf_op jit(solution)/shard_map/while/body/eval_jaxpr/ppermute | solution.py:12
  107.8 4.8 %fusion.30 = f32[4,32,384]{2,1,0:T(8,128)S(1)} fusion(f32[4,32,384]{2,1,0:T(8,128)S(1)} %get-tuple-element.223, s32[]{:T(128)S(6)} %select_n.101, bf16[384,8192]{1,0:T(8,128)(2,1)} %get-tuple-element.235, bf16[32,8192]{1,0:T(8,128)(2,1)S(1)} %copy.54, f32[8192]{0:T(1024)S(1)} %get-tuple-element.234, f32[32]{0:T(128)S(1)} %broadcast_multiply_fusion.3), kind=kOutput, calls=%fused_computation.10.clone.1 | convolution fusion | flops 202125312 | bytes 6898180 | tf_op jit(solution)/shard_map/while/body/eval_jaxpr/dot_general | solution.py:67
  112.5 9.4 %collective-permute-done = bf16[32,8192]{1,0:T(8,128)(2,1)S(1)} collective-permute-done((bf16[32,8192]{1,0:T(8,128)(2,1)S(1)}, bf16[32,8192]{1,0:T(8,128)(2,1)S(1)}, u32[]{:S(2)}, u32[]{:S(2)}) %collective-permute-start) | collective-permute-done | bytes 524320 | tf_op jit(solution)/shard_map/while/body/eval_jaxpr/ppermute | solution.py:12
  122.3 4.8 %fusion.30 = f32[4,32,384]{2,1,0:T(8,128)S(1)} fusion(f32[4,32,384]{2,1,0:T(8,128)S(1)} %get-tuple-element.223, s32[]{:T(128)S(6)} %select_n.101, bf16[384,8192]{1,0:T(8,128)(2,1)} %get-tuple-element.235, bf16[32,8192]{1,0:T(8,128)(2,1)S(1)} %copy.54, f32[8192]{0:T(1024)S(1)} %get-tuple-element.234, f32[32]{0:T(128)S(1)} %broadcast_multiply_fusion.3), kind=kOutput, calls=%fused_computation.10.clone.1 | convolution fusion | flops 202125312 | bytes 6898180 | tf_op jit(solution)/shard_map/while/body/eval_jaxpr/dot_general | solution.py:67
  127.1 10.4 %collective-permute-done = bf16[32,8192]{1,0:T(8,128)(2,1)S(1)} collective-permute-done((bf16[32,8192]{1,0:T(8,128)(2,1)S(1)}, bf16[32,8192]{1,0:T(8,128)(2,1)S(1)}, u32[]{:S(2)}, u32[]{:S(2)}) %collective-permute-start) | collective-permute-done | bytes 524320 | tf_op jit(solution)/shard_map/while/body/eval_jaxpr/ppermute | solution.py:12
  137.8 4.8 %fusion.30 = f32[4,32,384]{2,1,0:T(8,128)S(1)} fusion(f32[4,32,384]{2,1,0:T(8,128)S(1)} %get-tuple-element.223, s32[]{:T(128)S(6)} %select_n.101, bf16[384,8192]{1,0:T(8,128)(2,1)} %get-tuple-element.235, bf16[32,8192]{1,0:T(8,128)(2,1)S(1)} %copy.54, f32[8192]{0:T(1024)S(1)} %get-tuple-element.234, f32[32]{0:T(128)S(1)} %broadcast_multiply_fusion.3), kind=kOutput, calls=%fused_computation.10.clone.1 | convolution fusion | flops 202125312 | bytes 6898180 | tf_op jit(solution)/shard_map/while/body/eval_jaxpr/dot_general | solution.py:67
  142.6 9.5 %collective-permute-done = bf16[32,8192]{1,0:T(8,128)(2,1)S(1)} collective-permute-done((bf16[32,8192]{1,0:T(8,128)(2,1)S(1)}, bf16[32,8192]{1,0:T(8,128)(2,1)S(1)}, u32[]{:S(2)}, u32[]{:S(2)}) %collective-permute-start) | collective-permute-done | bytes 524320 | tf_op jit(solution)/shard_map/while/body/eval_jaxpr/ppermute | solution.py:12
  152.4 4.8 %fusion.5 = f32[4,32,384]{2,1,0:T(8,128)S(1)} fusion(f32[4,32,384]{2,1,0:T(8,128)S(1)} %get-tuple-element.158, s32[]{:T(128)S(6)} %select_n.87, bf16[384,8192]{1,0:T(8,128)(2,1)} %bitcast.10, bf16[32,8192]{1,0:T(8,128)(2,1)S(1)} %get-tuple-element.159, f32[8192]{0:T(1024)S(1)} %get-tuple-element.248, f32[32]{0:T(128)S(1)} %broadcast_multiply_fusion.1), kind=kOutput, calls=%fused_computation.19 | convolution fusion | flops 202125312 | bytes 6898180 | tf_op jit(solution)/shard_map/dot_general | solution.py:67
  157.9 3.2 %all-to-all-start.2 = ((f32[4,1,96]{2,1,0:T(1,128)}), f32[4,1,96]{2,1,0:T(1,128)S(1)}, u32[]{:S(2)}, u32[]{:S(2)}) async-start(f32[4,1,96]{2,1,0:T(1,128)} %all_to_all.24), calls=%async_computation.2 | async-start | bytes 4096 | tf_op jit(solution)/shard_map/all_to_all | solution.py:98
  162.0 2.8 %all-to-all-done.2 = f32[4,1,96]{2,1,0:T(1,128)S(1)} async-done(((f32[4,1,96]{2,1,0:T(1,128)}), f32[4,1,96]{2,1,0:T(1,128)S(1)}, u32[]{:S(2)}, u32[]{:S(2)}) %all-to-all-start.2) | async-done | bytes 1568 | tf_op jit(solution)/shard_map/all_to_all | solution.py:98
  164.8 3.2 %all-to-all-start.1 = ((f32[4,1,96]{2,1,0:T(1,128)}), f32[4,1,96]{2,1,0:T(1,128)S(1)}, u32[]{:S(2)}, u32[]{:S(2)}) async-start(f32[4,1,96]{2,1,0:T(1,128)} %all_to_all.22), calls=%async_computation.1 | async-start | bytes 4096 | tf_op jit(solution)/shard_map/all_to_all | solution.py:95
  168.1 3.4 %scatter_custom_fusion = s32[384]{0:T(512)S(1)} fusion(s32[768]{0:T(1024)S(1)} %fusion.14, s32[768]{0:T(1024)S(1)} %broadcast.146, s32[]{:T(128)} %constant.106.clone.1), kind=kCustom, calls=%fused_computation.57 | custom fusion | bytes 1540 | tf_op jit(solution)/shard_map/scatter | solution.py:61
  172.7 1.6 gather_fusion.2
  175.1 1.6 gather_fusion.1
  179.3 3.2 %all-to-all-start.3 = ((f32[4,1,96]{2,1,0:T(1,128)}), f32[4,1,96]{2,1,0:T(1,128)S(1)}, u32[]{:S(2)}, u32[]{:S(2)}) async-start(f32[4,1,96]{2,1,0:T(1,128)} %all_to_all.26), calls=%async_computation.3 | async-start | bytes 4096 | tf_op jit(solution)/shard_map/all_to_all | solution.py:110
  182.6 3.6 %all-to-all-done.3 = f32[4,1,96]{2,1,0:T(1,128)S(1)} async-done(((f32[4,1,96]{2,1,0:T(1,128)}), f32[4,1,96]{2,1,0:T(1,128)S(1)}, u32[]{:S(2)}, u32[]{:S(2)}) %all-to-all-start.3) | async-done | bytes 1568 | tf_op jit(solution)/shard_map/all_to_all | solution.py:110
  186.9 5.4 %convolution_convert_fusion = bf16[128,8192]{1,0:T(8,128)(2,1)} fusion(bf16[128,384]{1,0:T(8,128)(2,1)S(1)} %bitcast.41, bf16[384,8192]{1,0:T(8,128)(2,1)} %bitcast.10), kind=kOutput, calls=%fused_computation.14 | convolution fusion | flops 806354944 | bytes 8486912 | tf_op jit(solution)/shard_map/dot_general | solution.py:116
  192.4 40.8 %reduce-scatter.2.cloned.1.call-done = bf16[32,8192]{1,0:T(8,128)(2,1)} async-done(((bf16[128,8192]{1,0:T(8,128)(2,1)}), bf16[32,8192]{1,0:T(8,128)(2,1)}) %reduce-scatter.2.cloned.1.call-update) | async-done | bytes 524304 | tf_op jit(solution)/shard_map/reduce_scatter | solution.py:115
  233.2 2.1 bitcast_convert_fusion
  (99 shorter events, 16.3 us)
Async XLA Ops:
  21.1 5.4 %copy-start.2 = (s32[96,2]{0,1:T(2,128)S(1)}, s32[96,2]{0,1:T(2,128)}, u32[]{:S(2)}) copy-start(s32[96,2]{0,1:T(2,128)} %param.7) | copy-start | bytes 2308
  21.1 83.9 %copy-start = (bf16[1,32,8192]{2,1,0:T(8,128)(2,1)S(1)}, bf16[1,32,8192]{2,1,0:T(8,128)(2,1)}, u32[]{:S(2)}) copy-start(bf16[1,32,8192]{2,1,0:T(8,128)(2,1)} %param.8) | copy-start | bytes 1572868
  21.1 83.9 %copy-start.1 = (f32[8192]{0:T(1024)S(1)}, f32[8192]{0:T(1024)}, u32[]{:S(2)}) copy-start(f32[8192]{0:T(1024)} %param.9) | copy-start | bytes 98308
  21.1 83.9 %all-to-all-start = ((bf16[4,96,8192]{2,1,0:T(8,128)(2,1)}), bf16[4,96,8192]{2,1,0:T(8,128)(2,1)}, u32[]{:S(2)}, u32[]{:S(2)}) async-start(bf16[4,96,8192]{2,1,0:T(8,128)(2,1)} %bitcast.40), calls=%async_computation | async-start | bytes 12582912 | tf_op jit(solution)/shard_map/all_to_all | solution.py:52
  105.0 16.9 %collective-permute-start = (bf16[32,8192]{1,0:T(8,128)(2,1)S(1)}, bf16[32,8192]{1,0:T(8,128)(2,1)S(1)}, u32[]{:S(2)}, u32[]{:S(2)}) collective-permute-start(bf16[32,8192]{1,0:T(8,128)(2,1)S(1)} %copy.54), channel_id=1, source_target_pairs={{12,0},{0,4},{4,8},{8,12},{13,1},{1,5},{5,9},{9,13},{14,2},{2,6},{... | collective-permute-start | bytes 1572872 | tf_op jit(solution)/shard_map/while/body/eval_jaxpr/ppermute | solution.py:12
  122.0 15.5 %collective-permute-start = (bf16[32,8192]{1,0:T(8,128)(2,1)S(1)}, bf16[32,8192]{1,0:T(8,128)(2,1)S(1)}, u32[]{:S(2)}, u32[]{:S(2)}) collective-permute-start(bf16[32,8192]{1,0:T(8,128)(2,1)S(1)} %copy.54), channel_id=1, source_target_pairs={{12,0},{0,4},{4,8},{8,12},{13,1},{1,5},{5,9},{9,13},{14,2},{2,6},{... | collective-permute-start | bytes 1572872 | tf_op jit(solution)/shard_map/while/body/eval_jaxpr/ppermute | solution.py:12
  137.5 14.6 %collective-permute-start = (bf16[32,8192]{1,0:T(8,128)(2,1)S(1)}, bf16[32,8192]{1,0:T(8,128)(2,1)S(1)}, u32[]{:S(2)}, u32[]{:S(2)}) collective-permute-start(bf16[32,8192]{1,0:T(8,128)(2,1)S(1)} %copy.54), channel_id=1, source_target_pairs={{12,0},{0,4},{4,8},{8,12},{13,1},{1,5},{5,9},{9,13},{14,2},{2,6},{... | collective-permute-start | bytes 1572872 | tf_op jit(solution)/shard_map/while/body/eval_jaxpr/ppermute | solution.py:12
  157.9 6.9 %all-to-all-start.2 = ((f32[4,1,96]{2,1,0:T(1,128)}), f32[4,1,96]{2,1,0:T(1,128)S(1)}, u32[]{:S(2)}, u32[]{:S(2)}) async-start(f32[4,1,96]{2,1,0:T(1,128)} %all_to_all.24), calls=%async_computation.2 | async-start | bytes 4096 | tf_op jit(solution)/shard_map/all_to_all | solution.py:98
  164.8 9.6 %all-to-all-start.1 = ((f32[4,1,96]{2,1,0:T(1,128)}), f32[4,1,96]{2,1,0:T(1,128)S(1)}, u32[]{:S(2)}, u32[]{:S(2)}) async-start(f32[4,1,96]{2,1,0:T(1,128)} %all_to_all.22), calls=%async_computation.1 | async-start | bytes 4096 | tf_op jit(solution)/shard_map/all_to_all | solution.py:95
  177.2 15.2 %copy-start.3 = (f32[96]{0:T(128)}, f32[96]{0:T(128)S(1)}, u32[]{:S(2)}) copy-start(f32[96]{0:T(128)S(1)} %log_add_fusion) | copy-start | bytes 1156
  179.3 6.9 %all-to-all-start.3 = ((f32[4,1,96]{2,1,0:T(1,128)}), f32[4,1,96]{2,1,0:T(1,128)S(1)}, u32[]{:S(2)}, u32[]{:S(2)}) async-start(f32[4,1,96]{2,1,0:T(1,128)} %all_to_all.26), calls=%async_computation.3 | async-start | bytes 4096 | tf_op jit(solution)/shard_map/all_to_all | solution.py:110
  182.5 50.7 %reduce-scatter.2.cloned.1.call-start = ((), (), s32[]{:S(2)}) async-start(), calls=%async_computation.5 | async-start | bytes 2621440 | tf_op jit(solution)/shard_map/reduce_scatter | solution.py:115
Sparse Core Ops, SparseCore 0:
  192.5 40.6 reduce-scatter.1
where the time goes:
time: 243 us; the launch traced here: 242 us
  waiting for transfers between devices  76.6 us (32%)
  blocking collectives  72.1 us (30%)
  local copies, waits for them, and re-layouts  24.4 us (10%)
  matrix products  24.4 us (10%)
  starting transfers between devices  17.6 us (7%)
  between operations  14.4 us (6%)
  other arithmetic  12.4 us (5%)
    all_gather x1, blocking collectives, on_device(): lax.all_gather(routes, 'reader', axis=0, tiled=True)  72.1 us
    reduce_scatter x1, waiting for transfers between devices, on_device(): lax.psum_scatter(jnp.dot(posterior, received, preferred_element_type=jnp....  40.8 us
    ppermute x3, waiting for transfers between devices, from_behind(): return lax.ppermute(block, axis, route)  29.3 us
    dot_general x4, matrix products, score_block(): lax.dot_general(weighted, received, (((1,), (1,)), ((), ())), preferred_e...  19 us
    gather x1, local copies, waits for them, and re-layouts, on_device(): outgoing = padded[picker].reshape(groups, capacity, half_width)  7.16 us
    another operation x7, other arithmetic  6.21 us
    dot_general x1, matrix products, on_device(): jnp.dot(posterior, received, preferred_element_type=jnp.float32)  5.44 us
    all_to_all x1, starting transfers between devices, on_device(): lax.all_to_all(outgoing, 'reader', split_axis=0, concat_axis=0, tiled=True)  5.38 us
  transfers between devices with their start and end apart: 8, of which 6 were waited for; matrix products, arithmetic and copies ran while one was open for 11% of the time, Pallas kernels for 0%

commit v1 on v0

v1 whole, which is shorter than its diff:
```python
from functools import partial

import jax
import jax.numpy as jnp
from jax import lax
from jax.experimental import pallas as pl
from jax.experimental.pallas import tpu as pltpu
from jax.sharding import PartitionSpec as P

CHUNKS = 2
VMEM_BYTES = 48 * 1024 * 1024


def swap_bit(block, axis, bit):
    size = lax.axis_size(axis)
    return lax.ppermute(block, axis, [(i, i ^ bit) for i in range(size)])


def swap_gather(block, axis):
    size = lax.axis_size(axis)
    held = {0: block}
    bit = size // 2
    while bit:
        for k in list(held):
            held[k ^ bit] = swap_bit(held[k], axis, bit)
        bit //= 2
    return [held[k] for k in range(size)]


def line_gather(block, axis):
    size = lax.axis_size(axis)
    ahead, behind = [block], [block]
    for s in range(1, size):
        ahead.append(lax.ppermute(ahead[-1], axis, [(i, i + 1) for i in range(s - 1, size - 1)]))
        behind.append(lax.ppermute(behind[-1], axis, [(i, i - 1) for i in range(1, size - s + 1)]))
    return ahead, behind


def line_scatter(parts, axis):
    size = lax.axis_size(axis)
    up = down = None
    for s in range(1, size):
        send_up, send_down = parts[s], parts[size - s]
        if s > 1:
            send_up = add_rounded(send_up, up)
            send_down = add_rounded(send_down, down)
        up = lax.ppermute(send_up, axis, [(i, i + 1) for i in range(0, s) if i + 1 < size])
        down = lax.ppermute(send_down, axis, [(i, i - 1) for i in range(size - s, size) if i > 0])
    total = parts[0].astype(jnp.float32)
    if size > 1:
        total = total + up.astype(jnp.float32) + down.astype(jnp.float32)
    return total


def add_rounded(one, other):
    return (one.astype(jnp.float32) + other.astype(jnp.float32)).astype(jnp.bfloat16)


def score_kernel(readers, members, first, place_ref, *refs):
    refs = list(refs)
    image_refs = [refs.pop(0) for _ in range(readers)]
    ahead_refs = [refs.pop(0) for _ in range(members)]
    behind_refs = [None] + [refs.pop(0) for _ in range(members - 1)]
    noise_ref = refs.pop(0)
    earlier_ref = None if first else refs.pop(0)
    score_ref, all_ref, weighted_ref, penalty_ref = refs
    rows = image_refs[0].shape[0]
    count = ahead_refs[0].shape[0]
    reader, member = place_ref[0], place_ref[1]
    for k in range(readers):
        start = pl.multiple_of((reader ^ k) * rows, rows)
        all_ref[pl.ds(start, rows), :] = image_refs[k][...]
    noise = noise_ref[...]

    def weigh(s, ref):
        block = ref[...].astype(jnp.float32)
        scaled = block * noise
        weighted_ref[pl.ds(s * count, count), :] = scaled.astype(jnp.bfloat16)
        penalty_ref[pl.ds(s * count, count), :] = 0.5 * jnp.sum(
            scaled * block, axis=1, keepdims=True
        )

    weigh(0, ahead_refs[0])
    for s in range(1, members):

        @pl.when(member >= s)
        def _(s=s):
            weigh(s, ahead_refs[s])

        @pl.when(member < s)
        def _(s=s):
            weigh(s, behind_refs[members - s])

    scores = lax.dot_general(
        weighted_ref[...],
        all_ref[...],
        (((1,), (1,)), ((), ())),
        preferred_element_type=jnp.float32,
    )
    scores = scores - penalty_ref[...]
    if not first:
        scores = scores + earlier_ref[...]
    score_ref[...] = scores


def score_chunk(place, image_blocks, ahead, behind, noise, earlier):
    readers, members = len(image_blocks), len(ahead)
    rows, width = image_blocks[0].shape
    refs = ahead[0].shape[0] * members
    operands = [*image_blocks, *ahead, *behind[1:], noise]
    if earlier is not None:
        operands.append(earlier)
    vmem = pl.BlockSpec(memory_space=pltpu.VMEM)
    return pl.pallas_call(
        partial(score_kernel, readers, members, earlier is None),
        out_shape=(
            jax.ShapeDtypeStruct((refs, readers * rows), jnp.float32),
            jax.ShapeDtypeStruct((readers * rows, width), jnp.bfloat16),
        ),
        in_specs=[pl.BlockSpec(memory_space=pltpu.SMEM)] + [vmem] * len(operands),
        out_specs=(vmem, vmem),
        scratch_shapes=[
            pltpu.VMEM((refs, width), jnp.bfloat16),
            pltpu.VMEM((refs, 1), jnp.float32),
        ],
        compiler_params=pltpu.CompilerParams(vmem_limit_bytes=VMEM_BYTES),
        cost_estimate=pl.CostEstimate(
            flops=2 * refs * readers * rows * width,
            bytes_accessed=4 * readers * rows * width,
            transcendentals=0,
        ),
        name="scores",
    )(place, *operands)


def lse_kernel(score_ref, lse_ref):
    scores = score_ref[...]
    peak = jnp.max(scores, axis=0, keepdims=True)
    total = jnp.sum(jnp.exp(scores - peak), axis=0, keepdims=True)
    lse_ref[...] = peak + jnp.log(total)


def group_lse(scores):
    return pl.pallas_call(
        lse_kernel,
        out_shape=jax.ShapeDtypeStruct((1, scores.shape[1]), jnp.float32),
        name="group_lse",
    )(scores)


def posterior_kernel(readers, place_ref, score_ref, route_ref, *refs):
    lse_refs = refs[:readers]
    norm_ref, post_ref = refs[readers:]
    reader = place_ref[0]
    routes = route_ref[...]
    kept = []
    for k in range(readers):
        named = jnp.max(jnp.where(routes == (reader ^ k), 1.0, 0.0), axis=0, keepdims=True) > 0.0
        kept.append(jnp.where(named, lse_refs[k][...], -jnp.inf))
        if k == 0:
            mine = named
    highest = kept[0]
    for value in kept[1:]:
        highest = jnp.maximum(highest, value)
    spread = jnp.exp(kept[0] - highest)
    for value in kept[1:]:
        spread = spread + jnp.exp(value - highest)
    norm = highest + jnp.log(spread)
    norm_ref[...] = norm
    exponent = jnp.where(mine, score_ref[...] - norm, -jnp.inf)
    post_ref[...] = jnp.exp(exponent).astype(jnp.bfloat16)


def posteriors(place, scores, routes, lses):
    vmem = pl.BlockSpec(memory_space=pltpu.VMEM)
    return pl.pallas_call(
        partial(posterior_kernel, len(lses)),
        out_shape=(
            jax.ShapeDtypeStruct((1, scores.shape[1]), jnp.float32),
            jax.ShapeDtypeStruct(scores.shape, jnp.bfloat16),
        ),
        in_specs=[pl.BlockSpec(memory_space=pltpu.SMEM)] + [vmem] * (2 + len(lses)),
        out_specs=(vmem, vmem),
        name="posteriors",
    )(place, scores, routes, *lses)


def sums_kernel(members, post_ref, all_ref, *out_refs):
    sums = jnp.dot(post_ref[...], all_ref[...], preferred_element_type=jnp.float32)
    count = sums.shape[0] // members
    for s in range(members):
        out_refs[s][...] = sums[s * count : (s + 1) * count].astype(out_refs[s].dtype)


def sums_chunk(members, posterior, all_images):
    refs = posterior.shape[0]
    slots, width = all_images.shape
    tile = min(width, 1024)
    block = jax.ShapeDtypeStruct((refs // members, width), jnp.bfloat16)
    return pl.pallas_call(
        partial(sums_kernel, members),
        grid=(width // tile,),
        out_shape=(block,) * members,
        in_specs=[
            pl.BlockSpec((refs, slots), lambda i: (0, 0)),
            pl.BlockSpec((slots, tile), lambda i: (0, i)),
        ],
        out_specs=(pl.BlockSpec((refs // members, tile), lambda i: (0, i)),) * members,
        compiler_params=pltpu.CompilerParams(vmem_limit_bytes=VMEM_BYTES),
        cost_estimate=pl.CostEstimate(
            flops=2 * refs * slots * width,
            bytes_accessed=2 * slots * width,
            transcendentals=0,
        ),
        name="sums",
    )(posterior, all_images)


def on_device(images, routes, projections, noise_weights):
    readers = lax.axis_size("reader")
    members = lax.axis_size("blk")
    reader = lax.axis_index("reader")
    member = lax.axis_index("blk")
    place = jnp.stack([reader, member]).astype(jnp.int32)
    rows, half_width = images.shape
    width = half_width // CHUNKS
    projections = projections[0]
    noise = noise_weights.reshape(1, half_width)

    route_blocks = jnp.stack(swap_gather(routes.T, "reader"))
    order = jnp.arange(readers, dtype=jnp.int32) ^ reader
    all_routes = route_blocks[order].transpose(1, 0, 2).reshape(routes.shape[1], readers * rows)

    pieces = [slice(q * width, (q + 1) * width) for q in range(CHUNKS)]
    lines = [line_gather(projections[:, piece], "blk") for piece in pieces]
    gathered = [swap_gather(images[:, piece], "reader") for piece in pieces]
    scores = None
    all_images = []
    for piece, (ahead, behind), blocks in zip(pieces, lines, gathered):
        scores, every = score_chunk(place, blocks, ahead, behind, noise[:, piece], scores)
        all_images.append(every)
    if lax.axis_size("sub") > 1:
        scores = lax.psum(scores, "sub")
    mine = group_lse(scores)
    lses = [mine] + [swap_bit(mine, "reader", k) for k in range(1, readers)]
    norms, posterior = posteriors(place, scores, all_routes, lses)
    normalizer = lax.dynamic_slice(norms.reshape(-1), (reader * rows,), (rows,))
    totals = [
        line_scatter(sums_chunk(members, posterior, every), "blk") for every in all_images
    ]
    return (jnp.concatenate(totals, axis=1)[None], normalizer)


def solution(mesh):
    return jax.shard_map(
        on_device,
        mesh=mesh,
        in_specs=(
            P(("parts", "blk", "reader"), "sub"),
            P(("parts", "blk", "reader"), None),
            P(("parts", "reader"), "blk", "sub"),
            P(("parts", "sub")),
        ),
        out_specs=(P(("parts", "reader"), "blk", "sub"), P(("parts", "blk", "reader"))),
        check_vma=False,
    )
```

time: 243 us -> 124 us (0.51)
  blocking collectives: 72.1 us -> 0 us
  waiting for transfers between devices: 76.6 us -> 33.9 us
  starting transfers between devices: 17.6 us -> 52.6 us
  matrix products: 24.4 us -> 0 us
  Pallas kernels: 0 us -> 15.4 us
  between operations: 14.4 us -> 1.06 us
  local copies, waits for them, and re-layouts: 24.4 us -> 15.6 us
  other arithmetic: 12.4 us -> 4.71 us
    all_gather x1 -> x0, blocking collectives: 72.1 us -> none  [on_device(): lax.all_gather(routes, 'reader', axis=0, tiled=True)]
    ppermute x3 -> x36, starting transfers between devices: 2.57 us -> 52.6 us  [the longest x6 19.6 us: line_scatter(): lax.ppermute(send_up, axis, [(i, i + 1) for i in range(0, s) if i + 1 < s...]
    reduce_scatter x1 -> x0, waiting for transfers between devices: 40.8 us -> none  [on_device(): lax.psum_scatter(jnp.dot(posterior, received, preferred_element_type=jnp....]
    dot_general x5 -> x0, matrix products: 24.4 us -> none  [the longest x4 19 us: score_block(): lax.dot_general(weighted, received, (((1,), (1,)), ((), ())), preferred_e...]
    pallas_call x0 -> x6, Pallas kernels: none -> 15.4 us  [the longest x2 8.15 us: score_chunk(): pl.pallas_call(partial(score_kernel, readers, members, earlier is None),...]
    all_to_all x4 -> x0, starting transfers between devices: 15 us -> none  [the longest x1 5.38 us: on_device(): lax.all_to_all(outgoing, 'reader', split_axis=0, concat_axis=0, tiled=True)]
    gather x5 -> x1, local copies, waits for them, and re-layouts: 10.6 us -> 0.57 us  [on_device(): route_blocks[order].transpose(1, 0, 2)]
    unnamed x10 -> x46, local copies, waits for them, and re-layouts: 0.8 us -> 9.58 us
  transfers between devices with their start and end apart: 8 -> 36, of which waited for: 6 -> 12; matrix products, arithmetic and copies ran while one was open for 11% -> 7% of each run, Pallas kernels for 0% -> 9%
where the time goes in v1:
time: 124 us; the launch traced here: 123 us
  starting transfers between devices  52.6 us (42%)
  waiting for transfers between devices  33.9 us (27%)
  local copies, waits for them, and re-layouts  15.6 us (13%)
  Pallas kernels  15.4 us (12%)
  other arithmetic  4.71 us (4%)
    ppermute x6, starting transfers between devices, line_scatter(): lax.ppermute(send_up, axis, [(i, i + 1) for i in range(0, s) if i + 1 < s...  19.6 us
    ppermute x6, waiting for transfers between devices, line_gather(): lax.ppermute(behind[-1], axis, [(i, i - 1) for i in range(1, size - s + 1)])  14.6 us
    ppermute x6, starting transfers between devices, line_gather(): lax.ppermute(ahead[-1], axis, [(i, i + 1) for i in range(s - 1, size - 1)])  12.9 us
    ppermute x12, waiting for transfers between devices, swap_bit(): return lax.ppermute(block, axis, [(i, i ^ bit) for i in range(size)])  10.7 us
    unnamed x46, local copies, waits for them, and re-layouts  9.58 us
    pallas_call x2, Pallas kernels, score_chunk(): pl.pallas_call(partial(score_kernel, readers, members, earlier is None),...  8.15 us
    ppermute x6, starting transfers between devices, line_gather(): lax.ppermute(behind[-1], axis, [(i, i - 1) for i in range(1, size - s + 1)])  7.72 us
    ppermute x12, starting transfers between devices, swap_bit(): return lax.ppermute(block, axis, [(i, i ^ bit) for i in range(size)])  6.47 us
  transfers between devices with their start and end apart: 36, of which 12 were waited for; matrix products, arithmetic and copies ran while one was open for 7% of the time, Pallas kernels for 9%

profile of v1, /device:TPU:0, one launch (start us, length us, event | category | flops | bytes accessed | tf_op | source)
XLA Modules:
  0.0 123.3 jit_solution(7829915353258064616)
XLA Ops:
  1.7 4.9 %collective-permute-start.12 = (bf16[32,4096]{1,0:T(8,128)(2,1)S(1)}, bf16[32,4096]{1,0:T(8,128)(2,1)S(1)}, u32[]{:S(2)}, u32[]{:S(2)}) collective-permute-start(bf16[32,4096]{1,0:T(8,128)(2,1)S(1)} %get-tuple-element.32.refs_4_), channel_id=1, source_target_pairs={{0,4},{4,8},{8,12},{1,5},{5,9},{9,13},{2,6},{6,10},{10,14},{3,7},{... | collective-permute-start | bytes 786440 | tf_op jit(solution)/shard_map/ppermute | solution.py:34
  8.0 4.6 %collective-permute-start.3 = (bf16[32,4096]{1,0:T(8,128)(2,1)S(1)}, bf16[32,4096]{1,0:T(8,128)(2,1)S(1)}, u32[]{:S(2)}, u32[]{:S(2)}) collective-permute-start(bf16[32,4096]{1,0:T(8,128)(2,1)S(1)} %get-tuple-element.33.refs_4_), channel_id=1, source_target_pairs={{0,4},{4,8},{8,12},{1,5},{5,9},{9,13},{2,6},{6,10},{10,14},{3,7},{... | collective-permute-start | bytes 786440 | tf_op jit(solution)/shard_map/ppermute | solution.py:34
  12.6 2.4 %fusion.5 = (bf16[96,4096]{1,0:T(8,128)(2,1)S(1)}, bf16[96,4096]{1,0:T(8,128)(2,1)}) fusion(bf16[96,8192]{1,0:T(8,128)(2,1)} %param.4), kind=kLoop, calls=%fused_computation.22 | loop fusion | bytes 3145728 | tf_op jit(solution)/shard_map/slice | solution.py:236
  14.9 1.5 %collective-permute-start.10 = (bf16[96,4096]{1,0:T(8,128)(2,1)S(1)}, bf16[96,4096]{1,0:T(8,128)(2,1)S(1)}, u32[]{:S(2)}, u32[]{:S(2)}) collective-permute-start(bf16[96,4096]{1,0:T(8,128)(2,1)S(1)} %get-tuple-element.30.refs_0_), channel_id=1, source_target_pairs={{0,2},{1,3},{2,0},{3,1},{4,6},{5,7},{6,4},{7,5},{8,10},{9,11},{10,... | collective-permute-start | bytes 2359304 | tf_op jit(solution)/shard_map/ppermute | solution.py:16
  20.3 5.6 %collective-permute-done.6.refs_8_ = bf16[32,4096]{1,0:T(8,128)(2,1)S(1)} collective-permute-done((bf16[32,4096]{1,0:T(8,128)(2,1)S(1)}, bf16[32,4096]{1,0:T(8,128)(2,1)S(1)}, u32[]{:S(2)}, u32[]{:S(2)}) %collective-permute-start.6) | collective-permute-done | bytes 262176 | tf_op jit(solution)/shard_map/ppermute | solution.py:35
  32.6 6.0 %collective-permute-done.7.refs_9_ = bf16[32,4096]{1,0:T(8,128)(2,1)S(1)} collective-permute-done((bf16[32,4096]{1,0:T(8,128)(2,1)S(1)}, bf16[32,4096]{1,0:T(8,128)(2,1)S(1)}, u32[]{:S(2)}, u32[]{:S(2)}) %collective-permute-start.7) | collective-permute-done | bytes 262176 | tf_op jit(solution)/shard_map/ppermute | solution.py:35
  41.2 9.1 %collective-permute-done.1.refs_2_ = bf16[96,4096]{1,0:T(8,128)(2,1)} collective-permute-done((bf16[96,4096]{1,0:T(8,128)(2,1)}, bf16[96,4096]{1,0:T(8,128)(2,1)}, u32[]{:S(2)}, u32[]{:S(2)}) %collective-permute-start.1) | collective-permute-done | bytes 786464 | tf_op jit(solution)/shard_map/ppermute | solution.py:16
  52.5 1.6 %collective-permute-start.19 = (s32[2,96]{1,0:T(2,128)S(1)}, s32[2,96]{1,0:T(2,128)S(1)}, u32[]{:S(2)}, u32[]{:S(2)}) collective-permute-start(s32[2,96]{1,0:T(2,128)S(1)} %bitcast.20), channel_id=1, source_target_pairs={{0,2},{1,3},{2,0},{3,1},{4,6},{5,7},{6,4},{7,5},{8,10},{9,11},{10,... | collective-permute-start | bytes 2312 | tf_op jit(solution)/shard_map/ppermute | solution.py:16
  55.9 3.8 %scores.2 = (f32[128,384]{1,0:T(8,128)S(1)}, bf16[384,4096]{1,0:T(8,128)(2,1)}) custom-call(s32[2]{0:T(128)S(1)} %pad_add_fusion.1.place_ref, bf16[96,4096]{1,0:T(8,128)(2,1)S(1)} %get-tuple-element.30.refs_0_, bf16[96,4096]{1,0:T(8,128)(2,1)S(1)} %collective-permute-done.9.refs_1_, bf16[96,4096]{1,0:T(8,128)(2,1)S(1)} %collective-permute-done.10.refs_2_, ...), custom_call_target="tpu_custom_call" | custom-call | flops 402653184 | bytes 6291456 | tf_op jit(solution)/shard_map/scores/pallas_call | solution.py:114
  60.2 1.7 %collective-permute-done.8.refs_10_ = bf16[32,4096]{1,0:T(8,128)(2,1)S(1)} collective-permute-done((bf16[32,4096]{1,0:T(8,128)(2,1)}, bf16[32,4096]{1,0:T(8,128)(2,1)S(1)}, u32[]{:S(2)}, u32[]{:S(2)}) %collective-permute-start.8) | collective-permute-done | bytes 262176 | tf_op jit(solution)/shard_map/ppermute | solution.py:35
  61.9 4.4 %scores.3 = (f32[128,384]{1,0:T(8,128)S(1)}, bf16[384,4096]{1,0:T(8,128)(2,1)}) custom-call(s32[2]{0:T(128)S(1)} %pad_add_fusion.1.place_ref, bf16[96,4096]{1,0:T(8,128)(2,1)} %get-tuple-element.31.refs_0_, bf16[96,4096]{1,0:T(8,128)(2,1)} %collective-permute-done.refs_1_, bf16[96,4096]{1,0:T(8,128)(2,1)} %collective-permute-done.1.refs_2_, ...), custom_call_target="tpu_custom_call" | custom-call | flops 402653184 | bytes 6291456 | tf_op jit(solution)/shard_map/scores/pallas_call | solution.py:114
  67.0 1.6 %group_lse.1.refs_0_ = f32[1,384]{1,0:T(1,128)} custom-call(f32[128,384]{1,0:T(8,128)} %copy-done.2), custom_call_target="tpu_custom_call" | custom-call | tf_op jit(solution)/shard_map/group_lse/pallas_call | solution.py:144
  68.6 1.5 %collective-permute-start.22 = (f32[1,384]{1,0:T(1,128)}, f32[1,384]{1,0:T(1,128)S(1)}, u32[]{:S(2)}, u32[]{:S(2)}) collective-permute-start(f32[1,384]{1,0:T(1,128)} %group_lse.1.refs_0_), channel_id=1, source_target_pairs={{0,2},{1,3},{2,0},{3,1},{4,6},{5,7},{6,4},{7,5},{8,10},{9,11},{10,... | collective-permute-start | bytes 4616 | tf_op jit(solution)/shard_map/ppermute | solution.py:16
  73.9 1.7 %posteriors.1 = (f32[1,384]{1,0:T(1,128)}, bf16[128,384]{1,0:T(8,128)(2,1)}) custom-call(s32[2]{0:T(128)} %copy-done.17, f32[128,384]{1,0:T(8,128)} %copy-done.2, s32[2,384]{1,0:T(2,128)} %reshape.29.route_ref, f32[1,384]{1,0:T(1,128)} %group_lse.1.refs_0_, f32[1,384]{1,0:T(1,128)} %copy-done.19, f32[1,384]{1,0:T(1,128)} %copy-done.20, f32[1,384]{1,0:T(1,128)} %copy-done.21), custom_call_target="tpu_custom_call" | custom-call | tf_op jit(solution)/shard_map/posteriors/pallas_call | solution.py:176
  76.4 2.4 %sums.2 = (bf16[32,4096]{1,0:T(8,128)(2,1)S(1)}, bf16[32,4096]{1,0:T(8,128)(2,1)}, bf16[32,4096]{1,0:T(8,128)(2,1)S(1)}, bf16[32,4096]{1,0:T(8,128)(2,1)}) custom-call(bf16[128,384]{1,0:T(8,128)(2,1)S(1)} %copy-done.3, bf16[384,4096]{1,0:T(8,128)(2,1)S(1)} %copy-done), custom_call_target="tpu_custom_call" | custom-call | flops 402653184 | bytes 3145728 | tf_op jit(solution)/shard_map/sums/pallas_call | solution.py:200
  79.6 3.6 %collective-permute-start.24 = (bf16[32,4096]{1,0:T(8,128)(2,1)}, bf16[32,4096]{1,0:T(8,128)(2,1)}, u32[]{:S(2)}, u32[]{:S(2)}) collective-permute-start(bf16[32,4096]{1,0:T(8,128)(2,1)} %get-tuple-element.23), channel_id=1, source_target_pairs={{0,4},{1,5},{2,6},{3,7},{16,20},{17,21},{18,22},{19,23}} | collective-permute-start | bytes 786440 | tf_op jit(solution)/shard_map/ppermute | solution.py:47
  83.2 1.4 %collective-permute-start.27 = (bf16[32,4096]{1,0:T(8,128)(2,1)}, bf16[32,4096]{1,0:T(8,128)(2,1)}, u32[]{:S(2)}, u32[]{:S(2)}) collective-permute-start(bf16[32,4096]{1,0:T(8,128)(2,1)} %get-tuple-element.21), channel_id=1, source_target_pairs={{12,8},{13,9},{14,10},{15,11},{28,24},{29,25},{30,26},{31,27}} | collective-permute-start | bytes 786440 | tf_op jit(solution)/shard_map/ppermute | solution.py:48
  84.5 1.9 %copy-done.1 = bf16[384,4096]{1,0:T(8,128)(2,1)S(1)} copy-done((bf16[384,4096]{1,0:T(8,128)(2,1)S(1)}, bf16[384,4096]{1,0:T(8,128)(2,1)}, u32[]{:S(2)}) %copy-start.1) | copy-done | bytes 3145752
  86.4 1.6 %sums.3 = (bf16[32,4096]{1,0:T(8,128)(2,1)S(1)}, bf16[32,4096]{1,0:T(8,128)(2,1)S(1)}, bf16[32,4096]{1,0:T(8,128)(2,1)S(1)}, bf16[32,4096]{1,0:T(8,128)(2,1)S(1)}) custom-call(bf16[128,384]{1,0:T(8,128)(2,1)S(1)} %copy-done.4, bf16[384,4096]{1,0:T(8,128)(2,1)S(1)} %copy-done.1), custom_call_target="tpu_custom_call" | custom-call | flops 402653184 | bytes 3145728 | tf_op jit(solution)/shard_map/sums/pallas_call | solution.py:200
  95.9 4.4 %collective-permute-start.31 = (bf16[32,4096]{1,0:T(8,128)(2,1)S(1)}, bf16[32,4096]{1,0:T(8,128)(2,1)S(1)}, u32[]{:S(2)}, u32[]{:S(2)}) collective-permute-start(bf16[32,4096]{1,0:T(8,128)(2,1)S(1)} %get-tuple-element.36), channel_id=1, source_target_pairs={{0,4},{4,8},{1,5},{5,9},{2,6},{6,10},{3,7},{7,11},{16,20},{20,24},... | collective-permute-start | bytes 786440 | tf_op jit(solution)/shard_map/ppermute | solution.py:47
  102.4 4.4 %collective-permute-start.26 = (bf16[32,4096]{1,0:T(8,128)(2,1)S(1)}, bf16[32,4096]{1,0:T(8,128)(2,1)S(1)}, u32[]{:S(2)}, u32[]{:S(2)}) collective-permute-start(bf16[32,4096]{1,0:T(8,128)(2,1)S(1)} %add_convert_fusion.3), channel_id=1, source_target_pairs={{0,4},{4,8},{8,12},{1,5},{5,9},{9,13},{2,6},{6,10},{10,14},{3,7},{... | collective-permute-start | bytes 786440 | tf_op jit(solution)/shard_map/ppermute | solution.py:47
  109.2 4.6 %collective-permute-start.32 = (bf16[32,4096]{1,0:T(8,128)(2,1)S(1)}, bf16[32,4096]{1,0:T(8,128)(2,1)S(1)}, u32[]{:S(2)}, u32[]{:S(2)}) collective-permute-start(bf16[32,4096]{1,0:T(8,128)(2,1)S(1)} %add_convert_fusion.1), channel_id=1, source_target_pairs={{0,4},{4,8},{8,12},{1,5},{5,9},{9,13},{2,6},{6,10},{10,14},{3,7},{... | collective-permute-start | bytes 786440 | tf_op jit(solution)/shard_map/ppermute | solution.py:47
  115.2 1.6 %collective-permute-done.29 = bf16[32,4096]{1,0:T(8,128)(2,1)S(1)} collective-permute-done((bf16[32,4096]{1,0:T(8,128)(2,1)S(1)}, bf16[32,4096]{1,0:T(8,128)(2,1)S(1)}, u32[]{:S(2)}, u32[]{:S(2)}) %collective-permute-start.29) | collective-permute-done | bytes 262176 | tf_op jit(solution)/shard_map/ppermute | solution.py:48
  117.7 4.5 %collective-permute-done.35 = bf16[32,4096]{1,0:T(8,128)(2,1)S(1)} collective-permute-done((bf16[32,4096]{1,0:T(8,128)(2,1)S(1)}, bf16[32,4096]{1,0:T(8,128)(2,1)S(1)}, u32[]{:S(2)}, u32[]{:S(2)}) %collective-permute-start.35) | collective-permute-done | bytes 262176 | tf_op jit(solution)/shard_map/ppermute | solution.py:48
  (120 shorter events, 41.7 us)
Async XLA Ops:
  1.7 15.2 %collective-permute-start.12 = (bf16[32,4096]{1,0:T(8,128)(2,1)S(1)}, bf16[32,4096]{1,0:T(8,128)(2,1)S(1)}, u32[]{:S(2)}, u32[]{:S(2)}) collective-permute-start(bf16[32,4096]{1,0:T(8,128)(2,1)S(1)} %get-tuple-element.32.refs_4_), channel_id=1, source_target_pairs={{0,4},{4,8},{8,12},{1,5},{5,9},{9,13},{2,6},{6,10},{10,14},{3,7},{... | collective-permute-start | bytes 786440 | tf_op jit(solution)/shard_map/ppermute | solution.py:34
  6.7 11.6 %collective-permute-start.15 = (bf16[32,4096]{1,0:T(8,128)(2,1)S(1)}, bf16[32,4096]{1,0:T(8,128)(2,1)S(1)}, u32[]{:S(2)}, u32[]{:S(2)}) collective-permute-start(bf16[32,4096]{1,0:T(8,128)(2,1)S(1)} %get-tuple-element.32.refs_4_), channel_id=1, source_target_pairs={{4,0},{8,4},{12,8},{5,1},{9,5},{13,9},{6,2},{10,6},{14,10},{7,3},{... | collective-permute-start | bytes 786440 | tf_op jit(solution)/shard_map/ppermute | solution.py:35
  8.0 11.0 %collective-permute-start.3 = (bf16[32,4096]{1,0:T(8,128)(2,1)S(1)}, bf16[32,4096]{1,0:T(8,128)(2,1)S(1)}, u32[]{:S(2)}, u32[]{:S(2)}) collective-permute-start(bf16[32,4096]{1,0:T(8,128)(2,1)S(1)} %get-tuple-element.33.refs_4_), channel_id=1, source_target_pairs={{0,4},{4,8},{8,12},{1,5},{5,9},{9,13},{2,6},{6,10},{10,14},{3,7},{... | collective-permute-start | bytes 786440 | tf_op jit(solution)/shard_map/ppermute | solution.py:34
  14.9 25.8 %collective-permute-start.10 = (bf16[96,4096]{1,0:T(8,128)(2,1)S(1)}, bf16[96,4096]{1,0:T(8,128)(2,1)S(1)}, u32[]{:S(2)}, u32[]{:S(2)}) collective-permute-start(bf16[96,4096]{1,0:T(8,128)(2,1)S(1)} %get-tuple-element.30.refs_0_), channel_id=1, source_target_pairs={{0,2},{1,3},{2,0},{3,1},{4,6},{5,7},{6,4},{7,5},{8,10},{9,11},{10,... | collective-permute-start | bytes 2359304 | tf_op jit(solution)/shard_map/ppermute | solution.py:16
  16.4 33.9 %collective-permute-start.1 = (bf16[96,4096]{1,0:T(8,128)(2,1)}, bf16[96,4096]{1,0:T(8,128)(2,1)}, u32[]{:S(2)}, u32[]{:S(2)}) collective-permute-start(bf16[96,4096]{1,0:T(8,128)(2,1)} %get-tuple-element.31.refs_0_), channel_id=1, source_target_pairs={{0,2},{1,3},{2,0},{3,1},{4,6},{5,7},{6,4},{7,5},{8,10},{9,11},{10,... | collective-permute-start | bytes 2359304 | tf_op jit(solution)/shard_map/ppermute | solution.py:16
  18.3 9.7 %collective-permute-start.13 = (bf16[32,4096]{1,0:T(8,128)(2,1)S(1)}, bf16[32,4096]{1,0:T(8,128)(2,1)S(1)}, u32[]{:S(2)}, u32[]{:S(2)}) collective-permute-start(bf16[32,4096]{1,0:T(8,128)(2,1)S(1)} %collective-permute-done.12.refs_5_), channel_id=1, source_target_pairs={{4,8},{8,12},{5,9},{9,13},{6,10},{10,14},{7,11},{11,15},{20,24},{2... | collective-permute-start | bytes 786440 | tf_op jit(solution)/shard_map/ppermute | solution.py:34
  19.0 12.3 %collective-permute-start.16 = (bf16[32,4096]{1,0:T(8,128)(2,1)S(1)}, bf16[32,4096]{1,0:T(8,128)(2,1)}, u32[]{:S(2)}, u32[]{:S(2)}) collective-permute-start(bf16[32,4096]{1,0:T(8,128)(2,1)S(1)} %collective-permute-done.15.refs_8_), channel_id=1, source_target_pairs={{4,0},{8,4},{5,1},{9,5},{6,2},{10,6},{7,3},{11,7},{20,16},{24,20},... | collective-permute-start | bytes 786440 | tf_op jit(solution)/shard_map/ppermute | solution.py:35
  28.0 10.6 %collective-permute-start.7 = (bf16[32,4096]{1,0:T(8,128)(2,1)S(1)}, bf16[32,4096]{1,0:T(8,128)(2,1)S(1)}, u32[]{:S(2)}, u32[]{:S(2)}) collective-permute-start(bf16[32,4096]{1,0:T(8,128)(2,1)S(1)} %collective-permute-done.6.refs_8_), channel_id=1, source_target_pairs={{4,0},{8,4},{5,1},{9,5},{6,2},{10,6},{7,3},{11,7},{20,16},{24,20},... | collective-permute-start | bytes 786440 | tf_op jit(solution)/shard_map/ppermute | solution.py:35
  32.6 18.5 %collective-permute-start.9 = (bf16[96,4096]{1,0:T(8,128)(2,1)S(1)}, bf16[96,4096]{1,0:T(8,128)(2,1)S(1)}, u32[]{:S(2)}, u32[]{:S(2)}) collective-permute-start(bf16[96,4096]{1,0:T(8,128)(2,1)S(1)} %get-tuple-element.30.refs_0_), channel_id=1, source_target_pairs={{0,1},{1,0},{2,3},{3,2},{4,5},{5,4},{6,7},{7,6},{8,9},{9,8},{10,11... | collective-permute-start | bytes 2359304 | tf_op jit(solution)/shard_map/ppermute | solution.py:16
  38.6 23.3 %collective-permute-start = (bf16[96,4096]{1,0:T(8,128)(2,1)}, bf16[96,4096]{1,0:T(8,128)(2,1)}, u32[]{:S(2)}, u32[]{:S(2)}) collective-permute-start(bf16[96,4096]{1,0:T(8,128)(2,1)} %get-tuple-element.31.refs_0_), channel_id=1, source_target_pairs={{0,1},{1,0},{2,3},{3,2},{4,5},{5,4},{6,7},{7,6},{8,9},{9,8},{10,11... | collective-permute-start | bytes 2359304 | tf_op jit(solution)/shard_map/ppermute | solution.py:16
  39.4 11.0 %collective-permute-start.17 = (bf16[32,4096]{1,0:T(8,128)(2,1)}, bf16[32,4096]{1,0:T(8,128)(2,1)}, u32[]{:S(2)}, u32[]{:S(2)}) collective-permute-start(bf16[32,4096]{1,0:T(8,128)(2,1)} %collective-permute-done.16.refs_9_), channel_id=1, source_target_pairs={{4,0},{5,1},{6,2},{7,3},{20,16},{21,17},{22,18},{23,19}} | collective-permute-start | bytes 786440 | tf_op jit(solution)/shard_map/ppermute | solution.py:35
  40.7 11.7 %collective-permute-start.11 = (bf16[96,4096]{1,0:T(8,128)(2,1)S(1)}, bf16[96,4096]{1,0:T(8,128)(2,1)}, u32[]{:S(2)}, u32[]{:S(2)}) collective-permute-start(bf16[96,4096]{1,0:T(8,128)(2,1)S(1)} %collective-permute-done.10.refs_2_), channel_id=1, source_target_pairs={{0,1},{1,0},{2,3},{3,2},{4,5},{5,4},{6,7},{7,6},{8,9},{9,8},{10,11... | collective-permute-start | bytes 2359304 | tf_op jit(solution)/shard_map/ppermute | solution.py:16
  50.3 11.6 %collective-permute-start.2 = (bf16[96,4096]{1,0:T(8,128)(2,1)}, bf16[96,4096]{1,0:T(8,128)(2,1)}, u32[]{:S(2)}, u32[]{:S(2)}) collective-permute-start(bf16[96,4096]{1,0:T(8,128)(2,1)} %collective-permute-done.1.refs_2_), channel_id=1, source_target_pairs={{0,1},{1,0},{2,3},{3,2},{4,5},{5,4},{6,7},{7,6},{8,9},{9,8},{10,11... | collective-permute-start | bytes 2359304 | tf_op jit(solution)/shard_map/ppermute | solution.py:16
  50.4 9.5 %collective-permute-start.5 = (bf16[32,4096]{1,0:T(8,128)(2,1)}, bf16[32,4096]{1,0:T(8,128)(2,1)S(1)}, u32[]{:S(2)}, u32[]{:S(2)}) collective-permute-start(bf16[32,4096]{1,0:T(8,128)(2,1)} %collective-permute-done.4.refs_6_), channel_id=1, source_target_pairs={{8,12},{9,13},{10,14},{11,15},{24,28},{25,29},{26,30},{27,31}} | collective-permute-start | bytes 786440 | tf_op jit(solution)/shard_map/ppermute | solution.py:34
  51.1 10.8 %collective-permute-start.8 = (bf16[32,4096]{1,0:T(8,128)(2,1)}, bf16[32,4096]{1,0:T(8,128)(2,1)S(1)}, u32[]{:S(2)}, u32[]{:S(2)}) collective-permute-start(bf16[32,4096]{1,0:T(8,128)(2,1)} %copy-done.15), channel_id=1, source_target_pairs={{4,0},{5,1},{6,2},{7,3},{20,16},{21,17},{22,18},{23,19}} | collective-permute-start | bytes 786440 | tf_op jit(solution)/shard_map/ppermute | solution.py:35
  59.7 10.7 %collective-permute-start.18 = (s32[2,96]{1,0:T(2,128)S(1)}, s32[2,96]{1,0:T(2,128)S(1)}, u32[]{:S(2)}, u32[]{:S(2)}) collective-permute-start(s32[2,96]{1,0:T(2,128)S(1)} %bitcast.21), channel_id=1, source_target_pairs={{0,1},{1,0},{2,3},{3,2},{4,5},{5,4},{6,7},{7,6},{8,9},{9,8},{10,11... | collective-permute-start | bytes 2312 | tf_op jit(solution)/shard_map/ppermute | solution.py:16
  59.9 10.5 %collective-permute-start.20 = (s32[2,96]{1,0:T(2,128)S(1)}, s32[2,96]{1,0:T(2,128)S(1)}, u32[]{:S(2)}, u32[]{:S(2)}) collective-permute-start(s32[2,96]{1,0:T(2,128)S(1)} %collective-permute-done.19), channel_id=1, source_target_pairs={{0,1},{1,0},{2,3},{3,2},{4,5},{5,4},{6,7},{7,6},{8,9},{9,8},{10,11... | collective-permute-start | bytes 2312 | tf_op jit(solution)/shard_map/ppermute | solution.py:16
  79.6 11.7 %collective-permute-start.24 = (bf16[32,4096]{1,0:T(8,128)(2,1)}, bf16[32,4096]{1,0:T(8,128)(2,1)}, u32[]{:S(2)}, u32[]{:S(2)}) collective-permute-start(bf16[32,4096]{1,0:T(8,128)(2,1)} %get-tuple-element.23), channel_id=1, source_target_pairs={{0,4},{1,5},{2,6},{3,7},{16,20},{17,21},{18,22},{19,23}} | collective-permute-start | bytes 786440 | tf_op jit(solution)/shard_map/ppermute | solution.py:47
  92.4 9.0 %collective-permute-start.25 = (bf16[32,4096]{1,0:T(8,128)(2,1)S(1)}, bf16[32,4096]{1,0:T(8,128)(2,1)S(1)}, u32[]{:S(2)}, u32[]{:S(2)}) collective-permute-start(bf16[32,4096]{1,0:T(8,128)(2,1)S(1)} %get-tuple-element.34), channel_id=1, source_target_pairs={{0,4},{4,8},{1,5},{5,9},{2,6},{6,10},{3,7},{7,11},{16,20},{20,24},... | collective-permute-start | bytes 786440 | tf_op jit(solution)/shard_map/ppermute | solution.py:47
  93.7 13.1 %collective-permute-start.28 = (bf16[32,4096]{1,0:T(8,128)(2,1)S(1)}, bf16[32,4096]{1,0:T(8,128)(2,1)S(1)}, u32[]{:S(2)}, u32[]{:S(2)}) collective-permute-start(bf16[32,4096]{1,0:T(8,128)(2,1)S(1)} %get-tuple-element.35), channel_id=1, source_target_pairs={{8,4},{12,8},{9,5},{13,9},{10,6},{14,10},{11,7},{15,11},{24,20},{2... | collective-permute-start | bytes 786440 | tf_op jit(solution)/shard_map/ppermute | solution.py:48
  95.9 13.3 %collective-permute-start.31 = (bf16[32,4096]{1,0:T(8,128)(2,1)S(1)}, bf16[32,4096]{1,0:T(8,128)(2,1)S(1)}, u32[]{:S(2)}, u32[]{:S(2)}) collective-permute-start(bf16[32,4096]{1,0:T(8,128)(2,1)S(1)} %get-tuple-element.36), channel_id=1, source_target_pairs={{0,4},{4,8},{1,5},{5,9},{2,6},{6,10},{3,7},{7,11},{16,20},{20,24},... | collective-permute-start | bytes 786440 | tf_op jit(solution)/shard_map/ppermute | solution.py:47
  100.3 13.5 %collective-permute-start.34 = (bf16[32,4096]{1,0:T(8,128)(2,1)S(1)}, bf16[32,4096]{1,0:T(8,128)(2,1)S(1)}, u32[]{:S(2)}, u32[]{:S(2)}) collective-permute-start(bf16[32,4096]{1,0:T(8,128)(2,1)S(1)} %get-tuple-element.37), channel_id=1, source_target_pairs={{8,4},{12,8},{9,5},{13,9},{10,6},{14,10},{11,7},{15,11},{24,20},{2... | collective-permute-start | bytes 786440 | tf_op jit(solution)/shard_map/ppermute | solution.py:48
  102.4 12.8 %collective-permute-start.26 = (bf16[32,4096]{1,0:T(8,128)(2,1)S(1)}, bf16[32,4096]{1,0:T(8,128)(2,1)S(1)}, u32[]{:S(2)}, u32[]{:S(2)}) collective-permute-start(bf16[32,4096]{1,0:T(8,128)(2,1)S(1)} %add_convert_fusion.3), channel_id=1, source_target_pairs={{0,4},{4,8},{8,12},{1,5},{5,9},{9,13},{2,6},{6,10},{10,14},{3,7},{... | collective-permute-start | bytes 786440 | tf_op jit(solution)/shard_map/ppermute | solution.py:47
  107.8 8.9 %collective-permute-start.29 = (bf16[32,4096]{1,0:T(8,128)(2,1)S(1)}, bf16[32,4096]{1,0:T(8,128)(2,1)S(1)}, u32[]{:S(2)}, u32[]{:S(2)}) collective-permute-start(bf16[32,4096]{1,0:T(8,128)(2,1)S(1)} %add_convert_fusion.2), channel_id=1, source_target_pairs={{4,0},{8,4},{12,8},{5,1},{9,5},{13,9},{6,2},{10,6},{14,10},{7,3},{... | collective-permute-start | bytes 786440 | tf_op jit(solution)/shard_map/ppermute | solution.py:48
  (35 other events, 255.7 us)

commit v2 on v1

v2 whole, which is shorter than its diff:
```python
from functools import partial

import jax
import jax.numpy as jnp
from jax import lax
from jax.experimental import pallas as pl
from jax.experimental.pallas import tpu as pltpu
from jax.sharding import PartitionSpec as P

PIECES = 2
TILE = 1024
VMEM_BYTES = 48 * 1024 * 1024
SMEM_SPEC = pl.BlockSpec(memory_space=pltpu.SMEM)
VMEM_SPEC = pl.BlockSpec(memory_space=pltpu.VMEM)


def relative(member, s, members):
    if members == 4:
        return member ^ s
    return lax.rem(member + (members - s), members)


def swap_bits(block, axis, bits):
    return lax.ppermute(block, axis, [(i, i ^ bits) for i in range(lax.axis_size(axis))])


def add_rounded(one, other):
    return (one.astype(jnp.float32) + other.astype(jnp.float32)).astype(jnp.bfloat16)


def pair_scatter(parts, axis):
    member = lax.axis_index(axis)
    is_end = (member == 0) | (member == 3)
    sides = [(0, 1), (1, 0), (2, 3), (3, 2)]
    middle = [(1, 2), (2, 1), (0, 0), (3, 3)]
    for_far_end = lax.ppermute(parts[3], axis, sides)
    across_end = lax.ppermute(add_rounded(parts[2], for_far_end), axis, middle)
    for_far_middle = lax.ppermute(parts[2], axis, sides)
    across_middle = lax.ppermute(add_rounded(parts[3], for_far_middle), axis, middle)
    near = jnp.where(is_end, parts[1], add_rounded(parts[1], across_end))
    from_side = lax.ppermute(near, axis, sides)
    total = parts[0].astype(jnp.float32) + from_side.astype(jnp.float32)
    return total + jnp.where(is_end, 0.0, across_middle.astype(jnp.float32))


def line_scatter(parts, axis):
    size = lax.axis_size(axis)
    up = down = None
    for s in range(1, size):
        send_up, send_down = parts[s], parts[size - s]
        if s > 1:
            send_up = add_rounded(send_up, up)
            send_down = add_rounded(send_down, down)
        up = lax.ppermute(send_up, axis, [(i, i + 1) for i in range(0, s) if i + 1 < size])
        down = lax.ppermute(send_down, axis, [(i, i - 1) for i in range(size - s, size) if i > 0])
    total = parts[0].astype(jnp.float32)
    if size > 1:
        total = total + up.astype(jnp.float32) + down.astype(jnp.float32)
    return total


def column_lse(scores):
    peak = jnp.max(scores, axis=0, keepdims=True)
    total = jnp.sum(jnp.exp(scores - peak), axis=0, keepdims=True)
    return peak + jnp.log(total)


def score_kernel(
    members, finish, place_ref, image_ref, projection_ref, noise_ref, score_ref, lse_ref, weighted_ref
):
    step = pl.program_id(0)
    member = place_ref[1]
    count = projection_ref.shape[1]
    noise = noise_ref[...]

    @pl.when(step == 0)
    def _():
        score_ref[...] = jnp.zeros_like(score_ref)

    penalties = []
    for s in range(members):
        block = projection_ref[relative(member, s, members)].astype(jnp.float32)
        scaled = block * noise
        weighted_ref[pl.ds(s * count, count), :] = scaled.astype(jnp.bfloat16)
        penalties.append(0.5 * jnp.sum(scaled * block, axis=1, keepdims=True))
    scores = lax.dot_general(
        weighted_ref[...],
        image_ref[...],
        (((1,), (1,)), ((), ())),
        preferred_element_type=jnp.float32,
    )
    score_ref[...] += scores - jnp.concatenate(penalties, axis=0)

    @pl.when(step == pl.num_programs(0) - 1)
    def _():
        if finish:
            lse_ref[...] = column_lse(score_ref[...])


def all_scores(place, images, projections, noise, finish):
    members, count, width = projections.shape
    slots = images.shape[0]
    refs = members * count
    tile = min(TILE, width)
    return pl.pallas_call(
        partial(score_kernel, members, finish),
        grid=(width // tile,),
        out_shape=(
            jax.ShapeDtypeStruct((refs, slots), jnp.float32),
            jax.ShapeDtypeStruct((1, slots), jnp.float32),
        ),
        in_specs=[
            SMEM_SPEC,
            pl.BlockSpec((slots, tile), lambda i: (0, i)),
            pl.BlockSpec((members, count, tile), lambda i: (0, 0, i)),
            pl.BlockSpec((1, tile), lambda i: (0, i)),
        ],
        out_specs=(
            pl.BlockSpec((refs, slots), lambda i: (0, 0)),
            pl.BlockSpec((1, slots), lambda i: (0, 0)),
        ),
        scratch_shapes=[pltpu.VMEM((refs, tile), jnp.bfloat16)],
        compiler_params=pltpu.CompilerParams(vmem_limit_bytes=VMEM_BYTES),
        cost_estimate=pl.CostEstimate(
            flops=2 * refs * slots * width,
            bytes_accessed=2 * slots * width,
            transcendentals=0,
        ),
        name="scores",
    )(place, images, projections, noise)


def lse_kernel(score_ref, lse_ref):
    lse_ref[...] = column_lse(score_ref[...])


def group_lse(scores):
    return pl.pallas_call(
        lse_kernel,
        out_shape=jax.ShapeDtypeStruct((1, scores.shape[1]), jnp.float32),
        name="group_lse",
    )(scores)


def sums_kernel(readers, members, place_ref, score_ref, route_ref, *refs):
    lse_refs = refs[:readers]
    image_ref = refs[readers]
    out_refs = refs[readers + 1 : readers + 1 + members]
    norm_ref, post_ref = refs[readers + 1 + members :]

    @pl.when(pl.program_id(0) == 0)
    def _():
        reader = place_ref[0]
        routes = route_ref[...]
        kept = []
        for k in range(readers):
            hits = jnp.where(routes == (reader ^ k), 1.0, 0.0)
            named = jnp.max(hits, axis=0, keepdims=True) > 0.0
            kept.append(jnp.where(named, lse_refs[k][...], -jnp.inf))
            if k == 0:
                mine = named
        highest = kept[0]
        for value in kept[1:]:
            highest = jnp.maximum(highest, value)
        spread = jnp.exp(kept[0] - highest)
        for value in kept[1:]:
            spread = spread + jnp.exp(value - highest)
        norm = highest + jnp.log(spread)
        norm_ref[...] = norm
        exponent = jnp.where(mine, score_ref[...] - norm, -jnp.inf)
        post_ref[...] = jnp.exp(exponent).astype(jnp.bfloat16)

    sums = jnp.dot(post_ref[...], image_ref[...], preferred_element_type=jnp.float32)
    count = sums.shape[0] // members
    for s in range(members):
        out_refs[s][...] = sums[s * count : (s + 1) * count].astype(out_refs[s].dtype)


def group_sums(members, place, scores, routes, lses, images, piece, pieces):
    refs = scores.shape[0]
    slots, full = images.shape
    width = full // pieces
    tile = min(TILE, width)
    steps = width // tile
    block = jax.ShapeDtypeStruct((refs // members, width), jnp.bfloat16)
    whole = lambda i: (0, 0)
    outs = pl.pallas_call(
        partial(sums_kernel, len(lses), members),
        grid=(steps,),
        out_shape=(block,) * members + (jax.ShapeDtypeStruct((1, slots), jnp.float32),),
        in_specs=[
            SMEM_SPEC,
            pl.BlockSpec((refs, slots), whole),
            pl.BlockSpec(routes.shape, whole),
            *([pl.BlockSpec((1, slots), whole)] * len(lses)),
            pl.BlockSpec((slots, tile), lambda i: (0, piece * steps + i)),
        ],
        out_specs=(pl.BlockSpec((refs // members, tile), lambda i: (0, i)),) * members
        + (pl.BlockSpec((1, slots), whole),),
        scratch_shapes=[pltpu.VMEM((refs, slots), jnp.bfloat16)],
        compiler_params=pltpu.CompilerParams(vmem_limit_bytes=VMEM_BYTES),
        cost_estimate=pl.CostEstimate(
            flops=2 * refs * slots * width,
            bytes_accessed=2 * slots * width,
            transcendentals=0,
        ),
        name="sums",
    )(place, scores, routes, *lses, images)
    return outs[:members], outs[members]


def on_device(images, routes, projections, noise_weights):
    readers = lax.axis_size("reader")
    members = lax.axis_size("blk")
    reader = lax.axis_index("reader")
    place = jnp.stack([reader, lax.axis_index("blk")]).astype(jnp.int32)
    rows, width = images.shape
    noise = noise_weights.reshape(1, width)

    route_blocks = jnp.stack([routes.T] + [swap_bits(routes.T, "reader", k) for k in range(1, readers)])
    order = jnp.arange(readers, dtype=jnp.int32) ^ reader
    all_routes = route_blocks[order].transpose(1, 0, 2).reshape(routes.shape[1], readers * rows)

    all_images = lax.all_gather(images, "reader", axis=0, tiled=True)
    every = lax.all_gather(projections[0], "blk", axis=0)
    split = lax.axis_size("sub") > 1
    scores, mine = all_scores(place, all_images, every, noise, not split)
    if split:
        scores = lax.psum(scores, "sub")
        mine = group_lse(scores)
    lses = [mine] + [swap_bits(mine, "reader", k) for k in range(1, readers)]
    scatter = pair_scatter if members == 4 else line_scatter
    totals = []
    for piece in range(PIECES):
        parts, norms = group_sums(
            members, place, scores, all_routes, lses, all_images, piece, PIECES
        )
        totals.append(scatter(parts, "blk"))
    normalizer = lax.dynamic_slice(norms.reshape(-1), (reader * rows,), (rows,))
    return (jnp.concatenate(totals, axis=1)[None], normalizer)


def solution(mesh):
    return jax.shard_map(
        on_device,
        mesh=mesh,
        in_specs=(
            P(("parts", "blk", "reader"), "sub"),
            P(("parts", "blk", "reader"), None),
            P(("parts", "reader"), "blk", "sub"),
            P(("parts", "sub")),
        ),
        out_specs=(P(("parts", "reader"), "blk", "sub"), P(("parts", "blk", "reader"))),
        check_vma=False,
    )
```

time: 124 us -> 171 us (1.38)
  waiting for transfers between devices: 33.9 us -> 121 us
  starting transfers between devices: 52.6 us -> 16.6 us
  between operations: 1.06 us -> 14.2 us
  local copies, waits for them, and re-layouts: 15.6 us -> 2.84 us
  other arithmetic: 4.71 us -> 1.75 us
    all_gather x0 -> x2, waiting for transfers between devices: none -> 93 us  [the longest x1 46.7 us: on_device(): all_images = lax.all_gather(images, 'reader', axis=0, tiled=True)]
    ppermute x36 -> x16, starting transfers between devices: 52.6 us -> 16.5 us  [the longest x6 5.08 us: swap_bits(): lax.ppermute(block, axis, [(i, i ^ bits) for i in range(lax.axis_size(axi...]
    unnamed x46 -> x6, local copies, waits for them, and re-layouts: 9.58 us -> 1.6 us
    ppermute x36 -> x16, waiting for transfers between devices: 33.9 us -> 26.7 us  [the longest x2 10.6 us: pair_scatter(): from_side = lax.ppermute(near, axis, sides)]
    slice x3 -> x0, local copies, waits for them, and re-layouts: 3.46 us -> none  [the longest x1 2.38 us: on_device(): gathered = [swap_gather(images[:, piece], 'reader') for piece in pieces]]
    convert_element_type x6 -> x4, other arithmetic: 3.4 us -> 0.25 us  [add_rounded(): (one.astype(jnp.float32) + other.astype(jnp.float32)).astype(jnp.bfloat16)]
    pallas_call x6 -> x3, Pallas kernels: 15.4 us -> 14.4 us  [the longest x2 7.53 us: group_sums(): pl.pallas_call(partial(sums_kernel, len(lses), members), grid=(steps,), o...]
  transfers between devices with their start and end apart: 36 -> 18, of which waited for: 12 -> 9; matrix products, arithmetic and copies ran while one was open for 7% -> 1% of each run, Pallas kernels for 9% -> 6%
where the time goes in v2:
time: 171 us
  waiting for transfers between devices  121 us (71%)
  starting transfers between devices  16.6 us (10%)
  Pallas kernels  14.4 us (8%)
  between operations  14.2 us (8%)
  local copies, waits for them, and re-layouts  2.84 us (2%)
  other arithmetic  1.75 us (1%)
    all_gather x1, waiting for transfers between devices, on_device(): all_images = lax.all_gather(images, 'reader', axis=0, tiled=True)  46.7 us
    all_gather x1, waiting for transfers between devices, on_device(): every = lax.all_gather(projections[0], 'blk', axis=0)  46.3 us
    ppermute x2, waiting for transfers between devices, pair_scatter(): from_side = lax.ppermute(near, axis, sides)  10.6 us
    ppermute x2, waiting for transfers between devices, pair_scatter(): for_far_middle = lax.ppermute(parts[2], axis, sides)  8.89 us
    pallas_call x2, Pallas kernels, group_sums(): pl.pallas_call(partial(sums_kernel, len(lses), members), grid=(steps,), o...  7.53 us
    pallas_call x1, Pallas kernels, all_scores(): pl.pallas_call(partial(score_kernel, members, finish), grid=(width // til...  6.85 us
    ppermute x2, waiting for transfers between devices, pair_scatter(): for_far_end = lax.ppermute(parts[3], axis, sides)  5.81 us
    ppermute x6, starting transfers between devices, swap_bits(): lax.ppermute(block, axis, [(i, i ^ bits) for i in range(lax.axis_size(axi...  5.08 us
  transfers between devices with their start and end apart: 18, of which 9 were waited for; matrix products, arithmetic and copies ran while one was open for 1% of the time, Pallas kernels for 6%

profile of v2, /device:TPU:0, one launch (start us, length us, event | category | flops | bytes accessed | tf_op | source)
XLA Modules:
  0.0 170.8 jit_solution(7303886716820469980)
XLA Ops:
  7.2 0.7 all-gather.5.cloned.1.call-update
  8.0 0.7 all-gather.3.cloned.1.call-update
  9.2 2.6 %collective-permute-start.1 = (s32[2,96]{1,0:T(2,128)S(1)}, s32[2,96]{1,0:T(2,128)S(1)}, u32[]{:S(2)}, u32[]{:S(2)}) collective-permute-start(s32[2,96]{1,0:T(2,128)S(1)} %bitcast.19), channel_id=1, source_target_pairs={{0,2},{1,3},{2,0},{3,1},{4,6},{5,7},{6,4},{7,5},{8,10},{9,11},{10,... | collective-permute-start | bytes 2312 | tf_op jit(solution)/shard_map/ppermute | solution.py:24
  11.9 46.3 %all-gather.5.cloned.1.call-done.projection_ref = bf16[4,32,8192]{2,1,0:T(8,128)(2,1)} async-done(((bf16[1,32,8192]{2,1,0:T(8,128)(2,1)}), bf16[4,32,8192]{2,1,0:T(8,128)(2,1)}) %all-gather.5.cloned.1.call-update) | async-done | bytes 2097168 | tf_op jit(solution)/shard_map/all_gather | solution.py:225
  58.3 46.7 %all-gather.3.cloned.1.call-done.image_ref.refs_4_ = bf16[384,8192]{1,0:T(8,128)(2,1)} async-done(((bf16[96,8192]{1,0:T(8,128)(2,1)}), bf16[384,8192]{1,0:T(8,128)(2,1)}) %all-gather.3.cloned.1.call-update) | async-done | bytes 6291472 | tf_op jit(solution)/shard_map/all_gather | solution.py:224
  104.9 1.6 copy-done
  106.5 6.8 %scores.1 = (f32[128,384]{1,0:T(8,128)S(1)}, f32[1,384]{1,0:T(1,128)S(1)}) custom-call(s32[2]{0:T(128)S(1)} %pad_add_fusion.1.place_ref, bf16[384,8192]{1,0:T(8,128)(2,1)} %all-gather.3.cloned.1.call-done.image_ref.refs_4_, bf16[4,32,8192]{2,1,0:T(8,128)(2,1)S(1)} %copy-done, f32[1,8192]{1,0:T(1,128)S(1)} %bitcast.16), custom_call_target="tpu_custom_call" | custom-call | flops 805306368 | bytes 6291456 | tf_op jit(solution)/shard_map/scores/pallas_call | solution.py:105
  114.0 1.3 collective-permute-start.5
  116.0 1.3 collective-permute-done.4.refs_2_
  117.3 4.0 %sums.2 = (bf16[32,4096]{1,0:T(8,128)(2,1)S(1)}, bf16[32,4096]{1,0:T(8,128)(2,1)S(1)}, bf16[32,4096]{1,0:T(8,128)(2,1)S(1)}, bf16[32,4096]{1,0:T(8,128)(2,1)S(1)}, f32[1,384]{1,0:T(1,128)}) custom-call(s32[2]{0:T(128)S(1)} %pad_add_fusion.1.place_ref, f32[128,384]{1,0:T(8,128)S(1)} %get-tuple-element.13.score_ref, s32[2,384]{1,0:T(2,128)S(1)} %reshape.29.route_ref, ...), custom_call_target="tpu_custom_call" | custom-call | flops 402653184 | bytes 3145728 | tf_op jit(solution)/shard_map/sums/pallas_call | solution.py:187
  121.3 1.5 collective-permute-start.6
  123.4 3.5 %sums.3 = (bf16[32,4096]{1,0:T(8,128)(2,1)S(1)}, bf16[32,4096]{1,0:T(8,128)(2,1)S(1)}, bf16[32,4096]{1,0:T(8,128)(2,1)S(1)}, bf16[32,4096]{1,0:T(8,128)(2,1)S(1)}, f32[1,384]{1,0:T(1,128)S(1)}) custom-call(s32[2]{0:T(128)S(1)} %pad_add_fusion.1.place_ref, f32[128,384]{1,0:T(8,128)S(1)} %get-tuple-element.13.score_ref, s32[2,384]{1,0:T(2,128)S(1)} %reshape.29.route_ref, ...), custom_call_target="tpu_custom_call" | custom-call | flops 402653184 | bytes 3145728 | tf_op jit(solution)/shard_map/sums/pallas_call | solution.py:187
  126.9 1.6 collective-permute-start.11
  129.5 0.9 collective-permute-done.6
  130.6 0.7 collective-permute-start.7
  131.2 4.9 %collective-permute-done.9 = bf16[32,4096]{1,0:T(8,128)(2,1)S(1)} collective-permute-done((bf16[32,4096]{1,0:T(8,128)(2,1)S(1)}, bf16[32,4096]{1,0:T(8,128)(2,1)S(1)}, u32[]{:S(2)}, u32[]{:S(2)}) %collective-permute-start.9) | collective-permute-done | bytes 262176 | tf_op jit(solution)/shard_map/ppermute | solution.py:38
  136.2 0.7 collective-permute-start.10
  136.9 4.9 %collective-permute-done.11 = bf16[32,4096]{1,0:T(8,128)(2,1)S(1)} collective-permute-done((bf16[32,4096]{1,0:T(8,128)(2,1)S(1)}, bf16[32,4096]{1,0:T(8,128)(2,1)S(1)}, u32[]{:S(2)}, u32[]{:S(2)}) %collective-permute-start.11) | collective-permute-done | bytes 262176 | tf_op jit(solution)/shard_map/ppermute | solution.py:36
  141.8 0.7 collective-permute-start.12
  142.5 4.0 %collective-permute-done.14 = bf16[32,4096]{1,0:T(8,128)(2,1)S(1)} collective-permute-done((bf16[32,4096]{1,0:T(8,128)(2,1)S(1)}, bf16[32,4096]{1,0:T(8,128)(2,1)S(1)}, u32[]{:S(2)}, u32[]{:S(2)}) %collective-permute-start.14) | collective-permute-done | bytes 262176 | tf_op jit(solution)/shard_map/ppermute | solution.py:38
  147.4 4.3 %collective-permute-start.8 = (bf16[32,4096]{1,0:T(8,128)(2,1)S(1)}, bf16[32,4096]{1,0:T(8,128)(2,1)S(1)}, u32[]{:S(2)}, u32[]{:S(2)}) collective-permute-start(bf16[32,4096]{1,0:T(8,128)(2,1)S(1)} %fusion), channel_id=1, source_target_pairs={{0,4},{4,0},{8,12},{12,8},{1,5},{5,1},{9,13},{13,9},{2,6},{6,2},{1... | collective-permute-start | bytes 786440 | tf_op jit(solution)/shard_map/ppermute | solution.py:41
  152.0 6.9 %collective-permute-done.8 = bf16[32,4096]{1,0:T(8,128)(2,1)S(1)} collective-permute-done((bf16[32,4096]{1,0:T(8,128)(2,1)S(1)}, bf16[32,4096]{1,0:T(8,128)(2,1)S(1)}, u32[]{:S(2)}, u32[]{:S(2)}) %collective-permute-start.8) | collective-permute-done | bytes 262176 | tf_op jit(solution)/shard_map/ppermute | solution.py:41
  159.0 3.8 %collective-permute-done.13 = bf16[32,4096]{1,0:T(8,128)(2,1)S(1)} collective-permute-done((bf16[32,4096]{1,0:T(8,128)(2,1)S(1)}, bf16[32,4096]{1,0:T(8,128)(2,1)S(1)}, u32[]{:S(2)}, u32[]{:S(2)}) %collective-permute-start.13) | collective-permute-done | bytes 262176 | tf_op jit(solution)/shard_map/ppermute | solution.py:41
  162.9 1.0 maximum_bitcast_fusion
  (40 shorter events, 5.3 us)
Async XLA Ops:
  7.2 1.5 copy-start.2
  7.2 97.8 %copy-start.1 = (f32[8192]{0:T(1024)S(1)}, f32[8192]{0:T(1024)}, u32[]{:S(2)}) copy-start(f32[8192]{0:T(1024)} %param.7) | copy-start | bytes 98308
  7.2 51.1 %all-gather.5.cloned.1.call-start = ((), (), s32[]{:S(2)}) async-start(), calls=%async_computation.1 | async-start | bytes 2621440 | tf_op jit(solution)/shard_map/all_gather | solution.py:225
  7.9 97.0 %all-gather.3.cloned.1.call-start = ((), (), s32[]{:S(2)}) async-start(), calls=%async_computation | async-start | bytes 7864320 | tf_op jit(solution)/shard_map/all_gather | solution.py:224
  8.7 105.4 %collective-permute-start = (s32[2,96]{1,0:T(2,128)S(1)}, s32[2,96]{1,0:T(2,128)S(1)}, u32[]{:S(2)}, u32[]{:S(2)}) collective-permute-start(s32[2,96]{1,0:T(2,128)S(1)} %bitcast.18), channel_id=1, source_target_pairs={{0,1},{1,0},{2,3},{3,2},{4,5},{5,4},{6,7},{7,6},{8,9},{9,8},{10,11... | collective-permute-start | bytes 2312 | tf_op jit(solution)/shard_map/ppermute | solution.py:24
  9.2 106.1 %collective-permute-start.1 = (s32[2,96]{1,0:T(2,128)S(1)}, s32[2,96]{1,0:T(2,128)S(1)}, u32[]{:S(2)}, u32[]{:S(2)}) collective-permute-start(s32[2,96]{1,0:T(2,128)S(1)} %bitcast.19), channel_id=1, source_target_pairs={{0,2},{1,3},{2,0},{3,1},{4,6},{5,7},{6,4},{7,5},{8,10},{9,11},{10,... | collective-permute-start | bytes 2312 | tf_op jit(solution)/shard_map/ppermute | solution.py:24
  11.8 103.6 %collective-permute-start.2 = (s32[2,96]{1,0:T(2,128)S(1)}, s32[2,96]{1,0:T(2,128)S(1)}, u32[]{:S(2)}, u32[]{:S(2)}) collective-permute-start(s32[2,96]{1,0:T(2,128)S(1)} %bitcast.20), channel_id=1, source_target_pairs={{0,3},{1,2},{2,1},{3,0},{4,7},{5,6},{6,5},{7,4},{8,11},{9,10},{10,... | collective-permute-start | bytes 2312 | tf_op jit(solution)/shard_map/ppermute | solution.py:24
  104.9 1.6 copy-start
  113.4 2.6 %collective-permute-start.3 = (f32[1,384]{1,0:T(1,128)S(1)}, f32[1,384]{1,0:T(1,128)S(1)}, u32[]{:S(2)}, u32[]{:S(2)}) collective-permute-start(f32[1,384]{1,0:T(1,128)S(1)} %get-tuple-element.14.refs_0_), channel_id=1, source_target_pairs={{0,1},{1,0},{2,3},{3,2},{4,5},{5,4},{6,7},{7,6},{8,9},{9,8},{10,11... | collective-permute-start | bytes 4616 | tf_op jit(solution)/shard_map/ppermute | solution.py:24
  113.7 3.6 %collective-permute-start.4 = (f32[1,384]{1,0:T(1,128)S(1)}, f32[1,384]{1,0:T(1,128)S(1)}, u32[]{:S(2)}, u32[]{:S(2)}) collective-permute-start(f32[1,384]{1,0:T(1,128)S(1)} %get-tuple-element.14.refs_0_), channel_id=1, source_target_pairs={{0,2},{1,3},{2,0},{3,1},{4,6},{5,7},{6,4},{7,5},{8,10},{9,11},{10,... | collective-permute-start | bytes 4616 | tf_op jit(solution)/shard_map/ppermute | solution.py:24
  114.0 3.3 %collective-permute-start.5 = (f32[1,384]{1,0:T(1,128)S(1)}, f32[1,384]{1,0:T(1,128)S(1)}, u32[]{:S(2)}, u32[]{:S(2)}) collective-permute-start(f32[1,384]{1,0:T(1,128)S(1)} %get-tuple-element.14.refs_0_), channel_id=1, source_target_pairs={{0,3},{1,2},{2,1},{3,0},{4,7},{5,6},{6,5},{7,4},{8,11},{9,10},{10,... | collective-permute-start | bytes 4616 | tf_op jit(solution)/shard_map/ppermute | solution.py:24
  121.3 9.2 %collective-permute-start.6 = (bf16[32,4096]{1,0:T(8,128)(2,1)S(1)}, bf16[32,4096]{1,0:T(8,128)(2,1)S(1)}, u32[]{:S(2)}, u32[]{:S(2)}) collective-permute-start(bf16[32,4096]{1,0:T(8,128)(2,1)S(1)} %get-tuple-element.18), channel_id=1, source_target_pairs={{0,4},{4,0},{8,12},{12,8},{1,5},{5,1},{9,13},{13,9},{2,6},{6,2},{1... | collective-permute-start | bytes 786440 | tf_op jit(solution)/shard_map/ppermute | solution.py:36
  122.8 13.3 %collective-permute-start.9 = (bf16[32,4096]{1,0:T(8,128)(2,1)S(1)}, bf16[32,4096]{1,0:T(8,128)(2,1)S(1)}, u32[]{:S(2)}, u32[]{:S(2)}) collective-permute-start(bf16[32,4096]{1,0:T(8,128)(2,1)S(1)} %get-tuple-element.17), channel_id=1, source_target_pairs={{0,4},{4,0},{8,12},{12,8},{1,5},{5,1},{9,13},{13,9},{2,6},{6,2},{1... | collective-permute-start | bytes 786440 | tf_op jit(solution)/shard_map/ppermute | solution.py:38
  126.9 14.9 %collective-permute-start.11 = (bf16[32,4096]{1,0:T(8,128)(2,1)S(1)}, bf16[32,4096]{1,0:T(8,128)(2,1)S(1)}, u32[]{:S(2)}, u32[]{:S(2)}) collective-permute-start(bf16[32,4096]{1,0:T(8,128)(2,1)S(1)} %get-tuple-element.22), channel_id=1, source_target_pairs={{0,4},{4,0},{8,12},{12,8},{1,5},{5,1},{9,13},{13,9},{2,6},{6,2},{1... | collective-permute-start | bytes 786440 | tf_op jit(solution)/shard_map/ppermute | solution.py:36
  128.4 18.1 %collective-permute-start.14 = (bf16[32,4096]{1,0:T(8,128)(2,1)S(1)}, bf16[32,4096]{1,0:T(8,128)(2,1)S(1)}, u32[]{:S(2)}, u32[]{:S(2)}) collective-permute-start(bf16[32,4096]{1,0:T(8,128)(2,1)S(1)} %get-tuple-element.21), channel_id=1, source_target_pairs={{0,4},{4,0},{8,12},{12,8},{1,5},{5,1},{9,13},{13,9},{2,6},{6,2},{1... | collective-permute-start | bytes 786440 | tf_op jit(solution)/shard_map/ppermute | solution.py:38
  130.6 16.7 %collective-permute-start.7 = (bf16[32,4096]{1,0:T(8,128)(2,1)S(1)}, bf16[32,4096]{1,0:T(8,128)(2,1)S(1)}, u32[]{:S(2)}, u32[]{:S(2)}) collective-permute-start(bf16[32,4096]{1,0:T(8,128)(2,1)S(1)} %add_convert_fusion.5), channel_id=1, source_target_pairs={{4,8},{8,4},{0,0},{12,12},{5,9},{9,5},{1,1},{13,13},{6,10},{10,6},... | collective-permute-start | bytes 786440 | tf_op jit(solution)/shard_map/ppermute | solution.py:37
  136.2 15.8 %collective-permute-start.10 = (bf16[32,4096]{1,0:T(8,128)(2,1)S(1)}, bf16[32,4096]{1,0:T(8,128)(2,1)S(1)}, u32[]{:S(2)}, u32[]{:S(2)}) collective-permute-start(bf16[32,4096]{1,0:T(8,128)(2,1)S(1)} %add_convert_fusion.3), channel_id=1, source_target_pairs={{4,8},{8,4},{0,0},{12,12},{5,9},{9,5},{1,1},{13,13},{6,10},{10,6},... | collective-permute-start | bytes 786440 | tf_op jit(solution)/shard_map/ppermute | solution.py:39
  141.8 9.9 %collective-permute-start.12 = (bf16[32,4096]{1,0:T(8,128)(2,1)S(1)}, bf16[32,4096]{1,0:T(8,128)(2,1)S(1)}, u32[]{:S(2)}, u32[]{:S(2)}) collective-permute-start(bf16[32,4096]{1,0:T(8,128)(2,1)S(1)} %add_convert_fusion.2), channel_id=1, source_target_pairs={{4,8},{8,4},{0,0},{12,12},{5,9},{9,5},{1,1},{13,13},{6,10},{10,6},... | collective-permute-start | bytes 786440 | tf_op jit(solution)/shard_map/ppermute | solution.py:37
  146.6 12.4 %collective-permute-start.15 = (bf16[32,4096]{1,0:T(8,128)(2,1)S(1)}, bf16[32,4096]{1,0:T(8,128)(2,1)S(1)}, u32[]{:S(2)}, u32[]{:S(2)}) collective-permute-start(bf16[32,4096]{1,0:T(8,128)(2,1)S(1)} %add_convert_fusion), channel_id=1, source_target_pairs={{4,8},{8,4},{0,0},{12,12},{5,9},{9,5},{1,1},{13,13},{6,10},{10,6},... | collective-permute-start | bytes 786440 | tf_op jit(solution)/shard_map/ppermute | solution.py:39
  147.4 11.5 %collective-permute-start.8 = (bf16[32,4096]{1,0:T(8,128)(2,1)S(1)}, bf16[32,4096]{1,0:T(8,128)(2,1)S(1)}, u32[]{:S(2)}, u32[]{:S(2)}) collective-permute-start(bf16[32,4096]{1,0:T(8,128)(2,1)S(1)} %fusion), channel_id=1, source_target_pairs={{0,4},{4,0},{8,12},{12,8},{1,5},{5,1},{9,13},{13,9},{2,6},{6,2},{1... | collective-permute-start | bytes 786440 | tf_op jit(solution)/shard_map/ppermute | solution.py:41
  151.7 11.0 %collective-permute-start.13 = (bf16[32,4096]{1,0:T(8,128)(2,1)S(1)}, bf16[32,4096]{1,0:T(8,128)(2,1)S(1)}, u32[]{:S(2)}, u32[]{:S(2)}) collective-permute-start(bf16[32,4096]{1,0:T(8,128)(2,1)S(1)} %fusion.1), channel_id=1, source_target_pairs={{0,4},{4,0},{8,12},{12,8},{1,5},{5,1},{9,13},{13,9},{2,6},{6,2},{1... | collective-permute-start | bytes 786440 | tf_op jit(solution)/shard_map/ppermute | solution.py:41
Sparse Core Ops, SparseCore 0:
  9.6 48.6 all-gather.4
  59.8 45.0 all-gather.2

commit v3 on v2

v3 whole, which is shorter than its diff:
```python
from functools import partial

import jax
import jax.numpy as jnp
from jax import lax
from jax.experimental import pallas as pl
from jax.experimental.pallas import tpu as pltpu
from jax.sharding import PartitionSpec as P

EIGHTHS = (4, 4)
FAR_PARTS = (1, 2)
TILE = 1024
VMEM_BYTES = 48 * 1024 * 1024
SMEM_SPEC = pl.BlockSpec(memory_space=pltpu.SMEM)
VMEM_SPEC = pl.BlockSpec(memory_space=pltpu.VMEM)


def swap_bits(block, axis, bits):
    return lax.ppermute(block, axis, [(i, i ^ bits) for i in range(lax.axis_size(axis))])


def add_rounded(one, other):
    return (one.astype(jnp.float32) + other.astype(jnp.float32)).astype(jnp.bfloat16)


def pair_scatter(pieces, axis):
    member = lax.axis_index(axis)
    is_end = (member == 0) | (member == 3)
    sides = [(0, 1), (1, 0), (2, 3), (3, 2)]
    middle = [(1, 2), (2, 1), (0, 0), (3, 3)]
    for_far_end = [lax.ppermute(parts[3], axis, sides) for parts in pieces]
    second = lax.optimization_barrier([parts[2] for parts in pieces])
    for_far_middle = [lax.ppermute(part, axis, sides) for part in second]
    totals = []
    for parts, part, end, mid in zip(pieces, second, for_far_end, for_far_middle):
        across_end = lax.ppermute(add_rounded(part, end), axis, middle)
        across_middle = lax.ppermute(add_rounded(parts[3], mid), axis, middle)
        near = jnp.where(is_end, parts[1], add_rounded(parts[1], across_end))
        from_side = lax.ppermute(near, axis, sides)
        total = parts[0].astype(jnp.float32) + from_side.astype(jnp.float32)
        totals.append(total + jnp.where(is_end, 0.0, across_middle.astype(jnp.float32)))
    return totals


def line_scatter(pieces, axis):
    return [line_sum(parts, axis) for parts in pieces]


def line_sum(parts, axis):
    size = lax.axis_size(axis)
    up = down = None
    for s in range(1, size):
        send_up, send_down = parts[s], parts[size - s]
        if s > 1:
            send_up = add_rounded(send_up, up)
            send_down = add_rounded(send_down, down)
        up = lax.ppermute(send_up, axis, [(i, i + 1) for i in range(0, s) if i + 1 < size])
        down = lax.ppermute(send_down, axis, [(i, i - 1) for i in range(size - s, size) if i > 0])
    total = parts[0].astype(jnp.float32)
    if size > 1:
        total = total + up.astype(jnp.float32) + down.astype(jnp.float32)
    return total


def column_lse(scores):
    peak = jnp.max(scores, axis=0, keepdims=True)
    total = jnp.sum(jnp.exp(scores - peak), axis=0, keepdims=True)
    return peak + jnp.log(total)


def place_blocks(place_ref, groups, all_ref, steps):
    rows = groups[0][0].shape[0]
    step = pl.program_id(0)
    for k, refs in enumerate(groups):
        start = pl.multiple_of((place_ref[0] ^ k) * rows, rows)
        each = steps // len(refs)
        for i, ref in enumerate(refs):
            if len(refs) == 1:
                all_ref[pl.ds(start, rows), :] = ref[...]
                continue

            @pl.when((step >= i * each) & (step < (i + 1) * each))
            def _(start=start, ref=ref):
                all_ref[pl.ds(start, rows), :] = ref[...]


def take_groups(refs, counts):
    return [[refs.pop(0) for _ in range(n)] for n in counts]


def flat(groups):
    return [one for group in groups for one in group]


def score_kernel(counts, steps, first, finish, place_ref, *refs):
    parts, pairs = counts
    refs = list(refs)
    image_refs = take_groups(refs, parts)
    pair_refs = take_groups(refs, pairs)
    noise_ref = refs.pop(0)
    earlier_ref = None if first else refs.pop(0)
    score_ref, lse_ref, all_ref, weighted_ref, penalty_ref, sum_ref = refs
    step = pl.program_id(0)
    count = pair_refs[0][0].shape[0]
    noise = noise_ref[...]

    @pl.when(step == 0)
    def _():
        sum_ref[...] = jnp.zeros_like(sum_ref)
        penalty_ref[...] = jnp.zeros_like(penalty_ref)

    place_blocks(place_ref, image_refs, all_ref, steps)

    def weigh(s, ref):
        block = ref[...].astype(jnp.float32)
        scaled = block * noise
        weighted_ref[pl.ds(s * count, count), :] = scaled.astype(jnp.bfloat16)
        penalty_ref[pl.ds(s * count, count), :] += 0.5 * jnp.sum(
            scaled * block, axis=1, keepdims=True
        )

    for s, pair in enumerate(pair_refs):
        if len(pair) == 1:
            weigh(s, pair[0])
            continue

        @pl.when(place_ref[1] == 1)
        def _(s=s, pair=pair):
            weigh(s, pair[0])

        @pl.when(place_ref[1] == 0)
        def _(s=s, pair=pair):
            weigh(s, pair[1])

    sum_ref[...] += lax.dot_general(
        all_ref[...],
        weighted_ref[...],
        (((1,), (1,)), ((), ())),
        preferred_element_type=jnp.float32,
    )

    @pl.when(step == pl.num_programs(0) - 1)
    def _():
        scores = sum_ref[...].T - penalty_ref[...]
        if not first:
            scores = scores + earlier_ref[...]
        score_ref[...] = scores
        if finish:
            lse_ref[...] = column_lse(scores)


def column_specs(groups, tile, piece):
    steps = (piece.stop - piece.start) // tile
    specs = []
    for group in groups:
        for i, array in enumerate(group):
            rows, width = array.shape
            if len(group) == 1 and width >= piece.stop:
                index = lambda j: (0, piece.start // tile + j)
            else:
                each = width // tile
                index = lambda j, i=i, each=each: (0, jnp.clip(j - i * each, 0, each - 1))
            specs.append(pl.BlockSpec((rows, tile), index))
    return specs


def score_piece(place, piece, images, pairs, noise, earlier, finish):
    tile = min(TILE, piece.stop - piece.start)
    steps = (piece.stop - piece.start) // tile
    rows = images[0][0].shape[0]
    refs = len(pairs) * pairs[0][0].shape[0]
    slots = len(images) * rows
    blocks = [*flat(images), *flat(pairs), noise]
    specs = column_specs(images, tile, piece) + [
        spec for one in flat(pairs) + [noise] for spec in column_specs([[one]], tile, piece)
    ]
    whole = pl.BlockSpec((refs, slots), lambda i: (0, 0))
    if earlier is not None:
        blocks.append(earlier)
        specs.append(whole)
    return pl.pallas_call(
        partial(
            score_kernel,
            ([len(group) for group in images], [len(pair) for pair in pairs]),
            steps,
            earlier is None,
            finish,
        ),
        grid=(steps,),
        out_shape=(
            jax.ShapeDtypeStruct((refs, slots), jnp.float32),
            jax.ShapeDtypeStruct((1, slots), jnp.float32),
        ),
        in_specs=[SMEM_SPEC, *specs],
        out_specs=(whole, pl.BlockSpec((1, slots), lambda i: (0, 0))),
        scratch_shapes=[
            pltpu.VMEM((slots, tile), jnp.bfloat16),
            pltpu.VMEM((refs, tile), jnp.bfloat16),
            pltpu.VMEM((refs, 1), jnp.float32),
            pltpu.VMEM((slots, refs), jnp.float32),
        ],
        compiler_params=pltpu.CompilerParams(vmem_limit_bytes=VMEM_BYTES),
        cost_estimate=pl.CostEstimate(
            flops=2 * refs * slots * tile * steps,
            bytes_accessed=2 * slots * tile * steps,
            transcendentals=0,
        ),
        name="scores",
    )(place, *blocks)


def lse_kernel(score_ref, lse_ref):
    lse_ref[...] = column_lse(score_ref[...])


def group_lse(scores):
    return pl.pallas_call(
        lse_kernel,
        out_shape=jax.ShapeDtypeStruct((1, scores.shape[1]), jnp.float32),
        name="group_lse",
    )(scores)


def sums_kernel(parts, steps, members, place_ref, score_ref, route_ref, *refs):
    readers = len(parts)
    refs = list(refs)
    lse_refs = [refs.pop(0) for _ in range(readers)]
    image_refs = take_groups(refs, parts)
    out_refs = [refs.pop(0) for _ in range(members)]
    norm_ref, post_ref, all_ref = refs

    @pl.when(pl.program_id(0) == 0)
    def _():
        reader = place_ref[0]
        routes = route_ref[...]
        kept = []
        for k in range(readers):
            hits = jnp.where(routes == (reader ^ k), 1.0, 0.0)
            named = jnp.max(hits, axis=0, keepdims=True) > 0.0
            kept.append(jnp.where(named, lse_refs[k][...], -jnp.inf))
            if k == 0:
                mine = named
        highest = kept[0]
        for value in kept[1:]:
            highest = jnp.maximum(highest, value)
        spread = jnp.exp(kept[0] - highest)
        for value in kept[1:]:
            spread = spread + jnp.exp(value - highest)
        norm = highest + jnp.log(spread)
        norm_ref[...] = norm
        exponent = jnp.where(mine, score_ref[...] - norm, -jnp.inf)
        post_ref[...] = jnp.exp(exponent).astype(jnp.bfloat16)

    place_blocks(place_ref, image_refs, all_ref, steps)
    sums = jnp.dot(post_ref[...], all_ref[...], preferred_element_type=jnp.float32)
    count = sums.shape[0] // members
    for s in range(members):
        out_refs[s][...] = sums[s * count : (s + 1) * count].astype(out_refs[s].dtype)


def sums_piece(members, place, scores, routes, lses, images, piece):
    refs, slots = scores.shape
    width = piece.stop - piece.start
    tile = min(TILE, width)
    block = jax.ShapeDtypeStruct((refs // members, width), jnp.bfloat16)
    whole = lambda i: (0, 0)
    outs = pl.pallas_call(
        partial(sums_kernel, [len(group) for group in images], width // tile, members),
        grid=(width // tile,),
        out_shape=(block,) * members + (jax.ShapeDtypeStruct((1, slots), jnp.float32),),
        in_specs=[
            SMEM_SPEC,
            pl.BlockSpec((refs, slots), whole),
            pl.BlockSpec(routes.shape, whole),
            *([pl.BlockSpec((1, slots), whole)] * len(lses)),
            *column_specs(images, tile, piece),
        ],
        out_specs=(pl.BlockSpec((refs // members, tile), lambda i: (0, i)),) * members
        + (pl.BlockSpec((1, slots), whole),),
        scratch_shapes=[
            pltpu.VMEM((refs, slots), jnp.bfloat16),
            pltpu.VMEM((slots, tile), jnp.bfloat16),
        ],
        compiler_params=pltpu.CompilerParams(vmem_limit_bytes=VMEM_BYTES),
        cost_estimate=pl.CostEstimate(
            flops=2 * refs * slots * width,
            bytes_accessed=2 * slots * width,
            transcendentals=0,
        ),
        name="sums",
    )(place, scores, routes, *lses, *flat(images))
    return outs[:members], outs[members]


def swap_gather(block, axis, bit):
    held = {0: block}
    while bit:
        for k in list(held):
            held[k ^ bit] = swap_bits(held[k], axis, bit)
        bit //= 2
    return [held[k] for k in range(len(held))]


def pair_gather(block, axis):
    sides = [(0, 1), (1, 0), (2, 3), (3, 2)]
    middle = [(1, 2), (2, 1), (0, 0), (3, 3)]
    side, across = lax.optimization_barrier(
        (lax.ppermute(block, axis, sides), lax.ppermute(block, axis, middle))
    )
    far, across_far = lax.optimization_barrier(
        (lax.ppermute(across, axis, sides), lax.ppermute(side, axis, middle))
    )
    end = lax.ppermute(across_far, axis, sides)
    return [[block], [side], [far, across_far], [end, across]]


def line_gather(block, axis):
    size, member = lax.axis_size(axis), lax.axis_index(axis)
    ahead, behind = [block], [block]
    for s in range(1, size):
        ahead.append(lax.ppermute(ahead[-1], axis, [(i, i + 1) for i in range(s - 1, size - 1)]))
        behind.append(lax.ppermute(behind[-1], axis, [(i, i - 1) for i in range(1, size - s + 1)]))
    blocks = [block]
    for s in range(1, size):
        blocks.append(jnp.where(member >= s, ahead[s], behind[size - s]))
    return [[one] for one in blocks]


def cut(width, eighths):
    edges = [0]
    for part in eighths:
        edges.append(edges[-1] + width * part // 8)
    return [slice(a, b) for a, b in zip(edges, edges[1:])]


def on_device(images, routes, projections, noise_weights):
    readers = lax.axis_size("reader")
    members = lax.axis_size("blk")
    reader = lax.axis_index("reader")
    member = lax.axis_index("blk")
    is_end = (member == 0) | (member == members - 1)
    place = jnp.stack([reader, is_end.astype(jnp.int32)]).astype(jnp.int32)
    rows, width = images.shape
    noise = noise_weights.reshape(1, width)
    pieces = cut(width, EIGHTHS)

    far_blocks = []
    for piece, parts in zip(pieces, FAR_PARTS):
        first = swap_bits(images[:, piece], "reader", readers // 2)
        step = first.shape[1] // parts
        cuts = [
            swap_gather(first[:, i * step : (i + 1) * step], "reader", readers // 4)
            for i in range(parts)
        ]
        far_blocks.append([[first]] + [list(group) for group in list(zip(*cuts))[1:]])
    line = (pair_gather if members == 4 else line_gather)(projections[0], "blk")
    near_blocks = [[one] for one in swap_gather(images, "reader", readers // 4)]

    route_blocks = jnp.stack([routes.T] + [swap_bits(routes.T, "reader", k) for k in range(1, readers)])
    order = jnp.arange(readers, dtype=jnp.int32) ^ reader
    all_routes = route_blocks[order].transpose(1, 0, 2).reshape(routes.shape[1], readers * rows)

    split = lax.axis_size("sub") > 1
    scores = None
    for q, piece in enumerate(pieces):
        finish = q == len(pieces) - 1 and not split
        scores, mine = score_piece(
            place, piece, near_blocks + far_blocks[q], line, noise, scores, finish
        )
    if split:
        scores = lax.psum(scores, "sub")
        mine = group_lse(scores)
    lses = [mine] + [swap_bits(mine, "reader", k) for k in range(1, readers)]
    scatter = pair_scatter if members == 4 else line_scatter
    sums = []
    for q, piece in enumerate(pieces):
        parts, norms = sums_piece(
            members, place, scores, all_routes, lses, near_blocks + far_blocks[q], piece
        )
        sums.append(parts)
    totals = scatter(sums, "blk")
    normalizer = lax.dynamic_slice(norms.reshape(-1), (reader * rows,), (rows,))
    return (jnp.concatenate(totals, axis=1)[None], normalizer)


def solution(mesh):
    return jax.shard_map(
        on_device,
        mesh=mesh,
        in_specs=(
            P(("parts", "blk", "reader"), "sub"),
            P(("parts", "blk", "reader"), None),
            P(("parts", "reader"), "blk", "sub"),
            P(("parts", "sub")),
        ),
        out_specs=(P(("parts", "reader"), "blk", "sub"), P(("parts", "blk", "reader"))),
        check_vma=False,
    )
```

time: 171 us -> 131 us (0.77)
  waiting for transfers between devices: 121 us -> 46.1 us
  starting transfers between devices: 16.6 us -> 41.4 us
  local copies, waits for them, and re-layouts: 2.84 us -> 18.1 us
  between operations: 14.2 us -> 0.98 us
  Pallas kernels: 14.4 us -> 19.1 us
  other arithmetic: 1.75 us -> 4.25 us
    all_gather x2 -> x0, waiting for transfers between devices: 93 us -> none  [the longest x1 46.7 us: on_device(): all_images = lax.all_gather(images, 'reader', axis=0, tiled=True)]
    ppermute x8 -> x13, starting transfers between devices: 6.83 us -> 23 us  [the longest x2 5.06 us: pair_scatter(): for_far_middle = [lax.ppermute(part, axis, sides) for part in second]]
    ppermute x8 -> x13, waiting for transfers between devices: 14.7 us -> 27.6 us  [the longest x2 8.64 us: pair_scatter(): for_far_end = [lax.ppermute(parts[3], axis, sides) for parts in pieces]]
    ppermute x6 -> x12, waiting for transfers between devices: 1.3 us -> 12.9 us  [swap_bits(): lax.ppermute(block, axis, [(i, i ^ bits) for i in range(lax.axis_size(axi...]
    unnamed x6 -> x72, local copies, waits for them, and re-layouts: 1.6 us -> 11.1 us
    ppermute x2, starting transfers between devices: 4.57 us -> 12 us  [pair_scatter(): from_side = lax.ppermute(near, axis, sides)]
    ppermute x2, waiting for transfers between devices: 10.6 us -> 5.57 us  [pair_scatter(): from_side = lax.ppermute(near, axis, sides)]
    pallas_call x3 -> x4, Pallas kernels: 14.4 us -> 19.1 us  [the longest x2 10.6 us: score_piece(): pl.pallas_call(partial(score_kernel, ([len(group) for group in images], [...]
  transfers between devices with their start and end apart: 18 -> 27, of which waited for: 9 -> 10; matrix products, arithmetic and copies ran while one was open for 1% -> 8% of each run, Pallas kernels for 6% -> 8%
where the time goes in v3:
time: 131 us; the launch traced here: 130 us
  waiting for transfers between devices  46.1 us (35%)
  starting transfers between devices  41.4 us (32%)
  Pallas kernels  19.1 us (15%)
  local copies, waits for them, and re-layouts  18.1 us (14%)
  other arithmetic  4.25 us (3%)
    ppermute x12, waiting for transfers between devices, swap_bits(): lax.ppermute(block, axis, [(i, i ^ bits) for i in range(lax.axis_size(axi...  12.9 us
    ppermute x2, starting transfers between devices, pair_scatter(): from_side = lax.ppermute(near, axis, sides)  12 us
    unnamed x72, local copies, waits for them, and re-layouts  11.1 us
    pallas_call x2, Pallas kernels, score_piece(): pl.pallas_call(partial(score_kernel, ([len(group) for group in images], [...  10.6 us
    ppermute x2, waiting for transfers between devices, pair_scatter(): for_far_end = [lax.ppermute(parts[3], axis, sides) for parts in pieces]  8.64 us
    pallas_call x2, Pallas kernels, sums_piece(): pl.pallas_call(partial(sums_kernel, [len(group) for group in images], wid...  8.5 us
    ppermute x2, waiting for transfers between devices, pair_scatter(): for_far_middle = [lax.ppermute(part, axis, sides) for part in second]  7.82 us
    ppermute x1, waiting for transfers between devices, pair_gather(): lax.ppermute(block, axis, sides)  6.82 us
  transfers between devices with their start and end apart: 27, of which 10 were waited for; matrix products, arithmetic and copies ran while one was open for 8% of the time, Pallas kernels for 8%

profile of v3, /device:TPU:0, one launch (start us, length us, event | category | flops | bytes accessed | tf_op | source)
XLA Modules:
  0.0 129.9 jit_solution(17001288722657923947)
XLA Ops:
  0.6 3.1 %collective-permute-start.4 = (bf16[32,8192]{1,0:T(8,128)(2,1)}, bf16[32,8192]{1,0:T(8,128)(2,1)S(1)}, u32[]{:S(2)}, u32[]{:S(2)}) collective-permute-start(bf16[32,8192]{1,0:T(8,128)(2,1)} %bitcast.17), channel_id=1, source_target_pairs={{0,4},{4,0},{8,12},{12,8},{1,5},{5,1},{9,13},{13,9},{2,6},{6,2},{1... | collective-permute-start | bytes 1572872 | tf_op jit(solution)/shard_map/ppermute | solution.py:308
  3.7 1.7 %collective-permute-start.5 = (bf16[32,8192]{1,0:T(8,128)(2,1)}, bf16[32,8192]{1,0:T(8,128)(2,1)S(1)}, u32[]{:S(2)}, u32[]{:S(2)}) collective-permute-start(bf16[32,8192]{1,0:T(8,128)(2,1)} %bitcast.18), channel_id=1, source_target_pairs={{4,8},{8,4},{0,0},{12,12},{5,9},{9,5},{1,1},{13,13},{6,10},{10,6},... | collective-permute-start | bytes 1572872 | tf_op jit(solution)/shard_map/ppermute | solution.py:308
  5.4 1.5 %fusion.3 = (bf16[96,4096]{1,0:T(8,128)(2,1)S(1)}, bf16[96,4096]{1,0:T(8,128)(2,1)S(1)}) fusion(bf16[96,8192]{1,0:T(8,128)(2,1)} %refs_4_.3), kind=kLoop, calls=%fused_computation.18 | loop fusion | bytes 3145728 | tf_op jit(solution)/shard_map/slice | solution.py:349
  7.0 1.6 %collective-permute-start.9 = (bf16[96,4096]{1,0:T(8,128)(2,1)S(1)}, bf16[96,4096]{1,0:T(8,128)(2,1)}, u32[]{:S(2)}, u32[]{:S(2)}) collective-permute-start(bf16[96,4096]{1,0:T(8,128)(2,1)S(1)} %get-tuple-element.38), channel_id=1, source_target_pairs={{0,2},{1,3},{2,0},{3,1},{4,6},{5,7},{6,4},{7,5},{8,10},{9,11},{10,... | collective-permute-start | bytes 2359304 | tf_op jit(solution)/shard_map/ppermute | solution.py:19
  9.0 6.8 %collective-permute-done.4.refs_5_.refs_6_ = bf16[32,8192]{1,0:T(8,128)(2,1)S(1)} collective-permute-done((bf16[32,8192]{1,0:T(8,128)(2,1)}, bf16[32,8192]{1,0:T(8,128)(2,1)S(1)}, u32[]{:S(2)}, u32[]{:S(2)}) %collective-permute-start.4) | collective-permute-done | bytes 524320 | tf_op jit(solution)/shard_map/ppermute | solution.py:308
  15.9 4.8 %collective-permute-start.6 = (bf16[32,8192]{1,0:T(8,128)(2,1)S(1)}, bf16[32,8192]{1,0:T(8,128)(2,1)S(1)}, u32[]{:S(2)}, u32[]{:S(2)}) collective-permute-start(bf16[32,8192]{1,0:T(8,128)(2,1)S(1)} %collective-permute-done.5.refs_9_.refs_10_), channel_id=1, source_target_pairs={{0,4},{4,0},{8,12},{12,8},{1,5},{5,1},{9,13},{13,9},{2,6},{6,2},{1... | collective-permute-start | bytes 1572872 | tf_op jit(solution)/shard_map/ppermute | solution.py:311
  20.6 1.5 %collective-permute-start.7 = (bf16[32,8192]{1,0:T(8,128)(2,1)S(1)}, bf16[32,8192]{1,0:T(8,128)(2,1)}, u32[]{:S(2)}, u32[]{:S(2)}) collective-permute-start(bf16[32,8192]{1,0:T(8,128)(2,1)S(1)} %collective-permute-done.4.refs_5_.refs_6_), channel_id=1, source_target_pairs={{4,8},{8,4},{0,0},{12,12},{5,9},{9,5},{1,1},{13,13},{6,10},{10,6},... | collective-permute-start | bytes 1572872 | tf_op jit(solution)/shard_map/ppermute | solution.py:311
  22.1 5.5 %collective-permute-done.9.refs_2_.refs_6_ = bf16[96,4096]{1,0:T(8,128)(2,1)} collective-permute-done((bf16[96,4096]{1,0:T(8,128)(2,1)S(1)}, bf16[96,4096]{1,0:T(8,128)(2,1)}, u32[]{:S(2)}, u32[]{:S(2)}) %collective-permute-start.9) | collective-permute-done | bytes 786464 | tf_op jit(solution)/shard_map/ppermute | solution.py:19
  27.6 4.2 %collective-permute-done.6.refs_6_.refs_7_ = bf16[32,8192]{1,0:T(8,128)(2,1)S(1)} collective-permute-done((bf16[32,8192]{1,0:T(8,128)(2,1)S(1)}, bf16[32,8192]{1,0:T(8,128)(2,1)S(1)}, u32[]{:S(2)}, u32[]{:S(2)}) %collective-permute-start.6) | collective-permute-done | bytes 524320 | tf_op jit(solution)/shard_map/ppermute | solution.py:311
  31.8 3.7 %collective-permute-start.8 = (bf16[32,8192]{1,0:T(8,128)(2,1)}, bf16[32,8192]{1,0:T(8,128)(2,1)}, u32[]{:S(2)}, u32[]{:S(2)}) collective-permute-start(bf16[32,8192]{1,0:T(8,128)(2,1)} %collective-permute-done.7.refs_7_.refs_8_), channel_id=1, source_target_pairs={{0,4},{4,0},{8,12},{12,8},{1,5},{5,1},{9,13},{13,9},{2,6},{6,2},{1... | collective-permute-start | bytes 1572872 | tf_op jit(solution)/shard_map/ppermute | solution.py:313
  35.5 7.4 %collective-permute-done.1.refs_2_.refs_6_ = bf16[96,4096]{1,0:T(8,128)(2,1)S(1)} collective-permute-done((bf16[96,4096]{1,0:T(8,128)(2,1)S(1)}, bf16[96,4096]{1,0:T(8,128)(2,1)S(1)}, u32[]{:S(2)}, u32[]{:S(2)}) %collective-permute-start.1) | collective-permute-done | bytes 786464 | tf_op jit(solution)/shard_map/ppermute | solution.py:19
  53.2 5.5 %scores.2 = (f32[128,384]{1,0:T(8,128)S(1)}, f32[1,384]{1,0:T(1,128)}) custom-call(s32[2]{0:T(128)S(1)} %pad_add_fusion.1.place_ref, bf16[96,8192]{1,0:T(8,128)(2,1)} %refs_4_.3, bf16[96,8192]{1,0:T(8,128)(2,1)} %copy-done.2, bf16[96,4096]{1,0:T(8,128)(2,1)} %collective-permute-done.9.refs_2_.refs_6_, ...), custom_call_target="tpu_custom_call" | custom-call | flops 402653184 | bytes 3145728 | tf_op jit(solution)/shard_map/scores/pallas_call | solution.py:181
  58.8 5.1 %scores.3 = (f32[128,384]{1,0:T(8,128)S(1)}, f32[1,384]{1,0:T(1,128)S(1)}) custom-call(s32[2]{0:T(128)S(1)} %pad_add_fusion.1.place_ref, bf16[96,8192]{1,0:T(8,128)(2,1)} %refs_4_.3, bf16[96,8192]{1,0:T(8,128)(2,1)} %copy-done.2, bf16[96,4096]{1,0:T(8,128)(2,1)S(1)} %copy-done.5, bf16[96,2048]{1,0:T(8,128)(2,1)S(1)} %collective-permute-done.2.refs_3_.refs_7_, ...), custom_call_target="tpu_custom_call" | custom-call | flops 402653184 | bytes 3145728 | tf_op jit(solution)/shard_map/scores/pallas_call | solution.py:181
  70.9 4.2 %sums.2 = (bf16[32,4096]{1,0:T(8,128)(2,1)S(1)}, bf16[32,4096]{1,0:T(8,128)(2,1)S(1)}, bf16[32,4096]{1,0:T(8,128)(2,1)S(1)}, bf16[32,4096]{1,0:T(8,128)(2,1)S(1)}, f32[1,384]{1,0:T(1,128)}) custom-call(s32[2]{0:T(128)S(1)} %pad_add_fusion.1.place_ref, f32[128,384]{1,0:T(8,128)S(1)} %copy-done.18, s32[2,384]{1,0:T(2,128)S(1)} %reshape.29.route_ref, ...), custom_call_target="tpu_custom_call" | custom-call | flops 402653184 | bytes 3145728 | tf_op jit(solution)/shard_map/sums/pallas_call | solution.py:267
  75.8 4.3 %sums.3 = (bf16[32,4096]{1,0:T(8,128)(2,1)S(1)}, bf16[32,4096]{1,0:T(8,128)(2,1)S(1)}, bf16[32,4096]{1,0:T(8,128)(2,1)}, bf16[32,4096]{1,0:T(8,128)(2,1)S(1)}, f32[1,384]{1,0:T(1,128)S(1)}) custom-call(s32[2]{0:T(128)S(1)} %pad_add_fusion.1.place_ref, f32[128,384]{1,0:T(8,128)S(1)} %copy-done.18, s32[2,384]{1,0:T(2,128)S(1)} %reshape.29.route_ref, ...), custom_call_target="tpu_custom_call" | custom-call | flops 402653184 | bytes 3145728 | tf_op jit(solution)/shard_map/sums/pallas_call | solution.py:267
  82.7 3.1 %collective-permute-start.25 = (bf16[32,4096]{1,0:T(8,128)(2,1)}, bf16[32,4096]{1,0:T(8,128)(2,1)S(1)}, u32[]{:S(2)}, u32[]{:S(2)}) collective-permute-start(bf16[32,4096]{1,0:T(8,128)(2,1)} %get-tuple-element.35), channel_id=1, source_target_pairs={{0,4},{4,0},{8,12},{12,8},{1,5},{5,1},{9,13},{13,9},{2,6},{6,2},{1... | collective-permute-start | bytes 786440 | tf_op jit(solution)/shard_map/ppermute | solution.py:33
  85.8 2.0 %collective-permute-start.20 = (bf16[32,4096]{1,0:T(8,128)(2,1)}, bf16[32,4096]{1,0:T(8,128)(2,1)S(1)}, u32[]{:S(2)}, u32[]{:S(2)}) collective-permute-start(bf16[32,4096]{1,0:T(8,128)(2,1)} %copy-done.23), channel_id=1, source_target_pairs={{0,4},{4,0},{8,12},{12,8},{1,5},{5,1},{9,13},{13,9},{2,6},{6,2},{1... | collective-permute-start | bytes 786440 | tf_op jit(solution)/shard_map/ppermute | solution.py:33
  89.1 4.1 %collective-permute-done.25 = bf16[32,4096]{1,0:T(8,128)(2,1)S(1)} collective-permute-done((bf16[32,4096]{1,0:T(8,128)(2,1)}, bf16[32,4096]{1,0:T(8,128)(2,1)S(1)}, u32[]{:S(2)}, u32[]{:S(2)}) %collective-permute-start.25) | collective-permute-done | bytes 262176 | tf_op jit(solution)/shard_map/ppermute | solution.py:33
  95.0 3.8 %collective-permute-done.22 = bf16[32,4096]{1,0:T(8,128)(2,1)S(1)} collective-permute-done((bf16[32,4096]{1,0:T(8,128)(2,1)}, bf16[32,4096]{1,0:T(8,128)(2,1)S(1)}, u32[]{:S(2)}, u32[]{:S(2)}) %collective-permute-start.22) | collective-permute-done | bytes 262176 | tf_op jit(solution)/shard_map/ppermute | solution.py:31
  100.6 3.8 %collective-permute-done.20 = bf16[32,4096]{1,0:T(8,128)(2,1)S(1)} collective-permute-done((bf16[32,4096]{1,0:T(8,128)(2,1)}, bf16[32,4096]{1,0:T(8,128)(2,1)S(1)}, u32[]{:S(2)}, u32[]{:S(2)}) %collective-permute-start.20) | collective-permute-done | bytes 262176 | tf_op jit(solution)/shard_map/ppermute | solution.py:33
  105.1 4.9 %collective-permute-done.17 = bf16[32,4096]{1,0:T(8,128)(2,1)S(1)} collective-permute-done((bf16[32,4096]{1,0:T(8,128)(2,1)}, bf16[32,4096]{1,0:T(8,128)(2,1)S(1)}, u32[]{:S(2)}, u32[]{:S(2)}) %collective-permute-start.17) | collective-permute-done | bytes 262176 | tf_op jit(solution)/shard_map/ppermute | solution.py:31
  111.0 3.4 %collective-permute-start.24 = (bf16[32,4096]{1,0:T(8,128)(2,1)S(1)}, bf16[32,4096]{1,0:T(8,128)(2,1)S(1)}, u32[]{:S(2)}, u32[]{:S(2)}) collective-permute-start(bf16[32,4096]{1,0:T(8,128)(2,1)S(1)} %fusion.1), channel_id=1, source_target_pairs={{0,4},{4,0},{8,12},{12,8},{1,5},{5,1},{9,13},{13,9},{2,6},{6,2},{1... | collective-permute-start | bytes 786440 | tf_op jit(solution)/shard_map/ppermute | solution.py:39
  114.5 8.6 %collective-permute-start.19 = (bf16[32,4096]{1,0:T(8,128)(2,1)S(1)}, bf16[32,4096]{1,0:T(8,128)(2,1)S(1)}, u32[]{:S(2)}, u32[]{:S(2)}) collective-permute-start(bf16[32,4096]{1,0:T(8,128)(2,1)S(1)} %fusion), channel_id=1, source_target_pairs={{0,4},{4,0},{8,12},{12,8},{1,5},{5,1},{9,13},{13,9},{2,6},{6,2},{1... | collective-permute-start | bytes 786440 | tf_op jit(solution)/shard_map/ppermute | solution.py:39
  123.2 5.6 %collective-permute-done.19 = bf16[32,4096]{1,0:T(8,128)(2,1)S(1)} collective-permute-done((bf16[32,4096]{1,0:T(8,128)(2,1)S(1)}, bf16[32,4096]{1,0:T(8,128)(2,1)S(1)}, u32[]{:S(2)}, u32[]{:S(2)}) %collective-permute-start.19) | collective-permute-done | bytes 262176 | tf_op jit(solution)/shard_map/ppermute | solution.py:39
  (125 shorter events, 29.1 us)
Async XLA Ops:
  0.6 15.2 %collective-permute-start.4 = (bf16[32,8192]{1,0:T(8,128)(2,1)}, bf16[32,8192]{1,0:T(8,128)(2,1)S(1)}, u32[]{:S(2)}, u32[]{:S(2)}) collective-permute-start(bf16[32,8192]{1,0:T(8,128)(2,1)} %bitcast.17), channel_id=1, source_target_pairs={{0,4},{4,0},{8,12},{12,8},{1,5},{5,1},{9,13},{13,9},{2,6},{6,2},{1... | collective-permute-start | bytes 1572872 | tf_op jit(solution)/shard_map/ppermute | solution.py:308
  3.7 12.1 %collective-permute-start.5 = (bf16[32,8192]{1,0:T(8,128)(2,1)}, bf16[32,8192]{1,0:T(8,128)(2,1)S(1)}, u32[]{:S(2)}, u32[]{:S(2)}) collective-permute-start(bf16[32,8192]{1,0:T(8,128)(2,1)} %bitcast.18), channel_id=1, source_target_pairs={{4,8},{8,4},{0,0},{12,12},{5,9},{9,5},{1,1},{13,13},{6,10},{10,6},... | collective-permute-start | bytes 1572872 | tf_op jit(solution)/shard_map/ppermute | solution.py:308
  7.0 20.6 %collective-permute-start.9 = (bf16[96,4096]{1,0:T(8,128)(2,1)S(1)}, bf16[96,4096]{1,0:T(8,128)(2,1)}, u32[]{:S(2)}, u32[]{:S(2)}) collective-permute-start(bf16[96,4096]{1,0:T(8,128)(2,1)S(1)} %get-tuple-element.38), channel_id=1, source_target_pairs={{0,2},{1,3},{2,0},{3,1},{4,6},{5,7},{6,4},{7,5},{8,10},{9,11},{10,... | collective-permute-start | bytes 2359304 | tf_op jit(solution)/shard_map/ppermute | solution.py:19
  8.5 34.4 %collective-permute-start.1 = (bf16[96,4096]{1,0:T(8,128)(2,1)S(1)}, bf16[96,4096]{1,0:T(8,128)(2,1)S(1)}, u32[]{:S(2)}, u32[]{:S(2)}) collective-permute-start(bf16[96,4096]{1,0:T(8,128)(2,1)S(1)} %get-tuple-element.39), channel_id=1, source_target_pairs={{0,2},{1,3},{2,0},{3,1},{4,6},{5,7},{6,4},{7,5},{8,10},{9,11},{10,... | collective-permute-start | bytes 2359304 | tf_op jit(solution)/shard_map/ppermute | solution.py:19
  9.0 38.0 %collective-permute-start = (bf16[96,8192]{1,0:T(8,128)(2,1)S(1)}, bf16[96,8192]{1,0:T(8,128)(2,1)S(1)}, u32[]{:S(2)}, u32[]{:S(2)}) collective-permute-start(bf16[96,8192]{1,0:T(8,128)(2,1)S(1)} %copy-done), channel_id=1, source_target_pairs={{0,1},{1,0},{2,3},{3,2},{4,5},{5,4},{6,7},{7,6},{8,9},{9,8},{10,11... | collective-permute-start | bytes 4718600 | tf_op jit(solution)/shard_map/ppermute | solution.py:19
  15.9 15.9 %collective-permute-start.6 = (bf16[32,8192]{1,0:T(8,128)(2,1)S(1)}, bf16[32,8192]{1,0:T(8,128)(2,1)S(1)}, u32[]{:S(2)}, u32[]{:S(2)}) collective-permute-start(bf16[32,8192]{1,0:T(8,128)(2,1)S(1)} %collective-permute-done.5.refs_9_.refs_10_), channel_id=1, source_target_pairs={{0,4},{4,0},{8,12},{12,8},{1,5},{5,1},{9,13},{13,9},{2,6},{6,2},{1... | collective-permute-start | bytes 1572872 | tf_op jit(solution)/shard_map/ppermute | solution.py:311
  20.6 11.2 %collective-permute-start.7 = (bf16[32,8192]{1,0:T(8,128)(2,1)S(1)}, bf16[32,8192]{1,0:T(8,128)(2,1)}, u32[]{:S(2)}, u32[]{:S(2)}) collective-permute-start(bf16[32,8192]{1,0:T(8,128)(2,1)S(1)} %collective-permute-done.4.refs_5_.refs_6_), channel_id=1, source_target_pairs={{4,8},{8,4},{0,0},{12,12},{5,9},{9,5},{1,1},{13,13},{6,10},{10,6},... | collective-permute-start | bytes 1572872 | tf_op jit(solution)/shard_map/ppermute | solution.py:311
  27.6 20.1 %collective-permute-start.10 = (bf16[96,4096]{1,0:T(8,128)(2,1)}, bf16[96,4096]{1,0:T(8,128)(2,1)}, u32[]{:S(2)}, u32[]{:S(2)}) collective-permute-start(bf16[96,4096]{1,0:T(8,128)(2,1)} %collective-permute-done.9.refs_2_.refs_6_), channel_id=1, source_target_pairs={{0,1},{1,0},{2,3},{3,2},{4,5},{5,4},{6,7},{7,6},{8,9},{9,8},{10,11... | collective-permute-start | bytes 2359304 | tf_op jit(solution)/shard_map/ppermute | solution.py:19
  31.8 14.3 %collective-permute-start.8 = (bf16[32,8192]{1,0:T(8,128)(2,1)}, bf16[32,8192]{1,0:T(8,128)(2,1)}, u32[]{:S(2)}, u32[]{:S(2)}) collective-permute-start(bf16[32,8192]{1,0:T(8,128)(2,1)} %collective-permute-done.7.refs_7_.refs_8_), channel_id=1, source_target_pairs={{0,4},{4,0},{8,12},{12,8},{1,5},{5,1},{9,13},{13,9},{2,6},{6,2},{1... | collective-permute-start | bytes 1572872 | tf_op jit(solution)/shard_map/ppermute | solution.py:313
  44.7 14.0 %collective-permute-start.2 = (bf16[96,2048]{1,0:T(8,128)(2,1)}, bf16[96,2048]{1,0:T(8,128)(2,1)S(1)}, u32[]{:S(2)}, u32[]{:S(2)}) collective-permute-start(bf16[96,2048]{1,0:T(8,128)(2,1)} %get-tuple-element.41), channel_id=1, source_target_pairs={{0,1},{1,0},{2,3},{3,2},{4,5},{5,4},{6,7},{7,6},{8,9},{9,8},{10,11... | collective-permute-start | bytes 1179656 | tf_op jit(solution)/shard_map/ppermute | solution.py:19
  44.7 14.0 %collective-permute-start.3 = (bf16[96,2048]{1,0:T(8,128)(2,1)}, bf16[96,2048]{1,0:T(8,128)(2,1)}, u32[]{:S(2)}, u32[]{:S(2)}) collective-permute-start(bf16[96,2048]{1,0:T(8,128)(2,1)} %get-tuple-element.40), channel_id=1, source_target_pairs={{0,1},{1,0},{2,3},{3,2},{4,5},{5,4},{6,7},{7,6},{8,9},{9,8},{10,11... | collective-permute-start | bytes 1179656 | tf_op jit(solution)/shard_map/ppermute | solution.py:19
  46.1 19.9 %collective-permute-start.13 = (s32[2,96]{1,0:T(2,128)S(1)}, s32[2,96]{1,0:T(2,128)S(1)}, u32[]{:S(2)}, u32[]{:S(2)}) collective-permute-start(s32[2,96]{1,0:T(2,128)S(1)} %bitcast.24), channel_id=1, source_target_pairs={{0,3},{1,2},{2,1},{3,0},{4,7},{5,6},{6,5},{7,4},{8,11},{9,10},{10,... | collective-permute-start | bytes 2312 | tf_op jit(solution)/shard_map/ppermute | solution.py:19
  47.1 19.4 %collective-permute-start.12 = (s32[2,96]{1,0:T(2,128)S(1)}, s32[2,96]{1,0:T(2,128)S(1)}, u32[]{:S(2)}, u32[]{:S(2)}) collective-permute-start(s32[2,96]{1,0:T(2,128)S(1)} %bitcast.25), channel_id=1, source_target_pairs={{0,2},{1,3},{2,0},{3,1},{4,6},{5,7},{6,4},{7,5},{8,10},{9,11},{10,... | collective-permute-start | bytes 2312 | tf_op jit(solution)/shard_map/ppermute | solution.py:19
  47.6 18.9 %collective-permute-start.11 = (s32[2,96]{1,0:T(2,128)S(1)}, s32[2,96]{1,0:T(2,128)S(1)}, u32[]{:S(2)}, u32[]{:S(2)}) collective-permute-start(s32[2,96]{1,0:T(2,128)S(1)} %bitcast.26), channel_id=1, source_target_pairs={{0,1},{1,0},{2,3},{3,2},{4,5},{5,4},{6,7},{7,6},{8,9},{9,8},{10,11... | collective-permute-start | bytes 2312 | tf_op jit(solution)/shard_map/ppermute | solution.py:19
  64.6 5.3 %collective-permute-start.14 = (f32[1,384]{1,0:T(1,128)S(1)}, f32[1,384]{1,0:T(1,128)S(1)}, u32[]{:S(2)}, u32[]{:S(2)}) collective-permute-start(f32[1,384]{1,0:T(1,128)S(1)} %get-tuple-element.26.refs_0_), channel_id=1, source_target_pairs={{0,1},{1,0},{2,3},{3,2},{4,5},{5,4},{6,7},{7,6},{8,9},{9,8},{10,11... | collective-permute-start | bytes 4616 | tf_op jit(solution)/shard_map/ppermute | solution.py:19
  82.7 10.4 %collective-permute-start.25 = (bf16[32,4096]{1,0:T(8,128)(2,1)}, bf16[32,4096]{1,0:T(8,128)(2,1)S(1)}, u32[]{:S(2)}, u32[]{:S(2)}) collective-permute-start(bf16[32,4096]{1,0:T(8,128)(2,1)} %get-tuple-element.35), channel_id=1, source_target_pairs={{0,4},{4,0},{8,12},{12,8},{1,5},{5,1},{9,13},{13,9},{2,6},{6,2},{1... | collective-permute-start | bytes 786440 | tf_op jit(solution)/shard_map/ppermute | solution.py:33
  85.8 13.0 %collective-permute-start.22 = (bf16[32,4096]{1,0:T(8,128)(2,1)}, bf16[32,4096]{1,0:T(8,128)(2,1)S(1)}, u32[]{:S(2)}, u32[]{:S(2)}) collective-permute-start(bf16[32,4096]{1,0:T(8,128)(2,1)} %copy-done.27), channel_id=1, source_target_pairs={{0,4},{4,0},{8,12},{12,8},{1,5},{5,1},{9,13},{13,9},{2,6},{6,2},{1... | collective-permute-start | bytes 786440 | tf_op jit(solution)/shard_map/ppermute | solution.py:31
  85.8 18.5 %collective-permute-start.20 = (bf16[32,4096]{1,0:T(8,128)(2,1)}, bf16[32,4096]{1,0:T(8,128)(2,1)S(1)}, u32[]{:S(2)}, u32[]{:S(2)}) collective-permute-start(bf16[32,4096]{1,0:T(8,128)(2,1)} %copy-done.23), channel_id=1, source_target_pairs={{0,4},{4,0},{8,12},{12,8},{1,5},{5,1},{9,13},{13,9},{2,6},{6,2},{1... | collective-permute-start | bytes 786440 | tf_op jit(solution)/shard_map/ppermute | solution.py:33
  87.8 22.2 %collective-permute-start.17 = (bf16[32,4096]{1,0:T(8,128)(2,1)}, bf16[32,4096]{1,0:T(8,128)(2,1)S(1)}, u32[]{:S(2)}, u32[]{:S(2)}) collective-permute-start(bf16[32,4096]{1,0:T(8,128)(2,1)} %copy-done.25), channel_id=1, source_target_pairs={{0,4},{4,0},{8,12},{12,8},{1,5},{5,1},{9,13},{13,9},{2,6},{6,2},{1... | collective-permute-start | bytes 786440 | tf_op jit(solution)/shard_map/ppermute | solution.py:31
  94.2 28.9 %collective-permute-start.26 = (bf16[32,4096]{1,0:T(8,128)(2,1)S(1)}, bf16[32,4096]{1,0:T(8,128)(2,1)S(1)}, u32[]{:S(2)}, u32[]{:S(2)}) collective-permute-start(bf16[32,4096]{1,0:T(8,128)(2,1)S(1)} %add_convert_fusion), channel_id=1, source_target_pairs={{4,8},{8,4},{0,0},{12,12},{5,9},{9,5},{1,1},{13,13},{6,10},{10,6},... | collective-permute-start | bytes 786440 | tf_op jit(solution)/shard_map/ppermute | solution.py:37
  99.8 11.1 %collective-permute-start.23 = (bf16[32,4096]{1,0:T(8,128)(2,1)S(1)}, bf16[32,4096]{1,0:T(8,128)(2,1)S(1)}, u32[]{:S(2)}, u32[]{:S(2)}) collective-permute-start(bf16[32,4096]{1,0:T(8,128)(2,1)S(1)} %add_convert_fusion.2), channel_id=1, source_target_pairs={{4,8},{8,4},{0,0},{12,12},{5,9},{9,5},{1,1},{13,13},{6,10},{10,6},... | collective-permute-start | bytes 786440 | tf_op jit(solution)/shard_map/ppermute | solution.py:36
  104.4 18.8 %collective-permute-start.21 = (bf16[32,4096]{1,0:T(8,128)(2,1)S(1)}, bf16[32,4096]{1,0:T(8,128)(2,1)S(1)}, u32[]{:S(2)}, u32[]{:S(2)}) collective-permute-start(bf16[32,4096]{1,0:T(8,128)(2,1)S(1)} %add_convert_fusion.3), channel_id=1, source_target_pairs={{4,8},{8,4},{0,0},{12,12},{5,9},{9,5},{1,1},{13,13},{6,10},{10,6},... | collective-permute-start | bytes 786440 | tf_op jit(solution)/shard_map/ppermute | solution.py:37
  111.0 12.1 %collective-permute-start.24 = (bf16[32,4096]{1,0:T(8,128)(2,1)S(1)}, bf16[32,4096]{1,0:T(8,128)(2,1)S(1)}, u32[]{:S(2)}, u32[]{:S(2)}) collective-permute-start(bf16[32,4096]{1,0:T(8,128)(2,1)S(1)} %fusion.1), channel_id=1, source_target_pairs={{0,4},{4,0},{8,12},{12,8},{1,5},{5,1},{9,13},{13,9},{2,6},{6,2},{1... | collective-permute-start | bytes 786440 | tf_op jit(solution)/shard_map/ppermute | solution.py:39
  114.5 14.3 %collective-permute-start.19 = (bf16[32,4096]{1,0:T(8,128)(2,1)S(1)}, bf16[32,4096]{1,0:T(8,128)(2,1)S(1)}, u32[]{:S(2)}, u32[]{:S(2)}) collective-permute-start(bf16[32,4096]{1,0:T(8,128)(2,1)S(1)} %fusion), channel_id=1, source_target_pairs={{0,4},{4,0},{8,12},{12,8},{1,5},{5,1},{9,13},{13,9},{2,6},{6,2},{1... | collective-permute-start | bytes 786440 | tf_op jit(solution)/shard_map/ppermute | solution.py:39
  (39 other events, 345.3 us)

commit v4 on v1

v4 whole, which is shorter than its diff:
```python
from functools import partial

import jax
import jax.numpy as jnp
from jax import lax
from jax.experimental import pallas as pl
from jax.experimental.pallas import tpu as pltpu
from jax.sharding import PartitionSpec as P

VMEM_BYTES = 24 * 1024 * 1024
SMEM_SPEC = pl.BlockSpec(memory_space=pltpu.SMEM)
VMEM_SPEC = pl.BlockSpec(memory_space=pltpu.VMEM)
SIDES = [(0, 1), (1, 0), (2, 3), (3, 2)]
MIDDLE = [(1, 2), (2, 1), (0, 0), (3, 3)]


def swap_bits(block, axis, bits):
    return lax.ppermute(block, axis, [(i, i ^ bits) for i in range(lax.axis_size(axis))])


def swap_gather(block, axis, bit):
    held = {0: block}
    while bit:
        for k in list(held):
            held[k ^ bit] = swap_bits(held[k], axis, bit)
        bit //= 2
    return [held[k] for k in range(len(held))]


def add_rounded(one, other):
    return (one.astype(jnp.float32) + other.astype(jnp.float32)).astype(jnp.bfloat16)


def staged_gather(block, images, near_bits, far_bit):
    rows = images.shape[0]
    third = rows // 3
    thirds = [images[i * third : (i + 1) * third] for i in range(3)]
    near = swap_gather(images, "reader", near_bits)
    side = lax.ppermute(block, "blk", SIDES)
    across = lax.ppermute(block, "blk", MIDDLE)
    first = swap_bits(thirds[0], "reader", far_bit)
    side, across, first, thirds[1] = lax.optimization_barrier((side, across, first, thirds[1]))
    far = lax.ppermute(across, "blk", SIDES)
    across_far = lax.ppermute(side, "blk", MIDDLE)
    second = swap_bits(thirds[1], "reader", far_bit)
    firsts = swap_gather(first, "reader", near_bits)
    far, across_far, second, thirds[2], near, firsts = lax.optimization_barrier(
        (far, across_far, second, thirds[2], near, firsts)
    )
    end = lax.ppermute(across_far, "blk", SIDES)
    third = swap_bits(thirds[2], "reader", far_bit)
    seconds = swap_gather(second, "reader", near_bits)
    end, third, seconds = lax.optimization_barrier((end, third, seconds))
    lasts = swap_gather(third, "reader", near_bits)
    line = [[block], [side], [far, across_far], [end, across]]
    return line, [[one] for one in near] + [list(group) for group in zip(firsts, seconds, lasts)]


def plain_gather(block, images, near_bits, far_bit):
    near = swap_gather(images, "reader", near_bits)
    far = swap_gather(swap_bits(images, "reader", far_bit), "reader", near_bits)
    return line_gather(block, "blk"), [[one] for one in near + far]


def line_gather(block, axis):
    size, member = lax.axis_size(axis), lax.axis_index(axis)
    ahead, behind = [block], [block]
    for s in range(1, size):
        ahead.append(lax.ppermute(ahead[-1], axis, [(i, i + 1) for i in range(s - 1, size - 1)]))
        behind.append(lax.ppermute(behind[-1], axis, [(i, i - 1) for i in range(1, size - s + 1)]))
    blocks = [block]
    for s in range(1, size):
        blocks.append(jnp.where(member >= s, ahead[s], behind[size - s]))
    return [[one] for one in blocks]


def pair_scatter(pieces, axis):
    member = lax.axis_index(axis)
    is_end = (member == 0) | (member == 3)
    totals, across_end = [], None
    for parts in pieces:
        for_far_end = lax.ppermute(parts[3], axis, SIDES)
        for_far_middle = lax.ppermute(parts[2], axis, SIDES)
        if across_end is not None:
            for_far_end, for_far_middle, _ = lax.optimization_barrier(
                (for_far_end, for_far_middle, across_end)
            )
        across_end = lax.ppermute(add_rounded(parts[2], for_far_end), axis, MIDDLE)
        across_middle = lax.ppermute(add_rounded(parts[3], for_far_middle), axis, MIDDLE)
        near = jnp.where(is_end, parts[1], add_rounded(parts[1], across_end))
        from_side = lax.ppermute(near, axis, SIDES)
        total = parts[0].astype(jnp.float32) + from_side.astype(jnp.float32)
        totals.append(total + jnp.where(is_end, 0.0, across_middle.astype(jnp.float32)))
    return totals


def line_scatter(pieces, axis):
    return [line_sum(parts, axis) for parts in pieces]


def line_sum(parts, axis):
    size = lax.axis_size(axis)
    up = down = None
    for s in range(1, size):
        send_up, send_down = parts[s], parts[size - s]
        if s > 1:
            send_up = add_rounded(send_up, up)
            send_down = add_rounded(send_down, down)
        up = lax.ppermute(send_up, axis, [(i, i + 1) for i in range(0, s) if i + 1 < size])
        down = lax.ppermute(send_down, axis, [(i, i - 1) for i in range(size - s, size) if i > 0])
    total = parts[0].astype(jnp.float32)
    if size > 1:
        total = total + up.astype(jnp.float32) + down.astype(jnp.float32)
    return total


def column_lse(scores):
    peak = jnp.max(scores, axis=0, keepdims=True)
    total = jnp.sum(jnp.exp(scores - peak), axis=0, keepdims=True)
    return peak + jnp.log(total)


def take_groups(refs, counts):
    return [[refs.pop(0) for _ in range(n)] for n in counts]


def flat(groups):
    return [one for group in groups for one in group]


def score_kernel(counts, piece, first, finish, place_ref, *refs):
    image_counts, pair_counts = counts
    refs = list(refs)
    image_refs = take_groups(refs, image_counts)
    pair_refs = take_groups(refs, pair_counts)
    noise_ref = refs.pop(0)
    extra_ref = refs.pop(0)
    score_ref, all_ref, small_ref, weighted_ref, penalty_ref = refs
    reader = place_ref[0]
    count = pair_refs[0][0].shape[0]
    rows = image_refs[0][0].shape[0]
    width = piece.stop - piece.start

    def columns(ref):
        return ref[:, piece] if ref.shape[1] > width else ref[...]

    for k, group in enumerate(image_refs):
        each = rows // len(group)
        for i, ref in enumerate(group):
            start = pl.multiple_of((reader ^ k) * rows + i * each, each)
            all_ref[pl.ds(start, each), :] = columns(ref)
    noise = columns(noise_ref)

    def weigh(s, ref):
        block = columns(ref).astype(jnp.float32)
        scaled = block * noise
        weighted_ref[s * count : (s + 1) * count, :] = scaled.astype(jnp.bfloat16)
        penalty_ref[s * count : (s + 1) * count, :] = 0.5 * jnp.sum(
            scaled * block, axis=1, keepdims=True
        )

    for s, pair in enumerate(pair_refs):
        if len(pair) == 1:
            weigh(s, pair[0])
            continue

        @pl.when(place_ref[1] == 1)
        def _(s=s, pair=pair):
            weigh(s, pair[0])

        @pl.when(place_ref[1] == 0)
        def _(s=s, pair=pair):
            weigh(s, pair[1])

    scores = lax.dot_general(
        weighted_ref[...],
        all_ref[...],
        (((1,), (1,)), ((), ())),
        preferred_element_type=jnp.float32,
    )
    scores = scores - penalty_ref[...]
    if first:
        routes = extra_ref[...]
        for k in range(small_ref.shape[0]):
            hits = jnp.where(routes == (reader ^ k), 1.0, 0.0)
            small_ref[k : k + 1, :] = jnp.max(hits, axis=0, keepdims=True)
    else:
        scores = scores + extra_ref[...]
    score_ref[...] = scores
    if finish:
        small_ref[...] = column_lse(scores)


def score_piece(place, piece, pairs, images, noise, routes, earlier, finish):
    width = piece.stop - piece.start
    rows = images[0][0].shape[0]
    refs = len(pairs) * pairs[0][0].shape[0]
    slots = len(images) * rows
    first = earlier is None
    operands = [*flat(images), *flat(pairs), noise, routes if first else earlier]
    return pl.pallas_call(
        partial(
            score_kernel,
            ([len(group) for group in images], [len(pair) for pair in pairs]),
            piece,
            first,
            finish,
        ),
        out_shape=(
            jax.ShapeDtypeStruct((refs, slots), jnp.float32),
            jax.ShapeDtypeStruct((slots, width), jnp.bfloat16),
            jax.ShapeDtypeStruct((len(images) if first else 1, slots), jnp.float32),
        ),
        in_specs=[SMEM_SPEC] + [VMEM_SPEC] * len(operands),
        out_specs=(VMEM_SPEC,) * 3,
        scratch_shapes=[
            pltpu.VMEM((refs, width), jnp.bfloat16),
            pltpu.VMEM((refs, 1), jnp.float32),
        ],
        compiler_params=pltpu.CompilerParams(vmem_limit_bytes=VMEM_BYTES),
        cost_estimate=pl.CostEstimate(
            flops=refs * slots * width // 8,
            bytes_accessed=slots * width // 8,
            transcendentals=0,
        ),
        name="scores",
    )(place, *operands)


def lse_kernel(score_ref, lse_ref):
    lse_ref[...] = column_lse(score_ref[...])


def group_lse(scores):
    return pl.pallas_call(
        lse_kernel,
        out_shape=jax.ShapeDtypeStruct((1, scores.shape[1]), jnp.float32),
        name="group_lse",
    )(scores)


def emit_sums(posterior, all_ref, out_refs):
    sums = jnp.dot(posterior, all_ref[...], preferred_element_type=jnp.float32)
    count = sums.shape[0] // len(out_refs)
    for s, out_ref in enumerate(out_refs):
        out_ref[...] = sums[s * count : (s + 1) * count].astype(out_ref.dtype)


def first_sums_kernel(readers, members, score_ref, mask_ref, *refs):
    lse_refs = refs[:readers]
    all_ref = refs[readers]
    out_refs = refs[readers + 1 : readers + 1 + members]
    norm_ref, post_ref = refs[readers + 1 + members :]
    kept = []
    for k in range(readers):
        kept.append(jnp.where(mask_ref[k : k + 1, :] > 0.0, lse_refs[k][...], -jnp.inf))
    highest = kept[0]
    for value in kept[1:]:
        highest = jnp.maximum(highest, value)
    spread = jnp.exp(kept[0] - highest)
    for value in kept[1:]:
        spread = spread + jnp.exp(value - highest)
    norm = highest + jnp.log(spread)
    norm_ref[...] = norm
    exponent = jnp.where(mask_ref[0:1, :] > 0.0, score_ref[...] - norm, -jnp.inf)
    posterior = jnp.exp(exponent).astype(jnp.bfloat16)
    post_ref[...] = posterior
    emit_sums(posterior, all_ref, out_refs)


def later_sums_kernel(post_ref, all_ref, *out_refs):
    emit_sums(post_ref[...], all_ref, out_refs)


def sums_call(kernel, operands, extra, members, all_images, refs):
    slots, width = all_images.shape
    block = jax.ShapeDtypeStruct((refs // members, width), jnp.bfloat16)
    outs = pl.pallas_call(
        kernel,
        out_shape=(block,) * members + tuple(extra),
        in_specs=[VMEM_SPEC] * (len(operands) + 1),
        out_specs=(VMEM_SPEC,) * (members + len(extra)),
        compiler_params=pltpu.CompilerParams(vmem_limit_bytes=VMEM_BYTES),
        cost_estimate=pl.CostEstimate(
            flops=2 * refs * slots * width,
            bytes_accessed=2 * slots * width,
            transcendentals=0,
        ),
        name="sums",
    )(*operands, all_images)
    return outs[:members], outs[members:]


def on_device(images, routes, projections, noise_weights):
    readers = lax.axis_size("reader")
    members = lax.axis_size("blk")
    reader = lax.axis_index("reader")
    member = lax.axis_index("blk")
    is_end = (member == 0) | (member == members - 1)
    place = jnp.stack([reader, is_end.astype(jnp.int32)]).astype(jnp.int32)
    rows, width = images.shape
    noise = noise_weights.reshape(1, width)
    projections = projections[0]
    half = width // 2
    pieces = [slice(0, half), slice(half, width)]
    gather = staged_gather if members == 4 and rows % 48 == 0 else plain_gather
    streams = [
        gather(projections[:, piece], images[:, piece], readers // 4, readers // 2)
        for piece in pieces
    ]

    route_blocks = jnp.stack([routes.T] + [swap_bits(routes.T, "reader", k) for k in range(1, readers)])
    order = jnp.arange(readers, dtype=jnp.int32) ^ reader
    all_routes = route_blocks[order].transpose(1, 0, 2).reshape(routes.shape[1], readers * rows)

    split = lax.axis_size("sub") > 1
    scores, first_images, masks = score_piece(
        place, pieces[0], *streams[0], noise, all_routes, None, False
    )
    scores, last_images, mine = score_piece(
        place, pieces[1], *streams[1], noise, None, scores, not split
    )
    if split:
        scores = lax.psum(scores, "sub")
        mine = group_lse(scores)
    lses = [mine] + [swap_bits(mine, "reader", k) for k in range(1, readers)]
    refs, slots = scores.shape
    first_parts, (norms, posterior) = sums_call(
        partial(first_sums_kernel, readers, members),
        (scores, masks, *lses),
        (
            jax.ShapeDtypeStruct((1, slots), jnp.float32),
            jax.ShapeDtypeStruct((refs, slots), jnp.bfloat16),
        ),
        members,
        first_images,
        refs,
    )
    last_parts, _ = sums_call(later_sums_kernel, (posterior,), (), members, last_images, refs)
    scatter = pair_scatter if members == 4 else line_scatter
    totals = scatter((first_parts, last_parts), "blk")
    normalizer = lax.dynamic_slice(norms.reshape(-1), (reader * rows,), (rows,))
    return (jnp.concatenate(totals, axis=1)[None], normalizer)


def solution(mesh):
    return jax.shard_map(
        on_device,
        mesh=mesh,
        in_specs=(
            P(("parts", "blk", "reader"), "sub"),
            P(("parts", "blk", "reader"), None),
            P(("parts", "reader"), "blk", "sub"),
            P(("parts", "sub")),
        ),
        out_specs=(P(("parts", "reader"), "blk", "sub"), P(("parts", "blk", "reader"))),
        check_vma=False,
    )
```

time: 124 us -> 128 us (1.032)
  waiting for transfers between devices: 33.9 us -> 41 us
  Pallas kernels: 15.4 us -> 8.67 us
  starting transfers between devices: 52.6 us -> 56.9 us
    ppermute x36 -> x40, waiting for transfers between devices: 33.9 us -> 41 us  [the longest x2 14.1 us: pair_scatter(): for_far_middle = lax.ppermute(parts[2], axis, SIDES)]
    pallas_call x6 -> x4, Pallas kernels: 15.4 us -> 8.67 us  [the longest x2 6.51 us: score_piece(): pl.pallas_call(partial(score_kernel, ([len(group) for group in images], [...]
    ppermute x36 -> x40, starting transfers between devices: 52.6 us -> 56.9 us  [the longest x2 18.8 us: pair_scatter(): from_side = lax.ppermute(near, axis, SIDES)]
    unnamed x46 -> x54, local copies, waits for them, and re-layouts: 9.58 us -> 11.9 us
    convert_element_type x6 -> x4, other arithmetic: 3.4 us -> 2.15 us  [add_rounded(): (one.astype(jnp.float32) + other.astype(jnp.float32)).astype(jnp.bfloat16)]
  transfers between devices with their start and end apart: 36 -> 40, of which waited for: 12 -> 16; matrix products, arithmetic and copies ran while one was open for 7% -> 5% of each run, Pallas kernels for 9% -> 3%
where the time goes in v4:
time: 128 us
  starting transfers between devices  56.9 us (44%)
  waiting for transfers between devices  41 us (32%)
  local copies, waits for them, and re-layouts  16.5 us (13%)
  Pallas kernels  8.67 us (7%)
  other arithmetic  3.65 us (3%)
    ppermute x2, starting transfers between devices, pair_scatter(): from_side = lax.ppermute(near, axis, SIDES)  18.8 us
    ppermute x2, waiting for transfers between devices, pair_scatter(): for_far_middle = lax.ppermute(parts[2], axis, SIDES)  14.1 us
    ppermute x20, waiting for transfers between devices, swap_bits(): lax.ppermute(block, axis, [(i, i ^ bits) for i in range(lax.axis_size(axi...  13.5 us
    ppermute x20, starting transfers between devices, swap_bits(): lax.ppermute(block, axis, [(i, i ^ bits) for i in range(lax.axis_size(axi...  12.2 us
    unnamed x54, local copies, waits for them, and re-layouts  11.9 us
    ppermute x2, starting transfers between devices, staged_gather(): side = lax.ppermute(block, 'blk', SIDES)  7.69 us
    pallas_call x2, Pallas kernels, score_piece(): pl.pallas_call(partial(score_kernel, ([len(group) for group in images], [...  6.51 us
    ppermute x2, waiting for transfers between devices, staged_gather(): end = lax.ppermute(across_far, 'blk', SIDES)  4.5 us
  transfers between devices with their start and end apart: 40, of which 16 were waited for; matrix products, arithmetic and copies ran while one was open for 5% of the time, Pallas kernels for 3%

profile of v4, /device:TPU:0, one launch (start us, length us, event | category | flops | bytes accessed | tf_op | source)
XLA Modules:
  0.0 127.7 jit_solution(10258474287128848995)
XLA Ops:
  2.5 5.9 %collective-permute-start.12 = (bf16[32,4096]{1,0:T(8,128)(2,1)S(1)}, bf16[32,4096]{1,0:T(8,128)(2,1)S(1)}, u32[]{:S(2)}, u32[]{:S(2)}) collective-permute-start(bf16[32,4096]{1,0:T(8,128)(2,1)S(1)} %get-tuple-element.110.refs_8_), channel_id=1, source_target_pairs={{0,4},{4,0},{8,12},{12,8},{1,5},{5,1},{9,13},{13,9},{2,6},{6,2},{1... | collective-permute-start | bytes 786440 | tf_op jit(solution)/shard_map/ppermute | solution.py:39
  8.4 2.2 %fusion.4 = (bf16[32,4096]{1,0:T(8,128)(2,1)S(1)}, bf16[32,4096]{1,0:T(8,128)(2,1)S(1)}, bf16[32,4096]{1,0:T(8,128)(2,1)S(1)}, bf16[32,4096]{1,0:T(8,128)(2,1)},...) fusion(bf16[96,8192]{1,0:T(8,128)(2,1)} %param.4), kind=kLoop, calls=%fused_computation.19 | loop fusion | bytes 3145728 | tf_op jit(solution)/shard_map/slice | solution.py:37
  13.0 1.8 %collective-permute-start = (bf16[32,4096]{1,0:T(8,128)(2,1)S(1)}, bf16[32,4096]{1,0:T(8,128)(2,1)S(1)}, u32[]{:S(2)}, u32[]{:S(2)}) collective-permute-start(bf16[32,4096]{1,0:T(8,128)(2,1)S(1)} %get-tuple-element.111.refs_8_), channel_id=1, source_target_pairs={{0,4},{4,0},{8,12},{12,8},{1,5},{5,1},{9,13},{13,9},{2,6},{6,2},{1... | collective-permute-start | bytes 786440 | tf_op jit(solution)/shard_map/ppermute | solution.py:39
  14.8 1.5 %collective-permute-start.2 = (bf16[32,4096]{1,0:T(8,128)(2,1)S(1)}, bf16[32,4096]{1,0:T(8,128)(2,1)S(1)}, u32[]{:S(2)}, u32[]{:S(2)}) collective-permute-start(bf16[32,4096]{1,0:T(8,128)(2,1)S(1)} %get-tuple-element.109), channel_id=1, source_target_pairs={{0,2},{1,3},{2,0},{3,1},{4,6},{5,7},{6,4},{7,5},{8,10},{9,11},{10,... | collective-permute-start | bytes 786440 | tf_op jit(solution)/shard_map/ppermute | solution.py:18
  16.3 2.5 %collective-permute-done.14.refs_2_ = bf16[32,4096]{1,0:T(8,128)(2,1)S(1)} collective-permute-done((bf16[32,4096]{1,0:T(8,128)(2,1)S(1)}, bf16[32,4096]{1,0:T(8,128)(2,1)S(1)}, u32[]{:S(2)}, u32[]{:S(2)}) %collective-permute-start.14) | collective-permute-done | bytes 262176 | tf_op jit(solution)/shard_map/ppermute | solution.py:18
  18.8 2.4 %collective-permute-start.17 = (bf16[32,4096]{1,0:T(8,128)(2,1)S(1)}, bf16[32,4096]{1,0:T(8,128)(2,1)}, u32[]{:S(2)}, u32[]{:S(2)}) collective-permute-start(bf16[32,4096]{1,0:T(8,128)(2,1)S(1)} %get-tuple-element.70), channel_id=1, source_target_pairs={{0,2},{1,3},{2,0},{3,1},{4,6},{5,7},{6,4},{7,5},{8,10},{9,11},{10,... | collective-permute-start | bytes 786440 | tf_op jit(solution)/shard_map/ppermute | solution.py:18
  22.2 1.6 %collective-permute-start.15 = (bf16[32,4096]{1,0:T(8,128)(2,1)S(1)}, bf16[32,4096]{1,0:T(8,128)(2,1)S(1)}, u32[]{:S(2)}, u32[]{:S(2)}) collective-permute-start(bf16[32,4096]{1,0:T(8,128)(2,1)S(1)} %collective-permute-done.13.refs_13_), channel_id=1, source_target_pairs={{0,4},{4,0},{8,12},{12,8},{1,5},{5,1},{9,13},{13,9},{2,6},{6,2},{1... | collective-permute-start | bytes 786440 | tf_op jit(solution)/shard_map/ppermute | solution.py:43
  25.8 3.6 %collective-permute-done.17.refs_3_ = bf16[32,4096]{1,0:T(8,128)(2,1)} collective-permute-done((bf16[32,4096]{1,0:T(8,128)(2,1)S(1)}, bf16[32,4096]{1,0:T(8,128)(2,1)}, u32[]{:S(2)}, u32[]{:S(2)}) %collective-permute-start.17) | collective-permute-done | bytes 262176 | tf_op jit(solution)/shard_map/ppermute | solution.py:18
  32.4 2.3 %collective-permute-start.3 = (bf16[32,4096]{1,0:T(8,128)(2,1)S(1)}, bf16[32,4096]{1,0:T(8,128)(2,1)S(1)}, u32[]{:S(2)}, u32[]{:S(2)}) collective-permute-start(bf16[32,4096]{1,0:T(8,128)(2,1)S(1)} %collective-permute-done.1.refs_13_), channel_id=1, source_target_pairs={{0,4},{4,0},{8,12},{12,8},{1,5},{5,1},{9,13},{13,9},{2,6},{6,2},{1... | collective-permute-start | bytes 786440 | tf_op jit(solution)/shard_map/ppermute | solution.py:43
  43.3 1.5 %collective-permute-start.9 = (bf16[32,4096]{1,0:T(8,128)(2,1)}, bf16[32,4096]{1,0:T(8,128)(2,1)}, u32[]{:S(2)}, u32[]{:S(2)}) collective-permute-start(bf16[32,4096]{1,0:T(8,128)(2,1)} %get-tuple-element.60), channel_id=1, source_target_pairs={{0,2},{1,3},{2,0},{3,1},{4,6},{5,7},{6,4},{7,5},{8,10},{9,11},{10,... | collective-permute-start | bytes 786440 | tf_op jit(solution)/shard_map/ppermute | solution.py:18
  44.8 2.4 %collective-permute-start.8 = (bf16[32,4096]{1,0:T(8,128)(2,1)}, bf16[32,4096]{1,0:T(8,128)(2,1)}, u32[]{:S(2)}, u32[]{:S(2)}) collective-permute-start(bf16[32,4096]{1,0:T(8,128)(2,1)} %collective-permute-done.4.refs_11_), channel_id=1, source_target_pairs={{0,4},{4,0},{8,12},{12,8},{1,5},{5,1},{9,13},{13,9},{2,6},{6,2},{1... | collective-permute-start | bytes 786440 | tf_op jit(solution)/shard_map/ppermute | solution.py:50
  48.4 2.7 %collective-permute-done.20.refs_12_ = bf16[32,4096]{1,0:T(8,128)(2,1)} collective-permute-done((bf16[32,4096]{1,0:T(8,128)(2,1)}, bf16[32,4096]{1,0:T(8,128)(2,1)}, u32[]{:S(2)}, u32[]{:S(2)}) %collective-permute-start.20) | collective-permute-done | bytes 262176 | tf_op jit(solution)/shard_map/ppermute | solution.py:50
  51.2 2.1 %collective-permute-done.9.refs_4_ = bf16[32,4096]{1,0:T(8,128)(2,1)} collective-permute-done((bf16[32,4096]{1,0:T(8,128)(2,1)}, bf16[32,4096]{1,0:T(8,128)(2,1)}, u32[]{:S(2)}, u32[]{:S(2)}) %collective-permute-start.9) | collective-permute-done | bytes 262176 | tf_op jit(solution)/shard_map/ppermute | solution.py:18
  53.6 1.8 %collective-permute-done.8.refs_12_ = bf16[32,4096]{1,0:T(8,128)(2,1)} collective-permute-done((bf16[32,4096]{1,0:T(8,128)(2,1)}, bf16[32,4096]{1,0:T(8,128)(2,1)}, u32[]{:S(2)}, u32[]{:S(2)}) %collective-permute-start.8) | collective-permute-done | bytes 262176 | tf_op jit(solution)/shard_map/ppermute | solution.py:50
  60.2 3.3 %scores.2 = (f32[128,384]{1,0:T(8,128)S(1)}, bf16[384,4096]{1,0:T(8,128)(2,1)S(1)}, f32[4,384]{1,0:T(4,128)S(1)}) custom-call(s32[2]{0:T(128)S(1)} %pad_add_fusion.1.place_ref, bf16[96,4096]{1,0:T(8,128)(2,1)S(1)} %get-tuple-element.72.refs_0_, bf16[96,4096]{1,0:T(8,128)(2,1)S(1)} %collective-permute-done.18.refs_1_, bf16[32,4096]{1,0:T(8,128)(2,1)S(1)} %copy-done.9, ...), custom_call_target="tpu_custom_call" | custom-call | flops 25165824 | bytes 196608 | tf_op jit(solution)/shard_map/scores/pallas_call | solution.py:201
  64.8 3.2 %scores.3 = (f32[128,384]{1,0:T(8,128)S(1)}, bf16[384,4096]{1,0:T(8,128)(2,1)S(1)}, f32[1,384]{1,0:T(1,128)S(1)}) custom-call(s32[2]{0:T(128)S(1)} %pad_add_fusion.1.place_ref, bf16[96,4096]{1,0:T(8,128)(2,1)S(1)} %copy-done.1, bf16[96,4096]{1,0:T(8,128)(2,1)S(1)} %copy-done.3, bf16[32,4096]{1,0:T(8,128)(2,1)S(1)} %copy-done.11, ...), custom_call_target="tpu_custom_call" | custom-call | flops 25165824 | bytes 196608 | tf_op jit(solution)/shard_map/scores/pallas_call | solution.py:201
  68.2 1.6 %collective-permute-start.28 = (f32[1,384]{1,0:T(1,128)S(1)}, f32[1,384]{1,0:T(1,128)S(1)}, u32[]{:S(2)}, u32[]{:S(2)}) collective-permute-start(f32[1,384]{1,0:T(1,128)S(1)} %get-tuple-element.87.refs_0_), channel_id=1, source_target_pairs={{0,2},{1,3},{2,0},{3,1},{4,6},{5,7},{6,4},{7,5},{8,10},{9,11},{10,... | collective-permute-start | bytes 4616 | tf_op jit(solution)/shard_map/ppermute | solution.py:18
  74.6 2.1 %collective-permute-start.30 = (bf16[32,4096]{1,0:T(8,128)(2,1)}, bf16[32,4096]{1,0:T(8,128)(2,1)}, u32[]{:S(2)}, u32[]{:S(2)}) collective-permute-start(bf16[32,4096]{1,0:T(8,128)(2,1)} %get-tuple-element.92), channel_id=1, source_target_pairs={{0,4},{4,0},{8,12},{12,8},{1,5},{5,1},{9,13},{13,9},{2,6},{6,2},{1... | collective-permute-start | bytes 786440 | tf_op jit(solution)/shard_map/ppermute | solution.py:82
  77.6 2.0 %collective-permute-start.35 = (bf16[32,4096]{1,0:T(8,128)(2,1)S(1)}, bf16[32,4096]{1,0:T(8,128)(2,1)S(1)}, u32[]{:S(2)}, u32[]{:S(2)}) collective-permute-start(bf16[32,4096]{1,0:T(8,128)(2,1)S(1)} %get-tuple-element.98), channel_id=1, source_target_pairs={{0,4},{4,0},{8,12},{12,8},{1,5},{5,1},{9,13},{13,9},{2,6},{6,2},{1... | collective-permute-start | bytes 786440 | tf_op jit(solution)/shard_map/ppermute | solution.py:82
  80.3 3.9 %collective-permute-done.30 = bf16[32,4096]{1,0:T(8,128)(2,1)} collective-permute-done((bf16[32,4096]{1,0:T(8,128)(2,1)}, bf16[32,4096]{1,0:T(8,128)(2,1)}, u32[]{:S(2)}, u32[]{:S(2)}) %collective-permute-start.30) | collective-permute-done | bytes 262176 | tf_op jit(solution)/shard_map/ppermute | solution.py:82
  85.9 14.1 %collective-permute-done.33 = bf16[32,4096]{1,0:T(8,128)(2,1)S(1)} collective-permute-done((bf16[32,4096]{1,0:T(8,128)(2,1)S(1)}, bf16[32,4096]{1,0:T(8,128)(2,1)S(1)}, u32[]{:S(2)}, u32[]{:S(2)}) %collective-permute-start.33) | collective-permute-done | bytes 262176 | tf_op jit(solution)/shard_map/ppermute | solution.py:83
  103.3 7.8 %collective-permute-start.32 = (bf16[32,4096]{1,0:T(8,128)(2,1)S(1)}, bf16[32,4096]{1,0:T(8,128)(2,1)S(1)}, u32[]{:S(2)}, u32[]{:S(2)}) collective-permute-start(bf16[32,4096]{1,0:T(8,128)(2,1)S(1)} %fusion), channel_id=1, source_target_pairs={{0,4},{4,0},{8,12},{12,8},{1,5},{5,1},{9,13},{13,9},{2,6},{6,2},{1... | collective-permute-start | bytes 786440 | tf_op jit(solution)/shard_map/ppermute | solution.py:91
  111.3 10.9 %collective-permute-start.38 = (bf16[32,4096]{1,0:T(8,128)(2,1)S(1)}, bf16[32,4096]{1,0:T(8,128)(2,1)S(1)}, u32[]{:S(2)}, u32[]{:S(2)}) collective-permute-start(bf16[32,4096]{1,0:T(8,128)(2,1)S(1)} %fusion.1), channel_id=1, source_target_pairs={{0,4},{4,0},{8,12},{12,8},{1,5},{5,1},{9,13},{13,9},{2,6},{6,2},{1... | collective-permute-start | bytes 786440 | tf_op jit(solution)/shard_map/ppermute | solution.py:91
  122.3 4.2 %collective-permute-done.38 = bf16[32,4096]{1,0:T(8,128)(2,1)S(1)} collective-permute-done((bf16[32,4096]{1,0:T(8,128)(2,1)S(1)}, bf16[32,4096]{1,0:T(8,128)(2,1)S(1)}, u32[]{:S(2)}, u32[]{:S(2)}) %collective-permute-start.38) | collective-permute-done | bytes 262176 | tf_op jit(solution)/shard_map/ppermute | solution.py:91
  (134 shorter events, 39.1 us)
Async XLA Ops:
  1.7 11.3 %collective-permute-start.13 = (bf16[32,4096]{1,0:T(8,128)(2,1)S(1)}, bf16[32,4096]{1,0:T(8,128)(2,1)S(1)}, u32[]{:S(2)}, u32[]{:S(2)}) collective-permute-start(bf16[32,4096]{1,0:T(8,128)(2,1)S(1)} %get-tuple-element.110.refs_8_), channel_id=1, source_target_pairs={{4,8},{8,4},{0,0},{12,12},{5,9},{9,5},{1,1},{13,13},{6,10},{10,6},... | collective-permute-start | bytes 786440 | tf_op jit(solution)/shard_map/ppermute | solution.py:40
  2.5 12.3 %collective-permute-start.12 = (bf16[32,4096]{1,0:T(8,128)(2,1)S(1)}, bf16[32,4096]{1,0:T(8,128)(2,1)S(1)}, u32[]{:S(2)}, u32[]{:S(2)}) collective-permute-start(bf16[32,4096]{1,0:T(8,128)(2,1)S(1)} %get-tuple-element.110.refs_8_), channel_id=1, source_target_pairs={{0,4},{4,0},{8,12},{12,8},{1,5},{5,1},{9,13},{13,9},{2,6},{6,2},{1... | collective-permute-start | bytes 786440 | tf_op jit(solution)/shard_map/ppermute | solution.py:39
  12.2 25.8 %collective-permute-start.18 = (bf16[96,4096]{1,0:T(8,128)(2,1)S(1)}, bf16[96,4096]{1,0:T(8,128)(2,1)S(1)}, u32[]{:S(2)}, u32[]{:S(2)}) collective-permute-start(bf16[96,4096]{1,0:T(8,128)(2,1)S(1)} %get-tuple-element.72.refs_0_), channel_id=1, source_target_pairs={{0,1},{1,0},{2,3},{3,2},{4,5},{5,4},{6,7},{7,6},{8,9},{9,8},{10,11... | collective-permute-start | bytes 2359304 | tf_op jit(solution)/shard_map/ppermute | solution.py:18
  12.3 9.0 %collective-permute-start.1 = (bf16[32,4096]{1,0:T(8,128)(2,1)S(1)}, bf16[32,4096]{1,0:T(8,128)(2,1)S(1)}, u32[]{:S(2)}, u32[]{:S(2)}) collective-permute-start(bf16[32,4096]{1,0:T(8,128)(2,1)S(1)} %get-tuple-element.111.refs_8_), channel_id=1, source_target_pairs={{4,8},{8,4},{0,0},{12,12},{5,9},{9,5},{1,1},{13,13},{6,10},{10,6},... | collective-permute-start | bytes 786440 | tf_op jit(solution)/shard_map/ppermute | solution.py:40
  13.0 9.2 %collective-permute-start = (bf16[32,4096]{1,0:T(8,128)(2,1)S(1)}, bf16[32,4096]{1,0:T(8,128)(2,1)S(1)}, u32[]{:S(2)}, u32[]{:S(2)}) collective-permute-start(bf16[32,4096]{1,0:T(8,128)(2,1)S(1)} %get-tuple-element.111.refs_8_), channel_id=1, source_target_pairs={{0,4},{4,0},{8,12},{12,8},{1,5},{5,1},{9,13},{13,9},{2,6},{6,2},{1... | collective-permute-start | bytes 786440 | tf_op jit(solution)/shard_map/ppermute | solution.py:39
  14.8 9.6 %collective-permute-start.2 = (bf16[32,4096]{1,0:T(8,128)(2,1)S(1)}, bf16[32,4096]{1,0:T(8,128)(2,1)S(1)}, u32[]{:S(2)}, u32[]{:S(2)}) collective-permute-start(bf16[32,4096]{1,0:T(8,128)(2,1)S(1)} %get-tuple-element.109), channel_id=1, source_target_pairs={{0,2},{1,3},{2,0},{3,1},{4,6},{5,7},{6,4},{7,5},{8,10},{9,11},{10,... | collective-permute-start | bytes 786440 | tf_op jit(solution)/shard_map/ppermute | solution.py:18
  18.8 10.6 %collective-permute-start.17 = (bf16[32,4096]{1,0:T(8,128)(2,1)S(1)}, bf16[32,4096]{1,0:T(8,128)(2,1)}, u32[]{:S(2)}, u32[]{:S(2)}) collective-permute-start(bf16[32,4096]{1,0:T(8,128)(2,1)S(1)} %get-tuple-element.70), channel_id=1, source_target_pairs={{0,2},{1,3},{2,0},{3,1},{4,6},{5,7},{6,4},{7,5},{8,10},{9,11},{10,... | collective-permute-start | bytes 786440 | tf_op jit(solution)/shard_map/ppermute | solution.py:18
  21.3 22.1 %collective-permute-start.6 = (bf16[96,4096]{1,0:T(8,128)(2,1)S(1)}, bf16[96,4096]{1,0:T(8,128)(2,1)S(1)}, u32[]{:S(2)}, u32[]{:S(2)}) collective-permute-start(bf16[96,4096]{1,0:T(8,128)(2,1)S(1)} %get-tuple-element.56.refs_0_), channel_id=1, source_target_pairs={{0,1},{1,0},{2,3},{3,2},{4,5},{5,4},{6,7},{7,6},{8,9},{9,8},{10,11... | collective-permute-start | bytes 2359304 | tf_op jit(solution)/shard_map/ppermute | solution.py:18
  22.2 8.7 %collective-permute-start.15 = (bf16[32,4096]{1,0:T(8,128)(2,1)S(1)}, bf16[32,4096]{1,0:T(8,128)(2,1)S(1)}, u32[]{:S(2)}, u32[]{:S(2)}) collective-permute-start(bf16[32,4096]{1,0:T(8,128)(2,1)S(1)} %collective-permute-done.13.refs_13_), channel_id=1, source_target_pairs={{0,4},{4,0},{8,12},{12,8},{1,5},{5,1},{9,13},{13,9},{2,6},{6,2},{1... | collective-permute-start | bytes 786440 | tf_op jit(solution)/shard_map/ppermute | solution.py:43
  32.4 8.8 %collective-permute-start.3 = (bf16[32,4096]{1,0:T(8,128)(2,1)S(1)}, bf16[32,4096]{1,0:T(8,128)(2,1)S(1)}, u32[]{:S(2)}, u32[]{:S(2)}) collective-permute-start(bf16[32,4096]{1,0:T(8,128)(2,1)S(1)} %collective-permute-done.1.refs_13_), channel_id=1, source_target_pairs={{0,4},{4,0},{8,12},{12,8},{1,5},{5,1},{9,13},{13,9},{2,6},{6,2},{1... | collective-permute-start | bytes 786440 | tf_op jit(solution)/shard_map/ppermute | solution.py:43
  39.7 8.7 %collective-permute-start.21 = (bf16[32,4096]{1,0:T(8,128)(2,1)S(1)}, bf16[32,4096]{1,0:T(8,128)(2,1)}, u32[]{:S(2)}, u32[]{:S(2)}) collective-permute-start(bf16[32,4096]{1,0:T(8,128)(2,1)S(1)} %get-tuple-element.76), channel_id=1, source_target_pairs={{0,2},{1,3},{2,0},{3,1},{4,6},{5,7},{6,4},{7,5},{8,10},{9,11},{10,... | collective-permute-start | bytes 786440 | tf_op jit(solution)/shard_map/ppermute | solution.py:18
  41.9 9.2 %collective-permute-start.20 = (bf16[32,4096]{1,0:T(8,128)(2,1)}, bf16[32,4096]{1,0:T(8,128)(2,1)}, u32[]{:S(2)}, u32[]{:S(2)}) collective-permute-start(bf16[32,4096]{1,0:T(8,128)(2,1)} %collective-permute-done.16.refs_11_), channel_id=1, source_target_pairs={{0,4},{4,0},{8,12},{12,8},{1,5},{5,1},{9,13},{13,9},{2,6},{6,2},{1... | collective-permute-start | bytes 786440 | tf_op jit(solution)/shard_map/ppermute | solution.py:50
  43.3 9.9 %collective-permute-start.9 = (bf16[32,4096]{1,0:T(8,128)(2,1)}, bf16[32,4096]{1,0:T(8,128)(2,1)}, u32[]{:S(2)}, u32[]{:S(2)}) collective-permute-start(bf16[32,4096]{1,0:T(8,128)(2,1)} %get-tuple-element.60), channel_id=1, source_target_pairs={{0,2},{1,3},{2,0},{3,1},{4,6},{5,7},{6,4},{7,5},{8,10},{9,11},{10,... | collective-permute-start | bytes 786440 | tf_op jit(solution)/shard_map/ppermute | solution.py:18
  44.8 10.6 %collective-permute-start.8 = (bf16[32,4096]{1,0:T(8,128)(2,1)}, bf16[32,4096]{1,0:T(8,128)(2,1)}, u32[]{:S(2)}, u32[]{:S(2)}) collective-permute-start(bf16[32,4096]{1,0:T(8,128)(2,1)} %collective-permute-done.4.refs_11_), channel_id=1, source_target_pairs={{0,4},{4,0},{8,12},{12,8},{1,5},{5,1},{9,13},{13,9},{2,6},{6,2},{1... | collective-permute-start | bytes 786440 | tf_op jit(solution)/shard_map/ppermute | solution.py:50
  74.6 9.6 %collective-permute-start.30 = (bf16[32,4096]{1,0:T(8,128)(2,1)}, bf16[32,4096]{1,0:T(8,128)(2,1)}, u32[]{:S(2)}, u32[]{:S(2)}) collective-permute-start(bf16[32,4096]{1,0:T(8,128)(2,1)} %get-tuple-element.92), channel_id=1, source_target_pairs={{0,4},{4,0},{8,12},{12,8},{1,5},{5,1},{9,13},{13,9},{2,6},{6,2},{1... | collective-permute-start | bytes 786440 | tf_op jit(solution)/shard_map/ppermute | solution.py:82
  77.5 24.2 %collective-permute-start.36 = (bf16[32,4096]{1,0:T(8,128)(2,1)S(1)}, bf16[32,4096]{1,0:T(8,128)(2,1)S(1)}, u32[]{:S(2)}, u32[]{:S(2)}) collective-permute-start(bf16[32,4096]{1,0:T(8,128)(2,1)S(1)} %get-tuple-element.97), channel_id=1, source_target_pairs={{0,4},{4,0},{8,12},{12,8},{1,5},{5,1},{9,13},{13,9},{2,6},{6,2},{1... | collective-permute-start | bytes 786440 | tf_op jit(solution)/shard_map/ppermute | solution.py:83
  77.6 24.1 %collective-permute-start.35 = (bf16[32,4096]{1,0:T(8,128)(2,1)S(1)}, bf16[32,4096]{1,0:T(8,128)(2,1)S(1)}, u32[]{:S(2)}, u32[]{:S(2)}) collective-permute-start(bf16[32,4096]{1,0:T(8,128)(2,1)S(1)} %get-tuple-element.98), channel_id=1, source_target_pairs={{0,4},{4,0},{8,12},{12,8},{1,5},{5,1},{9,13},{13,9},{2,6},{6,2},{1... | collective-permute-start | bytes 786440 | tf_op jit(solution)/shard_map/ppermute | solution.py:82
  79.6 20.4 %collective-permute-start.33 = (bf16[32,4096]{1,0:T(8,128)(2,1)S(1)}, bf16[32,4096]{1,0:T(8,128)(2,1)S(1)}, u32[]{:S(2)}, u32[]{:S(2)}) collective-permute-start(bf16[32,4096]{1,0:T(8,128)(2,1)S(1)} %copy-done.21), channel_id=1, source_target_pairs={{0,4},{4,0},{8,12},{12,8},{1,5},{5,1},{9,13},{13,9},{2,6},{6,2},{1... | collective-permute-start | bytes 786440 | tf_op jit(solution)/shard_map/ppermute | solution.py:83
  85.2 16.5 %collective-permute-start.31 = (bf16[32,4096]{1,0:T(8,128)(2,1)S(1)}, bf16[32,4096]{1,0:T(8,128)(2,1)S(1)}, u32[]{:S(2)}, u32[]{:S(2)}) collective-permute-start(bf16[32,4096]{1,0:T(8,128)(2,1)S(1)} %add_convert_fusion.5), channel_id=1, source_target_pairs={{4,8},{8,4},{0,0},{12,12},{5,9},{9,5},{1,1},{13,13},{6,10},{10,6},... | collective-permute-start | bytes 786440 | tf_op jit(solution)/shard_map/ppermute | solution.py:88
  101.0 21.2 %collective-permute-start.34 = (bf16[32,4096]{1,0:T(8,128)(2,1)S(1)}, bf16[32,4096]{1,0:T(8,128)(2,1)S(1)}, u32[]{:S(2)}, u32[]{:S(2)}) collective-permute-start(bf16[32,4096]{1,0:T(8,128)(2,1)S(1)} %add_convert_fusion.3), channel_id=1, source_target_pairs={{4,8},{8,4},{0,0},{12,12},{5,9},{9,5},{1,1},{13,13},{6,10},{10,6},... | collective-permute-start | bytes 786440 | tf_op jit(solution)/shard_map/ppermute | solution.py:89
  101.9 20.4 %collective-permute-start.39 = (bf16[32,4096]{1,0:T(8,128)(2,1)S(1)}, bf16[32,4096]{1,0:T(8,128)(2,1)S(1)}, u32[]{:S(2)}, u32[]{:S(2)}) collective-permute-start(bf16[32,4096]{1,0:T(8,128)(2,1)S(1)} %add_convert_fusion), channel_id=1, source_target_pairs={{4,8},{8,4},{0,0},{12,12},{5,9},{9,5},{1,1},{13,13},{6,10},{10,6},... | collective-permute-start | bytes 786440 | tf_op jit(solution)/shard_map/ppermute | solution.py:89
  102.6 8.6 %collective-permute-start.37 = (bf16[32,4096]{1,0:T(8,128)(2,1)S(1)}, bf16[32,4096]{1,0:T(8,128)(2,1)S(1)}, u32[]{:S(2)}, u32[]{:S(2)}) collective-permute-start(bf16[32,4096]{1,0:T(8,128)(2,1)S(1)} %add_convert_fusion.2), channel_id=1, source_target_pairs={{4,8},{8,4},{0,0},{12,12},{5,9},{9,5},{1,1},{13,13},{6,10},{10,6},... | collective-permute-start | bytes 786440 | tf_op jit(solution)/shard_map/ppermute | solution.py:88
  103.3 18.9 %collective-permute-start.32 = (bf16[32,4096]{1,0:T(8,128)(2,1)S(1)}, bf16[32,4096]{1,0:T(8,128)(2,1)S(1)}, u32[]{:S(2)}, u32[]{:S(2)}) collective-permute-start(bf16[32,4096]{1,0:T(8,128)(2,1)S(1)} %fusion), channel_id=1, source_target_pairs={{0,4},{4,0},{8,12},{12,8},{1,5},{5,1},{9,13},{13,9},{2,6},{6,2},{1... | collective-permute-start | bytes 786440 | tf_op jit(solution)/shard_map/ppermute | solution.py:91
  111.3 15.3 %collective-permute-start.38 = (bf16[32,4096]{1,0:T(8,128)(2,1)S(1)}, bf16[32,4096]{1,0:T(8,128)(2,1)S(1)}, u32[]{:S(2)}, u32[]{:S(2)}) collective-permute-start(bf16[32,4096]{1,0:T(8,128)(2,1)S(1)} %fusion.1), channel_id=1, source_target_pairs={{0,4},{4,0},{8,12},{12,8},{1,5},{5,1},{9,13},{13,9},{2,6},{6,2},{1... | collective-permute-start | bytes 786440 | tf_op jit(solution)/shard_map/ppermute | solution.py:91
  (43 other events, 264.2 us)

commit v5 on v4

v5 whole, which is shorter than its diff:
```python
from functools import partial

import jax
import jax.numpy as jnp
from jax import lax
from jax.experimental import pallas as pl
from jax.experimental.pallas import tpu as pltpu
from jax.sharding import PartitionSpec as P

VMEM_BYTES = 56 * 1024 * 1024
CHUNK = 2048
PARTS = 4
SMEM_SPEC = pl.BlockSpec(memory_space=pltpu.SMEM)
VMEM_SPEC = pl.BlockSpec(memory_space=pltpu.VMEM)
ANY_SPEC = pl.BlockSpec(memory_space=pl.ANY)
SIDES = [(0, 1), (1, 0), (2, 3), (3, 2)]
MIDDLE = [(1, 2), (2, 1), (0, 0), (3, 3)]


def swap_bits(block, axis, bits):
    return lax.ppermute(block, axis, [(i, i ^ bits) for i in range(lax.axis_size(axis))])


def swap_gather(block, axis, bit):
    held = {0: block}
    while bit:
        for k in list(held):
            held[k ^ bit] = swap_bits(held[k], axis, bit)
        bit //= 2
    return [held[k] for k in range(len(held))]


def add_rounded(one, other):
    return (one.astype(jnp.float32) + other.astype(jnp.float32)).astype(jnp.bfloat16)


def staged_gather(block, images, routes, near_bits, far_bit):
    near = swap_gather(images, "reader", near_bits)
    crossed = swap_bits(images, "reader", far_bit)
    side = lax.ppermute(block, "blk", SIDES)
    across = lax.ppermute(block, "blk", MIDDLE)
    side, across = lax.optimization_barrier((side, across))
    far = lax.ppermute(across, "blk", SIDES)
    across_far = lax.ppermute(side, "blk", MIDDLE)
    far, across_far, routes, near = lax.optimization_barrier((far, across_far, routes, near))
    end = lax.ppermute(across_far, "blk", SIDES)
    line = [[block], [side], [far, across_far], [end, across]]
    crossed, _ = lax.optimization_barrier((crossed, across_far))
    step = images.shape[1] // PARTS
    parts = [
        swap_gather(crossed[:, i * step : (i + 1) * step], "reader", near_bits)
        for i in range(PARTS)
    ]
    far_blocks = [[crossed]] + [list(group) for group in list(zip(*parts))[1:]]
    return line, [[one] for one in near] + far_blocks, routes


def plain_gather(block, images, routes, near_bits, far_bit):
    near = swap_gather(images, "reader", near_bits)
    far = swap_gather(swap_bits(images, "reader", far_bit), "reader", near_bits)
    return line_gather(block, "blk"), [[one] for one in near + far], routes


def line_gather(block, axis):
    size, member = lax.axis_size(axis), lax.axis_index(axis)
    ahead, behind = [block], [block]
    for s in range(1, size):
        ahead.append(lax.ppermute(ahead[-1], axis, [(i, i + 1) for i in range(s - 1, size - 1)]))
        behind.append(lax.ppermute(behind[-1], axis, [(i, i - 1) for i in range(1, size - s + 1)]))
    blocks = [block]
    for s in range(1, size):
        blocks.append(jnp.where(member >= s, ahead[s], behind[size - s]))
    return [[one] for one in blocks]


def pair_scatter(pieces, axis):
    member = lax.axis_index(axis)
    is_end = (member == 0) | (member == 3)
    totals, across_end = [], None
    for parts in pieces:
        for_far_end = lax.ppermute(parts[3], axis, SIDES)
        for_far_middle = lax.ppermute(parts[2], axis, SIDES)
        if across_end is not None:
            for_far_end, for_far_middle, _ = lax.optimization_barrier(
                (for_far_end, for_far_middle, across_end)
            )
        across_end = lax.ppermute(add_rounded(parts[2], for_far_end), axis, MIDDLE)
        across_middle = lax.ppermute(add_rounded(parts[3], for_far_middle), axis, MIDDLE)
        near = jnp.where(is_end, parts[1], add_rounded(parts[1], across_end))
        from_side = lax.ppermute(near, axis, SIDES)
        total = parts[0].astype(jnp.float32) + from_side.astype(jnp.float32)
        totals.append(total + jnp.where(is_end, 0.0, across_middle.astype(jnp.float32)))
    return totals


def line_scatter(pieces, axis):
    return [line_sum(parts, axis) for parts in pieces]


def line_sum(parts, axis):
    size = lax.axis_size(axis)
    up = down = None
    for s in range(1, size):
        send_up, send_down = parts[s], parts[size - s]
        if s > 1:
            send_up = add_rounded(send_up, up)
            send_down = add_rounded(send_down, down)
        up = lax.ppermute(send_up, axis, [(i, i + 1) for i in range(0, s) if i + 1 < size])
        down = lax.ppermute(send_down, axis, [(i, i - 1) for i in range(size - s, size) if i > 0])
    total = parts[0].astype(jnp.float32)
    if size > 1:
        total = total + up.astype(jnp.float32) + down.astype(jnp.float32)
    return total


def column_lse(scores):
    peak = jnp.max(scores, axis=0, keepdims=True)
    total = jnp.sum(jnp.exp(scores - peak), axis=0, keepdims=True)
    return peak + jnp.log(total)


def take_groups(refs, counts):
    return [[refs.pop(0) for _ in range(n)] for n in counts]


def flat(groups):
    return [one for group in groups for one in group]


def copy_images(reader, groups, all_ref, sems, piece, chunk):
    rows = groups[0][0].shape[0]
    copies = []
    for c, start in enumerate(range(piece.start, piece.stop, chunk)):
        chunk_copies = []
        for k, group in enumerate(groups):
            each = group[0].shape[1]
            ref, offset = group[start // each], start % each
            row = pl.multiple_of((reader ^ k) * rows, 16)
            chunk_copies.append(
                pltpu.make_async_copy(
                    ref.at[:, pl.ds(offset, chunk)],
                    all_ref.at[pl.ds(row, rows), pl.ds(start - piece.start, chunk)],
                    sems.at[c, k],
                )
            )
        copies.append(chunk_copies)
    return copies


def score_kernel(counts, chunk, finish, place_ref, *refs):
    image_counts, pair_counts = counts
    refs = list(refs)
    image_refs = take_groups(refs, image_counts)
    pair_refs = take_groups(refs, pair_counts)
    noise_ref, route_ref, score_ref, mask_ref, lse_ref = refs[:5]
    all_ref, line_ref, weighted_ref, image_sems, line_sems = refs[5:]
    reader, is_end = place_ref[0], place_ref[1] == 1
    count, width = pair_refs[0][0].shape
    copies = copy_images(reader, image_refs, all_ref, image_sems, slice(0, width), chunk)

    def line_copy(s, ref, c):
        columns = pl.ds(c * chunk, chunk)
        return pltpu.make_async_copy(
            ref.at[:, columns],
            line_ref.at[pl.ds(s * count, count), columns],
            line_sems.at[c, s],
        )

    for c in range(width // chunk):
        for s, pair in enumerate(pair_refs):
            if len(pair) == 1:
                line_copy(s, pair[0], c).start()
                continue

            @pl.when(is_end)
            def _(s=s, pair=pair, c=c):
                line_copy(s, pair[0], c).start()

            @pl.when(jnp.logical_not(is_end))
            def _(s=s, pair=pair, c=c):
                line_copy(s, pair[1], c).start()

        for copy in copies[c]:
            copy.start()
    routes = route_ref[...]
    for k in range(mask_ref.shape[0]):
        hits = jnp.where(routes == (reader ^ k), 1.0, 0.0)
        mask_ref[k : k + 1, :] = jnp.max(hits, axis=0, keepdims=True)
    scores = jnp.zeros(score_ref.shape, jnp.float32)
    penalty = jnp.zeros((score_ref.shape[0], 1), jnp.float32)
    for c in range(width // chunk):
        columns = slice(c * chunk, (c + 1) * chunk)
        for s, pair in enumerate(pair_refs):
            line_copy(s, pair[0], c).wait()
        block = line_ref[:, columns].astype(jnp.float32)
        scaled = block * noise_ref[:, columns]
        weighted_ref[...] = scaled.astype(jnp.bfloat16)
        penalty = penalty + 0.5 * jnp.sum(scaled * block, axis=1, keepdims=True)
        for copy in copies[c]:
            copy.wait()
        scores = scores + lax.dot_general(
            weighted_ref[...],
            all_ref[:, columns],
            (((1,), (1,)), ((), ())),
            preferred_element_type=jnp.float32,
        )
    scores = scores - penalty
    score_ref[...] = scores
    if finish:
        lse_ref[...] = column_lse(scores)


def all_scores(place, pairs, images, noise, routes, finish):
    count, width = pairs[0][0].shape
    chunk = min(CHUNK, width // PARTS)
    refs = len(pairs) * count
    slots = routes.shape[1]
    moved = [*flat(images), *flat(pairs)]
    return pl.pallas_call(
        partial(
            score_kernel,
            ([len(group) for group in images], [len(pair) for pair in pairs]),
            chunk,
            finish,
        ),
        out_shape=(
            jax.ShapeDtypeStruct((refs, slots), jnp.float32),
            jax.ShapeDtypeStruct((len(images), slots), jnp.float32),
            jax.ShapeDtypeStruct((1, slots), jnp.float32),
        ),
        in_specs=[SMEM_SPEC] + [ANY_SPEC] * len(moved) + [VMEM_SPEC] * 2,
        out_specs=(VMEM_SPEC,) * 3,
        scratch_shapes=[
            pltpu.VMEM((slots, width), jnp.bfloat16),
            pltpu.VMEM((refs, width), jnp.bfloat16),
            pltpu.VMEM((refs, chunk), jnp.bfloat16),
            pltpu.SemaphoreType.DMA((width // chunk, len(images))),
            pltpu.SemaphoreType.DMA((width // chunk, len(pairs))),
        ],
        compiler_params=pltpu.CompilerParams(vmem_limit_bytes=VMEM_BYTES),
        cost_estimate=pl.CostEstimate(
            flops=2 * refs * slots * width,
            bytes_accessed=2 * (slots + refs) * width,
            transcendentals=0,
        ),
        name="scores",
    )(place, *moved, noise, routes)


def lse_kernel(score_ref, lse_ref):
    lse_ref[...] = column_lse(score_ref[...])


def group_lse(scores):
    return pl.pallas_call(
        lse_kernel,
        out_shape=jax.ShapeDtypeStruct((1, scores.shape[1]), jnp.float32),
        name="group_lse",
    )(scores)


def sums_kernel(parts, members, piece, chunk, first, place_ref, *refs):
    refs = list(refs)
    image_refs = take_groups(refs, parts)
    if first:
        score_ref, mask_ref, *lse_refs = [refs.pop(0) for _ in range(2 + len(parts))]
    else:
        post_ref = refs.pop(0)
    out_refs = [refs.pop(0) for _ in range(members)]
    if first:
        norm_ref, post_ref = refs.pop(0), refs.pop(0)
    all_ref, sems = refs
    copies = copy_images(place_ref[0], image_refs, all_ref, sems, piece, chunk)
    for chunk_copies in copies:
        for copy in chunk_copies:
            copy.start()
    if first:
        kept = []
        for k, lse_ref in enumerate(lse_refs):
            kept.append(jnp.where(mask_ref[k : k + 1, :] > 0.0, lse_ref[...], -jnp.inf))
        highest = kept[0]
        for value in kept[1:]:
            highest = jnp.maximum(highest, value)
        spread = jnp.exp(kept[0] - highest)
        for value in kept[1:]:
            spread = spread + jnp.exp(value - highest)
        norm = highest + jnp.log(spread)
        norm_ref[...] = norm
        exponent = jnp.where(mask_ref[0:1, :] > 0.0, score_ref[...] - norm, -jnp.inf)
        post_ref[...] = jnp.exp(exponent).astype(jnp.bfloat16)
    posterior = post_ref[...]
    count = posterior.shape[0] // members
    for c, chunk_copies in enumerate(copies):
        columns = slice(c * chunk, (c + 1) * chunk)
        for copy in chunk_copies:
            copy.wait()
        sums = jnp.dot(posterior, all_ref[:, columns], preferred_element_type=jnp.float32)
        for s, out_ref in enumerate(out_refs):
            out_ref[:, columns] = sums[s * count : (s + 1) * count].astype(out_ref.dtype)


def group_sums(place, piece, images, members, operands, first):
    refs, slots = operands[0].shape
    width = piece.stop - piece.start
    chunk = min(CHUNK, images[0][0].shape[1] // PARTS) // 2
    moved = flat(images)
    block = jax.ShapeDtypeStruct((refs // members, width), jnp.bfloat16)
    extra = (
        jax.ShapeDtypeStruct((1, slots), jnp.float32),
        jax.ShapeDtypeStruct((refs, slots), jnp.bfloat16),
    )
    extra = extra if first else ()
    outs = pl.pallas_call(
        partial(sums_kernel, [len(group) for group in images], members, piece, chunk, first),
        out_shape=(block,) * members + extra,
        in_specs=[SMEM_SPEC] + [ANY_SPEC] * len(moved) + [VMEM_SPEC] * len(operands),
        out_specs=(VMEM_SPEC,) * (members + len(extra)),
        scratch_shapes=[
            pltpu.VMEM((slots, width), jnp.bfloat16),
            pltpu.SemaphoreType.DMA((width // chunk, len(images))),
        ],
        compiler_params=pltpu.CompilerParams(vmem_limit_bytes=VMEM_BYTES),
        cost_estimate=pl.CostEstimate(
            flops=2 * refs * slots * width,
            bytes_accessed=2 * slots * width,
            transcendentals=0,
        ),
        name="sums",
    )(place, *moved, *operands)
    return outs[:members], outs[members:]


def on_device(images, routes, projections, noise_weights):
    readers = lax.axis_size("reader")
    members = lax.axis_size("blk")
    reader = lax.axis_index("reader")
    member = lax.axis_index("blk")
    is_end = (member == 0) | (member == members - 1)
    place = jnp.stack([reader, is_end.astype(jnp.int32)]).astype(jnp.int32)
    rows, width = images.shape
    noise = noise_weights.reshape(1, width)

    route_blocks = jnp.stack([routes.T] + [swap_bits(routes.T, "reader", k) for k in range(1, readers)])
    order = jnp.arange(readers, dtype=jnp.int32) ^ reader
    all_routes = route_blocks[order].transpose(1, 0, 2).reshape(routes.shape[1], readers * rows)
    gather = staged_gather if members == 4 and rows % 32 == 0 else plain_gather
    line, blocks, all_routes = gather(
        projections[0], images, all_routes, readers // 4, readers // 2
    )

    split = lax.axis_size("sub") > 1
    scores, masks, mine = all_scores(place, line, blocks, noise, all_routes, not split)
    if split:
        scores = lax.psum(scores, "sub")
        mine = group_lse(scores)
    lses = [mine] + [swap_bits(mine, "reader", k) for k in range(1, readers)]
    half = width // 2
    first_parts, (norms, posterior) = group_sums(
        place, slice(0, half), blocks, members, (scores, masks, *lses), True
    )
    last_parts, _ = group_sums(place, slice(half, width), blocks, members, (posterior,), False)
    scatter = pair_scatter if members == 4 else line_scatter
    totals = scatter((first_parts, last_parts), "blk")
    normalizer = lax.dynamic_slice(norms.reshape(-1), (reader * rows,), (rows,))
    return (jnp.concatenate(totals, axis=1)[None], normalizer)


def solution(mesh):
    return jax.shard_map(
        on_device,
        mesh=mesh,
        in_specs=(
            P(("parts", "blk", "reader"), "sub"),
            P(("parts", "blk", "reader"), None),
            P(("parts", "reader"), "blk", "sub"),
            P(("parts", "sub")),
        ),
        out_specs=(P(("parts", "reader"), "blk", "sub"), P(("parts", "blk", "reader"))),
        check_vma=False,
    )
```

time: 128 us -> 121 us (0.945)
  local copies, waits for them, and re-layouts: 16.5 us -> 4.58 us
  Pallas kernels: 8.67 us -> 16.2 us
  starting transfers between devices: 56.9 us -> 50.9 us
  waiting for transfers between devices: 41 us -> 44.4 us
    unnamed x54 -> x34, local copies, waits for them, and re-layouts: 11.9 us -> 0.96 us
    pallas_call x4 -> x3, Pallas kernels: 8.67 us -> 16.2 us  [the longest x2 9.09 us: group_sums(): pl.pallas_call(partial(sums_kernel, [len(group) for group in images], mem...]
    ppermute x2 -> x1, waiting for transfers between devices: 0.01 us -> 7.38 us  [staged_gather(): side = lax.ppermute(block, 'blk', SIDES)]
    ppermute x2 -> x1, starting transfers between devices: 7.69 us -> 1.58 us  [staged_gather(): side = lax.ppermute(block, 'blk', SIDES)]
    ppermute x2, waiting for transfers between devices: 14.1 us -> 8.09 us  [pair_scatter(): for_far_middle = lax.ppermute(parts[2], axis, SIDES)]
    ppermute x20 -> x12, starting transfers between devices: 12.2 us -> 7.55 us  [swap_bits(): lax.ppermute(block, axis, [(i, i ^ bits) for i in range(lax.axis_size(axi...]
    ppermute x2, waiting for transfers between devices: 3.94 us -> 0.01 us  [pair_scatter(): for_far_end = lax.ppermute(parts[3], axis, SIDES)]
    ppermute x2 -> x1, starting transfers between devices: 1.49 us -> 5.35 us  [staged_gather(): across = lax.ppermute(block, 'blk', MIDDLE)]
  transfers between devices with their start and end apart: 40 -> 27, of which waited for: 16 -> 13; matrix products, arithmetic and copies ran while one was open for 5% -> 4% of each run, Pallas kernels for 3% -> 4%
where the time goes in v5:
time: 121 us; the launch traced here: 120 us
  starting transfers between devices  50.9 us (42%)
  waiting for transfers between devices  44.4 us (37%)
  Pallas kernels  16.2 us (13%)
  local copies, waits for them, and re-layouts  4.58 us (4%)
  other arithmetic  2.91 us (2%)
    ppermute x2, starting transfers between devices, pair_scatter(): from_side = lax.ppermute(near, axis, SIDES)  17.5 us
    ppermute x12, waiting for transfers between devices, swap_bits(): lax.ppermute(block, axis, [(i, i ^ bits) for i in range(lax.axis_size(axi...  17.3 us
    pallas_call x2, Pallas kernels, group_sums(): pl.pallas_call(partial(sums_kernel, [len(group) for group in images], mem...  9.09 us
    ppermute x2, waiting for transfers between devices, pair_scatter(): for_far_middle = lax.ppermute(parts[2], axis, SIDES)  8.09 us
    ppermute x12, starting transfers between devices, swap_bits(): lax.ppermute(block, axis, [(i, i ^ bits) for i in range(lax.axis_size(axi...  7.55 us
    ppermute x1, waiting for transfers between devices, staged_gather(): side = lax.ppermute(block, 'blk', SIDES)  7.38 us
    ppermute x1, waiting for transfers between devices, staged_gather(): end = lax.ppermute(across_far, 'blk', SIDES)  7.36 us
    pallas_call x1, Pallas kernels, all_scores(): pl.pallas_call(partial(score_kernel, ([len(group) for group in images], [...  7.07 us
  transfers between devices with their start and end apart: 27, of which 13 were waited for; matrix products, arithmetic and copies ran while one was open for 4% of the time, Pallas kernels for 4%

profile of v5, /device:TPU:0, one launch (start us, length us, event | category | flops | bytes accessed | tf_op | source)
XLA Modules:
  0.0 119.9 jit_solution(16400643997550660314)
XLA Ops:
  1.1 2.6 %collective-permute-start.8 = (bf16[96,8192]{1,0:T(8,128)(2,1)}, bf16[96,8192]{1,0:T(8,128)(2,1)S(1)}, u32[]{:S(2)}, u32[]{:S(2)}) collective-permute-start(bf16[96,8192]{1,0:T(8,128)(2,1)} %refs_0_.2), channel_id=1, source_target_pairs={{0,2},{1,3},{2,0},{3,1},{4,6},{5,7},{6,4},{7,5},{8,10},{9,11},{10,... | collective-permute-start | bytes 4718600 | tf_op jit(solution)/shard_map/ppermute | solution.py:21
  3.7 1.6 %collective-permute-start = (bf16[32,8192]{1,0:T(8,128)(2,1)}, bf16[32,8192]{1,0:T(8,128)(2,1)}, u32[]{:S(2)}, u32[]{:S(2)}) collective-permute-start(bf16[32,8192]{1,0:T(8,128)(2,1)} %bitcast.17), channel_id=1, source_target_pairs={{0,4},{4,0},{8,12},{12,8},{1,5},{5,1},{9,13},{13,9},{2,6},{6,2},{1... | collective-permute-start | bytes 1572872 | tf_op jit(solution)/shard_map/ppermute | solution.py:40
  5.3 5.3 %collective-permute-start.1 = (bf16[32,8192]{1,0:T(8,128)(2,1)}, bf16[32,8192]{1,0:T(8,128)(2,1)}, u32[]{:S(2)}, u32[]{:S(2)}) collective-permute-start(bf16[32,8192]{1,0:T(8,128)(2,1)} %bitcast.18), channel_id=1, source_target_pairs={{4,8},{8,4},{0,0},{12,12},{5,9},{9,5},{1,1},{13,13},{6,10},{10,6},... | collective-permute-start | bytes 1572872 | tf_op jit(solution)/shard_map/ppermute | solution.py:41
  10.6 7.4 %collective-permute-done.refs_8_ = bf16[32,8192]{1,0:T(8,128)(2,1)} collective-permute-done((bf16[32,8192]{1,0:T(8,128)(2,1)}, bf16[32,8192]{1,0:T(8,128)(2,1)}, u32[]{:S(2)}, u32[]{:S(2)}) %collective-permute-start) | collective-permute-done | bytes 524320 | tf_op jit(solution)/shard_map/ppermute | solution.py:40
  18.0 4.6 %collective-permute-start.2 = (bf16[32,8192]{1,0:T(8,128)(2,1)}, bf16[32,8192]{1,0:T(8,128)(2,1)}, u32[]{:S(2)}, u32[]{:S(2)}) collective-permute-start(bf16[32,8192]{1,0:T(8,128)(2,1)} %collective-permute-done.1.refs_12_), channel_id=1, source_target_pairs={{0,4},{4,0},{8,12},{12,8},{1,5},{5,1},{9,13},{13,9},{2,6},{6,2},{1... | collective-permute-start | bytes 1572872 | tf_op jit(solution)/shard_map/ppermute | solution.py:43
  22.6 5.3 %collective-permute-start.3 = (bf16[32,8192]{1,0:T(8,128)(2,1)}, bf16[32,8192]{1,0:T(8,128)(2,1)}, u32[]{:S(2)}, u32[]{:S(2)}) collective-permute-start(bf16[32,8192]{1,0:T(8,128)(2,1)} %collective-permute-done.refs_8_), channel_id=1, source_target_pairs={{4,8},{8,4},{0,0},{12,12},{5,9},{9,5},{1,1},{13,13},{6,10},{10,6},... | collective-permute-start | bytes 1572872 | tf_op jit(solution)/shard_map/ppermute | solution.py:44
  28.0 1.3 %collective-permute-done.4 = s32[2,96]{1,0:T(2,128)S(1)} collective-permute-done((s32[2,96]{1,0:T(2,128)}, s32[2,96]{1,0:T(2,128)S(1)}, u32[]{:S(2)}, u32[]{:S(2)}) %collective-permute-start.4) | collective-permute-done | bytes 800 | tf_op jit(solution)/shard_map/ppermute | solution.py:21
  29.9 9.1 %collective-permute-done.5 = s32[2,96]{1,0:T(2,128)S(1)} collective-permute-done((s32[2,96]{1,0:T(2,128)}, s32[2,96]{1,0:T(2,128)S(1)}, u32[]{:S(2)}, u32[]{:S(2)}) %collective-permute-start.5) | collective-permute-done | bytes 800 | tf_op jit(solution)/shard_map/ppermute | solution.py:21
  40.0 2.2 %collective-permute-done.6 = s32[2,96]{1,0:T(2,128)S(1)} collective-permute-done((s32[2,96]{1,0:T(2,128)}, s32[2,96]{1,0:T(2,128)S(1)}, u32[]{:S(2)}, u32[]{:S(2)}) %collective-permute-start.6) | collective-permute-done | bytes 800 | tf_op jit(solution)/shard_map/ppermute | solution.py:21
  44.1 1.9 %collective-permute-start.13 = (bf16[32,8192]{1,0:T(8,128)(2,1)}, bf16[32,8192]{1,0:T(8,128)(2,1)}, u32[]{:S(2)}, u32[]{:S(2)}) collective-permute-start(bf16[32,8192]{1,0:T(8,128)(2,1)} %collective-permute-done.3.refs_10_), channel_id=1, source_target_pairs={{0,4},{4,0},{8,12},{12,8},{1,5},{5,1},{9,13},{13,9},{2,6},{6,2},{1... | collective-permute-start | bytes 1572872 | tf_op jit(solution)/shard_map/ppermute | solution.py:46
  51.2 7.4 %collective-permute-done.13.refs_11_ = bf16[32,8192]{1,0:T(8,128)(2,1)} collective-permute-done((bf16[32,8192]{1,0:T(8,128)(2,1)}, bf16[32,8192]{1,0:T(8,128)(2,1)}, u32[]{:S(2)}, u32[]{:S(2)}) %collective-permute-start.13) | collective-permute-done | bytes 524320 | tf_op jit(solution)/shard_map/ppermute | solution.py:46
  58.6 7.1 %scores.1 = (f32[128,384]{1,0:T(8,128)}, f32[4,384]{1,0:T(4,128)}, f32[1,384]{1,0:T(1,128)}) custom-call(s32[2]{0:T(128)} %pad_add_fusion.1.place_ref, bf16[96,8192]{1,0:T(8,128)(2,1)} %refs_0_.2, bf16[96,8192]{1,0:T(8,128)(2,1)} %copy-done.1, bf16[96,8192]{1,0:T(8,128)(2,1)} %copy-done, bf16[96,2048]{1,0:T(8,128)(2,1)} %copy-done.5, ...), custom_call_target="tpu_custom_call" | custom-call | flops 805306368 | bytes 8388608 | tf_op jit(solution)/shard_map/scores/pallas_call | solution.py:219
  65.7 1.2 %collective-permute-start.15 = (f32[1,384]{1,0:T(1,128)}, f32[1,384]{1,0:T(1,128)S(1)}, u32[]{:S(2)}, u32[]{:S(2)}) collective-permute-start(f32[1,384]{1,0:T(1,128)} %get-tuple-element.35.refs_9_), channel_id=1, source_target_pairs={{0,2},{1,3},{2,0},{3,1},{4,6},{5,7},{6,4},{7,5},{8,10},{9,11},{10,... | collective-permute-start | bytes 4616 | tf_op jit(solution)/shard_map/ppermute | solution.py:21
  67.6 2.0 %collective-permute-done.15.refs_11_ = f32[1,384]{1,0:T(1,128)S(1)} collective-permute-done((f32[1,384]{1,0:T(1,128)}, f32[1,384]{1,0:T(1,128)S(1)}, u32[]{:S(2)}, u32[]{:S(2)}) %collective-permute-start.15) | collective-permute-done | bytes 1568 | tf_op jit(solution)/shard_map/ppermute | solution.py:21
  70.7 4.5 %sums.2 = (bf16[32,4096]{1,0:T(8,128)(2,1)}, bf16[32,4096]{1,0:T(8,128)(2,1)}, bf16[32,4096]{1,0:T(8,128)(2,1)}, bf16[32,4096]{1,0:T(8,128)(2,1)}, f32[1,384]{1,0:T(1,128)}, /*index=5*/bf16[128,384]{1,0:T(8,128)(2,1)}) custom-call(s32[2]{0:T(128)} %pad_add_fusion.1.place_ref, bf16[96,8192]{1,0:T(8,128)(2,1)} %refs_0_.2, bf16[96,8192]{1,0:T(8,128)(2,1)} %copy-done.1, ...), custom_call_target="tpu_custom_call" | custom-call | flops 402653184 | bytes 3145728 | tf_op jit(solution)/shard_map/sums/pallas_call | solution.py:313
  75.2 1.6 %collective-permute-start.17 = (bf16[32,4096]{1,0:T(8,128)(2,1)}, bf16[32,4096]{1,0:T(8,128)(2,1)S(1)}, u32[]{:S(2)}, u32[]{:S(2)}) collective-permute-start(bf16[32,4096]{1,0:T(8,128)(2,1)} %get-tuple-element.39), channel_id=1, source_target_pairs={{0,4},{4,0},{8,12},{12,8},{1,5},{5,1},{9,13},{13,9},{2,6},{6,2},{1... | collective-permute-start | bytes 786440 | tf_op jit(solution)/shard_map/ppermute | solution.py:81
  77.3 4.6 %sums.3 = (bf16[32,4096]{1,0:T(8,128)(2,1)}, bf16[32,4096]{1,0:T(8,128)(2,1)}, bf16[32,4096]{1,0:T(8,128)(2,1)}, bf16[32,4096]{1,0:T(8,128)(2,1)}) custom-call(s32[2]{0:T(128)} %pad_add_fusion.1.place_ref, bf16[96,8192]{1,0:T(8,128)(2,1)} %refs_0_.2, bf16[96,8192]{1,0:T(8,128)(2,1)} %copy-done.1, bf16[96,8192]{1,0:T(8,128)(2,1)} %copy-done, ...), custom_call_target="tpu_custom_call" | custom-call | flops 402653184 | bytes 3145728 | tf_op jit(solution)/shard_map/sums/pallas_call | solution.py:313
  81.9 1.6 %collective-permute-start.22 = (bf16[32,4096]{1,0:T(8,128)(2,1)}, bf16[32,4096]{1,0:T(8,128)(2,1)S(1)}, u32[]{:S(2)}, u32[]{:S(2)}) collective-permute-start(bf16[32,4096]{1,0:T(8,128)(2,1)} %get-tuple-element.44), channel_id=1, source_target_pairs={{0,4},{4,0},{8,12},{12,8},{1,5},{5,1},{9,13},{13,9},{2,6},{6,2},{1... | collective-permute-start | bytes 786440 | tf_op jit(solution)/shard_map/ppermute | solution.py:81
  84.0 1.3 %dynamic-slice_bitcast_fusion = f32[96]{0:T(128)} fusion(f32[1,384]{1,0:T(1,128)} %get-tuple-element.47, s32[]{:T(128)S(6)} %select_n.41), kind=kLoop, calls=%fused_computation.17 | loop fusion | bytes 772 | tf_op jit(solution)/shard_map/dynamic_slice | solution.py:364
  86.2 4.1 %collective-permute-done.20 = bf16[32,4096]{1,0:T(8,128)(2,1)S(1)} collective-permute-done((bf16[32,4096]{1,0:T(8,128)(2,1)}, bf16[32,4096]{1,0:T(8,128)(2,1)S(1)}, u32[]{:S(2)}, u32[]{:S(2)}) %collective-permute-start.20) | collective-permute-done | bytes 262176 | tf_op jit(solution)/shard_map/ppermute | solution.py:82
  91.1 6.4 %collective-permute-start.19 = (bf16[32,4096]{1,0:T(8,128)(2,1)S(1)}, bf16[32,4096]{1,0:T(8,128)(2,1)S(1)}, u32[]{:S(2)}, u32[]{:S(2)}) collective-permute-start(bf16[32,4096]{1,0:T(8,128)(2,1)S(1)} %fusion), channel_id=1, source_target_pairs={{0,4},{4,0},{8,12},{12,8},{1,5},{5,1},{9,13},{13,9},{2,6},{6,2},{1... | collective-permute-start | bytes 786440 | tf_op jit(solution)/shard_map/ppermute | solution.py:90
  97.5 4.0 %collective-permute-done.23 = bf16[32,4096]{1,0:T(8,128)(2,1)S(1)} collective-permute-done((bf16[32,4096]{1,0:T(8,128)(2,1)}, bf16[32,4096]{1,0:T(8,128)(2,1)S(1)}, u32[]{:S(2)}, u32[]{:S(2)}) %collective-permute-start.23) | collective-permute-done | bytes 262176 | tf_op jit(solution)/shard_map/ppermute | solution.py:82
  103.3 11.1 %collective-permute-start.25 = (bf16[32,4096]{1,0:T(8,128)(2,1)S(1)}, bf16[32,4096]{1,0:T(8,128)(2,1)S(1)}, u32[]{:S(2)}, u32[]{:S(2)}) collective-permute-start(bf16[32,4096]{1,0:T(8,128)(2,1)S(1)} %fusion.1), channel_id=1, source_target_pairs={{0,4},{4,0},{8,12},{12,8},{1,5},{5,1},{9,13},{13,9},{2,6},{6,2},{1... | collective-permute-start | bytes 786440 | tf_op jit(solution)/shard_map/ppermute | solution.py:90
  114.5 4.2 %collective-permute-done.25 = bf16[32,4096]{1,0:T(8,128)(2,1)S(1)} collective-permute-done((bf16[32,4096]{1,0:T(8,128)(2,1)S(1)}, bf16[32,4096]{1,0:T(8,128)(2,1)S(1)}, u32[]{:S(2)}, u32[]{:S(2)}) %collective-permute-start.25) | collective-permute-done | bytes 262176 | tf_op jit(solution)/shard_map/ppermute | solution.py:90
  (85 shorter events, 16.6 us)
Async XLA Ops:
  0.6 43.5 %collective-permute-start.7 = (bf16[96,8192]{1,0:T(8,128)(2,1)}, bf16[96,8192]{1,0:T(8,128)(2,1)S(1)}, u32[]{:S(2)}, u32[]{:S(2)}) collective-permute-start(bf16[96,8192]{1,0:T(8,128)(2,1)} %refs_0_.2), channel_id=1, source_target_pairs={{0,1},{1,0},{2,3},{3,2},{4,5},{5,4},{6,7},{7,6},{8,9},{9,8},{10,11... | collective-permute-start | bytes 4718600 | tf_op jit(solution)/shard_map/ppermute | solution.py:21
  1.1 44.9 %collective-permute-start.8 = (bf16[96,8192]{1,0:T(8,128)(2,1)}, bf16[96,8192]{1,0:T(8,128)(2,1)S(1)}, u32[]{:S(2)}, u32[]{:S(2)}) collective-permute-start(bf16[96,8192]{1,0:T(8,128)(2,1)} %refs_0_.2), channel_id=1, source_target_pairs={{0,2},{1,3},{2,0},{3,1},{4,6},{5,7},{6,4},{7,5},{8,10},{9,11},{10,... | collective-permute-start | bytes 4718600 | tf_op jit(solution)/shard_map/ppermute | solution.py:21
  3.7 14.3 %collective-permute-start = (bf16[32,8192]{1,0:T(8,128)(2,1)}, bf16[32,8192]{1,0:T(8,128)(2,1)}, u32[]{:S(2)}, u32[]{:S(2)}) collective-permute-start(bf16[32,8192]{1,0:T(8,128)(2,1)} %bitcast.17), channel_id=1, source_target_pairs={{0,4},{4,0},{8,12},{12,8},{1,5},{5,1},{9,13},{13,9},{2,6},{6,2},{1... | collective-permute-start | bytes 1572872 | tf_op jit(solution)/shard_map/ppermute | solution.py:40
  5.3 12.7 %collective-permute-start.1 = (bf16[32,8192]{1,0:T(8,128)(2,1)}, bf16[32,8192]{1,0:T(8,128)(2,1)}, u32[]{:S(2)}, u32[]{:S(2)}) collective-permute-start(bf16[32,8192]{1,0:T(8,128)(2,1)} %bitcast.18), channel_id=1, source_target_pairs={{4,8},{8,4},{0,0},{12,12},{5,9},{9,5},{1,1},{13,13},{6,10},{10,6},... | collective-permute-start | bytes 1572872 | tf_op jit(solution)/shard_map/ppermute | solution.py:41
  18.0 26.1 %collective-permute-start.2 = (bf16[32,8192]{1,0:T(8,128)(2,1)}, bf16[32,8192]{1,0:T(8,128)(2,1)}, u32[]{:S(2)}, u32[]{:S(2)}) collective-permute-start(bf16[32,8192]{1,0:T(8,128)(2,1)} %collective-permute-done.1.refs_12_), channel_id=1, source_target_pairs={{0,4},{4,0},{8,12},{12,8},{1,5},{5,1},{9,13},{13,9},{2,6},{6,2},{1... | collective-permute-start | bytes 1572872 | tf_op jit(solution)/shard_map/ppermute | solution.py:43
  22.6 21.5 %collective-permute-start.3 = (bf16[32,8192]{1,0:T(8,128)(2,1)}, bf16[32,8192]{1,0:T(8,128)(2,1)}, u32[]{:S(2)}, u32[]{:S(2)}) collective-permute-start(bf16[32,8192]{1,0:T(8,128)(2,1)} %collective-permute-done.refs_8_), channel_id=1, source_target_pairs={{4,8},{8,4},{0,0},{12,12},{5,9},{9,5},{1,1},{13,13},{6,10},{10,6},... | collective-permute-start | bytes 1572872 | tf_op jit(solution)/shard_map/ppermute | solution.py:44
  29.3 9.6 %collective-permute-start.5 = (s32[2,96]{1,0:T(2,128)}, s32[2,96]{1,0:T(2,128)S(1)}, u32[]{:S(2)}, u32[]{:S(2)}) collective-permute-start(s32[2,96]{1,0:T(2,128)} %bitcast.23), channel_id=1, source_target_pairs={{0,2},{1,3},{2,0},{3,1},{4,6},{5,7},{6,4},{7,5},{8,10},{9,11},{10,... | collective-permute-start | bytes 2312 | tf_op jit(solution)/shard_map/ppermute | solution.py:21
  39.0 3.2 %collective-permute-start.6 = (s32[2,96]{1,0:T(2,128)}, s32[2,96]{1,0:T(2,128)S(1)}, u32[]{:S(2)}, u32[]{:S(2)}) collective-permute-start(s32[2,96]{1,0:T(2,128)} %bitcast.24), channel_id=1, source_target_pairs={{0,3},{1,2},{2,1},{3,0},{4,7},{5,6},{6,5},{7,4},{8,11},{9,10},{10,... | collective-permute-start | bytes 2312 | tf_op jit(solution)/shard_map/ppermute | solution.py:21
  44.1 14.4 %collective-permute-start.13 = (bf16[32,8192]{1,0:T(8,128)(2,1)}, bf16[32,8192]{1,0:T(8,128)(2,1)}, u32[]{:S(2)}, u32[]{:S(2)}) collective-permute-start(bf16[32,8192]{1,0:T(8,128)(2,1)} %collective-permute-done.3.refs_10_), channel_id=1, source_target_pairs={{0,4},{4,0},{8,12},{12,8},{1,5},{5,1},{9,13},{13,9},{2,6},{6,2},{1... | collective-permute-start | bytes 1572872 | tf_op jit(solution)/shard_map/ppermute | solution.py:46
  47.6 3.1 %collective-permute-start.11 = (bf16[96,2048]{1,0:T(8,128)(2,1)}, bf16[96,2048]{1,0:T(8,128)(2,1)S(1)}, u32[]{:S(2)}, u32[]{:S(2)}) collective-permute-start(bf16[96,2048]{1,0:T(8,128)(2,1)} %get-tuple-element.49), channel_id=1, source_target_pairs={{0,1},{1,0},{2,3},{3,2},{4,5},{5,4},{6,7},{7,6},{8,9},{9,8},{10,11... | collective-permute-start | bytes 1179656 | tf_op jit(solution)/shard_map/ppermute | solution.py:21
  48.1 3.1 %collective-permute-start.12 = (bf16[96,2048]{1,0:T(8,128)(2,1)}, bf16[96,2048]{1,0:T(8,128)(2,1)S(1)}, u32[]{:S(2)}, u32[]{:S(2)}) collective-permute-start(bf16[96,2048]{1,0:T(8,128)(2,1)} %get-tuple-element.48), channel_id=1, source_target_pairs={{0,1},{1,0},{2,3},{3,2},{4,5},{5,4},{6,7},{7,6},{8,9},{9,8},{10,11... | collective-permute-start | bytes 1179656 | tf_op jit(solution)/shard_map/ppermute | solution.py:21
  48.1 3.1 %collective-permute-start.9 = (bf16[96,2048]{1,0:T(8,128)(2,1)S(1)}, bf16[96,2048]{1,0:T(8,128)(2,1)S(1)}, u32[]{:S(2)}, u32[]{:S(2)}) collective-permute-start(bf16[96,2048]{1,0:T(8,128)(2,1)S(1)} %get-tuple-element.51), channel_id=1, source_target_pairs={{0,1},{1,0},{2,3},{3,2},{4,5},{5,4},{6,7},{7,6},{8,9},{9,8},{10,11... | collective-permute-start | bytes 1179656 | tf_op jit(solution)/shard_map/ppermute | solution.py:21
  65.6 1.9 %collective-permute-start.14 = (f32[1,384]{1,0:T(1,128)}, f32[1,384]{1,0:T(1,128)S(1)}, u32[]{:S(2)}, u32[]{:S(2)}) collective-permute-start(f32[1,384]{1,0:T(1,128)} %get-tuple-element.35.refs_9_), channel_id=1, source_target_pairs={{0,1},{1,0},{2,3},{3,2},{4,5},{5,4},{6,7},{7,6},{8,9},{9,8},{10,11... | collective-permute-start | bytes 4616 | tf_op jit(solution)/shard_map/ppermute | solution.py:21
  65.7 3.9 %collective-permute-start.15 = (f32[1,384]{1,0:T(1,128)}, f32[1,384]{1,0:T(1,128)S(1)}, u32[]{:S(2)}, u32[]{:S(2)}) collective-permute-start(f32[1,384]{1,0:T(1,128)} %get-tuple-element.35.refs_9_), channel_id=1, source_target_pairs={{0,2},{1,3},{2,0},{3,1},{4,6},{5,7},{6,4},{7,5},{8,10},{9,11},{10,... | collective-permute-start | bytes 4616 | tf_op jit(solution)/shard_map/ppermute | solution.py:21
  67.0 3.2 %collective-permute-start.16 = (f32[1,384]{1,0:T(1,128)}, f32[1,384]{1,0:T(1,128)S(1)}, u32[]{:S(2)}, u32[]{:S(2)}) collective-permute-start(f32[1,384]{1,0:T(1,128)} %get-tuple-element.35.refs_9_), channel_id=1, source_target_pairs={{0,3},{1,2},{2,1},{3,0},{4,7},{5,6},{6,5},{7,4},{8,11},{9,10},{10,... | collective-permute-start | bytes 4616 | tf_op jit(solution)/shard_map/ppermute | solution.py:21
  75.2 10.0 %collective-permute-start.17 = (bf16[32,4096]{1,0:T(8,128)(2,1)}, bf16[32,4096]{1,0:T(8,128)(2,1)S(1)}, u32[]{:S(2)}, u32[]{:S(2)}) collective-permute-start(bf16[32,4096]{1,0:T(8,128)(2,1)} %get-tuple-element.39), channel_id=1, source_target_pairs={{0,4},{4,0},{8,12},{12,8},{1,5},{5,1},{9,13},{13,9},{2,6},{6,2},{1... | collective-permute-start | bytes 786440 | tf_op jit(solution)/shard_map/ppermute | solution.py:81
  76.8 13.4 %collective-permute-start.20 = (bf16[32,4096]{1,0:T(8,128)(2,1)}, bf16[32,4096]{1,0:T(8,128)(2,1)S(1)}, u32[]{:S(2)}, u32[]{:S(2)}) collective-permute-start(bf16[32,4096]{1,0:T(8,128)(2,1)} %get-tuple-element.38), channel_id=1, source_target_pairs={{0,4},{4,0},{8,12},{12,8},{1,5},{5,1},{9,13},{13,9},{2,6},{6,2},{1... | collective-permute-start | bytes 786440 | tf_op jit(solution)/shard_map/ppermute | solution.py:82
  81.9 15.6 %collective-permute-start.22 = (bf16[32,4096]{1,0:T(8,128)(2,1)}, bf16[32,4096]{1,0:T(8,128)(2,1)S(1)}, u32[]{:S(2)}, u32[]{:S(2)}) collective-permute-start(bf16[32,4096]{1,0:T(8,128)(2,1)} %get-tuple-element.44), channel_id=1, source_target_pairs={{0,4},{4,0},{8,12},{12,8},{1,5},{5,1},{9,13},{13,9},{2,6},{6,2},{1... | collective-permute-start | bytes 786440 | tf_op jit(solution)/shard_map/ppermute | solution.py:81
  83.5 18.0 %collective-permute-start.23 = (bf16[32,4096]{1,0:T(8,128)(2,1)}, bf16[32,4096]{1,0:T(8,128)(2,1)S(1)}, u32[]{:S(2)}, u32[]{:S(2)}) collective-permute-start(bf16[32,4096]{1,0:T(8,128)(2,1)} %get-tuple-element.43), channel_id=1, source_target_pairs={{0,4},{4,0},{8,12},{12,8},{1,5},{5,1},{9,13},{13,9},{2,6},{6,2},{1... | collective-permute-start | bytes 786440 | tf_op jit(solution)/shard_map/ppermute | solution.py:82
  85.3 5.7 %collective-permute-start.18 = (bf16[32,4096]{1,0:T(8,128)(2,1)S(1)}, bf16[32,4096]{1,0:T(8,128)(2,1)S(1)}, u32[]{:S(2)}, u32[]{:S(2)}) collective-permute-start(bf16[32,4096]{1,0:T(8,128)(2,1)S(1)} %add_convert_fusion.5), channel_id=1, source_target_pairs={{4,8},{8,4},{0,0},{12,12},{5,9},{9,5},{1,1},{13,13},{6,10},{10,6},... | collective-permute-start | bytes 786440 | tf_op jit(solution)/shard_map/ppermute | solution.py:87
  90.3 24.0 %collective-permute-start.21 = (bf16[32,4096]{1,0:T(8,128)(2,1)S(1)}, bf16[32,4096]{1,0:T(8,128)(2,1)S(1)}, u32[]{:S(2)}, u32[]{:S(2)}) collective-permute-start(bf16[32,4096]{1,0:T(8,128)(2,1)S(1)} %add_convert_fusion.3), channel_id=1, source_target_pairs={{4,8},{8,4},{0,0},{12,12},{5,9},{9,5},{1,1},{13,13},{6,10},{10,6},... | collective-permute-start | bytes 786440 | tf_op jit(solution)/shard_map/ppermute | solution.py:88
  91.1 23.2 %collective-permute-start.19 = (bf16[32,4096]{1,0:T(8,128)(2,1)S(1)}, bf16[32,4096]{1,0:T(8,128)(2,1)S(1)}, u32[]{:S(2)}, u32[]{:S(2)}) collective-permute-start(bf16[32,4096]{1,0:T(8,128)(2,1)S(1)} %fusion), channel_id=1, source_target_pairs={{0,4},{4,0},{8,12},{12,8},{1,5},{5,1},{9,13},{13,9},{2,6},{6,2},{1... | collective-permute-start | bytes 786440 | tf_op jit(solution)/shard_map/ppermute | solution.py:90
  102.5 12.0 %collective-permute-start.26 = (bf16[32,4096]{1,0:T(8,128)(2,1)S(1)}, bf16[32,4096]{1,0:T(8,128)(2,1)S(1)}, u32[]{:S(2)}, u32[]{:S(2)}) collective-permute-start(bf16[32,4096]{1,0:T(8,128)(2,1)S(1)} %add_convert_fusion), channel_id=1, source_target_pairs={{4,8},{8,4},{0,0},{12,12},{5,9},{9,5},{1,1},{13,13},{6,10},{10,6},... | collective-permute-start | bytes 786440 | tf_op jit(solution)/shard_map/ppermute | solution.py:88
  103.3 15.4 %collective-permute-start.25 = (bf16[32,4096]{1,0:T(8,128)(2,1)S(1)}, bf16[32,4096]{1,0:T(8,128)(2,1)S(1)}, u32[]{:S(2)}, u32[]{:S(2)}) collective-permute-start(bf16[32,4096]{1,0:T(8,128)(2,1)S(1)} %fusion.1), channel_id=1, source_target_pairs={{0,4},{4,0},{8,12},{12,8},{1,5},{5,1},{9,13},{13,9},{2,6},{6,2},{1... | collective-permute-start | bytes 786440 | tf_op jit(solution)/shard_map/ppermute | solution.py:90
  (20 other events, 170.0 us)

commit v6 on v5

v6 whole, which is shorter than its diff:
```python
from functools import partial

import jax
import jax.numpy as jnp
from jax import lax
from jax.experimental import pallas as pl
from jax.experimental.pallas import tpu as pltpu
from jax.sharding import PartitionSpec as P

SCORE_VMEM = 20 * 1024 * 1024
SUMS_VMEM = 12 * 1024 * 1024
PARTS = 4
SMEM_SPEC = pl.BlockSpec(memory_space=pltpu.SMEM)
VMEM_SPEC = pl.BlockSpec(memory_space=pltpu.VMEM)
ANY_SPEC = pl.BlockSpec(memory_space=pl.ANY)
SIDES = [(0, 1), (1, 0), (2, 3), (3, 2)]
MIDDLE = [(1, 2), (2, 1), (0, 0), (3, 3)]


def swap_bits(block, axis, bits):
    return lax.ppermute(block, axis, [(i, i ^ bits) for i in range(lax.axis_size(axis))])


def swap_gather(block, axis, bit):
    held = {0: block}
    while bit:
        for k in list(held):
            held[k ^ bit] = swap_bits(held[k], axis, bit)
        bit //= 2
    return [held[k] for k in range(len(held))]


def add_rounded(one, other):
    return (one.astype(jnp.float32) + other.astype(jnp.float32)).astype(jnp.bfloat16)


def staged_gather(block, images, routes, near_bits, far_bit):
    crossed = swap_bits(images, "reader", far_bit)
    side = lax.ppermute(block, "blk", SIDES)
    across = lax.ppermute(block, "blk", MIDDLE)
    side, across, near = lax.optimization_barrier((side, across, images))
    near = swap_gather(near, "reader", near_bits)
    far = lax.ppermute(across, "blk", SIDES)
    across_far = lax.ppermute(side, "blk", MIDDLE)
    far, across_far = lax.optimization_barrier((far, across_far))
    end = lax.ppermute(across_far, "blk", SIDES)
    line = [[block], [side], [far, across_far], [end, across]]
    crossed, routes, _ = lax.optimization_barrier((crossed, routes, across_far))
    step = images.shape[1] // PARTS
    parts = [
        swap_gather(crossed[:, i * step : (i + 1) * step], "reader", near_bits)
        for i in range(PARTS)
    ]
    far_blocks = [[crossed]] + [list(group) for group in list(zip(*parts))[1:]]
    return line, [[one] for one in near] + far_blocks, swap_all(routes)


def swap_all(routes):
    return [routes] + [swap_bits(routes, "reader", k) for k in range(1, lax.axis_size("reader"))]


def plain_gather(block, images, routes, near_bits, far_bit):
    near = swap_gather(images, "reader", near_bits)
    far = swap_gather(swap_bits(images, "reader", far_bit), "reader", near_bits)
    return line_gather(block, "blk"), [[one] for one in near + far], swap_all(routes)


def line_gather(block, axis):
    size, member = lax.axis_size(axis), lax.axis_index(axis)
    ahead, behind = [block], [block]
    for s in range(1, size):
        ahead.append(lax.ppermute(ahead[-1], axis, [(i, i + 1) for i in range(s - 1, size - 1)]))
        behind.append(lax.ppermute(behind[-1], axis, [(i, i - 1) for i in range(1, size - s + 1)]))
    blocks = [block]
    for s in range(1, size):
        blocks.append(jnp.where(member >= s, ahead[s], behind[size - s]))
    return [[one] for one in blocks]


def pair_scatter(pieces, axis):
    member = lax.axis_index(axis)
    is_end = (member == 0) | (member == 3)
    for_far_end = [lax.ppermute(parts[3], axis, SIDES) for parts in pieces]
    *second, for_far_end[0] = lax.optimization_barrier(
        [parts[2] for parts in pieces] + for_far_end[:1]
    )
    for_far_middle = [lax.ppermute(part, axis, SIDES) for part in second]
    totals, across_end = [], None
    for parts, part, end, middle in zip(pieces, second, for_far_end, for_far_middle):
        if across_end is not None:
            end, _ = lax.optimization_barrier((end, across_end))
        across_end = lax.ppermute(add_rounded(part, end), axis, MIDDLE)
        across_middle = lax.ppermute(add_rounded(parts[3], middle), axis, MIDDLE)
        near = jnp.where(is_end, parts[1], add_rounded(parts[1], across_end))
        from_side = lax.ppermute(near, axis, SIDES)
        total = parts[0].astype(jnp.float32) + from_side.astype(jnp.float32)
        totals.append(total + jnp.where(is_end, 0.0, across_middle.astype(jnp.float32)))
    return totals


def line_scatter(pieces, axis):
    return [line_sum(parts, axis) for parts in pieces]


def line_sum(parts, axis):
    size = lax.axis_size(axis)
    up = down = None
    for s in range(1, size):
        send_up, send_down = parts[s], parts[size - s]
        if s > 1:
            send_up = add_rounded(send_up, up)
            send_down = add_rounded(send_down, down)
        up = lax.ppermute(send_up, axis, [(i, i + 1) for i in range(0, s) if i + 1 < size])
        down = lax.ppermute(send_down, axis, [(i, i - 1) for i in range(size - s, size) if i > 0])
    total = parts[0].astype(jnp.float32)
    if size > 1:
        total = total + up.astype(jnp.float32) + down.astype(jnp.float32)
    return total


def column_lse(scores):
    peak = jnp.max(scores, axis=0, keepdims=True)
    total = jnp.sum(jnp.exp(scores - peak), axis=0, keepdims=True)
    return peak + jnp.log(total)


def take_groups(refs, counts):
    return [[refs.pop(0) for _ in range(n)] for n in counts]


def flat(groups):
    return [one for group in groups for one in group]


def score_kernel(counts, halves, finish, place_ref, *refs):
    image_counts, pair_counts = counts
    refs = list(refs)
    image_refs = take_groups(refs, image_counts)
    pair_refs = take_groups(refs, pair_counts)
    noise_ref, route_ref, score_ref, mask_ref, lse_ref, all_ref = refs[:6]
    line_ref, weighted_ref, image_sems, line_sems = refs[6:]
    reader, is_end = place_ref[0], place_ref[1] == 1
    rows = image_refs[0][0].shape[0]
    count, width = pair_refs[0][0].shape
    half = width // halves

    def line_copy(s, ref, h):
        columns = pl.ds(h * half, half)
        return pltpu.make_async_copy(
            ref.at[:, columns],
            line_ref.at[pl.ds(s * count, count), columns],
            line_sems.at[h, s],
        )

    copies = []
    for h in range(halves):
        for s, pair in enumerate(pair_refs):
            if len(pair) == 1:
                line_copy(s, pair[0], h).start()
                continue

            @pl.when(is_end)
            def _(s=s, pair=pair, h=h):
                line_copy(s, pair[0], h).start()

            @pl.when(jnp.logical_not(is_end))
            def _(s=s, pair=pair, h=h):
                line_copy(s, pair[1], h).start()

        half_copies = []
        for k, group in enumerate(image_refs):
            row = pl.multiple_of((reader ^ k) * rows, 16)
            each = min(half, group[0].shape[1])
            for start in range(h * half, (h + 1) * half, each):
                own = group[0].shape[1]
                ref = group[start // own]
                copy = pltpu.make_async_copy(
                    ref.at[:, pl.ds(start % own, each)],
                    all_ref.at[pl.ds(row, rows), pl.ds(start, each)],
                    image_sems.at[h, len(half_copies)],
                )
                copy.start()
                half_copies.append(copy)
        copies.append(half_copies)
    routes = route_ref[...]
    for k in range(mask_ref.shape[0]):
        hits = jnp.where(routes == (reader ^ k), 1.0, 0.0)
        mask_ref[k : k + 1, :] = jnp.max(hits, axis=0, keepdims=True)
    scores = None
    penalty = jnp.zeros((line_ref.shape[0], 1), jnp.float32)
    step = half // 4
    for h in range(halves):
        for s, pair in enumerate(pair_refs):
            line_copy(s, pair[0], h).wait()
        for start in range(h * half, (h + 1) * half, step):
            columns = slice(start, start + step)
            block = line_ref[:, columns].astype(jnp.float32)
            scaled = block * noise_ref[:, columns]
            weighted_ref[:, columns] = scaled.astype(jnp.bfloat16)
            penalty = penalty + 0.5 * jnp.sum(scaled * block, axis=1, keepdims=True)
        for copy in copies[h]:
            copy.wait()
        columns = slice(h * half, (h + 1) * half)
        part = lax.dot_general(
            all_ref[:, columns],
            weighted_ref[:, columns],
            (((1,), (1,)), ((), ())),
            preferred_element_type=jnp.float32,
        )
        scores = part if scores is None else scores + part
    scores = scores.T - penalty
    score_ref[...] = scores
    if finish:
        lse_ref[...] = column_lse(scores)


def all_scores(place, pairs, images, noise, routes, finish):
    count, width = pairs[0][0].shape
    halves = 2
    refs = len(pairs) * count
    slots = routes.shape[1]
    moved = [*flat(images), *flat(pairs)]
    return pl.pallas_call(
        partial(
            score_kernel,
            ([len(group) for group in images], [len(pair) for pair in pairs]),
            halves,
            finish,
        ),
        out_shape=(
            jax.ShapeDtypeStruct((refs, slots), jnp.float32),
            jax.ShapeDtypeStruct((len(images), slots), jnp.float32),
            jax.ShapeDtypeStruct((1, slots), jnp.float32),
            jax.ShapeDtypeStruct((slots, width), jnp.bfloat16),
        ),
        in_specs=[SMEM_SPEC] + [ANY_SPEC] * len(moved) + [VMEM_SPEC] * 2,
        out_specs=(VMEM_SPEC,) * 4,
        scratch_shapes=[
            pltpu.VMEM((refs, width), jnp.bfloat16),
            pltpu.VMEM((refs, width), jnp.bfloat16),
            pltpu.SemaphoreType.DMA((halves, len(flat(images)))),
            pltpu.SemaphoreType.DMA((halves, len(pairs))),
        ],
        compiler_params=pltpu.CompilerParams(vmem_limit_bytes=SCORE_VMEM),
        cost_estimate=pl.CostEstimate(
            flops=2 * refs * slots * width,
            bytes_accessed=2 * (slots + refs) * width,
            transcendentals=0,
        ),
        name="scores",
    )(place, *moved, noise, routes)


def lse_kernel(score_ref, lse_ref):
    lse_ref[...] = column_lse(score_ref[...])


def group_lse(scores):
    return pl.pallas_call(
        lse_kernel,
        out_shape=jax.ShapeDtypeStruct((1, scores.shape[1]), jnp.float32),
        name="group_lse",
    )(scores)


def emit_sums(posterior, all_ref, piece, out_refs):
    sums = jnp.dot(posterior, all_ref[:, piece], preferred_element_type=jnp.float32)
    count = sums.shape[0] // len(out_refs)
    for s, out_ref in enumerate(out_refs):
        out_ref[...] = sums[s * count : (s + 1) * count].astype(out_ref.dtype)


def first_sums_kernel(readers, members, piece, all_ref, score_ref, mask_ref, *refs):
    lse_refs = refs[:readers]
    out_refs = refs[readers : readers + members]
    norm_ref, post_ref = refs[readers + members :]
    kept = []
    for k, lse_ref in enumerate(lse_refs):
        kept.append(jnp.where(mask_ref[k : k + 1, :] > 0.0, lse_ref[...], -jnp.inf))
    highest = kept[0]
    for value in kept[1:]:
        highest = jnp.maximum(highest, value)
    spread = jnp.exp(kept[0] - highest)
    for value in kept[1:]:
        spread = spread + jnp.exp(value - highest)
    norm = highest + jnp.log(spread)
    norm_ref[...] = norm
    exponent = jnp.where(mask_ref[0:1, :] > 0.0, score_ref[...] - norm, -jnp.inf)
    posterior = jnp.exp(exponent).astype(jnp.bfloat16)
    post_ref[...] = posterior
    emit_sums(posterior, all_ref, piece, out_refs)


def later_sums_kernel(piece, all_ref, post_ref, *out_refs):
    emit_sums(post_ref[...], all_ref, piece, out_refs)


def group_sums(kernel, piece, members, all_images, operands, extra):
    refs, slots = operands[0].shape
    width = piece.stop - piece.start
    block = jax.ShapeDtypeStruct((refs // members, width), jnp.bfloat16)
    outs = pl.pallas_call(
        kernel,
        out_shape=(block,) * members + extra,
        in_specs=[VMEM_SPEC] * (1 + len(operands)),
        out_specs=(VMEM_SPEC,) * (members + len(extra)),
        compiler_params=pltpu.CompilerParams(vmem_limit_bytes=SUMS_VMEM),
        cost_estimate=pl.CostEstimate(
            flops=2 * refs * slots * width,
            bytes_accessed=2 * slots * width,
            transcendentals=0,
        ),
        name="sums",
    )(all_images, *operands)
    return outs[:members], outs[members:]


def on_device(images, routes, projections, noise_weights):
    readers = lax.axis_size("reader")
    members = lax.axis_size("blk")
    reader = lax.axis_index("reader")
    member = lax.axis_index("blk")
    is_end = (member == 0) | (member == members - 1)
    place = jnp.stack([reader, is_end.astype(jnp.int32)]).astype(jnp.int32)
    rows, width = images.shape
    noise = noise_weights.reshape(1, width)

    gather = staged_gather if members == 4 and rows % 32 == 0 else plain_gather
    line, blocks, route_blocks = gather(
        projections[0], images, routes.T, readers // 4, readers // 2
    )
    order = jnp.arange(readers, dtype=jnp.int32) ^ reader
    all_routes = jnp.stack(route_blocks)[order].transpose(1, 0, 2)
    all_routes = all_routes.reshape(routes.shape[1], readers * rows)

    split = lax.axis_size("sub") > 1
    scores, masks, mine, all_images = all_scores(
        place, line, blocks, noise, all_routes, not split
    )
    if split:
        scores = lax.psum(scores, "sub")
        mine = group_lse(scores)
    lses = [mine] + [swap_bits(mine, "reader", k) for k in range(1, readers)]
    half = width // 2
    first, last = slice(0, half), slice(half, width)
    extra = (
        jax.ShapeDtypeStruct((1, scores.shape[1]), jnp.float32),
        jax.ShapeDtypeStruct(scores.shape, jnp.bfloat16),
    )
    first_parts, (norms, posterior) = group_sums(
        partial(first_sums_kernel, readers, members, first),
        first,
        members,
        all_images,
        (scores, masks, *lses),
        extra,
    )
    last_parts, _ = group_sums(
        partial(later_sums_kernel, last), last, members, all_images, (posterior,), ()
    )
    scatter = pair_scatter if members == 4 else line_scatter
    totals = scatter((first_parts, last_parts), "blk")
    normalizer = lax.dynamic_slice(norms.reshape(-1), (reader * rows,), (rows,))
    return (jnp.concatenate(totals, axis=1)[None], normalizer)


def solution(mesh):
    return jax.shard_map(
        on_device,
        mesh=mesh,
        in_specs=(
            P(("parts", "blk", "reader"), "sub"),
            P(("parts", "blk", "reader"), None),
            P(("parts", "reader"), "blk", "sub"),
            P(("parts", "sub")),
        ),
        out_specs=(P(("parts", "reader"), "blk", "sub"), P(("parts", "blk", "reader"))),
        check_vma=False,
    )
```

time: 121 us -> 108 us (0.89)
  starting transfers between devices: 50.9 us -> 40.6 us
  Pallas kernels: 16.2 us -> 6.17 us
  local copies, waits for them, and re-layouts: 4.58 us -> 9.79 us
  waiting for transfers between devices: 44.4 us -> 48.1 us
    ppermute x12, waiting for transfers between devices: 17.3 us -> 3.97 us  [swap_bits(): lax.ppermute(block, axis, [(i, i ^ bits) for i in range(lax.axis_size(axi...]
    ppermute x1, waiting for transfers between devices: 0.01 us -> 9.55 us  [staged_gather(): far = lax.ppermute(across, 'blk', SIDES)]
    pallas_call x2, Pallas kernels: 9.09 us -> 1.45 us  [group_sums(): pl.pallas_call(kernel, out_shape=(block,) * members + extra, in_specs=[VM...]
    unnamed x34 -> x20, local copies, waits for them, and re-layouts: 0.96 us -> 7.31 us
    ppermute x2, starting transfers between devices: 17.5 us -> 11.6 us  [pair_scatter(): from_side = lax.ppermute(near, axis, SIDES)]
    ppermute x1, waiting for transfers between devices: 7.38 us -> 11.6 us  [staged_gather(): side = lax.ppermute(block, 'blk', SIDES)]
    ppermute x1, starting transfers between devices: 5.35 us -> 1.46 us  [staged_gather(): across_far = lax.ppermute(side, 'blk', MIDDLE)]
    ppermute x1, starting transfers between devices: 5.35 us -> 1.69 us  [staged_gather(): across = lax.ppermute(block, 'blk', MIDDLE)]
  transfers between devices with their start and end apart: 27 -> 27, of which waited for: 13 -> 13; matrix products, arithmetic and copies ran while one was open for 4% -> 3% of each run, Pallas kernels for 4% -> 1%
where the time goes in v6:
time: 108 us; the launch traced here: 107 us
  waiting for transfers between devices  48.1 us (45%)
  starting transfers between devices  40.6 us (38%)
  local copies, waits for them, and re-layouts  9.79 us (9%)
  Pallas kernels  6.17 us (6%)
  other arithmetic  1.76 us (2%)
    ppermute x2, starting transfers between devices, pair_scatter(): from_side = lax.ppermute(near, axis, SIDES)  11.6 us
    ppermute x1, waiting for transfers between devices, staged_gather(): side = lax.ppermute(block, 'blk', SIDES)  11.6 us
    ppermute x1, waiting for transfers between devices, staged_gather(): far = lax.ppermute(across, 'blk', SIDES)  9.55 us
    ppermute x1, waiting for transfers between devices, staged_gather(): end = lax.ppermute(across_far, 'blk', SIDES)  8.71 us
    ppermute x12, starting transfers between devices, swap_bits(): lax.ppermute(block, axis, [(i, i ^ bits) for i in range(lax.axis_size(axi...  7.81 us
    unnamed x20, local copies, waits for them, and re-layouts  7.31 us
    ppermute x2, waiting for transfers between devices, pair_scatter(): for_far_end = [lax.ppermute(parts[3], axis, SIDES) for parts in pieces]  6.41 us
    pallas_call x1, Pallas kernels, all_scores(): pl.pallas_call(partial(score_kernel, ([len(group) for group in images], [...  4.73 us
  transfers between devices with their start and end apart: 27, of which 13 were waited for; matrix products, arithmetic and copies ran while one was open for 3% of the time, Pallas kernels for 1%

profile of v6, /device:TPU:0, one launch (start us, length us, event | category | flops | bytes accessed | tf_op | source)
XLA Modules:
  0.0 107.3 jit_solution(15728344000734925127)
XLA Ops:
  0.6 3.0 %collective-permute-start.3 = (bf16[96,8192]{1,0:T(8,128)(2,1)}, bf16[96,8192]{1,0:T(8,128)(2,1)S(1)}, u32[]{:S(2)}, u32[]{:S(2)}) collective-permute-start(bf16[96,8192]{1,0:T(8,128)(2,1)} %refs_0_), channel_id=1, source_target_pairs={{0,2},{1,3},{2,0},{3,1},{4,6},{5,7},{6,4},{7,5},{8,10},{9,11},{10,... | collective-permute-start | bytes 4718600 | tf_op jit(solution)/shard_map/ppermute | solution.py:21
  3.6 1.7 %collective-permute-start.1 = (bf16[32,8192]{1,0:T(8,128)(2,1)}, bf16[32,8192]{1,0:T(8,128)(2,1)S(1)}, u32[]{:S(2)}, u32[]{:S(2)}) collective-permute-start(bf16[32,8192]{1,0:T(8,128)(2,1)} %bitcast.16), channel_id=1, source_target_pairs={{4,8},{8,4},{0,0},{12,12},{5,9},{9,5},{1,1},{13,13},{6,10},{10,6},... | collective-permute-start | bytes 1572872 | tf_op jit(solution)/shard_map/ppermute | solution.py:40
  5.3 3.4 %collective-permute-start = (bf16[32,8192]{1,0:T(8,128)(2,1)}, bf16[32,8192]{1,0:T(8,128)(2,1)S(1)}, u32[]{:S(2)}, u32[]{:S(2)}) collective-permute-start(bf16[32,8192]{1,0:T(8,128)(2,1)} %bitcast.17), channel_id=1, source_target_pairs={{0,4},{4,0},{8,12},{12,8},{1,5},{5,1},{9,13},{13,9},{2,6},{6,2},{1... | collective-permute-start | bytes 1572872 | tf_op jit(solution)/shard_map/ppermute | solution.py:39
  8.8 11.6 %collective-permute-done.refs_8_ = bf16[32,8192]{1,0:T(8,128)(2,1)S(1)} collective-permute-done((bf16[32,8192]{1,0:T(8,128)(2,1)}, bf16[32,8192]{1,0:T(8,128)(2,1)S(1)}, u32[]{:S(2)}, u32[]{:S(2)}) %collective-permute-start) | collective-permute-done | bytes 524320 | tf_op jit(solution)/shard_map/ppermute | solution.py:39
  20.3 1.7 %collective-permute-start.4 = (bf16[32,8192]{1,0:T(8,128)(2,1)S(1)}, bf16[32,8192]{1,0:T(8,128)(2,1)S(1)}, u32[]{:S(2)}, u32[]{:S(2)}) collective-permute-start(bf16[32,8192]{1,0:T(8,128)(2,1)S(1)} %collective-permute-done.1.refs_12_), channel_id=1, source_target_pairs={{0,4},{4,0},{8,12},{12,8},{1,5},{5,1},{9,13},{13,9},{2,6},{6,2},{1... | collective-permute-start | bytes 1572872 | tf_op jit(solution)/shard_map/ppermute | solution.py:43
  22.9 1.5 %collective-permute-start.5 = (bf16[32,8192]{1,0:T(8,128)(2,1)S(1)}, bf16[32,8192]{1,0:T(8,128)(2,1)}, u32[]{:S(2)}, u32[]{:S(2)}) collective-permute-start(bf16[32,8192]{1,0:T(8,128)(2,1)S(1)} %collective-permute-done.refs_8_), channel_id=1, source_target_pairs={{4,8},{8,4},{0,0},{12,12},{5,9},{9,5},{1,1},{13,13},{6,10},{10,6},... | collective-permute-start | bytes 1572872 | tf_op jit(solution)/shard_map/ppermute | solution.py:44
  25.1 9.5 %collective-permute-done.4.refs_9_ = bf16[32,8192]{1,0:T(8,128)(2,1)S(1)} collective-permute-done((bf16[32,8192]{1,0:T(8,128)(2,1)S(1)}, bf16[32,8192]{1,0:T(8,128)(2,1)S(1)}, u32[]{:S(2)}, u32[]{:S(2)}) %collective-permute-start.4) | collective-permute-done | bytes 524320 | tf_op jit(solution)/shard_map/ppermute | solution.py:43
  35.5 3.7 %collective-permute-start.10 = (bf16[32,8192]{1,0:T(8,128)(2,1)}, bf16[32,8192]{1,0:T(8,128)(2,1)}, u32[]{:S(2)}, u32[]{:S(2)}) collective-permute-start(bf16[32,8192]{1,0:T(8,128)(2,1)} %collective-permute-done.5.refs_10_), channel_id=1, source_target_pairs={{0,4},{4,0},{8,12},{12,8},{1,5},{5,1},{9,13},{13,9},{2,6},{6,2},{1... | collective-permute-start | bytes 1572872 | tf_op jit(solution)/shard_map/ppermute | solution.py:46
  41.1 1.2 %fusion.3 = (bf16[96,2048]{1,0:T(8,128)(2,1)}, bf16[96,2048]{1,0:T(8,128)(2,1)}, bf16[96,2048]{1,0:T(8,128)(2,1)}, bf16[96,2048]{1,0:T(8,128)(2,1)}) fusion(bf16[96,8192]{1,0:T(8,128)(2,1)S(1)} %collective-permute-done.3.refs_2_), kind=kLoop, calls=%fused_computation.18 | loop fusion | bytes 3145728 | tf_op jit(solution)/shard_map/slice | solution.py:51
  42.3 8.7 %collective-permute-done.10.refs_11_ = bf16[32,8192]{1,0:T(8,128)(2,1)} collective-permute-done((bf16[32,8192]{1,0:T(8,128)(2,1)}, bf16[32,8192]{1,0:T(8,128)(2,1)}, u32[]{:S(2)}, u32[]{:S(2)}) %collective-permute-start.10) | collective-permute-done | bytes 524320 | tf_op jit(solution)/shard_map/ppermute | solution.py:46
  54.8 1.0 copy-done.1
  55.8 1.0 copy-done.3
  56.9 1.0 copy-done.5
  57.9 1.0 copy-done.7
  59.7 4.7 %scores.1 = (f32[128,384]{1,0:T(8,128)S(1)}, f32[4,384]{1,0:T(4,128)S(1)}, f32[1,384]{1,0:T(1,128)S(1)}, bf16[384,8192]{1,0:T(8,128)(2,1)S(1)}) custom-call(s32[2]{0:T(128)S(1)} %pad_add_fusion.1.place_ref, bf16[96,8192]{1,0:T(8,128)(2,1)S(1)} %copy-done, bf16[96,8192]{1,0:T(8,128)(2,1)} %collective-permute-done.2.refs_1_, ...), custom_call_target="tpu_custom_call" | custom-call | flops 805306368 | bytes 8388608 | tf_op jit(solution)/shard_map/scores/pallas_call | solution.py:223
  64.8 1.5 %collective-permute-start.15 = (f32[1,384]{1,0:T(1,128)S(1)}, f32[1,384]{1,0:T(1,128)S(1)}, u32[]{:S(2)}, u32[]{:S(2)}) collective-permute-start(f32[1,384]{1,0:T(1,128)S(1)} %get-tuple-element.37.refs_0_), channel_id=1, source_target_pairs={{0,2},{1,3},{2,0},{3,1},{4,6},{5,7},{6,4},{7,5},{8,10},{9,11},{10,... | collective-permute-start | bytes 4616 | tf_op jit(solution)/shard_map/ppermute | solution.py:21
  66.4 1.1 %collective-permute-done.16.refs_3_ = f32[1,384]{1,0:T(1,128)S(1)} collective-permute-done((f32[1,384]{1,0:T(1,128)S(1)}, f32[1,384]{1,0:T(1,128)S(1)}, u32[]{:S(2)}, u32[]{:S(2)}) %collective-permute-start.16) | collective-permute-done | bytes 1568 | tf_op jit(solution)/shard_map/ppermute | solution.py:21
  69.1 1.8 %collective-permute-start.17 = (bf16[32,4096]{1,0:T(8,128)(2,1)S(1)}, bf16[32,4096]{1,0:T(8,128)(2,1)S(1)}, u32[]{:S(2)}, u32[]{:S(2)}) collective-permute-start(bf16[32,4096]{1,0:T(8,128)(2,1)S(1)} %get-tuple-element.43), channel_id=1, source_target_pairs={{0,4},{4,0},{8,12},{12,8},{1,5},{5,1},{9,13},{13,9},{2,6},{6,2},{1... | collective-permute-start | bytes 786440 | tf_op jit(solution)/shard_map/ppermute | solution.py:83
  72.0 6.4 %collective-permute-done.17 = bf16[32,4096]{1,0:T(8,128)(2,1)S(1)} collective-permute-done((bf16[32,4096]{1,0:T(8,128)(2,1)S(1)}, bf16[32,4096]{1,0:T(8,128)(2,1)S(1)}, u32[]{:S(2)}, u32[]{:S(2)}) %collective-permute-start.17) | collective-permute-done | bytes 262176 | tf_op jit(solution)/shard_map/ppermute | solution.py:83
  79.8 4.3 %collective-permute-start.20 = (bf16[32,4096]{1,0:T(8,128)(2,1)S(1)}, bf16[32,4096]{1,0:T(8,128)(2,1)S(1)}, u32[]{:S(2)}, u32[]{:S(2)}) collective-permute-start(bf16[32,4096]{1,0:T(8,128)(2,1)S(1)} %get-tuple-element.44), channel_id=1, source_target_pairs={{0,4},{4,0},{8,12},{12,8},{1,5},{5,1},{9,13},{13,9},{2,6},{6,2},{1... | collective-permute-start | bytes 786440 | tf_op jit(solution)/shard_map/ppermute | solution.py:87
  84.9 7.0 %collective-permute-start.19 = (bf16[32,4096]{1,0:T(8,128)(2,1)S(1)}, bf16[32,4096]{1,0:T(8,128)(2,1)S(1)}, u32[]{:S(2)}, u32[]{:S(2)}) collective-permute-start(bf16[32,4096]{1,0:T(8,128)(2,1)S(1)} %fusion), channel_id=1, source_target_pairs={{0,4},{4,0},{8,12},{12,8},{1,5},{5,1},{9,13},{13,9},{2,6},{6,2},{1... | collective-permute-start | bytes 786440 | tf_op jit(solution)/shard_map/ppermute | solution.py:95
  92.7 3.7 %collective-permute-done.25 = bf16[32,4096]{1,0:T(8,128)(2,1)S(1)} collective-permute-done((bf16[32,4096]{1,0:T(8,128)(2,1)S(1)}, bf16[32,4096]{1,0:T(8,128)(2,1)S(1)}, u32[]{:S(2)}, u32[]{:S(2)}) %collective-permute-start.25) | collective-permute-done | bytes 262176 | tf_op jit(solution)/shard_map/ppermute | solution.py:87
  97.2 4.6 %collective-permute-start.24 = (bf16[32,4096]{1,0:T(8,128)(2,1)S(1)}, bf16[32,4096]{1,0:T(8,128)(2,1)S(1)}, u32[]{:S(2)}, u32[]{:S(2)}) collective-permute-start(bf16[32,4096]{1,0:T(8,128)(2,1)S(1)} %fusion.1), channel_id=1, source_target_pairs={{0,4},{4,0},{8,12},{12,8},{1,5},{5,1},{9,13},{13,9},{2,6},{6,2},{1... | collective-permute-start | bytes 786440 | tf_op jit(solution)/shard_map/ppermute | solution.py:95
  102.0 4.1 %collective-permute-done.24 = bf16[32,4096]{1,0:T(8,128)(2,1)S(1)} collective-permute-done((bf16[32,4096]{1,0:T(8,128)(2,1)S(1)}, bf16[32,4096]{1,0:T(8,128)(2,1)S(1)}, u32[]{:S(2)}, u32[]{:S(2)}) %collective-permute-start.24) | collective-permute-done | bytes 262176 | tf_op jit(solution)/shard_map/ppermute | solution.py:95
  (71 shorter events, 17.0 us)
Async XLA Ops:
  0.6 38.6 %collective-permute-start.3 = (bf16[96,8192]{1,0:T(8,128)(2,1)}, bf16[96,8192]{1,0:T(8,128)(2,1)S(1)}, u32[]{:S(2)}, u32[]{:S(2)}) collective-permute-start(bf16[96,8192]{1,0:T(8,128)(2,1)} %refs_0_), channel_id=1, source_target_pairs={{0,2},{1,3},{2,0},{3,1},{4,6},{5,7},{6,4},{7,5},{8,10},{9,11},{10,... | collective-permute-start | bytes 4718600 | tf_op jit(solution)/shard_map/ppermute | solution.py:21
  3.6 5.1 %collective-permute-start.1 = (bf16[32,8192]{1,0:T(8,128)(2,1)}, bf16[32,8192]{1,0:T(8,128)(2,1)S(1)}, u32[]{:S(2)}, u32[]{:S(2)}) collective-permute-start(bf16[32,8192]{1,0:T(8,128)(2,1)} %bitcast.16), channel_id=1, source_target_pairs={{4,8},{8,4},{0,0},{12,12},{5,9},{9,5},{1,1},{13,13},{6,10},{10,6},... | collective-permute-start | bytes 1572872 | tf_op jit(solution)/shard_map/ppermute | solution.py:40
  5.3 15.0 %collective-permute-start = (bf16[32,8192]{1,0:T(8,128)(2,1)}, bf16[32,8192]{1,0:T(8,128)(2,1)S(1)}, u32[]{:S(2)}, u32[]{:S(2)}) collective-permute-start(bf16[32,8192]{1,0:T(8,128)(2,1)} %bitcast.17), channel_id=1, source_target_pairs={{0,4},{4,0},{8,12},{12,8},{1,5},{5,1},{9,13},{13,9},{2,6},{6,2},{1... | collective-permute-start | bytes 1572872 | tf_op jit(solution)/shard_map/ppermute | solution.py:39
  20.3 34.4 %collective-permute-start.2 = (bf16[96,8192]{1,0:T(8,128)(2,1)}, bf16[96,8192]{1,0:T(8,128)(2,1)}, u32[]{:S(2)}, u32[]{:S(2)}) collective-permute-start(bf16[96,8192]{1,0:T(8,128)(2,1)} %refs_0_), channel_id=1, source_target_pairs={{0,1},{1,0},{2,3},{3,2},{4,5},{5,4},{6,7},{7,6},{8,9},{9,8},{10,11... | collective-permute-start | bytes 4718600 | tf_op jit(solution)/shard_map/ppermute | solution.py:21
  20.3 14.3 %collective-permute-start.4 = (bf16[32,8192]{1,0:T(8,128)(2,1)S(1)}, bf16[32,8192]{1,0:T(8,128)(2,1)S(1)}, u32[]{:S(2)}, u32[]{:S(2)}) collective-permute-start(bf16[32,8192]{1,0:T(8,128)(2,1)S(1)} %collective-permute-done.1.refs_12_), channel_id=1, source_target_pairs={{0,4},{4,0},{8,12},{12,8},{1,5},{5,1},{9,13},{13,9},{2,6},{6,2},{1... | collective-permute-start | bytes 1572872 | tf_op jit(solution)/shard_map/ppermute | solution.py:43
  22.9 12.6 %collective-permute-start.5 = (bf16[32,8192]{1,0:T(8,128)(2,1)S(1)}, bf16[32,8192]{1,0:T(8,128)(2,1)}, u32[]{:S(2)}, u32[]{:S(2)}) collective-permute-start(bf16[32,8192]{1,0:T(8,128)(2,1)S(1)} %collective-permute-done.refs_8_), channel_id=1, source_target_pairs={{4,8},{8,4},{0,0},{12,12},{5,9},{9,5},{1,1},{13,13},{6,10},{10,6},... | collective-permute-start | bytes 1572872 | tf_op jit(solution)/shard_map/ppermute | solution.py:44
  35.5 15.5 %collective-permute-start.10 = (bf16[32,8192]{1,0:T(8,128)(2,1)}, bf16[32,8192]{1,0:T(8,128)(2,1)}, u32[]{:S(2)}, u32[]{:S(2)}) collective-permute-start(bf16[32,8192]{1,0:T(8,128)(2,1)} %collective-permute-done.5.refs_10_), channel_id=1, source_target_pairs={{0,4},{4,0},{8,12},{12,8},{1,5},{5,1},{9,13},{13,9},{2,6},{6,2},{1... | collective-permute-start | bytes 1572872 | tf_op jit(solution)/shard_map/ppermute | solution.py:46
  39.2 11.8 %collective-permute-start.13 = (s32[2,96]{1,0:T(2,128)}, s32[2,96]{1,0:T(2,128)S(1)}, u32[]{:S(2)}, u32[]{:S(2)}) collective-permute-start(s32[2,96]{1,0:T(2,128)} %bitcast.21), channel_id=1, source_target_pairs={{0,3},{1,2},{2,1},{3,0},{4,7},{5,6},{6,5},{7,4},{8,11},{9,10},{10,... | collective-permute-start | bytes 2312 | tf_op jit(solution)/shard_map/ppermute | solution.py:21
  39.2 12.3 %collective-permute-start.12 = (s32[2,96]{1,0:T(2,128)}, s32[2,96]{1,0:T(2,128)S(1)}, u32[]{:S(2)}, u32[]{:S(2)}) collective-permute-start(s32[2,96]{1,0:T(2,128)} %bitcast.22), channel_id=1, source_target_pairs={{0,2},{1,3},{2,0},{3,1},{4,6},{5,7},{6,4},{7,5},{8,10},{9,11},{10,... | collective-permute-start | bytes 2312 | tf_op jit(solution)/shard_map/ppermute | solution.py:21
  40.0 11.6 %collective-permute-start.11 = (s32[2,96]{1,0:T(2,128)}, s32[2,96]{1,0:T(2,128)S(1)}, u32[]{:S(2)}, u32[]{:S(2)}) collective-permute-start(s32[2,96]{1,0:T(2,128)} %bitcast.23), channel_id=1, source_target_pairs={{0,1},{1,0},{2,3},{3,2},{4,5},{5,4},{6,7},{7,6},{8,9},{9,8},{10,11... | collective-permute-start | bytes 2312 | tf_op jit(solution)/shard_map/ppermute | solution.py:21
  51.5 2.7 %collective-permute-start.7 = (bf16[96,2048]{1,0:T(8,128)(2,1)}, bf16[96,2048]{1,0:T(8,128)(2,1)}, u32[]{:S(2)}, u32[]{:S(2)}) collective-permute-start(bf16[96,2048]{1,0:T(8,128)(2,1)} %get-tuple-element.54), channel_id=1, source_target_pairs={{0,1},{1,0},{2,3},{3,2},{4,5},{5,4},{6,7},{7,6},{8,9},{9,8},{10,11... | collective-permute-start | bytes 1179656 | tf_op jit(solution)/shard_map/ppermute | solution.py:21
  51.6 3.2 %collective-permute-start.6 = (bf16[96,2048]{1,0:T(8,128)(2,1)}, bf16[96,2048]{1,0:T(8,128)(2,1)}, u32[]{:S(2)}, u32[]{:S(2)}) collective-permute-start(bf16[96,2048]{1,0:T(8,128)(2,1)} %get-tuple-element.55), channel_id=1, source_target_pairs={{0,1},{1,0},{2,3},{3,2},{4,5},{5,4},{6,7},{7,6},{8,9},{9,8},{10,11... | collective-permute-start | bytes 1179656 | tf_op jit(solution)/shard_map/ppermute | solution.py:21
  64.4 3.1 %collective-permute-start.16 = (f32[1,384]{1,0:T(1,128)S(1)}, f32[1,384]{1,0:T(1,128)S(1)}, u32[]{:S(2)}, u32[]{:S(2)}) collective-permute-start(f32[1,384]{1,0:T(1,128)S(1)} %get-tuple-element.37.refs_0_), channel_id=1, source_target_pairs={{0,3},{1,2},{2,1},{3,0},{4,7},{5,6},{6,5},{7,4},{8,11},{9,10},{10,... | collective-permute-start | bytes 4616 | tf_op jit(solution)/shard_map/ppermute | solution.py:21
  64.8 3.6 %collective-permute-start.15 = (f32[1,384]{1,0:T(1,128)S(1)}, f32[1,384]{1,0:T(1,128)S(1)}, u32[]{:S(2)}, u32[]{:S(2)}) collective-permute-start(f32[1,384]{1,0:T(1,128)S(1)} %get-tuple-element.37.refs_0_), channel_id=1, source_target_pairs={{0,2},{1,3},{2,0},{3,1},{4,6},{5,7},{6,4},{7,5},{8,10},{9,11},{10,... | collective-permute-start | bytes 4616 | tf_op jit(solution)/shard_map/ppermute | solution.py:21
  69.1 9.3 %collective-permute-start.17 = (bf16[32,4096]{1,0:T(8,128)(2,1)S(1)}, bf16[32,4096]{1,0:T(8,128)(2,1)S(1)}, u32[]{:S(2)}, u32[]{:S(2)}) collective-permute-start(bf16[32,4096]{1,0:T(8,128)(2,1)S(1)} %get-tuple-element.43), channel_id=1, source_target_pairs={{0,4},{4,0},{8,12},{12,8},{1,5},{5,1},{9,13},{13,9},{2,6},{6,2},{1... | collective-permute-start | bytes 786440 | tf_op jit(solution)/shard_map/ppermute | solution.py:83
  71.6 12.4 %collective-permute-start.22 = (bf16[32,4096]{1,0:T(8,128)(2,1)S(1)}, bf16[32,4096]{1,0:T(8,128)(2,1)S(1)}, u32[]{:S(2)}, u32[]{:S(2)}) collective-permute-start(bf16[32,4096]{1,0:T(8,128)(2,1)S(1)} %get-tuple-element.49), channel_id=1, source_target_pairs={{0,4},{4,0},{8,12},{12,8},{1,5},{5,1},{9,13},{13,9},{2,6},{6,2},{1... | collective-permute-start | bytes 786440 | tf_op jit(solution)/shard_map/ppermute | solution.py:83
  78.5 5.6 %collective-permute-start.18 = (bf16[32,4096]{1,0:T(8,128)(2,1)S(1)}, bf16[32,4096]{1,0:T(8,128)(2,1)S(1)}, u32[]{:S(2)}, u32[]{:S(2)}) collective-permute-start(bf16[32,4096]{1,0:T(8,128)(2,1)S(1)} %add_convert_fusion.5), channel_id=1, source_target_pairs={{4,8},{8,4},{0,0},{12,12},{5,9},{9,5},{1,1},{13,13},{6,10},{10,6},... | collective-permute-start | bytes 786440 | tf_op jit(solution)/shard_map/ppermute | solution.py:92
  79.8 12.2 %collective-permute-start.20 = (bf16[32,4096]{1,0:T(8,128)(2,1)S(1)}, bf16[32,4096]{1,0:T(8,128)(2,1)S(1)}, u32[]{:S(2)}, u32[]{:S(2)}) collective-permute-start(bf16[32,4096]{1,0:T(8,128)(2,1)S(1)} %get-tuple-element.44), channel_id=1, source_target_pairs={{0,4},{4,0},{8,12},{12,8},{1,5},{5,1},{9,13},{13,9},{2,6},{6,2},{1... | collective-permute-start | bytes 786440 | tf_op jit(solution)/shard_map/ppermute | solution.py:87
  84.0 12.3 %collective-permute-start.25 = (bf16[32,4096]{1,0:T(8,128)(2,1)S(1)}, bf16[32,4096]{1,0:T(8,128)(2,1)S(1)}, u32[]{:S(2)}, u32[]{:S(2)}) collective-permute-start(bf16[32,4096]{1,0:T(8,128)(2,1)S(1)} %get-tuple-element.48), channel_id=1, source_target_pairs={{0,4},{4,0},{8,12},{12,8},{1,5},{5,1},{9,13},{13,9},{2,6},{6,2},{1... | collective-permute-start | bytes 786440 | tf_op jit(solution)/shard_map/ppermute | solution.py:87
  84.1 13.0 %collective-permute-start.23 = (bf16[32,4096]{1,0:T(8,128)(2,1)S(1)}, bf16[32,4096]{1,0:T(8,128)(2,1)S(1)}, u32[]{:S(2)}, u32[]{:S(2)}) collective-permute-start(bf16[32,4096]{1,0:T(8,128)(2,1)S(1)} %add_convert_fusion.2), channel_id=1, source_target_pairs={{4,8},{8,4},{0,0},{12,12},{5,9},{9,5},{1,1},{13,13},{6,10},{10,6},... | collective-permute-start | bytes 786440 | tf_op jit(solution)/shard_map/ppermute | solution.py:92
  84.9 17.0 %collective-permute-start.19 = (bf16[32,4096]{1,0:T(8,128)(2,1)S(1)}, bf16[32,4096]{1,0:T(8,128)(2,1)S(1)}, u32[]{:S(2)}, u32[]{:S(2)}) collective-permute-start(bf16[32,4096]{1,0:T(8,128)(2,1)S(1)} %fusion), channel_id=1, source_target_pairs={{0,4},{4,0},{8,12},{12,8},{1,5},{5,1},{9,13},{13,9},{2,6},{6,2},{1... | collective-permute-start | bytes 786440 | tf_op jit(solution)/shard_map/ppermute | solution.py:95
  92.0 9.9 %collective-permute-start.21 = (bf16[32,4096]{1,0:T(8,128)(2,1)S(1)}, bf16[32,4096]{1,0:T(8,128)(2,1)S(1)}, u32[]{:S(2)}, u32[]{:S(2)}) collective-permute-start(bf16[32,4096]{1,0:T(8,128)(2,1)S(1)} %add_convert_fusion.3), channel_id=1, source_target_pairs={{4,8},{8,4},{0,0},{12,12},{5,9},{9,5},{1,1},{13,13},{6,10},{10,6},... | collective-permute-start | bytes 786440 | tf_op jit(solution)/shard_map/ppermute | solution.py:93
  96.4 5.6 %collective-permute-start.26 = (bf16[32,4096]{1,0:T(8,128)(2,1)S(1)}, bf16[32,4096]{1,0:T(8,128)(2,1)S(1)}, u32[]{:S(2)}, u32[]{:S(2)}) collective-permute-start(bf16[32,4096]{1,0:T(8,128)(2,1)S(1)} %add_convert_fusion), channel_id=1, source_target_pairs={{4,8},{8,4},{0,0},{12,12},{5,9},{9,5},{1,1},{13,13},{6,10},{10,6},... | collective-permute-start | bytes 786440 | tf_op jit(solution)/shard_map/ppermute | solution.py:93
  97.2 9.0 %collective-permute-start.24 = (bf16[32,4096]{1,0:T(8,128)(2,1)S(1)}, bf16[32,4096]{1,0:T(8,128)(2,1)S(1)}, u32[]{:S(2)}, u32[]{:S(2)}) collective-permute-start(bf16[32,4096]{1,0:T(8,128)(2,1)S(1)} %fusion.1), channel_id=1, source_target_pairs={{0,4},{4,0},{8,12},{12,8},{1,5},{5,1},{9,13},{13,9},{2,6},{6,2},{1... | collective-permute-start | bytes 786440 | tf_op jit(solution)/shard_map/ppermute | solution.py:95
  (13 other events, 42.9 us)

commit v7 on v6

--- a/solution.py
+++ b/solution.py
@@ -9,12 +9,11 @@
 
 SCORE_VMEM = 20 * 1024 * 1024
 SUMS_VMEM = 12 * 1024 * 1024
-PARTS = 4
-SMEM_SPEC = pl.BlockSpec(memory_space=pltpu.SMEM)
 VMEM_SPEC = pl.BlockSpec(memory_space=pltpu.VMEM)
 ANY_SPEC = pl.BlockSpec(memory_space=pl.ANY)
 SIDES = [(0, 1), (1, 0), (2, 3), (3, 2)]
 MIDDLE = [(1, 2), (2, 1), (0, 0), (3, 3)]
+ENDS = [(0, 3), (3, 0), (1, 1), (2, 2)]
 
 
 def swap_bits(block, axis, bits):
@@ -35,24 +34,21 @@
 
 
 def staged_gather(block, images, routes, near_bits, far_bit):
+    routes = swap_all(routes)
+    own, images, *routes = lax.optimization_barrier((block, images, *routes))
     crossed = swap_bits(images, "reader", far_bit)
     side = lax.ppermute(block, "blk", SIDES)
     across = lax.ppermute(block, "blk", MIDDLE)
-    side, across, near = lax.optimization_barrier((side, across, images))
-    near = swap_gather(near, "reader", near_bits)
+    end = lax.ppermute(block, "blk", ENDS)
+    side, across, images = lax.optimization_barrier((side, across, images))
+    near = swap_gather(images, "reader", near_bits)
     far = lax.ppermute(across, "blk", SIDES)
     across_far = lax.ppermute(side, "blk", MIDDLE)
-    far, across_far = lax.optimization_barrier((far, across_far))
-    end = lax.ppermute(across_far, "blk", SIDES)
-    line = [[block], [side], [far, across_far], [end, across]]
-    crossed, routes, _ = lax.optimization_barrier((crossed, routes, across_far))
-    step = images.shape[1] // PARTS
-    parts = [
-        swap_gather(crossed[:, i * step : (i + 1) * step], "reader", near_bits)
-        for i in range(PARTS)
-    ]
-    far_blocks = [[crossed]] + [list(group) for group in list(zip(*parts))[1:]]
-    return line, [[one] for one in near] + far_blocks, swap_all(routes)
+    crossed, far, across_far, end, *near = lax.optimization_barrier(
+        (crossed, far, across_far, end, *near)
+    )
+    line = [[own], [side], [far, across_far], [end, across]]
+    return line, near + swap_gather(crossed, "reader", near_bits), routes
 
 
 def swap_all(routes):
@@ -62,7 +58,7 @@
 def plain_gather(block, images, routes, near_bits, far_bit):
     near = swap_gather(images, "reader", near_bits)
     far = swap_gather(swap_bits(images, "reader", far_bit), "reader", near_bits)
-    return line_gather(block, "blk"), [[one] for one in near + far], swap_all(routes)
+    return line_gather(block, "blk"), near + far, swap_all(routes)
 
 
 def line_gather(block, axis):
@@ -124,23 +120,16 @@
     return peak + jnp.log(total)
 
 
-def take_groups(refs, counts):
-    return [[refs.pop(0) for _ in range(n)] for n in counts]
-
-
-def flat(groups):
-    return [one for group in groups for one in group]
-
-
-def score_kernel(counts, halves, finish, place_ref, *refs):
-    image_counts, pair_counts = counts
+def score_kernel(readers, pair_counts, halves, finish, *refs):
     refs = list(refs)
-    image_refs = take_groups(refs, image_counts)
-    pair_refs = take_groups(refs, pair_counts)
-    noise_ref, route_ref, score_ref, mask_ref, lse_ref, all_ref = refs[:6]
-    line_ref, weighted_ref, image_sems, line_sems = refs[6:]
-    reader, is_end = place_ref[0], place_ref[1] == 1
-    rows = image_refs[0][0].shape[0]
+    image_refs = [refs.pop(0) for _ in range(readers)]
+    pair_refs = [[refs.pop(0) for _ in range(n)] for n in pair_counts]
+    route_refs = [refs.pop(0) for _ in range(readers)]
+    noise_ref, score_ref, mask_ref, lse_ref, all_ref = refs[:5]
+    line_ref, weighted_ref, image_sems, line_sems = refs[5:]
+    reader, member = lax.axis_index("reader"), lax.axis_index("blk")
+    is_end = (member == 0) | (member == lax.axis_size("blk") - 1)
+    rows = image_refs[0].shape[0]
     count, width = pair_refs[0][0].shape
     half = width // halves
 
@@ -167,25 +156,26 @@
             def _(s=s, pair=pair, h=h):
                 line_copy(s, pair[1], h).start()
 
+        columns = pl.ds(h * half, half)
         half_copies = []
-        for k, group in enumerate(image_refs):
+        for k, ref in enumerate(image_refs):
             row = pl.multiple_of((reader ^ k) * rows, 16)
-            each = min(half, group[0].shape[1])
-            for start in range(h * half, (h + 1) * half, each):
-                own = group[0].shape[1]
-                ref = group[start // own]
-                copy = pltpu.make_async_copy(
-                    ref.at[:, pl.ds(start % own, each)],
-                    all_ref.at[pl.ds(row, rows), pl.ds(start, each)],
-                    image_sems.at[h, len(half_copies)],
-                )
-                copy.start()
-                half_copies.append(copy)
+            copy = pltpu.make_async_copy(
+                ref.at[:, columns], all_ref.at[pl.ds(row, rows), columns], image_sems.at[h, k]
+            )
+            copy.start()
+            half_copies.append(copy)
         copies.append(half_copies)
-    routes = route_ref[...]
-    for k in range(mask_ref.shape[0]):
-        hits = jnp.where(routes == (reader ^ k), 1.0, 0.0)
-        mask_ref[k : k + 1, :] = jnp.max(hits, axis=0, keepdims=True)
+    routes = [ref[...] for ref in route_refs]
+    bit = 1
+    while bit < readers:
+        flip = (reader & bit) > 0
+        routes = [jnp.where(flip, routes[k ^ bit], one) for k, one in enumerate(routes)]
+        bit *= 2
+    for j, route in enumerate(routes):
+        for k in range(readers):
+            hits = jnp.where(route == (reader ^ k), 1.0, 0.0)
+            mask_ref[k : k + 1, j * rows : (j + 1) * rows] = jnp.max(hits, axis=0, keepdims=True)
     scores = None
     penalty = jnp.zeros((line_ref.shape[0], 1), jnp.float32)
     step = half // 4
@@ -214,16 +204,17 @@
         lse_ref[...] = column_lse(scores)
 
 
-def all_scores(place, pairs, images, noise, routes, finish):
+def all_scores(pairs, images, noise, routes, finish):
     count, width = pairs[0][0].shape
     halves = 2
     refs = len(pairs) * count
-    slots = routes.shape[1]
-    moved = [*flat(images), *flat(pairs)]
+    slots = len(images) * images[0].shape[0]
+    moved = [*images, *[one for pair in pairs for one in pair]]
     return pl.pallas_call(
         partial(
             score_kernel,
-            ([len(group) for group in images], [len(pair) for pair in pairs]),
+            len(images),
+            [len(pair) for pair in pairs],
             halves,
             finish,
         ),
@@ -233,12 +224,12 @@
             jax.ShapeDtypeStruct((1, slots), jnp.float32),
             jax.ShapeDtypeStruct((slots, width), jnp.bfloat16),
         ),
-        in_specs=[SMEM_SPEC] + [ANY_SPEC] * len(moved) + [VMEM_SPEC] * 2,
+        in_specs=[ANY_SPEC] * len(moved) + [VMEM_SPEC] * (len(routes) + 1),
         out_specs=(VMEM_SPEC,) * 4,
         scratch_shapes=[
             pltpu.VMEM((refs, width), jnp.bfloat16),
             pltpu.VMEM((refs, width), jnp.bfloat16),
-            pltpu.SemaphoreType.DMA((halves, len(flat(images)))),
+            pltpu.SemaphoreType.DMA((halves, len(images))),
             pltpu.SemaphoreType.DMA((halves, len(pairs))),
         ],
         compiler_params=pltpu.CompilerParams(vmem_limit_bytes=SCORE_VMEM),
@@ -248,7 +239,7 @@
             transcendentals=0,
         ),
         name="scores",
-    )(place, *moved, noise, routes)
+    )(*moved, *routes, noise)
 
 
 def lse_kernel(score_ref, lse_ref):
@@ -319,9 +310,6 @@
     readers = lax.axis_size("reader")
     members = lax.axis_size("blk")
     reader = lax.axis_index("reader")
-    member = lax.axis_index("blk")
-    is_end = (member == 0) | (member == members - 1)
-    place = jnp.stack([reader, is_end.astype(jnp.int32)]).astype(jnp.int32)
     rows, width = images.shape
     noise = noise_weights.reshape(1, width)
 
@@ -329,13 +317,9 @@
     line, blocks, route_blocks = gather(
         projections[0], images, routes.T, readers // 4, readers // 2
     )
-    order = jnp.arange(readers, dtype=jnp.int32) ^ reader
-    all_routes = jnp.stack(route_blocks)[order].transpose(1, 0, 2)
-    all_routes = all_routes.reshape(routes.shape[1], readers * rows)
-
     split = lax.axis_size("sub") > 1
     scores, masks, mine, all_images = all_scores(
-        place, line, blocks, noise, all_routes, not split
+        line, blocks, noise, route_blocks, not split
     )
     if split:
         scores = lax.psum(scores, "sub")

time: 108 us -> 113 us (1.046)
  waiting for transfers between devices: 48.1 us -> 57 us
  local copies, waits for them, and re-layouts: 9.79 us -> 4.47 us
  starting transfers between devices: 40.6 us -> 43.6 us
    ppermute x1, waiting for transfers between devices: 11.6 us -> 5.17 us  [staged_gather(): side = lax.ppermute(block, 'blk', SIDES)]
    ppermute x2, waiting for transfers between devices: 3.66 us -> 9.43 us  [pair_scatter(): for_far_middle = [lax.ppermute(part, axis, SIDES) for part in second]]
    ppermute x12 -> x9, waiting for transfers between devices: 3.97 us -> 9.7 us  [swap_bits(): lax.ppermute(block, axis, [(i, i ^ bits) for i in range(lax.axis_size(axi...]
    ppermute x2, starting transfers between devices: 11.6 us -> 16 us  [pair_scatter(): from_side = lax.ppermute(near, axis, SIDES)]
    ppermute x2, starting transfers between devices: 2.17 us -> 6.58 us  [pair_scatter(): for_far_end = [lax.ppermute(parts[3], axis, SIDES) for parts in pieces]]
    ppermute x12 -> x9, starting transfers between devices: 7.81 us -> 4.37 us  [swap_bits(): lax.ppermute(block, axis, [(i, i ^ bits) for i in range(lax.axis_size(axi...]
    unnamed x20 -> x8, local copies, waits for them, and re-layouts: 7.31 us -> 3.88 us
    ppermute x1, waiting for transfers between devices: 8.71 us -> 11.6 us  [staged_gather(): end = lax.ppermute(block, 'blk', ENDS)]
  transfers between devices with their start and end apart: 27 -> 24, of which waited for: 13 -> 12; matrix products, arithmetic and copies ran while one was open for 3% -> 1% of each run, Pallas kernels for 1% -> 1%
where the time goes in v7:
time: 113 us
  waiting for transfers between devices  57 us (50%)
  starting transfers between devices  43.6 us (39%)
  Pallas kernels  5.12 us (5%)
  local copies, waits for them, and re-layouts  4.47 us (4%)
  other arithmetic  1.66 us (1%)
    ppermute x2, starting transfers between devices, pair_scatter(): from_side = lax.ppermute(near, axis, SIDES)  16 us
    ppermute x1, waiting for transfers between devices, staged_gather(): end = lax.ppermute(block, 'blk', ENDS)  11.6 us
    ppermute x1, waiting for transfers between devices, staged_gather(): far = lax.ppermute(across, 'blk', SIDES)  10.9 us
    ppermute x9, waiting for transfers between devices, swap_bits(): lax.ppermute(block, axis, [(i, i ^ bits) for i in range(lax.axis_size(axi...  9.7 us
    ppermute x2, waiting for transfers between devices, pair_scatter(): for_far_middle = [lax.ppermute(part, axis, SIDES) for part in second]  9.43 us
    ppermute x2, starting transfers between devices, pair_scatter(): for_far_end = [lax.ppermute(parts[3], axis, SIDES) for parts in pieces]  6.58 us
    ppermute x2, waiting for transfers between devices, pair_scatter(): for_far_end = [lax.ppermute(parts[3], axis, SIDES) for parts in pieces]  5.85 us
    ppermute x1, starting transfers between devices, staged_gather(): end = lax.ppermute(block, 'blk', ENDS)  5.66 us
  transfers between devices with their start and end apart: 24, of which 12 were waited for; matrix products, arithmetic and copies ran while one was open for 1% of the time, Pallas kernels for 1%

profile of v7, /device:TPU:0, one launch (start us, length us, event | category | flops | bytes accessed | tf_op | source)
XLA Modules:
  0.0 112.6 jit_solution(8526160124949595382)
XLA Ops:
  0.6 3.1 %collective-permute-start.4 = (bf16[32,8192]{1,0:T(8,128)(2,1)}, bf16[32,8192]{1,0:T(8,128)(2,1)S(1)}, u32[]{:S(2)}, u32[]{:S(2)}) collective-permute-start(bf16[32,8192]{1,0:T(8,128)(2,1)} %bitcast.7), channel_id=1, source_target_pairs={{0,4},{4,0},{8,12},{12,8},{1,5},{5,1},{9,13},{13,9},{2,6},{6,2},{1... | collective-permute-start | bytes 1572872 | tf_op jit(solution)/shard_map/ppermute | solution.py:40
  3.7 1.7 %collective-permute-start.5 = (bf16[32,8192]{1,0:T(8,128)(2,1)}, bf16[32,8192]{1,0:T(8,128)(2,1)S(1)}, u32[]{:S(2)}, u32[]{:S(2)}) collective-permute-start(bf16[32,8192]{1,0:T(8,128)(2,1)} %bitcast.8), channel_id=1, source_target_pairs={{4,8},{8,4},{0,0},{12,12},{5,9},{9,5},{1,1},{13,13},{6,10},{10,6},... | collective-permute-start | bytes 1572872 | tf_op jit(solution)/shard_map/ppermute | solution.py:41
  5.4 1.5 %collective-permute-start.1 = (s32[2,96]{1,0:T(2,128)}, s32[2,96]{1,0:T(2,128)S(1)}, u32[]{:S(2)}, u32[]{:S(2)}) collective-permute-start(s32[2,96]{1,0:T(2,128)} %bitcast.13), channel_id=1, source_target_pairs={{0,2},{1,3},{2,0},{3,1},{4,6},{5,7},{6,4},{7,5},{8,10},{9,11},{10,... | collective-permute-start | bytes 2312 | tf_op jit(solution)/shard_map/ppermute | solution.py:20
  7.3 1.9 %collective-permute-done.1.refs_12_ = s32[2,96]{1,0:T(2,128)S(1)} collective-permute-done((s32[2,96]{1,0:T(2,128)}, s32[2,96]{1,0:T(2,128)S(1)}, u32[]{:S(2)}, u32[]{:S(2)}) %collective-permute-start.1) | collective-permute-done | bytes 800 | tf_op jit(solution)/shard_map/ppermute | solution.py:20
  10.7 5.2 %collective-permute-done.4.refs_5_ = bf16[32,8192]{1,0:T(8,128)(2,1)S(1)} collective-permute-done((bf16[32,8192]{1,0:T(8,128)(2,1)}, bf16[32,8192]{1,0:T(8,128)(2,1)S(1)}, u32[]{:S(2)}, u32[]{:S(2)}) %collective-permute-start.4) | collective-permute-done | bytes 524320 | tf_op jit(solution)/shard_map/ppermute | solution.py:40
  15.9 5.7 %collective-permute-start.8 = (bf16[32,8192]{1,0:T(8,128)(2,1)}, bf16[32,8192]{1,0:T(8,128)(2,1)S(1)}, u32[]{:S(2)}, u32[]{:S(2)}) collective-permute-start(bf16[32,8192]{1,0:T(8,128)(2,1)} %bitcast.9), channel_id=1, source_target_pairs={{0,12},{12,0},{4,4},{8,8},{1,13},{13,1},{5,5},{9,9},{2,14},{14,2},... | collective-permute-start | bytes 1572872 | tf_op jit(solution)/shard_map/ppermute | solution.py:42
  23.0 11.6 %collective-permute-done.8.refs_8_ = bf16[32,8192]{1,0:T(8,128)(2,1)S(1)} collective-permute-done((bf16[32,8192]{1,0:T(8,128)(2,1)}, bf16[32,8192]{1,0:T(8,128)(2,1)S(1)}, u32[]{:S(2)}, u32[]{:S(2)}) %collective-permute-start.8) | collective-permute-done | bytes 524320 | tf_op jit(solution)/shard_map/ppermute | solution.py:42
  34.6 10.9 %collective-permute-done.6.refs_6_ = bf16[32,8192]{1,0:T(8,128)(2,1)S(1)} collective-permute-done((bf16[32,8192]{1,0:T(8,128)(2,1)S(1)}, bf16[32,8192]{1,0:T(8,128)(2,1)S(1)}, u32[]{:S(2)}, u32[]{:S(2)}) %collective-permute-start.6) | collective-permute-done | bytes 524320 | tf_op jit(solution)/shard_map/ppermute | solution.py:45
  45.6 1.6 %collective-permute-done.3.refs_2_ = bf16[96,8192]{1,0:T(8,128)(2,1)S(1)} collective-permute-done((bf16[96,8192]{1,0:T(8,128)(2,1)}, bf16[96,8192]{1,0:T(8,128)(2,1)S(1)}, u32[]{:S(2)}, u32[]{:S(2)}) %collective-permute-start.3) | collective-permute-done | bytes 1572896 | tf_op jit(solution)/shard_map/ppermute | solution.py:20
  47.1 3.4 %collective-permute-done.10.refs_3_ = bf16[96,8192]{1,0:T(8,128)(2,1)S(1)} collective-permute-done((bf16[96,8192]{1,0:T(8,128)(2,1)S(1)}, bf16[96,8192]{1,0:T(8,128)(2,1)S(1)}, u32[]{:S(2)}, u32[]{:S(2)}) %collective-permute-start.10) | collective-permute-done | bytes 1572896 | tf_op jit(solution)/shard_map/ppermute | solution.py:20
  50.6 1.4 %copy-done = bf16[96,8192]{1,0:T(8,128)(2,1)S(1)} copy-done((bf16[96,8192]{1,0:T(8,128)(2,1)S(1)}, bf16[96,8192]{1,0:T(8,128)(2,1)}, u32[]{:S(2)}) %copy-start) | copy-done | bytes 1572888
  52.0 1.0 copy-done.1
  54.4 3.7 %scores.1 = (f32[128,384]{1,0:T(8,128)S(1)}, f32[4,384]{1,0:T(4,128)S(1)}, f32[1,384]{1,0:T(1,128)S(1)}, bf16[384,8192]{1,0:T(8,128)(2,1)S(1)}) custom-call(bf16[96,8192]{1,0:T(8,128)(2,1)S(1)} %copy-done, bf16[96,8192]{1,0:T(8,128)(2,1)S(1)} %collective-permute-done.9.refs_1_, bf16[96,8192]{1,0:T(8,128)(2,1)S(1)} %collective-permute-done.3.refs_2_, ...), custom_call_target="tpu_custom_call" | custom-call | flops 805306368 | bytes 8388608 | tf_op jit(solution)/shard_map/scores/pallas_call | solution.py:213
  58.9 1.2 %collective-permute-start.13 = (f32[1,384]{1,0:T(1,128)S(1)}, f32[1,384]{1,0:T(1,128)S(1)}, u32[]{:S(2)}, u32[]{:S(2)}) collective-permute-start(f32[1,384]{1,0:T(1,128)S(1)} %get-tuple-element.53.refs_0_), channel_id=1, source_target_pairs={{0,3},{1,2},{2,1},{3,0},{4,7},{5,6},{6,5},{7,4},{8,11},{9,10},{10,... | collective-permute-start | bytes 4616 | tf_op jit(solution)/shard_map/ppermute | solution.py:20
  60.1 1.9 %collective-permute-done.12.refs_2_ = f32[1,384]{1,0:T(1,128)S(1)} collective-permute-done((f32[1,384]{1,0:T(1,128)S(1)}, f32[1,384]{1,0:T(1,128)S(1)}, u32[]{:S(2)}, u32[]{:S(2)}) %collective-permute-start.12) | collective-permute-done | bytes 1568 | tf_op jit(solution)/shard_map/ppermute | solution.py:20
  62.7 3.5 %collective-permute-start.14 = (bf16[32,4096]{1,0:T(8,128)(2,1)S(1)}, bf16[32,4096]{1,0:T(8,128)(2,1)S(1)}, u32[]{:S(2)}, u32[]{:S(2)}) collective-permute-start(bf16[32,4096]{1,0:T(8,128)(2,1)S(1)} %get-tuple-element.59), channel_id=1, source_target_pairs={{0,4},{4,0},{8,12},{12,8},{1,5},{5,1},{9,13},{13,9},{2,6},{6,2},{1... | collective-permute-start | bytes 786440 | tf_op jit(solution)/shard_map/ppermute | solution.py:79
  66.9 5.9 %collective-permute-done.14 = bf16[32,4096]{1,0:T(8,128)(2,1)S(1)} collective-permute-done((bf16[32,4096]{1,0:T(8,128)(2,1)S(1)}, bf16[32,4096]{1,0:T(8,128)(2,1)S(1)}, u32[]{:S(2)}, u32[]{:S(2)}) %collective-permute-start.14) | collective-permute-done | bytes 262176 | tf_op jit(solution)/shard_map/ppermute | solution.py:79
  73.5 3.1 %collective-permute-start.19 = (bf16[32,4096]{1,0:T(8,128)(2,1)S(1)}, bf16[32,4096]{1,0:T(8,128)(2,1)S(1)}, u32[]{:S(2)}, u32[]{:S(2)}) collective-permute-start(bf16[32,4096]{1,0:T(8,128)(2,1)S(1)} %get-tuple-element.65), channel_id=1, source_target_pairs={{0,4},{4,0},{8,12},{12,8},{1,5},{5,1},{9,13},{13,9},{2,6},{6,2},{1... | collective-permute-start | bytes 786440 | tf_op jit(solution)/shard_map/ppermute | solution.py:79
  77.2 2.0 %collective-permute-start.22 = (bf16[32,4096]{1,0:T(8,128)(2,1)S(1)}, bf16[32,4096]{1,0:T(8,128)(2,1)S(1)}, u32[]{:S(2)}, u32[]{:S(2)}) collective-permute-start(bf16[32,4096]{1,0:T(8,128)(2,1)S(1)} %get-tuple-element.64), channel_id=1, source_target_pairs={{0,4},{4,0},{8,12},{12,8},{1,5},{5,1},{9,13},{13,9},{2,6},{6,2},{1... | collective-permute-start | bytes 786440 | tf_op jit(solution)/shard_map/ppermute | solution.py:83
  79.3 4.8 %collective-permute-start.16 = (bf16[32,4096]{1,0:T(8,128)(2,1)S(1)}, bf16[32,4096]{1,0:T(8,128)(2,1)S(1)}, u32[]{:S(2)}, u32[]{:S(2)}) collective-permute-start(bf16[32,4096]{1,0:T(8,128)(2,1)S(1)} %fusion), channel_id=1, source_target_pairs={{0,4},{4,0},{8,12},{12,8},{1,5},{5,1},{9,13},{13,9},{2,6},{6,2},{1... | collective-permute-start | bytes 786440 | tf_op jit(solution)/shard_map/ppermute | solution.py:91
  84.1 5.3 %collective-permute-done.17 = bf16[32,4096]{1,0:T(8,128)(2,1)S(1)} collective-permute-done((bf16[32,4096]{1,0:T(8,128)(2,1)S(1)}, bf16[32,4096]{1,0:T(8,128)(2,1)S(1)}, u32[]{:S(2)}, u32[]{:S(2)}) %collective-permute-start.17) | collective-permute-done | bytes 262176 | tf_op jit(solution)/shard_map/ppermute | solution.py:83
  90.9 4.1 %collective-permute-done.22 = bf16[32,4096]{1,0:T(8,128)(2,1)S(1)} collective-permute-done((bf16[32,4096]{1,0:T(8,128)(2,1)S(1)}, bf16[32,4096]{1,0:T(8,128)(2,1)S(1)}, u32[]{:S(2)}, u32[]{:S(2)}) %collective-permute-start.22) | collective-permute-done | bytes 262176 | tf_op jit(solution)/shard_map/ppermute | solution.py:83
  95.9 11.2 %collective-permute-start.21 = (bf16[32,4096]{1,0:T(8,128)(2,1)S(1)}, bf16[32,4096]{1,0:T(8,128)(2,1)S(1)}, u32[]{:S(2)}, u32[]{:S(2)}) collective-permute-start(bf16[32,4096]{1,0:T(8,128)(2,1)S(1)} %fusion.1), channel_id=1, source_target_pairs={{0,4},{4,0},{8,12},{12,8},{1,5},{5,1},{9,13},{13,9},{2,6},{6,2},{1... | collective-permute-start | bytes 786440 | tf_op jit(solution)/shard_map/ppermute | solution.py:91
  107.2 4.2 %collective-permute-done.21 = bf16[32,4096]{1,0:T(8,128)(2,1)S(1)} collective-permute-done((bf16[32,4096]{1,0:T(8,128)(2,1)S(1)}, bf16[32,4096]{1,0:T(8,128)(2,1)S(1)}, u32[]{:S(2)}, u32[]{:S(2)}) %collective-permute-start.21) | collective-permute-done | bytes 262176 | tf_op jit(solution)/shard_map/ppermute | solution.py:91
  (45 shorter events, 12.0 us)
Async XLA Ops:
  0.6 15.2 %collective-permute-start.4 = (bf16[32,8192]{1,0:T(8,128)(2,1)}, bf16[32,8192]{1,0:T(8,128)(2,1)S(1)}, u32[]{:S(2)}, u32[]{:S(2)}) collective-permute-start(bf16[32,8192]{1,0:T(8,128)(2,1)} %bitcast.7), channel_id=1, source_target_pairs={{0,4},{4,0},{8,12},{12,8},{1,5},{5,1},{9,13},{13,9},{2,6},{6,2},{1... | collective-permute-start | bytes 1572872 | tf_op jit(solution)/shard_map/ppermute | solution.py:40
  3.7 12.1 %collective-permute-start.5 = (bf16[32,8192]{1,0:T(8,128)(2,1)}, bf16[32,8192]{1,0:T(8,128)(2,1)S(1)}, u32[]{:S(2)}, u32[]{:S(2)}) collective-permute-start(bf16[32,8192]{1,0:T(8,128)(2,1)} %bitcast.8), channel_id=1, source_target_pairs={{4,8},{8,4},{0,0},{12,12},{5,9},{9,5},{1,1},{13,13},{6,10},{10,6},... | collective-permute-start | bytes 1572872 | tf_op jit(solution)/shard_map/ppermute | solution.py:41
  5.4 1.9 %collective-permute-start = (s32[2,96]{1,0:T(2,128)}, s32[2,96]{1,0:T(2,128)S(1)}, u32[]{:S(2)}, u32[]{:S(2)}) collective-permute-start(s32[2,96]{1,0:T(2,128)} %bitcast.12), channel_id=1, source_target_pairs={{0,1},{1,0},{2,3},{3,2},{4,5},{5,4},{6,7},{7,6},{8,9},{9,8},{10,11... | collective-permute-start | bytes 2312 | tf_op jit(solution)/shard_map/ppermute | solution.py:20
  5.4 3.8 %collective-permute-start.1 = (s32[2,96]{1,0:T(2,128)}, s32[2,96]{1,0:T(2,128)S(1)}, u32[]{:S(2)}, u32[]{:S(2)}) collective-permute-start(s32[2,96]{1,0:T(2,128)} %bitcast.13), channel_id=1, source_target_pairs={{0,2},{1,3},{2,0},{3,1},{4,6},{5,7},{6,4},{7,5},{8,10},{9,11},{10,... | collective-permute-start | bytes 2312 | tf_op jit(solution)/shard_map/ppermute | solution.py:20
  6.9 3.2 %collective-permute-start.2 = (s32[2,96]{1,0:T(2,128)}, s32[2,96]{1,0:T(2,128)S(1)}, u32[]{:S(2)}, u32[]{:S(2)}) collective-permute-start(s32[2,96]{1,0:T(2,128)} %bitcast.14), channel_id=1, source_target_pairs={{0,3},{1,2},{2,1},{3,0},{4,7},{5,6},{6,5},{7,4},{8,11},{9,10},{10,... | collective-permute-start | bytes 2312 | tf_op jit(solution)/shard_map/ppermute | solution.py:20
  10.1 37.0 %collective-permute-start.3 = (bf16[96,8192]{1,0:T(8,128)(2,1)}, bf16[96,8192]{1,0:T(8,128)(2,1)S(1)}, u32[]{:S(2)}, u32[]{:S(2)}) collective-permute-start(bf16[96,8192]{1,0:T(8,128)(2,1)} %refs_0_), channel_id=1, source_target_pairs={{0,2},{1,3},{2,0},{3,1},{4,6},{5,7},{6,4},{7,5},{8,10},{9,11},{10,... | collective-permute-start | bytes 4718600 | tf_op jit(solution)/shard_map/ppermute | solution.py:20
  15.9 31.3 %collective-permute-start.9 = (bf16[96,8192]{1,0:T(8,128)(2,1)}, bf16[96,8192]{1,0:T(8,128)(2,1)S(1)}, u32[]{:S(2)}, u32[]{:S(2)}) collective-permute-start(bf16[96,8192]{1,0:T(8,128)(2,1)} %refs_0_), channel_id=1, source_target_pairs={{0,1},{1,0},{2,3},{3,2},{4,5},{5,4},{6,7},{7,6},{8,9},{9,8},{10,11... | collective-permute-start | bytes 4718600 | tf_op jit(solution)/shard_map/ppermute | solution.py:20
  15.9 18.8 %collective-permute-start.8 = (bf16[32,8192]{1,0:T(8,128)(2,1)}, bf16[32,8192]{1,0:T(8,128)(2,1)S(1)}, u32[]{:S(2)}, u32[]{:S(2)}) collective-permute-start(bf16[32,8192]{1,0:T(8,128)(2,1)} %bitcast.9), channel_id=1, source_target_pairs={{0,12},{12,0},{4,4},{8,8},{1,13},{13,1},{5,5},{9,9},{2,14},{14,2},... | collective-permute-start | bytes 1572872 | tf_op jit(solution)/shard_map/ppermute | solution.py:42
  21.5 24.0 %collective-permute-start.6 = (bf16[32,8192]{1,0:T(8,128)(2,1)S(1)}, bf16[32,8192]{1,0:T(8,128)(2,1)S(1)}, u32[]{:S(2)}, u32[]{:S(2)}) collective-permute-start(bf16[32,8192]{1,0:T(8,128)(2,1)S(1)} %collective-permute-done.5.refs_9_), channel_id=1, source_target_pairs={{0,4},{4,0},{8,12},{12,8},{1,5},{5,1},{9,13},{13,9},{2,6},{6,2},{1... | collective-permute-start | bytes 1572872 | tf_op jit(solution)/shard_map/ppermute | solution.py:45
  22.3 23.3 %collective-permute-start.7 = (bf16[32,8192]{1,0:T(8,128)(2,1)S(1)}, bf16[32,8192]{1,0:T(8,128)(2,1)S(1)}, u32[]{:S(2)}, u32[]{:S(2)}) collective-permute-start(bf16[32,8192]{1,0:T(8,128)(2,1)S(1)} %collective-permute-done.4.refs_5_), channel_id=1, source_target_pairs={{4,8},{8,4},{0,0},{12,12},{5,9},{9,5},{1,1},{13,13},{6,10},{10,6},... | collective-permute-start | bytes 1572872 | tf_op jit(solution)/shard_map/ppermute | solution.py:46
  47.1 3.4 %collective-permute-start.10 = (bf16[96,8192]{1,0:T(8,128)(2,1)S(1)}, bf16[96,8192]{1,0:T(8,128)(2,1)S(1)}, u32[]{:S(2)}, u32[]{:S(2)}) collective-permute-start(bf16[96,8192]{1,0:T(8,128)(2,1)S(1)} %collective-permute-done.3.refs_2_), channel_id=1, source_target_pairs={{0,1},{1,0},{2,3},{3,2},{4,5},{5,4},{6,7},{7,6},{8,9},{9,8},{10,11... | collective-permute-start | bytes 4718600 | tf_op jit(solution)/shard_map/ppermute | solution.py:20
  58.1 1.9 %collective-permute-start.11 = (f32[1,384]{1,0:T(1,128)S(1)}, f32[1,384]{1,0:T(1,128)S(1)}, u32[]{:S(2)}, u32[]{:S(2)}) collective-permute-start(f32[1,384]{1,0:T(1,128)S(1)} %get-tuple-element.53.refs_0_), channel_id=1, source_target_pairs={{0,1},{1,0},{2,3},{3,2},{4,5},{5,4},{6,7},{7,6},{8,9},{9,8},{10,11... | collective-permute-start | bytes 4616 | tf_op jit(solution)/shard_map/ppermute | solution.py:20
  58.3 3.6 %collective-permute-start.12 = (f32[1,384]{1,0:T(1,128)S(1)}, f32[1,384]{1,0:T(1,128)S(1)}, u32[]{:S(2)}, u32[]{:S(2)}) collective-permute-start(f32[1,384]{1,0:T(1,128)S(1)} %get-tuple-element.53.refs_0_), channel_id=1, source_target_pairs={{0,2},{1,3},{2,0},{3,1},{4,6},{5,7},{6,4},{7,5},{8,10},{9,11},{10,... | collective-permute-start | bytes 4616 | tf_op jit(solution)/shard_map/ppermute | solution.py:20
  58.9 3.0 %collective-permute-start.13 = (f32[1,384]{1,0:T(1,128)S(1)}, f32[1,384]{1,0:T(1,128)S(1)}, u32[]{:S(2)}, u32[]{:S(2)}) collective-permute-start(f32[1,384]{1,0:T(1,128)S(1)} %get-tuple-element.53.refs_0_), channel_id=1, source_target_pairs={{0,3},{1,2},{2,1},{3,0},{4,7},{5,6},{6,5},{7,4},{8,11},{9,10},{10,... | collective-permute-start | bytes 4616 | tf_op jit(solution)/shard_map/ppermute | solution.py:20
  62.7 10.1 %collective-permute-start.14 = (bf16[32,4096]{1,0:T(8,128)(2,1)S(1)}, bf16[32,4096]{1,0:T(8,128)(2,1)S(1)}, u32[]{:S(2)}, u32[]{:S(2)}) collective-permute-start(bf16[32,4096]{1,0:T(8,128)(2,1)S(1)} %get-tuple-element.59), channel_id=1, source_target_pairs={{0,4},{4,0},{8,12},{12,8},{1,5},{5,1},{9,13},{13,9},{2,6},{6,2},{1... | collective-permute-start | bytes 786440 | tf_op jit(solution)/shard_map/ppermute | solution.py:79
  72.8 6.4 %collective-permute-start.15 = (bf16[32,4096]{1,0:T(8,128)(2,1)S(1)}, bf16[32,4096]{1,0:T(8,128)(2,1)S(1)}, u32[]{:S(2)}, u32[]{:S(2)}) collective-permute-start(bf16[32,4096]{1,0:T(8,128)(2,1)S(1)} %add_convert_fusion.5), channel_id=1, source_target_pairs={{4,8},{8,4},{0,0},{12,12},{5,9},{9,5},{1,1},{13,13},{6,10},{10,6},... | collective-permute-start | bytes 786440 | tf_op jit(solution)/shard_map/ppermute | solution.py:88
  73.5 16.7 %collective-permute-start.19 = (bf16[32,4096]{1,0:T(8,128)(2,1)S(1)}, bf16[32,4096]{1,0:T(8,128)(2,1)S(1)}, u32[]{:S(2)}, u32[]{:S(2)}) collective-permute-start(bf16[32,4096]{1,0:T(8,128)(2,1)S(1)} %get-tuple-element.65), channel_id=1, source_target_pairs={{0,4},{4,0},{8,12},{12,8},{1,5},{5,1},{9,13},{13,9},{2,6},{6,2},{1... | collective-permute-start | bytes 786440 | tf_op jit(solution)/shard_map/ppermute | solution.py:79
  77.2 12.3 %collective-permute-start.17 = (bf16[32,4096]{1,0:T(8,128)(2,1)S(1)}, bf16[32,4096]{1,0:T(8,128)(2,1)S(1)}, u32[]{:S(2)}, u32[]{:S(2)}) collective-permute-start(bf16[32,4096]{1,0:T(8,128)(2,1)S(1)} %get-tuple-element.60), channel_id=1, source_target_pairs={{0,4},{4,0},{8,12},{12,8},{1,5},{5,1},{9,13},{13,9},{2,6},{6,2},{1... | collective-permute-start | bytes 786440 | tf_op jit(solution)/shard_map/ppermute | solution.py:83
  77.2 17.9 %collective-permute-start.22 = (bf16[32,4096]{1,0:T(8,128)(2,1)S(1)}, bf16[32,4096]{1,0:T(8,128)(2,1)S(1)}, u32[]{:S(2)}, u32[]{:S(2)}) collective-permute-start(bf16[32,4096]{1,0:T(8,128)(2,1)S(1)} %get-tuple-element.64), channel_id=1, source_target_pairs={{0,4},{4,0},{8,12},{12,8},{1,5},{5,1},{9,13},{13,9},{2,6},{6,2},{1... | collective-permute-start | bytes 786440 | tf_op jit(solution)/shard_map/ppermute | solution.py:83
  79.3 27.8 %collective-permute-start.16 = (bf16[32,4096]{1,0:T(8,128)(2,1)S(1)}, bf16[32,4096]{1,0:T(8,128)(2,1)S(1)}, u32[]{:S(2)}, u32[]{:S(2)}) collective-permute-start(bf16[32,4096]{1,0:T(8,128)(2,1)S(1)} %fusion), channel_id=1, source_target_pairs={{0,4},{4,0},{8,12},{12,8},{1,5},{5,1},{9,13},{13,9},{2,6},{6,2},{1... | collective-permute-start | bytes 786440 | tf_op jit(solution)/shard_map/ppermute | solution.py:91
  89.5 17.6 %collective-permute-start.18 = (bf16[32,4096]{1,0:T(8,128)(2,1)S(1)}, bf16[32,4096]{1,0:T(8,128)(2,1)S(1)}, u32[]{:S(2)}, u32[]{:S(2)}) collective-permute-start(bf16[32,4096]{1,0:T(8,128)(2,1)S(1)} %add_convert_fusion.3), channel_id=1, source_target_pairs={{4,8},{8,4},{0,0},{12,12},{5,9},{9,5},{1,1},{13,13},{6,10},{10,6},... | collective-permute-start | bytes 786440 | tf_op jit(solution)/shard_map/ppermute | solution.py:89
  90.2 5.5 %collective-permute-start.20 = (bf16[32,4096]{1,0:T(8,128)(2,1)S(1)}, bf16[32,4096]{1,0:T(8,128)(2,1)S(1)}, u32[]{:S(2)}, u32[]{:S(2)}) collective-permute-start(bf16[32,4096]{1,0:T(8,128)(2,1)S(1)} %add_convert_fusion.2), channel_id=1, source_target_pairs={{4,8},{8,4},{0,0},{12,12},{5,9},{9,5},{1,1},{13,13},{6,10},{10,6},... | collective-permute-start | bytes 786440 | tf_op jit(solution)/shard_map/ppermute | solution.py:88
  95.1 12.1 %collective-permute-start.23 = (bf16[32,4096]{1,0:T(8,128)(2,1)S(1)}, bf16[32,4096]{1,0:T(8,128)(2,1)S(1)}, u32[]{:S(2)}, u32[]{:S(2)}) collective-permute-start(bf16[32,4096]{1,0:T(8,128)(2,1)S(1)} %add_convert_fusion), channel_id=1, source_target_pairs={{4,8},{8,4},{0,0},{12,12},{5,9},{9,5},{1,1},{13,13},{6,10},{10,6},... | collective-permute-start | bytes 786440 | tf_op jit(solution)/shard_map/ppermute | solution.py:89
  95.9 15.6 %collective-permute-start.21 = (bf16[32,4096]{1,0:T(8,128)(2,1)S(1)}, bf16[32,4096]{1,0:T(8,128)(2,1)S(1)}, u32[]{:S(2)}, u32[]{:S(2)}) collective-permute-start(bf16[32,4096]{1,0:T(8,128)(2,1)S(1)} %fusion.1), channel_id=1, source_target_pairs={{0,4},{4,0},{8,12},{12,8},{1,5},{5,1},{9,13},{13,9},{2,6},{6,2},{1... | collective-permute-start | bytes 786440 | tf_op jit(solution)/shard_map/ppermute | solution.py:91
  (4 other events, 3.9 us)

commit v8 on v7

v8 whole, which is shorter than its diff:
```python
from functools import partial

import jax
import jax.numpy as jnp
from jax import lax
from jax.experimental import pallas as pl
from jax.experimental.pallas import tpu as pltpu
from jax.sharding import PartitionSpec as P

SCORE_VMEM = 20 * 1024 * 1024
SUMS_VMEM = 12 * 1024 * 1024
STEP = 1024
VMEM_SPEC = pl.BlockSpec(memory_space=pltpu.VMEM)
ANY_SPEC = pl.BlockSpec(memory_space=pl.ANY)
SIDES = [(0, 1), (1, 0), (2, 3), (3, 2)]
MIDDLE = [(1, 2), (2, 1), (0, 0), (3, 3)]
ENDS = [(0, 3), (3, 0), (1, 1), (2, 2)]


def swap_bits(block, axis, bits):
    return lax.ppermute(block, axis, [(i, i ^ bits) for i in range(lax.axis_size(axis))])


def swap_gather(block, axis, bit):
    held = {0: block}
    while bit:
        for k in list(held):
            held[k ^ bit] = swap_bits(held[k], axis, bit)
        bit //= 2
    return [held[k] for k in range(len(held))]


def add_rounded(one, other):
    return (one.astype(jnp.float32) + other.astype(jnp.float32)).astype(jnp.bfloat16)


def staged_gather(block, images, noise, routes, near_bits, far_bit):
    routes = swap_all(routes)
    far_images, *routes = lax.optimization_barrier((images, *routes))
    near = swap_gather(images, "reader", near_bits)
    crossed = swap_bits(far_images, "reader", far_bit)
    side = lax.ppermute(block, "blk", SIDES)
    across = lax.ppermute(block, "blk", MIDDLE)
    end = lax.ppermute(block, "blk", ENDS)
    side, across = lax.optimization_barrier((side, across))
    far = lax.ppermute(across, "blk", SIDES)
    across_far = lax.ppermute(side, "blk", MIDDLE)
    staged = stage([[block], [side], None, [end, across]], near, noise)
    crossed, far, across_far, *staged = lax.optimization_barrier(
        (crossed, far, across_far, *staged)
    )
    return staged, [far, across_far], swap_gather(crossed, "reader", near_bits), routes


def swap_all(routes):
    return [routes] + [swap_bits(routes, "reader", k) for k in range(1, lax.axis_size("reader"))]


def plain_gather(block, images, noise, routes, near_bits, far_bit):
    near = swap_gather(images, "reader", near_bits)
    far = swap_gather(swap_bits(images, "reader", far_bit), "reader", near_bits)
    line = line_gather(block, "blk")
    staged = stage([[one] for one in line[:2]] + [None] + [[one] for one in line[3:]], near, noise)
    return staged, [line[2]], far, swap_all(routes)


def line_gather(block, axis):
    size, member = lax.axis_size(axis), lax.axis_index(axis)
    ahead, behind = [block], [block]
    for s in range(1, size):
        ahead.append(lax.ppermute(ahead[-1], axis, [(i, i + 1) for i in range(s - 1, size - 1)]))
        behind.append(lax.ppermute(behind[-1], axis, [(i, i - 1) for i in range(1, size - s + 1)]))
    blocks = [block]
    for s in range(1, size):
        blocks.append(jnp.where(member >= s, ahead[s], behind[size - s]))
    return blocks


def pair_scatter(pieces, axis):
    member = lax.axis_index(axis)
    is_end = (member == 0) | (member == 3)
    for_far_end = [lax.ppermute(parts[3], axis, SIDES) for parts in pieces]
    *second, for_far_end[0] = lax.optimization_barrier(
        [parts[2] for parts in pieces] + for_far_end[:1]
    )
    for_far_middle = [lax.ppermute(part, axis, SIDES) for part in second]
    totals = []
    for parts, part, end, middle in zip(pieces, second, for_far_end, for_far_middle):
        across_end = lax.ppermute(add_rounded(part, end), axis, MIDDLE)
        across_middle = lax.ppermute(add_rounded(parts[3], middle), axis, MIDDLE)
        near = jnp.where(is_end, parts[1], add_rounded(parts[1], across_end))
        from_side = lax.ppermute(near, axis, SIDES)
        total = parts[0].astype(jnp.float32) + from_side.astype(jnp.float32)
        totals.append(total + jnp.where(is_end, 0.0, across_middle.astype(jnp.float32)))
    return totals


def line_scatter(pieces, axis):
    return [line_sum(parts, axis) for parts in pieces]


def line_sum(parts, axis):
    size = lax.axis_size(axis)
    up = down = None
    for s in range(1, size):
        send_up, send_down = parts[s], parts[size - s]
        if s > 1:
            send_up = add_rounded(send_up, up)
            send_down = add_rounded(send_down, down)
        up = lax.ppermute(send_up, axis, [(i, i + 1) for i in range(0, s) if i + 1 < size])
        down = lax.ppermute(send_down, axis, [(i, i - 1) for i in range(size - s, size) if i > 0])
    total = parts[0].astype(jnp.float32)
    if size > 1:
        total = total + up.astype(jnp.float32) + down.astype(jnp.float32)
    return total


def column_lse(scores):
    peak = jnp.max(scores, axis=0, keepdims=True)
    total = jnp.sum(jnp.exp(scores - peak), axis=0, keepdims=True)
    return peak + jnp.log(total)


def at_end():
    member = lax.axis_index("blk")
    return (member == 0) | (member == lax.axis_size("blk") - 1)


def either(refs, act):
    if len(refs) == 1:
        act(refs[0])
        return
    is_end = at_end()

    @pl.when(is_end)
    def _():
        act(refs[0])

    @pl.when(jnp.logical_not(is_end))
    def _():
        act(refs[1])


def weigh(block_ref, noise_ref, weighted_ref, penalty_ref, start):
    count, width = block_ref.shape
    rows = slice(start, start + count)
    penalty = jnp.zeros((count, 1), jnp.float32)
    for column in range(0, width, STEP):
        columns = slice(column, column + STEP)
        block = block_ref[:, columns].astype(jnp.float32)
        scaled = block * noise_ref[:, columns]
        weighted_ref[rows, columns] = scaled.astype(jnp.bfloat16)
        penalty = penalty + 0.5 * jnp.sum(scaled * block, axis=1, keepdims=True)
    penalty_ref[rows, :] = penalty


def stage_kernel(near_count, counts, *refs):
    refs = list(refs)
    near_refs = [refs.pop(0) for _ in range(near_count)]
    pair_refs = [[refs.pop(0) for _ in range(n)] for n in counts]
    noise_ref, weighted_ref, penalty_ref, near_ref, noise_out_ref, block_ref, near_sems, sems = refs
    rows = near_refs[0].shape[0]
    count = block_ref.shape[1]
    copies = []
    for k, ref in enumerate(near_refs):
        copy = pltpu.make_async_copy(ref, near_ref.at[pl.ds(k * rows, rows), :], near_sems.at[k])
        copy.start()
        copies.append(copy)

    def block_copy(s, ref):
        return pltpu.make_async_copy(ref, block_ref.at[s], sems.at[s])

    for s, pair in enumerate(pair_refs):
        if pair:
            either(pair, lambda ref, s=s: block_copy(s, ref).start())
    noise_out_ref[...] = noise_ref[...]
    for s, pair in enumerate(pair_refs):
        if pair:
            block_copy(s, pair[0]).wait()
            weigh(block_ref.at[s], noise_ref, weighted_ref, penalty_ref, s * count)
        else:
            weighted_ref[s * count : (s + 1) * count, :] = jnp.zeros(
                (count, weighted_ref.shape[1]), jnp.bfloat16
            )
            penalty_ref[s * count : (s + 1) * count, :] = jnp.zeros((count, 1), jnp.float32)
    for copy in copies:
        copy.wait()


def stage(pairs, near, noise):
    count, width = pairs[0][0].shape
    refs = len(pairs) * count
    moved = [*near, *[one for pair in pairs for one in pair or []]]
    return pl.pallas_call(
        partial(stage_kernel, len(near), [len(pair or []) for pair in pairs]),
        out_shape=(
            jax.ShapeDtypeStruct((refs, width), jnp.bfloat16),
            jax.ShapeDtypeStruct((refs, 1), jnp.float32),
            jax.ShapeDtypeStruct((len(near) * near[0].shape[0], width), jnp.bfloat16),
            jax.ShapeDtypeStruct((1, width), jnp.float32),
        ),
        in_specs=[ANY_SPEC] * len(moved) + [VMEM_SPEC],
        out_specs=(VMEM_SPEC,) * 4,
        scratch_shapes=[
            pltpu.VMEM((len(pairs), count, width), jnp.bfloat16),
            pltpu.SemaphoreType.DMA((len(near),)),
            pltpu.SemaphoreType.DMA((len(pairs),)),
        ],
        compiler_params=pltpu.CompilerParams(vmem_limit_bytes=SCORE_VMEM),
        cost_estimate=pl.CostEstimate(
            flops=8 * refs * width, bytes_accessed=24_000_000, transcendentals=0
        ),
        name="stage",
    )(*moved, noise)


def score_kernel(readers, last_count, finish, *refs):
    refs = list(refs)
    near_ref = refs.pop(0)
    rows = near_ref.shape[0] * 2 // readers
    far_refs = [refs.pop(0) for _ in range(readers // 2)]
    last_refs = [refs.pop(0) for _ in range(last_count)]
    staged_ref, staged_penalty_ref, noise_ref = [refs.pop(0) for _ in range(3)]
    route_refs = [refs.pop(0) for _ in range(readers)]
    score_ref, mask_ref, lse_ref, all_ref = refs[:4]
    block_ref, weighted_ref, penalty_ref, image_sems, block_sem = refs[4:]
    reader = lax.axis_index("reader")
    count, width = block_ref.shape

    def block_copy(ref):
        return pltpu.make_async_copy(ref, block_ref, block_sem)

    either(last_refs, lambda ref: block_copy(ref).start())
    copies = []
    for k in range(readers):
        row = pl.multiple_of((reader ^ k) * rows, 16)
        if k < readers // 2:
            source = near_ref.at[pl.ds(k * rows, rows), :]
        else:
            source = far_refs[k - readers // 2]
        copy = pltpu.make_async_copy(source, all_ref.at[pl.ds(row, rows), :], image_sems.at[k])
        copy.start()
        copies.append(copy)
    routes = [ref[...] for ref in route_refs]
    bit = 1
    while bit < readers:
        flip = (reader & bit) > 0
        routes = [jnp.where(flip, routes[k ^ bit], one) for k, one in enumerate(routes)]
        bit *= 2
    for j, route in enumerate(routes):
        for k in range(readers):
            hits = jnp.where(route == (reader ^ k), 1.0, 0.0)
            mask_ref[k : k + 1, j * rows : (j + 1) * rows] = jnp.max(hits, axis=0, keepdims=True)
    weighted_ref[...] = staged_ref[...]
    penalty_ref[...] = staged_penalty_ref[...]
    block_copy(last_refs[0]).wait()
    weigh(block_ref, noise_ref, weighted_ref, penalty_ref, 2 * count)
    for copy in copies:
        copy.wait()
    scores = lax.dot_general(
        all_ref[...],
        weighted_ref[...],
        (((1,), (1,)), ((), ())),
        preferred_element_type=jnp.float32,
    )
    scores = scores.T - penalty_ref[...]
    score_ref[...] = scores
    if finish:
        lse_ref[...] = column_lse(scores)


def all_scores(staged, last, far, routes, finish):
    weighted, penalty, near, noise = staged
    count, width = last[0].shape
    refs = weighted.shape[0]
    slots = 2 * near.shape[0]
    moved = [near, *far, *last]
    return pl.pallas_call(
        partial(score_kernel, len(routes), len(last), finish),
        out_shape=(
            jax.ShapeDtypeStruct((refs, slots), jnp.float32),
            jax.ShapeDtypeStruct((len(routes), slots), jnp.float32),
            jax.ShapeDtypeStruct((1, slots), jnp.float32),
            jax.ShapeDtypeStruct((slots, width), jnp.bfloat16),
        ),
        in_specs=[ANY_SPEC] * len(moved) + [VMEM_SPEC] * (3 + len(routes)),
        out_specs=(VMEM_SPEC,) * 4,
        scratch_shapes=[
            pltpu.VMEM((count, width), jnp.bfloat16),
            pltpu.VMEM((refs, width), jnp.bfloat16),
            pltpu.VMEM((refs, 1), jnp.float32),
            pltpu.SemaphoreType.DMA((len(routes),)),
            pltpu.SemaphoreType.DMA,
        ],
        compiler_params=pltpu.CompilerParams(vmem_limit_bytes=SCORE_VMEM),
        cost_estimate=pl.CostEstimate(
            flops=2 * refs * slots * width,
            bytes_accessed=2 * (slots + refs) * width,
            transcendentals=0,
        ),
        name="scores",
    )(*moved, weighted, penalty, noise, *routes)


def lse_kernel(score_ref, lse_ref):
    lse_ref[...] = column_lse(score_ref[...])


def group_lse(scores):
    return pl.pallas_call(
        lse_kernel,
        out_shape=jax.ShapeDtypeStruct((1, scores.shape[1]), jnp.float32),
        name="group_lse",
    )(scores)


def sums_kernel(readers, members, pieces, all_ref, score_ref, mask_ref, *refs):
    lse_refs, norm_ref, out_refs = refs[:readers], refs[readers], refs[readers + 1 :]
    kept = []
    for k, lse_ref in enumerate(lse_refs):
        kept.append(jnp.where(mask_ref[k : k + 1, :] > 0.0, lse_ref[...], -jnp.inf))
    highest = kept[0]
    for value in kept[1:]:
        highest = jnp.maximum(highest, value)
    spread = jnp.exp(kept[0] - highest)
    for value in kept[1:]:
        spread = spread + jnp.exp(value - highest)
    norm = highest + jnp.log(spread)
    norm_ref[...] = norm
    exponent = jnp.where(mask_ref[0:1, :] > 0.0, score_ref[...] - norm, -jnp.inf)
    posterior = jnp.exp(exponent).astype(jnp.bfloat16)
    count = posterior.shape[0] // members
    for q, piece in enumerate(pieces):
        sums = jnp.dot(posterior, all_ref[:, piece], preferred_element_type=jnp.float32)
        for s, out_ref in enumerate(out_refs[q * members : (q + 1) * members]):
            out_ref[...] = sums[s * count : (s + 1) * count].astype(out_ref.dtype)


def group_sums(members, pieces, all_images, scores, masks, lses):
    refs, slots = scores.shape
    width = all_images.shape[1]
    blocks = [
        jax.ShapeDtypeStruct((refs // members, piece.stop - piece.start), jnp.bfloat16)
        for piece in pieces
        for _ in range(members)
    ]
    norms, *outs = pl.pallas_call(
        partial(sums_kernel, len(lses), members, pieces),
        out_shape=(jax.ShapeDtypeStruct((1, slots), jnp.float32), *blocks),
        in_specs=[VMEM_SPEC] * (3 + len(lses)),
        out_specs=(VMEM_SPEC,) * (1 + len(blocks)),
        compiler_params=pltpu.CompilerParams(vmem_limit_bytes=SUMS_VMEM),
        cost_estimate=pl.CostEstimate(
            flops=2 * refs * slots * width,
            bytes_accessed=2 * slots * width,
            transcendentals=0,
        ),
        name="sums",
    )(all_images, scores, masks, *lses)
    return norms, [outs[q * members : (q + 1) * members] for q in range(len(pieces))]


def on_device(images, routes, projections, noise_weights):
    readers = lax.axis_size("reader")
    members = lax.axis_size("blk")
    reader = lax.axis_index("reader")
    rows, width = images.shape
    noise = noise_weights.reshape(1, width)

    gather = staged_gather if members == 4 and rows % 32 == 0 else plain_gather
    staged, last, far, route_blocks = gather(
        projections[0], images, noise, routes.T, readers // 4, readers // 2
    )
    split = lax.axis_size("sub") > 1
    scores, masks, mine, all_images = all_scores(staged, last, far, route_blocks, not split)
    if split:
        scores = lax.psum(scores, "sub")
        mine = group_lse(scores)
    lses = [mine] + [swap_bits(mine, "reader", k) for k in range(1, readers)]
    pieces = [slice(0, width // 2), slice(width // 2, width)]
    norms, parts = group_sums(members, pieces, all_images, scores, masks, lses)
    scatter = pair_scatter if members == 4 else line_scatter
    totals = scatter(parts, "blk")
    normalizer = lax.dynamic_slice(norms.reshape(-1), (reader * rows,), (rows,))
    return (jnp.concatenate(totals, axis=1)[None], normalizer)


def solution(mesh):
    return jax.shard_map(
        on_device,
        mesh=mesh,
        in_specs=(
            P(("parts", "blk", "reader"), "sub"),
            P(("parts", "blk", "reader"), None),
            P(("parts", "reader"), "blk", "sub"),
            P(("parts", "sub")),
        ),
        out_specs=(P(("parts", "reader"), "blk", "sub"), P(("parts", "blk", "reader"))),
        check_vma=False,
    )
```

time: 113 us -> 100 us (0.88)
  waiting for transfers between devices: 57 us -> 37.4 us
  starting transfers between devices: 43.6 us -> 50.8 us
    ppermute x1, starting transfers between devices: 0.78 us -> 15.5 us  [staged_gather(): far = lax.ppermute(across, 'blk', SIDES)]
    ppermute x1, waiting for transfers between devices: 11.6 us -> 0.01 us  [staged_gather(): end = lax.ppermute(block, 'blk', ENDS)]
    ppermute x2, waiting for transfers between devices: 9.43 us -> 0.01 us  [pair_scatter(): for_far_middle = [lax.ppermute(part, axis, SIDES) for part in second]]
    ppermute x2, starting transfers between devices: 16 us -> 9.72 us  [pair_scatter(): from_side = lax.ppermute(near, axis, SIDES)]
    ppermute x2, waiting for transfers between devices: 4.23 us -> 9.67 us  [pair_scatter(): from_side = lax.ppermute(near, axis, SIDES)]
    ppermute x1, waiting for transfers between devices: 10.9 us -> 6 us  [staged_gather(): far = lax.ppermute(across, 'blk', SIDES)]
    ppermute x2, starting transfers between devices: 6.58 us -> 3.77 us  [pair_scatter(): for_far_end = [lax.ppermute(parts[3], axis, SIDES) for parts in pieces]]
    ppermute x2, starting transfers between devices: 2.03 us -> 4.81 us  [pair_scatter(): for_far_middle = [lax.ppermute(part, axis, SIDES) for part in second]]
where the time goes in v8:
time: 100 us; the launch traced here: 99.7 us
  starting transfers between devices  50.8 us (51%)
  waiting for transfers between devices  37.4 us (37%)
  Pallas kernels  5.16 us (5%)
  local copies, waits for them, and re-layouts  3.78 us (4%)
  other arithmetic  1.66 us (2%)
    ppermute x1, starting transfers between devices, staged_gather(): far = lax.ppermute(across, 'blk', SIDES)  15.5 us
    ppermute x2, starting transfers between devices, pair_scatter(): from_side = lax.ppermute(near, axis, SIDES)  9.72 us
    ppermute x2, waiting for transfers between devices, pair_scatter(): from_side = lax.ppermute(near, axis, SIDES)  9.67 us
    ppermute x9, waiting for transfers between devices, swap_bits(): lax.ppermute(block, axis, [(i, i ^ bits) for i in range(lax.axis_size(axi...  8.68 us
    ppermute x1, waiting for transfers between devices, staged_gather(): side = lax.ppermute(block, 'blk', SIDES)  6.58 us
    ppermute x2, waiting for transfers between devices, pair_scatter(): for_far_end = [lax.ppermute(parts[3], axis, SIDES) for parts in pieces]  6.49 us
    ppermute x9, starting transfers between devices, swap_bits(): lax.ppermute(block, axis, [(i, i ^ bits) for i in range(lax.axis_size(axi...  6.02 us
    ppermute x1, waiting for transfers between devices, staged_gather(): far = lax.ppermute(across, 'blk', SIDES)  6 us
  transfers between devices with their start and end apart: 24, of which 12 were waited for; matrix products, arithmetic and copies ran while one was open for 1% of the time, Pallas kernels for 1%

profile of v8, /device:TPU:0, one launch (start us, length us, event | category | flops | bytes accessed | tf_op | source)
XLA Modules:
  0.0 99.7 jit_solution(6826706936626398991)
XLA Ops:
  1.2 2.9 %collective-permute-start.1 = (s32[2,96]{1,0:T(2,128)}, s32[2,96]{1,0:T(2,128)S(1)}, u32[]{:S(2)}, u32[]{:S(2)}) collective-permute-start(s32[2,96]{1,0:T(2,128)} %bitcast.13), channel_id=1, source_target_pairs={{0,2},{1,3},{2,0},{3,1},{4,6},{5,7},{6,4},{7,5},{8,10},{9,11},{10,... | collective-permute-start | bytes 2312 | tf_op jit(solution)/shard_map/ppermute | solution.py:21
  4.4 1.5 %collective-permute-done.1.refs_10_ = s32[2,96]{1,0:T(2,128)S(1)} collective-permute-done((s32[2,96]{1,0:T(2,128)}, s32[2,96]{1,0:T(2,128)S(1)}, u32[]{:S(2)}, u32[]{:S(2)}) %collective-permute-start.1) | collective-permute-done | bytes 800 | tf_op jit(solution)/shard_map/ppermute | solution.py:21
  5.9 1.4 %collective-permute-done.2.refs_11_ = s32[2,96]{1,0:T(2,128)S(1)} collective-permute-done((s32[2,96]{1,0:T(2,128)}, s32[2,96]{1,0:T(2,128)S(1)}, u32[]{:S(2)}, u32[]{:S(2)}) %collective-permute-start.2) | collective-permute-done | bytes 800 | tf_op jit(solution)/shard_map/ppermute | solution.py:21
  7.9 1.6 %collective-permute-start.4 = (bf16[32,8192]{1,0:T(8,128)(2,1)}, bf16[32,8192]{1,0:T(8,128)(2,1)S(1)}, u32[]{:S(2)}, u32[]{:S(2)}) collective-permute-start(bf16[32,8192]{1,0:T(8,128)(2,1)} %bitcast.7), channel_id=1, source_target_pairs={{0,4},{4,0},{8,12},{12,8},{1,5},{5,1},{9,13},{13,9},{2,6},{6,2},{1... | collective-permute-start | bytes 1572872 | tf_op jit(solution)/shard_map/ppermute | solution.py:42
  9.5 1.7 %collective-permute-start.5 = (bf16[32,8192]{1,0:T(8,128)(2,1)}, bf16[32,8192]{1,0:T(8,128)(2,1)S(1)}, u32[]{:S(2)}, u32[]{:S(2)}) collective-permute-start(bf16[32,8192]{1,0:T(8,128)(2,1)} %bitcast.8), channel_id=1, source_target_pairs={{4,8},{8,4},{0,0},{12,12},{5,9},{9,5},{1,1},{13,13},{6,10},{10,6},... | collective-permute-start | bytes 1572872 | tf_op jit(solution)/shard_map/ppermute | solution.py:43
  11.2 4.4 %collective-permute-start.9 = (bf16[32,8192]{1,0:T(8,128)(2,1)}, bf16[32,8192]{1,0:T(8,128)(2,1)S(1)}, u32[]{:S(2)}, u32[]{:S(2)}) collective-permute-start(bf16[32,8192]{1,0:T(8,128)(2,1)} %bitcast.9), channel_id=1, source_target_pairs={{0,12},{12,0},{4,4},{8,8},{1,13},{13,1},{5,5},{9,9},{2,14},{14,2},... | collective-permute-start | bytes 1572872 | tf_op jit(solution)/shard_map/ppermute | solution.py:44
  15.6 6.6 %collective-permute-done.4.refs_3_ = bf16[32,8192]{1,0:T(8,128)(2,1)S(1)} collective-permute-done((bf16[32,8192]{1,0:T(8,128)(2,1)}, bf16[32,8192]{1,0:T(8,128)(2,1)S(1)}, u32[]{:S(2)}, u32[]{:S(2)}) %collective-permute-start.4) | collective-permute-done | bytes 524320 | tf_op jit(solution)/shard_map/ppermute | solution.py:42
  22.2 15.5 %collective-permute-start.6 = (bf16[32,8192]{1,0:T(8,128)(2,1)S(1)}, bf16[32,8192]{1,0:T(8,128)(2,1)S(1)}, u32[]{:S(2)}, u32[]{:S(2)}) collective-permute-start(bf16[32,8192]{1,0:T(8,128)(2,1)S(1)} %collective-permute-done.5.refs_5_), channel_id=1, source_target_pairs={{0,4},{4,0},{8,12},{12,8},{1,5},{5,1},{9,13},{13,9},{2,6},{6,2},{1... | collective-permute-start | bytes 1572872 | tf_op jit(solution)/shard_map/ppermute | solution.py:46
  38.4 1.4 %copy-done = bf16[96,8192]{1,0:T(8,128)(2,1)S(1)} copy-done((bf16[96,8192]{1,0:T(8,128)(2,1)S(1)}, bf16[96,8192]{1,0:T(8,128)(2,1)}, u32[]{:S(2)}) %copy-start) | copy-done | bytes 1572888
  39.8 1.0 %copy-done.1 = bf16[1,32,8192]{2,1,0:T(8,128)(2,1)S(1)} copy-done((bf16[1,32,8192]{2,1,0:T(8,128)(2,1)S(1)}, bf16[1,32,8192]{2,1,0:T(8,128)(2,1)}, u32[]{:S(2)}) %copy-start.1) | copy-done | bytes 524312
  41.6 1.1 %stage.1 = (bf16[128,8192]{1,0:T(8,128)(2,1)S(1)}, f32[128,1]{1,0:T(8,128)S(1)}, bf16[192,8192]{1,0:T(8,128)(2,1)S(1)}, f32[1,8192]{1,0:T(1,128)S(1)}) custom-call(bf16[96,8192]{1,0:T(8,128)(2,1)S(1)} %copy-done, bf16[96,8192]{1,0:T(8,128)(2,1)S(1)} %collective-permute-done.8.refs_1_, bf16[32,8192]{1,0:T(8,128)(2,1)S(1)} %bitcast.10, ...), custom_call_target="tpu_custom_call" | custom-call | flops 8388608 | bytes 24000000 | tf_op jit(solution)/shard_map/stage/pallas_call | solution.py:194
  42.7 6.0 %collective-permute-done.6.refs_3_ = bf16[32,8192]{1,0:T(8,128)(2,1)S(1)} collective-permute-done((bf16[32,8192]{1,0:T(8,128)(2,1)S(1)}, bf16[32,8192]{1,0:T(8,128)(2,1)S(1)}, u32[]{:S(2)}, u32[]{:S(2)}) %collective-permute-start.6) | collective-permute-done | bytes 524320 | tf_op jit(solution)/shard_map/ppermute | solution.py:46
  48.7 3.4 %collective-permute-done.10.refs_2_ = bf16[96,8192]{1,0:T(8,128)(2,1)S(1)} collective-permute-done((bf16[96,8192]{1,0:T(8,128)(2,1)S(1)}, bf16[96,8192]{1,0:T(8,128)(2,1)S(1)}, u32[]{:S(2)}, u32[]{:S(2)}) %collective-permute-start.10) | collective-permute-done | bytes 1572896 | tf_op jit(solution)/shard_map/ppermute | solution.py:21
  52.1 2.8 %scores.1 = (f32[128,384]{1,0:T(8,128)S(1)}, f32[4,384]{1,0:T(4,128)S(1)}, f32[1,384]{1,0:T(1,128)S(1)}, bf16[384,8192]{1,0:T(8,128)(2,1)S(1)}) custom-call(bf16[192,8192]{1,0:T(8,128)(2,1)S(1)} %get-tuple-element.43.refs_0_, bf16[96,8192]{1,0:T(8,128)(2,1)S(1)} %collective-permute-done.3.refs_1_, bf16[96,8192]{1,0:T(8,128)(2,1)S(1)} %collective-permute-done.10.refs_2_, ...), custom_call_target="tpu_custom_call" | custom-call | flops 805306368 | bytes 8388608 | tf_op jit(solution)/shard_map/scores/pallas_call | solution.py:278
  56.8 1.9 %collective-permute-done.12.refs_2_ = f32[1,384]{1,0:T(1,128)S(1)} collective-permute-done((f32[1,384]{1,0:T(1,128)S(1)}, f32[1,384]{1,0:T(1,128)S(1)}, u32[]{:S(2)}, u32[]{:S(2)}) %collective-permute-start.12) | collective-permute-done | bytes 1568 | tf_op jit(solution)/shard_map/ppermute | solution.py:21
  58.9 1.3 %sums.1 = (f32[1,384]{1,0:T(1,128)S(1)}, bf16[32,4096]{1,0:T(8,128)(2,1)S(1)}, bf16[32,4096]{1,0:T(8,128)(2,1)S(1)}, bf16[32,4096]{1,0:T(8,128)(2,1)S(1)}, bf16[...) custom-call(bf16[384,8192]{1,0:T(8,128)(2,1)S(1)} %get-tuple-element, ...), custom_call_target="tpu_custom_call" | custom-call | flops 805306368 | bytes 6291456 | tf_op jit(solution)/shard_map/sums/pallas_call | solution.py:347
  60.2 3.7 %collective-permute-start.14 = (bf16[32,4096]{1,0:T(8,128)(2,1)S(1)}, bf16[32,4096]{1,0:T(8,128)(2,1)S(1)}, u32[]{:S(2)}, u32[]{:S(2)}) collective-permute-start(bf16[32,4096]{1,0:T(8,128)(2,1)S(1)} %get-tuple-element.62), channel_id=1, source_target_pairs={{0,4},{4,0},{8,12},{12,8},{1,5},{5,1},{9,13},{13,9},{2,6},{6,2},{1... | collective-permute-start | bytes 786440 | tf_op jit(solution)/shard_map/ppermute | solution.py:82
  64.5 6.4 %collective-permute-done.14 = bf16[32,4096]{1,0:T(8,128)(2,1)S(1)} collective-permute-done((bf16[32,4096]{1,0:T(8,128)(2,1)S(1)}, bf16[32,4096]{1,0:T(8,128)(2,1)S(1)}, u32[]{:S(2)}, u32[]{:S(2)}) %collective-permute-start.14) | collective-permute-done | bytes 262176 | tf_op jit(solution)/shard_map/ppermute | solution.py:82
  70.9 2.1 %collective-permute-start.17 = (bf16[32,4096]{1,0:T(8,128)(2,1)S(1)}, bf16[32,4096]{1,0:T(8,128)(2,1)S(1)}, u32[]{:S(2)}, u32[]{:S(2)}) collective-permute-start(bf16[32,4096]{1,0:T(8,128)(2,1)S(1)} %get-tuple-element.63), channel_id=1, source_target_pairs={{0,4},{4,0},{8,12},{12,8},{1,5},{5,1},{9,13},{13,9},{2,6},{6,2},{1... | collective-permute-start | bytes 786440 | tf_op jit(solution)/shard_map/ppermute | solution.py:86
  73.8 2.7 %collective-permute-start.22 = (bf16[32,4096]{1,0:T(8,128)(2,1)S(1)}, bf16[32,4096]{1,0:T(8,128)(2,1)S(1)}, u32[]{:S(2)}, u32[]{:S(2)}) collective-permute-start(bf16[32,4096]{1,0:T(8,128)(2,1)S(1)} %get-tuple-element.67), channel_id=1, source_target_pairs={{0,4},{4,0},{8,12},{12,8},{1,5},{5,1},{9,13},{13,9},{2,6},{6,2},{1... | collective-permute-start | bytes 786440 | tf_op jit(solution)/shard_map/ppermute | solution.py:86
  77.4 5.0 %collective-permute-start.16 = (bf16[32,4096]{1,0:T(8,128)(2,1)S(1)}, bf16[32,4096]{1,0:T(8,128)(2,1)S(1)}, u32[]{:S(2)}, u32[]{:S(2)}) collective-permute-start(bf16[32,4096]{1,0:T(8,128)(2,1)S(1)} %fusion), channel_id=1, source_target_pairs={{0,4},{4,0},{8,12},{12,8},{1,5},{5,1},{9,13},{13,9},{2,6},{6,2},{1... | collective-permute-start | bytes 786440 | tf_op jit(solution)/shard_map/ppermute | solution.py:92
  83.2 4.8 %collective-permute-start.21 = (bf16[32,4096]{1,0:T(8,128)(2,1)S(1)}, bf16[32,4096]{1,0:T(8,128)(2,1)S(1)}, u32[]{:S(2)}, u32[]{:S(2)}) collective-permute-start(bf16[32,4096]{1,0:T(8,128)(2,1)S(1)} %fusion.1), channel_id=1, source_target_pairs={{0,4},{4,0},{8,12},{12,8},{1,5},{5,1},{9,13},{13,9},{2,6},{6,2},{1... | collective-permute-start | bytes 786440 | tf_op jit(solution)/shard_map/ppermute | solution.py:92
  88.7 4.7 %collective-permute-done.16 = bf16[32,4096]{1,0:T(8,128)(2,1)S(1)} collective-permute-done((bf16[32,4096]{1,0:T(8,128)(2,1)S(1)}, bf16[32,4096]{1,0:T(8,128)(2,1)S(1)}, u32[]{:S(2)}, u32[]{:S(2)}) %collective-permute-start.16) | collective-permute-done | bytes 262176 | tf_op jit(solution)/shard_map/ppermute | solution.py:92
  93.5 5.0 %collective-permute-done.21 = bf16[32,4096]{1,0:T(8,128)(2,1)S(1)} collective-permute-done((bf16[32,4096]{1,0:T(8,128)(2,1)S(1)}, bf16[32,4096]{1,0:T(8,128)(2,1)S(1)}, u32[]{:S(2)}, u32[]{:S(2)}) %collective-permute-start.21) | collective-permute-done | bytes 262176 | tf_op jit(solution)/shard_map/ppermute | solution.py:92
  (45 shorter events, 10.1 us)
Async XLA Ops:
  0.6 37.7 %collective-permute-start.8 = (bf16[96,8192]{1,0:T(8,128)(2,1)}, bf16[96,8192]{1,0:T(8,128)(2,1)S(1)}, u32[]{:S(2)}, u32[]{:S(2)}) collective-permute-start(bf16[96,8192]{1,0:T(8,128)(2,1)} %refs_0_.1), channel_id=1, source_target_pairs={{0,1},{1,0},{2,3},{3,2},{4,5},{5,4},{6,7},{7,6},{8,9},{9,8},{10,11... | collective-permute-start | bytes 4718600 | tf_op jit(solution)/shard_map/ppermute | solution.py:21
  1.1 3.2 %collective-permute-start = (s32[2,96]{1,0:T(2,128)}, s32[2,96]{1,0:T(2,128)S(1)}, u32[]{:S(2)}, u32[]{:S(2)}) collective-permute-start(s32[2,96]{1,0:T(2,128)} %bitcast.12), channel_id=1, source_target_pairs={{0,1},{1,0},{2,3},{3,2},{4,5},{5,4},{6,7},{7,6},{8,9},{9,8},{10,11... | collective-permute-start | bytes 2312 | tf_op jit(solution)/shard_map/ppermute | solution.py:21
  1.2 4.7 %collective-permute-start.1 = (s32[2,96]{1,0:T(2,128)}, s32[2,96]{1,0:T(2,128)S(1)}, u32[]{:S(2)}, u32[]{:S(2)}) collective-permute-start(s32[2,96]{1,0:T(2,128)} %bitcast.13), channel_id=1, source_target_pairs={{0,2},{1,3},{2,0},{3,1},{4,6},{5,7},{6,4},{7,5},{8,10},{9,11},{10,... | collective-permute-start | bytes 2312 | tf_op jit(solution)/shard_map/ppermute | solution.py:21
  4.1 3.2 %collective-permute-start.2 = (s32[2,96]{1,0:T(2,128)}, s32[2,96]{1,0:T(2,128)S(1)}, u32[]{:S(2)}, u32[]{:S(2)}) collective-permute-start(s32[2,96]{1,0:T(2,128)} %bitcast.14), channel_id=1, source_target_pairs={{0,3},{1,2},{2,1},{3,0},{4,7},{5,6},{6,5},{7,4},{8,11},{9,10},{10,... | collective-permute-start | bytes 2312 | tf_op jit(solution)/shard_map/ppermute | solution.py:21
  7.4 41.3 %collective-permute-start.3 = (bf16[96,8192]{1,0:T(8,128)(2,1)}, bf16[96,8192]{1,0:T(8,128)(2,1)S(1)}, u32[]{:S(2)}, u32[]{:S(2)}) collective-permute-start(bf16[96,8192]{1,0:T(8,128)(2,1)} %refs_0_.1), channel_id=1, source_target_pairs={{0,2},{1,3},{2,0},{3,1},{4,6},{5,7},{6,4},{7,5},{8,10},{9,11},{10,... | collective-permute-start | bytes 4718600 | tf_op jit(solution)/shard_map/ppermute | solution.py:21
  7.9 14.2 %collective-permute-start.4 = (bf16[32,8192]{1,0:T(8,128)(2,1)}, bf16[32,8192]{1,0:T(8,128)(2,1)S(1)}, u32[]{:S(2)}, u32[]{:S(2)}) collective-permute-start(bf16[32,8192]{1,0:T(8,128)(2,1)} %bitcast.7), channel_id=1, source_target_pairs={{0,4},{4,0},{8,12},{12,8},{1,5},{5,1},{9,13},{13,9},{2,6},{6,2},{1... | collective-permute-start | bytes 1572872 | tf_op jit(solution)/shard_map/ppermute | solution.py:42
  9.5 12.6 %collective-permute-start.5 = (bf16[32,8192]{1,0:T(8,128)(2,1)}, bf16[32,8192]{1,0:T(8,128)(2,1)S(1)}, u32[]{:S(2)}, u32[]{:S(2)}) collective-permute-start(bf16[32,8192]{1,0:T(8,128)(2,1)} %bitcast.8), channel_id=1, source_target_pairs={{4,8},{8,4},{0,0},{12,12},{5,9},{9,5},{1,1},{13,13},{6,10},{10,6},... | collective-permute-start | bytes 1572872 | tf_op jit(solution)/shard_map/ppermute | solution.py:43
  11.2 27.1 %collective-permute-start.9 = (bf16[32,8192]{1,0:T(8,128)(2,1)}, bf16[32,8192]{1,0:T(8,128)(2,1)S(1)}, u32[]{:S(2)}, u32[]{:S(2)}) collective-permute-start(bf16[32,8192]{1,0:T(8,128)(2,1)} %bitcast.9), channel_id=1, source_target_pairs={{0,12},{12,0},{4,4},{8,8},{1,13},{13,1},{5,5},{9,9},{2,14},{14,2},... | collective-permute-start | bytes 1572872 | tf_op jit(solution)/shard_map/ppermute | solution.py:44
  22.2 26.5 %collective-permute-start.6 = (bf16[32,8192]{1,0:T(8,128)(2,1)S(1)}, bf16[32,8192]{1,0:T(8,128)(2,1)S(1)}, u32[]{:S(2)}, u32[]{:S(2)}) collective-permute-start(bf16[32,8192]{1,0:T(8,128)(2,1)S(1)} %collective-permute-done.5.refs_5_), channel_id=1, source_target_pairs={{0,4},{4,0},{8,12},{12,8},{1,5},{5,1},{9,13},{13,9},{2,6},{6,2},{1... | collective-permute-start | bytes 1572872 | tf_op jit(solution)/shard_map/ppermute | solution.py:46
  37.6 11.0 %collective-permute-start.7 = (bf16[32,8192]{1,0:T(8,128)(2,1)S(1)}, bf16[32,8192]{1,0:T(8,128)(2,1)S(1)}, u32[]{:S(2)}, u32[]{:S(2)}) collective-permute-start(bf16[32,8192]{1,0:T(8,128)(2,1)S(1)} %collective-permute-done.4.refs_3_), channel_id=1, source_target_pairs={{4,8},{8,4},{0,0},{12,12},{5,9},{9,5},{1,1},{13,13},{6,10},{10,6},... | collective-permute-start | bytes 1572872 | tf_op jit(solution)/shard_map/ppermute | solution.py:47
  48.7 3.4 %collective-permute-start.10 = (bf16[96,8192]{1,0:T(8,128)(2,1)S(1)}, bf16[96,8192]{1,0:T(8,128)(2,1)S(1)}, u32[]{:S(2)}, u32[]{:S(2)}) collective-permute-start(bf16[96,8192]{1,0:T(8,128)(2,1)S(1)} %collective-permute-done.3.refs_1_), channel_id=1, source_target_pairs={{0,1},{1,0},{2,3},{3,2},{4,5},{5,4},{6,7},{7,6},{8,9},{9,8},{10,11... | collective-permute-start | bytes 4718600 | tf_op jit(solution)/shard_map/ppermute | solution.py:21
  54.9 1.9 %collective-permute-start.11 = (f32[1,384]{1,0:T(1,128)S(1)}, f32[1,384]{1,0:T(1,128)S(1)}, u32[]{:S(2)}, u32[]{:S(2)}) collective-permute-start(f32[1,384]{1,0:T(1,128)S(1)} %get-tuple-element.57.refs_0_), channel_id=1, source_target_pairs={{0,1},{1,0},{2,3},{3,2},{4,5},{5,4},{6,7},{7,6},{8,9},{9,8},{10,11... | collective-permute-start | bytes 4616 | tf_op jit(solution)/shard_map/ppermute | solution.py:21
  55.1 3.6 %collective-permute-start.12 = (f32[1,384]{1,0:T(1,128)S(1)}, f32[1,384]{1,0:T(1,128)S(1)}, u32[]{:S(2)}, u32[]{:S(2)}) collective-permute-start(f32[1,384]{1,0:T(1,128)S(1)} %get-tuple-element.57.refs_0_), channel_id=1, source_target_pairs={{0,2},{1,3},{2,0},{3,1},{4,6},{5,7},{6,4},{7,5},{8,10},{9,11},{10,... | collective-permute-start | bytes 4616 | tf_op jit(solution)/shard_map/ppermute | solution.py:21
  55.9 3.0 %collective-permute-start.13 = (f32[1,384]{1,0:T(1,128)S(1)}, f32[1,384]{1,0:T(1,128)S(1)}, u32[]{:S(2)}, u32[]{:S(2)}) collective-permute-start(f32[1,384]{1,0:T(1,128)S(1)} %get-tuple-element.57.refs_0_), channel_id=1, source_target_pairs={{0,3},{1,2},{2,1},{3,0},{4,7},{5,6},{6,5},{7,4},{8,11},{9,10},{10,... | collective-permute-start | bytes 4616 | tf_op jit(solution)/shard_map/ppermute | solution.py:21
  60.2 10.8 %collective-permute-start.14 = (bf16[32,4096]{1,0:T(8,128)(2,1)S(1)}, bf16[32,4096]{1,0:T(8,128)(2,1)S(1)}, u32[]{:S(2)}, u32[]{:S(2)}) collective-permute-start(bf16[32,4096]{1,0:T(8,128)(2,1)S(1)} %get-tuple-element.62), channel_id=1, source_target_pairs={{0,4},{4,0},{8,12},{12,8},{1,5},{5,1},{9,13},{13,9},{2,6},{6,2},{1... | collective-permute-start | bytes 786440 | tf_op jit(solution)/shard_map/ppermute | solution.py:82
  63.8 12.7 %collective-permute-start.19 = (bf16[32,4096]{1,0:T(8,128)(2,1)S(1)}, bf16[32,4096]{1,0:T(8,128)(2,1)S(1)}, u32[]{:S(2)}, u32[]{:S(2)}) collective-permute-start(bf16[32,4096]{1,0:T(8,128)(2,1)S(1)} %get-tuple-element.68), channel_id=1, source_target_pairs={{0,4},{4,0},{8,12},{12,8},{1,5},{5,1},{9,13},{13,9},{2,6},{6,2},{1... | collective-permute-start | bytes 786440 | tf_op jit(solution)/shard_map/ppermute | solution.py:82
  70.9 11.4 %collective-permute-start.17 = (bf16[32,4096]{1,0:T(8,128)(2,1)S(1)}, bf16[32,4096]{1,0:T(8,128)(2,1)S(1)}, u32[]{:S(2)}, u32[]{:S(2)}) collective-permute-start(bf16[32,4096]{1,0:T(8,128)(2,1)S(1)} %get-tuple-element.63), channel_id=1, source_target_pairs={{0,4},{4,0},{8,12},{12,8},{1,5},{5,1},{9,13},{13,9},{2,6},{6,2},{1... | collective-permute-start | bytes 786440 | tf_op jit(solution)/shard_map/ppermute | solution.py:86
  73.1 4.2 %collective-permute-start.15 = (bf16[32,4096]{1,0:T(8,128)(2,1)S(1)}, bf16[32,4096]{1,0:T(8,128)(2,1)S(1)}, u32[]{:S(2)}, u32[]{:S(2)}) collective-permute-start(bf16[32,4096]{1,0:T(8,128)(2,1)S(1)} %add_convert_fusion.5), channel_id=1, source_target_pairs={{4,8},{8,4},{0,0},{12,12},{5,9},{9,5},{1,1},{13,13},{6,10},{10,6},... | collective-permute-start | bytes 786440 | tf_op jit(solution)/shard_map/ppermute | solution.py:89
  73.8 14.2 %collective-permute-start.22 = (bf16[32,4096]{1,0:T(8,128)(2,1)S(1)}, bf16[32,4096]{1,0:T(8,128)(2,1)S(1)}, u32[]{:S(2)}, u32[]{:S(2)}) collective-permute-start(bf16[32,4096]{1,0:T(8,128)(2,1)S(1)} %get-tuple-element.67), channel_id=1, source_target_pairs={{0,4},{4,0},{8,12},{12,8},{1,5},{5,1},{9,13},{13,9},{2,6},{6,2},{1... | collective-permute-start | bytes 786440 | tf_op jit(solution)/shard_map/ppermute | solution.py:86
  76.6 6.5 %collective-permute-start.20 = (bf16[32,4096]{1,0:T(8,128)(2,1)S(1)}, bf16[32,4096]{1,0:T(8,128)(2,1)S(1)}, u32[]{:S(2)}, u32[]{:S(2)}) collective-permute-start(bf16[32,4096]{1,0:T(8,128)(2,1)S(1)} %add_convert_fusion.2), channel_id=1, source_target_pairs={{4,8},{8,4},{0,0},{12,12},{5,9},{9,5},{1,1},{13,13},{6,10},{10,6},... | collective-permute-start | bytes 786440 | tf_op jit(solution)/shard_map/ppermute | solution.py:89
  77.4 16.0 %collective-permute-start.16 = (bf16[32,4096]{1,0:T(8,128)(2,1)S(1)}, bf16[32,4096]{1,0:T(8,128)(2,1)S(1)}, u32[]{:S(2)}, u32[]{:S(2)}) collective-permute-start(bf16[32,4096]{1,0:T(8,128)(2,1)S(1)} %fusion), channel_id=1, source_target_pairs={{0,4},{4,0},{8,12},{12,8},{1,5},{5,1},{9,13},{13,9},{2,6},{6,2},{1... | collective-permute-start | bytes 786440 | tf_op jit(solution)/shard_map/ppermute | solution.py:92
  82.4 11.0 %collective-permute-start.18 = (bf16[32,4096]{1,0:T(8,128)(2,1)S(1)}, bf16[32,4096]{1,0:T(8,128)(2,1)S(1)}, u32[]{:S(2)}, u32[]{:S(2)}) collective-permute-start(bf16[32,4096]{1,0:T(8,128)(2,1)S(1)} %add_convert_fusion.3), channel_id=1, source_target_pairs={{4,8},{8,4},{0,0},{12,12},{5,9},{9,5},{1,1},{13,13},{6,10},{10,6},... | collective-permute-start | bytes 786440 | tf_op jit(solution)/shard_map/ppermute | solution.py:90
  83.2 15.3 %collective-permute-start.21 = (bf16[32,4096]{1,0:T(8,128)(2,1)S(1)}, bf16[32,4096]{1,0:T(8,128)(2,1)S(1)}, u32[]{:S(2)}, u32[]{:S(2)}) collective-permute-start(bf16[32,4096]{1,0:T(8,128)(2,1)S(1)} %fusion.1), channel_id=1, source_target_pairs={{0,4},{4,0},{8,12},{12,8},{1,5},{5,1},{9,13},{13,9},{2,6},{6,2},{1... | collective-permute-start | bytes 786440 | tf_op jit(solution)/shard_map/ppermute | solution.py:92
  88.1 10.5 %collective-permute-start.23 = (bf16[32,4096]{1,0:T(8,128)(2,1)S(1)}, bf16[32,4096]{1,0:T(8,128)(2,1)S(1)}, u32[]{:S(2)}, u32[]{:S(2)}) collective-permute-start(bf16[32,4096]{1,0:T(8,128)(2,1)S(1)} %add_convert_fusion), channel_id=1, source_target_pairs={{4,8},{8,4},{0,0},{12,12},{5,9},{9,5},{1,1},{13,13},{6,10},{10,6},... | collective-permute-start | bytes 786440 | tf_op jit(solution)/shard_map/ppermute | solution.py:90
  (4 other events, 13.8 us)

commit v9 on v8

--- a/solution.py
+++ b/solution.py
@@ -14,7 +14,6 @@
 ANY_SPEC = pl.BlockSpec(memory_space=pl.ANY)
 SIDES = [(0, 1), (1, 0), (2, 3), (3, 2)]
 MIDDLE = [(1, 2), (2, 1), (0, 0), (3, 3)]
-ENDS = [(0, 3), (3, 0), (1, 1), (2, 2)]
 
 
 def swap_bits(block, axis, bits):
@@ -35,21 +34,32 @@
 
 
 def staged_gather(block, images, noise, routes, near_bits, far_bit):
-    routes = swap_all(routes)
-    far_images, *routes = lax.optimization_barrier((images, *routes))
+    half = block.shape[1] // 2
+    halves = [block[:, :half], block[:, half:]]
+    crossed = swap_bits(images, "reader", far_bit)
     near = swap_gather(images, "reader", near_bits)
-    crossed = swap_bits(far_images, "reader", far_bit)
-    side = lax.ppermute(block, "blk", SIDES)
-    across = lax.ppermute(block, "blk", MIDDLE)
-    end = lax.ppermute(block, "blk", ENDS)
-    side, across = lax.optimization_barrier((side, across))
-    far = lax.ppermute(across, "blk", SIDES)
-    across_far = lax.ppermute(side, "blk", MIDDLE)
-    staged = stage([[block], [side], None, [end, across]], near, noise)
-    crossed, far, across_far, *staged = lax.optimization_barrier(
-        (crossed, far, across_far, *staged)
+    firsts = [
+        lax.optimization_barrier(
+            (lax.ppermute(one, "blk", SIDES), lax.ppermute(one, "blk", MIDDLE))
+        )
+        for one in halves
+    ]
+    early = stage(
+        [[[one] for one in halves], [[side] for side, _ in firsts]], near, noise
     )
-    return staged, [far, across_far], swap_gather(crossed, "reader", near_bits), routes
+    far_parts, end_parts = [], []
+    for side, across in firsts:
+        far = lax.ppermute(across, "blk", SIDES)
+        across_far = lax.ppermute(side, "blk", MIDDLE)
+        far, across_far, *early = lax.optimization_barrier((far, across_far, *early))
+        end = lax.ppermute(across_far, "blk", SIDES)
+        far_parts.append([far, across_far])
+        end_parts.append([end, across])
+    weighted, penalty, near, noise = early
+    weights = stage_rest([far_parts, end_parts], weighted, penalty, noise)
+    ends = [parts[0] for parts in end_parts]
+    routes, crossed, *_ = lax.optimization_barrier((routes, crossed, *ends))
+    return weights, near, swap_gather(crossed, "reader", near_bits), swap_all(routes)
 
 
 def swap_all(routes):
@@ -59,9 +69,10 @@
 def plain_gather(block, images, noise, routes, near_bits, far_bit):
     near = swap_gather(images, "reader", near_bits)
     far = swap_gather(swap_bits(images, "reader", far_bit), "reader", near_bits)
-    line = line_gather(block, "blk")
-    staged = stage([[one] for one in line[:2]] + [None] + [[one] for one in line[3:]], near, noise)
-    return staged, [line[2]], far, swap_all(routes)
+    line = [[[one]] for one in line_gather(block, "blk")]
+    weighted, penalty, near, noise = stage(line[:2], near, noise)
+    weights = stage_rest(line[2:], weighted, penalty, noise)
+    return weights, near, far, swap_all(routes)
 
 
 def line_gather(block, axis):
@@ -141,58 +152,68 @@
         act(refs[1])
 
 
-def weigh(block_ref, noise_ref, weighted_ref, penalty_ref, start):
-    count, width = block_ref.shape
-    rows = slice(start, start + count)
-    penalty = jnp.zeros((count, 1), jnp.float32)
-    for column in range(0, width, STEP):
-        columns = slice(column, column + STEP)
-        block = block_ref[:, columns].astype(jnp.float32)
-        scaled = block * noise_ref[:, columns]
-        weighted_ref[rows, columns] = scaled.astype(jnp.bfloat16)
-        penalty = penalty + 0.5 * jnp.sum(scaled * block, axis=1, keepdims=True)
-    penalty_ref[rows, :] = penalty
+def weigh_blocks(groups, noise_ref, weighted_ref, penalty_ref, parts_ref, sems, first):
+    count, width = parts_ref.shape[1:]
+
+    def part_copy(i, ref):
+        return pltpu.make_async_copy(ref, parts_ref.at[i], sems.at[i])
+
+    parts = [part for group in groups for part in group]
+    for i, part in enumerate(parts):
+        either(part, lambda ref, i=i: part_copy(i, ref).start())
+    i = 0
+    for s, group in enumerate(groups):
+        rows = slice((first + s) * count, (first + s + 1) * count)
+        penalty = jnp.zeros((count, 1), jnp.float32)
+        for q, part in enumerate(group):
+            part_copy(i, part[0]).wait()
+            for column in range(0, width, STEP):
+                columns = slice(q * width + column, q * width + column + STEP)
+                block = parts_ref[i, :, column : column + STEP].astype(jnp.float32)
+                scaled = block * noise_ref[:, columns]
+                weighted_ref[rows, columns] = scaled.astype(jnp.bfloat16)
+                penalty = penalty + 0.5 * jnp.sum(scaled * block, axis=1, keepdims=True)
+            i += 1
+        penalty_ref[rows, :] = penalty
+
+
+def take_blocks(refs, counts):
+    return [[[refs.pop(0) for _ in range(n)] for n in group] for group in counts]
+
+
+def block_counts(blocks):
+    return [[len(part) for part in group] for group in blocks]
+
+
+def flat(blocks):
+    return [one for group in blocks for part in group for one in part]
 
 
 def stage_kernel(near_count, counts, *refs):
     refs = list(refs)
     near_refs = [refs.pop(0) for _ in range(near_count)]
-    pair_refs = [[refs.pop(0) for _ in range(n)] for n in counts]
-    noise_ref, weighted_ref, penalty_ref, near_ref, noise_out_ref, block_ref, near_sems, sems = refs
+    groups = take_blocks(refs, counts)
+    noise_ref, weighted_ref, penalty_ref, near_ref, noise_out_ref, parts_ref, near_sems, sems = refs
     rows = near_refs[0].shape[0]
-    count = block_ref.shape[1]
     copies = []
     for k, ref in enumerate(near_refs):
         copy = pltpu.make_async_copy(ref, near_ref.at[pl.ds(k * rows, rows), :], near_sems.at[k])
         copy.start()
         copies.append(copy)
-
-    def block_copy(s, ref):
-        return pltpu.make_async_copy(ref, block_ref.at[s], sems.at[s])
-
-    for s, pair in enumerate(pair_refs):
-        if pair:
-            either(pair, lambda ref, s=s: block_copy(s, ref).start())
     noise_out_ref[...] = noise_ref[...]
-    for s, pair in enumerate(pair_refs):
-        if pair:
-            block_copy(s, pair[0]).wait()
-            weigh(block_ref.at[s], noise_ref, weighted_ref, penalty_ref, s * count)
-        else:
-            weighted_ref[s * count : (s + 1) * count, :] = jnp.zeros(
-                (count, weighted_ref.shape[1]), jnp.bfloat16
-            )
-            penalty_ref[s * count : (s + 1) * count, :] = jnp.zeros((count, 1), jnp.float32)
+    weigh_blocks(groups, noise_ref, weighted_ref, penalty_ref, parts_ref, sems, 0)
     for copy in copies:
         copy.wait()
 
 
-def stage(pairs, near, noise):
-    count, width = pairs[0][0].shape
-    refs = len(pairs) * count
-    moved = [*near, *[one for pair in pairs for one in pair or []]]
+def stage(blocks, near, noise):
+    count, part_width = blocks[0][0][0].shape
+    parts = sum(len(group) for group in blocks)
+    width = noise.shape[1]
+    refs = len(blocks) * count
+    moved = [*near, *flat(blocks)]
     return pl.pallas_call(
-        partial(stage_kernel, len(near), [len(pair or []) for pair in pairs]),
+        partial(stage_kernel, len(near), block_counts(blocks)),
         out_shape=(
             jax.ShapeDtypeStruct((refs, width), jnp.bfloat16),
             jax.ShapeDtypeStruct((refs, 1), jnp.float32),
@@ -202,42 +223,71 @@
         in_specs=[ANY_SPEC] * len(moved) + [VMEM_SPEC],
         out_specs=(VMEM_SPEC,) * 4,
         scratch_shapes=[
-            pltpu.VMEM((len(pairs), count, width), jnp.bfloat16),
+            pltpu.VMEM((parts, count, part_width), jnp.bfloat16),
             pltpu.SemaphoreType.DMA((len(near),)),
-            pltpu.SemaphoreType.DMA((len(pairs),)),
+            pltpu.SemaphoreType.DMA((parts,)),
         ],
         compiler_params=pltpu.CompilerParams(vmem_limit_bytes=SCORE_VMEM),
         cost_estimate=pl.CostEstimate(
-            flops=8 * refs * width, bytes_accessed=24_000_000, transcendentals=0
+            flops=8 * refs * width, bytes_accessed=12_000_000, transcendentals=0
         ),
         name="stage",
     )(*moved, noise)
 
 
-def score_kernel(readers, last_count, finish, *refs):
+def stage_rest_kernel(counts, *refs):
+    refs = list(refs)
+    groups = take_blocks(refs, counts)
+    early_ref, early_penalty_ref, noise_ref, weighted_ref, penalty_ref, parts_ref, sems = refs
+    done = early_ref.shape[0]
+    weighted_ref[:done, :] = early_ref[...]
+    penalty_ref[:done, :] = early_penalty_ref[...]
+    first = done // parts_ref.shape[1]
+    weigh_blocks(groups, noise_ref, weighted_ref, penalty_ref, parts_ref, sems, first)
+
+
+def stage_rest(blocks, weighted, penalty, noise):
+    count, part_width = blocks[0][0][0].shape
+    parts = sum(len(group) for group in blocks)
+    width = noise.shape[1]
+    refs = len(blocks) * count + weighted.shape[0]
+    moved = flat(blocks)
+    return pl.pallas_call(
+        partial(stage_rest_kernel, block_counts(blocks)),
+        out_shape=(
+            jax.ShapeDtypeStruct((refs, width), jnp.bfloat16),
+            jax.ShapeDtypeStruct((refs, 1), jnp.float32),
+        ),
+        in_specs=[ANY_SPEC] * len(moved) + [VMEM_SPEC] * 3,
+        out_specs=(VMEM_SPEC,) * 2,
+        scratch_shapes=[
+            pltpu.VMEM((parts, count, part_width), jnp.bfloat16),
+            pltpu.SemaphoreType.DMA((parts,)),
+        ],
+        compiler_params=pltpu.CompilerParams(vmem_limit_bytes=SCORE_VMEM),
+        cost_estimate=pl.CostEstimate(
+            flops=8 * refs * width, bytes_accessed=12_000_000, transcendentals=0
+        ),
+        name="stage_rest",
+    )(*moved, weighted, penalty, noise)
+
+
+def score_kernel(readers, finish, *refs):
     refs = list(refs)
     near_ref = refs.pop(0)
     rows = near_ref.shape[0] * 2 // readers
     far_refs = [refs.pop(0) for _ in range(readers // 2)]
-    last_refs = [refs.pop(0) for _ in range(last_count)]
-    staged_ref, staged_penalty_ref, noise_ref = [refs.pop(0) for _ in range(3)]
+    weighted_ref, penalty_ref = refs.pop(0), refs.pop(0)
     route_refs = [refs.pop(0) for _ in range(readers)]
-    score_ref, mask_ref, lse_ref, all_ref = refs[:4]
-    block_ref, weighted_ref, penalty_ref, image_sems, block_sem = refs[4:]
+    score_ref, mask_ref, lse_ref, all_ref, image_sems = refs
     reader = lax.axis_index("reader")
-    count, width = block_ref.shape
-
-    def block_copy(ref):
-        return pltpu.make_async_copy(ref, block_ref, block_sem)
-
-    either(last_refs, lambda ref: block_copy(ref).start())
     copies = []
     for k in range(readers):
-        row = pl.multiple_of((reader ^ k) * rows, 16)
         if k < readers // 2:
             source = near_ref.at[pl.ds(k * rows, rows), :]
         else:
             source = far_refs[k - readers // 2]
+        row = pl.multiple_of((reader ^ k) * rows, 16)
         copy = pltpu.make_async_copy(source, all_ref.at[pl.ds(row, rows), :], image_sems.at[k])
         copy.start()
         copies.append(copy)
@@ -251,10 +301,6 @@
         for k in range(readers):
             hits = jnp.where(route == (reader ^ k), 1.0, 0.0)
             mask_ref[k : k + 1, j * rows : (j + 1) * rows] = jnp.max(hits, axis=0, keepdims=True)
-    weighted_ref[...] = staged_ref[...]
-    penalty_ref[...] = staged_penalty_ref[...]
-    block_copy(last_refs[0]).wait()
-    weigh(block_ref, noise_ref, weighted_ref, penalty_ref, 2 * count)
     for copy in copies:
         copy.wait()
     scores = lax.dot_general(
@@ -269,29 +315,22 @@
         lse_ref[...] = column_lse(scores)
 
 
-def all_scores(staged, last, far, routes, finish):
-    weighted, penalty, near, noise = staged
-    count, width = last[0].shape
-    refs = weighted.shape[0]
+def all_scores(weights, near, far, routes, finish):
+    weighted, penalty = weights
+    refs, width = weighted.shape
     slots = 2 * near.shape[0]
-    moved = [near, *far, *last]
+    moved = [near, *far]
     return pl.pallas_call(
-        partial(score_kernel, len(routes), len(last), finish),
+        partial(score_kernel, len(routes), finish),
         out_shape=(
             jax.ShapeDtypeStruct((refs, slots), jnp.float32),
             jax.ShapeDtypeStruct((len(routes), slots), jnp.float32),
             jax.ShapeDtypeStruct((1, slots), jnp.float32),
             jax.ShapeDtypeStruct((slots, width), jnp.bfloat16),
         ),
-        in_specs=[ANY_SPEC] * len(moved) + [VMEM_SPEC] * (3 + len(routes)),
+        in_specs=[ANY_SPEC] * len(moved) + [VMEM_SPEC] * (2 + len(routes)),
         out_specs=(VMEM_SPEC,) * 4,
-        scratch_shapes=[
-            pltpu.VMEM((count, width), jnp.bfloat16),
-            pltpu.VMEM((refs, width), jnp.bfloat16),
-            pltpu.VMEM((refs, 1), jnp.float32),
-            pltpu.SemaphoreType.DMA((len(routes),)),
-            pltpu.SemaphoreType.DMA,
-        ],
+        scratch_shapes=[pltpu.SemaphoreType.DMA((len(routes),))],
         compiler_params=pltpu.CompilerParams(vmem_limit_bytes=SCORE_VMEM),
         cost_estimate=pl.CostEstimate(
             flops=2 * refs * slots * width,
@@ -299,7 +338,7 @@
             transcendentals=0,
         ),
         name="scores",
-    )(*moved, weighted, penalty, noise, *routes)
+    )(*moved, weighted, penalty, *routes)
 
 
 def lse_kernel(score_ref, lse_ref):
@@ -367,12 +406,12 @@
     rows, width = images.shape
     noise = noise_weights.reshape(1, width)
 
-    gather = staged_gather if members == 4 and rows % 32 == 0 else plain_gather
-    staged, last, far, route_blocks = gather(
+    gather = staged_gather if members == 4 and rows % 32 == 0 and readers > 1 else plain_gather
+    weights, near, far, route_blocks = gather(
         projections[0], images, noise, routes.T, readers // 4, readers // 2
     )
     split = lax.axis_size("sub") > 1
-    scores, masks, mine, all_images = all_scores(staged, last, far, route_blocks, not split)
+    scores, masks, mine, all_images = all_scores(weights, near, far, route_blocks, not split)
     if split:
         scores = lax.psum(scores, "sub")
         mine = group_lse(scores)

time: 100 us -> 96.2 us (0.962)
  starting transfers between devices: 50.8 us -> 47.9 us
  waiting for transfers between devices: 37.4 us -> 36 us
    ppermute x1 -> x2, starting transfers between devices: 15.5 us -> 9.17 us  [staged_gather(): far = lax.ppermute(across, 'blk', SIDES)]
    ppermute x3 -> x6, starting transfers between devices: 7.63 us -> 12.8 us  [the longest x2 6.09 us: staged_gather(): lax.ppermute(one, 'blk', SIDES)]
    ppermute x1 -> x2, waiting for transfers between devices: 6 us -> 1.48 us  [staged_gather(): far = lax.ppermute(across, 'blk', SIDES)]
    ppermute x3 -> x6, waiting for transfers between devices: 6.59 us -> 9.38 us  [the longest x2 6.71 us: staged_gather(): end = lax.ppermute(across_far, 'blk', SIDES)]
    ppermute x2, starting transfers between devices: 3.77 us -> 2.09 us  [pair_scatter(): for_far_end = [lax.ppermute(parts[3], axis, SIDES) for parts in pieces]]
    ppermute x2, starting transfers between devices: 9.72 us -> 8.38 us  [pair_scatter(): from_side = lax.ppermute(near, axis, SIDES)]
    ppermute x9, waiting for transfers between devices: 8.68 us -> 7.45 us  [swap_bits(): lax.ppermute(block, axis, [(i, i ^ bits) for i in range(lax.axis_size(axi...]
    ppermute x2, waiting for transfers between devices: 0.01 us -> 1.15 us  [pair_scatter(): for_far_middle = [lax.ppermute(part, axis, SIDES) for part in second]]
  transfers between devices with their start and end apart: 24 -> 29, of which waited for: 12 -> 16; matrix products, arithmetic and copies ran while one was open for 1% -> 2% of each run, Pallas kernels for 1% -> 2%
where the time goes in v9:
time: 96.2 us; the launch traced here: 95.8 us
  starting transfers between devices  47.9 us (50%)
  waiting for transfers between devices  36 us (37%)
  Pallas kernels  5.52 us (6%)
  local copies, waits for them, and re-layouts  3.81 us (4%)
  other arithmetic  1.66 us (2%)
    ppermute x2, waiting for transfers between devices, pair_scatter(): from_side = lax.ppermute(near, axis, SIDES)  9.61 us
    ppermute x2, starting transfers between devices, staged_gather(): far = lax.ppermute(across, 'blk', SIDES)  9.17 us
    ppermute x2, starting transfers between devices, pair_scatter(): from_side = lax.ppermute(near, axis, SIDES)  8.38 us
    ppermute x9, waiting for transfers between devices, swap_bits(): lax.ppermute(block, axis, [(i, i ^ bits) for i in range(lax.axis_size(axi...  7.45 us
    ppermute x2, waiting for transfers between devices, pair_scatter(): for_far_end = [lax.ppermute(parts[3], axis, SIDES) for parts in pieces]  6.93 us
    ppermute x9, starting transfers between devices, swap_bits(): lax.ppermute(block, axis, [(i, i ^ bits) for i in range(lax.axis_size(axi...  6.91 us
    ppermute x2, waiting for transfers between devices, staged_gather(): end = lax.ppermute(across_far, 'blk', SIDES)  6.71 us
    ppermute x2, starting transfers between devices, staged_gather(): lax.ppermute(one, 'blk', SIDES)  6.09 us
  transfers between devices with their start and end apart: 29, of which 16 were waited for; matrix products, arithmetic and copies ran while one was open for 2% of the time, Pallas kernels for 2%

profile of v9, /device:TPU:0, one launch (start us, length us, event | category | flops | bytes accessed | tf_op | source)
XLA Modules:
  0.0 95.8 jit_solution(16124230902973738530)
XLA Ops:
  1.1 2.6 %collective-permute-start.9 = (bf16[96,8192]{1,0:T(8,128)(2,1)}, bf16[96,8192]{1,0:T(8,128)(2,1)S(1)}, u32[]{:S(2)}, u32[]{:S(2)}) collective-permute-start(bf16[96,8192]{1,0:T(8,128)(2,1)} %refs_0_.1), channel_id=1, source_target_pairs={{0,2},{1,3},{2,0},{3,1},{4,6},{5,7},{6,4},{7,5},{8,10},{9,11},{10,... | collective-permute-start | bytes 4718600 | tf_op jit(solution)/shard_map/ppermute | solution.py:20
  4.8 1.6 %collective-permute-start.4 = (bf16[32,4096]{1,0:T(8,128)(2,1)S(1)}, bf16[32,4096]{1,0:T(8,128)(2,1)S(1)}, u32[]{:S(2)}, u32[]{:S(2)}) collective-permute-start(bf16[32,4096]{1,0:T(8,128)(2,1)S(1)} %get-tuple-element.82.refs_2_), channel_id=1, source_target_pairs={{0,4},{4,0},{8,12},{12,8},{1,5},{5,1},{9,13},{13,9},{2,6},{6,2},{1... | collective-permute-start | bytes 786440 | tf_op jit(solution)/shard_map/ppermute | solution.py:43
  7.1 4.4 %collective-permute-start = (bf16[32,4096]{1,0:T(8,128)(2,1)S(1)}, bf16[32,4096]{1,0:T(8,128)(2,1)S(1)}, u32[]{:S(2)}, u32[]{:S(2)}) collective-permute-start(bf16[32,4096]{1,0:T(8,128)(2,1)S(1)} %get-tuple-element.83.refs_3_), channel_id=1, source_target_pairs={{0,4},{4,0},{8,12},{12,8},{1,5},{5,1},{9,13},{13,9},{2,6},{6,2},{1... | collective-permute-start | bytes 786440 | tf_op jit(solution)/shard_map/ppermute | solution.py:43
  11.5 2.4 %collective-permute-done.4.refs_4_ = bf16[32,4096]{1,0:T(8,128)(2,1)S(1)} collective-permute-done((bf16[32,4096]{1,0:T(8,128)(2,1)S(1)}, bf16[32,4096]{1,0:T(8,128)(2,1)S(1)}, u32[]{:S(2)}, u32[]{:S(2)}) %collective-permute-start.4) | collective-permute-done | bytes 262176 | tf_op jit(solution)/shard_map/ppermute | solution.py:43
  14.7 4.4 %collective-permute-start.6 = (bf16[32,4096]{1,0:T(8,128)(2,1)S(1)}, bf16[32,4096]{1,0:T(8,128)(2,1)S(1)}, u32[]{:S(2)}, u32[]{:S(2)}) collective-permute-start(bf16[32,4096]{1,0:T(8,128)(2,1)S(1)} %collective-permute-done.5.refs_5_), channel_id=1, source_target_pairs={{0,4},{4,0},{8,12},{12,8},{1,5},{5,1},{9,13},{13,9},{2,6},{6,2},{1... | collective-permute-start | bytes 786440 | tf_op jit(solution)/shard_map/ppermute | solution.py:52
  20.0 4.7 %collective-permute-start.2 = (bf16[32,4096]{1,0:T(8,128)(2,1)S(1)}, bf16[32,4096]{1,0:T(8,128)(2,1)S(1)}, u32[]{:S(2)}, u32[]{:S(2)}) collective-permute-start(bf16[32,4096]{1,0:T(8,128)(2,1)S(1)} %collective-permute-done.1.refs_7_), channel_id=1, source_target_pairs={{0,4},{4,0},{8,12},{12,8},{1,5},{5,1},{9,13},{13,9},{2,6},{6,2},{1... | collective-permute-start | bytes 786440 | tf_op jit(solution)/shard_map/ppermute | solution.py:52
  25.4 1.4 %copy-done = bf16[96,8192]{1,0:T(8,128)(2,1)S(1)} copy-done((bf16[96,8192]{1,0:T(8,128)(2,1)S(1)}, bf16[96,8192]{1,0:T(8,128)(2,1)}, u32[]{:S(2)}) %copy-start) | copy-done | bytes 1572888
  28.6 1.5 %collective-permute-done.2.refs_2_ = bf16[32,4096]{1,0:T(8,128)(2,1)S(1)} collective-permute-done((bf16[32,4096]{1,0:T(8,128)(2,1)S(1)}, bf16[32,4096]{1,0:T(8,128)(2,1)S(1)}, u32[]{:S(2)}, u32[]{:S(2)}) %collective-permute-start.2) | collective-permute-done | bytes 262176 | tf_op jit(solution)/shard_map/ppermute | solution.py:52
  30.1 5.4 %collective-permute-start.11 = (bf16[32,4096]{1,0:T(8,128)(2,1)S(1)}, bf16[32,4096]{1,0:T(8,128)(2,1)S(1)}, u32[]{:S(2)}, u32[]{:S(2)}) collective-permute-start(bf16[32,4096]{1,0:T(8,128)(2,1)S(1)} %collective-permute-done.3.refs_3_), channel_id=1, source_target_pairs={{0,4},{4,0},{8,12},{12,8},{1,5},{5,1},{9,13},{13,9},{2,6},{6,2},{1... | collective-permute-start | bytes 786440 | tf_op jit(solution)/shard_map/ppermute | solution.py:55
  35.5 3.4 %collective-permute-done.9.refs_1_ = bf16[96,8192]{1,0:T(8,128)(2,1)S(1)} collective-permute-done((bf16[96,8192]{1,0:T(8,128)(2,1)}, bf16[96,8192]{1,0:T(8,128)(2,1)S(1)}, u32[]{:S(2)}, u32[]{:S(2)}) %collective-permute-start.9) | collective-permute-done | bytes 1572896 | tf_op jit(solution)/shard_map/ppermute | solution.py:20
  38.9 3.8 %collective-permute-done.11.refs_6_ = bf16[32,4096]{1,0:T(8,128)(2,1)S(1)} collective-permute-done((bf16[32,4096]{1,0:T(8,128)(2,1)S(1)}, bf16[32,4096]{1,0:T(8,128)(2,1)S(1)}, u32[]{:S(2)}, u32[]{:S(2)}) %collective-permute-start.11) | collective-permute-done | bytes 262176 | tf_op jit(solution)/shard_map/ppermute | solution.py:55
  42.7 2.9 %collective-permute-done.10.refs_4_ = bf16[32,4096]{1,0:T(8,128)(2,1)S(1)} collective-permute-done((bf16[32,4096]{1,0:T(8,128)(2,1)S(1)}, bf16[32,4096]{1,0:T(8,128)(2,1)S(1)}, u32[]{:S(2)}, u32[]{:S(2)}) %collective-permute-start.10) | collective-permute-done | bytes 262176 | tf_op jit(solution)/shard_map/ppermute | solution.py:55
  49.7 2.5 %scores.1 = (f32[128,384]{1,0:T(8,128)S(1)}, f32[4,384]{1,0:T(4,128)S(1)}, f32[1,384]{1,0:T(1,128)S(1)}, bf16[384,8192]{1,0:T(8,128)(2,1)S(1)}) custom-call(bf16[192,8192]{1,0:T(8,128)(2,1)S(1)} %get-tuple-element.54.refs_0_, bf16[96,8192]{1,0:T(8,128)(2,1)S(1)} %collective-permute-done.9.refs_1_, bf16[96,8192]{1,0:T(8,128)(2,1)S(1)} %collective-permute-done.12.refs_2_, ...), custom_call_target="tpu_custom_call" | custom-call | flops 805306368 | bytes 8388608 | tf_op jit(solution)/shard_map/scores/pallas_call | solution.py:323
  52.4 1.4 %collective-permute-start.17 = (f32[1,384]{1,0:T(1,128)S(1)}, f32[1,384]{1,0:T(1,128)S(1)}, u32[]{:S(2)}, u32[]{:S(2)}) collective-permute-start(f32[1,384]{1,0:T(1,128)S(1)} %get-tuple-element.69.refs_0_), channel_id=1, source_target_pairs={{0,2},{1,3},{2,0},{3,1},{4,6},{5,7},{6,4},{7,5},{8,10},{9,11},{10,... | collective-permute-start | bytes 4616 | tf_op jit(solution)/shard_map/ppermute | solution.py:20
  54.2 1.8 %collective-permute-done.17.refs_2_ = f32[1,384]{1,0:T(1,128)S(1)} collective-permute-done((f32[1,384]{1,0:T(1,128)S(1)}, f32[1,384]{1,0:T(1,128)S(1)}, u32[]{:S(2)}, u32[]{:S(2)}) %collective-permute-start.17) | collective-permute-done | bytes 1568 | tf_op jit(solution)/shard_map/ppermute | solution.py:20
  56.8 1.3 %sums.1 = (f32[1,384]{1,0:T(1,128)S(1)}, bf16[32,4096]{1,0:T(8,128)(2,1)S(1)}, bf16[32,4096]{1,0:T(8,128)(2,1)S(1)}, bf16[32,4096]{1,0:T(8,128)(2,1)S(1)}, bf16[...) custom-call(bf16[384,8192]{1,0:T(8,128)(2,1)S(1)} %get-tuple-element, ...), custom_call_target="tpu_custom_call" | custom-call | flops 805306368 | bytes 6291456 | tf_op jit(solution)/shard_map/sums/pallas_call | solution.py:386
  58.1 1.8 %collective-permute-start.19 = (bf16[32,4096]{1,0:T(8,128)(2,1)S(1)}, bf16[32,4096]{1,0:T(8,128)(2,1)S(1)}, u32[]{:S(2)}, u32[]{:S(2)}) collective-permute-start(bf16[32,4096]{1,0:T(8,128)(2,1)S(1)} %get-tuple-element.74), channel_id=1, source_target_pairs={{0,4},{4,0},{8,12},{12,8},{1,5},{5,1},{9,13},{13,9},{2,6},{6,2},{1... | collective-permute-start | bytes 786440 | tf_op jit(solution)/shard_map/ppermute | solution.py:93
  60.7 6.5 %collective-permute-done.19 = bf16[32,4096]{1,0:T(8,128)(2,1)S(1)} collective-permute-done((bf16[32,4096]{1,0:T(8,128)(2,1)S(1)}, bf16[32,4096]{1,0:T(8,128)(2,1)S(1)}, u32[]{:S(2)}, u32[]{:S(2)}) %collective-permute-start.19) | collective-permute-done | bytes 262176 | tf_op jit(solution)/shard_map/ppermute | solution.py:93
  67.3 1.7 %collective-permute-start.22 = (bf16[32,4096]{1,0:T(8,128)(2,1)S(1)}, bf16[32,4096]{1,0:T(8,128)(2,1)S(1)}, u32[]{:S(2)}, u32[]{:S(2)}) collective-permute-start(bf16[32,4096]{1,0:T(8,128)(2,1)S(1)} %get-tuple-element.75), channel_id=1, source_target_pairs={{0,4},{4,0},{8,12},{12,8},{1,5},{5,1},{9,13},{13,9},{2,6},{6,2},{1... | collective-permute-start | bytes 786440 | tf_op jit(solution)/shard_map/ppermute | solution.py:97
  69.8 2.7 %collective-permute-start.27 = (bf16[32,4096]{1,0:T(8,128)(2,1)S(1)}, bf16[32,4096]{1,0:T(8,128)(2,1)S(1)}, u32[]{:S(2)}, u32[]{:S(2)}) collective-permute-start(bf16[32,4096]{1,0:T(8,128)(2,1)S(1)} %get-tuple-element.79), channel_id=1, source_target_pairs={{0,4},{4,0},{8,12},{12,8},{1,5},{5,1},{9,13},{13,9},{2,6},{6,2},{1... | collective-permute-start | bytes 786440 | tf_op jit(solution)/shard_map/ppermute | solution.py:97
  73.7 4.2 %collective-permute-start.21 = (bf16[32,4096]{1,0:T(8,128)(2,1)S(1)}, bf16[32,4096]{1,0:T(8,128)(2,1)S(1)}, u32[]{:S(2)}, u32[]{:S(2)}) collective-permute-start(bf16[32,4096]{1,0:T(8,128)(2,1)S(1)} %fusion), channel_id=1, source_target_pairs={{0,4},{4,0},{8,12},{12,8},{1,5},{5,1},{9,13},{13,9},{2,6},{6,2},{1... | collective-permute-start | bytes 786440 | tf_op jit(solution)/shard_map/ppermute | solution.py:103
  79.4 4.2 %collective-permute-start.26 = (bf16[32,4096]{1,0:T(8,128)(2,1)S(1)}, bf16[32,4096]{1,0:T(8,128)(2,1)S(1)}, u32[]{:S(2)}, u32[]{:S(2)}) collective-permute-start(bf16[32,4096]{1,0:T(8,128)(2,1)S(1)} %fusion.1), channel_id=1, source_target_pairs={{0,4},{4,0},{8,12},{12,8},{1,5},{5,1},{9,13},{13,9},{2,6},{6,2},{1... | collective-permute-start | bytes 786440 | tf_op jit(solution)/shard_map/ppermute | solution.py:103
  84.9 4.9 %collective-permute-done.21 = bf16[32,4096]{1,0:T(8,128)(2,1)S(1)} collective-permute-done((bf16[32,4096]{1,0:T(8,128)(2,1)S(1)}, bf16[32,4096]{1,0:T(8,128)(2,1)S(1)}, u32[]{:S(2)}, u32[]{:S(2)}) %collective-permute-start.21) | collective-permute-done | bytes 262176 | tf_op jit(solution)/shard_map/ppermute | solution.py:103
  89.9 4.7 %collective-permute-done.26 = bf16[32,4096]{1,0:T(8,128)(2,1)S(1)} collective-permute-done((bf16[32,4096]{1,0:T(8,128)(2,1)S(1)}, bf16[32,4096]{1,0:T(8,128)(2,1)S(1)}, u32[]{:S(2)}, u32[]{:S(2)}) %collective-permute-start.26) | collective-permute-done | bytes 262176 | tf_op jit(solution)/shard_map/ppermute | solution.py:103
  (55 shorter events, 18.5 us)
Async XLA Ops:
  0.6 24.1 %collective-permute-start.8 = (bf16[96,8192]{1,0:T(8,128)(2,1)}, bf16[96,8192]{1,0:T(8,128)(2,1)S(1)}, u32[]{:S(2)}, u32[]{:S(2)}) collective-permute-start(bf16[96,8192]{1,0:T(8,128)(2,1)} %refs_0_.1), channel_id=1, source_target_pairs={{0,1},{1,0},{2,3},{3,2},{4,5},{5,4},{6,7},{7,6},{8,9},{9,8},{10,11... | collective-permute-start | bytes 4718600 | tf_op jit(solution)/shard_map/ppermute | solution.py:20
  1.1 37.8 %collective-permute-start.9 = (bf16[96,8192]{1,0:T(8,128)(2,1)}, bf16[96,8192]{1,0:T(8,128)(2,1)S(1)}, u32[]{:S(2)}, u32[]{:S(2)}) collective-permute-start(bf16[96,8192]{1,0:T(8,128)(2,1)} %refs_0_.1), channel_id=1, source_target_pairs={{0,2},{1,3},{2,0},{3,1},{4,6},{5,7},{6,4},{7,5},{8,10},{9,11},{10,... | collective-permute-start | bytes 4718600 | tf_op jit(solution)/shard_map/ppermute | solution.py:20
  4.8 9.2 %collective-permute-start.4 = (bf16[32,4096]{1,0:T(8,128)(2,1)S(1)}, bf16[32,4096]{1,0:T(8,128)(2,1)S(1)}, u32[]{:S(2)}, u32[]{:S(2)}) collective-permute-start(bf16[32,4096]{1,0:T(8,128)(2,1)S(1)} %get-tuple-element.82.refs_2_), channel_id=1, source_target_pairs={{0,4},{4,0},{8,12},{12,8},{1,5},{5,1},{9,13},{13,9},{2,6},{6,2},{1... | collective-permute-start | bytes 786440 | tf_op jit(solution)/shard_map/ppermute | solution.py:43
  6.4 8.2 %collective-permute-start.5 = (bf16[32,4096]{1,0:T(8,128)(2,1)S(1)}, bf16[32,4096]{1,0:T(8,128)(2,1)S(1)}, u32[]{:S(2)}, u32[]{:S(2)}) collective-permute-start(bf16[32,4096]{1,0:T(8,128)(2,1)S(1)} %get-tuple-element.82.refs_2_), channel_id=1, source_target_pairs={{4,8},{8,4},{0,0},{12,12},{5,9},{9,5},{1,1},{13,13},{6,10},{10,6},... | collective-permute-start | bytes 786440 | tf_op jit(solution)/shard_map/ppermute | solution.py:43
  7.1 12.2 %collective-permute-start = (bf16[32,4096]{1,0:T(8,128)(2,1)S(1)}, bf16[32,4096]{1,0:T(8,128)(2,1)S(1)}, u32[]{:S(2)}, u32[]{:S(2)}) collective-permute-start(bf16[32,4096]{1,0:T(8,128)(2,1)S(1)} %get-tuple-element.83.refs_3_), channel_id=1, source_target_pairs={{0,4},{4,0},{8,12},{12,8},{1,5},{5,1},{9,13},{13,9},{2,6},{6,2},{1... | collective-permute-start | bytes 786440 | tf_op jit(solution)/shard_map/ppermute | solution.py:43
  14.0 6.0 %collective-permute-start.1 = (bf16[32,4096]{1,0:T(8,128)(2,1)S(1)}, bf16[32,4096]{1,0:T(8,128)(2,1)S(1)}, u32[]{:S(2)}, u32[]{:S(2)}) collective-permute-start(bf16[32,4096]{1,0:T(8,128)(2,1)S(1)} %get-tuple-element.83.refs_3_), channel_id=1, source_target_pairs={{4,8},{8,4},{0,0},{12,12},{5,9},{9,5},{1,1},{13,13},{6,10},{10,6},... | collective-permute-start | bytes 786440 | tf_op jit(solution)/shard_map/ppermute | solution.py:43
  14.7 13.9 %collective-permute-start.6 = (bf16[32,4096]{1,0:T(8,128)(2,1)S(1)}, bf16[32,4096]{1,0:T(8,128)(2,1)S(1)}, u32[]{:S(2)}, u32[]{:S(2)}) collective-permute-start(bf16[32,4096]{1,0:T(8,128)(2,1)S(1)} %collective-permute-done.5.refs_5_), channel_id=1, source_target_pairs={{0,4},{4,0},{8,12},{12,8},{1,5},{5,1},{9,13},{13,9},{2,6},{6,2},{1... | collective-permute-start | bytes 786440 | tf_op jit(solution)/shard_map/ppermute | solution.py:52
  19.3 9.2 %collective-permute-start.7 = (bf16[32,4096]{1,0:T(8,128)(2,1)S(1)}, bf16[32,4096]{1,0:T(8,128)(2,1)S(1)}, u32[]{:S(2)}, u32[]{:S(2)}) collective-permute-start(bf16[32,4096]{1,0:T(8,128)(2,1)S(1)} %collective-permute-done.4.refs_4_), channel_id=1, source_target_pairs={{4,8},{8,4},{0,0},{12,12},{5,9},{9,5},{1,1},{13,13},{6,10},{10,6},... | collective-permute-start | bytes 786440 | tf_op jit(solution)/shard_map/ppermute | solution.py:53
  20.0 10.0 %collective-permute-start.2 = (bf16[32,4096]{1,0:T(8,128)(2,1)S(1)}, bf16[32,4096]{1,0:T(8,128)(2,1)S(1)}, u32[]{:S(2)}, u32[]{:S(2)}) collective-permute-start(bf16[32,4096]{1,0:T(8,128)(2,1)S(1)} %collective-permute-done.1.refs_7_), channel_id=1, source_target_pairs={{0,4},{4,0},{8,12},{12,8},{1,5},{5,1},{9,13},{13,9},{2,6},{6,2},{1... | collective-permute-start | bytes 786440 | tf_op jit(solution)/shard_map/ppermute | solution.py:52
  24.7 5.3 %collective-permute-start.3 = (bf16[32,4096]{1,0:T(8,128)(2,1)S(1)}, bf16[32,4096]{1,0:T(8,128)(2,1)S(1)}, u32[]{:S(2)}, u32[]{:S(2)}) collective-permute-start(bf16[32,4096]{1,0:T(8,128)(2,1)S(1)} %collective-permute-done.refs_5_), channel_id=1, source_target_pairs={{4,8},{8,4},{0,0},{12,12},{5,9},{9,5},{1,1},{13,13},{6,10},{10,6},... | collective-permute-start | bytes 786440 | tf_op jit(solution)/shard_map/ppermute | solution.py:53
  30.1 12.6 %collective-permute-start.11 = (bf16[32,4096]{1,0:T(8,128)(2,1)S(1)}, bf16[32,4096]{1,0:T(8,128)(2,1)S(1)}, u32[]{:S(2)}, u32[]{:S(2)}) collective-permute-start(bf16[32,4096]{1,0:T(8,128)(2,1)S(1)} %collective-permute-done.3.refs_3_), channel_id=1, source_target_pairs={{0,4},{4,0},{8,12},{12,8},{1,5},{5,1},{9,13},{13,9},{2,6},{6,2},{1... | collective-permute-start | bytes 786440 | tf_op jit(solution)/shard_map/ppermute | solution.py:55
  35.5 10.2 %collective-permute-start.10 = (bf16[32,4096]{1,0:T(8,128)(2,1)S(1)}, bf16[32,4096]{1,0:T(8,128)(2,1)S(1)}, u32[]{:S(2)}, u32[]{:S(2)}) collective-permute-start(bf16[32,4096]{1,0:T(8,128)(2,1)S(1)} %collective-permute-done.7.refs_1_), channel_id=1, source_target_pairs={{0,4},{4,0},{8,12},{12,8},{1,5},{5,1},{9,13},{13,9},{2,6},{6,2},{1... | collective-permute-start | bytes 786440 | tf_op jit(solution)/shard_map/ppermute | solution.py:55
  45.6 4.1 %collective-permute-start.12 = (bf16[96,8192]{1,0:T(8,128)(2,1)S(1)}, bf16[96,8192]{1,0:T(8,128)(2,1)S(1)}, u32[]{:S(2)}, u32[]{:S(2)}) collective-permute-start(bf16[96,8192]{1,0:T(8,128)(2,1)S(1)} %collective-permute-done.9.refs_1_), channel_id=1, source_target_pairs={{0,1},{1,0},{2,3},{3,2},{4,5},{5,4},{6,7},{7,6},{8,9},{9,8},{10,11... | collective-permute-start | bytes 4718600 | tf_op jit(solution)/shard_map/ppermute | solution.py:20
  52.4 3.6 %collective-permute-start.17 = (f32[1,384]{1,0:T(1,128)S(1)}, f32[1,384]{1,0:T(1,128)S(1)}, u32[]{:S(2)}, u32[]{:S(2)}) collective-permute-start(f32[1,384]{1,0:T(1,128)S(1)} %get-tuple-element.69.refs_0_), channel_id=1, source_target_pairs={{0,2},{1,3},{2,0},{3,1},{4,6},{5,7},{6,4},{7,5},{8,10},{9,11},{10,... | collective-permute-start | bytes 4616 | tf_op jit(solution)/shard_map/ppermute | solution.py:20
  58.1 9.2 %collective-permute-start.19 = (bf16[32,4096]{1,0:T(8,128)(2,1)S(1)}, bf16[32,4096]{1,0:T(8,128)(2,1)S(1)}, u32[]{:S(2)}, u32[]{:S(2)}) collective-permute-start(bf16[32,4096]{1,0:T(8,128)(2,1)S(1)} %get-tuple-element.74), channel_id=1, source_target_pairs={{0,4},{4,0},{8,12},{12,8},{1,5},{5,1},{9,13},{13,9},{2,6},{6,2},{1... | collective-permute-start | bytes 786440 | tf_op jit(solution)/shard_map/ppermute | solution.py:93
  59.9 13.0 %collective-permute-start.24 = (bf16[32,4096]{1,0:T(8,128)(2,1)S(1)}, bf16[32,4096]{1,0:T(8,128)(2,1)S(1)}, u32[]{:S(2)}, u32[]{:S(2)}) collective-permute-start(bf16[32,4096]{1,0:T(8,128)(2,1)S(1)} %get-tuple-element.80), channel_id=1, source_target_pairs={{0,4},{4,0},{8,12},{12,8},{1,5},{5,1},{9,13},{13,9},{2,6},{6,2},{1... | collective-permute-start | bytes 786440 | tf_op jit(solution)/shard_map/ppermute | solution.py:93
  67.3 11.2 %collective-permute-start.22 = (bf16[32,4096]{1,0:T(8,128)(2,1)S(1)}, bf16[32,4096]{1,0:T(8,128)(2,1)S(1)}, u32[]{:S(2)}, u32[]{:S(2)}) collective-permute-start(bf16[32,4096]{1,0:T(8,128)(2,1)S(1)} %get-tuple-element.75), channel_id=1, source_target_pairs={{0,4},{4,0},{8,12},{12,8},{1,5},{5,1},{9,13},{13,9},{2,6},{6,2},{1... | collective-permute-start | bytes 786440 | tf_op jit(solution)/shard_map/ppermute | solution.py:97
  69.1 4.6 %collective-permute-start.20 = (bf16[32,4096]{1,0:T(8,128)(2,1)S(1)}, bf16[32,4096]{1,0:T(8,128)(2,1)S(1)}, u32[]{:S(2)}, u32[]{:S(2)}) collective-permute-start(bf16[32,4096]{1,0:T(8,128)(2,1)S(1)} %add_convert_fusion.5), channel_id=1, source_target_pairs={{4,8},{8,4},{0,0},{12,12},{5,9},{9,5},{1,1},{13,13},{6,10},{10,6},... | collective-permute-start | bytes 786440 | tf_op jit(solution)/shard_map/ppermute | solution.py:100
  69.8 14.4 %collective-permute-start.27 = (bf16[32,4096]{1,0:T(8,128)(2,1)S(1)}, bf16[32,4096]{1,0:T(8,128)(2,1)S(1)}, u32[]{:S(2)}, u32[]{:S(2)}) collective-permute-start(bf16[32,4096]{1,0:T(8,128)(2,1)S(1)} %get-tuple-element.79), channel_id=1, source_target_pairs={{0,4},{4,0},{8,12},{12,8},{1,5},{5,1},{9,13},{13,9},{2,6},{6,2},{1... | collective-permute-start | bytes 786440 | tf_op jit(solution)/shard_map/ppermute | solution.py:97
  73.0 6.3 %collective-permute-start.25 = (bf16[32,4096]{1,0:T(8,128)(2,1)S(1)}, bf16[32,4096]{1,0:T(8,128)(2,1)S(1)}, u32[]{:S(2)}, u32[]{:S(2)}) collective-permute-start(bf16[32,4096]{1,0:T(8,128)(2,1)S(1)} %add_convert_fusion.2), channel_id=1, source_target_pairs={{4,8},{8,4},{0,0},{12,12},{5,9},{9,5},{1,1},{13,13},{6,10},{10,6},... | collective-permute-start | bytes 786440 | tf_op jit(solution)/shard_map/ppermute | solution.py:100
  73.7 16.0 %collective-permute-start.21 = (bf16[32,4096]{1,0:T(8,128)(2,1)S(1)}, bf16[32,4096]{1,0:T(8,128)(2,1)S(1)}, u32[]{:S(2)}, u32[]{:S(2)}) collective-permute-start(bf16[32,4096]{1,0:T(8,128)(2,1)S(1)} %fusion), channel_id=1, source_target_pairs={{0,4},{4,0},{8,12},{12,8},{1,5},{5,1},{9,13},{13,9},{2,6},{6,2},{1... | collective-permute-start | bytes 786440 | tf_op jit(solution)/shard_map/ppermute | solution.py:103
  78.6 11.2 %collective-permute-start.23 = (bf16[32,4096]{1,0:T(8,128)(2,1)S(1)}, bf16[32,4096]{1,0:T(8,128)(2,1)S(1)}, u32[]{:S(2)}, u32[]{:S(2)}) collective-permute-start(bf16[32,4096]{1,0:T(8,128)(2,1)S(1)} %add_convert_fusion.3), channel_id=1, source_target_pairs={{4,8},{8,4},{0,0},{12,12},{5,9},{9,5},{1,1},{13,13},{6,10},{10,6},... | collective-permute-start | bytes 786440 | tf_op jit(solution)/shard_map/ppermute | solution.py:101
  79.4 15.2 %collective-permute-start.26 = (bf16[32,4096]{1,0:T(8,128)(2,1)S(1)}, bf16[32,4096]{1,0:T(8,128)(2,1)S(1)}, u32[]{:S(2)}, u32[]{:S(2)}) collective-permute-start(bf16[32,4096]{1,0:T(8,128)(2,1)S(1)} %fusion.1), channel_id=1, source_target_pairs={{0,4},{4,0},{8,12},{12,8},{1,5},{5,1},{9,13},{13,9},{2,6},{6,2},{1... | collective-permute-start | bytes 786440 | tf_op jit(solution)/shard_map/ppermute | solution.py:103
  84.2 10.4 %collective-permute-start.28 = (bf16[32,4096]{1,0:T(8,128)(2,1)S(1)}, bf16[32,4096]{1,0:T(8,128)(2,1)S(1)}, u32[]{:S(2)}, u32[]{:S(2)}) collective-permute-start(bf16[32,4096]{1,0:T(8,128)(2,1)S(1)} %add_convert_fusion), channel_id=1, source_target_pairs={{4,8},{8,4},{0,0},{12,12},{5,9},{9,5},{1,1},{13,13},{6,10},{10,6},... | collective-permute-start | bytes 786440 | tf_op jit(solution)/shard_map/ppermute | solution.py:101
  (8 other events, 35.2 us)

commit v10 on v9

--- a/solution.py
+++ b/solution.py
@@ -13,7 +13,7 @@
 VMEM_SPEC = pl.BlockSpec(memory_space=pltpu.VMEM)
 ANY_SPEC = pl.BlockSpec(memory_space=pl.ANY)
 SIDES = [(0, 1), (1, 0), (2, 3), (3, 2)]
-MIDDLE = [(1, 2), (2, 1), (0, 0), (3, 3)]
+MIDDLE = [(1, 2), (2, 1)]
 
 
 def swap_bits(block, axis, bits):
@@ -34,18 +34,18 @@
 
 
 def staged_gather(block, images, noise, routes, near_bits, far_bit):
-    half = block.shape[1] // 2
-    halves = [block[:, :half], block[:, half:]]
+    cut = block.shape[1] // 16 * 9
+    cuts = [block[:, :cut], block[:, cut:]]
     crossed = swap_bits(images, "reader", far_bit)
     near = swap_gather(images, "reader", near_bits)
     firsts = [
         lax.optimization_barrier(
             (lax.ppermute(one, "blk", SIDES), lax.ppermute(one, "blk", MIDDLE))
         )
-        for one in halves
+        for one in cuts
     ]
     early = stage(
-        [[[one] for one in halves], [[side] for side, _ in firsts]], near, noise
+        [[[one] for one in cuts], [[side] for side, _ in firsts]], near, noise
     )
     far_parts, end_parts = [], []
     for side, across in firsts:
@@ -103,11 +103,36 @@
         from_side = lax.ppermute(near, axis, SIDES)
         total = parts[0].astype(jnp.float32) + from_side.astype(jnp.float32)
         totals.append(total + jnp.where(is_end, 0.0, across_middle.astype(jnp.float32)))
-    return totals
+    return beside(totals)
+
+
+def beside_kernel(count, *refs):
+    out_ref, sems = refs[count:]
+    copies, stop = [], out_ref.shape[1]
+    for i, ref in enumerate(refs[:count]):
+        start = stop - ref.shape[1]
+        copies.append(pltpu.make_async_copy(ref, out_ref.at[:, start:stop], sems.at[i]))
+        copies[-1].start()
+        stop = start
+    for copy in copies:
+        copy.wait()
+
+
+def beside(pieces):
+    width = sum(piece.shape[1] for piece in pieces)
+    return pl.pallas_call(
+        partial(beside_kernel, len(pieces)),
+        out_shape=jax.ShapeDtypeStruct((pieces[0].shape[0], width), pieces[0].dtype),
+        in_specs=[VMEM_SPEC] * len(pieces),
+        out_specs=ANY_SPEC,
+        scratch_shapes=[pltpu.SemaphoreType.DMA((len(pieces),))],
+        compiler_params=pltpu.CompilerParams(vmem_limit_bytes=SUMS_VMEM),
+        name="beside",
+    )(*pieces[::-1])
 
 
 def line_scatter(pieces, axis):
-    return [line_sum(parts, axis) for parts in pieces]
+    return jnp.concatenate([line_sum(parts, axis) for parts in pieces], axis=1)
 
 
 def line_sum(parts, axis):
@@ -152,28 +177,35 @@
         act(refs[1])
 
 
-def weigh_blocks(groups, noise_ref, weighted_ref, penalty_ref, parts_ref, sems, first):
-    count, width = parts_ref.shape[1:]
+def weigh_blocks(groups, noise_ref, weighted_ref, penalty_ref, block_ref, sems, first):
+    count = block_ref.shape[1]
+    parts = []
+    for s, group in enumerate(groups):
+        start = 0
+        for refs in group:
+            stop = start + refs[0].shape[1]
+            parts.append((s, slice(start, stop), refs))
+            start = stop
 
     def part_copy(i, ref):
-        return pltpu.make_async_copy(ref, parts_ref.at[i], sems.at[i])
-
-    parts = [part for group in groups for part in group]
-    for i, part in enumerate(parts):
-        either(part, lambda ref, i=i: part_copy(i, ref).start())
-    i = 0
-    for s, group in enumerate(groups):
+        s, columns, _ = parts[i]
+        return pltpu.make_async_copy(ref, block_ref.at[s, :, columns], sems.at[i])
+
+    for i, (_, _, refs) in enumerate(parts):
+        either(refs, lambda ref, i=i: part_copy(i, ref).start())
+    for s in range(len(groups)):
         rows = slice((first + s) * count, (first + s + 1) * count)
         penalty = jnp.zeros((count, 1), jnp.float32)
-        for q, part in enumerate(group):
-            part_copy(i, part[0]).wait()
-            for column in range(0, width, STEP):
-                columns = slice(q * width + column, q * width + column + STEP)
-                block = parts_ref[i, :, column : column + STEP].astype(jnp.float32)
-                scaled = block * noise_ref[:, columns]
-                weighted_ref[rows, columns] = scaled.astype(jnp.bfloat16)
+        for i, (t, columns, refs) in enumerate(parts):
+            if t != s:
+                continue
+            part_copy(i, refs[0]).wait()
+            for start in range(columns.start, columns.stop, STEP):
+                piece = slice(start, min(start + STEP, columns.stop))
+                block = block_ref[s, :, piece].astype(jnp.float32)
+                scaled = block * noise_ref[:, piece]
+                weighted_ref[rows, piece] = scaled.astype(jnp.bfloat16)
                 penalty = penalty + 0.5 * jnp.sum(scaled * block, axis=1, keepdims=True)
-            i += 1
         penalty_ref[rows, :] = penalty
 
 
@@ -193,7 +225,7 @@
     refs = list(refs)
     near_refs = [refs.pop(0) for _ in range(near_count)]
     groups = take_blocks(refs, counts)
-    noise_ref, weighted_ref, penalty_ref, near_ref, noise_out_ref, parts_ref, near_sems, sems = refs
+    noise_ref, weighted_ref, penalty_ref, near_ref, noise_out_ref, block_ref, near_sems, sems = refs
     rows = near_refs[0].shape[0]
     copies = []
     for k, ref in enumerate(near_refs):
@@ -201,13 +233,13 @@
         copy.start()
         copies.append(copy)
     noise_out_ref[...] = noise_ref[...]
-    weigh_blocks(groups, noise_ref, weighted_ref, penalty_ref, parts_ref, sems, 0)
+    weigh_blocks(groups, noise_ref, weighted_ref, penalty_ref, block_ref, sems, 0)
     for copy in copies:
         copy.wait()
 
 
 def stage(blocks, near, noise):
-    count, part_width = blocks[0][0][0].shape
+    count = blocks[0][0][0].shape[0]
     parts = sum(len(group) for group in blocks)
     width = noise.shape[1]
     refs = len(blocks) * count
@@ -223,7 +255,7 @@
         in_specs=[ANY_SPEC] * len(moved) + [VMEM_SPEC],
         out_specs=(VMEM_SPEC,) * 4,
         scratch_shapes=[
-            pltpu.VMEM((parts, count, part_width), jnp.bfloat16),
+            pltpu.VMEM((len(blocks), count, width), jnp.bfloat16),
             pltpu.SemaphoreType.DMA((len(near),)),
             pltpu.SemaphoreType.DMA((parts,)),
         ],
@@ -238,16 +270,16 @@
 def stage_rest_kernel(counts, *refs):
     refs = list(refs)
     groups = take_blocks(refs, counts)
-    early_ref, early_penalty_ref, noise_ref, weighted_ref, penalty_ref, parts_ref, sems = refs
+    early_ref, early_penalty_ref, noise_ref, weighted_ref, penalty_ref, block_ref, sems = refs
     done = early_ref.shape[0]
     weighted_ref[:done, :] = early_ref[...]
     penalty_ref[:done, :] = early_penalty_ref[...]
-    first = done // parts_ref.shape[1]
-    weigh_blocks(groups, noise_ref, weighted_ref, penalty_ref, parts_ref, sems, first)
+    first = done // block_ref.shape[1]
+    weigh_blocks(groups, noise_ref, weighted_ref, penalty_ref, block_ref, sems, first)
 
 
 def stage_rest(blocks, weighted, penalty, noise):
-    count, part_width = blocks[0][0][0].shape
+    count = blocks[0][0][0].shape[0]
     parts = sum(len(group) for group in blocks)
     width = noise.shape[1]
     refs = len(blocks) * count + weighted.shape[0]
@@ -261,7 +293,7 @@
         in_specs=[ANY_SPEC] * len(moved) + [VMEM_SPEC] * 3,
         out_specs=(VMEM_SPEC,) * 2,
         scratch_shapes=[
-            pltpu.VMEM((parts, count, part_width), jnp.bfloat16),
+            pltpu.VMEM((len(blocks), count, width), jnp.bfloat16),
             pltpu.SemaphoreType.DMA((parts,)),
         ],
         compiler_params=pltpu.CompilerParams(vmem_limit_bytes=SCORE_VMEM),
@@ -419,9 +451,9 @@
     pieces = [slice(0, width // 2), slice(width // 2, width)]
     norms, parts = group_sums(members, pieces, all_images, scores, masks, lses)
     scatter = pair_scatter if members == 4 else line_scatter
-    totals = scatter(parts, "blk")
+    total = scatter(parts, "blk")
     normalizer = lax.dynamic_slice(norms.reshape(-1), (reader * rows,), (rows,))
-    return (jnp.concatenate(totals, axis=1)[None], normalizer)
+    return (total[None], normalizer)
 
 
 def solution(mesh):

time: 96.2 us -> 92.6 us (0.963)
  waiting for transfers between devices: 36 us -> 28.5 us
  starting transfers between devices: 47.9 us -> 50.7 us
  Pallas kernels: 5.52 us -> 6.75 us
  other arithmetic: 1.66 us -> 0.62 us
    ppermute x2, waiting for transfers between devices: 6.71 us -> 2.87 us  [staged_gather(): end = lax.ppermute(across_far, 'blk', SIDES)]
    ppermute x2, starting transfers between devices: 5.42 us -> 7.26 us  [staged_gather(): end = lax.ppermute(across_far, 'blk', SIDES)]
    ppermute x2, waiting for transfers between devices: 1.48 us -> 0.01 us  [staged_gather(): far = lax.ppermute(across, 'blk', SIDES)]
    ppermute x2, waiting for transfers between devices: 1.15 us -> 0.01 us  [pair_scatter(): for_far_middle = [lax.ppermute(part, axis, SIDES) for part in second]]
    broadcast_in_dim x1 -> x0, other arithmetic: 1.04 us -> none  [on_device(): return (jnp.concatenate(totals, axis=1)[None], normalizer)]
    ppermute x2, starting transfers between devices: 4.47 us -> 5.5 us  [pair_scatter(): for_far_middle = [lax.ppermute(part, axis, SIDES) for part in second]]
    ppermute x2, starting transfers between devices: 9.17 us -> 8.16 us  [staged_gather(): far = lax.ppermute(across, 'blk', SIDES)]
    pallas_call x0 -> x1, Pallas kernels: none -> 0.99 us  [beside(): pl.pallas_call(partial(beside_kernel, len(pieces)), out_shape=jax.ShapeDt...]
  transfers between devices with their start and end apart: 29 -> 29, of which waited for: 16 -> 10; matrix products, arithmetic and copies ran while one was open for 2% -> 3% of each run, Pallas kernels for 2% -> 2%
where the time goes in v10:
time: 92.6 us; the launch traced here: 92.1 us
  starting transfers between devices  50.7 us (55%)
  waiting for transfers between devices  28.5 us (31%)
  Pallas kernels  6.75 us (7%)
  local copies, waits for them, and re-layouts  4.68 us (5%)
    ppermute x2, waiting for transfers between devices, pair_scatter(): from_side = lax.ppermute(near, axis, SIDES)  9.61 us
    ppermute x2, starting transfers between devices, pair_scatter(): from_side = lax.ppermute(near, axis, SIDES)  9.19 us
    ppermute x2, starting transfers between devices, staged_gather(): far = lax.ppermute(across, 'blk', SIDES)  8.16 us
    ppermute x9, waiting for transfers between devices, swap_bits(): lax.ppermute(block, axis, [(i, i ^ bits) for i in range(lax.axis_size(axi...  7.38 us
    ppermute x2, starting transfers between devices, staged_gather(): end = lax.ppermute(across_far, 'blk', SIDES)  7.26 us
    ppermute x9, starting transfers between devices, swap_bits(): lax.ppermute(block, axis, [(i, i ^ bits) for i in range(lax.axis_size(axi...  6.97 us
    ppermute x2, waiting for transfers between devices, pair_scatter(): for_far_end = [lax.ppermute(parts[3], axis, SIDES) for parts in pieces]  6.42 us
    ppermute x2, starting transfers between devices, staged_gather(): lax.ppermute(one, 'blk', SIDES)  6.09 us
  transfers between devices with their start and end apart: 29, of which 10 were waited for; matrix products, arithmetic and copies ran while one was open for 3% of the time, Pallas kernels for 2%

profile of v10, /device:TPU:0, one launch (start us, length us, event | category | flops | bytes accessed | tf_op | source)
XLA Modules:
  0.0 92.1 jit_solution(16766195078055067220)
XLA Ops:
  1.1 2.6 %collective-permute-start.9 = (bf16[96,8192]{1,0:T(8,128)(2,1)}, bf16[96,8192]{1,0:T(8,128)(2,1)S(1)}, u32[]{:S(2)}, u32[]{:S(2)}) collective-permute-start(bf16[96,8192]{1,0:T(8,128)(2,1)} %refs_0_.1), channel_id=1, source_target_pairs={{0,2},{1,3},{2,0},{3,1},{4,6},{5,7},{6,4},{7,5},{8,10},{9,11},{10,... | collective-permute-start | bytes 4718600 | tf_op jit(solution)/shard_map/ppermute | solution.py:20
  4.7 1.6 %collective-permute-start.4 = (bf16[32,4608]{1,0:T(8,128)(2,1)S(1)}, bf16[32,4608]{1,0:T(8,128)(2,1)S(1)}, u32[]{:S(2)}, u32[]{:S(2)}) collective-permute-start(bf16[32,4608]{1,0:T(8,128)(2,1)S(1)} %slice.9.refs_2_), channel_id=1, source_target_pairs={{0,4},{4,0},{8,12},{12,8},{1,5},{5,1},{9,13},{13,9},{2,6},{6,2},{1... | collective-permute-start | bytes 884744 | tf_op jit(solution)/shard_map/ppermute | solution.py:43
  8.0 4.4 %collective-permute-start = (bf16[32,3584]{1,0:T(8,128)(2,1)S(1)}, bf16[32,3584]{1,0:T(8,128)(2,1)S(1)}, u32[]{:S(2)}, u32[]{:S(2)}) collective-permute-start(bf16[32,3584]{1,0:T(8,128)(2,1)S(1)} %slice.8.refs_3_), channel_id=1, source_target_pairs={{0,4},{4,0},{8,12},{12,8},{1,5},{5,1},{9,13},{13,9},{2,6},{6,2},{1... | collective-permute-start | bytes 688136 | tf_op jit(solution)/shard_map/ppermute | solution.py:43
  12.4 2.2 %collective-permute-done.4.refs_4_ = bf16[32,4608]{1,0:T(8,128)(2,1)S(1)} collective-permute-done((bf16[32,4608]{1,0:T(8,128)(2,1)S(1)}, bf16[32,4608]{1,0:T(8,128)(2,1)S(1)}, u32[]{:S(2)}, u32[]{:S(2)}) %collective-permute-start.4) | collective-permute-done | bytes 294944 | tf_op jit(solution)/shard_map/ppermute | solution.py:43
  15.3 4.5 %collective-permute-start.6 = (bf16[32,4608]{1,0:T(8,128)(2,1)S(1)}, bf16[32,4608]{1,0:T(8,128)(2,1)S(1)}, u32[]{:S(2)}, u32[]{:S(2)}) collective-permute-start(bf16[32,4608]{1,0:T(8,128)(2,1)S(1)} %collective-permute-done.5.refs_5_), channel_id=1, source_target_pairs={{0,4},{4,0},{8,12},{12,8},{1,5},{5,1},{9,13},{13,9},{2,6},{6,2},{1... | collective-permute-start | bytes 884744 | tf_op jit(solution)/shard_map/ppermute | solution.py:52
  20.4 3.7 %collective-permute-start.2 = (bf16[32,3584]{1,0:T(8,128)(2,1)S(1)}, bf16[32,3584]{1,0:T(8,128)(2,1)S(1)}, u32[]{:S(2)}, u32[]{:S(2)}) collective-permute-start(bf16[32,3584]{1,0:T(8,128)(2,1)S(1)} %collective-permute-done.1.refs_7_), channel_id=1, source_target_pairs={{0,4},{4,0},{8,12},{12,8},{1,5},{5,1},{9,13},{13,9},{2,6},{6,2},{1... | collective-permute-start | bytes 688136 | tf_op jit(solution)/shard_map/ppermute | solution.py:52
  24.8 1.4 %copy-done = bf16[96,8192]{1,0:T(8,128)(2,1)S(1)} copy-done((bf16[96,8192]{1,0:T(8,128)(2,1)S(1)}, bf16[96,8192]{1,0:T(8,128)(2,1)}, u32[]{:S(2)}) %copy-start) | copy-done | bytes 1572888
  27.0 1.1 %stage.1 = (bf16[64,8192]{1,0:T(8,128)(2,1)S(1)}, f32[64,1]{1,0:T(8,128)S(1)}, bf16[192,8192]{1,0:T(8,128)(2,1)S(1)}, f32[1,8192]{1,0:T(1,128)S(1)}) custom-call(bf16[96,8192]{1,0:T(8,128)(2,1)S(1)} %copy-done, bf16[96,8192]{1,0:T(8,128)(2,1)S(1)} %collective-permute-done.8.refs_1_, bf16[32,4608]{1,0:T(8,128)(2,1)S(1)} %slice.9.refs_2_, ...), custom_call_target="tpu_custom_call" | custom-call | flops 4194304 | bytes 12000000 | tf_op jit(solution)/shard_map/stage/pallas_call | solution.py:247
  28.1 4.0 %collective-permute-start.10 = (bf16[32,4608]{1,0:T(8,128)(2,1)S(1)}, bf16[32,4608]{1,0:T(8,128)(2,1)S(1)}, u32[]{:S(2)}, u32[]{:S(2)}) collective-permute-start(bf16[32,4608]{1,0:T(8,128)(2,1)S(1)} %collective-permute-done.7.refs_1_), channel_id=1, source_target_pairs={{0,4},{4,0},{8,12},{12,8},{1,5},{5,1},{9,13},{13,9},{2,6},{6,2},{1... | collective-permute-start | bytes 884744 | tf_op jit(solution)/shard_map/ppermute | solution.py:55
  32.2 3.2 %collective-permute-start.11 = (bf16[32,3584]{1,0:T(8,128)(2,1)S(1)}, bf16[32,3584]{1,0:T(8,128)(2,1)S(1)}, u32[]{:S(2)}, u32[]{:S(2)}) collective-permute-start(bf16[32,3584]{1,0:T(8,128)(2,1)S(1)} %collective-permute-done.3.refs_3_), channel_id=1, source_target_pairs={{0,4},{4,0},{8,12},{12,8},{1,5},{5,1},{9,13},{13,9},{2,6},{6,2},{1... | collective-permute-start | bytes 688136 | tf_op jit(solution)/shard_map/ppermute | solution.py:55
  35.4 3.5 %collective-permute-done.9.refs_1_ = bf16[96,8192]{1,0:T(8,128)(2,1)S(1)} collective-permute-done((bf16[96,8192]{1,0:T(8,128)(2,1)}, bf16[96,8192]{1,0:T(8,128)(2,1)S(1)}, u32[]{:S(2)}, u32[]{:S(2)}) %collective-permute-start.9) | collective-permute-done | bytes 1572896 | tf_op jit(solution)/shard_map/ppermute | solution.py:20
  38.9 2.9 %collective-permute-done.11.refs_6_ = bf16[32,3584]{1,0:T(8,128)(2,1)S(1)} collective-permute-done((bf16[32,3584]{1,0:T(8,128)(2,1)S(1)}, bf16[32,3584]{1,0:T(8,128)(2,1)S(1)}, u32[]{:S(2)}, u32[]{:S(2)}) %collective-permute-start.11) | collective-permute-done | bytes 229408 | tf_op jit(solution)/shard_map/ppermute | solution.py:55
  45.9 2.5 %scores.1 = (f32[128,384]{1,0:T(8,128)S(1)}, f32[4,384]{1,0:T(4,128)S(1)}, f32[1,384]{1,0:T(1,128)S(1)}, bf16[384,8192]{1,0:T(8,128)(2,1)S(1)}) custom-call(bf16[192,8192]{1,0:T(8,128)(2,1)S(1)} %get-tuple-element.54.refs_0_, bf16[96,8192]{1,0:T(8,128)(2,1)S(1)} %collective-permute-done.9.refs_1_, bf16[96,8192]{1,0:T(8,128)(2,1)S(1)} %collective-permute-done.12.refs_2_, ...), custom_call_target="tpu_custom_call" | custom-call | flops 805306368 | bytes 8388608 | tf_op jit(solution)/shard_map/scores/pallas_call | solution.py:355
  48.5 1.4 %collective-permute-start.17 = (f32[1,384]{1,0:T(1,128)S(1)}, f32[1,384]{1,0:T(1,128)S(1)}, u32[]{:S(2)}, u32[]{:S(2)}) collective-permute-start(f32[1,384]{1,0:T(1,128)S(1)} %get-tuple-element.69.refs_0_), channel_id=1, source_target_pairs={{0,2},{1,3},{2,0},{3,1},{4,6},{5,7},{6,4},{7,5},{8,10},{9,11},{10,... | collective-permute-start | bytes 4616 | tf_op jit(solution)/shard_map/ppermute | solution.py:20
  50.3 1.8 %collective-permute-done.17.refs_2_ = f32[1,384]{1,0:T(1,128)S(1)} collective-permute-done((f32[1,384]{1,0:T(1,128)S(1)}, f32[1,384]{1,0:T(1,128)S(1)}, u32[]{:S(2)}, u32[]{:S(2)}) %collective-permute-start.17) | collective-permute-done | bytes 1568 | tf_op jit(solution)/shard_map/ppermute | solution.py:20
  52.9 1.3 %sums.1 = (f32[1,384]{1,0:T(1,128)S(1)}, bf16[32,4096]{1,0:T(8,128)(2,1)S(1)}, bf16[32,4096]{1,0:T(8,128)(2,1)S(1)}, bf16[32,4096]{1,0:T(8,128)(2,1)S(1)}, bf16[...) custom-call(bf16[384,8192]{1,0:T(8,128)(2,1)S(1)} %get-tuple-element, ...), custom_call_target="tpu_custom_call" | custom-call | flops 805306368 | bytes 6291456 | tf_op jit(solution)/shard_map/sums/pallas_call | solution.py:418
  54.2 2.1 %collective-permute-start.19 = (bf16[32,4096]{1,0:T(8,128)(2,1)S(1)}, bf16[32,4096]{1,0:T(8,128)(2,1)S(1)}, u32[]{:S(2)}, u32[]{:S(2)}) collective-permute-start(bf16[32,4096]{1,0:T(8,128)(2,1)S(1)} %get-tuple-element.74), channel_id=1, source_target_pairs={{0,4},{4,0},{8,12},{12,8},{1,5},{5,1},{9,13},{13,9},{2,6},{6,2},{1... | collective-permute-start | bytes 786440 | tf_op jit(solution)/shard_map/ppermute | solution.py:93
  57.0 6.4 %collective-permute-done.19 = bf16[32,4096]{1,0:T(8,128)(2,1)S(1)} collective-permute-done((bf16[32,4096]{1,0:T(8,128)(2,1)S(1)}, bf16[32,4096]{1,0:T(8,128)(2,1)S(1)}, u32[]{:S(2)}, u32[]{:S(2)}) %collective-permute-start.19) | collective-permute-done | bytes 262176 | tf_op jit(solution)/shard_map/ppermute | solution.py:93
  63.4 2.1 %collective-permute-start.27 = (bf16[32,4096]{1,0:T(8,128)(2,1)S(1)}, bf16[32,4096]{1,0:T(8,128)(2,1)S(1)}, u32[]{:S(2)}, u32[]{:S(2)}) collective-permute-start(bf16[32,4096]{1,0:T(8,128)(2,1)S(1)} %get-tuple-element.79), channel_id=1, source_target_pairs={{0,4},{4,0},{8,12},{12,8},{1,5},{5,1},{9,13},{13,9},{2,6},{6,2},{1... | collective-permute-start | bytes 786440 | tf_op jit(solution)/shard_map/ppermute | solution.py:97
  66.2 3.4 %collective-permute-start.23 = (bf16[32,4096]{1,0:T(8,128)(2,1)S(1)}, bf16[32,4096]{1,0:T(8,128)(2,1)S(1)}, u32[]{:S(2)}, u32[]{:S(2)}) collective-permute-start(bf16[32,4096]{1,0:T(8,128)(2,1)S(1)} %get-tuple-element.75), channel_id=1, source_target_pairs={{0,4},{4,0},{8,12},{12,8},{1,5},{5,1},{9,13},{13,9},{2,6},{6,2},{1... | collective-permute-start | bytes 786440 | tf_op jit(solution)/shard_map/ppermute | solution.py:97
  70.5 4.4 %collective-permute-start.26 = (bf16[32,4096]{1,0:T(8,128)(2,1)S(1)}, bf16[32,4096]{1,0:T(8,128)(2,1)S(1)}, u32[]{:S(2)}, u32[]{:S(2)}) collective-permute-start(bf16[32,4096]{1,0:T(8,128)(2,1)S(1)} %fusion.1), channel_id=1, source_target_pairs={{0,4},{4,0},{8,12},{12,8},{1,5},{5,1},{9,13},{13,9},{2,6},{6,2},{1... | collective-permute-start | bytes 786440 | tf_op jit(solution)/shard_map/ppermute | solution.py:103
  75.8 4.8 %collective-permute-start.22 = (bf16[32,4096]{1,0:T(8,128)(2,1)S(1)}, bf16[32,4096]{1,0:T(8,128)(2,1)S(1)}, u32[]{:S(2)}, u32[]{:S(2)}) collective-permute-start(bf16[32,4096]{1,0:T(8,128)(2,1)S(1)} %fusion), channel_id=1, source_target_pairs={{0,4},{4,0},{8,12},{12,8},{1,5},{5,1},{9,13},{13,9},{2,6},{6,2},{1... | collective-permute-start | bytes 786440 | tf_op jit(solution)/shard_map/ppermute | solution.py:103
  81.3 4.6 %collective-permute-done.26 = bf16[32,4096]{1,0:T(8,128)(2,1)S(1)} collective-permute-done((bf16[32,4096]{1,0:T(8,128)(2,1)S(1)}, bf16[32,4096]{1,0:T(8,128)(2,1)S(1)}, u32[]{:S(2)}, u32[]{:S(2)}) %collective-permute-start.26) | collective-permute-done | bytes 262176 | tf_op jit(solution)/shard_map/ppermute | solution.py:103
  86.0 5.1 %collective-permute-done.22 = bf16[32,4096]{1,0:T(8,128)(2,1)S(1)} collective-permute-done((bf16[32,4096]{1,0:T(8,128)(2,1)S(1)}, bf16[32,4096]{1,0:T(8,128)(2,1)S(1)}, u32[]{:S(2)}, u32[]{:S(2)}) %collective-permute-start.22) | collective-permute-done | bytes 262176 | tf_op jit(solution)/shard_map/ppermute | solution.py:103
  (56 shorter events, 16.4 us)
Async XLA Ops:
  0.6 23.5 %collective-permute-start.8 = (bf16[96,8192]{1,0:T(8,128)(2,1)}, bf16[96,8192]{1,0:T(8,128)(2,1)S(1)}, u32[]{:S(2)}, u32[]{:S(2)}) collective-permute-start(bf16[96,8192]{1,0:T(8,128)(2,1)} %refs_0_.1), channel_id=1, source_target_pairs={{0,1},{1,0},{2,3},{3,2},{4,5},{5,4},{6,7},{7,6},{8,9},{9,8},{10,11... | collective-permute-start | bytes 4718600 | tf_op jit(solution)/shard_map/ppermute | solution.py:20
  1.1 37.8 %collective-permute-start.9 = (bf16[96,8192]{1,0:T(8,128)(2,1)}, bf16[96,8192]{1,0:T(8,128)(2,1)S(1)}, u32[]{:S(2)}, u32[]{:S(2)}) collective-permute-start(bf16[96,8192]{1,0:T(8,128)(2,1)} %refs_0_.1), channel_id=1, source_target_pairs={{0,2},{1,3},{2,0},{3,1},{4,6},{5,7},{6,4},{7,5},{8,10},{9,11},{10,... | collective-permute-start | bytes 4718600 | tf_op jit(solution)/shard_map/ppermute | solution.py:20
  4.7 9.9 %collective-permute-start.4 = (bf16[32,4608]{1,0:T(8,128)(2,1)S(1)}, bf16[32,4608]{1,0:T(8,128)(2,1)S(1)}, u32[]{:S(2)}, u32[]{:S(2)}) collective-permute-start(bf16[32,4608]{1,0:T(8,128)(2,1)S(1)} %slice.9.refs_2_), channel_id=1, source_target_pairs={{0,4},{4,0},{8,12},{12,8},{1,5},{5,1},{9,13},{13,9},{2,6},{6,2},{1... | collective-permute-start | bytes 884744 | tf_op jit(solution)/shard_map/ppermute | solution.py:43
  6.3 8.9 %collective-permute-start.5 = (bf16[32,4608]{1,0:T(8,128)(2,1)S(1)}, bf16[32,4608]{1,0:T(8,128)(2,1)S(1)}, u32[]{:S(2)}, u32[]{:S(2)}) collective-permute-start(bf16[32,4608]{1,0:T(8,128)(2,1)S(1)} %slice.9.refs_2_), channel_id=1, source_target_pairs={{4,8},{8,4},{5,9},{9,5},{6,10},{10,6},{7,11},{11,7},{20,24},{24,20... | collective-permute-start | bytes 884744 | tf_op jit(solution)/shard_map/ppermute | solution.py:43
  8.0 11.8 %collective-permute-start = (bf16[32,3584]{1,0:T(8,128)(2,1)S(1)}, bf16[32,3584]{1,0:T(8,128)(2,1)S(1)}, u32[]{:S(2)}, u32[]{:S(2)}) collective-permute-start(bf16[32,3584]{1,0:T(8,128)(2,1)S(1)} %slice.8.refs_3_), channel_id=1, source_target_pairs={{0,4},{4,0},{8,12},{12,8},{1,5},{5,1},{9,13},{13,9},{2,6},{6,2},{1... | collective-permute-start | bytes 688136 | tf_op jit(solution)/shard_map/ppermute | solution.py:43
  14.6 5.8 %collective-permute-start.1 = (bf16[32,3584]{1,0:T(8,128)(2,1)S(1)}, bf16[32,3584]{1,0:T(8,128)(2,1)S(1)}, u32[]{:S(2)}, u32[]{:S(2)}) collective-permute-start(bf16[32,3584]{1,0:T(8,128)(2,1)S(1)} %slice.8.refs_3_), channel_id=1, source_target_pairs={{4,8},{8,4},{5,9},{9,5},{6,10},{10,6},{7,11},{11,7},{20,24},{24,20... | collective-permute-start | bytes 688136 | tf_op jit(solution)/shard_map/ppermute | solution.py:43
  15.3 12.8 %collective-permute-start.6 = (bf16[32,4608]{1,0:T(8,128)(2,1)S(1)}, bf16[32,4608]{1,0:T(8,128)(2,1)S(1)}, u32[]{:S(2)}, u32[]{:S(2)}) collective-permute-start(bf16[32,4608]{1,0:T(8,128)(2,1)S(1)} %collective-permute-done.5.refs_5_), channel_id=1, source_target_pairs={{0,4},{4,0},{8,12},{12,8},{1,5},{5,1},{9,13},{13,9},{2,6},{6,2},{1... | collective-permute-start | bytes 884744 | tf_op jit(solution)/shard_map/ppermute | solution.py:52
  19.8 8.4 %collective-permute-start.7 = (bf16[32,4608]{1,0:T(8,128)(2,1)S(1)}, bf16[32,4608]{1,0:T(8,128)(2,1)S(1)}, u32[]{:S(2)}, u32[]{:S(2)}) collective-permute-start(bf16[32,4608]{1,0:T(8,128)(2,1)S(1)} %collective-permute-done.4.refs_4_), channel_id=1, source_target_pairs={{4,8},{8,4},{5,9},{9,5},{6,10},{10,6},{7,11},{11,7},{20,24},{24,20... | collective-permute-start | bytes 884744 | tf_op jit(solution)/shard_map/ppermute | solution.py:53
  20.4 11.7 %collective-permute-start.2 = (bf16[32,3584]{1,0:T(8,128)(2,1)S(1)}, bf16[32,3584]{1,0:T(8,128)(2,1)S(1)}, u32[]{:S(2)}, u32[]{:S(2)}) collective-permute-start(bf16[32,3584]{1,0:T(8,128)(2,1)S(1)} %collective-permute-done.1.refs_7_), channel_id=1, source_target_pairs={{0,4},{4,0},{8,12},{12,8},{1,5},{5,1},{9,13},{13,9},{2,6},{6,2},{1... | collective-permute-start | bytes 688136 | tf_op jit(solution)/shard_map/ppermute | solution.py:52
  24.1 8.0 %collective-permute-start.3 = (bf16[32,3584]{1,0:T(8,128)(2,1)S(1)}, bf16[32,3584]{1,0:T(8,128)(2,1)S(1)}, u32[]{:S(2)}, u32[]{:S(2)}) collective-permute-start(bf16[32,3584]{1,0:T(8,128)(2,1)S(1)} %collective-permute-done.refs_5_), channel_id=1, source_target_pairs={{4,8},{8,4},{5,9},{9,5},{6,10},{10,6},{7,11},{11,7},{20,24},{24,20... | collective-permute-start | bytes 688136 | tf_op jit(solution)/shard_map/ppermute | solution.py:53
  28.1 13.7 %collective-permute-start.10 = (bf16[32,4608]{1,0:T(8,128)(2,1)S(1)}, bf16[32,4608]{1,0:T(8,128)(2,1)S(1)}, u32[]{:S(2)}, u32[]{:S(2)}) collective-permute-start(bf16[32,4608]{1,0:T(8,128)(2,1)S(1)} %collective-permute-done.7.refs_1_), channel_id=1, source_target_pairs={{0,4},{4,0},{8,12},{12,8},{1,5},{5,1},{9,13},{13,9},{2,6},{6,2},{1... | collective-permute-start | bytes 884744 | tf_op jit(solution)/shard_map/ppermute | solution.py:55
  32.2 9.6 %collective-permute-start.11 = (bf16[32,3584]{1,0:T(8,128)(2,1)S(1)}, bf16[32,3584]{1,0:T(8,128)(2,1)S(1)}, u32[]{:S(2)}, u32[]{:S(2)}) collective-permute-start(bf16[32,3584]{1,0:T(8,128)(2,1)S(1)} %collective-permute-done.3.refs_3_), channel_id=1, source_target_pairs={{0,4},{4,0},{8,12},{12,8},{1,5},{5,1},{9,13},{13,9},{2,6},{6,2},{1... | collective-permute-start | bytes 688136 | tf_op jit(solution)/shard_map/ppermute | solution.py:55
  41.8 4.1 %collective-permute-start.12 = (bf16[96,8192]{1,0:T(8,128)(2,1)S(1)}, bf16[96,8192]{1,0:T(8,128)(2,1)S(1)}, u32[]{:S(2)}, u32[]{:S(2)}) collective-permute-start(bf16[96,8192]{1,0:T(8,128)(2,1)S(1)} %collective-permute-done.9.refs_1_), channel_id=1, source_target_pairs={{0,1},{1,0},{2,3},{3,2},{4,5},{5,4},{6,7},{7,6},{8,9},{9,8},{10,11... | collective-permute-start | bytes 4718600 | tf_op jit(solution)/shard_map/ppermute | solution.py:20
  48.5 3.6 %collective-permute-start.17 = (f32[1,384]{1,0:T(1,128)S(1)}, f32[1,384]{1,0:T(1,128)S(1)}, u32[]{:S(2)}, u32[]{:S(2)}) collective-permute-start(f32[1,384]{1,0:T(1,128)S(1)} %get-tuple-element.69.refs_0_), channel_id=1, source_target_pairs={{0,2},{1,3},{2,0},{3,1},{4,6},{5,7},{6,4},{7,5},{8,10},{9,11},{10,... | collective-permute-start | bytes 4616 | tf_op jit(solution)/shard_map/ppermute | solution.py:20
  54.2 9.2 %collective-permute-start.19 = (bf16[32,4096]{1,0:T(8,128)(2,1)S(1)}, bf16[32,4096]{1,0:T(8,128)(2,1)S(1)}, u32[]{:S(2)}, u32[]{:S(2)}) collective-permute-start(bf16[32,4096]{1,0:T(8,128)(2,1)S(1)} %get-tuple-element.74), channel_id=1, source_target_pairs={{0,4},{4,0},{8,12},{12,8},{1,5},{5,1},{9,13},{13,9},{2,6},{6,2},{1... | collective-permute-start | bytes 786440 | tf_op jit(solution)/shard_map/ppermute | solution.py:93
  56.3 13.3 %collective-permute-start.20 = (bf16[32,4096]{1,0:T(8,128)(2,1)S(1)}, bf16[32,4096]{1,0:T(8,128)(2,1)S(1)}, u32[]{:S(2)}, u32[]{:S(2)}) collective-permute-start(bf16[32,4096]{1,0:T(8,128)(2,1)S(1)} %get-tuple-element.76), channel_id=1, source_target_pairs={{0,4},{4,0},{8,12},{12,8},{1,5},{5,1},{9,13},{13,9},{2,6},{6,2},{1... | collective-permute-start | bytes 786440 | tf_op jit(solution)/shard_map/ppermute | solution.py:93
  63.4 11.5 %collective-permute-start.27 = (bf16[32,4096]{1,0:T(8,128)(2,1)S(1)}, bf16[32,4096]{1,0:T(8,128)(2,1)S(1)}, u32[]{:S(2)}, u32[]{:S(2)}) collective-permute-start(bf16[32,4096]{1,0:T(8,128)(2,1)S(1)} %get-tuple-element.79), channel_id=1, source_target_pairs={{0,4},{4,0},{8,12},{12,8},{1,5},{5,1},{9,13},{13,9},{2,6},{6,2},{1... | collective-permute-start | bytes 786440 | tf_op jit(solution)/shard_map/ppermute | solution.py:97
  65.5 4.9 %collective-permute-start.25 = (bf16[32,4096]{1,0:T(8,128)(2,1)S(1)}, bf16[32,4096]{1,0:T(8,128)(2,1)S(1)}, u32[]{:S(2)}, u32[]{:S(2)}) collective-permute-start(bf16[32,4096]{1,0:T(8,128)(2,1)S(1)} %add_convert_fusion.2), channel_id=1, source_target_pairs={{4,8},{8,4},{5,9},{9,5},{6,10},{10,6},{7,11},{11,7},{20,24},{24,20... | collective-permute-start | bytes 786440 | tf_op jit(solution)/shard_map/ppermute | solution.py:100
  66.2 14.3 %collective-permute-start.23 = (bf16[32,4096]{1,0:T(8,128)(2,1)S(1)}, bf16[32,4096]{1,0:T(8,128)(2,1)S(1)}, u32[]{:S(2)}, u32[]{:S(2)}) collective-permute-start(bf16[32,4096]{1,0:T(8,128)(2,1)S(1)} %get-tuple-element.75), channel_id=1, source_target_pairs={{0,4},{4,0},{8,12},{12,8},{1,5},{5,1},{9,13},{13,9},{2,6},{6,2},{1... | collective-permute-start | bytes 786440 | tf_op jit(solution)/shard_map/ppermute | solution.py:97
  69.7 6.0 %collective-permute-start.21 = (bf16[32,4096]{1,0:T(8,128)(2,1)S(1)}, bf16[32,4096]{1,0:T(8,128)(2,1)S(1)}, u32[]{:S(2)}, u32[]{:S(2)}) collective-permute-start(bf16[32,4096]{1,0:T(8,128)(2,1)S(1)} %add_convert_fusion.5), channel_id=1, source_target_pairs={{4,8},{8,4},{5,9},{9,5},{6,10},{10,6},{7,11},{11,7},{20,24},{24,20... | collective-permute-start | bytes 786440 | tf_op jit(solution)/shard_map/ppermute | solution.py:100
  70.5 15.4 %collective-permute-start.26 = (bf16[32,4096]{1,0:T(8,128)(2,1)S(1)}, bf16[32,4096]{1,0:T(8,128)(2,1)S(1)}, u32[]{:S(2)}, u32[]{:S(2)}) collective-permute-start(bf16[32,4096]{1,0:T(8,128)(2,1)S(1)} %fusion.1), channel_id=1, source_target_pairs={{0,4},{4,0},{8,12},{12,8},{1,5},{5,1},{9,13},{13,9},{2,6},{6,2},{1... | collective-permute-start | bytes 786440 | tf_op jit(solution)/shard_map/ppermute | solution.py:103
  75.0 10.9 %collective-permute-start.28 = (bf16[32,4096]{1,0:T(8,128)(2,1)S(1)}, bf16[32,4096]{1,0:T(8,128)(2,1)S(1)}, u32[]{:S(2)}, u32[]{:S(2)}) collective-permute-start(bf16[32,4096]{1,0:T(8,128)(2,1)S(1)} %add_convert_fusion), channel_id=1, source_target_pairs={{4,8},{8,4},{5,9},{9,5},{6,10},{10,6},{7,11},{11,7},{20,24},{24,20... | collective-permute-start | bytes 786440 | tf_op jit(solution)/shard_map/ppermute | solution.py:101
  75.8 15.2 %collective-permute-start.22 = (bf16[32,4096]{1,0:T(8,128)(2,1)S(1)}, bf16[32,4096]{1,0:T(8,128)(2,1)S(1)}, u32[]{:S(2)}, u32[]{:S(2)}) collective-permute-start(bf16[32,4096]{1,0:T(8,128)(2,1)S(1)} %fusion), channel_id=1, source_target_pairs={{0,4},{4,0},{8,12},{12,8},{1,5},{5,1},{9,13},{13,9},{2,6},{6,2},{1... | collective-permute-start | bytes 786440 | tf_op jit(solution)/shard_map/ppermute | solution.py:103
  80.6 10.4 %collective-permute-start.24 = (bf16[32,4096]{1,0:T(8,128)(2,1)S(1)}, bf16[32,4096]{1,0:T(8,128)(2,1)S(1)}, u32[]{:S(2)}, u32[]{:S(2)}) collective-permute-start(bf16[32,4096]{1,0:T(8,128)(2,1)S(1)} %add_convert_fusion.3), channel_id=1, source_target_pairs={{4,8},{8,4},{5,9},{9,5},{6,10},{10,6},{7,11},{11,7},{20,24},{24,20... | collective-permute-start | bytes 786440 | tf_op jit(solution)/shard_map/ppermute | solution.py:101
  (8 other events, 31.9 us)

commit v11 on v10

--- a/solution.py
+++ b/solution.py
@@ -59,7 +59,8 @@
     weights = stage_rest([far_parts, end_parts], weighted, penalty, noise)
     ends = [parts[0] for parts in end_parts]
     routes, crossed, *_ = lax.optimization_barrier((routes, crossed, *ends))
-    return weights, near, swap_gather(crossed, "reader", near_bits), swap_all(routes)
+    far = [[one] for one in swap_gather(crossed, "reader", near_bits)]
+    return weights, near, far, swap_all(routes)
 
 
 def swap_all(routes):
@@ -72,7 +73,7 @@
     line = [[[one]] for one in line_gather(block, "blk")]
     weighted, penalty, near, noise = stage(line[:2], near, noise)
     weights = stage_rest(line[2:], weighted, penalty, noise)
-    return weights, near, far, swap_all(routes)
+    return weights, near, [[one] for one in far], swap_all(routes)
 
 
 def line_gather(block, axis):
@@ -270,12 +271,17 @@
 def stage_rest_kernel(counts, *refs):
     refs = list(refs)
     groups = take_blocks(refs, counts)
-    early_ref, early_penalty_ref, noise_ref, weighted_ref, penalty_ref, block_ref, sems = refs
+    early_ref, early_penalty_ref, noise_ref, turned_ref, penalty_ref = refs[:5]
+    weighted_ref, block_ref, sems = refs[5:]
     done = early_ref.shape[0]
     weighted_ref[:done, :] = early_ref[...]
     penalty_ref[:done, :] = early_penalty_ref[...]
     first = done // block_ref.shape[1]
     weigh_blocks(groups, noise_ref, weighted_ref, penalty_ref, block_ref, sems, first)
+    width = weighted_ref.shape[1]
+    for start in range(0, width, STEP):
+        piece = slice(start, min(start + STEP, width))
+        turned_ref[piece, :] = weighted_ref[:, piece].T
 
 
 def stage_rest(blocks, weighted, penalty, noise):
@@ -287,12 +293,13 @@
     return pl.pallas_call(
         partial(stage_rest_kernel, block_counts(blocks)),
         out_shape=(
-            jax.ShapeDtypeStruct((refs, width), jnp.bfloat16),
+            jax.ShapeDtypeStruct((width, refs), jnp.bfloat16),
             jax.ShapeDtypeStruct((refs, 1), jnp.float32),
         ),
         in_specs=[ANY_SPEC] * len(moved) + [VMEM_SPEC] * 3,
         out_specs=(VMEM_SPEC,) * 2,
         scratch_shapes=[
+            pltpu.VMEM((refs, width), jnp.bfloat16),
             pltpu.VMEM((len(blocks), count, width), jnp.bfloat16),
             pltpu.SemaphoreType.DMA((parts,)),
         ],
@@ -304,11 +311,11 @@
     )(*moved, weighted, penalty, noise)
 
 
-def score_kernel(readers, finish, *refs):
+def score_kernel(readers, far_counts, finish, *refs):
     refs = list(refs)
     near_ref = refs.pop(0)
     rows = near_ref.shape[0] * 2 // readers
-    far_refs = [refs.pop(0) for _ in range(readers // 2)]
+    far_refs = [[refs.pop(0) for _ in range(n)] for n in far_counts]
     weighted_ref, penalty_ref = refs.pop(0), refs.pop(0)
     route_refs = [refs.pop(0) for _ in range(readers)]
     score_ref, mask_ref, lse_ref, all_ref, image_sems = refs
@@ -316,13 +323,18 @@
     copies = []
     for k in range(readers):
         if k < readers // 2:
-            source = near_ref.at[pl.ds(k * rows, rows), :]
+            sources = [near_ref.at[pl.ds(k * rows, rows), :]]
         else:
-            source = far_refs[k - readers // 2]
-        row = pl.multiple_of((reader ^ k) * rows, 16)
-        copy = pltpu.make_async_copy(source, all_ref.at[pl.ds(row, rows), :], image_sems.at[k])
-        copy.start()
-        copies.append(copy)
+            sources = far_refs[k - readers // 2]
+        row, start = pl.multiple_of((reader ^ k) * rows, 16), 0
+        for source in sources:
+            columns = pl.ds(start, source.shape[1])
+            copy = pltpu.make_async_copy(
+                source, all_ref.at[pl.ds(row, rows), columns], image_sems.at[len(copies)]
+            )
+            copy.start()
+            copies.append(copy)
+            start += source.shape[1]
     routes = [ref[...] for ref in route_refs]
     bit = 1
     while bit < readers:
@@ -335,12 +347,7 @@
             mask_ref[k : k + 1, j * rows : (j + 1) * rows] = jnp.max(hits, axis=0, keepdims=True)
     for copy in copies:
         copy.wait()
-    scores = lax.dot_general(
-        all_ref[...],
-        weighted_ref[...],
-        (((1,), (1,)), ((), ())),
-        preferred_element_type=jnp.float32,
-    )
+    scores = jnp.dot(all_ref[...], weighted_ref[...], preferred_element_type=jnp.float32)
     scores = scores.T - penalty_ref[...]
     score_ref[...] = scores
     if finish:
@@ -349,11 +356,11 @@
 
 def all_scores(weights, near, far, routes, finish):
     weighted, penalty = weights
-    refs, width = weighted.shape
+    width, refs = weighted.shape
     slots = 2 * near.shape[0]
-    moved = [near, *far]
+    moved = [near, *[one for group in far for one in group]]
     return pl.pallas_call(
-        partial(score_kernel, len(routes), finish),
+        partial(score_kernel, len(routes), [len(group) for group in far], finish),
         out_shape=(
             jax.ShapeDtypeStruct((refs, slots), jnp.float32),
             jax.ShapeDtypeStruct((len(routes), slots), jnp.float32),
@@ -362,7 +369,7 @@
         ),
         in_specs=[ANY_SPEC] * len(moved) + [VMEM_SPEC] * (2 + len(routes)),
         out_specs=(VMEM_SPEC,) * 4,
-        scratch_shapes=[pltpu.SemaphoreType.DMA((len(routes),))],
+        scratch_shapes=[pltpu.SemaphoreType.DMA((len(moved) + len(routes),))],
         compiler_params=pltpu.CompilerParams(vmem_limit_bytes=SCORE_VMEM),
         cost_estimate=pl.CostEstimate(
             flops=2 * refs * slots * width,
@@ -438,7 +445,7 @@
     rows, width = images.shape
     noise = noise_weights.reshape(1, width)
 
-    gather = staged_gather if members == 4 and rows % 32 == 0 and readers > 1 else plain_gather
+    gather = staged_gather if members == 4 and rows % 16 == 0 and readers > 1 else plain_gather
     weights, near, far, route_blocks = gather(
         projections[0], images, noise, routes.T, readers // 4, readers // 2
     )

time: 92.6 us -> 92.6 us (level)
  transfers between devices with their start and end apart: 29 -> 29, of which waited for: 10 -> 9; matrix products, arithmetic and copies ran while one was open for 3% -> 3% of each run, Pallas kernels for 2% -> 3%
where the time goes in v11:
time: 92.6 us; the launch traced here: 92.2 us
  starting transfers between devices  50.7 us (55%)
  waiting for transfers between devices  28 us (30%)
  Pallas kernels  7.32 us (8%)
  local copies, waits for them, and re-layouts  4.68 us (5%)
    ppermute x2, waiting for transfers between devices, pair_scatter(): from_side = lax.ppermute(near, axis, SIDES)  9.61 us
    ppermute x2, starting transfers between devices, pair_scatter(): from_side = lax.ppermute(near, axis, SIDES)  9.16 us
    ppermute x2, starting transfers between devices, staged_gather(): far = lax.ppermute(across, 'blk', SIDES)  8.16 us
    ppermute x2, starting transfers between devices, staged_gather(): end = lax.ppermute(across_far, 'blk', SIDES)  7.26 us
    ppermute x9, starting transfers between devices, swap_bits(): lax.ppermute(block, axis, [(i, i ^ bits) for i in range(lax.axis_size(axi...  6.97 us
    ppermute x9, waiting for transfers between devices, swap_bits(): lax.ppermute(block, axis, [(i, i ^ bits) for i in range(lax.axis_size(axi...  6.83 us
    ppermute x2, waiting for transfers between devices, pair_scatter(): for_far_end = [lax.ppermute(parts[3], axis, SIDES) for parts in pieces]  6.42 us
    ppermute x2, starting transfers between devices, staged_gather(): lax.ppermute(one, 'blk', SIDES)  6.09 us
  transfers between devices with their start and end apart: 29, of which 9 were waited for; matrix products, arithmetic and copies ran while one was open for 3% of the time, Pallas kernels for 3%

profile of v11, /device:TPU:0, one launch (start us, length us, event | category | flops | bytes accessed | tf_op | source)
XLA Modules:
  0.0 92.2 jit_solution(15604167035000859731)
XLA Ops:
  1.1 2.6 %collective-permute-start.9 = (bf16[96,8192]{1,0:T(8,128)(2,1)}, bf16[96,8192]{1,0:T(8,128)(2,1)S(1)}, u32[]{:S(2)}, u32[]{:S(2)}) collective-permute-start(bf16[96,8192]{1,0:T(8,128)(2,1)} %refs_0_.1), channel_id=1, source_target_pairs={{0,2},{1,3},{2,0},{3,1},{4,6},{5,7},{6,4},{7,5},{8,10},{9,11},{10,... | collective-permute-start | bytes 4718600 | tf_op jit(solution)/shard_map/ppermute | solution.py:20
  4.7 1.6 %collective-permute-start.4 = (bf16[32,4608]{1,0:T(8,128)(2,1)S(1)}, bf16[32,4608]{1,0:T(8,128)(2,1)S(1)}, u32[]{:S(2)}, u32[]{:S(2)}) collective-permute-start(bf16[32,4608]{1,0:T(8,128)(2,1)S(1)} %slice.9.refs_2_), channel_id=1, source_target_pairs={{0,4},{4,0},{8,12},{12,8},{1,5},{5,1},{9,13},{13,9},{2,6},{6,2},{1... | collective-permute-start | bytes 884744 | tf_op jit(solution)/shard_map/ppermute | solution.py:43
  8.0 4.4 %collective-permute-start = (bf16[32,3584]{1,0:T(8,128)(2,1)S(1)}, bf16[32,3584]{1,0:T(8,128)(2,1)S(1)}, u32[]{:S(2)}, u32[]{:S(2)}) collective-permute-start(bf16[32,3584]{1,0:T(8,128)(2,1)S(1)} %slice.8.refs_3_), channel_id=1, source_target_pairs={{0,4},{4,0},{8,12},{12,8},{1,5},{5,1},{9,13},{13,9},{2,6},{6,2},{1... | collective-permute-start | bytes 688136 | tf_op jit(solution)/shard_map/ppermute | solution.py:43
  12.4 2.2 %collective-permute-done.4.refs_4_ = bf16[32,4608]{1,0:T(8,128)(2,1)S(1)} collective-permute-done((bf16[32,4608]{1,0:T(8,128)(2,1)S(1)}, bf16[32,4608]{1,0:T(8,128)(2,1)S(1)}, u32[]{:S(2)}, u32[]{:S(2)}) %collective-permute-start.4) | collective-permute-done | bytes 294944 | tf_op jit(solution)/shard_map/ppermute | solution.py:43
  15.3 4.5 %collective-permute-start.6 = (bf16[32,4608]{1,0:T(8,128)(2,1)S(1)}, bf16[32,4608]{1,0:T(8,128)(2,1)S(1)}, u32[]{:S(2)}, u32[]{:S(2)}) collective-permute-start(bf16[32,4608]{1,0:T(8,128)(2,1)S(1)} %collective-permute-done.5.refs_5_), channel_id=1, source_target_pairs={{0,4},{4,0},{8,12},{12,8},{1,5},{5,1},{9,13},{13,9},{2,6},{6,2},{1... | collective-permute-start | bytes 884744 | tf_op jit(solution)/shard_map/ppermute | solution.py:52
  20.4 3.7 %collective-permute-start.2 = (bf16[32,3584]{1,0:T(8,128)(2,1)S(1)}, bf16[32,3584]{1,0:T(8,128)(2,1)S(1)}, u32[]{:S(2)}, u32[]{:S(2)}) collective-permute-start(bf16[32,3584]{1,0:T(8,128)(2,1)S(1)} %collective-permute-done.1.refs_7_), channel_id=1, source_target_pairs={{0,4},{4,0},{8,12},{12,8},{1,5},{5,1},{9,13},{13,9},{2,6},{6,2},{1... | collective-permute-start | bytes 688136 | tf_op jit(solution)/shard_map/ppermute | solution.py:52
  24.8 1.4 %copy-done = bf16[96,8192]{1,0:T(8,128)(2,1)S(1)} copy-done((bf16[96,8192]{1,0:T(8,128)(2,1)S(1)}, bf16[96,8192]{1,0:T(8,128)(2,1)}, u32[]{:S(2)}) %copy-start) | copy-done | bytes 1572888
  28.1 4.0 %collective-permute-start.10 = (bf16[32,4608]{1,0:T(8,128)(2,1)S(1)}, bf16[32,4608]{1,0:T(8,128)(2,1)S(1)}, u32[]{:S(2)}, u32[]{:S(2)}) collective-permute-start(bf16[32,4608]{1,0:T(8,128)(2,1)S(1)} %collective-permute-done.7.refs_1_), channel_id=1, source_target_pairs={{0,4},{4,0},{8,12},{12,8},{1,5},{5,1},{9,13},{13,9},{2,6},{6,2},{1... | collective-permute-start | bytes 884744 | tf_op jit(solution)/shard_map/ppermute | solution.py:55
  32.2 3.2 %collective-permute-start.11 = (bf16[32,3584]{1,0:T(8,128)(2,1)S(1)}, bf16[32,3584]{1,0:T(8,128)(2,1)S(1)}, u32[]{:S(2)}, u32[]{:S(2)}) collective-permute-start(bf16[32,3584]{1,0:T(8,128)(2,1)S(1)} %collective-permute-done.3.refs_3_), channel_id=1, source_target_pairs={{0,4},{4,0},{8,12},{12,8},{1,5},{5,1},{9,13},{13,9},{2,6},{6,2},{1... | collective-permute-start | bytes 688136 | tf_op jit(solution)/shard_map/ppermute | solution.py:55
  35.4 3.5 %collective-permute-done.9.refs_1_ = bf16[96,8192]{1,0:T(8,128)(2,1)S(1)} collective-permute-done((bf16[96,8192]{1,0:T(8,128)(2,1)}, bf16[96,8192]{1,0:T(8,128)(2,1)S(1)}, u32[]{:S(2)}, u32[]{:S(2)}) %collective-permute-start.9) | collective-permute-done | bytes 1572896 | tf_op jit(solution)/shard_map/ppermute | solution.py:20
  38.9 2.9 %collective-permute-done.11.refs_6_ = bf16[32,3584]{1,0:T(8,128)(2,1)S(1)} collective-permute-done((bf16[32,3584]{1,0:T(8,128)(2,1)S(1)}, bf16[32,3584]{1,0:T(8,128)(2,1)S(1)}, u32[]{:S(2)}, u32[]{:S(2)}) %collective-permute-start.11) | collective-permute-done | bytes 229408 | tf_op jit(solution)/shard_map/ppermute | solution.py:55
  43.7 1.5 %stage_rest.1 = (bf16[8192,128]{1,0:T(8,128)(2,1)S(1)}, f32[128,1]{1,0:T(8,128)S(1)}) custom-call(bf16[32,4608]{1,0:T(8,128)(2,1)S(1)} %collective-permute-done.6.refs_0_, bf16[32,4608]{1,0:T(8,128)(2,1)S(1)} %collective-permute-done.7.refs_1_, bf16[32,3584]{1,0:T(8,128)(2,1)S(1)} %collective-permute-done.2.refs_2_, ...), custom_call_target="tpu_custom_call" | custom-call | flops 8388608 | bytes 12000000 | tf_op jit(solution)/shard_map/stage_rest/pallas_call | solution.py:293
  45.9 2.5 %scores.1 = (f32[128,384]{1,0:T(8,128)S(1)}, f32[4,384]{1,0:T(4,128)S(1)}, f32[1,384]{1,0:T(1,128)S(1)}, bf16[384,8192]{1,0:T(8,128)(2,1)S(1)}) custom-call(bf16[192,8192]{1,0:T(8,128)(2,1)S(1)} %get-tuple-element.54.refs_0_, bf16[96,8192]{1,0:T(8,128)(2,1)S(1)} %collective-permute-done.9.refs_1_, bf16[96,8192]{1,0:T(8,128)(2,1)S(1)} %collective-permute-done.12.refs_2_, ...), custom_call_target="tpu_custom_call" | custom-call | flops 805306368 | bytes 8388608 | tf_op jit(solution)/shard_map/scores/pallas_call | solution.py:362
  48.6 1.4 %collective-permute-start.17 = (f32[1,384]{1,0:T(1,128)S(1)}, f32[1,384]{1,0:T(1,128)S(1)}, u32[]{:S(2)}, u32[]{:S(2)}) collective-permute-start(f32[1,384]{1,0:T(1,128)S(1)} %get-tuple-element.69.refs_0_), channel_id=1, source_target_pairs={{0,2},{1,3},{2,0},{3,1},{4,6},{5,7},{6,4},{7,5},{8,10},{9,11},{10,... | collective-permute-start | bytes 4616 | tf_op jit(solution)/shard_map/ppermute | solution.py:20
  50.3 1.8 %collective-permute-done.17.refs_2_ = f32[1,384]{1,0:T(1,128)S(1)} collective-permute-done((f32[1,384]{1,0:T(1,128)S(1)}, f32[1,384]{1,0:T(1,128)S(1)}, u32[]{:S(2)}, u32[]{:S(2)}) %collective-permute-start.17) | collective-permute-done | bytes 1568 | tf_op jit(solution)/shard_map/ppermute | solution.py:20
  53.0 1.3 %sums.1 = (f32[1,384]{1,0:T(1,128)S(1)}, bf16[32,4096]{1,0:T(8,128)(2,1)S(1)}, bf16[32,4096]{1,0:T(8,128)(2,1)S(1)}, bf16[32,4096]{1,0:T(8,128)(2,1)S(1)}, bf16[...) custom-call(bf16[384,8192]{1,0:T(8,128)(2,1)S(1)} %get-tuple-element, ...), custom_call_target="tpu_custom_call" | custom-call | flops 805306368 | bytes 6291456 | tf_op jit(solution)/shard_map/sums/pallas_call | solution.py:425
  54.2 2.1 %collective-permute-start.19 = (bf16[32,4096]{1,0:T(8,128)(2,1)S(1)}, bf16[32,4096]{1,0:T(8,128)(2,1)S(1)}, u32[]{:S(2)}, u32[]{:S(2)}) collective-permute-start(bf16[32,4096]{1,0:T(8,128)(2,1)S(1)} %get-tuple-element.74), channel_id=1, source_target_pairs={{0,4},{4,0},{8,12},{12,8},{1,5},{5,1},{9,13},{13,9},{2,6},{6,2},{1... | collective-permute-start | bytes 786440 | tf_op jit(solution)/shard_map/ppermute | solution.py:94
  57.0 6.4 %collective-permute-done.19 = bf16[32,4096]{1,0:T(8,128)(2,1)S(1)} collective-permute-done((bf16[32,4096]{1,0:T(8,128)(2,1)S(1)}, bf16[32,4096]{1,0:T(8,128)(2,1)S(1)}, u32[]{:S(2)}, u32[]{:S(2)}) %collective-permute-start.19) | collective-permute-done | bytes 262176 | tf_op jit(solution)/shard_map/ppermute | solution.py:94
  63.4 2.1 %collective-permute-start.27 = (bf16[32,4096]{1,0:T(8,128)(2,1)S(1)}, bf16[32,4096]{1,0:T(8,128)(2,1)S(1)}, u32[]{:S(2)}, u32[]{:S(2)}) collective-permute-start(bf16[32,4096]{1,0:T(8,128)(2,1)S(1)} %get-tuple-element.79), channel_id=1, source_target_pairs={{0,4},{4,0},{8,12},{12,8},{1,5},{5,1},{9,13},{13,9},{2,6},{6,2},{1... | collective-permute-start | bytes 786440 | tf_op jit(solution)/shard_map/ppermute | solution.py:98
  66.2 3.5 %collective-permute-start.23 = (bf16[32,4096]{1,0:T(8,128)(2,1)S(1)}, bf16[32,4096]{1,0:T(8,128)(2,1)S(1)}, u32[]{:S(2)}, u32[]{:S(2)}) collective-permute-start(bf16[32,4096]{1,0:T(8,128)(2,1)S(1)} %get-tuple-element.75), channel_id=1, source_target_pairs={{0,4},{4,0},{8,12},{12,8},{1,5},{5,1},{9,13},{13,9},{2,6},{6,2},{1... | collective-permute-start | bytes 786440 | tf_op jit(solution)/shard_map/ppermute | solution.py:98
  70.6 4.4 %collective-permute-start.26 = (bf16[32,4096]{1,0:T(8,128)(2,1)S(1)}, bf16[32,4096]{1,0:T(8,128)(2,1)S(1)}, u32[]{:S(2)}, u32[]{:S(2)}) collective-permute-start(bf16[32,4096]{1,0:T(8,128)(2,1)S(1)} %fusion.1), channel_id=1, source_target_pairs={{0,4},{4,0},{8,12},{12,8},{1,5},{5,1},{9,13},{13,9},{2,6},{6,2},{1... | collective-permute-start | bytes 786440 | tf_op jit(solution)/shard_map/ppermute | solution.py:104
  75.8 4.8 %collective-permute-start.22 = (bf16[32,4096]{1,0:T(8,128)(2,1)S(1)}, bf16[32,4096]{1,0:T(8,128)(2,1)S(1)}, u32[]{:S(2)}, u32[]{:S(2)}) collective-permute-start(bf16[32,4096]{1,0:T(8,128)(2,1)S(1)} %fusion), channel_id=1, source_target_pairs={{0,4},{4,0},{8,12},{12,8},{1,5},{5,1},{9,13},{13,9},{2,6},{6,2},{1... | collective-permute-start | bytes 786440 | tf_op jit(solution)/shard_map/ppermute | solution.py:104
  81.3 4.6 %collective-permute-done.26 = bf16[32,4096]{1,0:T(8,128)(2,1)S(1)} collective-permute-done((bf16[32,4096]{1,0:T(8,128)(2,1)S(1)}, bf16[32,4096]{1,0:T(8,128)(2,1)S(1)}, u32[]{:S(2)}, u32[]{:S(2)}) %collective-permute-start.26) | collective-permute-done | bytes 262176 | tf_op jit(solution)/shard_map/ppermute | solution.py:104
  86.0 5.1 %collective-permute-done.22 = bf16[32,4096]{1,0:T(8,128)(2,1)S(1)} collective-permute-done((bf16[32,4096]{1,0:T(8,128)(2,1)S(1)}, bf16[32,4096]{1,0:T(8,128)(2,1)S(1)}, u32[]{:S(2)}, u32[]{:S(2)}) %collective-permute-start.22) | collective-permute-done | bytes 262176 | tf_op jit(solution)/shard_map/ppermute | solution.py:104
  (56 shorter events, 16.0 us)
Async XLA Ops:
  0.6 23.5 %collective-permute-start.8 = (bf16[96,8192]{1,0:T(8,128)(2,1)}, bf16[96,8192]{1,0:T(8,128)(2,1)S(1)}, u32[]{:S(2)}, u32[]{:S(2)}) collective-permute-start(bf16[96,8192]{1,0:T(8,128)(2,1)} %refs_0_.1), channel_id=1, source_target_pairs={{0,1},{1,0},{2,3},{3,2},{4,5},{5,4},{6,7},{7,6},{8,9},{9,8},{10,11... | collective-permute-start | bytes 4718600 | tf_op jit(solution)/shard_map/ppermute | solution.py:20
  1.1 37.8 %collective-permute-start.9 = (bf16[96,8192]{1,0:T(8,128)(2,1)}, bf16[96,8192]{1,0:T(8,128)(2,1)S(1)}, u32[]{:S(2)}, u32[]{:S(2)}) collective-permute-start(bf16[96,8192]{1,0:T(8,128)(2,1)} %refs_0_.1), channel_id=1, source_target_pairs={{0,2},{1,3},{2,0},{3,1},{4,6},{5,7},{6,4},{7,5},{8,10},{9,11},{10,... | collective-permute-start | bytes 4718600 | tf_op jit(solution)/shard_map/ppermute | solution.py:20
  4.7 9.9 %collective-permute-start.4 = (bf16[32,4608]{1,0:T(8,128)(2,1)S(1)}, bf16[32,4608]{1,0:T(8,128)(2,1)S(1)}, u32[]{:S(2)}, u32[]{:S(2)}) collective-permute-start(bf16[32,4608]{1,0:T(8,128)(2,1)S(1)} %slice.9.refs_2_), channel_id=1, source_target_pairs={{0,4},{4,0},{8,12},{12,8},{1,5},{5,1},{9,13},{13,9},{2,6},{6,2},{1... | collective-permute-start | bytes 884744 | tf_op jit(solution)/shard_map/ppermute | solution.py:43
  6.3 8.9 %collective-permute-start.5 = (bf16[32,4608]{1,0:T(8,128)(2,1)S(1)}, bf16[32,4608]{1,0:T(8,128)(2,1)S(1)}, u32[]{:S(2)}, u32[]{:S(2)}) collective-permute-start(bf16[32,4608]{1,0:T(8,128)(2,1)S(1)} %slice.9.refs_2_), channel_id=1, source_target_pairs={{4,8},{8,4},{5,9},{9,5},{6,10},{10,6},{7,11},{11,7},{20,24},{24,20... | collective-permute-start | bytes 884744 | tf_op jit(solution)/shard_map/ppermute | solution.py:43
  8.0 11.8 %collective-permute-start = (bf16[32,3584]{1,0:T(8,128)(2,1)S(1)}, bf16[32,3584]{1,0:T(8,128)(2,1)S(1)}, u32[]{:S(2)}, u32[]{:S(2)}) collective-permute-start(bf16[32,3584]{1,0:T(8,128)(2,1)S(1)} %slice.8.refs_3_), channel_id=1, source_target_pairs={{0,4},{4,0},{8,12},{12,8},{1,5},{5,1},{9,13},{13,9},{2,6},{6,2},{1... | collective-permute-start | bytes 688136 | tf_op jit(solution)/shard_map/ppermute | solution.py:43
  14.6 5.8 %collective-permute-start.1 = (bf16[32,3584]{1,0:T(8,128)(2,1)S(1)}, bf16[32,3584]{1,0:T(8,128)(2,1)S(1)}, u32[]{:S(2)}, u32[]{:S(2)}) collective-permute-start(bf16[32,3584]{1,0:T(8,128)(2,1)S(1)} %slice.8.refs_3_), channel_id=1, source_target_pairs={{4,8},{8,4},{5,9},{9,5},{6,10},{10,6},{7,11},{11,7},{20,24},{24,20... | collective-permute-start | bytes 688136 | tf_op jit(solution)/shard_map/ppermute | solution.py:43
  15.3 12.8 %collective-permute-start.6 = (bf16[32,4608]{1,0:T(8,128)(2,1)S(1)}, bf16[32,4608]{1,0:T(8,128)(2,1)S(1)}, u32[]{:S(2)}, u32[]{:S(2)}) collective-permute-start(bf16[32,4608]{1,0:T(8,128)(2,1)S(1)} %collective-permute-done.5.refs_5_), channel_id=1, source_target_pairs={{0,4},{4,0},{8,12},{12,8},{1,5},{5,1},{9,13},{13,9},{2,6},{6,2},{1... | collective-permute-start | bytes 884744 | tf_op jit(solution)/shard_map/ppermute | solution.py:52
  19.8 8.4 %collective-permute-start.7 = (bf16[32,4608]{1,0:T(8,128)(2,1)S(1)}, bf16[32,4608]{1,0:T(8,128)(2,1)S(1)}, u32[]{:S(2)}, u32[]{:S(2)}) collective-permute-start(bf16[32,4608]{1,0:T(8,128)(2,1)S(1)} %collective-permute-done.4.refs_4_), channel_id=1, source_target_pairs={{4,8},{8,4},{5,9},{9,5},{6,10},{10,6},{7,11},{11,7},{20,24},{24,20... | collective-permute-start | bytes 884744 | tf_op jit(solution)/shard_map/ppermute | solution.py:53
  20.4 11.7 %collective-permute-start.2 = (bf16[32,3584]{1,0:T(8,128)(2,1)S(1)}, bf16[32,3584]{1,0:T(8,128)(2,1)S(1)}, u32[]{:S(2)}, u32[]{:S(2)}) collective-permute-start(bf16[32,3584]{1,0:T(8,128)(2,1)S(1)} %collective-permute-done.1.refs_7_), channel_id=1, source_target_pairs={{0,4},{4,0},{8,12},{12,8},{1,5},{5,1},{9,13},{13,9},{2,6},{6,2},{1... | collective-permute-start | bytes 688136 | tf_op jit(solution)/shard_map/ppermute | solution.py:52
  24.1 8.0 %collective-permute-start.3 = (bf16[32,3584]{1,0:T(8,128)(2,1)S(1)}, bf16[32,3584]{1,0:T(8,128)(2,1)S(1)}, u32[]{:S(2)}, u32[]{:S(2)}) collective-permute-start(bf16[32,3584]{1,0:T(8,128)(2,1)S(1)} %collective-permute-done.refs_5_), channel_id=1, source_target_pairs={{4,8},{8,4},{5,9},{9,5},{6,10},{10,6},{7,11},{11,7},{20,24},{24,20... | collective-permute-start | bytes 688136 | tf_op jit(solution)/shard_map/ppermute | solution.py:53
  28.1 13.7 %collective-permute-start.10 = (bf16[32,4608]{1,0:T(8,128)(2,1)S(1)}, bf16[32,4608]{1,0:T(8,128)(2,1)S(1)}, u32[]{:S(2)}, u32[]{:S(2)}) collective-permute-start(bf16[32,4608]{1,0:T(8,128)(2,1)S(1)} %collective-permute-done.7.refs_1_), channel_id=1, source_target_pairs={{0,4},{4,0},{8,12},{12,8},{1,5},{5,1},{9,13},{13,9},{2,6},{6,2},{1... | collective-permute-start | bytes 884744 | tf_op jit(solution)/shard_map/ppermute | solution.py:55
  32.2 9.6 %collective-permute-start.11 = (bf16[32,3584]{1,0:T(8,128)(2,1)S(1)}, bf16[32,3584]{1,0:T(8,128)(2,1)S(1)}, u32[]{:S(2)}, u32[]{:S(2)}) collective-permute-start(bf16[32,3584]{1,0:T(8,128)(2,1)S(1)} %collective-permute-done.3.refs_3_), channel_id=1, source_target_pairs={{0,4},{4,0},{8,12},{12,8},{1,5},{5,1},{9,13},{13,9},{2,6},{6,2},{1... | collective-permute-start | bytes 688136 | tf_op jit(solution)/shard_map/ppermute | solution.py:55
  41.8 4.1 %collective-permute-start.12 = (bf16[96,8192]{1,0:T(8,128)(2,1)S(1)}, bf16[96,8192]{1,0:T(8,128)(2,1)S(1)}, u32[]{:S(2)}, u32[]{:S(2)}) collective-permute-start(bf16[96,8192]{1,0:T(8,128)(2,1)S(1)} %collective-permute-done.9.refs_1_), channel_id=1, source_target_pairs={{0,1},{1,0},{2,3},{3,2},{4,5},{5,4},{6,7},{7,6},{8,9},{9,8},{10,11... | collective-permute-start | bytes 4718600 | tf_op jit(solution)/shard_map/ppermute | solution.py:20
  48.6 3.6 %collective-permute-start.17 = (f32[1,384]{1,0:T(1,128)S(1)}, f32[1,384]{1,0:T(1,128)S(1)}, u32[]{:S(2)}, u32[]{:S(2)}) collective-permute-start(f32[1,384]{1,0:T(1,128)S(1)} %get-tuple-element.69.refs_0_), channel_id=1, source_target_pairs={{0,2},{1,3},{2,0},{3,1},{4,6},{5,7},{6,4},{7,5},{8,10},{9,11},{10,... | collective-permute-start | bytes 4616 | tf_op jit(solution)/shard_map/ppermute | solution.py:20
  54.2 9.2 %collective-permute-start.19 = (bf16[32,4096]{1,0:T(8,128)(2,1)S(1)}, bf16[32,4096]{1,0:T(8,128)(2,1)S(1)}, u32[]{:S(2)}, u32[]{:S(2)}) collective-permute-start(bf16[32,4096]{1,0:T(8,128)(2,1)S(1)} %get-tuple-element.74), channel_id=1, source_target_pairs={{0,4},{4,0},{8,12},{12,8},{1,5},{5,1},{9,13},{13,9},{2,6},{6,2},{1... | collective-permute-start | bytes 786440 | tf_op jit(solution)/shard_map/ppermute | solution.py:94
  56.3 13.4 %collective-permute-start.20 = (bf16[32,4096]{1,0:T(8,128)(2,1)S(1)}, bf16[32,4096]{1,0:T(8,128)(2,1)S(1)}, u32[]{:S(2)}, u32[]{:S(2)}) collective-permute-start(bf16[32,4096]{1,0:T(8,128)(2,1)S(1)} %get-tuple-element.76), channel_id=1, source_target_pairs={{0,4},{4,0},{8,12},{12,8},{1,5},{5,1},{9,13},{13,9},{2,6},{6,2},{1... | collective-permute-start | bytes 786440 | tf_op jit(solution)/shard_map/ppermute | solution.py:94
  63.4 11.5 %collective-permute-start.27 = (bf16[32,4096]{1,0:T(8,128)(2,1)S(1)}, bf16[32,4096]{1,0:T(8,128)(2,1)S(1)}, u32[]{:S(2)}, u32[]{:S(2)}) collective-permute-start(bf16[32,4096]{1,0:T(8,128)(2,1)S(1)} %get-tuple-element.79), channel_id=1, source_target_pairs={{0,4},{4,0},{8,12},{12,8},{1,5},{5,1},{9,13},{13,9},{2,6},{6,2},{1... | collective-permute-start | bytes 786440 | tf_op jit(solution)/shard_map/ppermute | solution.py:98
  65.6 4.9 %collective-permute-start.25 = (bf16[32,4096]{1,0:T(8,128)(2,1)S(1)}, bf16[32,4096]{1,0:T(8,128)(2,1)S(1)}, u32[]{:S(2)}, u32[]{:S(2)}) collective-permute-start(bf16[32,4096]{1,0:T(8,128)(2,1)S(1)} %add_convert_fusion.2), channel_id=1, source_target_pairs={{4,8},{8,4},{5,9},{9,5},{6,10},{10,6},{7,11},{11,7},{20,24},{24,20... | collective-permute-start | bytes 786440 | tf_op jit(solution)/shard_map/ppermute | solution.py:101
  66.2 14.3 %collective-permute-start.23 = (bf16[32,4096]{1,0:T(8,128)(2,1)S(1)}, bf16[32,4096]{1,0:T(8,128)(2,1)S(1)}, u32[]{:S(2)}, u32[]{:S(2)}) collective-permute-start(bf16[32,4096]{1,0:T(8,128)(2,1)S(1)} %get-tuple-element.75), channel_id=1, source_target_pairs={{0,4},{4,0},{8,12},{12,8},{1,5},{5,1},{9,13},{13,9},{2,6},{6,2},{1... | collective-permute-start | bytes 786440 | tf_op jit(solution)/shard_map/ppermute | solution.py:98
  69.8 5.9 %collective-permute-start.21 = (bf16[32,4096]{1,0:T(8,128)(2,1)S(1)}, bf16[32,4096]{1,0:T(8,128)(2,1)S(1)}, u32[]{:S(2)}, u32[]{:S(2)}) collective-permute-start(bf16[32,4096]{1,0:T(8,128)(2,1)S(1)} %add_convert_fusion.5), channel_id=1, source_target_pairs={{4,8},{8,4},{5,9},{9,5},{6,10},{10,6},{7,11},{11,7},{20,24},{24,20... | collective-permute-start | bytes 786440 | tf_op jit(solution)/shard_map/ppermute | solution.py:101
  70.6 15.3 %collective-permute-start.26 = (bf16[32,4096]{1,0:T(8,128)(2,1)S(1)}, bf16[32,4096]{1,0:T(8,128)(2,1)S(1)}, u32[]{:S(2)}, u32[]{:S(2)}) collective-permute-start(bf16[32,4096]{1,0:T(8,128)(2,1)S(1)} %fusion.1), channel_id=1, source_target_pairs={{0,4},{4,0},{8,12},{12,8},{1,5},{5,1},{9,13},{13,9},{2,6},{6,2},{1... | collective-permute-start | bytes 786440 | tf_op jit(solution)/shard_map/ppermute | solution.py:104
  75.0 10.9 %collective-permute-start.28 = (bf16[32,4096]{1,0:T(8,128)(2,1)S(1)}, bf16[32,4096]{1,0:T(8,128)(2,1)S(1)}, u32[]{:S(2)}, u32[]{:S(2)}) collective-permute-start(bf16[32,4096]{1,0:T(8,128)(2,1)S(1)} %add_convert_fusion), channel_id=1, source_target_pairs={{4,8},{8,4},{5,9},{9,5},{6,10},{10,6},{7,11},{11,7},{20,24},{24,20... | collective-permute-start | bytes 786440 | tf_op jit(solution)/shard_map/ppermute | solution.py:102
  75.8 15.2 %collective-permute-start.22 = (bf16[32,4096]{1,0:T(8,128)(2,1)S(1)}, bf16[32,4096]{1,0:T(8,128)(2,1)S(1)}, u32[]{:S(2)}, u32[]{:S(2)}) collective-permute-start(bf16[32,4096]{1,0:T(8,128)(2,1)S(1)} %fusion), channel_id=1, source_target_pairs={{0,4},{4,0},{8,12},{12,8},{1,5},{5,1},{9,13},{13,9},{2,6},{6,2},{1... | collective-permute-start | bytes 786440 | tf_op jit(solution)/shard_map/ppermute | solution.py:104
  80.7 10.4 %collective-permute-start.24 = (bf16[32,4096]{1,0:T(8,128)(2,1)S(1)}, bf16[32,4096]{1,0:T(8,128)(2,1)S(1)}, u32[]{:S(2)}, u32[]{:S(2)}) collective-permute-start(bf16[32,4096]{1,0:T(8,128)(2,1)S(1)} %add_convert_fusion.3), channel_id=1, source_target_pairs={{4,8},{8,4},{5,9},{9,5},{6,10},{10,6},{7,11},{11,7},{20,24},{24,20... | collective-permute-start | bytes 786440 | tf_op jit(solution)/shard_map/ppermute | solution.py:102
  (8 other events, 31.9 us)

commit v12 on v11

--- a/solution.py
+++ b/solution.py
@@ -56,11 +56,11 @@
         far_parts.append([far, across_far])
         end_parts.append([end, across])
     weighted, penalty, near, noise = early
-    weights = stage_rest([far_parts, end_parts], weighted, penalty, noise)
     ends = [parts[0] for parts in end_parts]
     routes, crossed, *_ = lax.optimization_barrier((routes, crossed, *ends))
-    far = [[one] for one in swap_gather(crossed, "reader", near_bits)]
-    return weights, near, far, swap_all(routes)
+    far = swap_gather(crossed, "reader", near_bits)
+    weights = stage_rest([far_parts, end_parts], near, crossed, weighted, penalty, noise)
+    return weights, far[1:], swap_all(routes)
 
 
 def swap_all(routes):
@@ -72,8 +72,8 @@
     far = swap_gather(swap_bits(images, "reader", far_bit), "reader", near_bits)
     line = [[[one]] for one in line_gather(block, "blk")]
     weighted, penalty, near, noise = stage(line[:2], near, noise)
-    weights = stage_rest(line[2:], weighted, penalty, noise)
-    return weights, near, [[one] for one in far], swap_all(routes)
+    weights = stage_rest(line[2:], near, far[0], weighted, penalty, noise)
+    return weights, far[1:], swap_all(routes)
 
 
 def line_gather(block, axis):
@@ -268,11 +268,28 @@
     )(*moved, noise)
 
 
-def stage_rest_kernel(counts, *refs):
+def image_copies(groups, rows, all_ref, sems):
+    reader = lax.axis_index("reader")
+    copies = []
+    for k, source in groups:
+        row = pl.multiple_of((reader ^ k) * rows, 16)
+        copies.append(
+            pltpu.make_async_copy(source, all_ref.at[pl.ds(row, rows), :], sems.at[len(copies)])
+        )
+    return copies
+
+
+def stage_rest_kernel(readers, counts, *refs):
     refs = list(refs)
     groups = take_blocks(refs, counts)
-    early_ref, early_penalty_ref, noise_ref, turned_ref, penalty_ref = refs[:5]
-    weighted_ref, block_ref, sems = refs[5:]
+    near_ref, far_ref = refs.pop(0), refs.pop(0)
+    early_ref, early_penalty_ref, noise_ref, turned_ref, penalty_ref, all_ref = refs[:6]
+    weighted_ref, block_ref, sems, image_sems = refs[6:]
+    rows = far_ref.shape[0]
+    sources = [(k, near_ref.at[pl.ds(k * rows, rows), :]) for k in range(readers // 2)]
+    copies = image_copies(sources + [(readers // 2, far_ref)], rows, all_ref, image_sems)
+    for copy in copies:
+        copy.start()
     done = early_ref.shape[0]
     weighted_ref[:done, :] = early_ref[...]
     penalty_ref[:done, :] = early_penalty_ref[...]
@@ -282,26 +299,31 @@
     for start in range(0, width, STEP):
         piece = slice(start, min(start + STEP, width))
         turned_ref[piece, :] = weighted_ref[:, piece].T
-
-
-def stage_rest(blocks, weighted, penalty, noise):
+    for copy in copies:
+        copy.wait()
+
+
+def stage_rest(blocks, near, crossed, weighted, penalty, noise):
     count = blocks[0][0][0].shape[0]
     parts = sum(len(group) for group in blocks)
     width = noise.shape[1]
     refs = len(blocks) * count + weighted.shape[0]
-    moved = flat(blocks)
+    readers = 2 * near.shape[0] // crossed.shape[0]
+    moved = [*flat(blocks), near, crossed]
     return pl.pallas_call(
-        partial(stage_rest_kernel, block_counts(blocks)),
+        partial(stage_rest_kernel, readers, block_counts(blocks)),
         out_shape=(
             jax.ShapeDtypeStruct((width, refs), jnp.bfloat16),
             jax.ShapeDtypeStruct((refs, 1), jnp.float32),
+            jax.ShapeDtypeStruct((2 * near.shape[0], width), jnp.bfloat16),
         ),
         in_specs=[ANY_SPEC] * len(moved) + [VMEM_SPEC] * 3,
-        out_specs=(VMEM_SPEC,) * 2,
+        out_specs=(VMEM_SPEC,) * 3,
         scratch_shapes=[
             pltpu.VMEM((refs, width), jnp.bfloat16),
             pltpu.VMEM((len(blocks), count, width), jnp.bfloat16),
             pltpu.SemaphoreType.DMA((parts,)),
+            pltpu.SemaphoreType.DMA((readers // 2 + 1,)),
         ],
         compiler_params=pltpu.CompilerParams(vmem_limit_bytes=SCORE_VMEM),
         cost_estimate=pl.CostEstimate(
@@ -311,30 +333,18 @@
     )(*moved, weighted, penalty, noise)
 
 
-def score_kernel(readers, far_counts, finish, *refs):
+def score_kernel(readers, finish, *refs):
     refs = list(refs)
-    near_ref = refs.pop(0)
-    rows = near_ref.shape[0] * 2 // readers
-    far_refs = [[refs.pop(0) for _ in range(n)] for n in far_counts]
-    weighted_ref, penalty_ref = refs.pop(0), refs.pop(0)
+    far_refs = [refs.pop(0) for _ in range(readers // 2 - 1)]
+    weighted_ref, penalty_ref, _ = refs.pop(0), refs.pop(0), refs.pop(0)
     route_refs = [refs.pop(0) for _ in range(readers)]
     score_ref, mask_ref, lse_ref, all_ref, image_sems = refs
     reader = lax.axis_index("reader")
-    copies = []
-    for k in range(readers):
-        if k < readers // 2:
-            sources = [near_ref.at[pl.ds(k * rows, rows), :]]
-        else:
-            sources = far_refs[k - readers // 2]
-        row, start = pl.multiple_of((reader ^ k) * rows, 16), 0
-        for source in sources:
-            columns = pl.ds(start, source.shape[1])
-            copy = pltpu.make_async_copy(
-                source, all_ref.at[pl.ds(row, rows), columns], image_sems.at[len(copies)]
-            )
-            copy.start()
-            copies.append(copy)
-            start += source.shape[1]
+    rows = route_refs[0].shape[1]
+    sources = [(readers // 2 + 1 + i, ref) for i, ref in enumerate(far_refs)]
+    copies = image_copies(sources, rows, all_ref, image_sems)
+    for copy in copies:
+        copy.start()
     routes = [ref[...] for ref in route_refs]
     bit = 1
     while bit < readers:
@@ -354,22 +364,22 @@
         lse_ref[...] = column_lse(scores)
 
 
-def all_scores(weights, near, far, routes, finish):
-    weighted, penalty = weights
+def all_scores(weights, far, routes, finish):
+    weighted, penalty, images = weights
     width, refs = weighted.shape
-    slots = 2 * near.shape[0]
-    moved = [near, *[one for group in far for one in group]]
+    slots = images.shape[0]
     return pl.pallas_call(
-        partial(score_kernel, len(routes), [len(group) for group in far], finish),
+        partial(score_kernel, len(routes), finish),
         out_shape=(
             jax.ShapeDtypeStruct((refs, slots), jnp.float32),
             jax.ShapeDtypeStruct((len(routes), slots), jnp.float32),
             jax.ShapeDtypeStruct((1, slots), jnp.float32),
             jax.ShapeDtypeStruct((slots, width), jnp.bfloat16),
         ),
-        in_specs=[ANY_SPEC] * len(moved) + [VMEM_SPEC] * (2 + len(routes)),
+        in_specs=[ANY_SPEC] * len(far) + [VMEM_SPEC] * (3 + len(routes)),
         out_specs=(VMEM_SPEC,) * 4,
-        scratch_shapes=[pltpu.SemaphoreType.DMA((len(moved) + len(routes),))],
+        scratch_shapes=[pltpu.SemaphoreType.DMA((len(far),))],
+        input_output_aliases={len(far) + 2: 3},
         compiler_params=pltpu.CompilerParams(vmem_limit_bytes=SCORE_VMEM),
         cost_estimate=pl.CostEstimate(
             flops=2 * refs * slots * width,
@@ -377,7 +387,7 @@
             transcendentals=0,
         ),
         name="scores",
-    )(*moved, weighted, penalty, *routes)
+    )(*far, weighted, penalty, images, *routes)
 
 
 def lse_kernel(score_ref, lse_ref):
@@ -446,11 +456,11 @@
     noise = noise_weights.reshape(1, width)
 
     gather = staged_gather if members == 4 and rows % 16 == 0 and readers > 1 else plain_gather
-    weights, near, far, route_blocks = gather(
+    weights, far, route_blocks = gather(
         projections[0], images, noise, routes.T, readers // 4, readers // 2
     )
     split = lax.axis_size("sub") > 1
-    scores, masks, mine, all_images = all_scores(weights, near, far, route_blocks, not split)
+    scores, masks, mine, all_images = all_scores(weights, far, route_blocks, not split)
     if split:
         scores = lax.psum(scores, "sub")
         mine = group_lse(scores)

time: 92.6 us -> 93.4 us (level)
  waiting for transfers between devices: 28 us -> 30 us
  starting transfers between devices: 50.7 us -> 49.5 us
    ppermute x2, starting transfers between devices: 7.26 us -> 3.65 us  [staged_gather(): end = lax.ppermute(across_far, 'blk', SIDES)]
    ppermute x2, starting transfers between devices: 8.16 us -> 11 us  [staged_gather(): far = lax.ppermute(across, 'blk', SIDES)]
    ppermute x2, waiting for transfers between devices: 0.01 us -> 1.33 us  [staged_gather(): far = lax.ppermute(across, 'blk', SIDES)]
    ppermute x2, starting transfers between devices: 5.53 us -> 4.33 us  [pair_scatter(): for_far_middle = [lax.ppermute(part, axis, SIDES) for part in second]]
    ppermute x2, waiting for transfers between devices: 2.87 us -> 4.03 us  [staged_gather(): end = lax.ppermute(across_far, 'blk', SIDES)]
  transfers between devices with their start and end apart: 29 -> 29, of which waited for: 9 -> 11; matrix products, arithmetic and copies ran while one was open for 3% -> 3% of each run, Pallas kernels for 3% -> 3%
where the time goes in v12:
time: 93.4 us; the launch traced here: 93 us
  starting transfers between devices  49.5 us (53%)
  waiting for transfers between devices  30 us (32%)
  Pallas kernels  7.28 us (8%)
  local copies, waits for them, and re-layouts  4.69 us (5%)
    ppermute x2, starting transfers between devices, staged_gather(): far = lax.ppermute(across, 'blk', SIDES)  11 us
    ppermute x2, starting transfers between devices, pair_scatter(): from_side = lax.ppermute(near, axis, SIDES)  9.83 us
    ppermute x2, waiting for transfers between devices, pair_scatter(): from_side = lax.ppermute(near, axis, SIDES)  9.61 us
    ppermute x9, starting transfers between devices, swap_bits(): lax.ppermute(block, axis, [(i, i ^ bits) for i in range(lax.axis_size(axi...  6.96 us
    ppermute x2, waiting for transfers between devices, pair_scatter(): for_far_end = [lax.ppermute(parts[3], axis, SIDES) for parts in pieces]  6.95 us
    ppermute x2, starting transfers between devices, staged_gather(): lax.ppermute(one, 'blk', SIDES)  6.09 us
    ppermute x9, waiting for transfers between devices, swap_bits(): lax.ppermute(block, axis, [(i, i ^ bits) for i in range(lax.axis_size(axi...  5.9 us
    ppermute x2, starting transfers between devices, pair_scatter(): for_far_middle = [lax.ppermute(part, axis, SIDES) for part in second]  4.33 us
  transfers between devices with their start and end apart: 29, of which 11 were waited for; matrix products, arithmetic and copies ran while one was open for 3% of the time, Pallas kernels for 3%

profile of v12, /device:TPU:0, one launch (start us, length us, event | category | flops | bytes accessed | tf_op | source)
XLA Modules:
  0.0 93.0 jit_solution(9368122953751189013)
XLA Ops:
  1.1 2.6 %collective-permute-start = (bf16[96,8192]{1,0:T(8,128)(2,1)}, bf16[96,8192]{1,0:T(8,128)(2,1)S(1)}, u32[]{:S(2)}, u32[]{:S(2)}) collective-permute-start(bf16[96,8192]{1,0:T(8,128)(2,1)} %refs_0_.1), channel_id=1, source_target_pairs={{0,2},{1,3},{2,0},{3,1},{4,6},{5,7},{6,4},{7,5},{8,10},{9,11},{10,... | collective-permute-start | bytes 4718600 | tf_op jit(solution)/shard_map/ppermute | solution.py:20
  4.7 1.6 %collective-permute-start.1 = (bf16[32,4608]{1,0:T(8,128)(2,1)S(1)}, bf16[32,4608]{1,0:T(8,128)(2,1)S(1)}, u32[]{:S(2)}, u32[]{:S(2)}) collective-permute-start(bf16[32,4608]{1,0:T(8,128)(2,1)S(1)} %slice.8.refs_2_), channel_id=1, source_target_pairs={{0,4},{4,0},{8,12},{12,8},{1,5},{5,1},{9,13},{13,9},{2,6},{6,2},{1... | collective-permute-start | bytes 884744 | tf_op jit(solution)/shard_map/ppermute | solution.py:43
  8.0 4.4 %collective-permute-start.6 = (bf16[32,3584]{1,0:T(8,128)(2,1)S(1)}, bf16[32,3584]{1,0:T(8,128)(2,1)S(1)}, u32[]{:S(2)}, u32[]{:S(2)}) collective-permute-start(bf16[32,3584]{1,0:T(8,128)(2,1)S(1)} %slice.9.refs_3_), channel_id=1, source_target_pairs={{0,4},{4,0},{8,12},{12,8},{1,5},{5,1},{9,13},{13,9},{2,6},{6,2},{1... | collective-permute-start | bytes 688136 | tf_op jit(solution)/shard_map/ppermute | solution.py:43
  12.4 2.2 %collective-permute-done.1.refs_4_ = bf16[32,4608]{1,0:T(8,128)(2,1)S(1)} collective-permute-done((bf16[32,4608]{1,0:T(8,128)(2,1)S(1)}, bf16[32,4608]{1,0:T(8,128)(2,1)S(1)}, u32[]{:S(2)}, u32[]{:S(2)}) %collective-permute-start.1) | collective-permute-done | bytes 294944 | tf_op jit(solution)/shard_map/ppermute | solution.py:43
  15.3 4.5 %collective-permute-start.3 = (bf16[32,4608]{1,0:T(8,128)(2,1)S(1)}, bf16[32,4608]{1,0:T(8,128)(2,1)S(1)}, u32[]{:S(2)}, u32[]{:S(2)}) collective-permute-start(bf16[32,4608]{1,0:T(8,128)(2,1)S(1)} %collective-permute-done.2.refs_5_), channel_id=1, source_target_pairs={{0,4},{4,0},{8,12},{12,8},{1,5},{5,1},{9,13},{13,9},{2,6},{6,2},{1... | collective-permute-start | bytes 884744 | tf_op jit(solution)/shard_map/ppermute | solution.py:52
  21.1 6.6 %collective-permute-start.9 = (bf16[32,3584]{1,0:T(8,128)(2,1)S(1)}, bf16[32,3584]{1,0:T(8,128)(2,1)S(1)}, u32[]{:S(2)}, u32[]{:S(2)}) collective-permute-start(bf16[32,3584]{1,0:T(8,128)(2,1)S(1)} %collective-permute-done.7.refs_7_), channel_id=1, source_target_pairs={{0,4},{4,0},{8,12},{12,8},{1,5},{5,1},{9,13},{13,9},{2,6},{6,2},{1... | collective-permute-start | bytes 688136 | tf_op jit(solution)/shard_map/ppermute | solution.py:52
  27.7 1.4 %copy-done = bf16[96,8192]{1,0:T(8,128)(2,1)S(1)} copy-done((bf16[96,8192]{1,0:T(8,128)(2,1)S(1)}, bf16[96,8192]{1,0:T(8,128)(2,1)}, u32[]{:S(2)}) %copy-start) | copy-done | bytes 1572888
  31.0 1.2 %collective-permute-start.8 = (bf16[32,4608]{1,0:T(8,128)(2,1)S(1)}, bf16[32,4608]{1,0:T(8,128)(2,1)S(1)}, u32[]{:S(2)}, u32[]{:S(2)}) collective-permute-start(bf16[32,4608]{1,0:T(8,128)(2,1)S(1)} %collective-permute-done.4.refs_1_), channel_id=1, source_target_pairs={{0,4},{4,0},{8,12},{12,8},{1,5},{5,1},{9,13},{13,9},{2,6},{6,2},{1... | collective-permute-start | bytes 884744 | tf_op jit(solution)/shard_map/ppermute | solution.py:55
  32.2 1.3 %collective-permute-done.9.refs_2_ = bf16[32,3584]{1,0:T(8,128)(2,1)S(1)} collective-permute-done((bf16[32,3584]{1,0:T(8,128)(2,1)S(1)}, bf16[32,3584]{1,0:T(8,128)(2,1)S(1)}, u32[]{:S(2)}, u32[]{:S(2)}) %collective-permute-start.9) | collective-permute-done | bytes 229408 | tf_op jit(solution)/shard_map/ppermute | solution.py:52
  33.5 2.5 %collective-permute-start.11 = (bf16[32,3584]{1,0:T(8,128)(2,1)S(1)}, bf16[32,3584]{1,0:T(8,128)(2,1)S(1)}, u32[]{:S(2)}, u32[]{:S(2)}) collective-permute-start(bf16[32,3584]{1,0:T(8,128)(2,1)S(1)} %collective-permute-done.10.refs_3_), channel_id=1, source_target_pairs={{0,4},{4,0},{8,12},{12,8},{1,5},{5,1},{9,13},{13,9},{2,6},{6,2},{1... | collective-permute-start | bytes 688136 | tf_op jit(solution)/shard_map/ppermute | solution.py:55
  36.0 2.9 %collective-permute-done.refs_9_ = bf16[96,8192]{1,0:T(8,128)(2,1)S(1)} collective-permute-done((bf16[96,8192]{1,0:T(8,128)(2,1)}, bf16[96,8192]{1,0:T(8,128)(2,1)S(1)}, u32[]{:S(2)}, u32[]{:S(2)}) %collective-permute-start) | collective-permute-done | bytes 1572896 | tf_op jit(solution)/shard_map/ppermute | solution.py:20
  38.9 4.0 %collective-permute-done.11.refs_6_ = bf16[32,3584]{1,0:T(8,128)(2,1)S(1)} collective-permute-done((bf16[32,3584]{1,0:T(8,128)(2,1)S(1)}, bf16[32,3584]{1,0:T(8,128)(2,1)S(1)}, u32[]{:S(2)}, u32[]{:S(2)}) %collective-permute-start.11) | collective-permute-done | bytes 229408 | tf_op jit(solution)/shard_map/ppermute | solution.py:55
  44.9 1.8 %stage_rest.1 = (bf16[8192,128]{1,0:T(8,128)(2,1)S(1)}, f32[128,1]{1,0:T(8,128)S(1)}, bf16[384,8192]{1,0:T(8,128)(2,1)S(1)}) custom-call(bf16[32,4608]{1,0:T(8,128)(2,1)S(1)} %collective-permute-done.3.refs_0_, bf16[32,4608]{1,0:T(8,128)(2,1)S(1)} %collective-permute-done.4.refs_1_, bf16[32,3584]{1,0:T(8,128)(2,1)S(1)} %collective-permute-done.9.refs_2_, ...), custom_call_target="tpu_custom_call" | custom-call | flops 8388608 | bytes 12000000 | tf_op jit(solution)/shard_map/stage_rest/pallas_call | solution.py:313
  47.0 2.1 %scores.1 = (f32[128,384]{1,0:T(8,128)S(1)}, f32[4,384]{1,0:T(4,128)S(1)}, f32[1,384]{1,0:T(1,128)S(1)}, bf16[384,8192]{1,0:T(8,128)(2,1)S(1)}) custom-call(bf16[96,8192]{1,0:T(8,128)(2,1)S(1)} %collective-permute-done.12.refs_0_, bf16[8192,128]{1,0:T(8,128)(2,1)S(1)} %get-tuple-element.64.refs_1_, ...), custom_call_target="tpu_custom_call", output_to_operand_aliasing={{3}: (3, {})} | custom-call | flops 805306368 | bytes 8388608 | tf_op jit(solution)/shard_map/scores/pallas_call | solution.py:371
  51.1 2.1 %collective-permute-done.17.refs_2_ = f32[1,384]{1,0:T(1,128)S(1)} collective-permute-done((f32[1,384]{1,0:T(1,128)S(1)}, f32[1,384]{1,0:T(1,128)S(1)}, u32[]{:S(2)}, u32[]{:S(2)}) %collective-permute-start.17) | collective-permute-done | bytes 1568 | tf_op jit(solution)/shard_map/ppermute | solution.py:20
  53.8 1.3 %sums.1 = (f32[1,384]{1,0:T(1,128)S(1)}, bf16[32,4096]{1,0:T(8,128)(2,1)S(1)}, bf16[32,4096]{1,0:T(8,128)(2,1)S(1)}, bf16[32,4096]{1,0:T(8,128)(2,1)S(1)}, bf16[...) custom-call(bf16[384,8192]{1,0:T(8,128)(2,1)S(1)} %get-tuple-element, ...), custom_call_target="tpu_custom_call" | custom-call | flops 805306368 | bytes 6291456 | tf_op jit(solution)/shard_map/sums/pallas_call | solution.py:435
  55.0 2.1 %collective-permute-start.19 = (bf16[32,4096]{1,0:T(8,128)(2,1)S(1)}, bf16[32,4096]{1,0:T(8,128)(2,1)S(1)}, u32[]{:S(2)}, u32[]{:S(2)}) collective-permute-start(bf16[32,4096]{1,0:T(8,128)(2,1)S(1)} %get-tuple-element.76), channel_id=1, source_target_pairs={{0,4},{4,0},{8,12},{12,8},{1,5},{5,1},{9,13},{13,9},{2,6},{6,2},{1... | collective-permute-start | bytes 786440 | tf_op jit(solution)/shard_map/ppermute | solution.py:94
  57.8 6.4 %collective-permute-done.19 = bf16[32,4096]{1,0:T(8,128)(2,1)S(1)} collective-permute-done((bf16[32,4096]{1,0:T(8,128)(2,1)S(1)}, bf16[32,4096]{1,0:T(8,128)(2,1)S(1)}, u32[]{:S(2)}, u32[]{:S(2)}) %collective-permute-start.19) | collective-permute-done | bytes 262176 | tf_op jit(solution)/shard_map/ppermute | solution.py:94
  64.2 2.1 %collective-permute-start.27 = (bf16[32,4096]{1,0:T(8,128)(2,1)S(1)}, bf16[32,4096]{1,0:T(8,128)(2,1)S(1)}, u32[]{:S(2)}, u32[]{:S(2)}) collective-permute-start(bf16[32,4096]{1,0:T(8,128)(2,1)S(1)} %get-tuple-element.81), channel_id=1, source_target_pairs={{0,4},{4,0},{8,12},{12,8},{1,5},{5,1},{9,13},{13,9},{2,6},{6,2},{1... | collective-permute-start | bytes 786440 | tf_op jit(solution)/shard_map/ppermute | solution.py:98
  67.0 2.3 %collective-permute-start.23 = (bf16[32,4096]{1,0:T(8,128)(2,1)S(1)}, bf16[32,4096]{1,0:T(8,128)(2,1)S(1)}, u32[]{:S(2)}, u32[]{:S(2)}) collective-permute-start(bf16[32,4096]{1,0:T(8,128)(2,1)S(1)} %get-tuple-element.77), channel_id=1, source_target_pairs={{0,4},{4,0},{8,12},{12,8},{1,5},{5,1},{9,13},{13,9},{2,6},{6,2},{1... | collective-permute-start | bytes 786440 | tf_op jit(solution)/shard_map/ppermute | solution.py:98
  70.7 5.1 %collective-permute-start.26 = (bf16[32,4096]{1,0:T(8,128)(2,1)S(1)}, bf16[32,4096]{1,0:T(8,128)(2,1)S(1)}, u32[]{:S(2)}, u32[]{:S(2)}) collective-permute-start(bf16[32,4096]{1,0:T(8,128)(2,1)S(1)} %fusion.1), channel_id=1, source_target_pairs={{0,4},{4,0},{8,12},{12,8},{1,5},{5,1},{9,13},{13,9},{2,6},{6,2},{1... | collective-permute-start | bytes 786440 | tf_op jit(solution)/shard_map/ppermute | solution.py:104
  76.6 4.8 %collective-permute-start.22 = (bf16[32,4096]{1,0:T(8,128)(2,1)S(1)}, bf16[32,4096]{1,0:T(8,128)(2,1)S(1)}, u32[]{:S(2)}, u32[]{:S(2)}) collective-permute-start(bf16[32,4096]{1,0:T(8,128)(2,1)S(1)} %fusion), channel_id=1, source_target_pairs={{0,4},{4,0},{8,12},{12,8},{1,5},{5,1},{9,13},{13,9},{2,6},{6,2},{1... | collective-permute-start | bytes 786440 | tf_op jit(solution)/shard_map/ppermute | solution.py:104
  82.1 4.6 %collective-permute-done.26 = bf16[32,4096]{1,0:T(8,128)(2,1)S(1)} collective-permute-done((bf16[32,4096]{1,0:T(8,128)(2,1)S(1)}, bf16[32,4096]{1,0:T(8,128)(2,1)S(1)}, u32[]{:S(2)}, u32[]{:S(2)}) %collective-permute-start.26) | collective-permute-done | bytes 262176 | tf_op jit(solution)/shard_map/ppermute | solution.py:104
  86.8 5.1 %collective-permute-done.22 = bf16[32,4096]{1,0:T(8,128)(2,1)S(1)} collective-permute-done((bf16[32,4096]{1,0:T(8,128)(2,1)S(1)}, bf16[32,4096]{1,0:T(8,128)(2,1)S(1)}, u32[]{:S(2)}, u32[]{:S(2)}) %collective-permute-start.22) | collective-permute-done | bytes 262176 | tf_op jit(solution)/shard_map/ppermute | solution.py:104
  (56 shorter events, 17.2 us)
Async XLA Ops:
  0.6 20.5 %collective-permute-start.5 = (bf16[96,8192]{1,0:T(8,128)(2,1)}, bf16[96,8192]{1,0:T(8,128)(2,1)S(1)}, u32[]{:S(2)}, u32[]{:S(2)}) collective-permute-start(bf16[96,8192]{1,0:T(8,128)(2,1)} %refs_0_.1), channel_id=1, source_target_pairs={{0,1},{1,0},{2,3},{3,2},{4,5},{5,4},{6,7},{7,6},{8,9},{9,8},{10,11... | collective-permute-start | bytes 4718600 | tf_op jit(solution)/shard_map/ppermute | solution.py:20
  1.1 37.8 %collective-permute-start = (bf16[96,8192]{1,0:T(8,128)(2,1)}, bf16[96,8192]{1,0:T(8,128)(2,1)S(1)}, u32[]{:S(2)}, u32[]{:S(2)}) collective-permute-start(bf16[96,8192]{1,0:T(8,128)(2,1)} %refs_0_.1), channel_id=1, source_target_pairs={{0,2},{1,3},{2,0},{3,1},{4,6},{5,7},{6,4},{7,5},{8,10},{9,11},{10,... | collective-permute-start | bytes 4718600 | tf_op jit(solution)/shard_map/ppermute | solution.py:20
  4.7 9.9 %collective-permute-start.1 = (bf16[32,4608]{1,0:T(8,128)(2,1)S(1)}, bf16[32,4608]{1,0:T(8,128)(2,1)S(1)}, u32[]{:S(2)}, u32[]{:S(2)}) collective-permute-start(bf16[32,4608]{1,0:T(8,128)(2,1)S(1)} %slice.8.refs_2_), channel_id=1, source_target_pairs={{0,4},{4,0},{8,12},{12,8},{1,5},{5,1},{9,13},{13,9},{2,6},{6,2},{1... | collective-permute-start | bytes 884744 | tf_op jit(solution)/shard_map/ppermute | solution.py:43
  6.3 8.9 %collective-permute-start.2 = (bf16[32,4608]{1,0:T(8,128)(2,1)S(1)}, bf16[32,4608]{1,0:T(8,128)(2,1)S(1)}, u32[]{:S(2)}, u32[]{:S(2)}) collective-permute-start(bf16[32,4608]{1,0:T(8,128)(2,1)S(1)} %slice.8.refs_2_), channel_id=1, source_target_pairs={{4,8},{8,4},{5,9},{9,5},{6,10},{10,6},{7,11},{11,7},{20,24},{24,20... | collective-permute-start | bytes 884744 | tf_op jit(solution)/shard_map/ppermute | solution.py:43
  8.0 11.8 %collective-permute-start.6 = (bf16[32,3584]{1,0:T(8,128)(2,1)S(1)}, bf16[32,3584]{1,0:T(8,128)(2,1)S(1)}, u32[]{:S(2)}, u32[]{:S(2)}) collective-permute-start(bf16[32,3584]{1,0:T(8,128)(2,1)S(1)} %slice.9.refs_3_), channel_id=1, source_target_pairs={{0,4},{4,0},{8,12},{12,8},{1,5},{5,1},{9,13},{13,9},{2,6},{6,2},{1... | collective-permute-start | bytes 688136 | tf_op jit(solution)/shard_map/ppermute | solution.py:43
  14.6 5.8 %collective-permute-start.7 = (bf16[32,3584]{1,0:T(8,128)(2,1)S(1)}, bf16[32,3584]{1,0:T(8,128)(2,1)S(1)}, u32[]{:S(2)}, u32[]{:S(2)}) collective-permute-start(bf16[32,3584]{1,0:T(8,128)(2,1)S(1)} %slice.9.refs_3_), channel_id=1, source_target_pairs={{4,8},{8,4},{5,9},{9,5},{6,10},{10,6},{7,11},{11,7},{20,24},{24,20... | collective-permute-start | bytes 688136 | tf_op jit(solution)/shard_map/ppermute | solution.py:43
  15.3 15.7 %collective-permute-start.3 = (bf16[32,4608]{1,0:T(8,128)(2,1)S(1)}, bf16[32,4608]{1,0:T(8,128)(2,1)S(1)}, u32[]{:S(2)}, u32[]{:S(2)}) collective-permute-start(bf16[32,4608]{1,0:T(8,128)(2,1)S(1)} %collective-permute-done.2.refs_5_), channel_id=1, source_target_pairs={{0,4},{4,0},{8,12},{12,8},{1,5},{5,1},{9,13},{13,9},{2,6},{6,2},{1... | collective-permute-start | bytes 884744 | tf_op jit(solution)/shard_map/ppermute | solution.py:52
  19.8 11.2 %collective-permute-start.4 = (bf16[32,4608]{1,0:T(8,128)(2,1)S(1)}, bf16[32,4608]{1,0:T(8,128)(2,1)S(1)}, u32[]{:S(2)}, u32[]{:S(2)}) collective-permute-start(bf16[32,4608]{1,0:T(8,128)(2,1)S(1)} %collective-permute-done.1.refs_4_), channel_id=1, source_target_pairs={{4,8},{8,4},{5,9},{9,5},{6,10},{10,6},{7,11},{11,7},{20,24},{24,20... | collective-permute-start | bytes 884744 | tf_op jit(solution)/shard_map/ppermute | solution.py:53
  20.4 11.7 %collective-permute-start.10 = (bf16[32,3584]{1,0:T(8,128)(2,1)S(1)}, bf16[32,3584]{1,0:T(8,128)(2,1)S(1)}, u32[]{:S(2)}, u32[]{:S(2)}) collective-permute-start(bf16[32,3584]{1,0:T(8,128)(2,1)S(1)} %collective-permute-done.6.refs_5_), channel_id=1, source_target_pairs={{4,8},{8,4},{5,9},{9,5},{6,10},{10,6},{7,11},{11,7},{20,24},{24,20... | collective-permute-start | bytes 688136 | tf_op jit(solution)/shard_map/ppermute | solution.py:53
  21.1 12.4 %collective-permute-start.9 = (bf16[32,3584]{1,0:T(8,128)(2,1)S(1)}, bf16[32,3584]{1,0:T(8,128)(2,1)S(1)}, u32[]{:S(2)}, u32[]{:S(2)}) collective-permute-start(bf16[32,3584]{1,0:T(8,128)(2,1)S(1)} %collective-permute-done.7.refs_7_), channel_id=1, source_target_pairs={{0,4},{4,0},{8,12},{12,8},{1,5},{5,1},{9,13},{13,9},{2,6},{6,2},{1... | collective-permute-start | bytes 688136 | tf_op jit(solution)/shard_map/ppermute | solution.py:52
  31.0 11.9 %collective-permute-start.8 = (bf16[32,4608]{1,0:T(8,128)(2,1)S(1)}, bf16[32,4608]{1,0:T(8,128)(2,1)S(1)}, u32[]{:S(2)}, u32[]{:S(2)}) collective-permute-start(bf16[32,4608]{1,0:T(8,128)(2,1)S(1)} %collective-permute-done.4.refs_1_), channel_id=1, source_target_pairs={{0,4},{4,0},{8,12},{12,8},{1,5},{5,1},{9,13},{13,9},{2,6},{6,2},{1... | collective-permute-start | bytes 884744 | tf_op jit(solution)/shard_map/ppermute | solution.py:55
  33.5 9.4 %collective-permute-start.11 = (bf16[32,3584]{1,0:T(8,128)(2,1)S(1)}, bf16[32,3584]{1,0:T(8,128)(2,1)S(1)}, u32[]{:S(2)}, u32[]{:S(2)}) collective-permute-start(bf16[32,3584]{1,0:T(8,128)(2,1)S(1)} %collective-permute-done.10.refs_3_), channel_id=1, source_target_pairs={{0,4},{4,0},{8,12},{12,8},{1,5},{5,1},{9,13},{13,9},{2,6},{6,2},{1... | collective-permute-start | bytes 688136 | tf_op jit(solution)/shard_map/ppermute | solution.py:55
  42.9 4.1 %collective-permute-start.12 = (bf16[96,8192]{1,0:T(8,128)(2,1)S(1)}, bf16[96,8192]{1,0:T(8,128)(2,1)S(1)}, u32[]{:S(2)}, u32[]{:S(2)}) collective-permute-start(bf16[96,8192]{1,0:T(8,128)(2,1)S(1)} %collective-permute-done.refs_9_), channel_id=1, source_target_pairs={{0,1},{1,0},{2,3},{3,2},{4,5},{5,4},{6,7},{7,6},{8,9},{9,8},{10,11... | collective-permute-start | bytes 4718600 | tf_op jit(solution)/shard_map/ppermute | solution.py:20
  43.0 3.8 %collective-permute-start.13 = (s32[2,96]{1,0:T(2,128)S(1)}, s32[2,96]{1,0:T(2,128)S(1)}, u32[]{:S(2)}, u32[]{:S(2)}) collective-permute-start(s32[2,96]{1,0:T(2,128)S(1)} %bitcast.7), channel_id=1, source_target_pairs={{0,1},{1,0},{2,3},{3,2},{4,5},{5,4},{6,7},{7,6},{8,9},{9,8},{10,11... | collective-permute-start | bytes 2312 | tf_op jit(solution)/shard_map/ppermute | solution.py:20
  55.0 9.2 %collective-permute-start.19 = (bf16[32,4096]{1,0:T(8,128)(2,1)S(1)}, bf16[32,4096]{1,0:T(8,128)(2,1)S(1)}, u32[]{:S(2)}, u32[]{:S(2)}) collective-permute-start(bf16[32,4096]{1,0:T(8,128)(2,1)S(1)} %get-tuple-element.76), channel_id=1, source_target_pairs={{0,4},{4,0},{8,12},{12,8},{1,5},{5,1},{9,13},{13,9},{2,6},{6,2},{1... | collective-permute-start | bytes 786440 | tf_op jit(solution)/shard_map/ppermute | solution.py:94
  57.1 12.7 %collective-permute-start.20 = (bf16[32,4096]{1,0:T(8,128)(2,1)S(1)}, bf16[32,4096]{1,0:T(8,128)(2,1)S(1)}, u32[]{:S(2)}, u32[]{:S(2)}) collective-permute-start(bf16[32,4096]{1,0:T(8,128)(2,1)S(1)} %get-tuple-element.78), channel_id=1, source_target_pairs={{0,4},{4,0},{8,12},{12,8},{1,5},{5,1},{9,13},{13,9},{2,6},{6,2},{1... | collective-permute-start | bytes 786440 | tf_op jit(solution)/shard_map/ppermute | solution.py:94
  64.2 11.5 %collective-permute-start.27 = (bf16[32,4096]{1,0:T(8,128)(2,1)S(1)}, bf16[32,4096]{1,0:T(8,128)(2,1)S(1)}, u32[]{:S(2)}, u32[]{:S(2)}) collective-permute-start(bf16[32,4096]{1,0:T(8,128)(2,1)S(1)} %get-tuple-element.81), channel_id=1, source_target_pairs={{0,4},{4,0},{8,12},{12,8},{1,5},{5,1},{9,13},{13,9},{2,6},{6,2},{1... | collective-permute-start | bytes 786440 | tf_op jit(solution)/shard_map/ppermute | solution.py:98
  66.3 4.2 %collective-permute-start.25 = (bf16[32,4096]{1,0:T(8,128)(2,1)S(1)}, bf16[32,4096]{1,0:T(8,128)(2,1)S(1)}, u32[]{:S(2)}, u32[]{:S(2)}) collective-permute-start(bf16[32,4096]{1,0:T(8,128)(2,1)S(1)} %add_convert_fusion.2), channel_id=1, source_target_pairs={{4,8},{8,4},{5,9},{9,5},{6,10},{10,6},{7,11},{11,7},{20,24},{24,20... | collective-permute-start | bytes 786440 | tf_op jit(solution)/shard_map/ppermute | solution.py:101
  67.0 14.3 %collective-permute-start.23 = (bf16[32,4096]{1,0:T(8,128)(2,1)S(1)}, bf16[32,4096]{1,0:T(8,128)(2,1)S(1)}, u32[]{:S(2)}, u32[]{:S(2)}) collective-permute-start(bf16[32,4096]{1,0:T(8,128)(2,1)S(1)} %get-tuple-element.77), channel_id=1, source_target_pairs={{0,4},{4,0},{8,12},{12,8},{1,5},{5,1},{9,13},{13,9},{2,6},{6,2},{1... | collective-permute-start | bytes 786440 | tf_op jit(solution)/shard_map/ppermute | solution.py:98
  69.9 6.6 %collective-permute-start.21 = (bf16[32,4096]{1,0:T(8,128)(2,1)S(1)}, bf16[32,4096]{1,0:T(8,128)(2,1)S(1)}, u32[]{:S(2)}, u32[]{:S(2)}) collective-permute-start(bf16[32,4096]{1,0:T(8,128)(2,1)S(1)} %add_convert_fusion.5), channel_id=1, source_target_pairs={{4,8},{8,4},{5,9},{9,5},{6,10},{10,6},{7,11},{11,7},{20,24},{24,20... | collective-permute-start | bytes 786440 | tf_op jit(solution)/shard_map/ppermute | solution.py:101
  70.7 16.0 %collective-permute-start.26 = (bf16[32,4096]{1,0:T(8,128)(2,1)S(1)}, bf16[32,4096]{1,0:T(8,128)(2,1)S(1)}, u32[]{:S(2)}, u32[]{:S(2)}) collective-permute-start(bf16[32,4096]{1,0:T(8,128)(2,1)S(1)} %fusion.1), channel_id=1, source_target_pairs={{0,4},{4,0},{8,12},{12,8},{1,5},{5,1},{9,13},{13,9},{2,6},{6,2},{1... | collective-permute-start | bytes 786440 | tf_op jit(solution)/shard_map/ppermute | solution.py:104
  75.8 10.9 %collective-permute-start.28 = (bf16[32,4096]{1,0:T(8,128)(2,1)S(1)}, bf16[32,4096]{1,0:T(8,128)(2,1)S(1)}, u32[]{:S(2)}, u32[]{:S(2)}) collective-permute-start(bf16[32,4096]{1,0:T(8,128)(2,1)S(1)} %add_convert_fusion), channel_id=1, source_target_pairs={{4,8},{8,4},{5,9},{9,5},{6,10},{10,6},{7,11},{11,7},{20,24},{24,20... | collective-permute-start | bytes 786440 | tf_op jit(solution)/shard_map/ppermute | solution.py:102
  76.6 15.2 %collective-permute-start.22 = (bf16[32,4096]{1,0:T(8,128)(2,1)S(1)}, bf16[32,4096]{1,0:T(8,128)(2,1)S(1)}, u32[]{:S(2)}, u32[]{:S(2)}) collective-permute-start(bf16[32,4096]{1,0:T(8,128)(2,1)S(1)} %fusion), channel_id=1, source_target_pairs={{0,4},{4,0},{8,12},{12,8},{1,5},{5,1},{9,13},{13,9},{2,6},{6,2},{1... | collective-permute-start | bytes 786440 | tf_op jit(solution)/shard_map/ppermute | solution.py:104
  81.4 10.4 %collective-permute-start.24 = (bf16[32,4096]{1,0:T(8,128)(2,1)S(1)}, bf16[32,4096]{1,0:T(8,128)(2,1)S(1)}, u32[]{:S(2)}, u32[]{:S(2)}) collective-permute-start(bf16[32,4096]{1,0:T(8,128)(2,1)S(1)} %add_convert_fusion.3), channel_id=1, source_target_pairs={{4,8},{8,4},{5,9},{9,5},{6,10},{10,6},{7,11},{11,7},{20,24},{24,20... | collective-permute-start | bytes 786440 | tf_op jit(solution)/shard_map/ppermute | solution.py:102
  (8 other events, 30.4 us)

commit v13 on v10

--- a/solution.py
+++ b/solution.py
@@ -385,8 +385,15 @@
     )(scores)
 
 
-def sums_kernel(readers, members, pieces, all_ref, score_ref, mask_ref, *refs):
-    lse_refs, norm_ref, out_refs = refs[:readers], refs[readers], refs[readers + 1 :]
+def emit_sums(posterior, all_ref, piece, out_refs):
+    sums = jnp.dot(posterior, all_ref[:, piece], preferred_element_type=jnp.float32)
+    count = sums.shape[0] // len(out_refs)
+    for s, out_ref in enumerate(out_refs):
+        out_ref[...] = sums[s * count : (s + 1) * count].astype(out_ref.dtype)
+
+
+def first_sums_kernel(readers, piece, all_ref, score_ref, mask_ref, *refs):
+    lse_refs, norm_ref, post_ref = refs[:readers], refs[readers], refs[readers + 1]
     kept = []
     for k, lse_ref in enumerate(lse_refs):
         kept.append(jnp.where(mask_ref[k : k + 1, :] > 0.0, lse_ref[...], -jnp.inf))
@@ -400,26 +407,23 @@
     norm_ref[...] = norm
     exponent = jnp.where(mask_ref[0:1, :] > 0.0, score_ref[...] - norm, -jnp.inf)
     posterior = jnp.exp(exponent).astype(jnp.bfloat16)
-    count = posterior.shape[0] // members
-    for q, piece in enumerate(pieces):
-        sums = jnp.dot(posterior, all_ref[:, piece], preferred_element_type=jnp.float32)
-        for s, out_ref in enumerate(out_refs[q * members : (q + 1) * members]):
-            out_ref[...] = sums[s * count : (s + 1) * count].astype(out_ref.dtype)
-
-
-def group_sums(members, pieces, all_images, scores, masks, lses):
-    refs, slots = scores.shape
-    width = all_images.shape[1]
-    blocks = [
-        jax.ShapeDtypeStruct((refs // members, piece.stop - piece.start), jnp.bfloat16)
-        for piece in pieces
-        for _ in range(members)
-    ]
-    norms, *outs = pl.pallas_call(
-        partial(sums_kernel, len(lses), members, pieces),
-        out_shape=(jax.ShapeDtypeStruct((1, slots), jnp.float32), *blocks),
-        in_specs=[VMEM_SPEC] * (3 + len(lses)),
-        out_specs=(VMEM_SPEC,) * (1 + len(blocks)),
+    post_ref[...] = posterior
+    emit_sums(posterior, all_ref, piece, refs[readers + 2 :])
+
+
+def later_sums_kernel(piece, all_ref, post_ref, *out_refs):
+    emit_sums(post_ref[...], all_ref, piece, out_refs)
+
+
+def group_sums(kernel, piece, members, all_images, operands, extra):
+    refs, slots = operands[0].shape
+    width = piece.stop - piece.start
+    block = jax.ShapeDtypeStruct((refs // members, width), jnp.bfloat16)
+    outs = pl.pallas_call(
+        kernel,
+        out_shape=tuple(extra) + (block,) * members,
+        in_specs=[VMEM_SPEC] * (1 + len(operands)),
+        out_specs=(VMEM_SPEC,) * (len(extra) + members),
         compiler_params=pltpu.CompilerParams(vmem_limit_bytes=SUMS_VMEM),
         cost_estimate=pl.CostEstimate(
             flops=2 * refs * slots * width,
@@ -427,8 +431,8 @@
             transcendentals=0,
         ),
         name="sums",
-    )(all_images, scores, masks, *lses)
-    return norms, [outs[q * members : (q + 1) * members] for q in range(len(pieces))]
+    )(all_images, *operands)
+    return outs[: len(extra)], outs[len(extra) :]
 
 
 def on_device(images, routes, projections, noise_weights):
@@ -449,7 +453,22 @@
         mine = group_lse(scores)
     lses = [mine] + [swap_bits(mine, "reader", k) for k in range(1, readers)]
     pieces = [slice(0, width // 2), slice(width // 2, width)]
-    norms, parts = group_sums(members, pieces, all_images, scores, masks, lses)
+    extra = (
+        jax.ShapeDtypeStruct((1, scores.shape[1]), jnp.float32),
+        jax.ShapeDtypeStruct(scores.shape, jnp.bfloat16),
+    )
+    (norms, posterior), first = group_sums(
+        partial(first_sums_kernel, readers, pieces[0]),
+        pieces[0],
+        members,
+        all_images,
+        (scores, masks, *lses),
+        extra,
+    )
+    _, last = group_sums(
+        partial(later_sums_kernel, pieces[1]), pieces[1], members, all_images, (posterior,), ()
+    )
+    parts = [first, last]
     scatter = pair_scatter if members == 4 else line_scatter
     total = scatter(parts, "blk")
     normalizer = lax.dynamic_slice(norms.reshape(-1), (reader * rows,), (rows,))

time: 92.6 us -> 92.1 us (level)
  waiting for transfers between devices: 28.5 us -> 25 us
  local copies, waits for them, and re-layouts: 4.68 us -> 7.47 us
    ppermute x2, waiting for transfers between devices: 6.42 us -> 2.91 us  [pair_scatter(): for_far_end = [lax.ppermute(parts[3], axis, SIDES) for parts in pieces]]
    unnamed x6 -> x10, local copies, waits for them, and re-layouts: 2.16 us -> 4.95 us
  transfers between devices with their start and end apart: 29 -> 29, of which waited for: 10 -> 10; matrix products, arithmetic and copies ran while one was open for 3% -> 3% of each run, Pallas kernels for 2% -> 3%
where the time goes in v13:
time: 92.1 us; the launch traced here: 91.6 us
  starting transfers between devices  50.7 us (55%)
  waiting for transfers between devices  25 us (27%)
  local copies, waits for them, and re-layouts  7.47 us (8%)
  Pallas kernels  6.92 us (8%)
    ppermute x2, waiting for transfers between devices, pair_scatter(): from_side = lax.ppermute(near, axis, SIDES)  9.61 us
    ppermute x2, starting transfers between devices, pair_scatter(): from_side = lax.ppermute(near, axis, SIDES)  9.2 us
    ppermute x2, starting transfers between devices, staged_gather(): far = lax.ppermute(across, 'blk', SIDES)  8.16 us
    ppermute x9, waiting for transfers between devices, swap_bits(): lax.ppermute(block, axis, [(i, i ^ bits) for i in range(lax.axis_size(axi...  7.38 us
    ppermute x2, starting transfers between devices, staged_gather(): end = lax.ppermute(across_far, 'blk', SIDES)  7.26 us
    ppermute x9, starting transfers between devices, swap_bits(): lax.ppermute(block, axis, [(i, i ^ bits) for i in range(lax.axis_size(axi...  6.97 us
    ppermute x2, starting transfers between devices, staged_gather(): lax.ppermute(one, 'blk', SIDES)  6.09 us
    ppermute x2, starting transfers between devices, pair_scatter(): for_far_middle = [lax.ppermute(part, axis, SIDES) for part in second]  5.51 us
  transfers between devices with their start and end apart: 29, of which 10 were waited for; matrix products, arithmetic and copies ran while one was open for 3% of the time, Pallas kernels for 3%

profile of v13, /device:TPU:0, one launch (start us, length us, event | category | flops | bytes accessed | tf_op | source)
XLA Modules:
  0.0 91.6 jit_solution(13677385402954339351)
XLA Ops:
  1.1 2.6 %collective-permute-start.9 = (bf16[96,8192]{1,0:T(8,128)(2,1)}, bf16[96,8192]{1,0:T(8,128)(2,1)S(1)}, u32[]{:S(2)}, u32[]{:S(2)}) collective-permute-start(bf16[96,8192]{1,0:T(8,128)(2,1)} %refs_0_.1), channel_id=1, source_target_pairs={{0,2},{1,3},{2,0},{3,1},{4,6},{5,7},{6,4},{7,5},{8,10},{9,11},{10,... | collective-permute-start | bytes 4718600 | tf_op jit(solution)/shard_map/ppermute | solution.py:20
  4.7 1.6 %collective-permute-start.4 = (bf16[32,4608]{1,0:T(8,128)(2,1)S(1)}, bf16[32,4608]{1,0:T(8,128)(2,1)S(1)}, u32[]{:S(2)}, u32[]{:S(2)}) collective-permute-start(bf16[32,4608]{1,0:T(8,128)(2,1)S(1)} %slice.9.refs_2_), channel_id=1, source_target_pairs={{0,4},{4,0},{8,12},{12,8},{1,5},{5,1},{9,13},{13,9},{2,6},{6,2},{1... | collective-permute-start | bytes 884744 | tf_op jit(solution)/shard_map/ppermute | solution.py:43
  8.0 4.4 %collective-permute-start = (bf16[32,3584]{1,0:T(8,128)(2,1)S(1)}, bf16[32,3584]{1,0:T(8,128)(2,1)S(1)}, u32[]{:S(2)}, u32[]{:S(2)}) collective-permute-start(bf16[32,3584]{1,0:T(8,128)(2,1)S(1)} %slice.8.refs_3_), channel_id=1, source_target_pairs={{0,4},{4,0},{8,12},{12,8},{1,5},{5,1},{9,13},{13,9},{2,6},{6,2},{1... | collective-permute-start | bytes 688136 | tf_op jit(solution)/shard_map/ppermute | solution.py:43
  12.4 2.2 %collective-permute-done.4.refs_4_ = bf16[32,4608]{1,0:T(8,128)(2,1)S(1)} collective-permute-done((bf16[32,4608]{1,0:T(8,128)(2,1)S(1)}, bf16[32,4608]{1,0:T(8,128)(2,1)S(1)}, u32[]{:S(2)}, u32[]{:S(2)}) %collective-permute-start.4) | collective-permute-done | bytes 294944 | tf_op jit(solution)/shard_map/ppermute | solution.py:43
  15.3 4.5 %collective-permute-start.6 = (bf16[32,4608]{1,0:T(8,128)(2,1)S(1)}, bf16[32,4608]{1,0:T(8,128)(2,1)S(1)}, u32[]{:S(2)}, u32[]{:S(2)}) collective-permute-start(bf16[32,4608]{1,0:T(8,128)(2,1)S(1)} %collective-permute-done.5.refs_5_), channel_id=1, source_target_pairs={{0,4},{4,0},{8,12},{12,8},{1,5},{5,1},{9,13},{13,9},{2,6},{6,2},{1... | collective-permute-start | bytes 884744 | tf_op jit(solution)/shard_map/ppermute | solution.py:52
  20.4 3.7 %collective-permute-start.2 = (bf16[32,3584]{1,0:T(8,128)(2,1)S(1)}, bf16[32,3584]{1,0:T(8,128)(2,1)S(1)}, u32[]{:S(2)}, u32[]{:S(2)}) collective-permute-start(bf16[32,3584]{1,0:T(8,128)(2,1)S(1)} %collective-permute-done.1.refs_7_), channel_id=1, source_target_pairs={{0,4},{4,0},{8,12},{12,8},{1,5},{5,1},{9,13},{13,9},{2,6},{6,2},{1... | collective-permute-start | bytes 688136 | tf_op jit(solution)/shard_map/ppermute | solution.py:52
  24.8 1.4 %copy-done.2 = bf16[96,8192]{1,0:T(8,128)(2,1)S(1)} copy-done((bf16[96,8192]{1,0:T(8,128)(2,1)S(1)}, bf16[96,8192]{1,0:T(8,128)(2,1)}, u32[]{:S(2)}) %copy-start.2) | copy-done | bytes 1572888
  27.0 1.1 %stage.1 = (bf16[64,8192]{1,0:T(8,128)(2,1)S(1)}, f32[64,1]{1,0:T(8,128)S(1)}, bf16[192,8192]{1,0:T(8,128)(2,1)S(1)}, f32[1,8192]{1,0:T(1,128)S(1)}) custom-call(bf16[96,8192]{1,0:T(8,128)(2,1)S(1)} %copy-done.2, bf16[96,8192]{1,0:T(8,128)(2,1)S(1)} %collective-permute-done.8.refs_1_, bf16[32,4608]{1,0:T(8,128)(2,1)S(1)} %slice.9.refs_2_, ...), custom_call_target="tpu_custom_call" | custom-call | flops 4194304 | bytes 12000000 | tf_op jit(solution)/shard_map/stage/pallas_call | solution.py:247
  28.1 4.0 %collective-permute-start.10 = (bf16[32,4608]{1,0:T(8,128)(2,1)S(1)}, bf16[32,4608]{1,0:T(8,128)(2,1)S(1)}, u32[]{:S(2)}, u32[]{:S(2)}) collective-permute-start(bf16[32,4608]{1,0:T(8,128)(2,1)S(1)} %collective-permute-done.7.refs_1_), channel_id=1, source_target_pairs={{0,4},{4,0},{8,12},{12,8},{1,5},{5,1},{9,13},{13,9},{2,6},{6,2},{1... | collective-permute-start | bytes 884744 | tf_op jit(solution)/shard_map/ppermute | solution.py:55
  32.2 3.2 %collective-permute-start.11 = (bf16[32,3584]{1,0:T(8,128)(2,1)S(1)}, bf16[32,3584]{1,0:T(8,128)(2,1)S(1)}, u32[]{:S(2)}, u32[]{:S(2)}) collective-permute-start(bf16[32,3584]{1,0:T(8,128)(2,1)S(1)} %collective-permute-done.3.refs_3_), channel_id=1, source_target_pairs={{0,4},{4,0},{8,12},{12,8},{1,5},{5,1},{9,13},{13,9},{2,6},{6,2},{1... | collective-permute-start | bytes 688136 | tf_op jit(solution)/shard_map/ppermute | solution.py:55
  35.4 3.5 %collective-permute-done.9.refs_1_ = bf16[96,8192]{1,0:T(8,128)(2,1)S(1)} collective-permute-done((bf16[96,8192]{1,0:T(8,128)(2,1)}, bf16[96,8192]{1,0:T(8,128)(2,1)S(1)}, u32[]{:S(2)}, u32[]{:S(2)}) %collective-permute-start.9) | collective-permute-done | bytes 1572896 | tf_op jit(solution)/shard_map/ppermute | solution.py:20
  38.9 2.9 %collective-permute-done.11.refs_6_ = bf16[32,3584]{1,0:T(8,128)(2,1)S(1)} collective-permute-done((bf16[32,3584]{1,0:T(8,128)(2,1)S(1)}, bf16[32,3584]{1,0:T(8,128)(2,1)S(1)}, u32[]{:S(2)}, u32[]{:S(2)}) %collective-permute-start.11) | collective-permute-done | bytes 229408 | tf_op jit(solution)/shard_map/ppermute | solution.py:55
  45.9 2.5 %scores.1 = (f32[128,384]{1,0:T(8,128)S(1)}, f32[4,384]{1,0:T(4,128)S(1)}, f32[1,384]{1,0:T(1,128)S(1)}, bf16[384,8192]{1,0:T(8,128)(2,1)S(1)}) custom-call(bf16[192,8192]{1,0:T(8,128)(2,1)S(1)} %get-tuple-element.55.refs_0_, bf16[96,8192]{1,0:T(8,128)(2,1)S(1)} %collective-permute-done.9.refs_1_, bf16[96,8192]{1,0:T(8,128)(2,1)S(1)} %collective-permute-done.12.refs_2_, ...), custom_call_target="tpu_custom_call" | custom-call | flops 805306368 | bytes 8388608 | tf_op jit(solution)/shard_map/scores/pallas_call | solution.py:355
  48.5 1.4 %collective-permute-start.17 = (f32[1,384]{1,0:T(1,128)S(1)}, f32[1,384]{1,0:T(1,128)S(1)}, u32[]{:S(2)}, u32[]{:S(2)}) collective-permute-start(f32[1,384]{1,0:T(1,128)S(1)} %get-tuple-element.70.refs_0_), channel_id=1, source_target_pairs={{0,2},{1,3},{2,0},{3,1},{4,6},{5,7},{6,4},{7,5},{8,10},{9,11},{10,... | collective-permute-start | bytes 4616 | tf_op jit(solution)/shard_map/ppermute | solution.py:20
  50.3 1.8 %collective-permute-done.17.refs_2_ = f32[1,384]{1,0:T(1,128)S(1)} collective-permute-done((f32[1,384]{1,0:T(1,128)S(1)}, f32[1,384]{1,0:T(1,128)S(1)}, u32[]{:S(2)}, u32[]{:S(2)}) %collective-permute-start.17) | collective-permute-done | bytes 1568 | tf_op jit(solution)/shard_map/ppermute | solution.py:20
  53.7 2.1 %collective-permute-start.19 = (bf16[32,4096]{1,0:T(8,128)(2,1)S(1)}, bf16[32,4096]{1,0:T(8,128)(2,1)S(1)}, u32[]{:S(2)}, u32[]{:S(2)}) collective-permute-start(bf16[32,4096]{1,0:T(8,128)(2,1)S(1)} %get-tuple-element.76), channel_id=1, source_target_pairs={{0,4},{4,0},{8,12},{12,8},{1,5},{5,1},{9,13},{13,9},{2,6},{6,2},{1... | collective-permute-start | bytes 786440 | tf_op jit(solution)/shard_map/ppermute | solution.py:93
  55.8 2.8 %copy-done.1 = bf16[384,8192]{1,0:T(8,128)(2,1)S(1)} copy-done((bf16[384,8192]{1,0:T(8,128)(2,1)S(1)}, bf16[384,8192]{1,0:T(8,128)(2,1)}, u32[]{:S(2)}) %copy-start.1) | copy-done | bytes 6291480
  60.0 2.9 %collective-permute-done.19 = bf16[32,4096]{1,0:T(8,128)(2,1)S(1)} collective-permute-done((bf16[32,4096]{1,0:T(8,128)(2,1)S(1)}, bf16[32,4096]{1,0:T(8,128)(2,1)S(1)}, u32[]{:S(2)}, u32[]{:S(2)}) %collective-permute-start.19) | collective-permute-done | bytes 262176 | tf_op jit(solution)/shard_map/ppermute | solution.py:93
  62.9 2.1 %collective-permute-start.27 = (bf16[32,4096]{1,0:T(8,128)(2,1)S(1)}, bf16[32,4096]{1,0:T(8,128)(2,1)S(1)}, u32[]{:S(2)}, u32[]{:S(2)}) collective-permute-start(bf16[32,4096]{1,0:T(8,128)(2,1)S(1)} %get-tuple-element.81), channel_id=1, source_target_pairs={{0,4},{4,0},{8,12},{12,8},{1,5},{5,1},{9,13},{13,9},{2,6},{6,2},{1... | collective-permute-start | bytes 786440 | tf_op jit(solution)/shard_map/ppermute | solution.py:97
  65.7 3.5 %collective-permute-start.23 = (bf16[32,4096]{1,0:T(8,128)(2,1)S(1)}, bf16[32,4096]{1,0:T(8,128)(2,1)S(1)}, u32[]{:S(2)}, u32[]{:S(2)}) collective-permute-start(bf16[32,4096]{1,0:T(8,128)(2,1)S(1)} %get-tuple-element.77), channel_id=1, source_target_pairs={{0,4},{4,0},{8,12},{12,8},{1,5},{5,1},{9,13},{13,9},{2,6},{6,2},{1... | collective-permute-start | bytes 786440 | tf_op jit(solution)/shard_map/ppermute | solution.py:97
  70.0 4.4 %collective-permute-start.26 = (bf16[32,4096]{1,0:T(8,128)(2,1)S(1)}, bf16[32,4096]{1,0:T(8,128)(2,1)S(1)}, u32[]{:S(2)}, u32[]{:S(2)}) collective-permute-start(bf16[32,4096]{1,0:T(8,128)(2,1)S(1)} %fusion.1), channel_id=1, source_target_pairs={{0,4},{4,0},{8,12},{12,8},{1,5},{5,1},{9,13},{13,9},{2,6},{6,2},{1... | collective-permute-start | bytes 786440 | tf_op jit(solution)/shard_map/ppermute | solution.py:103
  75.3 4.8 %collective-permute-start.22 = (bf16[32,4096]{1,0:T(8,128)(2,1)S(1)}, bf16[32,4096]{1,0:T(8,128)(2,1)S(1)}, u32[]{:S(2)}, u32[]{:S(2)}) collective-permute-start(bf16[32,4096]{1,0:T(8,128)(2,1)S(1)} %fusion), channel_id=1, source_target_pairs={{0,4},{4,0},{8,12},{12,8},{1,5},{5,1},{9,13},{13,9},{2,6},{6,2},{1... | collective-permute-start | bytes 786440 | tf_op jit(solution)/shard_map/ppermute | solution.py:103
  80.8 4.6 %collective-permute-done.26 = bf16[32,4096]{1,0:T(8,128)(2,1)S(1)} collective-permute-done((bf16[32,4096]{1,0:T(8,128)(2,1)S(1)}, bf16[32,4096]{1,0:T(8,128)(2,1)S(1)}, u32[]{:S(2)}, u32[]{:S(2)}) %collective-permute-start.26) | collective-permute-done | bytes 262176 | tf_op jit(solution)/shard_map/ppermute | solution.py:103
  85.6 5.0 %collective-permute-done.22 = bf16[32,4096]{1,0:T(8,128)(2,1)S(1)} collective-permute-done((bf16[32,4096]{1,0:T(8,128)(2,1)S(1)}, bf16[32,4096]{1,0:T(8,128)(2,1)S(1)}, u32[]{:S(2)}, u32[]{:S(2)}) %collective-permute-start.22) | collective-permute-done | bytes 262176 | tf_op jit(solution)/shard_map/ppermute | solution.py:103
  (61 shorter events, 17.8 us)
Async XLA Ops:
  0.6 23.5 %collective-permute-start.8 = (bf16[96,8192]{1,0:T(8,128)(2,1)}, bf16[96,8192]{1,0:T(8,128)(2,1)S(1)}, u32[]{:S(2)}, u32[]{:S(2)}) collective-permute-start(bf16[96,8192]{1,0:T(8,128)(2,1)} %refs_0_.1), channel_id=1, source_target_pairs={{0,1},{1,0},{2,3},{3,2},{4,5},{5,4},{6,7},{7,6},{8,9},{9,8},{10,11... | collective-permute-start | bytes 4718600 | tf_op jit(solution)/shard_map/ppermute | solution.py:20
  1.1 37.8 %collective-permute-start.9 = (bf16[96,8192]{1,0:T(8,128)(2,1)}, bf16[96,8192]{1,0:T(8,128)(2,1)S(1)}, u32[]{:S(2)}, u32[]{:S(2)}) collective-permute-start(bf16[96,8192]{1,0:T(8,128)(2,1)} %refs_0_.1), channel_id=1, source_target_pairs={{0,2},{1,3},{2,0},{3,1},{4,6},{5,7},{6,4},{7,5},{8,10},{9,11},{10,... | collective-permute-start | bytes 4718600 | tf_op jit(solution)/shard_map/ppermute | solution.py:20
  4.7 9.9 %collective-permute-start.4 = (bf16[32,4608]{1,0:T(8,128)(2,1)S(1)}, bf16[32,4608]{1,0:T(8,128)(2,1)S(1)}, u32[]{:S(2)}, u32[]{:S(2)}) collective-permute-start(bf16[32,4608]{1,0:T(8,128)(2,1)S(1)} %slice.9.refs_2_), channel_id=1, source_target_pairs={{0,4},{4,0},{8,12},{12,8},{1,5},{5,1},{9,13},{13,9},{2,6},{6,2},{1... | collective-permute-start | bytes 884744 | tf_op jit(solution)/shard_map/ppermute | solution.py:43
  6.3 8.9 %collective-permute-start.5 = (bf16[32,4608]{1,0:T(8,128)(2,1)S(1)}, bf16[32,4608]{1,0:T(8,128)(2,1)S(1)}, u32[]{:S(2)}, u32[]{:S(2)}) collective-permute-start(bf16[32,4608]{1,0:T(8,128)(2,1)S(1)} %slice.9.refs_2_), channel_id=1, source_target_pairs={{4,8},{8,4},{5,9},{9,5},{6,10},{10,6},{7,11},{11,7},{20,24},{24,20... | collective-permute-start | bytes 884744 | tf_op jit(solution)/shard_map/ppermute | solution.py:43
  8.0 11.8 %collective-permute-start = (bf16[32,3584]{1,0:T(8,128)(2,1)S(1)}, bf16[32,3584]{1,0:T(8,128)(2,1)S(1)}, u32[]{:S(2)}, u32[]{:S(2)}) collective-permute-start(bf16[32,3584]{1,0:T(8,128)(2,1)S(1)} %slice.8.refs_3_), channel_id=1, source_target_pairs={{0,4},{4,0},{8,12},{12,8},{1,5},{5,1},{9,13},{13,9},{2,6},{6,2},{1... | collective-permute-start | bytes 688136 | tf_op jit(solution)/shard_map/ppermute | solution.py:43
  14.6 5.8 %collective-permute-start.1 = (bf16[32,3584]{1,0:T(8,128)(2,1)S(1)}, bf16[32,3584]{1,0:T(8,128)(2,1)S(1)}, u32[]{:S(2)}, u32[]{:S(2)}) collective-permute-start(bf16[32,3584]{1,0:T(8,128)(2,1)S(1)} %slice.8.refs_3_), channel_id=1, source_target_pairs={{4,8},{8,4},{5,9},{9,5},{6,10},{10,6},{7,11},{11,7},{20,24},{24,20... | collective-permute-start | bytes 688136 | tf_op jit(solution)/shard_map/ppermute | solution.py:43
  15.3 12.8 %collective-permute-start.6 = (bf16[32,4608]{1,0:T(8,128)(2,1)S(1)}, bf16[32,4608]{1,0:T(8,128)(2,1)S(1)}, u32[]{:S(2)}, u32[]{:S(2)}) collective-permute-start(bf16[32,4608]{1,0:T(8,128)(2,1)S(1)} %collective-permute-done.5.refs_5_), channel_id=1, source_target_pairs={{0,4},{4,0},{8,12},{12,8},{1,5},{5,1},{9,13},{13,9},{2,6},{6,2},{1... | collective-permute-start | bytes 884744 | tf_op jit(solution)/shard_map/ppermute | solution.py:52
  19.8 8.4 %collective-permute-start.7 = (bf16[32,4608]{1,0:T(8,128)(2,1)S(1)}, bf16[32,4608]{1,0:T(8,128)(2,1)S(1)}, u32[]{:S(2)}, u32[]{:S(2)}) collective-permute-start(bf16[32,4608]{1,0:T(8,128)(2,1)S(1)} %collective-permute-done.4.refs_4_), channel_id=1, source_target_pairs={{4,8},{8,4},{5,9},{9,5},{6,10},{10,6},{7,11},{11,7},{20,24},{24,20... | collective-permute-start | bytes 884744 | tf_op jit(solution)/shard_map/ppermute | solution.py:53
  20.4 11.7 %collective-permute-start.2 = (bf16[32,3584]{1,0:T(8,128)(2,1)S(1)}, bf16[32,3584]{1,0:T(8,128)(2,1)S(1)}, u32[]{:S(2)}, u32[]{:S(2)}) collective-permute-start(bf16[32,3584]{1,0:T(8,128)(2,1)S(1)} %collective-permute-done.1.refs_7_), channel_id=1, source_target_pairs={{0,4},{4,0},{8,12},{12,8},{1,5},{5,1},{9,13},{13,9},{2,6},{6,2},{1... | collective-permute-start | bytes 688136 | tf_op jit(solution)/shard_map/ppermute | solution.py:52
  24.1 8.0 %collective-permute-start.3 = (bf16[32,3584]{1,0:T(8,128)(2,1)S(1)}, bf16[32,3584]{1,0:T(8,128)(2,1)S(1)}, u32[]{:S(2)}, u32[]{:S(2)}) collective-permute-start(bf16[32,3584]{1,0:T(8,128)(2,1)S(1)} %collective-permute-done.refs_5_), channel_id=1, source_target_pairs={{4,8},{8,4},{5,9},{9,5},{6,10},{10,6},{7,11},{11,7},{20,24},{24,20... | collective-permute-start | bytes 688136 | tf_op jit(solution)/shard_map/ppermute | solution.py:53
  28.1 13.7 %collective-permute-start.10 = (bf16[32,4608]{1,0:T(8,128)(2,1)S(1)}, bf16[32,4608]{1,0:T(8,128)(2,1)S(1)}, u32[]{:S(2)}, u32[]{:S(2)}) collective-permute-start(bf16[32,4608]{1,0:T(8,128)(2,1)S(1)} %collective-permute-done.7.refs_1_), channel_id=1, source_target_pairs={{0,4},{4,0},{8,12},{12,8},{1,5},{5,1},{9,13},{13,9},{2,6},{6,2},{1... | collective-permute-start | bytes 884744 | tf_op jit(solution)/shard_map/ppermute | solution.py:55
  32.2 9.6 %collective-permute-start.11 = (bf16[32,3584]{1,0:T(8,128)(2,1)S(1)}, bf16[32,3584]{1,0:T(8,128)(2,1)S(1)}, u32[]{:S(2)}, u32[]{:S(2)}) collective-permute-start(bf16[32,3584]{1,0:T(8,128)(2,1)S(1)} %collective-permute-done.3.refs_3_), channel_id=1, source_target_pairs={{0,4},{4,0},{8,12},{12,8},{1,5},{5,1},{9,13},{13,9},{2,6},{6,2},{1... | collective-permute-start | bytes 688136 | tf_op jit(solution)/shard_map/ppermute | solution.py:55
  41.8 4.1 %collective-permute-start.12 = (bf16[96,8192]{1,0:T(8,128)(2,1)S(1)}, bf16[96,8192]{1,0:T(8,128)(2,1)S(1)}, u32[]{:S(2)}, u32[]{:S(2)}) collective-permute-start(bf16[96,8192]{1,0:T(8,128)(2,1)S(1)} %collective-permute-done.9.refs_1_), channel_id=1, source_target_pairs={{0,1},{1,0},{2,3},{3,2},{4,5},{5,4},{6,7},{7,6},{8,9},{9,8},{10,11... | collective-permute-start | bytes 4718600 | tf_op jit(solution)/shard_map/ppermute | solution.py:20
  48.5 3.6 %collective-permute-start.17 = (f32[1,384]{1,0:T(1,128)S(1)}, f32[1,384]{1,0:T(1,128)S(1)}, u32[]{:S(2)}, u32[]{:S(2)}) collective-permute-start(f32[1,384]{1,0:T(1,128)S(1)} %get-tuple-element.70.refs_0_), channel_id=1, source_target_pairs={{0,2},{1,3},{2,0},{3,1},{4,6},{5,7},{6,4},{7,5},{8,10},{9,11},{10,... | collective-permute-start | bytes 4616 | tf_op jit(solution)/shard_map/ppermute | solution.py:20
  53.7 9.2 %collective-permute-start.19 = (bf16[32,4096]{1,0:T(8,128)(2,1)S(1)}, bf16[32,4096]{1,0:T(8,128)(2,1)S(1)}, u32[]{:S(2)}, u32[]{:S(2)}) collective-permute-start(bf16[32,4096]{1,0:T(8,128)(2,1)S(1)} %get-tuple-element.76), channel_id=1, source_target_pairs={{0,4},{4,0},{8,12},{12,8},{1,5},{5,1},{9,13},{13,9},{2,6},{6,2},{1... | collective-permute-start | bytes 786440 | tf_op jit(solution)/shard_map/ppermute | solution.py:93
  59.3 9.9 %collective-permute-start.20 = (bf16[32,4096]{1,0:T(8,128)(2,1)S(1)}, bf16[32,4096]{1,0:T(8,128)(2,1)S(1)}, u32[]{:S(2)}, u32[]{:S(2)}) collective-permute-start(bf16[32,4096]{1,0:T(8,128)(2,1)S(1)} %get-tuple-element.78), channel_id=1, source_target_pairs={{0,4},{4,0},{8,12},{12,8},{1,5},{5,1},{9,13},{13,9},{2,6},{6,2},{1... | collective-permute-start | bytes 786440 | tf_op jit(solution)/shard_map/ppermute | solution.py:93
  62.9 11.6 %collective-permute-start.27 = (bf16[32,4096]{1,0:T(8,128)(2,1)S(1)}, bf16[32,4096]{1,0:T(8,128)(2,1)S(1)}, u32[]{:S(2)}, u32[]{:S(2)}) collective-permute-start(bf16[32,4096]{1,0:T(8,128)(2,1)S(1)} %get-tuple-element.81), channel_id=1, source_target_pairs={{0,4},{4,0},{8,12},{12,8},{1,5},{5,1},{9,13},{13,9},{2,6},{6,2},{1... | collective-permute-start | bytes 786440 | tf_op jit(solution)/shard_map/ppermute | solution.py:97
  65.0 4.9 %collective-permute-start.25 = (bf16[32,4096]{1,0:T(8,128)(2,1)S(1)}, bf16[32,4096]{1,0:T(8,128)(2,1)S(1)}, u32[]{:S(2)}, u32[]{:S(2)}) collective-permute-start(bf16[32,4096]{1,0:T(8,128)(2,1)S(1)} %add_convert_fusion.2), channel_id=1, source_target_pairs={{4,8},{8,4},{5,9},{9,5},{6,10},{10,6},{7,11},{11,7},{20,24},{24,20... | collective-permute-start | bytes 786440 | tf_op jit(solution)/shard_map/ppermute | solution.py:100
  65.7 14.4 %collective-permute-start.23 = (bf16[32,4096]{1,0:T(8,128)(2,1)S(1)}, bf16[32,4096]{1,0:T(8,128)(2,1)S(1)}, u32[]{:S(2)}, u32[]{:S(2)}) collective-permute-start(bf16[32,4096]{1,0:T(8,128)(2,1)S(1)} %get-tuple-element.77), channel_id=1, source_target_pairs={{0,4},{4,0},{8,12},{12,8},{1,5},{5,1},{9,13},{13,9},{2,6},{6,2},{1... | collective-permute-start | bytes 786440 | tf_op jit(solution)/shard_map/ppermute | solution.py:97
  69.2 6.0 %collective-permute-start.21 = (bf16[32,4096]{1,0:T(8,128)(2,1)S(1)}, bf16[32,4096]{1,0:T(8,128)(2,1)S(1)}, u32[]{:S(2)}, u32[]{:S(2)}) collective-permute-start(bf16[32,4096]{1,0:T(8,128)(2,1)S(1)} %add_convert_fusion.5), channel_id=1, source_target_pairs={{4,8},{8,4},{5,9},{9,5},{6,10},{10,6},{7,11},{11,7},{20,24},{24,20... | collective-permute-start | bytes 786440 | tf_op jit(solution)/shard_map/ppermute | solution.py:100
  70.0 15.5 %collective-permute-start.26 = (bf16[32,4096]{1,0:T(8,128)(2,1)S(1)}, bf16[32,4096]{1,0:T(8,128)(2,1)S(1)}, u32[]{:S(2)}, u32[]{:S(2)}) collective-permute-start(bf16[32,4096]{1,0:T(8,128)(2,1)S(1)} %fusion.1), channel_id=1, source_target_pairs={{0,4},{4,0},{8,12},{12,8},{1,5},{5,1},{9,13},{13,9},{2,6},{6,2},{1... | collective-permute-start | bytes 786440 | tf_op jit(solution)/shard_map/ppermute | solution.py:103
  74.5 11.0 %collective-permute-start.28 = (bf16[32,4096]{1,0:T(8,128)(2,1)S(1)}, bf16[32,4096]{1,0:T(8,128)(2,1)S(1)}, u32[]{:S(2)}, u32[]{:S(2)}) collective-permute-start(bf16[32,4096]{1,0:T(8,128)(2,1)S(1)} %add_convert_fusion), channel_id=1, source_target_pairs={{4,8},{8,4},{5,9},{9,5},{6,10},{10,6},{7,11},{11,7},{20,24},{24,20... | collective-permute-start | bytes 786440 | tf_op jit(solution)/shard_map/ppermute | solution.py:101
  75.3 15.2 %collective-permute-start.22 = (bf16[32,4096]{1,0:T(8,128)(2,1)S(1)}, bf16[32,4096]{1,0:T(8,128)(2,1)S(1)}, u32[]{:S(2)}, u32[]{:S(2)}) collective-permute-start(bf16[32,4096]{1,0:T(8,128)(2,1)S(1)} %fusion), channel_id=1, source_target_pairs={{0,4},{4,0},{8,12},{12,8},{1,5},{5,1},{9,13},{13,9},{2,6},{6,2},{1... | collective-permute-start | bytes 786440 | tf_op jit(solution)/shard_map/ppermute | solution.py:103
  80.1 10.4 %collective-permute-start.24 = (bf16[32,4096]{1,0:T(8,128)(2,1)S(1)}, bf16[32,4096]{1,0:T(8,128)(2,1)S(1)}, u32[]{:S(2)}, u32[]{:S(2)}) collective-permute-start(bf16[32,4096]{1,0:T(8,128)(2,1)S(1)} %add_convert_fusion.3), channel_id=1, source_target_pairs={{4,8},{8,4},{5,9},{9,5},{6,10},{10,6},{7,11},{11,7},{20,24},{24,20... | collective-permute-start | bytes 786440 | tf_op jit(solution)/shard_map/ppermute | solution.py:101
  (10 other events, 40.1 us)

commit v14 on v13

--- a/solution.py
+++ b/solution.py
@@ -38,6 +38,7 @@
     cuts = [block[:, :cut], block[:, cut:]]
     crossed = swap_bits(images, "reader", far_bit)
     near = swap_gather(images, "reader", near_bits)
+    near_routes = swap_gather(routes, "reader", near_bits)
     firsts = [
         lax.optimization_barrier(
             (lax.ppermute(one, "blk", SIDES), lax.ppermute(one, "blk", MIDDLE))
@@ -45,7 +46,7 @@
         for one in cuts
     ]
     early = stage(
-        [[[one] for one in cuts], [[side] for side, _ in firsts]], near, noise
+        [[[one] for one in cuts], [[side] for side, _ in firsts]], near, noise, near_routes
     )
     far_parts, end_parts = [], []
     for side, across in firsts:
@@ -55,24 +56,23 @@
         end = lax.ppermute(across_far, "blk", SIDES)
         far_parts.append([far, across_far])
         end_parts.append([end, across])
-    weighted, penalty, near, noise = early
-    weights = stage_rest([far_parts, end_parts], weighted, penalty, noise)
+    weighted, penalty, near, noise, routes = early
     ends = [parts[0] for parts in end_parts]
-    routes, crossed, *_ = lax.optimization_barrier((routes, crossed, *ends))
-    return weights, near, swap_gather(crossed, "reader", near_bits), swap_all(routes)
-
-
-def swap_all(routes):
-    return [routes] + [swap_bits(routes, "reader", k) for k in range(1, lax.axis_size("reader"))]
+    far_routes, crossed, *_ = lax.optimization_barrier((routes, crossed, *ends))
+    far_routes = swap_bits(far_routes, "reader", far_bit)
+    far = swap_gather(crossed, "reader", near_bits)
+    staged = stage_rest([far_parts, end_parts], near, crossed, weighted, penalty, noise)
+    return staged, far[1:], (routes, far_routes)
 
 
 def plain_gather(block, images, noise, routes, near_bits, far_bit):
     near = swap_gather(images, "reader", near_bits)
+    near_routes = swap_gather(routes, "reader", near_bits)
     far = swap_gather(swap_bits(images, "reader", far_bit), "reader", near_bits)
     line = [[[one]] for one in line_gather(block, "blk")]
-    weighted, penalty, near, noise = stage(line[:2], near, noise)
-    weights = stage_rest(line[2:], weighted, penalty, noise)
-    return weights, near, far, swap_all(routes)
+    weighted, penalty, near, noise, routes = stage(line[:2], near, noise, near_routes)
+    staged = stage_rest(line[2:], near, far[0], weighted, penalty, noise)
+    return staged, far[1:], (routes, swap_bits(routes, "reader", far_bit))
 
 
 def line_gather(block, axis):
@@ -225,8 +225,13 @@
     refs = list(refs)
     near_refs = [refs.pop(0) for _ in range(near_count)]
     groups = take_blocks(refs, counts)
-    noise_ref, weighted_ref, penalty_ref, near_ref, noise_out_ref, block_ref, near_sems, sems = refs
+    route_refs = [refs.pop(0) for _ in range(near_count)]
+    noise_ref, weighted_ref, penalty_ref, near_ref, noise_out_ref, route_ref = refs[:6]
+    block_ref, near_sems, sems = refs[6:]
     rows = near_refs[0].shape[0]
+    top = route_refs[0].shape[0]
+    for k, ref in enumerate(route_refs):
+        route_ref[k * top : (k + 1) * top, :] = ref[...]
     copies = []
     for k, ref in enumerate(near_refs):
         copy = pltpu.make_async_copy(ref, near_ref.at[pl.ds(k * rows, rows), :], near_sems.at[k])
@@ -238,11 +243,12 @@
         copy.wait()
 
 
-def stage(blocks, near, noise):
+def stage(blocks, near, noise, routes):
     count = blocks[0][0][0].shape[0]
     parts = sum(len(group) for group in blocks)
     width = noise.shape[1]
     refs = len(blocks) * count
+    rows = near[0].shape[0]
     moved = [*near, *flat(blocks)]
     return pl.pallas_call(
         partial(stage_kernel, len(near), block_counts(blocks)),
@@ -251,9 +257,10 @@
             jax.ShapeDtypeStruct((refs, 1), jnp.float32),
             jax.ShapeDtypeStruct((len(near) * near[0].shape[0], width), jnp.bfloat16),
             jax.ShapeDtypeStruct((1, width), jnp.float32),
-        ),
-        in_specs=[ANY_SPEC] * len(moved) + [VMEM_SPEC],
-        out_specs=(VMEM_SPEC,) * 4,
+            jax.ShapeDtypeStruct((len(routes) * routes[0].shape[0], rows), jnp.int32),
+        ),
+        in_specs=[ANY_SPEC] * len(moved) + [VMEM_SPEC] * (len(routes) + 1),
+        out_specs=(VMEM_SPEC,) * 5,
         scratch_shapes=[
             pltpu.VMEM((len(blocks), count, width), jnp.bfloat16),
             pltpu.SemaphoreType.DMA((len(near),)),
@@ -264,66 +271,98 @@
             flops=8 * refs * width, bytes_accessed=12_000_000, transcendentals=0
         ),
         name="stage",
-    )(*moved, noise)
-
-
-def stage_rest_kernel(counts, *refs):
+    )(*moved, *routes, noise)
+
+
+def place_images(k, source, all_ref, sem):
+    rows = source.shape[0]
+    row = pl.multiple_of((lax.axis_index("reader") ^ k) * rows, 16)
+    return pltpu.make_async_copy(source, all_ref.at[pl.ds(row, rows), :], sem), pl.ds(row, rows)
+
+
+def stage_rest_kernel(readers, counts, *refs):
     refs = list(refs)
     groups = take_blocks(refs, counts)
-    early_ref, early_penalty_ref, noise_ref, weighted_ref, penalty_ref, block_ref, sems = refs
+    near_ref, far_ref, early_ref, early_penalty_ref, noise_ref = [refs.pop(0) for _ in range(5)]
+    turned_ref, penalty_ref, all_ref, product_ref = refs[:4]
+    weighted_ref, block_ref, sems, image_sems = refs[4:]
+    rows = far_ref.shape[0]
+    half = readers // 2
+    sources = [near_ref.at[pl.ds(k * rows, rows), :] for k in range(half)] + [far_ref]
+    placed = [place_images(k, one, all_ref, image_sems.at[k]) for k, one in enumerate(sources)]
+    for copy, _ in placed:
+        copy.start()
     done = early_ref.shape[0]
     weighted_ref[:done, :] = early_ref[...]
     penalty_ref[:done, :] = early_penalty_ref[...]
     first = done // block_ref.shape[1]
     weigh_blocks(groups, noise_ref, weighted_ref, penalty_ref, block_ref, sems, first)
-
-
-def stage_rest(blocks, weighted, penalty, noise):
+    width = weighted_ref.shape[1]
+    for start in range(0, width, STEP):
+        piece = slice(start, min(start + STEP, width))
+        turned_ref[piece, :] = weighted_ref[:, piece].T
+    products = jnp.dot(near_ref[...], turned_ref[...], preferred_element_type=jnp.float32)
+    for k in range(half):
+        product_ref[placed[k][1], :] = products[k * rows : (k + 1) * rows]
+    product_ref[placed[half][1], :] = jnp.dot(
+        far_ref[...], turned_ref[...], preferred_element_type=jnp.float32
+    )
+    for copy, _ in placed:
+        copy.wait()
+
+
+def stage_rest(blocks, near, crossed, weighted, penalty, noise):
     count = blocks[0][0][0].shape[0]
     parts = sum(len(group) for group in blocks)
     width = noise.shape[1]
     refs = len(blocks) * count + weighted.shape[0]
+    slots = 2 * near.shape[0]
+    readers = slots // crossed.shape[0]
     moved = flat(blocks)
     return pl.pallas_call(
-        partial(stage_rest_kernel, block_counts(blocks)),
+        partial(stage_rest_kernel, readers, block_counts(blocks)),
         out_shape=(
-            jax.ShapeDtypeStruct((refs, width), jnp.bfloat16),
+            jax.ShapeDtypeStruct((width, refs), jnp.bfloat16),
             jax.ShapeDtypeStruct((refs, 1), jnp.float32),
-        ),
-        in_specs=[ANY_SPEC] * len(moved) + [VMEM_SPEC] * 3,
-        out_specs=(VMEM_SPEC,) * 2,
+            jax.ShapeDtypeStruct((slots, width), jnp.bfloat16),
+            jax.ShapeDtypeStruct((slots, refs), jnp.float32),
+        ),
+        in_specs=[ANY_SPEC] * len(moved) + [VMEM_SPEC] * 5,
+        out_specs=(VMEM_SPEC,) * 4,
         scratch_shapes=[
+            pltpu.VMEM((refs, width), jnp.bfloat16),
             pltpu.VMEM((len(blocks), count, width), jnp.bfloat16),
             pltpu.SemaphoreType.DMA((parts,)),
+            pltpu.SemaphoreType.DMA((readers // 2 + 1,)),
         ],
         compiler_params=pltpu.CompilerParams(vmem_limit_bytes=SCORE_VMEM),
         cost_estimate=pl.CostEstimate(
             flops=8 * refs * width, bytes_accessed=12_000_000, transcendentals=0
         ),
         name="stage_rest",
-    )(*moved, weighted, penalty, noise)
+    )(*moved, near, crossed, weighted, penalty, noise)
 
 
 def score_kernel(readers, finish, *refs):
     refs = list(refs)
-    near_ref = refs.pop(0)
-    rows = near_ref.shape[0] * 2 // readers
-    far_refs = [refs.pop(0) for _ in range(readers // 2)]
-    weighted_ref, penalty_ref = refs.pop(0), refs.pop(0)
-    route_refs = [refs.pop(0) for _ in range(readers)]
-    score_ref, mask_ref, lse_ref, all_ref, image_sems = refs
+    half = readers // 2
+    far_refs = [refs.pop(0) for _ in range(half - 1)]
+    turned_ref, penalty_ref, _, product_ref, near_route_ref, far_route_ref = refs[:6]
+    score_ref, mask_ref, lse_ref, all_ref, sum_ref, image_sems = refs[6:]
     reader = lax.axis_index("reader")
-    copies = []
-    for k in range(readers):
-        if k < readers // 2:
-            source = near_ref.at[pl.ds(k * rows, rows), :]
-        else:
-            source = far_refs[k - readers // 2]
-        row = pl.multiple_of((reader ^ k) * rows, 16)
-        copy = pltpu.make_async_copy(source, all_ref.at[pl.ds(row, rows), :], image_sems.at[k])
+    placed = [
+        place_images(half + 1 + i, ref, all_ref, image_sems.at[i])
+        for i, ref in enumerate(far_refs)
+    ]
+    for copy, _ in placed:
         copy.start()
-        copies.append(copy)
-    routes = [ref[...] for ref in route_refs]
+    sum_ref[...] = product_ref[...]
+    for (_, place), ref in zip(placed, far_refs):
+        sum_ref[place, :] = jnp.dot(
+            ref[...], turned_ref[...], preferred_element_type=jnp.float32
+        )
+    top, rows = near_route_ref.shape[0] // half, near_route_ref.shape[1]
+    routes = [ref[k * top : (k + 1) * top, :] for ref in (near_route_ref, far_route_ref) for k in range(half)]
     bit = 1
     while bit < readers:
         flip = (reader & bit) > 0
@@ -333,36 +372,34 @@
         for k in range(readers):
             hits = jnp.where(route == (reader ^ k), 1.0, 0.0)
             mask_ref[k : k + 1, j * rows : (j + 1) * rows] = jnp.max(hits, axis=0, keepdims=True)
-    for copy in copies:
-        copy.wait()
-    scores = lax.dot_general(
-        all_ref[...],
-        weighted_ref[...],
-        (((1,), (1,)), ((), ())),
-        preferred_element_type=jnp.float32,
-    )
-    scores = scores.T - penalty_ref[...]
+    scores = sum_ref[...].T - penalty_ref[...]
     score_ref[...] = scores
     if finish:
         lse_ref[...] = column_lse(scores)
-
-
-def all_scores(weights, near, far, routes, finish):
-    weighted, penalty = weights
-    refs, width = weighted.shape
-    slots = 2 * near.shape[0]
-    moved = [near, *far]
+    for copy, _ in placed:
+        copy.wait()
+
+
+def all_scores(staged, far, routes, finish):
+    turned, penalty, images, products = staged
+    width, refs = turned.shape
+    slots, rows = images.shape[0], far[0].shape[0]
+    readers = slots // rows
     return pl.pallas_call(
-        partial(score_kernel, len(routes), finish),
+        partial(score_kernel, readers, finish),
         out_shape=(
             jax.ShapeDtypeStruct((refs, slots), jnp.float32),
-            jax.ShapeDtypeStruct((len(routes), slots), jnp.float32),
+            jax.ShapeDtypeStruct((readers, slots), jnp.float32),
             jax.ShapeDtypeStruct((1, slots), jnp.float32),
             jax.ShapeDtypeStruct((slots, width), jnp.bfloat16),
         ),
-        in_specs=[ANY_SPEC] * len(moved) + [VMEM_SPEC] * (2 + len(routes)),
+        in_specs=[VMEM_SPEC] * (len(far) + 6),
         out_specs=(VMEM_SPEC,) * 4,
-        scratch_shapes=[pltpu.SemaphoreType.DMA((len(routes),))],
+        scratch_shapes=[
+            pltpu.VMEM((slots, refs), jnp.float32),
+            pltpu.SemaphoreType.DMA((len(far),)),
+        ],
+        input_output_aliases={len(far) + 2: 3},
         compiler_params=pltpu.CompilerParams(vmem_limit_bytes=SCORE_VMEM),
         cost_estimate=pl.CostEstimate(
             flops=2 * refs * slots * width,
@@ -370,7 +407,7 @@
             transcendentals=0,
         ),
         name="scores",
-    )(*moved, weighted, penalty, *routes)
+    )(*far, turned, penalty, images, products, *routes)
 
 
 def lse_kernel(score_ref, lse_ref):
@@ -443,11 +480,11 @@
     noise = noise_weights.reshape(1, width)
 
     gather = staged_gather if members == 4 and rows % 32 == 0 and readers > 1 else plain_gather
-    weights, near, far, route_blocks = gather(
+    staged, far, all_routes = gather(
         projections[0], images, noise, routes.T, readers // 4, readers // 2
     )
     split = lax.axis_size("sub") > 1
-    scores, masks, mine, all_images = all_scores(weights, near, far, route_blocks, not split)
+    scores, masks, mine, all_images = all_scores(staged, far, all_routes, not split)
     if split:
         scores = lax.psum(scores, "sub")
         mine = group_lse(scores)

time: 92.1 us -> 93 us (level)
  starting transfers between devices: 50.7 us -> 45.1 us
  waiting for transfers between devices: 25 us -> 30.5 us
    ppermute x2, waiting for transfers between devices: 2.87 us -> 6.12 us  [staged_gather(): end = lax.ppermute(across_far, 'blk', SIDES)]
    ppermute x2, starting transfers between devices: 7.26 us -> 5.23 us  [staged_gather(): end = lax.ppermute(across_far, 'blk', SIDES)]
    ppermute x2, starting transfers between devices: 5.51 us -> 3.84 us  [pair_scatter(): for_far_middle = [lax.ppermute(part, axis, SIDES) for part in second]]
    ppermute x9 -> x8, starting transfers between devices: 6.97 us -> 5.64 us  [swap_bits(): lax.ppermute(block, axis, [(i, i ^ bits) for i in range(lax.axis_size(axi...]
    ppermute x9 -> x8, waiting for transfers between devices: 7.38 us -> 7.74 us  [swap_bits(): lax.ppermute(block, axis, [(i, i ^ bits) for i in range(lax.axis_size(axi...]
  transfers between devices with their start and end apart: 29 -> 28, of which waited for: 10 -> 13; matrix products, arithmetic and copies ran while one was open for 3% -> 3% of each run, Pallas kernels for 3% -> 5%
where the time goes in v14:
time: 93 us; the launch traced here: 92.5 us
  starting transfers between devices  45.1 us (48%)
  waiting for transfers between devices  30.5 us (33%)
  local copies, waits for them, and re-layouts  8.15 us (9%)
  Pallas kernels  7.28 us (8%)
    ppermute x2, waiting for transfers between devices, pair_scatter(): from_side = lax.ppermute(near, axis, SIDES)  9.82 us
    ppermute x2, starting transfers between devices, pair_scatter(): from_side = lax.ppermute(near, axis, SIDES)  8.68 us
    ppermute x2, starting transfers between devices, staged_gather(): far = lax.ppermute(across, 'blk', SIDES)  8.09 us
    ppermute x8, waiting for transfers between devices, swap_bits(): lax.ppermute(block, axis, [(i, i ^ bits) for i in range(lax.axis_size(axi...  7.74 us
    ppermute x2, waiting for transfers between devices, staged_gather(): end = lax.ppermute(across_far, 'blk', SIDES)  6.12 us
    ppermute x2, starting transfers between devices, staged_gather(): lax.ppermute(one, 'blk', SIDES)  6.09 us
    ppermute x8, starting transfers between devices, swap_bits(): lax.ppermute(block, axis, [(i, i ^ bits) for i in range(lax.axis_size(axi...  5.64 us
    unnamed x10, local copies, waits for them, and re-layouts  5.63 us
  transfers between devices with their start and end apart: 28, of which 13 were waited for; matrix products, arithmetic and copies ran while one was open for 3% of the time, Pallas kernels for 5%

profile of v14, /device:TPU:0, one launch (start us, length us, event | category | flops | bytes accessed | tf_op | source)
XLA Modules:
  0.0 92.5 jit_solution(12379083496684489799)
XLA Ops:
  1.1 2.6 %collective-permute-start.10 = (bf16[96,8192]{1,0:T(8,128)(2,1)}, bf16[96,8192]{1,0:T(8,128)(2,1)S(1)}, u32[]{:S(2)}, u32[]{:S(2)}) collective-permute-start(bf16[96,8192]{1,0:T(8,128)(2,1)} %refs_0_.1), channel_id=1, source_target_pairs={{0,2},{1,3},{2,0},{3,1},{4,6},{5,7},{6,4},{7,5},{8,10},{9,11},{10,... | collective-permute-start | bytes 4718600 | tf_op jit(solution)/shard_map/ppermute | solution.py:20
  4.7 1.6 %collective-permute-start.4 = (bf16[32,4608]{1,0:T(8,128)(2,1)S(1)}, bf16[32,4608]{1,0:T(8,128)(2,1)S(1)}, u32[]{:S(2)}, u32[]{:S(2)}) collective-permute-start(bf16[32,4608]{1,0:T(8,128)(2,1)S(1)} %slice.9.refs_2_), channel_id=1, source_target_pairs={{0,4},{4,0},{8,12},{12,8},{1,5},{5,1},{9,13},{13,9},{2,6},{6,2},{1... | collective-permute-start | bytes 884744 | tf_op jit(solution)/shard_map/ppermute | solution.py:44
  8.0 4.4 %collective-permute-start = (bf16[32,3584]{1,0:T(8,128)(2,1)S(1)}, bf16[32,3584]{1,0:T(8,128)(2,1)S(1)}, u32[]{:S(2)}, u32[]{:S(2)}) collective-permute-start(bf16[32,3584]{1,0:T(8,128)(2,1)S(1)} %slice.8.refs_3_), channel_id=1, source_target_pairs={{0,4},{4,0},{8,12},{12,8},{1,5},{5,1},{9,13},{13,9},{2,6},{6,2},{1... | collective-permute-start | bytes 688136 | tf_op jit(solution)/shard_map/ppermute | solution.py:44
  12.4 2.2 %collective-permute-done.4.refs_4_ = bf16[32,4608]{1,0:T(8,128)(2,1)S(1)} collective-permute-done((bf16[32,4608]{1,0:T(8,128)(2,1)S(1)}, bf16[32,4608]{1,0:T(8,128)(2,1)S(1)}, u32[]{:S(2)}, u32[]{:S(2)}) %collective-permute-start.4) | collective-permute-done | bytes 294944 | tf_op jit(solution)/shard_map/ppermute | solution.py:44
  15.3 4.5 %collective-permute-start.6 = (bf16[32,4608]{1,0:T(8,128)(2,1)S(1)}, bf16[32,4608]{1,0:T(8,128)(2,1)S(1)}, u32[]{:S(2)}, u32[]{:S(2)}) collective-permute-start(bf16[32,4608]{1,0:T(8,128)(2,1)S(1)} %collective-permute-done.5.refs_5_), channel_id=1, source_target_pairs={{0,4},{4,0},{8,12},{12,8},{1,5},{5,1},{9,13},{13,9},{2,6},{6,2},{1... | collective-permute-start | bytes 884744 | tf_op jit(solution)/shard_map/ppermute | solution.py:53
  20.5 1.3 %collective-permute-done.9.refs_7_ = s32[2,96]{1,0:T(2,128)S(1)} collective-permute-done((s32[2,96]{1,0:T(2,128)}, s32[2,96]{1,0:T(2,128)S(1)}, u32[]{:S(2)}, u32[]{:S(2)}) %collective-permute-start.9) | collective-permute-done | bytes 800 | tf_op jit(solution)/shard_map/ppermute | solution.py:20
  21.9 3.6 %collective-permute-start.2 = (bf16[32,3584]{1,0:T(8,128)(2,1)S(1)}, bf16[32,3584]{1,0:T(8,128)(2,1)S(1)}, u32[]{:S(2)}, u32[]{:S(2)}) collective-permute-start(bf16[32,3584]{1,0:T(8,128)(2,1)S(1)} %collective-permute-done.1.refs_7_), channel_id=1, source_target_pairs={{0,4},{4,0},{8,12},{12,8},{1,5},{5,1},{9,13},{13,9},{2,6},{6,2},{1... | collective-permute-start | bytes 688136 | tf_op jit(solution)/shard_map/ppermute | solution.py:53
  26.2 1.4 %copy-done.2 = bf16[96,8192]{1,0:T(8,128)(2,1)S(1)} copy-done((bf16[96,8192]{1,0:T(8,128)(2,1)S(1)}, bf16[96,8192]{1,0:T(8,128)(2,1)}, u32[]{:S(2)}) %copy-start.2) | copy-done | bytes 1572888
  30.1 2.9 %collective-permute-start.11 = (bf16[32,4608]{1,0:T(8,128)(2,1)S(1)}, bf16[32,4608]{1,0:T(8,128)(2,1)S(1)}, u32[]{:S(2)}, u32[]{:S(2)}) collective-permute-start(bf16[32,4608]{1,0:T(8,128)(2,1)S(1)} %collective-permute-done.7.refs_1_), channel_id=1, source_target_pairs={{0,4},{4,0},{8,12},{12,8},{1,5},{5,1},{9,13},{13,9},{2,6},{6,2},{1... | collective-permute-start | bytes 884744 | tf_op jit(solution)/shard_map/ppermute | solution.py:56
  33.0 2.3 %collective-permute-start.12 = (bf16[32,3584]{1,0:T(8,128)(2,1)S(1)}, bf16[32,3584]{1,0:T(8,128)(2,1)S(1)}, u32[]{:S(2)}, u32[]{:S(2)}) collective-permute-start(bf16[32,3584]{1,0:T(8,128)(2,1)S(1)} %collective-permute-done.3.refs_3_), channel_id=1, source_target_pairs={{0,4},{4,0},{8,12},{12,8},{1,5},{5,1},{9,13},{13,9},{2,6},{6,2},{1... | collective-permute-start | bytes 688136 | tf_op jit(solution)/shard_map/ppermute | solution.py:56
  35.4 3.5 %collective-permute-done.10.refs_9_ = bf16[96,8192]{1,0:T(8,128)(2,1)S(1)} collective-permute-done((bf16[96,8192]{1,0:T(8,128)(2,1)}, bf16[96,8192]{1,0:T(8,128)(2,1)S(1)}, u32[]{:S(2)}, u32[]{:S(2)}) %collective-permute-start.10) | collective-permute-done | bytes 1572896 | tf_op jit(solution)/shard_map/ppermute | solution.py:20
  38.9 6.1 %collective-permute-done.12.refs_6_ = bf16[32,3584]{1,0:T(8,128)(2,1)S(1)} collective-permute-done((bf16[32,3584]{1,0:T(8,128)(2,1)S(1)}, bf16[32,3584]{1,0:T(8,128)(2,1)S(1)}, u32[]{:S(2)}, u32[]{:S(2)}) %collective-permute-start.12) | collective-permute-done | bytes 229408 | tf_op jit(solution)/shard_map/ppermute | solution.py:56
  45.6 2.8 %stage_rest.1 = (bf16[8192,128]{1,0:T(8,128)(2,1)S(1)}, f32[128,1]{1,0:T(8,128)S(1)}, bf16[384,8192]{1,0:T(8,128)(2,1)S(1)}, f32[384,128]{1,0:T(8,128)S(1)}) custom-call(bf16[32,4608]{1,0:T(8,128)(2,1)S(1)} %collective-permute-done.6.refs_0_, bf16[32,4608]{1,0:T(8,128)(2,1)S(1)} %collective-permute-done.7.refs_1_, ...), custom_call_target="tpu_custom_call" | custom-call | flops 8388608 | bytes 12000000 | tf_op jit(solution)/shard_map/stage_rest/pallas_call | solution.py:322
  49.7 1.5 %collective-permute-start.16 = (f32[1,384]{1,0:T(1,128)S(1)}, f32[1,384]{1,0:T(1,128)S(1)}, u32[]{:S(2)}, u32[]{:S(2)}) collective-permute-start(f32[1,384]{1,0:T(1,128)S(1)} %get-tuple-element.80.refs_0_), channel_id=1, source_target_pairs={{0,2},{1,3},{2,0},{3,1},{4,6},{5,7},{6,4},{7,5},{8,10},{9,11},{10,... | collective-permute-start | bytes 4616 | tf_op jit(solution)/shard_map/ppermute | solution.py:20
  51.5 1.8 %collective-permute-done.16.refs_2_ = f32[1,384]{1,0:T(1,128)S(1)} collective-permute-done((f32[1,384]{1,0:T(1,128)S(1)}, f32[1,384]{1,0:T(1,128)S(1)}, u32[]{:S(2)}, u32[]{:S(2)}) %collective-permute-start.16) | collective-permute-done | bytes 1568 | tf_op jit(solution)/shard_map/ppermute | solution.py:20
  54.9 1.8 %collective-permute-start.18 = (bf16[32,4096]{1,0:T(8,128)(2,1)S(1)}, bf16[32,4096]{1,0:T(8,128)(2,1)S(1)}, u32[]{:S(2)}, u32[]{:S(2)}) collective-permute-start(bf16[32,4096]{1,0:T(8,128)(2,1)S(1)} %get-tuple-element.86), channel_id=1, source_target_pairs={{0,4},{4,0},{8,12},{12,8},{1,5},{5,1},{9,13},{13,9},{2,6},{6,2},{1... | collective-permute-start | bytes 786440 | tf_op jit(solution)/shard_map/ppermute | solution.py:93
  56.7 2.8 %copy-done.1 = bf16[384,8192]{1,0:T(8,128)(2,1)S(1)} copy-done((bf16[384,8192]{1,0:T(8,128)(2,1)S(1)}, bf16[384,8192]{1,0:T(8,128)(2,1)}, u32[]{:S(2)}) %copy-start.1) | copy-done | bytes 6291480
  61.2 2.7 %collective-permute-done.18 = bf16[32,4096]{1,0:T(8,128)(2,1)S(1)} collective-permute-done((bf16[32,4096]{1,0:T(8,128)(2,1)S(1)}, bf16[32,4096]{1,0:T(8,128)(2,1)S(1)}, u32[]{:S(2)}, u32[]{:S(2)}) %collective-permute-start.18) | collective-permute-done | bytes 262176 | tf_op jit(solution)/shard_map/ppermute | solution.py:93
  63.8 2.0 %collective-permute-start.26 = (bf16[32,4096]{1,0:T(8,128)(2,1)S(1)}, bf16[32,4096]{1,0:T(8,128)(2,1)S(1)}, u32[]{:S(2)}, u32[]{:S(2)}) collective-permute-start(bf16[32,4096]{1,0:T(8,128)(2,1)S(1)} %get-tuple-element.91), channel_id=1, source_target_pairs={{0,4},{4,0},{8,12},{12,8},{1,5},{5,1},{9,13},{13,9},{2,6},{6,2},{1... | collective-permute-start | bytes 786440 | tf_op jit(solution)/shard_map/ppermute | solution.py:97
  66.6 1.8 %collective-permute-start.22 = (bf16[32,4096]{1,0:T(8,128)(2,1)S(1)}, bf16[32,4096]{1,0:T(8,128)(2,1)S(1)}, u32[]{:S(2)}, u32[]{:S(2)}) collective-permute-start(bf16[32,4096]{1,0:T(8,128)(2,1)S(1)} %get-tuple-element.87), channel_id=1, source_target_pairs={{0,4},{4,0},{8,12},{12,8},{1,5},{5,1},{9,13},{13,9},{2,6},{6,2},{1... | collective-permute-start | bytes 786440 | tf_op jit(solution)/shard_map/ppermute | solution.py:97
  70.3 4.3 %collective-permute-start.25 = (bf16[32,4096]{1,0:T(8,128)(2,1)S(1)}, bf16[32,4096]{1,0:T(8,128)(2,1)S(1)}, u32[]{:S(2)}, u32[]{:S(2)}) collective-permute-start(bf16[32,4096]{1,0:T(8,128)(2,1)S(1)} %fusion.1), channel_id=1, source_target_pairs={{0,4},{4,0},{8,12},{12,8},{1,5},{5,1},{9,13},{13,9},{2,6},{6,2},{1... | collective-permute-start | bytes 786440 | tf_op jit(solution)/shard_map/ppermute | solution.py:103
  76.0 4.3 %collective-permute-start.21 = (bf16[32,4096]{1,0:T(8,128)(2,1)S(1)}, bf16[32,4096]{1,0:T(8,128)(2,1)S(1)}, u32[]{:S(2)}, u32[]{:S(2)}) collective-permute-start(bf16[32,4096]{1,0:T(8,128)(2,1)S(1)} %fusion), channel_id=1, source_target_pairs={{0,4},{4,0},{8,12},{12,8},{1,5},{5,1},{9,13},{13,9},{2,6},{6,2},{1... | collective-permute-start | bytes 786440 | tf_op jit(solution)/shard_map/ppermute | solution.py:103
  81.5 4.9 %collective-permute-done.25 = bf16[32,4096]{1,0:T(8,128)(2,1)S(1)} collective-permute-done((bf16[32,4096]{1,0:T(8,128)(2,1)S(1)}, bf16[32,4096]{1,0:T(8,128)(2,1)S(1)}, u32[]{:S(2)}, u32[]{:S(2)}) %collective-permute-start.25) | collective-permute-done | bytes 262176 | tf_op jit(solution)/shard_map/ppermute | solution.py:103
  86.5 5.0 %collective-permute-done.21 = bf16[32,4096]{1,0:T(8,128)(2,1)S(1)} collective-permute-done((bf16[32,4096]{1,0:T(8,128)(2,1)S(1)}, bf16[32,4096]{1,0:T(8,128)(2,1)S(1)}, u32[]{:S(2)}, u32[]{:S(2)}) %collective-permute-start.21) | collective-permute-done | bytes 262176 | tf_op jit(solution)/shard_map/ppermute | solution.py:103
  (59 shorter events, 19.4 us)
Async XLA Ops:
  0.6 24.9 %collective-permute-start.8 = (bf16[96,8192]{1,0:T(8,128)(2,1)}, bf16[96,8192]{1,0:T(8,128)(2,1)S(1)}, u32[]{:S(2)}, u32[]{:S(2)}) collective-permute-start(bf16[96,8192]{1,0:T(8,128)(2,1)} %refs_0_.1), channel_id=1, source_target_pairs={{0,1},{1,0},{2,3},{3,2},{4,5},{5,4},{6,7},{7,6},{8,9},{9,8},{10,11... | collective-permute-start | bytes 4718600 | tf_op jit(solution)/shard_map/ppermute | solution.py:20
  1.1 37.8 %collective-permute-start.10 = (bf16[96,8192]{1,0:T(8,128)(2,1)}, bf16[96,8192]{1,0:T(8,128)(2,1)S(1)}, u32[]{:S(2)}, u32[]{:S(2)}) collective-permute-start(bf16[96,8192]{1,0:T(8,128)(2,1)} %refs_0_.1), channel_id=1, source_target_pairs={{0,2},{1,3},{2,0},{3,1},{4,6},{5,7},{6,4},{7,5},{8,10},{9,11},{10,... | collective-permute-start | bytes 4718600 | tf_op jit(solution)/shard_map/ppermute | solution.py:20
  4.7 9.9 %collective-permute-start.4 = (bf16[32,4608]{1,0:T(8,128)(2,1)S(1)}, bf16[32,4608]{1,0:T(8,128)(2,1)S(1)}, u32[]{:S(2)}, u32[]{:S(2)}) collective-permute-start(bf16[32,4608]{1,0:T(8,128)(2,1)S(1)} %slice.9.refs_2_), channel_id=1, source_target_pairs={{0,4},{4,0},{8,12},{12,8},{1,5},{5,1},{9,13},{13,9},{2,6},{6,2},{1... | collective-permute-start | bytes 884744 | tf_op jit(solution)/shard_map/ppermute | solution.py:44
  6.3 8.9 %collective-permute-start.5 = (bf16[32,4608]{1,0:T(8,128)(2,1)S(1)}, bf16[32,4608]{1,0:T(8,128)(2,1)S(1)}, u32[]{:S(2)}, u32[]{:S(2)}) collective-permute-start(bf16[32,4608]{1,0:T(8,128)(2,1)S(1)} %slice.9.refs_2_), channel_id=1, source_target_pairs={{4,8},{8,4},{5,9},{9,5},{6,10},{10,6},{7,11},{11,7},{20,24},{24,20... | collective-permute-start | bytes 884744 | tf_op jit(solution)/shard_map/ppermute | solution.py:44
  8.0 11.8 %collective-permute-start = (bf16[32,3584]{1,0:T(8,128)(2,1)S(1)}, bf16[32,3584]{1,0:T(8,128)(2,1)S(1)}, u32[]{:S(2)}, u32[]{:S(2)}) collective-permute-start(bf16[32,3584]{1,0:T(8,128)(2,1)S(1)} %slice.8.refs_3_), channel_id=1, source_target_pairs={{0,4},{4,0},{8,12},{12,8},{1,5},{5,1},{9,13},{13,9},{2,6},{6,2},{1... | collective-permute-start | bytes 688136 | tf_op jit(solution)/shard_map/ppermute | solution.py:44
  14.6 5.8 %collective-permute-start.1 = (bf16[32,3584]{1,0:T(8,128)(2,1)S(1)}, bf16[32,3584]{1,0:T(8,128)(2,1)S(1)}, u32[]{:S(2)}, u32[]{:S(2)}) collective-permute-start(bf16[32,3584]{1,0:T(8,128)(2,1)S(1)} %slice.8.refs_3_), channel_id=1, source_target_pairs={{4,8},{8,4},{5,9},{9,5},{6,10},{10,6},{7,11},{11,7},{20,24},{24,20... | collective-permute-start | bytes 688136 | tf_op jit(solution)/shard_map/ppermute | solution.py:44
  15.3 14.8 %collective-permute-start.6 = (bf16[32,4608]{1,0:T(8,128)(2,1)S(1)}, bf16[32,4608]{1,0:T(8,128)(2,1)S(1)}, u32[]{:S(2)}, u32[]{:S(2)}) collective-permute-start(bf16[32,4608]{1,0:T(8,128)(2,1)S(1)} %collective-permute-done.5.refs_5_), channel_id=1, source_target_pairs={{0,4},{4,0},{8,12},{12,8},{1,5},{5,1},{9,13},{13,9},{2,6},{6,2},{1... | collective-permute-start | bytes 884744 | tf_op jit(solution)/shard_map/ppermute | solution.py:53
  19.8 10.4 %collective-permute-start.7 = (bf16[32,4608]{1,0:T(8,128)(2,1)S(1)}, bf16[32,4608]{1,0:T(8,128)(2,1)S(1)}, u32[]{:S(2)}, u32[]{:S(2)}) collective-permute-start(bf16[32,4608]{1,0:T(8,128)(2,1)S(1)} %collective-permute-done.4.refs_4_), channel_id=1, source_target_pairs={{4,8},{8,4},{5,9},{9,5},{6,10},{10,6},{7,11},{11,7},{20,24},{24,20... | collective-permute-start | bytes 884744 | tf_op jit(solution)/shard_map/ppermute | solution.py:54
  21.9 11.2 %collective-permute-start.2 = (bf16[32,3584]{1,0:T(8,128)(2,1)S(1)}, bf16[32,3584]{1,0:T(8,128)(2,1)S(1)}, u32[]{:S(2)}, u32[]{:S(2)}) collective-permute-start(bf16[32,3584]{1,0:T(8,128)(2,1)S(1)} %collective-permute-done.1.refs_7_), channel_id=1, source_target_pairs={{0,4},{4,0},{8,12},{12,8},{1,5},{5,1},{9,13},{13,9},{2,6},{6,2},{1... | collective-permute-start | bytes 688136 | tf_op jit(solution)/shard_map/ppermute | solution.py:53
  25.5 7.5 %collective-permute-start.3 = (bf16[32,3584]{1,0:T(8,128)(2,1)S(1)}, bf16[32,3584]{1,0:T(8,128)(2,1)S(1)}, u32[]{:S(2)}, u32[]{:S(2)}) collective-permute-start(bf16[32,3584]{1,0:T(8,128)(2,1)S(1)} %collective-permute-done.refs_5_), channel_id=1, source_target_pairs={{4,8},{8,4},{5,9},{9,5},{6,10},{10,6},{7,11},{11,7},{20,24},{24,20... | collective-permute-start | bytes 688136 | tf_op jit(solution)/shard_map/ppermute | solution.py:54
  30.1 14.9 %collective-permute-start.11 = (bf16[32,4608]{1,0:T(8,128)(2,1)S(1)}, bf16[32,4608]{1,0:T(8,128)(2,1)S(1)}, u32[]{:S(2)}, u32[]{:S(2)}) collective-permute-start(bf16[32,4608]{1,0:T(8,128)(2,1)S(1)} %collective-permute-done.7.refs_1_), channel_id=1, source_target_pairs={{0,4},{4,0},{8,12},{12,8},{1,5},{5,1},{9,13},{13,9},{2,6},{6,2},{1... | collective-permute-start | bytes 884744 | tf_op jit(solution)/shard_map/ppermute | solution.py:56
  33.0 12.0 %collective-permute-start.12 = (bf16[32,3584]{1,0:T(8,128)(2,1)S(1)}, bf16[32,3584]{1,0:T(8,128)(2,1)S(1)}, u32[]{:S(2)}, u32[]{:S(2)}) collective-permute-start(bf16[32,3584]{1,0:T(8,128)(2,1)S(1)} %collective-permute-done.3.refs_3_), channel_id=1, source_target_pairs={{0,4},{4,0},{8,12},{12,8},{1,5},{5,1},{9,13},{13,9},{2,6},{6,2},{1... | collective-permute-start | bytes 688136 | tf_op jit(solution)/shard_map/ppermute | solution.py:56
  45.0 3.6 %collective-permute-start.13 = (bf16[96,8192]{1,0:T(8,128)(2,1)S(1)}, bf16[96,8192]{1,0:T(8,128)(2,1)S(1)}, u32[]{:S(2)}, u32[]{:S(2)}) collective-permute-start(bf16[96,8192]{1,0:T(8,128)(2,1)S(1)} %collective-permute-done.10.refs_9_), channel_id=1, source_target_pairs={{0,1},{1,0},{2,3},{3,2},{4,5},{5,4},{6,7},{7,6},{8,9},{9,8},{10,11... | collective-permute-start | bytes 4718600 | tf_op jit(solution)/shard_map/ppermute | solution.py:20
  49.7 3.6 %collective-permute-start.16 = (f32[1,384]{1,0:T(1,128)S(1)}, f32[1,384]{1,0:T(1,128)S(1)}, u32[]{:S(2)}, u32[]{:S(2)}) collective-permute-start(f32[1,384]{1,0:T(1,128)S(1)} %get-tuple-element.80.refs_0_), channel_id=1, source_target_pairs={{0,2},{1,3},{2,0},{3,1},{4,6},{5,7},{6,4},{7,5},{8,10},{9,11},{10,... | collective-permute-start | bytes 4616 | tf_op jit(solution)/shard_map/ppermute | solution.py:20
  54.9 8.9 %collective-permute-start.18 = (bf16[32,4096]{1,0:T(8,128)(2,1)S(1)}, bf16[32,4096]{1,0:T(8,128)(2,1)S(1)}, u32[]{:S(2)}, u32[]{:S(2)}) collective-permute-start(bf16[32,4096]{1,0:T(8,128)(2,1)S(1)} %get-tuple-element.86), channel_id=1, source_target_pairs={{0,4},{4,0},{8,12},{12,8},{1,5},{5,1},{9,13},{13,9},{2,6},{6,2},{1... | collective-permute-start | bytes 786440 | tf_op jit(solution)/shard_map/ppermute | solution.py:93
  60.2 9.3 %collective-permute-start.19 = (bf16[32,4096]{1,0:T(8,128)(2,1)S(1)}, bf16[32,4096]{1,0:T(8,128)(2,1)S(1)}, u32[]{:S(2)}, u32[]{:S(2)}) collective-permute-start(bf16[32,4096]{1,0:T(8,128)(2,1)S(1)} %get-tuple-element.88), channel_id=1, source_target_pairs={{0,4},{4,0},{8,12},{12,8},{1,5},{5,1},{9,13},{13,9},{2,6},{6,2},{1... | collective-permute-start | bytes 786440 | tf_op jit(solution)/shard_map/ppermute | solution.py:93
  63.8 11.3 %collective-permute-start.26 = (bf16[32,4096]{1,0:T(8,128)(2,1)S(1)}, bf16[32,4096]{1,0:T(8,128)(2,1)S(1)}, u32[]{:S(2)}, u32[]{:S(2)}) collective-permute-start(bf16[32,4096]{1,0:T(8,128)(2,1)S(1)} %get-tuple-element.91), channel_id=1, source_target_pairs={{0,4},{4,0},{8,12},{12,8},{1,5},{5,1},{9,13},{13,9},{2,6},{6,2},{1... | collective-permute-start | bytes 786440 | tf_op jit(solution)/shard_map/ppermute | solution.py:97
  65.9 4.3 %collective-permute-start.24 = (bf16[32,4096]{1,0:T(8,128)(2,1)S(1)}, bf16[32,4096]{1,0:T(8,128)(2,1)S(1)}, u32[]{:S(2)}, u32[]{:S(2)}) collective-permute-start(bf16[32,4096]{1,0:T(8,128)(2,1)S(1)} %add_convert_fusion.2), channel_id=1, source_target_pairs={{4,8},{8,4},{5,9},{9,5},{6,10},{10,6},{7,11},{11,7},{20,24},{24,20... | collective-permute-start | bytes 786440 | tf_op jit(solution)/shard_map/ppermute | solution.py:100
  66.6 14.1 %collective-permute-start.22 = (bf16[32,4096]{1,0:T(8,128)(2,1)S(1)}, bf16[32,4096]{1,0:T(8,128)(2,1)S(1)}, u32[]{:S(2)}, u32[]{:S(2)}) collective-permute-start(bf16[32,4096]{1,0:T(8,128)(2,1)S(1)} %get-tuple-element.87), channel_id=1, source_target_pairs={{0,4},{4,0},{8,12},{12,8},{1,5},{5,1},{9,13},{13,9},{2,6},{6,2},{1... | collective-permute-start | bytes 786440 | tf_op jit(solution)/shard_map/ppermute | solution.py:97
  69.6 6.3 %collective-permute-start.20 = (bf16[32,4096]{1,0:T(8,128)(2,1)S(1)}, bf16[32,4096]{1,0:T(8,128)(2,1)S(1)}, u32[]{:S(2)}, u32[]{:S(2)}) collective-permute-start(bf16[32,4096]{1,0:T(8,128)(2,1)S(1)} %add_convert_fusion.5), channel_id=1, source_target_pairs={{4,8},{8,4},{5,9},{9,5},{6,10},{10,6},{7,11},{11,7},{20,24},{24,20... | collective-permute-start | bytes 786440 | tf_op jit(solution)/shard_map/ppermute | solution.py:100
  70.3 16.0 %collective-permute-start.25 = (bf16[32,4096]{1,0:T(8,128)(2,1)S(1)}, bf16[32,4096]{1,0:T(8,128)(2,1)S(1)}, u32[]{:S(2)}, u32[]{:S(2)}) collective-permute-start(bf16[32,4096]{1,0:T(8,128)(2,1)S(1)} %fusion.1), channel_id=1, source_target_pairs={{0,4},{4,0},{8,12},{12,8},{1,5},{5,1},{9,13},{13,9},{2,6},{6,2},{1... | collective-permute-start | bytes 786440 | tf_op jit(solution)/shard_map/ppermute | solution.py:103
  75.2 11.2 %collective-permute-start.27 = (bf16[32,4096]{1,0:T(8,128)(2,1)S(1)}, bf16[32,4096]{1,0:T(8,128)(2,1)S(1)}, u32[]{:S(2)}, u32[]{:S(2)}) collective-permute-start(bf16[32,4096]{1,0:T(8,128)(2,1)S(1)} %add_convert_fusion), channel_id=1, source_target_pairs={{4,8},{8,4},{5,9},{9,5},{6,10},{10,6},{7,11},{11,7},{20,24},{24,20... | collective-permute-start | bytes 786440 | tf_op jit(solution)/shard_map/ppermute | solution.py:101
  76.0 15.5 %collective-permute-start.21 = (bf16[32,4096]{1,0:T(8,128)(2,1)S(1)}, bf16[32,4096]{1,0:T(8,128)(2,1)S(1)}, u32[]{:S(2)}, u32[]{:S(2)}) collective-permute-start(bf16[32,4096]{1,0:T(8,128)(2,1)S(1)} %fusion), channel_id=1, source_target_pairs={{0,4},{4,0},{8,12},{12,8},{1,5},{5,1},{9,13},{13,9},{2,6},{6,2},{1... | collective-permute-start | bytes 786440 | tf_op jit(solution)/shard_map/ppermute | solution.py:103
  80.8 10.6 %collective-permute-start.23 = (bf16[32,4096]{1,0:T(8,128)(2,1)S(1)}, bf16[32,4096]{1,0:T(8,128)(2,1)S(1)}, u32[]{:S(2)}, u32[]{:S(2)}) collective-permute-start(bf16[32,4096]{1,0:T(8,128)(2,1)S(1)} %add_convert_fusion.3), channel_id=1, source_target_pairs={{4,8},{8,4},{5,9},{9,5},{6,10},{10,6},{7,11},{11,7},{20,24},{24,20... | collective-permute-start | bytes 786440 | tf_op jit(solution)/shard_map/ppermute | solution.py:101
  (9 other events, 21.0 us)

commit v15 on v14

--- a/solution.py
+++ b/solution.py
@@ -38,7 +38,6 @@
     cuts = [block[:, :cut], block[:, cut:]]
     crossed = swap_bits(images, "reader", far_bit)
     near = swap_gather(images, "reader", near_bits)
-    near_routes = swap_gather(routes, "reader", near_bits)
     firsts = [
         lax.optimization_barrier(
             (lax.ppermute(one, "blk", SIDES), lax.ppermute(one, "blk", MIDDLE))
@@ -46,33 +45,36 @@
         for one in cuts
     ]
     early = stage(
-        [[[one] for one in cuts], [[side] for side, _ in firsts]], near, noise, near_routes
+        [[[one] for one in cuts], [[side] for side, _ in firsts]], near, noise
     )
     far_parts, end_parts = [], []
     for side, across in firsts:
         far = lax.ppermute(across, "blk", SIDES)
+        side, *_ = lax.optimization_barrier((side, *near))
         across_far = lax.ppermute(side, "blk", MIDDLE)
         far, across_far, *early = lax.optimization_barrier((far, across_far, *early))
         end = lax.ppermute(across_far, "blk", SIDES)
         far_parts.append([far, across_far])
         end_parts.append([end, across])
-    weighted, penalty, near, noise, routes = early
+    weighted, penalty, staged_near, noise = early
     ends = [parts[0] for parts in end_parts]
-    far_routes, crossed, *_ = lax.optimization_barrier((routes, crossed, *ends))
-    far_routes = swap_bits(far_routes, "reader", far_bit)
+    routes, crossed, *_ = lax.optimization_barrier((routes, crossed, *ends))
     far = swap_gather(crossed, "reader", near_bits)
-    staged = stage_rest([far_parts, end_parts], near, crossed, weighted, penalty, noise)
-    return staged, far[1:], (routes, far_routes)
+    staged = stage_rest([far_parts, end_parts], staged_near, crossed, weighted, penalty, noise)
+    return staged, far[1:], swap_all(routes)
+
+
+def swap_all(routes):
+    return [routes] + [swap_bits(routes, "reader", k) for k in range(1, lax.axis_size("reader"))]
 
 
 def plain_gather(block, images, noise, routes, near_bits, far_bit):
     near = swap_gather(images, "reader", near_bits)
-    near_routes = swap_gather(routes, "reader", near_bits)
     far = swap_gather(swap_bits(images, "reader", far_bit), "reader", near_bits)
     line = [[[one]] for one in line_gather(block, "blk")]
-    weighted, penalty, near, noise, routes = stage(line[:2], near, noise, near_routes)
+    weighted, penalty, near, noise = stage(line[:2], near, noise)
     staged = stage_rest(line[2:], near, far[0], weighted, penalty, noise)
-    return staged, far[1:], (routes, swap_bits(routes, "reader", far_bit))
+    return staged, far[1:], swap_all(routes)
 
 
 def line_gather(block, axis):
@@ -225,13 +227,8 @@
     refs = list(refs)
     near_refs = [refs.pop(0) for _ in range(near_count)]
     groups = take_blocks(refs, counts)
-    route_refs = [refs.pop(0) for _ in range(near_count)]
-    noise_ref, weighted_ref, penalty_ref, near_ref, noise_out_ref, route_ref = refs[:6]
-    block_ref, near_sems, sems = refs[6:]
+    noise_ref, weighted_ref, penalty_ref, near_ref, noise_out_ref, block_ref, near_sems, sems = refs
     rows = near_refs[0].shape[0]
-    top = route_refs[0].shape[0]
-    for k, ref in enumerate(route_refs):
-        route_ref[k * top : (k + 1) * top, :] = ref[...]
     copies = []
     for k, ref in enumerate(near_refs):
         copy = pltpu.make_async_copy(ref, near_ref.at[pl.ds(k * rows, rows), :], near_sems.at[k])
@@ -243,12 +240,11 @@
         copy.wait()
 
 
-def stage(blocks, near, noise, routes):
+def stage(blocks, near, noise):
     count = blocks[0][0][0].shape[0]
     parts = sum(len(group) for group in blocks)
     width = noise.shape[1]
     refs = len(blocks) * count
-    rows = near[0].shape[0]
     moved = [*near, *flat(blocks)]
     return pl.pallas_call(
         partial(stage_kernel, len(near), block_counts(blocks)),
@@ -257,10 +253,9 @@
             jax.ShapeDtypeStruct((refs, 1), jnp.float32),
             jax.ShapeDtypeStruct((len(near) * near[0].shape[0], width), jnp.bfloat16),
             jax.ShapeDtypeStruct((1, width), jnp.float32),
-            jax.ShapeDtypeStruct((len(routes) * routes[0].shape[0], rows), jnp.int32),
-        ),
-        in_specs=[ANY_SPEC] * len(moved) + [VMEM_SPEC] * (len(routes) + 1),
-        out_specs=(VMEM_SPEC,) * 5,
+        ),
+        in_specs=[ANY_SPEC] * len(moved) + [VMEM_SPEC],
+        out_specs=(VMEM_SPEC,) * 4,
         scratch_shapes=[
             pltpu.VMEM((len(blocks), count, width), jnp.bfloat16),
             pltpu.SemaphoreType.DMA((len(near),)),
@@ -271,7 +266,7 @@
             flops=8 * refs * width, bytes_accessed=12_000_000, transcendentals=0
         ),
         name="stage",
-    )(*moved, *routes, noise)
+    )(*moved, noise)
 
 
 def place_images(k, source, all_ref, sem):
@@ -347,8 +342,9 @@
     refs = list(refs)
     half = readers // 2
     far_refs = [refs.pop(0) for _ in range(half - 1)]
-    turned_ref, penalty_ref, _, product_ref, near_route_ref, far_route_ref = refs[:6]
-    score_ref, mask_ref, lse_ref, all_ref, sum_ref, image_sems = refs[6:]
+    turned_ref, penalty_ref, _, product_ref = [refs.pop(0) for _ in range(4)]
+    route_refs = [refs.pop(0) for _ in range(readers)]
+    score_ref, mask_ref, lse_ref, all_ref, sum_ref, image_sems = refs
     reader = lax.axis_index("reader")
     placed = [
         place_images(half + 1 + i, ref, all_ref, image_sems.at[i])
@@ -361,8 +357,8 @@
         sum_ref[place, :] = jnp.dot(
             ref[...], turned_ref[...], preferred_element_type=jnp.float32
         )
-    top, rows = near_route_ref.shape[0] // half, near_route_ref.shape[1]
-    routes = [ref[k * top : (k + 1) * top, :] for ref in (near_route_ref, far_route_ref) for k in range(half)]
+    rows = route_refs[0].shape[1]
+    routes = [ref[...] for ref in route_refs]
     bit = 1
     while bit < readers:
         flip = (reader & bit) > 0
@@ -393,7 +389,7 @@
             jax.ShapeDtypeStruct((1, slots), jnp.float32),
             jax.ShapeDtypeStruct((slots, width), jnp.bfloat16),
         ),
-        in_specs=[VMEM_SPEC] * (len(far) + 6),
+        in_specs=[VMEM_SPEC] * (len(far) + 4 + len(routes)),
         out_specs=(VMEM_SPEC,) * 4,
         scratch_shapes=[
             pltpu.VMEM((slots, refs), jnp.float32),

time: 93 us -> 91.7 us (0.986)
  waiting for transfers between devices: 30.5 us -> 25.4 us
  starting transfers between devices: 45.1 us -> 49.6 us
    ppermute x2, waiting for transfers between devices: 6.12 us -> 3.83 us  [staged_gather(): end = lax.ppermute(across_far, 'blk', SIDES)]
    ppermute x8 -> x9, waiting for transfers between devices: 7.74 us -> 5.69 us  [swap_bits(): lax.ppermute(block, axis, [(i, i ^ bits) for i in range(lax.axis_size(axi...]
    ppermute x2, starting transfers between devices: 8.09 us -> 9.77 us  [staged_gather(): far = lax.ppermute(across, 'blk', SIDES)]
    ppermute x8 -> x9, starting transfers between devices: 5.64 us -> 7.23 us  [swap_bits(): lax.ppermute(block, axis, [(i, i ^ bits) for i in range(lax.axis_size(axi...]
  transfers between devices with their start and end apart: 28 -> 29, of which waited for: 13 -> 10; matrix products, arithmetic and copies ran while one was open for 3% -> 3% of each run, Pallas kernels for 5% -> 5%
where the time goes in v15:
time: 91.7 us; the launch traced here: 91.2 us
  starting transfers between devices  49.6 us (54%)
  waiting for transfers between devices  25.4 us (28%)
  local copies, waits for them, and re-layouts  7.47 us (8%)
  Pallas kernels  7.24 us (8%)
  between operations  0.92 us (1%)
    ppermute x2, waiting for transfers between devices, pair_scatter(): from_side = lax.ppermute(near, axis, SIDES)  9.8 us
    ppermute x2, starting transfers between devices, staged_gather(): far = lax.ppermute(across, 'blk', SIDES)  9.77 us
    ppermute x2, starting transfers between devices, pair_scatter(): from_side = lax.ppermute(near, axis, SIDES)  8.81 us
    ppermute x9, starting transfers between devices, swap_bits(): lax.ppermute(block, axis, [(i, i ^ bits) for i in range(lax.axis_size(axi...  7.23 us
    ppermute x2, starting transfers between devices, staged_gather(): lax.ppermute(one, 'blk', SIDES)  6.09 us
    ppermute x9, waiting for transfers between devices, swap_bits(): lax.ppermute(block, axis, [(i, i ^ bits) for i in range(lax.axis_size(axi...  5.69 us
    ppermute x2, starting transfers between devices, staged_gather(): end = lax.ppermute(across_far, 'blk', SIDES)  5.65 us
    unnamed x10, local copies, waits for them, and re-layouts  4.95 us
  transfers between devices with their start and end apart: 29, of which 10 were waited for; matrix products, arithmetic and copies ran while one was open for 3% of the time, Pallas kernels for 5%

profile of v15, /device:TPU:0, one launch (start us, length us, event | category | flops | bytes accessed | tf_op | source)
XLA Modules:
  0.0 91.2 jit_solution(16932621604208384816)
XLA Ops:
  1.1 2.6 %collective-permute-start = (bf16[96,8192]{1,0:T(8,128)(2,1)}, bf16[96,8192]{1,0:T(8,128)(2,1)S(1)}, u32[]{:S(2)}, u32[]{:S(2)}) collective-permute-start(bf16[96,8192]{1,0:T(8,128)(2,1)} %refs_0_.1), channel_id=1, source_target_pairs={{0,2},{1,3},{2,0},{3,1},{4,6},{5,7},{6,4},{7,5},{8,10},{9,11},{10,... | collective-permute-start | bytes 4718600 | tf_op jit(solution)/shard_map/ppermute | solution.py:20
  4.7 1.6 %collective-permute-start.1 = (bf16[32,4608]{1,0:T(8,128)(2,1)S(1)}, bf16[32,4608]{1,0:T(8,128)(2,1)S(1)}, u32[]{:S(2)}, u32[]{:S(2)}) collective-permute-start(bf16[32,4608]{1,0:T(8,128)(2,1)S(1)} %slice.8.refs_2_), channel_id=1, source_target_pairs={{0,4},{4,0},{8,12},{12,8},{1,5},{5,1},{9,13},{13,9},{2,6},{6,2},{1... | collective-permute-start | bytes 884744 | tf_op jit(solution)/shard_map/ppermute | solution.py:43
  8.0 4.4 %collective-permute-start.6 = (bf16[32,3584]{1,0:T(8,128)(2,1)S(1)}, bf16[32,3584]{1,0:T(8,128)(2,1)S(1)}, u32[]{:S(2)}, u32[]{:S(2)}) collective-permute-start(bf16[32,3584]{1,0:T(8,128)(2,1)S(1)} %slice.9.refs_3_), channel_id=1, source_target_pairs={{0,4},{4,0},{8,12},{12,8},{1,5},{5,1},{9,13},{13,9},{2,6},{6,2},{1... | collective-permute-start | bytes 688136 | tf_op jit(solution)/shard_map/ppermute | solution.py:43
  12.4 2.2 %collective-permute-done.1.refs_4_ = bf16[32,4608]{1,0:T(8,128)(2,1)S(1)} collective-permute-done((bf16[32,4608]{1,0:T(8,128)(2,1)S(1)}, bf16[32,4608]{1,0:T(8,128)(2,1)S(1)}, u32[]{:S(2)}, u32[]{:S(2)}) %collective-permute-start.1) | collective-permute-done | bytes 294944 | tf_op jit(solution)/shard_map/ppermute | solution.py:43
  15.3 4.5 %collective-permute-start.3 = (bf16[32,4608]{1,0:T(8,128)(2,1)S(1)}, bf16[32,4608]{1,0:T(8,128)(2,1)S(1)}, u32[]{:S(2)}, u32[]{:S(2)}) collective-permute-start(bf16[32,4608]{1,0:T(8,128)(2,1)S(1)} %collective-permute-done.2.refs_5_), channel_id=1, source_target_pairs={{0,4},{4,0},{8,12},{12,8},{1,5},{5,1},{9,13},{13,9},{2,6},{6,2},{1... | collective-permute-start | bytes 884744 | tf_op jit(solution)/shard_map/ppermute | solution.py:52
  20.4 5.3 %collective-permute-start.9 = (bf16[32,3584]{1,0:T(8,128)(2,1)S(1)}, bf16[32,3584]{1,0:T(8,128)(2,1)S(1)}, u32[]{:S(2)}, u32[]{:S(2)}) collective-permute-start(bf16[32,3584]{1,0:T(8,128)(2,1)S(1)} %collective-permute-done.7.refs_7_), channel_id=1, source_target_pairs={{0,4},{4,0},{8,12},{12,8},{1,5},{5,1},{9,13},{13,9},{2,6},{6,2},{1... | collective-permute-start | bytes 688136 | tf_op jit(solution)/shard_map/ppermute | solution.py:52
  26.4 1.4 %copy-done.2 = bf16[96,8192]{1,0:T(8,128)(2,1)S(1)} copy-done((bf16[96,8192]{1,0:T(8,128)(2,1)S(1)}, bf16[96,8192]{1,0:T(8,128)(2,1)}, u32[]{:S(2)}) %copy-start.2) | copy-done | bytes 1572888
  28.6 1.1 %stage.1 = (bf16[64,8192]{1,0:T(8,128)(2,1)S(1)}, f32[64,1]{1,0:T(8,128)S(1)}, bf16[192,8192]{1,0:T(8,128)(2,1)S(1)}, f32[1,8192]{1,0:T(1,128)S(1)}) custom-call(bf16[96,8192]{1,0:T(8,128)(2,1)S(1)} %copy-done.2, bf16[96,8192]{1,0:T(8,128)(2,1)S(1)} %collective-permute-done.4.refs_1_, bf16[32,4608]{1,0:T(8,128)(2,1)S(1)} %slice.8.refs_2_, ...), custom_call_target="tpu_custom_call" | custom-call | flops 4194304 | bytes 12000000 | tf_op jit(solution)/shard_map/stage/pallas_call | solution.py:249
  29.7 3.4 %collective-permute-start.8 = (bf16[32,4608]{1,0:T(8,128)(2,1)S(1)}, bf16[32,4608]{1,0:T(8,128)(2,1)S(1)}, u32[]{:S(2)}, u32[]{:S(2)}) collective-permute-start(bf16[32,4608]{1,0:T(8,128)(2,1)S(1)} %collective-permute-done.5.refs_1_), channel_id=1, source_target_pairs={{0,4},{4,0},{8,12},{12,8},{1,5},{5,1},{9,13},{13,9},{2,6},{6,2},{1... | collective-permute-start | bytes 884744 | tf_op jit(solution)/shard_map/ppermute | solution.py:56
  33.1 2.3 %collective-permute-start.11 = (bf16[32,3584]{1,0:T(8,128)(2,1)S(1)}, bf16[32,3584]{1,0:T(8,128)(2,1)S(1)}, u32[]{:S(2)}, u32[]{:S(2)}) collective-permute-start(bf16[32,3584]{1,0:T(8,128)(2,1)S(1)} %collective-permute-done.10.refs_3_), channel_id=1, source_target_pairs={{0,4},{4,0},{8,12},{12,8},{1,5},{5,1},{9,13},{13,9},{2,6},{6,2},{1... | collective-permute-start | bytes 688136 | tf_op jit(solution)/shard_map/ppermute | solution.py:56
  35.4 3.5 %collective-permute-done.refs_9_ = bf16[96,8192]{1,0:T(8,128)(2,1)S(1)} collective-permute-done((bf16[96,8192]{1,0:T(8,128)(2,1)}, bf16[96,8192]{1,0:T(8,128)(2,1)S(1)}, u32[]{:S(2)}, u32[]{:S(2)}) %collective-permute-start) | collective-permute-done | bytes 1572896 | tf_op jit(solution)/shard_map/ppermute | solution.py:20
  38.9 3.8 %collective-permute-done.11.refs_6_ = bf16[32,3584]{1,0:T(8,128)(2,1)S(1)} collective-permute-done((bf16[32,3584]{1,0:T(8,128)(2,1)S(1)}, bf16[32,3584]{1,0:T(8,128)(2,1)S(1)}, u32[]{:S(2)}, u32[]{:S(2)}) %collective-permute-start.11) | collective-permute-done | bytes 229408 | tf_op jit(solution)/shard_map/ppermute | solution.py:56
  44.7 2.8 %stage_rest.1 = (bf16[8192,128]{1,0:T(8,128)(2,1)S(1)}, f32[128,1]{1,0:T(8,128)S(1)}, bf16[384,8192]{1,0:T(8,128)(2,1)S(1)}, f32[384,128]{1,0:T(8,128)S(1)}) custom-call(bf16[32,4608]{1,0:T(8,128)(2,1)S(1)} %collective-permute-done.3.refs_0_, bf16[32,4608]{1,0:T(8,128)(2,1)S(1)} %collective-permute-done.5.refs_1_, ...), custom_call_target="tpu_custom_call" | custom-call | flops 8388608 | bytes 12000000 | tf_op jit(solution)/shard_map/stage_rest/pallas_call | solution.py:317
  50.7 2.1 %collective-permute-done.17.refs_2_ = f32[1,384]{1,0:T(1,128)S(1)} collective-permute-done((f32[1,384]{1,0:T(1,128)S(1)}, f32[1,384]{1,0:T(1,128)S(1)}, u32[]{:S(2)}, u32[]{:S(2)}) %collective-permute-start.17) | collective-permute-done | bytes 1568 | tf_op jit(solution)/shard_map/ppermute | solution.py:20
  53.6 1.9 %collective-permute-start.19 = (bf16[32,4096]{1,0:T(8,128)(2,1)S(1)}, bf16[32,4096]{1,0:T(8,128)(2,1)S(1)}, u32[]{:S(2)}, u32[]{:S(2)}) collective-permute-start(bf16[32,4096]{1,0:T(8,128)(2,1)S(1)} %get-tuple-element.84), channel_id=1, source_target_pairs={{0,4},{4,0},{8,12},{12,8},{1,5},{5,1},{9,13},{13,9},{2,6},{6,2},{1... | collective-permute-start | bytes 786440 | tf_op jit(solution)/shard_map/ppermute | solution.py:95
  55.5 2.8 %copy-done.1 = bf16[384,8192]{1,0:T(8,128)(2,1)S(1)} copy-done((bf16[384,8192]{1,0:T(8,128)(2,1)S(1)}, bf16[384,8192]{1,0:T(8,128)(2,1)}, u32[]{:S(2)}) %copy-start.1) | copy-done | bytes 6291480
  59.8 2.7 %collective-permute-done.19 = bf16[32,4096]{1,0:T(8,128)(2,1)S(1)} collective-permute-done((bf16[32,4096]{1,0:T(8,128)(2,1)S(1)}, bf16[32,4096]{1,0:T(8,128)(2,1)S(1)}, u32[]{:S(2)}, u32[]{:S(2)}) %collective-permute-start.19) | collective-permute-done | bytes 262176 | tf_op jit(solution)/shard_map/ppermute | solution.py:95
  62.5 2.1 %collective-permute-start.27 = (bf16[32,4096]{1,0:T(8,128)(2,1)S(1)}, bf16[32,4096]{1,0:T(8,128)(2,1)S(1)}, u32[]{:S(2)}, u32[]{:S(2)}) collective-permute-start(bf16[32,4096]{1,0:T(8,128)(2,1)S(1)} %get-tuple-element.89), channel_id=1, source_target_pairs={{0,4},{4,0},{8,12},{12,8},{1,5},{5,1},{9,13},{13,9},{2,6},{6,2},{1... | collective-permute-start | bytes 786440 | tf_op jit(solution)/shard_map/ppermute | solution.py:99
  65.4 2.4 %collective-permute-start.23 = (bf16[32,4096]{1,0:T(8,128)(2,1)S(1)}, bf16[32,4096]{1,0:T(8,128)(2,1)S(1)}, u32[]{:S(2)}, u32[]{:S(2)}) collective-permute-start(bf16[32,4096]{1,0:T(8,128)(2,1)S(1)} %get-tuple-element.85), channel_id=1, source_target_pairs={{0,4},{4,0},{8,12},{12,8},{1,5},{5,1},{9,13},{13,9},{2,6},{6,2},{1... | collective-permute-start | bytes 786440 | tf_op jit(solution)/shard_map/ppermute | solution.py:99
  69.1 4.4 %collective-permute-start.26 = (bf16[32,4096]{1,0:T(8,128)(2,1)S(1)}, bf16[32,4096]{1,0:T(8,128)(2,1)S(1)}, u32[]{:S(2)}, u32[]{:S(2)}) collective-permute-start(bf16[32,4096]{1,0:T(8,128)(2,1)S(1)} %fusion.1), channel_id=1, source_target_pairs={{0,4},{4,0},{8,12},{12,8},{1,5},{5,1},{9,13},{13,9},{2,6},{6,2},{1... | collective-permute-start | bytes 786440 | tf_op jit(solution)/shard_map/ppermute | solution.py:105
  74.7 4.4 %collective-permute-start.22 = (bf16[32,4096]{1,0:T(8,128)(2,1)S(1)}, bf16[32,4096]{1,0:T(8,128)(2,1)S(1)}, u32[]{:S(2)}, u32[]{:S(2)}) collective-permute-start(bf16[32,4096]{1,0:T(8,128)(2,1)S(1)} %fusion), channel_id=1, source_target_pairs={{0,4},{4,0},{8,12},{12,8},{1,5},{5,1},{9,13},{13,9},{2,6},{6,2},{1... | collective-permute-start | bytes 786440 | tf_op jit(solution)/shard_map/ppermute | solution.py:105
  80.2 4.9 %collective-permute-done.26 = bf16[32,4096]{1,0:T(8,128)(2,1)S(1)} collective-permute-done((bf16[32,4096]{1,0:T(8,128)(2,1)S(1)}, bf16[32,4096]{1,0:T(8,128)(2,1)S(1)}, u32[]{:S(2)}, u32[]{:S(2)}) %collective-permute-start.26) | collective-permute-done | bytes 262176 | tf_op jit(solution)/shard_map/ppermute | solution.py:105
  85.2 4.9 %collective-permute-done.22 = bf16[32,4096]{1,0:T(8,128)(2,1)S(1)} collective-permute-done((bf16[32,4096]{1,0:T(8,128)(2,1)S(1)}, bf16[32,4096]{1,0:T(8,128)(2,1)S(1)}, u32[]{:S(2)}, u32[]{:S(2)}) %collective-permute-start.22) | collective-permute-done | bytes 262176 | tf_op jit(solution)/shard_map/ppermute | solution.py:105
  90.2 1.0 %beside.1 = f32[32,8192]{1,0:T(8,128)} custom-call(f32[32,4096]{1,0:T(8,128)S(1)} %select_add_fusion.1.refs_0_, f32[32,4096]{1,0:T(8,128)S(1)} %select_add_fusion.refs_1_), custom_call_target="tpu_custom_call" | custom-call | tf_op jit(solution)/shard_map/beside/pallas_call | solution.py:125
  (61 shorter events, 17.8 us)
Async XLA Ops:
  0.6 19.1 %collective-permute-start.4 = (bf16[96,8192]{1,0:T(8,128)(2,1)}, bf16[96,8192]{1,0:T(8,128)(2,1)S(1)}, u32[]{:S(2)}, u32[]{:S(2)}) collective-permute-start(bf16[96,8192]{1,0:T(8,128)(2,1)} %refs_0_.1), channel_id=1, source_target_pairs={{0,1},{1,0},{2,3},{3,2},{4,5},{5,4},{6,7},{7,6},{8,9},{9,8},{10,11... | collective-permute-start | bytes 4718600 | tf_op jit(solution)/shard_map/ppermute | solution.py:20
  1.1 37.8 %collective-permute-start = (bf16[96,8192]{1,0:T(8,128)(2,1)}, bf16[96,8192]{1,0:T(8,128)(2,1)S(1)}, u32[]{:S(2)}, u32[]{:S(2)}) collective-permute-start(bf16[96,8192]{1,0:T(8,128)(2,1)} %refs_0_.1), channel_id=1, source_target_pairs={{0,2},{1,3},{2,0},{3,1},{4,6},{5,7},{6,4},{7,5},{8,10},{9,11},{10,... | collective-permute-start | bytes 4718600 | tf_op jit(solution)/shard_map/ppermute | solution.py:20
  4.7 9.9 %collective-permute-start.1 = (bf16[32,4608]{1,0:T(8,128)(2,1)S(1)}, bf16[32,4608]{1,0:T(8,128)(2,1)S(1)}, u32[]{:S(2)}, u32[]{:S(2)}) collective-permute-start(bf16[32,4608]{1,0:T(8,128)(2,1)S(1)} %slice.8.refs_2_), channel_id=1, source_target_pairs={{0,4},{4,0},{8,12},{12,8},{1,5},{5,1},{9,13},{13,9},{2,6},{6,2},{1... | collective-permute-start | bytes 884744 | tf_op jit(solution)/shard_map/ppermute | solution.py:43
  6.3 8.9 %collective-permute-start.2 = (bf16[32,4608]{1,0:T(8,128)(2,1)S(1)}, bf16[32,4608]{1,0:T(8,128)(2,1)S(1)}, u32[]{:S(2)}, u32[]{:S(2)}) collective-permute-start(bf16[32,4608]{1,0:T(8,128)(2,1)S(1)} %slice.8.refs_2_), channel_id=1, source_target_pairs={{4,8},{8,4},{5,9},{9,5},{6,10},{10,6},{7,11},{11,7},{20,24},{24,20... | collective-permute-start | bytes 884744 | tf_op jit(solution)/shard_map/ppermute | solution.py:43
  8.0 12.5 %collective-permute-start.6 = (bf16[32,3584]{1,0:T(8,128)(2,1)S(1)}, bf16[32,3584]{1,0:T(8,128)(2,1)S(1)}, u32[]{:S(2)}, u32[]{:S(2)}) collective-permute-start(bf16[32,3584]{1,0:T(8,128)(2,1)S(1)} %slice.9.refs_3_), channel_id=1, source_target_pairs={{0,4},{4,0},{8,12},{12,8},{1,5},{5,1},{9,13},{13,9},{2,6},{6,2},{1... | collective-permute-start | bytes 688136 | tf_op jit(solution)/shard_map/ppermute | solution.py:43
  14.6 5.8 %collective-permute-start.7 = (bf16[32,3584]{1,0:T(8,128)(2,1)S(1)}, bf16[32,3584]{1,0:T(8,128)(2,1)S(1)}, u32[]{:S(2)}, u32[]{:S(2)}) collective-permute-start(bf16[32,3584]{1,0:T(8,128)(2,1)S(1)} %slice.9.refs_3_), channel_id=1, source_target_pairs={{4,8},{8,4},{5,9},{9,5},{6,10},{10,6},{7,11},{11,7},{20,24},{24,20... | collective-permute-start | bytes 688136 | tf_op jit(solution)/shard_map/ppermute | solution.py:43
  15.3 14.4 %collective-permute-start.3 = (bf16[32,4608]{1,0:T(8,128)(2,1)S(1)}, bf16[32,4608]{1,0:T(8,128)(2,1)S(1)}, u32[]{:S(2)}, u32[]{:S(2)}) collective-permute-start(bf16[32,4608]{1,0:T(8,128)(2,1)S(1)} %collective-permute-done.2.refs_5_), channel_id=1, source_target_pairs={{0,4},{4,0},{8,12},{12,8},{1,5},{5,1},{9,13},{13,9},{2,6},{6,2},{1... | collective-permute-start | bytes 884744 | tf_op jit(solution)/shard_map/ppermute | solution.py:52
  19.8 10.0 %collective-permute-start.5 = (bf16[32,4608]{1,0:T(8,128)(2,1)S(1)}, bf16[32,4608]{1,0:T(8,128)(2,1)S(1)}, u32[]{:S(2)}, u32[]{:S(2)}) collective-permute-start(bf16[32,4608]{1,0:T(8,128)(2,1)S(1)} %collective-permute-done.1.refs_4_), channel_id=1, source_target_pairs={{4,8},{8,4},{5,9},{9,5},{6,10},{10,6},{7,11},{11,7},{20,24},{24,20... | collective-permute-start | bytes 884744 | tf_op jit(solution)/shard_map/ppermute | solution.py:54
  20.4 12.7 %collective-permute-start.9 = (bf16[32,3584]{1,0:T(8,128)(2,1)S(1)}, bf16[32,3584]{1,0:T(8,128)(2,1)S(1)}, u32[]{:S(2)}, u32[]{:S(2)}) collective-permute-start(bf16[32,3584]{1,0:T(8,128)(2,1)S(1)} %collective-permute-done.7.refs_7_), channel_id=1, source_target_pairs={{0,4},{4,0},{8,12},{12,8},{1,5},{5,1},{9,13},{13,9},{2,6},{6,2},{1... | collective-permute-start | bytes 688136 | tf_op jit(solution)/shard_map/ppermute | solution.py:52
  25.8 7.4 %collective-permute-start.10 = (bf16[32,3584]{1,0:T(8,128)(2,1)S(1)}, bf16[32,3584]{1,0:T(8,128)(2,1)S(1)}, u32[]{:S(2)}, u32[]{:S(2)}) collective-permute-start(bf16[32,3584]{1,0:T(8,128)(2,1)S(1)} %collective-permute-done.6.refs_5_), channel_id=1, source_target_pairs={{4,8},{8,4},{5,9},{9,5},{6,10},{10,6},{7,11},{11,7},{20,24},{24,20... | collective-permute-start | bytes 688136 | tf_op jit(solution)/shard_map/ppermute | solution.py:54
  29.7 13.0 %collective-permute-start.8 = (bf16[32,4608]{1,0:T(8,128)(2,1)S(1)}, bf16[32,4608]{1,0:T(8,128)(2,1)S(1)}, u32[]{:S(2)}, u32[]{:S(2)}) collective-permute-start(bf16[32,4608]{1,0:T(8,128)(2,1)S(1)} %collective-permute-done.5.refs_1_), channel_id=1, source_target_pairs={{0,4},{4,0},{8,12},{12,8},{1,5},{5,1},{9,13},{13,9},{2,6},{6,2},{1... | collective-permute-start | bytes 884744 | tf_op jit(solution)/shard_map/ppermute | solution.py:56
  33.1 9.6 %collective-permute-start.11 = (bf16[32,3584]{1,0:T(8,128)(2,1)S(1)}, bf16[32,3584]{1,0:T(8,128)(2,1)S(1)}, u32[]{:S(2)}, u32[]{:S(2)}) collective-permute-start(bf16[32,3584]{1,0:T(8,128)(2,1)S(1)} %collective-permute-done.10.refs_3_), channel_id=1, source_target_pairs={{0,4},{4,0},{8,12},{12,8},{1,5},{5,1},{9,13},{13,9},{2,6},{6,2},{1... | collective-permute-start | bytes 688136 | tf_op jit(solution)/shard_map/ppermute | solution.py:56
  42.7 4.8 %collective-permute-start.12 = (bf16[96,8192]{1,0:T(8,128)(2,1)S(1)}, bf16[96,8192]{1,0:T(8,128)(2,1)S(1)}, u32[]{:S(2)}, u32[]{:S(2)}) collective-permute-start(bf16[96,8192]{1,0:T(8,128)(2,1)S(1)} %collective-permute-done.refs_9_), channel_id=1, source_target_pairs={{0,1},{1,0},{2,3},{3,2},{4,5},{5,4},{6,7},{7,6},{8,9},{9,8},{10,11... | collective-permute-start | bytes 4718600 | tf_op jit(solution)/shard_map/ppermute | solution.py:20
  42.7 4.8 %collective-permute-start.13 = (s32[2,96]{1,0:T(2,128)S(1)}, s32[2,96]{1,0:T(2,128)S(1)}, u32[]{:S(2)}, u32[]{:S(2)}) collective-permute-start(s32[2,96]{1,0:T(2,128)S(1)} %bitcast.7), channel_id=1, source_target_pairs={{0,1},{1,0},{2,3},{3,2},{4,5},{5,4},{6,7},{7,6},{8,9},{9,8},{10,11... | collective-permute-start | bytes 2312 | tf_op jit(solution)/shard_map/ppermute | solution.py:20
  53.6 9.0 %collective-permute-start.19 = (bf16[32,4096]{1,0:T(8,128)(2,1)S(1)}, bf16[32,4096]{1,0:T(8,128)(2,1)S(1)}, u32[]{:S(2)}, u32[]{:S(2)}) collective-permute-start(bf16[32,4096]{1,0:T(8,128)(2,1)S(1)} %get-tuple-element.84), channel_id=1, source_target_pairs={{0,4},{4,0},{8,12},{12,8},{1,5},{5,1},{9,13},{13,9},{2,6},{6,2},{1... | collective-permute-start | bytes 786440 | tf_op jit(solution)/shard_map/ppermute | solution.py:95
  59.0 9.3 %collective-permute-start.20 = (bf16[32,4096]{1,0:T(8,128)(2,1)S(1)}, bf16[32,4096]{1,0:T(8,128)(2,1)S(1)}, u32[]{:S(2)}, u32[]{:S(2)}) collective-permute-start(bf16[32,4096]{1,0:T(8,128)(2,1)S(1)} %get-tuple-element.86), channel_id=1, source_target_pairs={{0,4},{4,0},{8,12},{12,8},{1,5},{5,1},{9,13},{13,9},{2,6},{6,2},{1... | collective-permute-start | bytes 786440 | tf_op jit(solution)/shard_map/ppermute | solution.py:95
  62.5 11.3 %collective-permute-start.27 = (bf16[32,4096]{1,0:T(8,128)(2,1)S(1)}, bf16[32,4096]{1,0:T(8,128)(2,1)S(1)}, u32[]{:S(2)}, u32[]{:S(2)}) collective-permute-start(bf16[32,4096]{1,0:T(8,128)(2,1)S(1)} %get-tuple-element.89), channel_id=1, source_target_pairs={{0,4},{4,0},{8,12},{12,8},{1,5},{5,1},{9,13},{13,9},{2,6},{6,2},{1... | collective-permute-start | bytes 786440 | tf_op jit(solution)/shard_map/ppermute | solution.py:99
  64.7 4.3 %collective-permute-start.25 = (bf16[32,4096]{1,0:T(8,128)(2,1)S(1)}, bf16[32,4096]{1,0:T(8,128)(2,1)S(1)}, u32[]{:S(2)}, u32[]{:S(2)}) collective-permute-start(bf16[32,4096]{1,0:T(8,128)(2,1)S(1)} %add_convert_fusion.2), channel_id=1, source_target_pairs={{4,8},{8,4},{5,9},{9,5},{6,10},{10,6},{7,11},{11,7},{20,24},{24,20... | collective-permute-start | bytes 786440 | tf_op jit(solution)/shard_map/ppermute | solution.py:102
  65.4 14.1 %collective-permute-start.23 = (bf16[32,4096]{1,0:T(8,128)(2,1)S(1)}, bf16[32,4096]{1,0:T(8,128)(2,1)S(1)}, u32[]{:S(2)}, u32[]{:S(2)}) collective-permute-start(bf16[32,4096]{1,0:T(8,128)(2,1)S(1)} %get-tuple-element.85), channel_id=1, source_target_pairs={{0,4},{4,0},{8,12},{12,8},{1,5},{5,1},{9,13},{13,9},{2,6},{6,2},{1... | collective-permute-start | bytes 786440 | tf_op jit(solution)/shard_map/ppermute | solution.py:99
  68.3 6.3 %collective-permute-start.21 = (bf16[32,4096]{1,0:T(8,128)(2,1)S(1)}, bf16[32,4096]{1,0:T(8,128)(2,1)S(1)}, u32[]{:S(2)}, u32[]{:S(2)}) collective-permute-start(bf16[32,4096]{1,0:T(8,128)(2,1)S(1)} %add_convert_fusion.5), channel_id=1, source_target_pairs={{4,8},{8,4},{5,9},{9,5},{6,10},{10,6},{7,11},{11,7},{20,24},{24,20... | collective-permute-start | bytes 786440 | tf_op jit(solution)/shard_map/ppermute | solution.py:102
  69.1 16.0 %collective-permute-start.26 = (bf16[32,4096]{1,0:T(8,128)(2,1)S(1)}, bf16[32,4096]{1,0:T(8,128)(2,1)S(1)}, u32[]{:S(2)}, u32[]{:S(2)}) collective-permute-start(bf16[32,4096]{1,0:T(8,128)(2,1)S(1)} %fusion.1), channel_id=1, source_target_pairs={{0,4},{4,0},{8,12},{12,8},{1,5},{5,1},{9,13},{13,9},{2,6},{6,2},{1... | collective-permute-start | bytes 786440 | tf_op jit(solution)/shard_map/ppermute | solution.py:105
  73.9 11.2 %collective-permute-start.28 = (bf16[32,4096]{1,0:T(8,128)(2,1)S(1)}, bf16[32,4096]{1,0:T(8,128)(2,1)S(1)}, u32[]{:S(2)}, u32[]{:S(2)}) collective-permute-start(bf16[32,4096]{1,0:T(8,128)(2,1)S(1)} %add_convert_fusion), channel_id=1, source_target_pairs={{4,8},{8,4},{5,9},{9,5},{6,10},{10,6},{7,11},{11,7},{20,24},{24,20... | collective-permute-start | bytes 786440 | tf_op jit(solution)/shard_map/ppermute | solution.py:103
  74.7 15.4 %collective-permute-start.22 = (bf16[32,4096]{1,0:T(8,128)(2,1)S(1)}, bf16[32,4096]{1,0:T(8,128)(2,1)S(1)}, u32[]{:S(2)}, u32[]{:S(2)}) collective-permute-start(bf16[32,4096]{1,0:T(8,128)(2,1)S(1)} %fusion), channel_id=1, source_target_pairs={{0,4},{4,0},{8,12},{12,8},{1,5},{5,1},{9,13},{13,9},{2,6},{6,2},{1... | collective-permute-start | bytes 786440 | tf_op jit(solution)/shard_map/ppermute | solution.py:105
  79.5 10.6 %collective-permute-start.24 = (bf16[32,4096]{1,0:T(8,128)(2,1)S(1)}, bf16[32,4096]{1,0:T(8,128)(2,1)S(1)}, u32[]{:S(2)}, u32[]{:S(2)}) collective-permute-start(bf16[32,4096]{1,0:T(8,128)(2,1)S(1)} %add_convert_fusion.3), channel_id=1, source_target_pairs={{4,8},{8,4},{5,9},{9,5},{6,10},{10,6},{7,11},{11,7},{20,24},{24,20... | collective-permute-start | bytes 786440 | tf_op jit(solution)/shard_map/ppermute | solution.py:103
  (10 other events, 41.1 us)

commit v16 on v15

--- a/solution.py
+++ b/solution.py
@@ -48,20 +48,26 @@
         [[[one] for one in cuts], [[side] for side, _ in firsts]], near, noise
     )
     far_parts, end_parts = [], []
-    for side, across in firsts:
+    for last, (side, across) in enumerate(firsts):
         far = lax.ppermute(across, "blk", SIDES)
         side, *_ = lax.optimization_barrier((side, *near))
         across_far = lax.ppermute(side, "blk", MIDDLE)
-        far, across_far, *early = lax.optimization_barrier((far, across_far, *early))
+        if last:
+            far, across_far, *early = lax.optimization_barrier((far, across_far, *early))
+        else:
+            far, across_far = lax.optimization_barrier((far, across_far))
         end = lax.ppermute(across_far, "blk", SIDES)
         far_parts.append([far, across_far])
         end_parts.append([end, across])
     weighted, penalty, staged_near, noise = early
     ends = [parts[0] for parts in end_parts]
-    routes, crossed, *_ = lax.optimization_barrier((routes, crossed, *ends))
+    routes, crossed = lax.optimization_barrier((routes, crossed))
+    routes = swap_all(routes)
+    crossed, *rest = lax.optimization_barrier((crossed, *routes, *ends))
+    routes = rest[: len(routes)]
     far = swap_gather(crossed, "reader", near_bits)
     staged = stage_rest([far_parts, end_parts], staged_near, crossed, weighted, penalty, noise)
-    return staged, far[1:], swap_all(routes)
+    return staged, far[1:], routes
 
 
 def swap_all(routes):

time: 91.7 us -> 90.7 us (0.989)
  waiting for transfers between devices: 25.4 us -> 23.1 us
  starting transfers between devices: 49.6 us -> 50.9 us
    ppermute x2, waiting for transfers between devices: 3.83 us -> 0.01 us  [staged_gather(): end = lax.ppermute(across_far, 'blk', SIDES)]
    ppermute x9, waiting for transfers between devices: 5.69 us -> 8.6 us  [swap_bits(): lax.ppermute(block, axis, [(i, i ^ bits) for i in range(lax.axis_size(axi...]
    ppermute x2, starting transfers between devices: 4.5 us -> 6.19 us  [pair_scatter(): for_far_middle = [lax.ppermute(part, axis, SIDES) for part in second]]
    ppermute x2, waiting for transfers between devices: 9.8 us -> 8.23 us  [pair_scatter(): from_side = lax.ppermute(near, axis, SIDES)]
    ppermute x2, waiting for transfers between devices: 0.01 us -> 1.23 us  [staged_gather(): far = lax.ppermute(across, 'blk', SIDES)]
    ppermute x2, starting transfers between devices: 5.65 us -> 4.49 us  [staged_gather(): end = lax.ppermute(across_far, 'blk', SIDES)]
where the time goes in v16:
time: 90.7 us; the launch traced here: 90.2 us
  starting transfers between devices  50.9 us (56%)
  waiting for transfers between devices  23.1 us (25%)
  local copies, waits for them, and re-layouts  7.48 us (8%)
  Pallas kernels  7.23 us (8%)
    ppermute x2, starting transfers between devices, staged_gather(): far = lax.ppermute(across, 'blk', SIDES)  9.77 us
    ppermute x2, starting transfers between devices, pair_scatter(): from_side = lax.ppermute(near, axis, SIDES)  9.65 us
    ppermute x9, waiting for transfers between devices, swap_bits(): lax.ppermute(block, axis, [(i, i ^ bits) for i in range(lax.axis_size(axi...  8.6 us
    ppermute x2, waiting for transfers between devices, pair_scatter(): from_side = lax.ppermute(near, axis, SIDES)  8.23 us
    ppermute x9, starting transfers between devices, swap_bits(): lax.ppermute(block, axis, [(i, i ^ bits) for i in range(lax.axis_size(axi...  7.14 us
    ppermute x2, starting transfers between devices, pair_scatter(): for_far_middle = [lax.ppermute(part, axis, SIDES) for part in second]  6.19 us
    ppermute x2, starting transfers between devices, staged_gather(): lax.ppermute(one, 'blk', SIDES)  6.09 us
    unnamed x10, local copies, waits for them, and re-layouts  4.96 us
  transfers between devices with their start and end apart: 29, of which 10 were waited for; matrix products, arithmetic and copies ran while one was open for 3% of the time, Pallas kernels for 5%

profile of v16, /device:TPU:0, one launch (start us, length us, event | category | flops | bytes accessed | tf_op | source)
XLA Modules:
  0.0 90.2 jit_solution(6213110747945985214)
XLA Ops:
  1.1 2.6 %collective-permute-start = (bf16[96,8192]{1,0:T(8,128)(2,1)}, bf16[96,8192]{1,0:T(8,128)(2,1)S(1)}, u32[]{:S(2)}, u32[]{:S(2)}) collective-permute-start(bf16[96,8192]{1,0:T(8,128)(2,1)} %refs_0_.1), channel_id=1, source_target_pairs={{0,2},{1,3},{2,0},{3,1},{4,6},{5,7},{6,4},{7,5},{8,10},{9,11},{10,... | collective-permute-start | bytes 4718600 | tf_op jit(solution)/shard_map/ppermute | solution.py:20
  4.7 1.6 %collective-permute-start.4 = (bf16[32,4608]{1,0:T(8,128)(2,1)S(1)}, bf16[32,4608]{1,0:T(8,128)(2,1)S(1)}, u32[]{:S(2)}, u32[]{:S(2)}) collective-permute-start(bf16[32,4608]{1,0:T(8,128)(2,1)S(1)} %slice.8.refs_2_), channel_id=1, source_target_pairs={{0,4},{4,0},{8,12},{12,8},{1,5},{5,1},{9,13},{13,9},{2,6},{6,2},{1... | collective-permute-start | bytes 884744 | tf_op jit(solution)/shard_map/ppermute | solution.py:43
  8.0 4.4 %collective-permute-start.10 = (bf16[32,3584]{1,0:T(8,128)(2,1)S(1)}, bf16[32,3584]{1,0:T(8,128)(2,1)S(1)}, u32[]{:S(2)}, u32[]{:S(2)}) collective-permute-start(bf16[32,3584]{1,0:T(8,128)(2,1)S(1)} %slice.9.refs_3_), channel_id=1, source_target_pairs={{0,4},{4,0},{8,12},{12,8},{1,5},{5,1},{9,13},{13,9},{2,6},{6,2},{1... | collective-permute-start | bytes 688136 | tf_op jit(solution)/shard_map/ppermute | solution.py:43
  12.4 2.2 %collective-permute-done.4.refs_4_ = bf16[32,4608]{1,0:T(8,128)(2,1)S(1)} collective-permute-done((bf16[32,4608]{1,0:T(8,128)(2,1)S(1)}, bf16[32,4608]{1,0:T(8,128)(2,1)S(1)}, u32[]{:S(2)}, u32[]{:S(2)}) %collective-permute-start.4) | collective-permute-done | bytes 294944 | tf_op jit(solution)/shard_map/ppermute | solution.py:43
  15.3 4.5 %collective-permute-start.6 = (bf16[32,4608]{1,0:T(8,128)(2,1)S(1)}, bf16[32,4608]{1,0:T(8,128)(2,1)S(1)}, u32[]{:S(2)}, u32[]{:S(2)}) collective-permute-start(bf16[32,4608]{1,0:T(8,128)(2,1)S(1)} %collective-permute-done.5.refs_5_), channel_id=1, source_target_pairs={{0,4},{4,0},{8,12},{12,8},{1,5},{5,1},{9,13},{13,9},{2,6},{6,2},{1... | collective-permute-start | bytes 884744 | tf_op jit(solution)/shard_map/ppermute | solution.py:52
  20.4 5.3 %collective-permute-start.12 = (bf16[32,3584]{1,0:T(8,128)(2,1)S(1)}, bf16[32,3584]{1,0:T(8,128)(2,1)S(1)}, u32[]{:S(2)}, u32[]{:S(2)}) collective-permute-start(bf16[32,3584]{1,0:T(8,128)(2,1)S(1)} %collective-permute-done.11.refs_7_), channel_id=1, source_target_pairs={{0,4},{4,0},{8,12},{12,8},{1,5},{5,1},{9,13},{13,9},{2,6},{6,2},{1... | collective-permute-start | bytes 688136 | tf_op jit(solution)/shard_map/ppermute | solution.py:52
  26.4 1.2 %collective-permute-done.6.refs_0_ = bf16[32,4608]{1,0:T(8,128)(2,1)S(1)} collective-permute-done((bf16[32,4608]{1,0:T(8,128)(2,1)S(1)}, bf16[32,4608]{1,0:T(8,128)(2,1)S(1)}, u32[]{:S(2)}, u32[]{:S(2)}) %collective-permute-start.6) | collective-permute-done | bytes 294944 | tf_op jit(solution)/shard_map/ppermute | solution.py:52
  27.7 4.4 %collective-permute-start.9 = (bf16[32,4608]{1,0:T(8,128)(2,1)S(1)}, bf16[32,4608]{1,0:T(8,128)(2,1)S(1)}, u32[]{:S(2)}, u32[]{:S(2)}) collective-permute-start(bf16[32,4608]{1,0:T(8,128)(2,1)S(1)} %collective-permute-done.8.refs_1_), channel_id=1, source_target_pairs={{0,4},{4,0},{8,12},{12,8},{1,5},{5,1},{9,13},{13,9},{2,6},{6,2},{1... | collective-permute-start | bytes 884744 | tf_op jit(solution)/shard_map/ppermute | solution.py:59
  32.1 1.4 %copy-done.2 = bf16[96,8192]{1,0:T(8,128)(2,1)S(1)} copy-done((bf16[96,8192]{1,0:T(8,128)(2,1)S(1)}, bf16[96,8192]{1,0:T(8,128)(2,1)}, u32[]{:S(2)}) %copy-start.2) | copy-done | bytes 1572888
  35.5 3.5 %collective-permute-done.refs_9_ = bf16[96,8192]{1,0:T(8,128)(2,1)S(1)} collective-permute-done((bf16[96,8192]{1,0:T(8,128)(2,1)}, bf16[96,8192]{1,0:T(8,128)(2,1)S(1)}, u32[]{:S(2)}, u32[]{:S(2)}) %collective-permute-start) | collective-permute-done | bytes 1572896 | tf_op jit(solution)/shard_map/ppermute | solution.py:20
  38.9 1.8 %collective-permute-start.2 = (s32[2,96]{1,0:T(2,128)S(1)}, s32[2,96]{1,0:T(2,128)S(1)}, u32[]{:S(2)}, u32[]{:S(2)}) collective-permute-start(s32[2,96]{1,0:T(2,128)S(1)} %bitcast.8), channel_id=1, source_target_pairs={{0,2},{1,3},{2,0},{3,1},{4,6},{5,7},{6,4},{7,5},{8,10},{9,11},{10,... | collective-permute-start | bytes 2312 | tf_op jit(solution)/shard_map/ppermute | solution.py:20
  40.8 1.7 %collective-permute-done.2.refs_7_ = s32[2,96]{1,0:T(2,128)S(1)} collective-permute-done((s32[2,96]{1,0:T(2,128)S(1)}, s32[2,96]{1,0:T(2,128)S(1)}, u32[]{:S(2)}, u32[]{:S(2)}) %collective-permute-start.2) | collective-permute-done | bytes 800 | tf_op jit(solution)/shard_map/ppermute | solution.py:20
  42.5 1.2 %collective-permute-done.3.refs_8_ = s32[2,96]{1,0:T(2,128)S(1)} collective-permute-done((s32[2,96]{1,0:T(2,128)S(1)}, s32[2,96]{1,0:T(2,128)S(1)}, u32[]{:S(2)}, u32[]{:S(2)}) %collective-permute-start.3) | collective-permute-done | bytes 800 | tf_op jit(solution)/shard_map/ppermute | solution.py:20
  43.9 2.8 %stage_rest.1 = (bf16[8192,128]{1,0:T(8,128)(2,1)S(1)}, f32[128,1]{1,0:T(8,128)S(1)}, bf16[384,8192]{1,0:T(8,128)(2,1)S(1)}, f32[384,128]{1,0:T(8,128)S(1)}) custom-call(bf16[32,4608]{1,0:T(8,128)(2,1)S(1)} %collective-permute-done.6.refs_0_, bf16[32,4608]{1,0:T(8,128)(2,1)S(1)} %collective-permute-done.8.refs_1_, ...), custom_call_target="tpu_custom_call" | custom-call | flops 8388608 | bytes 12000000 | tf_op jit(solution)/shard_map/stage_rest/pallas_call | solution.py:323
  49.9 1.9 %collective-permute-done.17.refs_2_ = f32[1,384]{1,0:T(1,128)S(1)} collective-permute-done((f32[1,384]{1,0:T(1,128)S(1)}, f32[1,384]{1,0:T(1,128)S(1)}, u32[]{:S(2)}, u32[]{:S(2)}) %collective-permute-start.17) | collective-permute-done | bytes 1568 | tf_op jit(solution)/shard_map/ppermute | solution.py:20
  52.6 1.6 %collective-permute-start.19 = (bf16[32,4096]{1,0:T(8,128)(2,1)S(1)}, bf16[32,4096]{1,0:T(8,128)(2,1)S(1)}, u32[]{:S(2)}, u32[]{:S(2)}) collective-permute-start(bf16[32,4096]{1,0:T(8,128)(2,1)S(1)} %get-tuple-element.86), channel_id=1, source_target_pairs={{0,4},{4,0},{8,12},{12,8},{1,5},{5,1},{9,13},{13,9},{2,6},{6,2},{1... | collective-permute-start | bytes 786440 | tf_op jit(solution)/shard_map/ppermute | solution.py:101
  54.3 2.8 %copy-done.1 = bf16[384,8192]{1,0:T(8,128)(2,1)S(1)} copy-done((bf16[384,8192]{1,0:T(8,128)(2,1)S(1)}, bf16[384,8192]{1,0:T(8,128)(2,1)}, u32[]{:S(2)}) %copy-start.1) | copy-done | bytes 6291480
  58.9 2.8 %collective-permute-done.19 = bf16[32,4096]{1,0:T(8,128)(2,1)S(1)} collective-permute-done((bf16[32,4096]{1,0:T(8,128)(2,1)S(1)}, bf16[32,4096]{1,0:T(8,128)(2,1)S(1)}, u32[]{:S(2)}, u32[]{:S(2)}) %collective-permute-start.19) | collective-permute-done | bytes 262176 | tf_op jit(solution)/shard_map/ppermute | solution.py:101
  61.7 1.7 %collective-permute-start.27 = (bf16[32,4096]{1,0:T(8,128)(2,1)S(1)}, bf16[32,4096]{1,0:T(8,128)(2,1)S(1)}, u32[]{:S(2)}, u32[]{:S(2)}) collective-permute-start(bf16[32,4096]{1,0:T(8,128)(2,1)S(1)} %get-tuple-element.91), channel_id=1, source_target_pairs={{0,4},{4,0},{8,12},{12,8},{1,5},{5,1},{9,13},{13,9},{2,6},{6,2},{1... | collective-permute-start | bytes 786440 | tf_op jit(solution)/shard_map/ppermute | solution.py:105
  64.2 4.5 %collective-permute-start.23 = (bf16[32,4096]{1,0:T(8,128)(2,1)S(1)}, bf16[32,4096]{1,0:T(8,128)(2,1)S(1)}, u32[]{:S(2)}, u32[]{:S(2)}) collective-permute-start(bf16[32,4096]{1,0:T(8,128)(2,1)S(1)} %get-tuple-element.87), channel_id=1, source_target_pairs={{0,4},{4,0},{8,12},{12,8},{1,5},{5,1},{9,13},{13,9},{2,6},{6,2},{1... | collective-permute-start | bytes 786440 | tf_op jit(solution)/shard_map/ppermute | solution.py:105
  69.5 4.9 %collective-permute-start.26 = (bf16[32,4096]{1,0:T(8,128)(2,1)S(1)}, bf16[32,4096]{1,0:T(8,128)(2,1)S(1)}, u32[]{:S(2)}, u32[]{:S(2)}) collective-permute-start(bf16[32,4096]{1,0:T(8,128)(2,1)S(1)} %fusion.1), channel_id=1, source_target_pairs={{0,4},{4,0},{8,12},{12,8},{1,5},{5,1},{9,13},{13,9},{2,6},{6,2},{1... | collective-permute-start | bytes 786440 | tf_op jit(solution)/shard_map/ppermute | solution.py:111
  75.2 4.8 %collective-permute-start.22 = (bf16[32,4096]{1,0:T(8,128)(2,1)S(1)}, bf16[32,4096]{1,0:T(8,128)(2,1)S(1)}, u32[]{:S(2)}, u32[]{:S(2)}) collective-permute-start(bf16[32,4096]{1,0:T(8,128)(2,1)S(1)} %fusion), channel_id=1, source_target_pairs={{0,4},{4,0},{8,12},{12,8},{1,5},{5,1},{9,13},{13,9},{2,6},{6,2},{1... | collective-permute-start | bytes 786440 | tf_op jit(solution)/shard_map/ppermute | solution.py:111
  80.7 3.4 %collective-permute-done.26 = bf16[32,4096]{1,0:T(8,128)(2,1)S(1)} collective-permute-done((bf16[32,4096]{1,0:T(8,128)(2,1)S(1)}, bf16[32,4096]{1,0:T(8,128)(2,1)S(1)}, u32[]{:S(2)}, u32[]{:S(2)}) %collective-permute-start.26) | collective-permute-done | bytes 262176 | tf_op jit(solution)/shard_map/ppermute | solution.py:111
  84.3 4.8 %collective-permute-done.22 = bf16[32,4096]{1,0:T(8,128)(2,1)S(1)} collective-permute-done((bf16[32,4096]{1,0:T(8,128)(2,1)S(1)}, bf16[32,4096]{1,0:T(8,128)(2,1)S(1)}, u32[]{:S(2)}, u32[]{:S(2)}) %collective-permute-start.22) | collective-permute-done | bytes 262176 | tf_op jit(solution)/shard_map/ppermute | solution.py:111
  (61 shorter events, 17.5 us)
Async XLA Ops:
  0.6 19.1 %collective-permute-start.7 = (bf16[96,8192]{1,0:T(8,128)(2,1)}, bf16[96,8192]{1,0:T(8,128)(2,1)S(1)}, u32[]{:S(2)}, u32[]{:S(2)}) collective-permute-start(bf16[96,8192]{1,0:T(8,128)(2,1)} %refs_0_.1), channel_id=1, source_target_pairs={{0,1},{1,0},{2,3},{3,2},{4,5},{5,4},{6,7},{7,6},{8,9},{9,8},{10,11... | collective-permute-start | bytes 4718600 | tf_op jit(solution)/shard_map/ppermute | solution.py:20
  1.1 37.8 %collective-permute-start = (bf16[96,8192]{1,0:T(8,128)(2,1)}, bf16[96,8192]{1,0:T(8,128)(2,1)S(1)}, u32[]{:S(2)}, u32[]{:S(2)}) collective-permute-start(bf16[96,8192]{1,0:T(8,128)(2,1)} %refs_0_.1), channel_id=1, source_target_pairs={{0,2},{1,3},{2,0},{3,1},{4,6},{5,7},{6,4},{7,5},{8,10},{9,11},{10,... | collective-permute-start | bytes 4718600 | tf_op jit(solution)/shard_map/ppermute | solution.py:20
  4.7 9.9 %collective-permute-start.4 = (bf16[32,4608]{1,0:T(8,128)(2,1)S(1)}, bf16[32,4608]{1,0:T(8,128)(2,1)S(1)}, u32[]{:S(2)}, u32[]{:S(2)}) collective-permute-start(bf16[32,4608]{1,0:T(8,128)(2,1)S(1)} %slice.8.refs_2_), channel_id=1, source_target_pairs={{0,4},{4,0},{8,12},{12,8},{1,5},{5,1},{9,13},{13,9},{2,6},{6,2},{1... | collective-permute-start | bytes 884744 | tf_op jit(solution)/shard_map/ppermute | solution.py:43
  6.3 8.9 %collective-permute-start.5 = (bf16[32,4608]{1,0:T(8,128)(2,1)S(1)}, bf16[32,4608]{1,0:T(8,128)(2,1)S(1)}, u32[]{:S(2)}, u32[]{:S(2)}) collective-permute-start(bf16[32,4608]{1,0:T(8,128)(2,1)S(1)} %slice.8.refs_2_), channel_id=1, source_target_pairs={{4,8},{8,4},{5,9},{9,5},{6,10},{10,6},{7,11},{11,7},{20,24},{24,20... | collective-permute-start | bytes 884744 | tf_op jit(solution)/shard_map/ppermute | solution.py:43
  8.0 12.5 %collective-permute-start.10 = (bf16[32,3584]{1,0:T(8,128)(2,1)S(1)}, bf16[32,3584]{1,0:T(8,128)(2,1)S(1)}, u32[]{:S(2)}, u32[]{:S(2)}) collective-permute-start(bf16[32,3584]{1,0:T(8,128)(2,1)S(1)} %slice.9.refs_3_), channel_id=1, source_target_pairs={{0,4},{4,0},{8,12},{12,8},{1,5},{5,1},{9,13},{13,9},{2,6},{6,2},{1... | collective-permute-start | bytes 688136 | tf_op jit(solution)/shard_map/ppermute | solution.py:43
  14.6 5.8 %collective-permute-start.11 = (bf16[32,3584]{1,0:T(8,128)(2,1)S(1)}, bf16[32,3584]{1,0:T(8,128)(2,1)S(1)}, u32[]{:S(2)}, u32[]{:S(2)}) collective-permute-start(bf16[32,3584]{1,0:T(8,128)(2,1)S(1)} %slice.9.refs_3_), channel_id=1, source_target_pairs={{4,8},{8,4},{5,9},{9,5},{6,10},{10,6},{7,11},{11,7},{20,24},{24,20... | collective-permute-start | bytes 688136 | tf_op jit(solution)/shard_map/ppermute | solution.py:43
  15.3 12.4 %collective-permute-start.6 = (bf16[32,4608]{1,0:T(8,128)(2,1)S(1)}, bf16[32,4608]{1,0:T(8,128)(2,1)S(1)}, u32[]{:S(2)}, u32[]{:S(2)}) collective-permute-start(bf16[32,4608]{1,0:T(8,128)(2,1)S(1)} %collective-permute-done.5.refs_5_), channel_id=1, source_target_pairs={{0,4},{4,0},{8,12},{12,8},{1,5},{5,1},{9,13},{13,9},{2,6},{6,2},{1... | collective-permute-start | bytes 884744 | tf_op jit(solution)/shard_map/ppermute | solution.py:52
  19.8 7.9 %collective-permute-start.8 = (bf16[32,4608]{1,0:T(8,128)(2,1)S(1)}, bf16[32,4608]{1,0:T(8,128)(2,1)S(1)}, u32[]{:S(2)}, u32[]{:S(2)}) collective-permute-start(bf16[32,4608]{1,0:T(8,128)(2,1)S(1)} %collective-permute-done.4.refs_4_), channel_id=1, source_target_pairs={{4,8},{8,4},{5,9},{9,5},{6,10},{10,6},{7,11},{11,7},{20,24},{24,20... | collective-permute-start | bytes 884744 | tf_op jit(solution)/shard_map/ppermute | solution.py:54
  20.4 14.9 %collective-permute-start.12 = (bf16[32,3584]{1,0:T(8,128)(2,1)S(1)}, bf16[32,3584]{1,0:T(8,128)(2,1)S(1)}, u32[]{:S(2)}, u32[]{:S(2)}) collective-permute-start(bf16[32,3584]{1,0:T(8,128)(2,1)S(1)} %collective-permute-done.11.refs_7_), channel_id=1, source_target_pairs={{0,4},{4,0},{8,12},{12,8},{1,5},{5,1},{9,13},{13,9},{2,6},{6,2},{1... | collective-permute-start | bytes 688136 | tf_op jit(solution)/shard_map/ppermute | solution.py:52
  25.8 9.6 %collective-permute-start.13 = (bf16[32,3584]{1,0:T(8,128)(2,1)S(1)}, bf16[32,3584]{1,0:T(8,128)(2,1)S(1)}, u32[]{:S(2)}, u32[]{:S(2)}) collective-permute-start(bf16[32,3584]{1,0:T(8,128)(2,1)S(1)} %collective-permute-done.10.refs_5_), channel_id=1, source_target_pairs={{4,8},{8,4},{5,9},{9,5},{6,10},{10,6},{7,11},{11,7},{20,24},{24,20... | collective-permute-start | bytes 688136 | tf_op jit(solution)/shard_map/ppermute | solution.py:54
  27.7 16.0 %collective-permute-start.9 = (bf16[32,4608]{1,0:T(8,128)(2,1)S(1)}, bf16[32,4608]{1,0:T(8,128)(2,1)S(1)}, u32[]{:S(2)}, u32[]{:S(2)}) collective-permute-start(bf16[32,4608]{1,0:T(8,128)(2,1)S(1)} %collective-permute-done.8.refs_1_), channel_id=1, source_target_pairs={{0,4},{4,0},{8,12},{12,8},{1,5},{5,1},{9,13},{13,9},{2,6},{6,2},{1... | collective-permute-start | bytes 884744 | tf_op jit(solution)/shard_map/ppermute | solution.py:59
  35.4 8.3 %collective-permute-start.14 = (bf16[32,3584]{1,0:T(8,128)(2,1)S(1)}, bf16[32,3584]{1,0:T(8,128)(2,1)S(1)}, u32[]{:S(2)}, u32[]{:S(2)}) collective-permute-start(bf16[32,3584]{1,0:T(8,128)(2,1)S(1)} %collective-permute-done.13.refs_3_), channel_id=1, source_target_pairs={{0,4},{4,0},{8,12},{12,8},{1,5},{5,1},{9,13},{13,9},{2,6},{6,2},{1... | collective-permute-start | bytes 688136 | tf_op jit(solution)/shard_map/ppermute | solution.py:59
  38.9 3.6 %collective-permute-start.2 = (s32[2,96]{1,0:T(2,128)S(1)}, s32[2,96]{1,0:T(2,128)S(1)}, u32[]{:S(2)}, u32[]{:S(2)}) collective-permute-start(s32[2,96]{1,0:T(2,128)S(1)} %bitcast.8), channel_id=1, source_target_pairs={{0,2},{1,3},{2,0},{3,1},{4,6},{5,7},{6,4},{7,5},{8,10},{9,11},{10,... | collective-permute-start | bytes 2312 | tf_op jit(solution)/shard_map/ppermute | solution.py:20
  48.3 3.6 %collective-permute-start.17 = (f32[1,384]{1,0:T(1,128)S(1)}, f32[1,384]{1,0:T(1,128)S(1)}, u32[]{:S(2)}, u32[]{:S(2)}) collective-permute-start(f32[1,384]{1,0:T(1,128)S(1)} %get-tuple-element.80.refs_0_), channel_id=1, source_target_pairs={{0,2},{1,3},{2,0},{3,1},{4,6},{5,7},{6,4},{7,5},{8,10},{9,11},{10,... | collective-permute-start | bytes 4616 | tf_op jit(solution)/shard_map/ppermute | solution.py:20
  52.6 9.1 %collective-permute-start.19 = (bf16[32,4096]{1,0:T(8,128)(2,1)S(1)}, bf16[32,4096]{1,0:T(8,128)(2,1)S(1)}, u32[]{:S(2)}, u32[]{:S(2)}) collective-permute-start(bf16[32,4096]{1,0:T(8,128)(2,1)S(1)} %get-tuple-element.86), channel_id=1, source_target_pairs={{0,4},{4,0},{8,12},{12,8},{1,5},{5,1},{9,13},{13,9},{2,6},{6,2},{1... | collective-permute-start | bytes 786440 | tf_op jit(solution)/shard_map/ppermute | solution.py:101
  57.8 10.9 %collective-permute-start.20 = (bf16[32,4096]{1,0:T(8,128)(2,1)S(1)}, bf16[32,4096]{1,0:T(8,128)(2,1)S(1)}, u32[]{:S(2)}, u32[]{:S(2)}) collective-permute-start(bf16[32,4096]{1,0:T(8,128)(2,1)S(1)} %get-tuple-element.88), channel_id=1, source_target_pairs={{0,4},{4,0},{8,12},{12,8},{1,5},{5,1},{9,13},{13,9},{2,6},{6,2},{1... | collective-permute-start | bytes 786440 | tf_op jit(solution)/shard_map/ppermute | solution.py:101
  61.7 12.7 %collective-permute-start.27 = (bf16[32,4096]{1,0:T(8,128)(2,1)S(1)}, bf16[32,4096]{1,0:T(8,128)(2,1)S(1)}, u32[]{:S(2)}, u32[]{:S(2)}) collective-permute-start(bf16[32,4096]{1,0:T(8,128)(2,1)S(1)} %get-tuple-element.91), channel_id=1, source_target_pairs={{0,4},{4,0},{8,12},{12,8},{1,5},{5,1},{9,13},{13,9},{2,6},{6,2},{1... | collective-permute-start | bytes 786440 | tf_op jit(solution)/shard_map/ppermute | solution.py:105
  63.5 5.9 %collective-permute-start.25 = (bf16[32,4096]{1,0:T(8,128)(2,1)S(1)}, bf16[32,4096]{1,0:T(8,128)(2,1)S(1)}, u32[]{:S(2)}, u32[]{:S(2)}) collective-permute-start(bf16[32,4096]{1,0:T(8,128)(2,1)S(1)} %add_convert_fusion.2), channel_id=1, source_target_pairs={{4,8},{8,4},{5,9},{9,5},{6,10},{10,6},{7,11},{11,7},{20,24},{24,20... | collective-permute-start | bytes 786440 | tf_op jit(solution)/shard_map/ppermute | solution.py:108
  64.2 15.8 %collective-permute-start.23 = (bf16[32,4096]{1,0:T(8,128)(2,1)S(1)}, bf16[32,4096]{1,0:T(8,128)(2,1)S(1)}, u32[]{:S(2)}, u32[]{:S(2)}) collective-permute-start(bf16[32,4096]{1,0:T(8,128)(2,1)S(1)} %get-tuple-element.87), channel_id=1, source_target_pairs={{0,4},{4,0},{8,12},{12,8},{1,5},{5,1},{9,13},{13,9},{2,6},{6,2},{1... | collective-permute-start | bytes 786440 | tf_op jit(solution)/shard_map/ppermute | solution.py:105
  68.7 6.4 %collective-permute-start.21 = (bf16[32,4096]{1,0:T(8,128)(2,1)S(1)}, bf16[32,4096]{1,0:T(8,128)(2,1)S(1)}, u32[]{:S(2)}, u32[]{:S(2)}) collective-permute-start(bf16[32,4096]{1,0:T(8,128)(2,1)S(1)} %add_convert_fusion.5), channel_id=1, source_target_pairs={{4,8},{8,4},{5,9},{9,5},{6,10},{10,6},{7,11},{11,7},{20,24},{24,20... | collective-permute-start | bytes 786440 | tf_op jit(solution)/shard_map/ppermute | solution.py:108
  69.5 14.7 %collective-permute-start.26 = (bf16[32,4096]{1,0:T(8,128)(2,1)S(1)}, bf16[32,4096]{1,0:T(8,128)(2,1)S(1)}, u32[]{:S(2)}, u32[]{:S(2)}) collective-permute-start(bf16[32,4096]{1,0:T(8,128)(2,1)S(1)} %fusion.1), channel_id=1, source_target_pairs={{0,4},{4,0},{8,12},{12,8},{1,5},{5,1},{9,13},{13,9},{2,6},{6,2},{1... | collective-permute-start | bytes 786440 | tf_op jit(solution)/shard_map/ppermute | solution.py:111
  74.4 9.7 %collective-permute-start.28 = (bf16[32,4096]{1,0:T(8,128)(2,1)S(1)}, bf16[32,4096]{1,0:T(8,128)(2,1)S(1)}, u32[]{:S(2)}, u32[]{:S(2)}) collective-permute-start(bf16[32,4096]{1,0:T(8,128)(2,1)S(1)} %add_convert_fusion), channel_id=1, source_target_pairs={{4,8},{8,4},{5,9},{9,5},{6,10},{10,6},{7,11},{11,7},{20,24},{24,20... | collective-permute-start | bytes 786440 | tf_op jit(solution)/shard_map/ppermute | solution.py:109
  75.2 13.9 %collective-permute-start.22 = (bf16[32,4096]{1,0:T(8,128)(2,1)S(1)}, bf16[32,4096]{1,0:T(8,128)(2,1)S(1)}, u32[]{:S(2)}, u32[]{:S(2)}) collective-permute-start(bf16[32,4096]{1,0:T(8,128)(2,1)S(1)} %fusion), channel_id=1, source_target_pairs={{0,4},{4,0},{8,12},{12,8},{1,5},{5,1},{9,13},{13,9},{2,6},{6,2},{1... | collective-permute-start | bytes 786440 | tf_op jit(solution)/shard_map/ppermute | solution.py:111
  80.1 9.0 %collective-permute-start.24 = (bf16[32,4096]{1,0:T(8,128)(2,1)S(1)}, bf16[32,4096]{1,0:T(8,128)(2,1)S(1)}, u32[]{:S(2)}, u32[]{:S(2)}) collective-permute-start(bf16[32,4096]{1,0:T(8,128)(2,1)S(1)} %add_convert_fusion.3), channel_id=1, source_target_pairs={{4,8},{8,4},{5,9},{9,5},{6,10},{10,6},{7,11},{11,7},{20,24},{24,20... | collective-permute-start | bytes 786440 | tf_op jit(solution)/shard_map/ppermute | solution.py:109
  (10 other events, 27.5 us)

commit v17 on v14

--- a/solution.py
+++ b/solution.py
@@ -38,30 +38,33 @@
     cuts = [block[:, :cut], block[:, cut:]]
     crossed = swap_bits(images, "reader", far_bit)
     near = swap_gather(images, "reader", near_bits)
-    near_routes = swap_gather(routes, "reader", near_bits)
     firsts = [
         lax.optimization_barrier(
             (lax.ppermute(one, "blk", SIDES), lax.ppermute(one, "blk", MIDDLE))
         )
         for one in cuts
     ]
-    early = stage(
-        [[[one] for one in cuts], [[side] for side, _ in firsts]], near, noise, near_routes
-    )
     far_parts, end_parts = [], []
-    for side, across in firsts:
+    for last, (side, across) in enumerate(firsts):
         far = lax.ppermute(across, "blk", SIDES)
+        side, *_ = lax.optimization_barrier((side, *near))
         across_far = lax.ppermute(side, "blk", MIDDLE)
-        far, across_far, *early = lax.optimization_barrier((far, across_far, *early))
+        if last:
+            far, across_far, *early = lax.optimization_barrier((far, across_far, *early))
+        else:
+            far, across_far, routes = lax.optimization_barrier((far, across_far, routes))
+            blocks = [[[one] for one in cuts], [[one] for one, _ in firsts]]
+            early = stage(blocks, near, noise, swap_gather(routes, "reader", near_bits))
         end = lax.ppermute(across_far, "blk", SIDES)
         far_parts.append([far, across_far])
         end_parts.append([end, across])
-    weighted, penalty, near, noise, routes = early
+    weighted, penalty, staged_near, noise, routes = early
     ends = [parts[0] for parts in end_parts]
-    far_routes, crossed, *_ = lax.optimization_barrier((routes, crossed, *ends))
+    far_routes, crossed = lax.optimization_barrier((routes, crossed))
     far_routes = swap_bits(far_routes, "reader", far_bit)
+    crossed, far_routes, *_ = lax.optimization_barrier((crossed, far_routes, *ends))
     far = swap_gather(crossed, "reader", near_bits)
-    staged = stage_rest([far_parts, end_parts], near, crossed, weighted, penalty, noise)
+    staged = stage_rest([far_parts, end_parts], staged_near, crossed, weighted, penalty, noise)
     return staged, far[1:], (routes, far_routes)
 
 
@@ -347,8 +350,9 @@
     refs = list(refs)
     half = readers // 2
     far_refs = [refs.pop(0) for _ in range(half - 1)]
-    turned_ref, penalty_ref, _, product_ref, near_route_ref, far_route_ref = refs[:6]
-    score_ref, mask_ref, lse_ref, all_ref, sum_ref, image_sems = refs[6:]
+    turned_ref, penalty_ref, _, product_ref = [refs.pop(0) for _ in range(4)]
+    near_route_ref, far_route_ref = refs.pop(0), refs.pop(0)
+    score_ref, mask_ref, lse_ref, all_ref, sum_ref, image_sems = refs
     reader = lax.axis_index("reader")
     placed = [
         place_images(half + 1 + i, ref, all_ref, image_sems.at[i])
@@ -362,7 +366,8 @@
             ref[...], turned_ref[...], preferred_element_type=jnp.float32
         )
     top, rows = near_route_ref.shape[0] // half, near_route_ref.shape[1]
-    routes = [ref[k * top : (k + 1) * top, :] for ref in (near_route_ref, far_route_ref) for k in range(half)]
+    routes = [near_route_ref[k * top : (k + 1) * top, :] for k in range(half)]
+    routes += [far_route_ref[k * top : (k + 1) * top, :] for k in range(half)]
     bit = 1
     while bit < readers:
         flip = (reader & bit) > 0
@@ -393,7 +398,7 @@
             jax.ShapeDtypeStruct((1, slots), jnp.float32),
             jax.ShapeDtypeStruct((slots, width), jnp.bfloat16),
         ),
-        in_specs=[VMEM_SPEC] * (len(far) + 6),
+        in_specs=[VMEM_SPEC] * (len(far) + 4 + len(routes)),
         out_specs=(VMEM_SPEC,) * 4,
         scratch_shapes=[
             pltpu.VMEM((slots, refs), jnp.float32),

time: 93 us -> 92.1 us (level)
  waiting for transfers between devices: 30.5 us -> 24.9 us
  starting transfers between devices: 45.1 us -> 49.8 us
    ppermute x2, waiting for transfers between devices: 6.12 us -> 2.68 us  [staged_gather(): end = lax.ppermute(across_far, 'blk', SIDES)]
    ppermute x2, starting transfers between devices: 8.09 us -> 9.77 us  [staged_gather(): far = lax.ppermute(across, 'blk', SIDES)]
    ppermute x2, starting transfers between devices: 3.84 us -> 5.39 us  [pair_scatter(): for_far_middle = [lax.ppermute(part, axis, SIDES) for part in second]]
    ppermute x2, waiting for transfers between devices: 0.01 us -> 1.23 us  [staged_gather(): far = lax.ppermute(across, 'blk', SIDES)]
    ppermute x8, starting transfers between devices: 5.64 us -> 6.77 us  [swap_bits(): lax.ppermute(block, axis, [(i, i ^ bits) for i in range(lax.axis_size(axi...]
    ppermute x2, starting transfers between devices: 8.68 us -> 9.72 us  [pair_scatter(): from_side = lax.ppermute(near, axis, SIDES)]
    ppermute x2, waiting for transfers between devices: 9.82 us -> 8.79 us  [pair_scatter(): from_side = lax.ppermute(near, axis, SIDES)]
  transfers between devices with their start and end apart: 28 -> 28, of which waited for: 13 -> 11; matrix products, arithmetic and copies ran while one was open for 3% -> 3% of each run, Pallas kernels for 5% -> 5%
where the time goes in v17:
time: 92.1 us; the launch traced here: 91.6 us
  starting transfers between devices  49.8 us (54%)
  waiting for transfers between devices  24.9 us (27%)
  local copies, waits for them, and re-layouts  8.15 us (9%)
  Pallas kernels  7.27 us (8%)
    ppermute x2, starting transfers between devices, staged_gather(): far = lax.ppermute(across, 'blk', SIDES)  9.77 us
    ppermute x2, starting transfers between devices, pair_scatter(): from_side = lax.ppermute(near, axis, SIDES)  9.72 us
    ppermute x2, waiting for transfers between devices, pair_scatter(): from_side = lax.ppermute(near, axis, SIDES)  8.79 us
    ppermute x8, waiting for transfers between devices, swap_bits(): lax.ppermute(block, axis, [(i, i ^ bits) for i in range(lax.axis_size(axi...  7.03 us
    ppermute x8, starting transfers between devices, swap_bits(): lax.ppermute(block, axis, [(i, i ^ bits) for i in range(lax.axis_size(axi...  6.77 us
    ppermute x2, starting transfers between devices, staged_gather(): lax.ppermute(one, 'blk', SIDES)  6.09 us
    unnamed x10, local copies, waits for them, and re-layouts  5.63 us
    ppermute x2, starting transfers between devices, pair_scatter(): for_far_middle = [lax.ppermute(part, axis, SIDES) for part in second]  5.39 us
  transfers between devices with their start and end apart: 28, of which 11 were waited for; matrix products, arithmetic and copies ran while one was open for 3% of the time, Pallas kernels for 5%

profile of v17, /device:TPU:0, one launch (start us, length us, event | category | flops | bytes accessed | tf_op | source)
XLA Modules:
  0.0 91.6 jit_solution(12693037082438521799)
XLA Ops:
  1.1 2.6 %collective-permute-start.10 = (bf16[96,8192]{1,0:T(8,128)(2,1)}, bf16[96,8192]{1,0:T(8,128)(2,1)S(1)}, u32[]{:S(2)}, u32[]{:S(2)}) collective-permute-start(bf16[96,8192]{1,0:T(8,128)(2,1)} %refs_0_.1), channel_id=1, source_target_pairs={{0,2},{1,3},{2,0},{3,1},{4,6},{5,7},{6,4},{7,5},{8,10},{9,11},{10,... | collective-permute-start | bytes 4718600 | tf_op jit(solution)/shard_map/ppermute | solution.py:20
  4.7 1.6 %collective-permute-start.5 = (bf16[32,4608]{1,0:T(8,128)(2,1)S(1)}, bf16[32,4608]{1,0:T(8,128)(2,1)S(1)}, u32[]{:S(2)}, u32[]{:S(2)}) collective-permute-start(bf16[32,4608]{1,0:T(8,128)(2,1)S(1)} %slice.9.refs_2_), channel_id=1, source_target_pairs={{0,4},{4,0},{8,12},{12,8},{1,5},{5,1},{9,13},{13,9},{2,6},{6,2},{1... | collective-permute-start | bytes 884744 | tf_op jit(solution)/shard_map/ppermute | solution.py:43
  8.0 4.4 %collective-permute-start = (bf16[32,3584]{1,0:T(8,128)(2,1)S(1)}, bf16[32,3584]{1,0:T(8,128)(2,1)S(1)}, u32[]{:S(2)}, u32[]{:S(2)}) collective-permute-start(bf16[32,3584]{1,0:T(8,128)(2,1)S(1)} %slice.8.refs_3_), channel_id=1, source_target_pairs={{0,4},{4,0},{8,12},{12,8},{1,5},{5,1},{9,13},{13,9},{2,6},{6,2},{1... | collective-permute-start | bytes 688136 | tf_op jit(solution)/shard_map/ppermute | solution.py:43
  12.4 2.2 %collective-permute-done.5.refs_4_ = bf16[32,4608]{1,0:T(8,128)(2,1)S(1)} collective-permute-done((bf16[32,4608]{1,0:T(8,128)(2,1)S(1)}, bf16[32,4608]{1,0:T(8,128)(2,1)S(1)}, u32[]{:S(2)}, u32[]{:S(2)}) %collective-permute-start.5) | collective-permute-done | bytes 294944 | tf_op jit(solution)/shard_map/ppermute | solution.py:43
  15.3 4.5 %collective-permute-start.7 = (bf16[32,4608]{1,0:T(8,128)(2,1)S(1)}, bf16[32,4608]{1,0:T(8,128)(2,1)S(1)}, u32[]{:S(2)}, u32[]{:S(2)}) collective-permute-start(bf16[32,4608]{1,0:T(8,128)(2,1)S(1)} %collective-permute-done.6.refs_5_), channel_id=1, source_target_pairs={{0,4},{4,0},{8,12},{12,8},{1,5},{5,1},{9,13},{13,9},{2,6},{6,2},{1... | collective-permute-start | bytes 884744 | tf_op jit(solution)/shard_map/ppermute | solution.py:49
  20.4 5.3 %collective-permute-start.2 = (bf16[32,3584]{1,0:T(8,128)(2,1)S(1)}, bf16[32,3584]{1,0:T(8,128)(2,1)S(1)}, u32[]{:S(2)}, u32[]{:S(2)}) collective-permute-start(bf16[32,3584]{1,0:T(8,128)(2,1)S(1)} %collective-permute-done.1.refs_7_), channel_id=1, source_target_pairs={{0,4},{4,0},{8,12},{12,8},{1,5},{5,1},{9,13},{13,9},{2,6},{6,2},{1... | collective-permute-start | bytes 688136 | tf_op jit(solution)/shard_map/ppermute | solution.py:49
  26.4 1.2 %collective-permute-done.7.refs_0_ = bf16[32,4608]{1,0:T(8,128)(2,1)S(1)} collective-permute-done((bf16[32,4608]{1,0:T(8,128)(2,1)S(1)}, bf16[32,4608]{1,0:T(8,128)(2,1)S(1)}, u32[]{:S(2)}, u32[]{:S(2)}) %collective-permute-start.7) | collective-permute-done | bytes 294944 | tf_op jit(solution)/shard_map/ppermute | solution.py:49
  27.7 4.4 %collective-permute-start.12 = (bf16[32,4608]{1,0:T(8,128)(2,1)S(1)}, bf16[32,4608]{1,0:T(8,128)(2,1)S(1)}, u32[]{:S(2)}, u32[]{:S(2)}) collective-permute-start(bf16[32,4608]{1,0:T(8,128)(2,1)S(1)} %collective-permute-done.8.refs_1_), channel_id=1, source_target_pairs={{0,4},{4,0},{8,12},{12,8},{1,5},{5,1},{9,13},{13,9},{2,6},{6,2},{1... | collective-permute-start | bytes 884744 | tf_op jit(solution)/shard_map/ppermute | solution.py:58
  32.1 1.3 %collective-permute-done.9.refs_7_ = s32[2,96]{1,0:T(2,128)S(1)} collective-permute-done((s32[2,96]{1,0:T(2,128)}, s32[2,96]{1,0:T(2,128)S(1)}, u32[]{:S(2)}, u32[]{:S(2)}) %collective-permute-start.9) | collective-permute-done | bytes 800 | tf_op jit(solution)/shard_map/ppermute | solution.py:20
  33.4 1.4 %copy-done.2 = bf16[96,8192]{1,0:T(8,128)(2,1)S(1)} copy-done((bf16[96,8192]{1,0:T(8,128)(2,1)S(1)}, bf16[96,8192]{1,0:T(8,128)(2,1)}, u32[]{:S(2)}) %copy-start.2) | copy-done | bytes 1572888
  37.5 1.4 %collective-permute-done.10.refs_9_ = bf16[96,8192]{1,0:T(8,128)(2,1)S(1)} collective-permute-done((bf16[96,8192]{1,0:T(8,128)(2,1)}, bf16[96,8192]{1,0:T(8,128)(2,1)S(1)}, u32[]{:S(2)}, u32[]{:S(2)}) %collective-permute-start.10) | collective-permute-done | bytes 1572896 | tf_op jit(solution)/shard_map/ppermute | solution.py:20
  38.9 1.8 %collective-permute-start.11 = (s32[4,96]{1,0:T(4,128)S(1)}, s32[4,96]{1,0:T(4,128)S(1)}, u32[]{:S(2)}, u32[]{:S(2)}) collective-permute-start(s32[4,96]{1,0:T(4,128)S(1)} %get-tuple-element.62.refs_5_), channel_id=1, source_target_pairs={{0,2},{1,3},{2,0},{3,1},{4,6},{5,7},{6,4},{7,5},{8,10},{9,11},{10,... | collective-permute-start | bytes 4616 | tf_op jit(solution)/shard_map/ppermute | solution.py:20
  40.7 1.8 %collective-permute-done.11.refs_6_ = s32[4,96]{1,0:T(4,128)S(1)} collective-permute-done((s32[4,96]{1,0:T(4,128)S(1)}, s32[4,96]{1,0:T(4,128)S(1)}, u32[]{:S(2)}, u32[]{:S(2)}) %collective-permute-start.11) | collective-permute-done | bytes 1568 | tf_op jit(solution)/shard_map/ppermute | solution.py:20
  42.5 2.7 %collective-permute-done.13.refs_6_ = bf16[32,3584]{1,0:T(8,128)(2,1)S(1)} collective-permute-done((bf16[32,3584]{1,0:T(8,128)(2,1)S(1)}, bf16[32,3584]{1,0:T(8,128)(2,1)S(1)}, u32[]{:S(2)}, u32[]{:S(2)}) %collective-permute-start.13) | collective-permute-done | bytes 229408 | tf_op jit(solution)/shard_map/ppermute | solution.py:58
  45.2 2.8 %stage_rest.1 = (bf16[8192,128]{1,0:T(8,128)(2,1)S(1)}, f32[128,1]{1,0:T(8,128)S(1)}, bf16[384,8192]{1,0:T(8,128)(2,1)S(1)}, f32[384,128]{1,0:T(8,128)S(1)}) custom-call(bf16[32,4608]{1,0:T(8,128)(2,1)S(1)} %collective-permute-done.7.refs_0_, bf16[32,4608]{1,0:T(8,128)(2,1)S(1)} %collective-permute-done.8.refs_1_, ...), custom_call_target="tpu_custom_call" | custom-call | flops 8388608 | bytes 12000000 | tf_op jit(solution)/shard_map/stage_rest/pallas_call | solution.py:325
  51.4 1.9 %collective-permute-done.16.refs_2_ = f32[1,384]{1,0:T(1,128)S(1)} collective-permute-done((f32[1,384]{1,0:T(1,128)S(1)}, f32[1,384]{1,0:T(1,128)S(1)}, u32[]{:S(2)}, u32[]{:S(2)}) %collective-permute-start.16) | collective-permute-done | bytes 1568 | tf_op jit(solution)/shard_map/ppermute | solution.py:20
  54.4 2.8 %copy-done.1 = bf16[384,8192]{1,0:T(8,128)(2,1)S(1)} copy-done((bf16[384,8192]{1,0:T(8,128)(2,1)S(1)}, bf16[384,8192]{1,0:T(8,128)(2,1)}, u32[]{:S(2)}) %copy-start.1) | copy-done | bytes 6291480
  57.9 1.8 %collective-permute-start.19 = (bf16[32,4096]{1,0:T(8,128)(2,1)S(1)}, bf16[32,4096]{1,0:T(8,128)(2,1)S(1)}, u32[]{:S(2)}, u32[]{:S(2)}) collective-permute-start(bf16[32,4096]{1,0:T(8,128)(2,1)S(1)} %get-tuple-element.88), channel_id=1, source_target_pairs={{0,4},{4,0},{8,12},{12,8},{1,5},{5,1},{9,13},{13,9},{2,6},{6,2},{1... | collective-permute-start | bytes 786440 | tf_op jit(solution)/shard_map/ppermute | solution.py:96
  60.3 3.0 %collective-permute-done.18 = bf16[32,4096]{1,0:T(8,128)(2,1)S(1)} collective-permute-done((bf16[32,4096]{1,0:T(8,128)(2,1)S(1)}, bf16[32,4096]{1,0:T(8,128)(2,1)S(1)}, u32[]{:S(2)}, u32[]{:S(2)}) %collective-permute-start.18) | collective-permute-done | bytes 262176 | tf_op jit(solution)/shard_map/ppermute | solution.py:96
  64.0 5.4 %collective-permute-start.22 = (bf16[32,4096]{1,0:T(8,128)(2,1)S(1)}, bf16[32,4096]{1,0:T(8,128)(2,1)S(1)}, u32[]{:S(2)}, u32[]{:S(2)}) collective-permute-start(bf16[32,4096]{1,0:T(8,128)(2,1)S(1)} %get-tuple-element.87), channel_id=1, source_target_pairs={{0,4},{4,0},{8,12},{12,8},{1,5},{5,1},{9,13},{13,9},{2,6},{6,2},{1... | collective-permute-start | bytes 786440 | tf_op jit(solution)/shard_map/ppermute | solution.py:100
  70.3 5.0 %collective-permute-start.25 = (bf16[32,4096]{1,0:T(8,128)(2,1)S(1)}, bf16[32,4096]{1,0:T(8,128)(2,1)S(1)}, u32[]{:S(2)}, u32[]{:S(2)}) collective-permute-start(bf16[32,4096]{1,0:T(8,128)(2,1)S(1)} %fusion.1), channel_id=1, source_target_pairs={{0,4},{4,0},{8,12},{12,8},{1,5},{5,1},{9,13},{13,9},{2,6},{6,2},{1... | collective-permute-start | bytes 786440 | tf_op jit(solution)/shard_map/ppermute | solution.py:106
  76.1 4.8 %collective-permute-start.21 = (bf16[32,4096]{1,0:T(8,128)(2,1)S(1)}, bf16[32,4096]{1,0:T(8,128)(2,1)S(1)}, u32[]{:S(2)}, u32[]{:S(2)}) collective-permute-start(bf16[32,4096]{1,0:T(8,128)(2,1)S(1)} %fusion), channel_id=1, source_target_pairs={{0,4},{4,0},{8,12},{12,8},{1,5},{5,1},{9,13},{13,9},{2,6},{6,2},{1... | collective-permute-start | bytes 786440 | tf_op jit(solution)/shard_map/ppermute | solution.py:106
  81.6 4.1 %collective-permute-done.25 = bf16[32,4096]{1,0:T(8,128)(2,1)S(1)} collective-permute-done((bf16[32,4096]{1,0:T(8,128)(2,1)S(1)}, bf16[32,4096]{1,0:T(8,128)(2,1)S(1)}, u32[]{:S(2)}, u32[]{:S(2)}) %collective-permute-start.25) | collective-permute-done | bytes 262176 | tf_op jit(solution)/shard_map/ppermute | solution.py:106
  85.9 4.7 %collective-permute-done.21 = bf16[32,4096]{1,0:T(8,128)(2,1)S(1)} collective-permute-done((bf16[32,4096]{1,0:T(8,128)(2,1)S(1)}, bf16[32,4096]{1,0:T(8,128)(2,1)S(1)}, u32[]{:S(2)}, u32[]{:S(2)}) %collective-permute-start.21) | collective-permute-done | bytes 262176 | tf_op jit(solution)/shard_map/ppermute | solution.py:106
  (59 shorter events, 17.9 us)
Async XLA Ops:
  0.6 19.1 %collective-permute-start.3 = (bf16[96,8192]{1,0:T(8,128)(2,1)}, bf16[96,8192]{1,0:T(8,128)(2,1)S(1)}, u32[]{:S(2)}, u32[]{:S(2)}) collective-permute-start(bf16[96,8192]{1,0:T(8,128)(2,1)} %refs_0_.1), channel_id=1, source_target_pairs={{0,1},{1,0},{2,3},{3,2},{4,5},{5,4},{6,7},{7,6},{8,9},{9,8},{10,11... | collective-permute-start | bytes 4718600 | tf_op jit(solution)/shard_map/ppermute | solution.py:20
  1.1 37.8 %collective-permute-start.10 = (bf16[96,8192]{1,0:T(8,128)(2,1)}, bf16[96,8192]{1,0:T(8,128)(2,1)S(1)}, u32[]{:S(2)}, u32[]{:S(2)}) collective-permute-start(bf16[96,8192]{1,0:T(8,128)(2,1)} %refs_0_.1), channel_id=1, source_target_pairs={{0,2},{1,3},{2,0},{3,1},{4,6},{5,7},{6,4},{7,5},{8,10},{9,11},{10,... | collective-permute-start | bytes 4718600 | tf_op jit(solution)/shard_map/ppermute | solution.py:20
  4.7 9.9 %collective-permute-start.5 = (bf16[32,4608]{1,0:T(8,128)(2,1)S(1)}, bf16[32,4608]{1,0:T(8,128)(2,1)S(1)}, u32[]{:S(2)}, u32[]{:S(2)}) collective-permute-start(bf16[32,4608]{1,0:T(8,128)(2,1)S(1)} %slice.9.refs_2_), channel_id=1, source_target_pairs={{0,4},{4,0},{8,12},{12,8},{1,5},{5,1},{9,13},{13,9},{2,6},{6,2},{1... | collective-permute-start | bytes 884744 | tf_op jit(solution)/shard_map/ppermute | solution.py:43
  6.3 8.9 %collective-permute-start.6 = (bf16[32,4608]{1,0:T(8,128)(2,1)S(1)}, bf16[32,4608]{1,0:T(8,128)(2,1)S(1)}, u32[]{:S(2)}, u32[]{:S(2)}) collective-permute-start(bf16[32,4608]{1,0:T(8,128)(2,1)S(1)} %slice.9.refs_2_), channel_id=1, source_target_pairs={{4,8},{8,4},{5,9},{9,5},{6,10},{10,6},{7,11},{11,7},{20,24},{24,20... | collective-permute-start | bytes 884744 | tf_op jit(solution)/shard_map/ppermute | solution.py:43
  8.0 12.5 %collective-permute-start = (bf16[32,3584]{1,0:T(8,128)(2,1)S(1)}, bf16[32,3584]{1,0:T(8,128)(2,1)S(1)}, u32[]{:S(2)}, u32[]{:S(2)}) collective-permute-start(bf16[32,3584]{1,0:T(8,128)(2,1)S(1)} %slice.8.refs_3_), channel_id=1, source_target_pairs={{0,4},{4,0},{8,12},{12,8},{1,5},{5,1},{9,13},{13,9},{2,6},{6,2},{1... | collective-permute-start | bytes 688136 | tf_op jit(solution)/shard_map/ppermute | solution.py:43
  14.6 5.8 %collective-permute-start.1 = (bf16[32,3584]{1,0:T(8,128)(2,1)S(1)}, bf16[32,3584]{1,0:T(8,128)(2,1)S(1)}, u32[]{:S(2)}, u32[]{:S(2)}) collective-permute-start(bf16[32,3584]{1,0:T(8,128)(2,1)S(1)} %slice.8.refs_3_), channel_id=1, source_target_pairs={{4,8},{8,4},{5,9},{9,5},{6,10},{10,6},{7,11},{11,7},{20,24},{24,20... | collective-permute-start | bytes 688136 | tf_op jit(solution)/shard_map/ppermute | solution.py:43
  15.3 12.4 %collective-permute-start.7 = (bf16[32,4608]{1,0:T(8,128)(2,1)S(1)}, bf16[32,4608]{1,0:T(8,128)(2,1)S(1)}, u32[]{:S(2)}, u32[]{:S(2)}) collective-permute-start(bf16[32,4608]{1,0:T(8,128)(2,1)S(1)} %collective-permute-done.6.refs_5_), channel_id=1, source_target_pairs={{0,4},{4,0},{8,12},{12,8},{1,5},{5,1},{9,13},{13,9},{2,6},{6,2},{1... | collective-permute-start | bytes 884744 | tf_op jit(solution)/shard_map/ppermute | solution.py:49
  19.8 7.9 %collective-permute-start.8 = (bf16[32,4608]{1,0:T(8,128)(2,1)S(1)}, bf16[32,4608]{1,0:T(8,128)(2,1)S(1)}, u32[]{:S(2)}, u32[]{:S(2)}) collective-permute-start(bf16[32,4608]{1,0:T(8,128)(2,1)S(1)} %collective-permute-done.5.refs_4_), channel_id=1, source_target_pairs={{4,8},{8,4},{5,9},{9,5},{6,10},{10,6},{7,11},{11,7},{20,24},{24,20... | collective-permute-start | bytes 884744 | tf_op jit(solution)/shard_map/ppermute | solution.py:51
  20.4 16.9 %collective-permute-start.2 = (bf16[32,3584]{1,0:T(8,128)(2,1)S(1)}, bf16[32,3584]{1,0:T(8,128)(2,1)S(1)}, u32[]{:S(2)}, u32[]{:S(2)}) collective-permute-start(bf16[32,3584]{1,0:T(8,128)(2,1)S(1)} %collective-permute-done.1.refs_7_), channel_id=1, source_target_pairs={{0,4},{4,0},{8,12},{12,8},{1,5},{5,1},{9,13},{13,9},{2,6},{6,2},{1... | collective-permute-start | bytes 688136 | tf_op jit(solution)/shard_map/ppermute | solution.py:49
  25.8 11.6 %collective-permute-start.4 = (bf16[32,3584]{1,0:T(8,128)(2,1)S(1)}, bf16[32,3584]{1,0:T(8,128)(2,1)S(1)}, u32[]{:S(2)}, u32[]{:S(2)}) collective-permute-start(bf16[32,3584]{1,0:T(8,128)(2,1)S(1)} %collective-permute-done.refs_5_), channel_id=1, source_target_pairs={{4,8},{8,4},{5,9},{9,5},{6,10},{10,6},{7,11},{11,7},{20,24},{24,20... | collective-permute-start | bytes 688136 | tf_op jit(solution)/shard_map/ppermute | solution.py:51
  27.7 17.5 %collective-permute-start.12 = (bf16[32,4608]{1,0:T(8,128)(2,1)S(1)}, bf16[32,4608]{1,0:T(8,128)(2,1)S(1)}, u32[]{:S(2)}, u32[]{:S(2)}) collective-permute-start(bf16[32,4608]{1,0:T(8,128)(2,1)S(1)} %collective-permute-done.8.refs_1_), channel_id=1, source_target_pairs={{0,4},{4,0},{8,12},{12,8},{1,5},{5,1},{9,13},{13,9},{2,6},{6,2},{1... | collective-permute-start | bytes 884744 | tf_op jit(solution)/shard_map/ppermute | solution.py:58
  37.4 7.8 %collective-permute-start.13 = (bf16[32,3584]{1,0:T(8,128)(2,1)S(1)}, bf16[32,3584]{1,0:T(8,128)(2,1)S(1)}, u32[]{:S(2)}, u32[]{:S(2)}) collective-permute-start(bf16[32,3584]{1,0:T(8,128)(2,1)S(1)} %collective-permute-done.4.refs_3_), channel_id=1, source_target_pairs={{0,4},{4,0},{8,12},{12,8},{1,5},{5,1},{9,13},{13,9},{2,6},{6,2},{1... | collective-permute-start | bytes 688136 | tf_op jit(solution)/shard_map/ppermute | solution.py:58
  38.9 3.6 %collective-permute-start.11 = (s32[4,96]{1,0:T(4,128)S(1)}, s32[4,96]{1,0:T(4,128)S(1)}, u32[]{:S(2)}, u32[]{:S(2)}) collective-permute-start(s32[4,96]{1,0:T(4,128)S(1)} %get-tuple-element.62.refs_5_), channel_id=1, source_target_pairs={{0,2},{1,3},{2,0},{3,1},{4,6},{5,7},{6,4},{7,5},{8,10},{9,11},{10,... | collective-permute-start | bytes 4616 | tf_op jit(solution)/shard_map/ppermute | solution.py:20
  49.7 3.6 %collective-permute-start.16 = (f32[1,384]{1,0:T(1,128)S(1)}, f32[1,384]{1,0:T(1,128)S(1)}, u32[]{:S(2)}, u32[]{:S(2)}) collective-permute-start(f32[1,384]{1,0:T(1,128)S(1)} %get-tuple-element.80.refs_0_), channel_id=1, source_target_pairs={{0,2},{1,3},{2,0},{3,1},{4,6},{5,7},{6,4},{7,5},{8,10},{9,11},{10,... | collective-permute-start | bytes 4616 | tf_op jit(solution)/shard_map/ppermute | solution.py:20
  54.1 9.2 %collective-permute-start.18 = (bf16[32,4096]{1,0:T(8,128)(2,1)S(1)}, bf16[32,4096]{1,0:T(8,128)(2,1)S(1)}, u32[]{:S(2)}, u32[]{:S(2)}) collective-permute-start(bf16[32,4096]{1,0:T(8,128)(2,1)S(1)} %get-tuple-element.86), channel_id=1, source_target_pairs={{0,4},{4,0},{8,12},{12,8},{1,5},{5,1},{9,13},{13,9},{2,6},{6,2},{1... | collective-permute-start | bytes 786440 | tf_op jit(solution)/shard_map/ppermute | solution.py:96
  57.9 11.5 %collective-permute-start.19 = (bf16[32,4096]{1,0:T(8,128)(2,1)S(1)}, bf16[32,4096]{1,0:T(8,128)(2,1)S(1)}, u32[]{:S(2)}, u32[]{:S(2)}) collective-permute-start(bf16[32,4096]{1,0:T(8,128)(2,1)S(1)} %get-tuple-element.88), channel_id=1, source_target_pairs={{0,4},{4,0},{8,12},{12,8},{1,5},{5,1},{9,13},{13,9},{2,6},{6,2},{1... | collective-permute-start | bytes 786440 | tf_op jit(solution)/shard_map/ppermute | solution.py:96
  63.3 12.0 %collective-permute-start.26 = (bf16[32,4096]{1,0:T(8,128)(2,1)S(1)}, bf16[32,4096]{1,0:T(8,128)(2,1)S(1)}, u32[]{:S(2)}, u32[]{:S(2)}) collective-permute-start(bf16[32,4096]{1,0:T(8,128)(2,1)S(1)} %get-tuple-element.91), channel_id=1, source_target_pairs={{0,4},{4,0},{8,12},{12,8},{1,5},{5,1},{9,13},{13,9},{2,6},{6,2},{1... | collective-permute-start | bytes 786440 | tf_op jit(solution)/shard_map/ppermute | solution.py:100
  63.4 6.8 %collective-permute-start.24 = (bf16[32,4096]{1,0:T(8,128)(2,1)S(1)}, bf16[32,4096]{1,0:T(8,128)(2,1)S(1)}, u32[]{:S(2)}, u32[]{:S(2)}) collective-permute-start(bf16[32,4096]{1,0:T(8,128)(2,1)S(1)} %add_convert_fusion.2), channel_id=1, source_target_pairs={{4,8},{8,4},{5,9},{9,5},{6,10},{10,6},{7,11},{11,7},{20,24},{24,20... | collective-permute-start | bytes 786440 | tf_op jit(solution)/shard_map/ppermute | solution.py:103
  64.0 16.8 %collective-permute-start.22 = (bf16[32,4096]{1,0:T(8,128)(2,1)S(1)}, bf16[32,4096]{1,0:T(8,128)(2,1)S(1)}, u32[]{:S(2)}, u32[]{:S(2)}) collective-permute-start(bf16[32,4096]{1,0:T(8,128)(2,1)S(1)} %get-tuple-element.87), channel_id=1, source_target_pairs={{0,4},{4,0},{8,12},{12,8},{1,5},{5,1},{9,13},{13,9},{2,6},{6,2},{1... | collective-permute-start | bytes 786440 | tf_op jit(solution)/shard_map/ppermute | solution.py:100
  69.5 6.5 %collective-permute-start.20 = (bf16[32,4096]{1,0:T(8,128)(2,1)S(1)}, bf16[32,4096]{1,0:T(8,128)(2,1)S(1)}, u32[]{:S(2)}, u32[]{:S(2)}) collective-permute-start(bf16[32,4096]{1,0:T(8,128)(2,1)S(1)} %add_convert_fusion.5), channel_id=1, source_target_pairs={{4,8},{8,4},{5,9},{9,5},{6,10},{10,6},{7,11},{11,7},{20,24},{24,20... | collective-permute-start | bytes 786440 | tf_op jit(solution)/shard_map/ppermute | solution.py:103
  70.3 15.5 %collective-permute-start.25 = (bf16[32,4096]{1,0:T(8,128)(2,1)S(1)}, bf16[32,4096]{1,0:T(8,128)(2,1)S(1)}, u32[]{:S(2)}, u32[]{:S(2)}) collective-permute-start(bf16[32,4096]{1,0:T(8,128)(2,1)S(1)} %fusion.1), channel_id=1, source_target_pairs={{0,4},{4,0},{8,12},{12,8},{1,5},{5,1},{9,13},{13,9},{2,6},{6,2},{1... | collective-permute-start | bytes 786440 | tf_op jit(solution)/shard_map/ppermute | solution.py:106
  75.3 10.4 %collective-permute-start.27 = (bf16[32,4096]{1,0:T(8,128)(2,1)S(1)}, bf16[32,4096]{1,0:T(8,128)(2,1)S(1)}, u32[]{:S(2)}, u32[]{:S(2)}) collective-permute-start(bf16[32,4096]{1,0:T(8,128)(2,1)S(1)} %add_convert_fusion), channel_id=1, source_target_pairs={{4,8},{8,4},{5,9},{9,5},{6,10},{10,6},{7,11},{11,7},{20,24},{24,20... | collective-permute-start | bytes 786440 | tf_op jit(solution)/shard_map/ppermute | solution.py:104
  76.1 14.4 %collective-permute-start.21 = (bf16[32,4096]{1,0:T(8,128)(2,1)S(1)}, bf16[32,4096]{1,0:T(8,128)(2,1)S(1)}, u32[]{:S(2)}, u32[]{:S(2)}) collective-permute-start(bf16[32,4096]{1,0:T(8,128)(2,1)S(1)} %fusion), channel_id=1, source_target_pairs={{0,4},{4,0},{8,12},{12,8},{1,5},{5,1},{9,13},{13,9},{2,6},{6,2},{1... | collective-permute-start | bytes 786440 | tf_op jit(solution)/shard_map/ppermute | solution.py:106
  80.9 9.6 %collective-permute-start.23 = (bf16[32,4096]{1,0:T(8,128)(2,1)S(1)}, bf16[32,4096]{1,0:T(8,128)(2,1)S(1)}, u32[]{:S(2)}, u32[]{:S(2)}) collective-permute-start(bf16[32,4096]{1,0:T(8,128)(2,1)S(1)} %add_convert_fusion.3), channel_id=1, source_target_pairs={{4,8},{8,4},{5,9},{9,5},{6,10},{10,6},{7,11},{11,7},{20,24},{24,20... | collective-permute-start | bytes 786440 | tf_op jit(solution)/shard_map/ppermute | solution.py:104
  (9 other events, 19.9 us)

commit v18 on v17

--- a/solution.py
+++ b/solution.py
@@ -45,19 +45,16 @@
         for one in cuts
     ]
     far_parts, end_parts = [], []
-    for last, (side, across) in enumerate(firsts):
+    for side, across in firsts:
         far = lax.ppermute(across, "blk", SIDES)
         side, *_ = lax.optimization_barrier((side, *near))
         across_far = lax.ppermute(side, "blk", MIDDLE)
-        if last:
-            far, across_far, *early = lax.optimization_barrier((far, across_far, *early))
-        else:
-            far, across_far, routes = lax.optimization_barrier((far, across_far, routes))
-            blocks = [[[one] for one in cuts], [[one] for one, _ in firsts]]
-            early = stage(blocks, near, noise, swap_gather(routes, "reader", near_bits))
+        far, across_far, routes = lax.optimization_barrier((far, across_far, routes))
         end = lax.ppermute(across_far, "blk", SIDES)
         far_parts.append([far, across_far])
         end_parts.append([end, across])
+    blocks = [[[one] for one in cuts], [[one] for one, _ in firsts]]
+    early = stage(blocks, near, noise, swap_gather(routes, "reader", near_bits))
     weighted, penalty, staged_near, noise, routes = early
     ends = [parts[0] for parts in end_parts]
     far_routes, crossed = lax.optimization_barrier((routes, crossed))

time: 92.1 us -> 91.3 us (level)
  waiting for transfers between devices: 24.9 us -> 22.1 us
  starting transfers between devices: 49.8 us -> 51.8 us
    ppermute x2, starting transfers between devices: 4.49 us -> 7.71 us  [staged_gather(): end = lax.ppermute(across_far, 'blk', SIDES)]
    ppermute x2, waiting for transfers between devices: 2.68 us -> 0.01 us  [staged_gather(): end = lax.ppermute(across_far, 'blk', SIDES)]
    ppermute x8, starting transfers between devices: 6.77 us -> 5.62 us  [swap_bits(): lax.ppermute(block, axis, [(i, i ^ bits) for i in range(lax.axis_size(axi...]
  transfers between devices with their start and end apart: 28 -> 28, of which waited for: 11 -> 9; matrix products, arithmetic and copies ran while one was open for 3% -> 3% of each run, Pallas kernels for 5% -> 5%
where the time goes in v18:
time: 91.3 us; the launch traced here: 90.8 us
  starting transfers between devices  51.8 us (57%)
  waiting for transfers between devices  22.1 us (24%)
  local copies, waits for them, and re-layouts  8.15 us (9%)
  Pallas kernels  7.3 us (8%)
    ppermute x2, starting transfers between devices, staged_gather(): far = lax.ppermute(across, 'blk', SIDES)  9.77 us
    ppermute x2, starting transfers between devices, pair_scatter(): from_side = lax.ppermute(near, axis, SIDES)  9.72 us
    ppermute x2, waiting for transfers between devices, pair_scatter(): from_side = lax.ppermute(near, axis, SIDES)  8.86 us
    ppermute x2, starting transfers between devices, staged_gather(): end = lax.ppermute(across_far, 'blk', SIDES)  7.71 us
    ppermute x8, waiting for transfers between devices, swap_bits(): lax.ppermute(block, axis, [(i, i ^ bits) for i in range(lax.axis_size(axi...  6.81 us
    ppermute x2, starting transfers between devices, staged_gather(): lax.ppermute(one, 'blk', SIDES)  6.09 us
    unnamed x10, local copies, waits for them, and re-layouts  5.63 us
    ppermute x8, starting transfers between devices, swap_bits(): lax.ppermute(block, axis, [(i, i ^ bits) for i in range(lax.axis_size(axi...  5.62 us
  transfers between devices with their start and end apart: 28, of which 9 were waited for; matrix products, arithmetic and copies ran while one was open for 3% of the time, Pallas kernels for 5%

profile of v18, /device:TPU:0, one launch (start us, length us, event | category | flops | bytes accessed | tf_op | source)
XLA Modules:
  0.0 90.8 jit_solution(16534473351165571092)
XLA Ops:
  1.1 2.6 %collective-permute-start.10 = (bf16[96,8192]{1,0:T(8,128)(2,1)}, bf16[96,8192]{1,0:T(8,128)(2,1)S(1)}, u32[]{:S(2)}, u32[]{:S(2)}) collective-permute-start(bf16[96,8192]{1,0:T(8,128)(2,1)} %refs_0_.1), channel_id=1, source_target_pairs={{0,2},{1,3},{2,0},{3,1},{4,6},{5,7},{6,4},{7,5},{8,10},{9,11},{10,... | collective-permute-start | bytes 4718600 | tf_op jit(solution)/shard_map/ppermute | solution.py:20
  4.7 1.6 %collective-permute-start.1 = (bf16[32,4608]{1,0:T(8,128)(2,1)S(1)}, bf16[32,4608]{1,0:T(8,128)(2,1)S(1)}, u32[]{:S(2)}, u32[]{:S(2)}) collective-permute-start(bf16[32,4608]{1,0:T(8,128)(2,1)S(1)} %slice.8.refs_2_), channel_id=1, source_target_pairs={{0,4},{4,0},{8,12},{12,8},{1,5},{5,1},{9,13},{13,9},{2,6},{6,2},{1... | collective-permute-start | bytes 884744 | tf_op jit(solution)/shard_map/ppermute | solution.py:43
  8.0 4.4 %collective-permute-start.3 = (bf16[32,3584]{1,0:T(8,128)(2,1)S(1)}, bf16[32,3584]{1,0:T(8,128)(2,1)S(1)}, u32[]{:S(2)}, u32[]{:S(2)}) collective-permute-start(bf16[32,3584]{1,0:T(8,128)(2,1)S(1)} %slice.9.refs_3_), channel_id=1, source_target_pairs={{0,4},{4,0},{8,12},{12,8},{1,5},{5,1},{9,13},{13,9},{2,6},{6,2},{1... | collective-permute-start | bytes 688136 | tf_op jit(solution)/shard_map/ppermute | solution.py:43
  12.4 2.2 %collective-permute-done.1.refs_4_ = bf16[32,4608]{1,0:T(8,128)(2,1)S(1)} collective-permute-done((bf16[32,4608]{1,0:T(8,128)(2,1)S(1)}, bf16[32,4608]{1,0:T(8,128)(2,1)S(1)}, u32[]{:S(2)}, u32[]{:S(2)}) %collective-permute-start.1) | collective-permute-done | bytes 294944 | tf_op jit(solution)/shard_map/ppermute | solution.py:43
  15.3 4.5 %collective-permute-start.7 = (bf16[32,4608]{1,0:T(8,128)(2,1)S(1)}, bf16[32,4608]{1,0:T(8,128)(2,1)S(1)}, u32[]{:S(2)}, u32[]{:S(2)}) collective-permute-start(bf16[32,4608]{1,0:T(8,128)(2,1)S(1)} %collective-permute-done.2.refs_5_), channel_id=1, source_target_pairs={{0,4},{4,0},{8,12},{12,8},{1,5},{5,1},{9,13},{13,9},{2,6},{6,2},{1... | collective-permute-start | bytes 884744 | tf_op jit(solution)/shard_map/ppermute | solution.py:49
  20.4 5.3 %collective-permute-start.5 = (bf16[32,3584]{1,0:T(8,128)(2,1)S(1)}, bf16[32,3584]{1,0:T(8,128)(2,1)S(1)}, u32[]{:S(2)}, u32[]{:S(2)}) collective-permute-start(bf16[32,3584]{1,0:T(8,128)(2,1)S(1)} %collective-permute-done.4.refs_7_), channel_id=1, source_target_pairs={{0,4},{4,0},{8,12},{12,8},{1,5},{5,1},{9,13},{13,9},{2,6},{6,2},{1... | collective-permute-start | bytes 688136 | tf_op jit(solution)/shard_map/ppermute | solution.py:49
  26.4 1.2 %collective-permute-done.7.refs_0_ = bf16[32,4608]{1,0:T(8,128)(2,1)S(1)} collective-permute-done((bf16[32,4608]{1,0:T(8,128)(2,1)S(1)}, bf16[32,4608]{1,0:T(8,128)(2,1)S(1)}, u32[]{:S(2)}, u32[]{:S(2)}) %collective-permute-start.7) | collective-permute-done | bytes 294944 | tf_op jit(solution)/shard_map/ppermute | solution.py:49
  27.7 4.4 %collective-permute-start.12 = (bf16[32,4608]{1,0:T(8,128)(2,1)S(1)}, bf16[32,4608]{1,0:T(8,128)(2,1)S(1)}, u32[]{:S(2)}, u32[]{:S(2)}) collective-permute-start(bf16[32,4608]{1,0:T(8,128)(2,1)S(1)} %collective-permute-done.8.refs_1_), channel_id=1, source_target_pairs={{0,4},{4,0},{8,12},{12,8},{1,5},{5,1},{9,13},{13,9},{2,6},{6,2},{1... | collective-permute-start | bytes 884744 | tf_op jit(solution)/shard_map/ppermute | solution.py:53
  32.1 3.3 %collective-permute-start.13 = (bf16[32,3584]{1,0:T(8,128)(2,1)S(1)}, bf16[32,3584]{1,0:T(8,128)(2,1)S(1)}, u32[]{:S(2)}, u32[]{:S(2)}) collective-permute-start(bf16[32,3584]{1,0:T(8,128)(2,1)S(1)} %collective-permute-done.6.refs_3_), channel_id=1, source_target_pairs={{0,4},{4,0},{8,12},{12,8},{1,5},{5,1},{9,13},{13,9},{2,6},{6,2},{1... | collective-permute-start | bytes 688136 | tf_op jit(solution)/shard_map/ppermute | solution.py:53
  35.4 1.3 %collective-permute-done.9.refs_7_ = s32[2,96]{1,0:T(2,128)S(1)} collective-permute-done((s32[2,96]{1,0:T(2,128)}, s32[2,96]{1,0:T(2,128)S(1)}, u32[]{:S(2)}, u32[]{:S(2)}) %collective-permute-start.9) | collective-permute-done | bytes 800 | tf_op jit(solution)/shard_map/ppermute | solution.py:20
  36.7 1.4 %copy-done.2 = bf16[96,8192]{1,0:T(8,128)(2,1)S(1)} copy-done((bf16[96,8192]{1,0:T(8,128)(2,1)S(1)}, bf16[96,8192]{1,0:T(8,128)(2,1)}, u32[]{:S(2)}) %copy-start.2) | copy-done | bytes 1572888
  39.6 1.1 %stage.1 = (bf16[64,8192]{1,0:T(8,128)(2,1)S(1)}, f32[64,1]{1,0:T(8,128)S(1)}, bf16[192,8192]{1,0:T(8,128)(2,1)S(1)}, f32[1,8192]{1,0:T(1,128)S(1)}, s32[4,96]{1,0:T(4,128)S(1)}) custom-call(bf16[96,8192]{1,0:T(8,128)(2,1)S(1)} %copy-done.2, bf16[96,8192]{1,0:T(8,128)(2,1)S(1)} %collective-permute-done.refs_1_, bf16[32,4608]{1,0:T(8,128)(2,1)S(1)} %slice.8.refs_2_, ...), custom_call_target="tpu_custom_call" | custom-call | flops 4194304 | bytes 12000000 | tf_op jit(solution)/shard_map/stage/pallas_call | solution.py:253
  41.3 3.0 %collective-permute-done.11.refs_6_ = s32[4,96]{1,0:T(4,128)S(1)} collective-permute-done((s32[4,96]{1,0:T(4,128)S(1)}, s32[4,96]{1,0:T(4,128)S(1)}, u32[]{:S(2)}, u32[]{:S(2)}) %collective-permute-start.11) | collective-permute-done | bytes 1568 | tf_op jit(solution)/shard_map/ppermute | solution.py:20
  44.4 2.9 %stage_rest.1 = (bf16[8192,128]{1,0:T(8,128)(2,1)S(1)}, f32[128,1]{1,0:T(8,128)S(1)}, bf16[384,8192]{1,0:T(8,128)(2,1)S(1)}, f32[384,128]{1,0:T(8,128)S(1)}) custom-call(bf16[32,4608]{1,0:T(8,128)(2,1)S(1)} %collective-permute-done.7.refs_0_, bf16[32,4608]{1,0:T(8,128)(2,1)S(1)} %collective-permute-done.8.refs_1_, ...), custom_call_target="tpu_custom_call" | custom-call | flops 8388608 | bytes 12000000 | tf_op jit(solution)/shard_map/stage_rest/pallas_call | solution.py:322
  49.4 1.2 %collective-permute-start.17 = (f32[1,384]{1,0:T(1,128)S(1)}, f32[1,384]{1,0:T(1,128)S(1)}, u32[]{:S(2)}, u32[]{:S(2)}) collective-permute-start(f32[1,384]{1,0:T(1,128)S(1)} %get-tuple-element.72.refs_0_), channel_id=1, source_target_pairs={{0,3},{1,2},{2,1},{3,0},{4,7},{5,6},{6,5},{7,4},{8,11},{9,10},{10,... | collective-permute-start | bytes 4616 | tf_op jit(solution)/shard_map/ppermute | solution.py:20
  50.6 1.9 %collective-permute-done.16.refs_2_ = f32[1,384]{1,0:T(1,128)S(1)} collective-permute-done((f32[1,384]{1,0:T(1,128)S(1)}, f32[1,384]{1,0:T(1,128)S(1)}, u32[]{:S(2)}, u32[]{:S(2)}) %collective-permute-start.16) | collective-permute-done | bytes 1568 | tf_op jit(solution)/shard_map/ppermute | solution.py:20
  54.2 2.8 %copy-done.1 = bf16[384,8192]{1,0:T(8,128)(2,1)S(1)} copy-done((bf16[384,8192]{1,0:T(8,128)(2,1)S(1)}, bf16[384,8192]{1,0:T(8,128)(2,1)}, u32[]{:S(2)}) %copy-start.1) | copy-done | bytes 6291480
  57.7 1.2 %collective-permute-start.19 = (bf16[32,4096]{1,0:T(8,128)(2,1)S(1)}, bf16[32,4096]{1,0:T(8,128)(2,1)S(1)}, u32[]{:S(2)}, u32[]{:S(2)}) collective-permute-start(bf16[32,4096]{1,0:T(8,128)(2,1)S(1)} %get-tuple-element.80), channel_id=1, source_target_pairs={{0,4},{4,0},{8,12},{12,8},{1,5},{5,1},{9,13},{13,9},{2,6},{6,2},{1... | collective-permute-start | bytes 786440 | tf_op jit(solution)/shard_map/ppermute | solution.py:93
  59.5 3.0 %collective-permute-done.18 = bf16[32,4096]{1,0:T(8,128)(2,1)S(1)} collective-permute-done((bf16[32,4096]{1,0:T(8,128)(2,1)S(1)}, bf16[32,4096]{1,0:T(8,128)(2,1)S(1)}, u32[]{:S(2)}, u32[]{:S(2)}) %collective-permute-start.18) | collective-permute-done | bytes 262176 | tf_op jit(solution)/shard_map/ppermute | solution.py:93
  64.1 4.4 %collective-permute-start.22 = (bf16[32,4096]{1,0:T(8,128)(2,1)S(1)}, bf16[32,4096]{1,0:T(8,128)(2,1)S(1)}, u32[]{:S(2)}, u32[]{:S(2)}) collective-permute-start(bf16[32,4096]{1,0:T(8,128)(2,1)S(1)} %get-tuple-element.79), channel_id=1, source_target_pairs={{0,4},{4,0},{8,12},{12,8},{1,5},{5,1},{9,13},{13,9},{2,6},{6,2},{1... | collective-permute-start | bytes 786440 | tf_op jit(solution)/shard_map/ppermute | solution.py:97
  69.4 5.0 %collective-permute-start.25 = (bf16[32,4096]{1,0:T(8,128)(2,1)S(1)}, bf16[32,4096]{1,0:T(8,128)(2,1)S(1)}, u32[]{:S(2)}, u32[]{:S(2)}) collective-permute-start(bf16[32,4096]{1,0:T(8,128)(2,1)S(1)} %fusion.1), channel_id=1, source_target_pairs={{0,4},{4,0},{8,12},{12,8},{1,5},{5,1},{9,13},{13,9},{2,6},{6,2},{1... | collective-permute-start | bytes 786440 | tf_op jit(solution)/shard_map/ppermute | solution.py:103
  75.2 4.8 %collective-permute-start.21 = (bf16[32,4096]{1,0:T(8,128)(2,1)S(1)}, bf16[32,4096]{1,0:T(8,128)(2,1)S(1)}, u32[]{:S(2)}, u32[]{:S(2)}) collective-permute-start(bf16[32,4096]{1,0:T(8,128)(2,1)S(1)} %fusion), channel_id=1, source_target_pairs={{0,4},{4,0},{8,12},{12,8},{1,5},{5,1},{9,13},{13,9},{2,6},{6,2},{1... | collective-permute-start | bytes 786440 | tf_op jit(solution)/shard_map/ppermute | solution.py:103
  80.7 4.2 %collective-permute-done.25 = bf16[32,4096]{1,0:T(8,128)(2,1)S(1)} collective-permute-done((bf16[32,4096]{1,0:T(8,128)(2,1)S(1)}, bf16[32,4096]{1,0:T(8,128)(2,1)S(1)}, u32[]{:S(2)}, u32[]{:S(2)}) %collective-permute-start.25) | collective-permute-done | bytes 262176 | tf_op jit(solution)/shard_map/ppermute | solution.py:103
  85.0 4.7 %collective-permute-done.21 = bf16[32,4096]{1,0:T(8,128)(2,1)S(1)} collective-permute-done((bf16[32,4096]{1,0:T(8,128)(2,1)S(1)}, bf16[32,4096]{1,0:T(8,128)(2,1)S(1)}, u32[]{:S(2)}, u32[]{:S(2)}) %collective-permute-start.21) | collective-permute-done | bytes 262176 | tf_op jit(solution)/shard_map/ppermute | solution.py:103
  (59 shorter events, 17.6 us)
Async XLA Ops:
  0.6 19.1 %collective-permute-start = (bf16[96,8192]{1,0:T(8,128)(2,1)}, bf16[96,8192]{1,0:T(8,128)(2,1)S(1)}, u32[]{:S(2)}, u32[]{:S(2)}) collective-permute-start(bf16[96,8192]{1,0:T(8,128)(2,1)} %refs_0_.1), channel_id=1, source_target_pairs={{0,1},{1,0},{2,3},{3,2},{4,5},{5,4},{6,7},{7,6},{8,9},{9,8},{10,11... | collective-permute-start | bytes 4718600 | tf_op jit(solution)/shard_map/ppermute | solution.py:20
  1.1 39.5 %collective-permute-start.10 = (bf16[96,8192]{1,0:T(8,128)(2,1)}, bf16[96,8192]{1,0:T(8,128)(2,1)S(1)}, u32[]{:S(2)}, u32[]{:S(2)}) collective-permute-start(bf16[96,8192]{1,0:T(8,128)(2,1)} %refs_0_.1), channel_id=1, source_target_pairs={{0,2},{1,3},{2,0},{3,1},{4,6},{5,7},{6,4},{7,5},{8,10},{9,11},{10,... | collective-permute-start | bytes 4718600 | tf_op jit(solution)/shard_map/ppermute | solution.py:20
  4.7 9.9 %collective-permute-start.1 = (bf16[32,4608]{1,0:T(8,128)(2,1)S(1)}, bf16[32,4608]{1,0:T(8,128)(2,1)S(1)}, u32[]{:S(2)}, u32[]{:S(2)}) collective-permute-start(bf16[32,4608]{1,0:T(8,128)(2,1)S(1)} %slice.8.refs_2_), channel_id=1, source_target_pairs={{0,4},{4,0},{8,12},{12,8},{1,5},{5,1},{9,13},{13,9},{2,6},{6,2},{1... | collective-permute-start | bytes 884744 | tf_op jit(solution)/shard_map/ppermute | solution.py:43
  6.3 8.9 %collective-permute-start.2 = (bf16[32,4608]{1,0:T(8,128)(2,1)S(1)}, bf16[32,4608]{1,0:T(8,128)(2,1)S(1)}, u32[]{:S(2)}, u32[]{:S(2)}) collective-permute-start(bf16[32,4608]{1,0:T(8,128)(2,1)S(1)} %slice.8.refs_2_), channel_id=1, source_target_pairs={{4,8},{8,4},{5,9},{9,5},{6,10},{10,6},{7,11},{11,7},{20,24},{24,20... | collective-permute-start | bytes 884744 | tf_op jit(solution)/shard_map/ppermute | solution.py:43
  8.0 12.5 %collective-permute-start.3 = (bf16[32,3584]{1,0:T(8,128)(2,1)S(1)}, bf16[32,3584]{1,0:T(8,128)(2,1)S(1)}, u32[]{:S(2)}, u32[]{:S(2)}) collective-permute-start(bf16[32,3584]{1,0:T(8,128)(2,1)S(1)} %slice.9.refs_3_), channel_id=1, source_target_pairs={{0,4},{4,0},{8,12},{12,8},{1,5},{5,1},{9,13},{13,9},{2,6},{6,2},{1... | collective-permute-start | bytes 688136 | tf_op jit(solution)/shard_map/ppermute | solution.py:43
  14.6 5.8 %collective-permute-start.4 = (bf16[32,3584]{1,0:T(8,128)(2,1)S(1)}, bf16[32,3584]{1,0:T(8,128)(2,1)S(1)}, u32[]{:S(2)}, u32[]{:S(2)}) collective-permute-start(bf16[32,3584]{1,0:T(8,128)(2,1)S(1)} %slice.9.refs_3_), channel_id=1, source_target_pairs={{4,8},{8,4},{5,9},{9,5},{6,10},{10,6},{7,11},{11,7},{20,24},{24,20... | collective-permute-start | bytes 688136 | tf_op jit(solution)/shard_map/ppermute | solution.py:43
  15.3 12.4 %collective-permute-start.7 = (bf16[32,4608]{1,0:T(8,128)(2,1)S(1)}, bf16[32,4608]{1,0:T(8,128)(2,1)S(1)}, u32[]{:S(2)}, u32[]{:S(2)}) collective-permute-start(bf16[32,4608]{1,0:T(8,128)(2,1)S(1)} %collective-permute-done.2.refs_5_), channel_id=1, source_target_pairs={{0,4},{4,0},{8,12},{12,8},{1,5},{5,1},{9,13},{13,9},{2,6},{6,2},{1... | collective-permute-start | bytes 884744 | tf_op jit(solution)/shard_map/ppermute | solution.py:49
  19.8 7.9 %collective-permute-start.8 = (bf16[32,4608]{1,0:T(8,128)(2,1)S(1)}, bf16[32,4608]{1,0:T(8,128)(2,1)S(1)}, u32[]{:S(2)}, u32[]{:S(2)}) collective-permute-start(bf16[32,4608]{1,0:T(8,128)(2,1)S(1)} %collective-permute-done.1.refs_4_), channel_id=1, source_target_pairs={{4,8},{8,4},{5,9},{9,5},{6,10},{10,6},{7,11},{11,7},{20,24},{24,20... | collective-permute-start | bytes 884744 | tf_op jit(solution)/shard_map/ppermute | solution.py:51
  20.4 11.6 %collective-permute-start.5 = (bf16[32,3584]{1,0:T(8,128)(2,1)S(1)}, bf16[32,3584]{1,0:T(8,128)(2,1)S(1)}, u32[]{:S(2)}, u32[]{:S(2)}) collective-permute-start(bf16[32,3584]{1,0:T(8,128)(2,1)S(1)} %collective-permute-done.4.refs_7_), channel_id=1, source_target_pairs={{0,4},{4,0},{8,12},{12,8},{1,5},{5,1},{9,13},{13,9},{2,6},{6,2},{1... | collective-permute-start | bytes 688136 | tf_op jit(solution)/shard_map/ppermute | solution.py:49
  25.8 6.3 %collective-permute-start.6 = (bf16[32,3584]{1,0:T(8,128)(2,1)S(1)}, bf16[32,3584]{1,0:T(8,128)(2,1)S(1)}, u32[]{:S(2)}, u32[]{:S(2)}) collective-permute-start(bf16[32,3584]{1,0:T(8,128)(2,1)S(1)} %collective-permute-done.3.refs_5_), channel_id=1, source_target_pairs={{4,8},{8,4},{5,9},{9,5},{6,10},{10,6},{7,11},{11,7},{20,24},{24,20... | collective-permute-start | bytes 688136 | tf_op jit(solution)/shard_map/ppermute | solution.py:51
  27.7 16.7 %collective-permute-start.12 = (bf16[32,4608]{1,0:T(8,128)(2,1)S(1)}, bf16[32,4608]{1,0:T(8,128)(2,1)S(1)}, u32[]{:S(2)}, u32[]{:S(2)}) collective-permute-start(bf16[32,4608]{1,0:T(8,128)(2,1)S(1)} %collective-permute-done.8.refs_1_), channel_id=1, source_target_pairs={{0,4},{4,0},{8,12},{12,8},{1,5},{5,1},{9,13},{13,9},{2,6},{6,2},{1... | collective-permute-start | bytes 884744 | tf_op jit(solution)/shard_map/ppermute | solution.py:53
  32.1 12.3 %collective-permute-start.13 = (bf16[32,3584]{1,0:T(8,128)(2,1)S(1)}, bf16[32,3584]{1,0:T(8,128)(2,1)S(1)}, u32[]{:S(2)}, u32[]{:S(2)}) collective-permute-start(bf16[32,3584]{1,0:T(8,128)(2,1)S(1)} %collective-permute-done.6.refs_3_), channel_id=1, source_target_pairs={{0,4},{4,0},{8,12},{12,8},{1,5},{5,1},{9,13},{13,9},{2,6},{6,2},{1... | collective-permute-start | bytes 688136 | tf_op jit(solution)/shard_map/ppermute | solution.py:53
  40.7 3.7 %collective-permute-start.11 = (s32[4,96]{1,0:T(4,128)S(1)}, s32[4,96]{1,0:T(4,128)S(1)}, u32[]{:S(2)}, u32[]{:S(2)}) collective-permute-start(s32[4,96]{1,0:T(4,128)S(1)} %get-tuple-element.54.refs_5_), channel_id=1, source_target_pairs={{0,2},{1,3},{2,0},{3,1},{4,6},{5,7},{6,4},{7,5},{8,10},{9,11},{10,... | collective-permute-start | bytes 4616 | tf_op jit(solution)/shard_map/ppermute | solution.py:20
  48.9 3.6 %collective-permute-start.16 = (f32[1,384]{1,0:T(1,128)S(1)}, f32[1,384]{1,0:T(1,128)S(1)}, u32[]{:S(2)}, u32[]{:S(2)}) collective-permute-start(f32[1,384]{1,0:T(1,128)S(1)} %get-tuple-element.72.refs_0_), channel_id=1, source_target_pairs={{0,2},{1,3},{2,0},{3,1},{4,6},{5,7},{6,4},{7,5},{8,10},{9,11},{10,... | collective-permute-start | bytes 4616 | tf_op jit(solution)/shard_map/ppermute | solution.py:20
  53.2 9.2 %collective-permute-start.18 = (bf16[32,4096]{1,0:T(8,128)(2,1)S(1)}, bf16[32,4096]{1,0:T(8,128)(2,1)S(1)}, u32[]{:S(2)}, u32[]{:S(2)}) collective-permute-start(bf16[32,4096]{1,0:T(8,128)(2,1)S(1)} %get-tuple-element.78), channel_id=1, source_target_pairs={{0,4},{4,0},{8,12},{12,8},{1,5},{5,1},{9,13},{13,9},{2,6},{6,2},{1... | collective-permute-start | bytes 786440 | tf_op jit(solution)/shard_map/ppermute | solution.py:93
  57.7 10.8 %collective-permute-start.19 = (bf16[32,4096]{1,0:T(8,128)(2,1)S(1)}, bf16[32,4096]{1,0:T(8,128)(2,1)S(1)}, u32[]{:S(2)}, u32[]{:S(2)}) collective-permute-start(bf16[32,4096]{1,0:T(8,128)(2,1)S(1)} %get-tuple-element.80), channel_id=1, source_target_pairs={{0,4},{4,0},{8,12},{12,8},{1,5},{5,1},{9,13},{13,9},{2,6},{6,2},{1... | collective-permute-start | bytes 786440 | tf_op jit(solution)/shard_map/ppermute | solution.py:93
  62.5 11.9 %collective-permute-start.26 = (bf16[32,4096]{1,0:T(8,128)(2,1)S(1)}, bf16[32,4096]{1,0:T(8,128)(2,1)S(1)}, u32[]{:S(2)}, u32[]{:S(2)}) collective-permute-start(bf16[32,4096]{1,0:T(8,128)(2,1)S(1)} %get-tuple-element.83), channel_id=1, source_target_pairs={{0,4},{4,0},{8,12},{12,8},{1,5},{5,1},{9,13},{13,9},{2,6},{6,2},{1... | collective-permute-start | bytes 786440 | tf_op jit(solution)/shard_map/ppermute | solution.py:97
  63.4 5.9 %collective-permute-start.24 = (bf16[32,4096]{1,0:T(8,128)(2,1)S(1)}, bf16[32,4096]{1,0:T(8,128)(2,1)S(1)}, u32[]{:S(2)}, u32[]{:S(2)}) collective-permute-start(bf16[32,4096]{1,0:T(8,128)(2,1)S(1)} %add_convert_fusion.2), channel_id=1, source_target_pairs={{4,8},{8,4},{5,9},{9,5},{6,10},{10,6},{7,11},{11,7},{20,24},{24,20... | collective-permute-start | bytes 786440 | tf_op jit(solution)/shard_map/ppermute | solution.py:100
  64.1 15.9 %collective-permute-start.22 = (bf16[32,4096]{1,0:T(8,128)(2,1)S(1)}, bf16[32,4096]{1,0:T(8,128)(2,1)S(1)}, u32[]{:S(2)}, u32[]{:S(2)}) collective-permute-start(bf16[32,4096]{1,0:T(8,128)(2,1)S(1)} %get-tuple-element.79), channel_id=1, source_target_pairs={{0,4},{4,0},{8,12},{12,8},{1,5},{5,1},{9,13},{13,9},{2,6},{6,2},{1... | collective-permute-start | bytes 786440 | tf_op jit(solution)/shard_map/ppermute | solution.py:97
  68.6 6.5 %collective-permute-start.20 = (bf16[32,4096]{1,0:T(8,128)(2,1)S(1)}, bf16[32,4096]{1,0:T(8,128)(2,1)S(1)}, u32[]{:S(2)}, u32[]{:S(2)}) collective-permute-start(bf16[32,4096]{1,0:T(8,128)(2,1)S(1)} %add_convert_fusion.5), channel_id=1, source_target_pairs={{4,8},{8,4},{5,9},{9,5},{6,10},{10,6},{7,11},{11,7},{20,24},{24,20... | collective-permute-start | bytes 786440 | tf_op jit(solution)/shard_map/ppermute | solution.py:100
  69.4 15.5 %collective-permute-start.25 = (bf16[32,4096]{1,0:T(8,128)(2,1)S(1)}, bf16[32,4096]{1,0:T(8,128)(2,1)S(1)}, u32[]{:S(2)}, u32[]{:S(2)}) collective-permute-start(bf16[32,4096]{1,0:T(8,128)(2,1)S(1)} %fusion.1), channel_id=1, source_target_pairs={{0,4},{4,0},{8,12},{12,8},{1,5},{5,1},{9,13},{13,9},{2,6},{6,2},{1... | collective-permute-start | bytes 786440 | tf_op jit(solution)/shard_map/ppermute | solution.py:103
  74.4 10.5 %collective-permute-start.27 = (bf16[32,4096]{1,0:T(8,128)(2,1)S(1)}, bf16[32,4096]{1,0:T(8,128)(2,1)S(1)}, u32[]{:S(2)}, u32[]{:S(2)}) collective-permute-start(bf16[32,4096]{1,0:T(8,128)(2,1)S(1)} %add_convert_fusion), channel_id=1, source_target_pairs={{4,8},{8,4},{5,9},{9,5},{6,10},{10,6},{7,11},{11,7},{20,24},{24,20... | collective-permute-start | bytes 786440 | tf_op jit(solution)/shard_map/ppermute | solution.py:101
  75.2 14.5 %collective-permute-start.21 = (bf16[32,4096]{1,0:T(8,128)(2,1)S(1)}, bf16[32,4096]{1,0:T(8,128)(2,1)S(1)}, u32[]{:S(2)}, u32[]{:S(2)}) collective-permute-start(bf16[32,4096]{1,0:T(8,128)(2,1)S(1)} %fusion), channel_id=1, source_target_pairs={{0,4},{4,0},{8,12},{12,8},{1,5},{5,1},{9,13},{13,9},{2,6},{6,2},{1... | collective-permute-start | bytes 786440 | tf_op jit(solution)/shard_map/ppermute | solution.py:103
  80.1 9.7 %collective-permute-start.23 = (bf16[32,4096]{1,0:T(8,128)(2,1)S(1)}, bf16[32,4096]{1,0:T(8,128)(2,1)S(1)}, u32[]{:S(2)}, u32[]{:S(2)}) collective-permute-start(bf16[32,4096]{1,0:T(8,128)(2,1)S(1)} %add_convert_fusion.3), channel_id=1, source_target_pairs={{4,8},{8,4},{5,9},{9,5},{6,10},{10,6},{7,11},{11,7},{20,24},{24,20... | collective-permute-start | bytes 786440 | tf_op jit(solution)/shard_map/ppermute | solution.py:101
  (9 other events, 19.9 us)

commit v19 on v16

--- a/solution.py
+++ b/solution.py
@@ -33,7 +33,7 @@
     return (one.astype(jnp.float32) + other.astype(jnp.float32)).astype(jnp.bfloat16)
 
 
-def staged_gather(block, images, noise, routes, near_bits, far_bit):
+def staged_gather(block, images, noise, near_bits, far_bit):
     cut = block.shape[1] // 16 * 9
     cuts = [block[:, :cut], block[:, cut:]]
     crossed = swap_bits(images, "reader", far_bit)
@@ -61,26 +61,19 @@
         end_parts.append([end, across])
     weighted, penalty, staged_near, noise = early
     ends = [parts[0] for parts in end_parts]
-    routes, crossed = lax.optimization_barrier((routes, crossed))
-    routes = swap_all(routes)
-    crossed, *rest = lax.optimization_barrier((crossed, *routes, *ends))
-    routes = rest[: len(routes)]
+    crossed, *_ = lax.optimization_barrier((crossed, *ends))
     far = swap_gather(crossed, "reader", near_bits)
     staged = stage_rest([far_parts, end_parts], staged_near, crossed, weighted, penalty, noise)
-    return staged, far[1:], routes
-
-
-def swap_all(routes):
-    return [routes] + [swap_bits(routes, "reader", k) for k in range(1, lax.axis_size("reader"))]
-
-
-def plain_gather(block, images, noise, routes, near_bits, far_bit):
+    return staged, far[1:]
+
+
+def plain_gather(block, images, noise, near_bits, far_bit):
     near = swap_gather(images, "reader", near_bits)
     far = swap_gather(swap_bits(images, "reader", far_bit), "reader", near_bits)
     line = [[[one]] for one in line_gather(block, "blk")]
     weighted, penalty, near, noise = stage(line[:2], near, noise)
     staged = stage_rest(line[2:], near, far[0], weighted, penalty, noise)
-    return staged, far[1:], swap_all(routes)
+    return staged, far[1:]
 
 
 def line_gather(block, axis):
@@ -344,14 +337,20 @@
     )(*moved, near, crossed, weighted, penalty, noise)
 
 
+def write_packet(packet_ref, scores, route_ref):
+    top, rows = route_ref.shape
+    packet_ref[0:1, :] = column_lse(scores)
+    packet_ref[1:2, :] = jnp.zeros((1, packet_ref.shape[1]), jnp.float32)
+    for t in range(top):
+        packet_ref[1:2, t * rows : (t + 1) * rows] = route_ref[t : t + 1, :].astype(jnp.float32)
+
+
 def score_kernel(readers, finish, *refs):
     refs = list(refs)
     half = readers // 2
     far_refs = [refs.pop(0) for _ in range(half - 1)]
-    turned_ref, penalty_ref, _, product_ref = [refs.pop(0) for _ in range(4)]
-    route_refs = [refs.pop(0) for _ in range(readers)]
-    score_ref, mask_ref, lse_ref, all_ref, sum_ref, image_sems = refs
-    reader = lax.axis_index("reader")
+    turned_ref, penalty_ref, _, product_ref, route_ref = refs[:5]
+    score_ref, packet_ref, all_ref, sum_ref, image_sems = refs[5:]
     placed = [
         place_images(half + 1 + i, ref, all_ref, image_sems.at[i])
         for i, ref in enumerate(far_refs)
@@ -363,21 +362,10 @@
         sum_ref[place, :] = jnp.dot(
             ref[...], turned_ref[...], preferred_element_type=jnp.float32
         )
-    rows = route_refs[0].shape[1]
-    routes = [ref[...] for ref in route_refs]
-    bit = 1
-    while bit < readers:
-        flip = (reader & bit) > 0
-        routes = [jnp.where(flip, routes[k ^ bit], one) for k, one in enumerate(routes)]
-        bit *= 2
-    for j, route in enumerate(routes):
-        for k in range(readers):
-            hits = jnp.where(route == (reader ^ k), 1.0, 0.0)
-            mask_ref[k : k + 1, j * rows : (j + 1) * rows] = jnp.max(hits, axis=0, keepdims=True)
     scores = sum_ref[...].T - penalty_ref[...]
     score_ref[...] = scores
     if finish:
-        lse_ref[...] = column_lse(scores)
+        write_packet(packet_ref, scores, route_ref)
     for copy, _ in placed:
         copy.wait()
 
@@ -386,22 +374,20 @@
     turned, penalty, images, products = staged
     width, refs = turned.shape
     slots, rows = images.shape[0], far[0].shape[0]
-    readers = slots // rows
     return pl.pallas_call(
-        partial(score_kernel, readers, finish),
+        partial(score_kernel, slots // rows, finish),
         out_shape=(
             jax.ShapeDtypeStruct((refs, slots), jnp.float32),
-            jax.ShapeDtypeStruct((readers, slots), jnp.float32),
-            jax.ShapeDtypeStruct((1, slots), jnp.float32),
+            jax.ShapeDtypeStruct((2, slots), jnp.float32),
             jax.ShapeDtypeStruct((slots, width), jnp.bfloat16),
         ),
-        in_specs=[VMEM_SPEC] * (len(far) + 4 + len(routes)),
-        out_specs=(VMEM_SPEC,) * 4,
+        in_specs=[VMEM_SPEC] * (len(far) + 5),
+        out_specs=(VMEM_SPEC,) * 3,
         scratch_shapes=[
             pltpu.VMEM((slots, refs), jnp.float32),
             pltpu.SemaphoreType.DMA((len(far),)),
         ],
-        input_output_aliases={len(far) + 2: 3},
+        input_output_aliases={len(far) + 2: 2},
         compiler_params=pltpu.CompilerParams(vmem_limit_bytes=SCORE_VMEM),
         cost_estimate=pl.CostEstimate(
             flops=2 * refs * slots * width,
@@ -409,19 +395,38 @@
             transcendentals=0,
         ),
         name="scores",
-    )(*far, turned, penalty, images, products, *routes)
-
-
-def lse_kernel(score_ref, lse_ref):
-    lse_ref[...] = column_lse(score_ref[...])
-
-
-def group_lse(scores):
+    )(*far, turned, penalty, images, products, routes)
+
+
+def packet_kernel(score_ref, route_ref, packet_ref):
+    write_packet(packet_ref, score_ref[...], route_ref)
+
+
+def make_packet(scores, routes):
     return pl.pallas_call(
-        lse_kernel,
-        out_shape=jax.ShapeDtypeStruct((1, scores.shape[1]), jnp.float32),
-        name="group_lse",
-    )(scores)
+        packet_kernel,
+        out_shape=jax.ShapeDtypeStruct((2, scores.shape[1]), jnp.float32),
+        name="packet",
+    )(scores, routes)
+
+
+def write_masks(packets, rows, top, mask_ref):
+    reader = lax.axis_index("reader")
+    readers = len(packets)
+    for t in range(top):
+        routes = [ref[1:2, t * rows : (t + 1) * rows] for ref in packets]
+        bit = 1
+        while bit < readers:
+            flip = (reader & bit) > 0
+            routes = [jnp.where(flip, routes[k ^ bit], one) for k, one in enumerate(routes)]
+            bit *= 2
+        for j, route in enumerate(routes):
+            columns = slice(j * rows, (j + 1) * rows)
+            for k in range(readers):
+                hits = jnp.where(route == (reader ^ k).astype(jnp.float32), 1.0, 0.0)
+                if t:
+                    hits = jnp.maximum(hits, mask_ref[k : k + 1, columns])
+                mask_ref[k : k + 1, columns] = hits
 
 
 def emit_sums(posterior, all_ref, piece, out_refs):
@@ -431,11 +436,15 @@
         out_ref[...] = sums[s * count : (s + 1) * count].astype(out_ref.dtype)
 
 
-def first_sums_kernel(readers, piece, all_ref, score_ref, mask_ref, *refs):
-    lse_refs, norm_ref, post_ref = refs[:readers], refs[readers], refs[readers + 1]
+def first_sums_kernel(readers, top, piece, all_ref, score_ref, *refs):
+    refs = list(refs)
+    packets = [refs.pop(0) for _ in range(readers)]
+    mask_ref = refs.pop()
+    norm_ref, post_ref, *out_refs = refs
+    write_masks(packets, packets[0].shape[1] // readers, top, mask_ref)
     kept = []
-    for k, lse_ref in enumerate(lse_refs):
-        kept.append(jnp.where(mask_ref[k : k + 1, :] > 0.0, lse_ref[...], -jnp.inf))
+    for k, packet in enumerate(packets):
+        kept.append(jnp.where(mask_ref[k : k + 1, :] > 0.0, packet[0:1, :], -jnp.inf))
     highest = kept[0]
     for value in kept[1:]:
         highest = jnp.maximum(highest, value)
@@ -447,14 +456,14 @@
     exponent = jnp.where(mask_ref[0:1, :] > 0.0, score_ref[...] - norm, -jnp.inf)
     posterior = jnp.exp(exponent).astype(jnp.bfloat16)
     post_ref[...] = posterior
-    emit_sums(posterior, all_ref, piece, refs[readers + 2 :])
+    emit_sums(posterior, all_ref, piece, out_refs)
 
 
 def later_sums_kernel(piece, all_ref, post_ref, *out_refs):
     emit_sums(post_ref[...], all_ref, piece, out_refs)
 
 
-def group_sums(kernel, piece, members, all_images, operands, extra):
+def group_sums(kernel, piece, members, all_images, operands, extra, scratch=()):
     refs, slots = operands[0].shape
     width = piece.stop - piece.start
     block = jax.ShapeDtypeStruct((refs // members, width), jnp.bfloat16)
@@ -463,6 +472,7 @@
         out_shape=tuple(extra) + (block,) * members,
         in_specs=[VMEM_SPEC] * (1 + len(operands)),
         out_specs=(VMEM_SPEC,) * (len(extra) + members),
+        scratch_shapes=scratch,
         compiler_params=pltpu.CompilerParams(vmem_limit_bytes=SUMS_VMEM),
         cost_estimate=pl.CostEstimate(
             flops=2 * refs * slots * width,
@@ -482,27 +492,26 @@
     noise = noise_weights.reshape(1, width)
 
     gather = staged_gather if members == 4 and rows % 32 == 0 and readers > 1 else plain_gather
-    staged, far, all_routes = gather(
-        projections[0], images, noise, routes.T, readers // 4, readers // 2
-    )
+    staged, far = gather(projections[0], images, noise, readers // 4, readers // 2)
     split = lax.axis_size("sub") > 1
-    scores, masks, mine, all_images = all_scores(staged, far, all_routes, not split)
+    scores, mine, all_images = all_scores(staged, far, routes.T, not split)
     if split:
         scores = lax.psum(scores, "sub")
-        mine = group_lse(scores)
-    lses = [mine] + [swap_bits(mine, "reader", k) for k in range(1, readers)]
+        mine = make_packet(scores, routes.T)
+    packets = [mine] + [swap_bits(mine, "reader", k) for k in range(1, readers)]
     pieces = [slice(0, width // 2), slice(width // 2, width)]
     extra = (
         jax.ShapeDtypeStruct((1, scores.shape[1]), jnp.float32),
         jax.ShapeDtypeStruct(scores.shape, jnp.bfloat16),
     )
     (norms, posterior), first = group_sums(
-        partial(first_sums_kernel, readers, pieces[0]),
+        partial(first_sums_kernel, readers, routes.shape[1], pieces[0]),
         pieces[0],
         members,
         all_images,
-        (scores, masks, *lses),
+        (scores, *packets),
         extra,
+        (pltpu.VMEM((readers, scores.shape[1]), jnp.float32),),
     )
     _, last = group_sums(
         partial(later_sums_kernel, pieces[1]), pieces[1], members, all_images, (posterior,), ()

time: 90.7 us -> 89.4 us (0.986)
  starting transfers between devices: 50.9 us -> 47.8 us
  waiting for transfers between devices: 23.1 us -> 24.4 us
    ppermute x2, waiting for transfers between devices: 0.01 us -> 2.79 us  [staged_gather(): end = lax.ppermute(across_far, 'blk', SIDES)]
    ppermute x9 -> x6, waiting for transfers between devices: 8.6 us -> 5.9 us  [swap_bits(): lax.ppermute(block, axis, [(i, i ^ bits) for i in range(lax.axis_size(axi...]
    ppermute x9 -> x6, starting transfers between devices: 7.14 us -> 5.01 us  [swap_bits(): lax.ppermute(block, axis, [(i, i ^ bits) for i in range(lax.axis_size(axi...]
    ppermute x2, waiting for transfers between devices: 8.23 us -> 9.39 us  [pair_scatter(): from_side = lax.ppermute(near, axis, SIDES)]
  transfers between devices with their start and end apart: 29 -> 26, of which waited for: 10 -> 9; matrix products, arithmetic and copies ran while one was open for 3% -> 3% of each run, Pallas kernels for 5% -> 5%
where the time goes in v19:
time: 89.4 us; the launch traced here: 89 us
  starting transfers between devices  47.8 us (53%)
  waiting for transfers between devices  24.4 us (27%)
  Pallas kernels  7.75 us (9%)
  local copies, waits for them, and re-layouts  7.48 us (8%)
    ppermute x2, starting transfers between devices, staged_gather(): far = lax.ppermute(across, 'blk', SIDES)  9.77 us
    ppermute x2, starting transfers between devices, pair_scatter(): from_side = lax.ppermute(near, axis, SIDES)  9.51 us
    ppermute x2, waiting for transfers between devices, pair_scatter(): from_side = lax.ppermute(near, axis, SIDES)  9.39 us
    ppermute x2, starting transfers between devices, staged_gather(): lax.ppermute(one, 'blk', SIDES)  6.09 us
    ppermute x6, waiting for transfers between devices, swap_bits(): lax.ppermute(block, axis, [(i, i ^ bits) for i in range(lax.axis_size(axi...  5.9 us
    ppermute x2, starting transfers between devices, pair_scatter(): for_far_middle = [lax.ppermute(part, axis, SIDES) for part in second]  5.36 us
    ppermute x6, starting transfers between devices, swap_bits(): lax.ppermute(block, axis, [(i, i ^ bits) for i in range(lax.axis_size(axi...  5.01 us
    unnamed x10, local copies, waits for them, and re-layouts  4.96 us
  transfers between devices with their start and end apart: 26, of which 9 were waited for; matrix products, arithmetic and copies ran while one was open for 3% of the time, Pallas kernels for 5%

profile of v19, /device:TPU:0, one launch (start us, length us, event | category | flops | bytes accessed | tf_op | source)
XLA Modules:
  0.0 89.0 jit_solution(10129697230685212879)
XLA Ops:
  1.1 2.6 %collective-permute-start = (bf16[96,8192]{1,0:T(8,128)(2,1)}, bf16[96,8192]{1,0:T(8,128)(2,1)S(1)}, u32[]{:S(2)}, u32[]{:S(2)}) collective-permute-start(bf16[96,8192]{1,0:T(8,128)(2,1)} %refs_0_.1), channel_id=1, source_target_pairs={{0,2},{1,3},{2,0},{3,1},{4,6},{5,7},{6,4},{7,5},{8,10},{9,11},{10,... | collective-permute-start | bytes 4718600 | tf_op jit(solution)/shard_map/ppermute | solution.py:20
  4.7 1.6 %collective-permute-start.1 = (bf16[32,4608]{1,0:T(8,128)(2,1)S(1)}, bf16[32,4608]{1,0:T(8,128)(2,1)S(1)}, u32[]{:S(2)}, u32[]{:S(2)}) collective-permute-start(bf16[32,4608]{1,0:T(8,128)(2,1)S(1)} %slice.8.refs_2_), channel_id=1, source_target_pairs={{0,4},{4,0},{8,12},{12,8},{1,5},{5,1},{9,13},{13,9},{2,6},{6,2},{1... | collective-permute-start | bytes 884744 | tf_op jit(solution)/shard_map/ppermute | solution.py:43
  8.0 4.4 %collective-permute-start.7 = (bf16[32,3584]{1,0:T(8,128)(2,1)S(1)}, bf16[32,3584]{1,0:T(8,128)(2,1)S(1)}, u32[]{:S(2)}, u32[]{:S(2)}) collective-permute-start(bf16[32,3584]{1,0:T(8,128)(2,1)S(1)} %slice.9.refs_3_), channel_id=1, source_target_pairs={{0,4},{4,0},{8,12},{12,8},{1,5},{5,1},{9,13},{13,9},{2,6},{6,2},{1... | collective-permute-start | bytes 688136 | tf_op jit(solution)/shard_map/ppermute | solution.py:43
  12.4 2.2 %collective-permute-done.1.refs_4_ = bf16[32,4608]{1,0:T(8,128)(2,1)S(1)} collective-permute-done((bf16[32,4608]{1,0:T(8,128)(2,1)S(1)}, bf16[32,4608]{1,0:T(8,128)(2,1)S(1)}, u32[]{:S(2)}, u32[]{:S(2)}) %collective-permute-start.1) | collective-permute-done | bytes 294944 | tf_op jit(solution)/shard_map/ppermute | solution.py:43
  15.3 4.5 %collective-permute-start.3 = (bf16[32,4608]{1,0:T(8,128)(2,1)S(1)}, bf16[32,4608]{1,0:T(8,128)(2,1)S(1)}, u32[]{:S(2)}, u32[]{:S(2)}) collective-permute-start(bf16[32,4608]{1,0:T(8,128)(2,1)S(1)} %collective-permute-done.2.refs_5_), channel_id=1, source_target_pairs={{0,4},{4,0},{8,12},{12,8},{1,5},{5,1},{9,13},{13,9},{2,6},{6,2},{1... | collective-permute-start | bytes 884744 | tf_op jit(solution)/shard_map/ppermute | solution.py:52
  20.4 5.3 %collective-permute-start.9 = (bf16[32,3584]{1,0:T(8,128)(2,1)S(1)}, bf16[32,3584]{1,0:T(8,128)(2,1)S(1)}, u32[]{:S(2)}, u32[]{:S(2)}) collective-permute-start(bf16[32,3584]{1,0:T(8,128)(2,1)S(1)} %collective-permute-done.8.refs_7_), channel_id=1, source_target_pairs={{0,4},{4,0},{8,12},{12,8},{1,5},{5,1},{9,13},{13,9},{2,6},{6,2},{1... | collective-permute-start | bytes 688136 | tf_op jit(solution)/shard_map/ppermute | solution.py:52
  26.4 1.2 %collective-permute-done.3.refs_0_ = bf16[32,4608]{1,0:T(8,128)(2,1)S(1)} collective-permute-done((bf16[32,4608]{1,0:T(8,128)(2,1)S(1)}, bf16[32,4608]{1,0:T(8,128)(2,1)S(1)}, u32[]{:S(2)}, u32[]{:S(2)}) %collective-permute-start.3) | collective-permute-done | bytes 294944 | tf_op jit(solution)/shard_map/ppermute | solution.py:52
  27.7 4.4 %collective-permute-start.6 = (bf16[32,4608]{1,0:T(8,128)(2,1)S(1)}, bf16[32,4608]{1,0:T(8,128)(2,1)S(1)}, u32[]{:S(2)}, u32[]{:S(2)}) collective-permute-start(bf16[32,4608]{1,0:T(8,128)(2,1)S(1)} %collective-permute-done.5.refs_1_), channel_id=1, source_target_pairs={{0,4},{4,0},{8,12},{12,8},{1,5},{5,1},{9,13},{13,9},{2,6},{6,2},{1... | collective-permute-start | bytes 884744 | tf_op jit(solution)/shard_map/ppermute | solution.py:59
  32.1 1.4 %copy-done.2 = bf16[96,8192]{1,0:T(8,128)(2,1)S(1)} copy-done((bf16[96,8192]{1,0:T(8,128)(2,1)S(1)}, bf16[96,8192]{1,0:T(8,128)(2,1)}, u32[]{:S(2)}) %copy-start.2) | copy-done | bytes 1572888
  35.5 3.4 %collective-permute-done.refs_9_ = bf16[96,8192]{1,0:T(8,128)(2,1)S(1)} collective-permute-done((bf16[96,8192]{1,0:T(8,128)(2,1)}, bf16[96,8192]{1,0:T(8,128)(2,1)S(1)}, u32[]{:S(2)}, u32[]{:S(2)}) %collective-permute-start) | collective-permute-done | bytes 1572896 | tf_op jit(solution)/shard_map/ppermute | solution.py:20
  38.9 2.8 %collective-permute-done.11.refs_6_ = bf16[32,3584]{1,0:T(8,128)(2,1)S(1)} collective-permute-done((bf16[32,3584]{1,0:T(8,128)(2,1)S(1)}, bf16[32,3584]{1,0:T(8,128)(2,1)S(1)}, u32[]{:S(2)}, u32[]{:S(2)}) %collective-permute-start.11) | collective-permute-done | bytes 229408 | tf_op jit(solution)/shard_map/ppermute | solution.py:59
  41.7 2.8 %stage_rest.1 = (bf16[8192,128]{1,0:T(8,128)(2,1)S(1)}, f32[128,1]{1,0:T(8,128)S(1)}, bf16[384,8192]{1,0:T(8,128)(2,1)S(1)}, f32[384,128]{1,0:T(8,128)S(1)}) custom-call(bf16[32,4608]{1,0:T(8,128)(2,1)S(1)} %collective-permute-done.3.refs_0_, bf16[32,4608]{1,0:T(8,128)(2,1)S(1)} %collective-permute-done.5.refs_1_, ...), custom_call_target="tpu_custom_call" | custom-call | flops 8388608 | bytes 12000000 | tf_op jit(solution)/shard_map/stage_rest/pallas_call | solution.py:316
  46.8 1.2 %collective-permute-start.15 = (f32[2,384]{1,0:T(2,128)S(1)}, f32[2,384]{1,0:T(2,128)S(1)}, u32[]{:S(2)}, u32[]{:S(2)}) collective-permute-start(f32[2,384]{1,0:T(2,128)S(1)} %get-tuple-element.66.refs_0_), channel_id=1, source_target_pairs={{0,3},{1,2},{2,1},{3,0},{4,7},{5,6},{6,5},{7,4},{8,11},{9,10},{10,... | collective-permute-start | bytes 9224 | tf_op jit(solution)/shard_map/ppermute | solution.py:20
  47.9 1.9 %collective-permute-done.14.refs_2_ = f32[2,384]{1,0:T(2,128)S(1)} collective-permute-done((f32[2,384]{1,0:T(2,128)S(1)}, f32[2,384]{1,0:T(2,128)S(1)}, u32[]{:S(2)}, u32[]{:S(2)}) %collective-permute-start.14) | collective-permute-done | bytes 3104 | tf_op jit(solution)/shard_map/ppermute | solution.py:20
  49.8 1.2 %sums.2 = (f32[1,384]{1,0:T(1,128)S(1)}, bf16[128,384]{1,0:T(8,128)(2,1)S(1)}, bf16[32,4096]{1,0:T(8,128)(2,1)S(1)}, bf16[32,4096]{1,0:T(8,128)(2,1)S(1)}, bf16[...) custom-call(bf16[384,8192]{1,0:T(8,128)(2,1)S(1)} %get-tuple-element.64.all_ref, ...), custom_call_target="tpu_custom_call" | custom-call | flops 402653184 | bytes 3145728 | tf_op jit(solution)/shard_map/sums/pallas_call | solution.py:470
  51.1 2.1 %collective-permute-start.16 = (bf16[32,4096]{1,0:T(8,128)(2,1)S(1)}, bf16[32,4096]{1,0:T(8,128)(2,1)S(1)}, u32[]{:S(2)}, u32[]{:S(2)}) collective-permute-start(bf16[32,4096]{1,0:T(8,128)(2,1)S(1)} %get-tuple-element.72), channel_id=1, source_target_pairs={{0,4},{4,0},{8,12},{12,8},{1,5},{5,1},{9,13},{13,9},{2,6},{6,2},{1... | collective-permute-start | bytes 786440 | tf_op jit(solution)/shard_map/ppermute | solution.py:94
  53.2 2.8 %copy-done.1 = bf16[384,8192]{1,0:T(8,128)(2,1)S(1)} copy-done((bf16[384,8192]{1,0:T(8,128)(2,1)S(1)}, bf16[384,8192]{1,0:T(8,128)(2,1)}, u32[]{:S(2)}) %copy-start.1) | copy-done | bytes 6291480
  57.4 2.9 %collective-permute-done.16 = bf16[32,4096]{1,0:T(8,128)(2,1)S(1)} collective-permute-done((bf16[32,4096]{1,0:T(8,128)(2,1)S(1)}, bf16[32,4096]{1,0:T(8,128)(2,1)S(1)}, u32[]{:S(2)}, u32[]{:S(2)}) %collective-permute-start.16) | collective-permute-done | bytes 262176 | tf_op jit(solution)/shard_map/ppermute | solution.py:94
  60.3 2.1 %collective-permute-start.24 = (bf16[32,4096]{1,0:T(8,128)(2,1)S(1)}, bf16[32,4096]{1,0:T(8,128)(2,1)S(1)}, u32[]{:S(2)}, u32[]{:S(2)}) collective-permute-start(bf16[32,4096]{1,0:T(8,128)(2,1)S(1)} %get-tuple-element.77), channel_id=1, source_target_pairs={{0,4},{4,0},{8,12},{12,8},{1,5},{5,1},{9,13},{13,9},{2,6},{6,2},{1... | collective-permute-start | bytes 786440 | tf_op jit(solution)/shard_map/ppermute | solution.py:98
  63.1 3.3 %collective-permute-start.20 = (bf16[32,4096]{1,0:T(8,128)(2,1)S(1)}, bf16[32,4096]{1,0:T(8,128)(2,1)S(1)}, u32[]{:S(2)}, u32[]{:S(2)}) collective-permute-start(bf16[32,4096]{1,0:T(8,128)(2,1)S(1)} %get-tuple-element.73), channel_id=1, source_target_pairs={{0,4},{4,0},{8,12},{12,8},{1,5},{5,1},{9,13},{13,9},{2,6},{6,2},{1... | collective-permute-start | bytes 786440 | tf_op jit(solution)/shard_map/ppermute | solution.py:98
  67.2 4.8 %collective-permute-start.23 = (bf16[32,4096]{1,0:T(8,128)(2,1)S(1)}, bf16[32,4096]{1,0:T(8,128)(2,1)S(1)}, u32[]{:S(2)}, u32[]{:S(2)}) collective-permute-start(bf16[32,4096]{1,0:T(8,128)(2,1)S(1)} %fusion.1), channel_id=1, source_target_pairs={{0,4},{4,0},{8,12},{12,8},{1,5},{5,1},{9,13},{13,9},{2,6},{6,2},{1... | collective-permute-start | bytes 786440 | tf_op jit(solution)/shard_map/ppermute | solution.py:104
  72.8 4.8 %collective-permute-start.19 = (bf16[32,4096]{1,0:T(8,128)(2,1)S(1)}, bf16[32,4096]{1,0:T(8,128)(2,1)S(1)}, u32[]{:S(2)}, u32[]{:S(2)}) collective-permute-start(bf16[32,4096]{1,0:T(8,128)(2,1)S(1)} %fusion), channel_id=1, source_target_pairs={{0,4},{4,0},{8,12},{12,8},{1,5},{5,1},{9,13},{13,9},{2,6},{6,2},{1... | collective-permute-start | bytes 786440 | tf_op jit(solution)/shard_map/ppermute | solution.py:104
  78.4 4.5 %collective-permute-done.23 = bf16[32,4096]{1,0:T(8,128)(2,1)S(1)} collective-permute-done((bf16[32,4096]{1,0:T(8,128)(2,1)S(1)}, bf16[32,4096]{1,0:T(8,128)(2,1)S(1)}, u32[]{:S(2)}, u32[]{:S(2)}) %collective-permute-start.23) | collective-permute-done | bytes 262176 | tf_op jit(solution)/shard_map/ppermute | solution.py:104
  83.0 4.9 %collective-permute-done.19 = bf16[32,4096]{1,0:T(8,128)(2,1)S(1)} collective-permute-done((bf16[32,4096]{1,0:T(8,128)(2,1)S(1)}, bf16[32,4096]{1,0:T(8,128)(2,1)S(1)}, u32[]{:S(2)}, u32[]{:S(2)}) %collective-permute-start.19) | collective-permute-done | bytes 262176 | tf_op jit(solution)/shard_map/ppermute | solution.py:104
  (55 shorter events, 15.0 us)
Async XLA Ops:
  0.6 19.1 %collective-permute-start.4 = (bf16[96,8192]{1,0:T(8,128)(2,1)}, bf16[96,8192]{1,0:T(8,128)(2,1)S(1)}, u32[]{:S(2)}, u32[]{:S(2)}) collective-permute-start(bf16[96,8192]{1,0:T(8,128)(2,1)} %refs_0_.1), channel_id=1, source_target_pairs={{0,1},{1,0},{2,3},{3,2},{4,5},{5,4},{6,7},{7,6},{8,9},{9,8},{10,11... | collective-permute-start | bytes 4718600 | tf_op jit(solution)/shard_map/ppermute | solution.py:20
  1.1 37.8 %collective-permute-start = (bf16[96,8192]{1,0:T(8,128)(2,1)}, bf16[96,8192]{1,0:T(8,128)(2,1)S(1)}, u32[]{:S(2)}, u32[]{:S(2)}) collective-permute-start(bf16[96,8192]{1,0:T(8,128)(2,1)} %refs_0_.1), channel_id=1, source_target_pairs={{0,2},{1,3},{2,0},{3,1},{4,6},{5,7},{6,4},{7,5},{8,10},{9,11},{10,... | collective-permute-start | bytes 4718600 | tf_op jit(solution)/shard_map/ppermute | solution.py:20
  4.7 9.9 %collective-permute-start.1 = (bf16[32,4608]{1,0:T(8,128)(2,1)S(1)}, bf16[32,4608]{1,0:T(8,128)(2,1)S(1)}, u32[]{:S(2)}, u32[]{:S(2)}) collective-permute-start(bf16[32,4608]{1,0:T(8,128)(2,1)S(1)} %slice.8.refs_2_), channel_id=1, source_target_pairs={{0,4},{4,0},{8,12},{12,8},{1,5},{5,1},{9,13},{13,9},{2,6},{6,2},{1... | collective-permute-start | bytes 884744 | tf_op jit(solution)/shard_map/ppermute | solution.py:43
  6.3 8.9 %collective-permute-start.2 = (bf16[32,4608]{1,0:T(8,128)(2,1)S(1)}, bf16[32,4608]{1,0:T(8,128)(2,1)S(1)}, u32[]{:S(2)}, u32[]{:S(2)}) collective-permute-start(bf16[32,4608]{1,0:T(8,128)(2,1)S(1)} %slice.8.refs_2_), channel_id=1, source_target_pairs={{4,8},{8,4},{5,9},{9,5},{6,10},{10,6},{7,11},{11,7},{20,24},{24,20... | collective-permute-start | bytes 884744 | tf_op jit(solution)/shard_map/ppermute | solution.py:43
  8.0 12.5 %collective-permute-start.7 = (bf16[32,3584]{1,0:T(8,128)(2,1)S(1)}, bf16[32,3584]{1,0:T(8,128)(2,1)S(1)}, u32[]{:S(2)}, u32[]{:S(2)}) collective-permute-start(bf16[32,3584]{1,0:T(8,128)(2,1)S(1)} %slice.9.refs_3_), channel_id=1, source_target_pairs={{0,4},{4,0},{8,12},{12,8},{1,5},{5,1},{9,13},{13,9},{2,6},{6,2},{1... | collective-permute-start | bytes 688136 | tf_op jit(solution)/shard_map/ppermute | solution.py:43
  14.6 5.8 %collective-permute-start.8 = (bf16[32,3584]{1,0:T(8,128)(2,1)S(1)}, bf16[32,3584]{1,0:T(8,128)(2,1)S(1)}, u32[]{:S(2)}, u32[]{:S(2)}) collective-permute-start(bf16[32,3584]{1,0:T(8,128)(2,1)S(1)} %slice.9.refs_3_), channel_id=1, source_target_pairs={{4,8},{8,4},{5,9},{9,5},{6,10},{10,6},{7,11},{11,7},{20,24},{24,20... | collective-permute-start | bytes 688136 | tf_op jit(solution)/shard_map/ppermute | solution.py:43
  15.3 12.4 %collective-permute-start.3 = (bf16[32,4608]{1,0:T(8,128)(2,1)S(1)}, bf16[32,4608]{1,0:T(8,128)(2,1)S(1)}, u32[]{:S(2)}, u32[]{:S(2)}) collective-permute-start(bf16[32,4608]{1,0:T(8,128)(2,1)S(1)} %collective-permute-done.2.refs_5_), channel_id=1, source_target_pairs={{0,4},{4,0},{8,12},{12,8},{1,5},{5,1},{9,13},{13,9},{2,6},{6,2},{1... | collective-permute-start | bytes 884744 | tf_op jit(solution)/shard_map/ppermute | solution.py:52
  19.8 7.9 %collective-permute-start.5 = (bf16[32,4608]{1,0:T(8,128)(2,1)S(1)}, bf16[32,4608]{1,0:T(8,128)(2,1)S(1)}, u32[]{:S(2)}, u32[]{:S(2)}) collective-permute-start(bf16[32,4608]{1,0:T(8,128)(2,1)S(1)} %collective-permute-done.1.refs_4_), channel_id=1, source_target_pairs={{4,8},{8,4},{5,9},{9,5},{6,10},{10,6},{7,11},{11,7},{20,24},{24,20... | collective-permute-start | bytes 884744 | tf_op jit(solution)/shard_map/ppermute | solution.py:54
  20.4 14.9 %collective-permute-start.9 = (bf16[32,3584]{1,0:T(8,128)(2,1)S(1)}, bf16[32,3584]{1,0:T(8,128)(2,1)S(1)}, u32[]{:S(2)}, u32[]{:S(2)}) collective-permute-start(bf16[32,3584]{1,0:T(8,128)(2,1)S(1)} %collective-permute-done.8.refs_7_), channel_id=1, source_target_pairs={{0,4},{4,0},{8,12},{12,8},{1,5},{5,1},{9,13},{13,9},{2,6},{6,2},{1... | collective-permute-start | bytes 688136 | tf_op jit(solution)/shard_map/ppermute | solution.py:52
  25.8 9.6 %collective-permute-start.10 = (bf16[32,3584]{1,0:T(8,128)(2,1)S(1)}, bf16[32,3584]{1,0:T(8,128)(2,1)S(1)}, u32[]{:S(2)}, u32[]{:S(2)}) collective-permute-start(bf16[32,3584]{1,0:T(8,128)(2,1)S(1)} %collective-permute-done.7.refs_5_), channel_id=1, source_target_pairs={{4,8},{8,4},{5,9},{9,5},{6,10},{10,6},{7,11},{11,7},{20,24},{24,20... | collective-permute-start | bytes 688136 | tf_op jit(solution)/shard_map/ppermute | solution.py:54
  27.7 14.0 %collective-permute-start.6 = (bf16[32,4608]{1,0:T(8,128)(2,1)S(1)}, bf16[32,4608]{1,0:T(8,128)(2,1)S(1)}, u32[]{:S(2)}, u32[]{:S(2)}) collective-permute-start(bf16[32,4608]{1,0:T(8,128)(2,1)S(1)} %collective-permute-done.5.refs_1_), channel_id=1, source_target_pairs={{0,4},{4,0},{8,12},{12,8},{1,5},{5,1},{9,13},{13,9},{2,6},{6,2},{1... | collective-permute-start | bytes 884744 | tf_op jit(solution)/shard_map/ppermute | solution.py:59
  35.4 6.3 %collective-permute-start.11 = (bf16[32,3584]{1,0:T(8,128)(2,1)S(1)}, bf16[32,3584]{1,0:T(8,128)(2,1)S(1)}, u32[]{:S(2)}, u32[]{:S(2)}) collective-permute-start(bf16[32,3584]{1,0:T(8,128)(2,1)S(1)} %collective-permute-done.10.refs_3_), channel_id=1, source_target_pairs={{0,4},{4,0},{8,12},{12,8},{1,5},{5,1},{9,13},{13,9},{2,6},{6,2},{1... | collective-permute-start | bytes 688136 | tf_op jit(solution)/shard_map/ppermute | solution.py:59
  41.7 3.4 %collective-permute-start.12 = (bf16[96,8192]{1,0:T(8,128)(2,1)S(1)}, bf16[96,8192]{1,0:T(8,128)(2,1)S(1)}, u32[]{:S(2)}, u32[]{:S(2)}) collective-permute-start(bf16[96,8192]{1,0:T(8,128)(2,1)S(1)} %collective-permute-done.refs_9_), channel_id=1, source_target_pairs={{0,1},{1,0},{2,3},{3,2},{4,5},{5,4},{6,7},{7,6},{8,9},{9,8},{10,11... | collective-permute-start | bytes 4718600 | tf_op jit(solution)/shard_map/ppermute | solution.py:20
  46.2 3.6 %collective-permute-start.14 = (f32[2,384]{1,0:T(2,128)S(1)}, f32[2,384]{1,0:T(2,128)S(1)}, u32[]{:S(2)}, u32[]{:S(2)}) collective-permute-start(f32[2,384]{1,0:T(2,128)S(1)} %get-tuple-element.66.refs_0_), channel_id=1, source_target_pairs={{0,2},{1,3},{2,0},{3,1},{4,6},{5,7},{6,4},{7,5},{8,10},{9,11},{10,... | collective-permute-start | bytes 9224 | tf_op jit(solution)/shard_map/ppermute | solution.py:20
  51.1 9.2 %collective-permute-start.16 = (bf16[32,4096]{1,0:T(8,128)(2,1)S(1)}, bf16[32,4096]{1,0:T(8,128)(2,1)S(1)}, u32[]{:S(2)}, u32[]{:S(2)}) collective-permute-start(bf16[32,4096]{1,0:T(8,128)(2,1)S(1)} %get-tuple-element.72), channel_id=1, source_target_pairs={{0,4},{4,0},{8,12},{12,8},{1,5},{5,1},{9,13},{13,9},{2,6},{6,2},{1... | collective-permute-start | bytes 786440 | tf_op jit(solution)/shard_map/ppermute | solution.py:94
  56.7 9.7 %collective-permute-start.17 = (bf16[32,4096]{1,0:T(8,128)(2,1)S(1)}, bf16[32,4096]{1,0:T(8,128)(2,1)S(1)}, u32[]{:S(2)}, u32[]{:S(2)}) collective-permute-start(bf16[32,4096]{1,0:T(8,128)(2,1)S(1)} %get-tuple-element.74), channel_id=1, source_target_pairs={{0,4},{4,0},{8,12},{12,8},{1,5},{5,1},{9,13},{13,9},{2,6},{6,2},{1... | collective-permute-start | bytes 786440 | tf_op jit(solution)/shard_map/ppermute | solution.py:94
  60.3 11.7 %collective-permute-start.24 = (bf16[32,4096]{1,0:T(8,128)(2,1)S(1)}, bf16[32,4096]{1,0:T(8,128)(2,1)S(1)}, u32[]{:S(2)}, u32[]{:S(2)}) collective-permute-start(bf16[32,4096]{1,0:T(8,128)(2,1)S(1)} %get-tuple-element.77), channel_id=1, source_target_pairs={{0,4},{4,0},{8,12},{12,8},{1,5},{5,1},{9,13},{13,9},{2,6},{6,2},{1... | collective-permute-start | bytes 786440 | tf_op jit(solution)/shard_map/ppermute | solution.py:98
  62.4 4.7 %collective-permute-start.22 = (bf16[32,4096]{1,0:T(8,128)(2,1)S(1)}, bf16[32,4096]{1,0:T(8,128)(2,1)S(1)}, u32[]{:S(2)}, u32[]{:S(2)}) collective-permute-start(bf16[32,4096]{1,0:T(8,128)(2,1)S(1)} %add_convert_fusion.2), channel_id=1, source_target_pairs={{4,8},{8,4},{5,9},{9,5},{6,10},{10,6},{7,11},{11,7},{20,24},{24,20... | collective-permute-start | bytes 786440 | tf_op jit(solution)/shard_map/ppermute | solution.py:101
  63.1 14.5 %collective-permute-start.20 = (bf16[32,4096]{1,0:T(8,128)(2,1)S(1)}, bf16[32,4096]{1,0:T(8,128)(2,1)S(1)}, u32[]{:S(2)}, u32[]{:S(2)}) collective-permute-start(bf16[32,4096]{1,0:T(8,128)(2,1)S(1)} %get-tuple-element.73), channel_id=1, source_target_pairs={{0,4},{4,0},{8,12},{12,8},{1,5},{5,1},{9,13},{13,9},{2,6},{6,2},{1... | collective-permute-start | bytes 786440 | tf_op jit(solution)/shard_map/ppermute | solution.py:98
  66.5 6.3 %collective-permute-start.18 = (bf16[32,4096]{1,0:T(8,128)(2,1)S(1)}, bf16[32,4096]{1,0:T(8,128)(2,1)S(1)}, u32[]{:S(2)}, u32[]{:S(2)}) collective-permute-start(bf16[32,4096]{1,0:T(8,128)(2,1)S(1)} %add_convert_fusion.5), channel_id=1, source_target_pairs={{4,8},{8,4},{5,9},{9,5},{6,10},{10,6},{7,11},{11,7},{20,24},{24,20... | collective-permute-start | bytes 786440 | tf_op jit(solution)/shard_map/ppermute | solution.py:101
  67.2 15.6 %collective-permute-start.23 = (bf16[32,4096]{1,0:T(8,128)(2,1)S(1)}, bf16[32,4096]{1,0:T(8,128)(2,1)S(1)}, u32[]{:S(2)}, u32[]{:S(2)}) collective-permute-start(bf16[32,4096]{1,0:T(8,128)(2,1)S(1)} %fusion.1), channel_id=1, source_target_pairs={{0,4},{4,0},{8,12},{12,8},{1,5},{5,1},{9,13},{13,9},{2,6},{6,2},{1... | collective-permute-start | bytes 786440 | tf_op jit(solution)/shard_map/ppermute | solution.py:104
  72.1 10.8 %collective-permute-start.25 = (bf16[32,4096]{1,0:T(8,128)(2,1)S(1)}, bf16[32,4096]{1,0:T(8,128)(2,1)S(1)}, u32[]{:S(2)}, u32[]{:S(2)}) collective-permute-start(bf16[32,4096]{1,0:T(8,128)(2,1)S(1)} %add_convert_fusion), channel_id=1, source_target_pairs={{4,8},{8,4},{5,9},{9,5},{6,10},{10,6},{7,11},{11,7},{20,24},{24,20... | collective-permute-start | bytes 786440 | tf_op jit(solution)/shard_map/ppermute | solution.py:102
  72.8 15.0 %collective-permute-start.19 = (bf16[32,4096]{1,0:T(8,128)(2,1)S(1)}, bf16[32,4096]{1,0:T(8,128)(2,1)S(1)}, u32[]{:S(2)}, u32[]{:S(2)}) collective-permute-start(bf16[32,4096]{1,0:T(8,128)(2,1)S(1)} %fusion), channel_id=1, source_target_pairs={{0,4},{4,0},{8,12},{12,8},{1,5},{5,1},{9,13},{13,9},{2,6},{6,2},{1... | collective-permute-start | bytes 786440 | tf_op jit(solution)/shard_map/ppermute | solution.py:104
  77.7 10.2 %collective-permute-start.21 = (bf16[32,4096]{1,0:T(8,128)(2,1)S(1)}, bf16[32,4096]{1,0:T(8,128)(2,1)S(1)}, u32[]{:S(2)}, u32[]{:S(2)}) collective-permute-start(bf16[32,4096]{1,0:T(8,128)(2,1)S(1)} %add_convert_fusion.3), channel_id=1, source_target_pairs={{4,8},{8,4},{5,9},{9,5},{6,10},{10,6},{7,11},{11,7},{20,24},{24,20... | collective-permute-start | bytes 786440 | tf_op jit(solution)/shard_map/ppermute | solution.py:102
  (7 other events, 24.8 us)

commit v20 on v19

--- a/solution.py
+++ b/solution.py
@@ -410,10 +410,10 @@
     )(scores, routes)
 
 
-def write_masks(packets, rows, top, mask_ref):
+def write_routes(packets, rows, route_ref):
     reader = lax.axis_index("reader")
     readers = len(packets)
-    for t in range(top):
+    for t in range(route_ref.shape[0]):
         routes = [ref[1:2, t * rows : (t + 1) * rows] for ref in packets]
         bit = 1
         while bit < readers:
@@ -421,12 +421,7 @@
             routes = [jnp.where(flip, routes[k ^ bit], one) for k, one in enumerate(routes)]
             bit *= 2
         for j, route in enumerate(routes):
-            columns = slice(j * rows, (j + 1) * rows)
-            for k in range(readers):
-                hits = jnp.where(route == (reader ^ k).astype(jnp.float32), 1.0, 0.0)
-                if t:
-                    hits = jnp.maximum(hits, mask_ref[k : k + 1, columns])
-                mask_ref[k : k + 1, columns] = hits
+            route_ref[t : t + 1, j * rows : (j + 1) * rows] = route
 
 
 def emit_sums(posterior, all_ref, piece, out_refs):
@@ -436,15 +431,20 @@
         out_ref[...] = sums[s * count : (s + 1) * count].astype(out_ref.dtype)
 
 
-def first_sums_kernel(readers, top, piece, all_ref, score_ref, *refs):
+def first_sums_kernel(readers, piece, all_ref, score_ref, *refs):
     refs = list(refs)
     packets = [refs.pop(0) for _ in range(readers)]
-    mask_ref = refs.pop()
+    route_ref = refs.pop()
     norm_ref, post_ref, *out_refs = refs
-    write_masks(packets, packets[0].shape[1] // readers, top, mask_ref)
-    kept = []
+    write_routes(packets, packets[0].shape[1] // readers, route_ref)
+    routes = route_ref[...]
+    kept, mine = [], None
     for k, packet in enumerate(packets):
-        kept.append(jnp.where(mask_ref[k : k + 1, :] > 0.0, packet[0:1, :], -jnp.inf))
+        group = (lax.axis_index("reader") ^ k).astype(jnp.float32)
+        hits = jnp.where(routes == group, 1.0, 0.0)
+        named = jnp.max(hits, axis=0, keepdims=True) > 0.0
+        kept.append(jnp.where(named, packet[0:1, :], -jnp.inf))
+        mine = named if k == 0 else mine
     highest = kept[0]
     for value in kept[1:]:
         highest = jnp.maximum(highest, value)
@@ -453,7 +453,7 @@
         spread = spread + jnp.exp(value - highest)
     norm = highest + jnp.log(spread)
     norm_ref[...] = norm
-    exponent = jnp.where(mask_ref[0:1, :] > 0.0, score_ref[...] - norm, -jnp.inf)
+    exponent = jnp.where(mine, score_ref[...] - norm, -jnp.inf)
     posterior = jnp.exp(exponent).astype(jnp.bfloat16)
     post_ref[...] = posterior
     emit_sums(posterior, all_ref, piece, out_refs)
@@ -505,13 +505,13 @@
         jax.ShapeDtypeStruct(scores.shape, jnp.bfloat16),
     )
     (norms, posterior), first = group_sums(
-        partial(first_sums_kernel, readers, routes.shape[1], pieces[0]),
+        partial(first_sums_kernel, readers, pieces[0]),
         pieces[0],
         members,
         all_images,
         (scores, *packets),
         extra,
-        (pltpu.VMEM((readers, scores.shape[1]), jnp.float32),),
+        (pltpu.VMEM((routes.shape[1], scores.shape[1]), jnp.float32),),
     )
     _, last = group_sums(
         partial(later_sums_kernel, pieces[1]), pieces[1], members, all_images, (posterior,), ()

time: 89.4 us -> 89 us (level)
  no operation moved by 1% of the time
where the time goes in v20:
time: 89 us; the launch traced here: 88.5 us
  starting transfers between devices  47.8 us (54%)
  waiting for transfers between devices  24.4 us (27%)
  local copies, waits for them, and re-layouts  7.48 us (8%)
  Pallas kernels  7.33 us (8%)
  between operations  0.89 us (1%)
    ppermute x2, starting transfers between devices, staged_gather(): far = lax.ppermute(across, 'blk', SIDES)  9.77 us
    ppermute x2, starting transfers between devices, pair_scatter(): from_side = lax.ppermute(near, axis, SIDES)  9.54 us
    ppermute x2, waiting for transfers between devices, pair_scatter(): from_side = lax.ppermute(near, axis, SIDES)  9.37 us
    ppermute x2, starting transfers between devices, staged_gather(): lax.ppermute(one, 'blk', SIDES)  6.09 us
    ppermute x6, waiting for transfers between devices, swap_bits(): lax.ppermute(block, axis, [(i, i ^ bits) for i in range(lax.axis_size(axi...  5.9 us
    ppermute x2, starting transfers between devices, pair_scatter(): for_far_middle = [lax.ppermute(part, axis, SIDES) for part in second]  5.32 us
    ppermute x6, starting transfers between devices, swap_bits(): lax.ppermute(block, axis, [(i, i ^ bits) for i in range(lax.axis_size(axi...  5.01 us
    unnamed x10, local copies, waits for them, and re-layouts  4.96 us
  transfers between devices with their start and end apart: 26, of which 9 were waited for; matrix products, arithmetic and copies ran while one was open for 3% of the time, Pallas kernels for 5%

profile of v20, /device:TPU:0, one launch (start us, length us, event | category | flops | bytes accessed | tf_op | source)
XLA Modules:
  0.0 88.5 jit_solution(3782401947450097179)
XLA Ops:
  1.1 2.6 %collective-permute-start = (bf16[96,8192]{1,0:T(8,128)(2,1)}, bf16[96,8192]{1,0:T(8,128)(2,1)S(1)}, u32[]{:S(2)}, u32[]{:S(2)}) collective-permute-start(bf16[96,8192]{1,0:T(8,128)(2,1)} %refs_0_.1), channel_id=1, source_target_pairs={{0,2},{1,3},{2,0},{3,1},{4,6},{5,7},{6,4},{7,5},{8,10},{9,11},{10,... | collective-permute-start | bytes 4718600 | tf_op jit(solution)/shard_map/ppermute | solution.py:20
  4.7 1.6 %collective-permute-start.1 = (bf16[32,4608]{1,0:T(8,128)(2,1)S(1)}, bf16[32,4608]{1,0:T(8,128)(2,1)S(1)}, u32[]{:S(2)}, u32[]{:S(2)}) collective-permute-start(bf16[32,4608]{1,0:T(8,128)(2,1)S(1)} %slice.8.refs_2_), channel_id=1, source_target_pairs={{0,4},{4,0},{8,12},{12,8},{1,5},{5,1},{9,13},{13,9},{2,6},{6,2},{1... | collective-permute-start | bytes 884744 | tf_op jit(solution)/shard_map/ppermute | solution.py:43
  8.0 4.4 %collective-permute-start.7 = (bf16[32,3584]{1,0:T(8,128)(2,1)S(1)}, bf16[32,3584]{1,0:T(8,128)(2,1)S(1)}, u32[]{:S(2)}, u32[]{:S(2)}) collective-permute-start(bf16[32,3584]{1,0:T(8,128)(2,1)S(1)} %slice.9.refs_3_), channel_id=1, source_target_pairs={{0,4},{4,0},{8,12},{12,8},{1,5},{5,1},{9,13},{13,9},{2,6},{6,2},{1... | collective-permute-start | bytes 688136 | tf_op jit(solution)/shard_map/ppermute | solution.py:43
  12.4 2.2 %collective-permute-done.1.refs_4_ = bf16[32,4608]{1,0:T(8,128)(2,1)S(1)} collective-permute-done((bf16[32,4608]{1,0:T(8,128)(2,1)S(1)}, bf16[32,4608]{1,0:T(8,128)(2,1)S(1)}, u32[]{:S(2)}, u32[]{:S(2)}) %collective-permute-start.1) | collective-permute-done | bytes 294944 | tf_op jit(solution)/shard_map/ppermute | solution.py:43
  15.3 4.5 %collective-permute-start.3 = (bf16[32,4608]{1,0:T(8,128)(2,1)S(1)}, bf16[32,4608]{1,0:T(8,128)(2,1)S(1)}, u32[]{:S(2)}, u32[]{:S(2)}) collective-permute-start(bf16[32,4608]{1,0:T(8,128)(2,1)S(1)} %collective-permute-done.2.refs_5_), channel_id=1, source_target_pairs={{0,4},{4,0},{8,12},{12,8},{1,5},{5,1},{9,13},{13,9},{2,6},{6,2},{1... | collective-permute-start | bytes 884744 | tf_op jit(solution)/shard_map/ppermute | solution.py:52
  20.4 5.3 %collective-permute-start.9 = (bf16[32,3584]{1,0:T(8,128)(2,1)S(1)}, bf16[32,3584]{1,0:T(8,128)(2,1)S(1)}, u32[]{:S(2)}, u32[]{:S(2)}) collective-permute-start(bf16[32,3584]{1,0:T(8,128)(2,1)S(1)} %collective-permute-done.8.refs_7_), channel_id=1, source_target_pairs={{0,4},{4,0},{8,12},{12,8},{1,5},{5,1},{9,13},{13,9},{2,6},{6,2},{1... | collective-permute-start | bytes 688136 | tf_op jit(solution)/shard_map/ppermute | solution.py:52
  26.4 1.2 %collective-permute-done.3.refs_0_ = bf16[32,4608]{1,0:T(8,128)(2,1)S(1)} collective-permute-done((bf16[32,4608]{1,0:T(8,128)(2,1)S(1)}, bf16[32,4608]{1,0:T(8,128)(2,1)S(1)}, u32[]{:S(2)}, u32[]{:S(2)}) %collective-permute-start.3) | collective-permute-done | bytes 294944 | tf_op jit(solution)/shard_map/ppermute | solution.py:52
  27.7 4.4 %collective-permute-start.6 = (bf16[32,4608]{1,0:T(8,128)(2,1)S(1)}, bf16[32,4608]{1,0:T(8,128)(2,1)S(1)}, u32[]{:S(2)}, u32[]{:S(2)}) collective-permute-start(bf16[32,4608]{1,0:T(8,128)(2,1)S(1)} %collective-permute-done.5.refs_1_), channel_id=1, source_target_pairs={{0,4},{4,0},{8,12},{12,8},{1,5},{5,1},{9,13},{13,9},{2,6},{6,2},{1... | collective-permute-start | bytes 884744 | tf_op jit(solution)/shard_map/ppermute | solution.py:59
  32.1 1.4 %copy-done.2 = bf16[96,8192]{1,0:T(8,128)(2,1)S(1)} copy-done((bf16[96,8192]{1,0:T(8,128)(2,1)S(1)}, bf16[96,8192]{1,0:T(8,128)(2,1)}, u32[]{:S(2)}) %copy-start.2) | copy-done | bytes 1572888
  34.2 1.1 %stage.1 = (bf16[64,8192]{1,0:T(8,128)(2,1)S(1)}, f32[64,1]{1,0:T(8,128)S(1)}, bf16[192,8192]{1,0:T(8,128)(2,1)S(1)}, f32[1,8192]{1,0:T(1,128)S(1)}) custom-call(bf16[96,8192]{1,0:T(8,128)(2,1)S(1)} %copy-done.2, bf16[96,8192]{1,0:T(8,128)(2,1)S(1)} %collective-permute-done.4.refs_1_, bf16[32,4608]{1,0:T(8,128)(2,1)S(1)} %slice.8.refs_2_, ...), custom_call_target="tpu_custom_call" | custom-call | flops 4194304 | bytes 12000000 | tf_op jit(solution)/shard_map/stage/pallas_call | solution.py:248
  35.5 3.4 %collective-permute-done.refs_9_ = bf16[96,8192]{1,0:T(8,128)(2,1)S(1)} collective-permute-done((bf16[96,8192]{1,0:T(8,128)(2,1)}, bf16[96,8192]{1,0:T(8,128)(2,1)S(1)}, u32[]{:S(2)}, u32[]{:S(2)}) %collective-permute-start) | collective-permute-done | bytes 1572896 | tf_op jit(solution)/shard_map/ppermute | solution.py:20
  38.9 2.8 %collective-permute-done.11.refs_6_ = bf16[32,3584]{1,0:T(8,128)(2,1)S(1)} collective-permute-done((bf16[32,3584]{1,0:T(8,128)(2,1)S(1)}, bf16[32,3584]{1,0:T(8,128)(2,1)S(1)}, u32[]{:S(2)}, u32[]{:S(2)}) %collective-permute-start.11) | collective-permute-done | bytes 229408 | tf_op jit(solution)/shard_map/ppermute | solution.py:59
  41.7 2.8 %stage_rest.1 = (bf16[8192,128]{1,0:T(8,128)(2,1)S(1)}, f32[128,1]{1,0:T(8,128)S(1)}, bf16[384,8192]{1,0:T(8,128)(2,1)S(1)}, f32[384,128]{1,0:T(8,128)S(1)}) custom-call(bf16[32,4608]{1,0:T(8,128)(2,1)S(1)} %collective-permute-done.3.refs_0_, bf16[32,4608]{1,0:T(8,128)(2,1)S(1)} %collective-permute-done.5.refs_1_, ...), custom_call_target="tpu_custom_call" | custom-call | flops 8388608 | bytes 12000000 | tf_op jit(solution)/shard_map/stage_rest/pallas_call | solution.py:316
  46.8 1.2 %collective-permute-start.15 = (f32[2,384]{1,0:T(2,128)S(1)}, f32[2,384]{1,0:T(2,128)S(1)}, u32[]{:S(2)}, u32[]{:S(2)}) collective-permute-start(f32[2,384]{1,0:T(2,128)S(1)} %get-tuple-element.66.refs_0_), channel_id=1, source_target_pairs={{0,3},{1,2},{2,1},{3,0},{4,7},{5,6},{6,5},{7,4},{8,11},{9,10},{10,... | collective-permute-start | bytes 9224 | tf_op jit(solution)/shard_map/ppermute | solution.py:20
  47.9 1.9 %collective-permute-done.14.refs_2_ = f32[2,384]{1,0:T(2,128)S(1)} collective-permute-done((f32[2,384]{1,0:T(2,128)S(1)}, f32[2,384]{1,0:T(2,128)S(1)}, u32[]{:S(2)}, u32[]{:S(2)}) %collective-permute-start.14) | collective-permute-done | bytes 3104 | tf_op jit(solution)/shard_map/ppermute | solution.py:20
  50.7 2.1 %collective-permute-start.16 = (bf16[32,4096]{1,0:T(8,128)(2,1)S(1)}, bf16[32,4096]{1,0:T(8,128)(2,1)S(1)}, u32[]{:S(2)}, u32[]{:S(2)}) collective-permute-start(bf16[32,4096]{1,0:T(8,128)(2,1)S(1)} %get-tuple-element.72), channel_id=1, source_target_pairs={{0,4},{4,0},{8,12},{12,8},{1,5},{5,1},{9,13},{13,9},{2,6},{6,2},{1... | collective-permute-start | bytes 786440 | tf_op jit(solution)/shard_map/ppermute | solution.py:94
  52.8 2.8 %copy-done.1 = bf16[384,8192]{1,0:T(8,128)(2,1)S(1)} copy-done((bf16[384,8192]{1,0:T(8,128)(2,1)S(1)}, bf16[384,8192]{1,0:T(8,128)(2,1)}, u32[]{:S(2)}) %copy-start.1) | copy-done | bytes 6291480
  56.9 2.9 %collective-permute-done.16 = bf16[32,4096]{1,0:T(8,128)(2,1)S(1)} collective-permute-done((bf16[32,4096]{1,0:T(8,128)(2,1)S(1)}, bf16[32,4096]{1,0:T(8,128)(2,1)S(1)}, u32[]{:S(2)}, u32[]{:S(2)}) %collective-permute-start.16) | collective-permute-done | bytes 262176 | tf_op jit(solution)/shard_map/ppermute | solution.py:94
  59.9 2.1 %collective-permute-start.24 = (bf16[32,4096]{1,0:T(8,128)(2,1)S(1)}, bf16[32,4096]{1,0:T(8,128)(2,1)S(1)}, u32[]{:S(2)}, u32[]{:S(2)}) collective-permute-start(bf16[32,4096]{1,0:T(8,128)(2,1)S(1)} %get-tuple-element.77), channel_id=1, source_target_pairs={{0,4},{4,0},{8,12},{12,8},{1,5},{5,1},{9,13},{13,9},{2,6},{6,2},{1... | collective-permute-start | bytes 786440 | tf_op jit(solution)/shard_map/ppermute | solution.py:98
  62.7 3.3 %collective-permute-start.20 = (bf16[32,4096]{1,0:T(8,128)(2,1)S(1)}, bf16[32,4096]{1,0:T(8,128)(2,1)S(1)}, u32[]{:S(2)}, u32[]{:S(2)}) collective-permute-start(bf16[32,4096]{1,0:T(8,128)(2,1)S(1)} %get-tuple-element.73), channel_id=1, source_target_pairs={{0,4},{4,0},{8,12},{12,8},{1,5},{5,1},{9,13},{13,9},{2,6},{6,2},{1... | collective-permute-start | bytes 786440 | tf_op jit(solution)/shard_map/ppermute | solution.py:98
  66.8 4.8 %collective-permute-start.23 = (bf16[32,4096]{1,0:T(8,128)(2,1)S(1)}, bf16[32,4096]{1,0:T(8,128)(2,1)S(1)}, u32[]{:S(2)}, u32[]{:S(2)}) collective-permute-start(bf16[32,4096]{1,0:T(8,128)(2,1)S(1)} %fusion.1), channel_id=1, source_target_pairs={{0,4},{4,0},{8,12},{12,8},{1,5},{5,1},{9,13},{13,9},{2,6},{6,2},{1... | collective-permute-start | bytes 786440 | tf_op jit(solution)/shard_map/ppermute | solution.py:104
  72.4 4.8 %collective-permute-start.19 = (bf16[32,4096]{1,0:T(8,128)(2,1)S(1)}, bf16[32,4096]{1,0:T(8,128)(2,1)S(1)}, u32[]{:S(2)}, u32[]{:S(2)}) collective-permute-start(bf16[32,4096]{1,0:T(8,128)(2,1)S(1)} %fusion), channel_id=1, source_target_pairs={{0,4},{4,0},{8,12},{12,8},{1,5},{5,1},{9,13},{13,9},{2,6},{6,2},{1... | collective-permute-start | bytes 786440 | tf_op jit(solution)/shard_map/ppermute | solution.py:104
  77.9 4.5 %collective-permute-done.23 = bf16[32,4096]{1,0:T(8,128)(2,1)S(1)} collective-permute-done((bf16[32,4096]{1,0:T(8,128)(2,1)S(1)}, bf16[32,4096]{1,0:T(8,128)(2,1)S(1)}, u32[]{:S(2)}, u32[]{:S(2)}) %collective-permute-start.23) | collective-permute-done | bytes 262176 | tf_op jit(solution)/shard_map/ppermute | solution.py:104
  82.5 4.9 %collective-permute-done.19 = bf16[32,4096]{1,0:T(8,128)(2,1)S(1)} collective-permute-done((bf16[32,4096]{1,0:T(8,128)(2,1)S(1)}, bf16[32,4096]{1,0:T(8,128)(2,1)S(1)}, u32[]{:S(2)}, u32[]{:S(2)}) %collective-permute-start.19) | collective-permute-done | bytes 262176 | tf_op jit(solution)/shard_map/ppermute | solution.py:104
  (55 shorter events, 14.7 us)
Async XLA Ops:
  0.6 19.1 %collective-permute-start.4 = (bf16[96,8192]{1,0:T(8,128)(2,1)}, bf16[96,8192]{1,0:T(8,128)(2,1)S(1)}, u32[]{:S(2)}, u32[]{:S(2)}) collective-permute-start(bf16[96,8192]{1,0:T(8,128)(2,1)} %refs_0_.1), channel_id=1, source_target_pairs={{0,1},{1,0},{2,3},{3,2},{4,5},{5,4},{6,7},{7,6},{8,9},{9,8},{10,11... | collective-permute-start | bytes 4718600 | tf_op jit(solution)/shard_map/ppermute | solution.py:20
  1.1 37.8 %collective-permute-start = (bf16[96,8192]{1,0:T(8,128)(2,1)}, bf16[96,8192]{1,0:T(8,128)(2,1)S(1)}, u32[]{:S(2)}, u32[]{:S(2)}) collective-permute-start(bf16[96,8192]{1,0:T(8,128)(2,1)} %refs_0_.1), channel_id=1, source_target_pairs={{0,2},{1,3},{2,0},{3,1},{4,6},{5,7},{6,4},{7,5},{8,10},{9,11},{10,... | collective-permute-start | bytes 4718600 | tf_op jit(solution)/shard_map/ppermute | solution.py:20
  4.7 9.9 %collective-permute-start.1 = (bf16[32,4608]{1,0:T(8,128)(2,1)S(1)}, bf16[32,4608]{1,0:T(8,128)(2,1)S(1)}, u32[]{:S(2)}, u32[]{:S(2)}) collective-permute-start(bf16[32,4608]{1,0:T(8,128)(2,1)S(1)} %slice.8.refs_2_), channel_id=1, source_target_pairs={{0,4},{4,0},{8,12},{12,8},{1,5},{5,1},{9,13},{13,9},{2,6},{6,2},{1... | collective-permute-start | bytes 884744 | tf_op jit(solution)/shard_map/ppermute | solution.py:43
  6.3 8.9 %collective-permute-start.2 = (bf16[32,4608]{1,0:T(8,128)(2,1)S(1)}, bf16[32,4608]{1,0:T(8,128)(2,1)S(1)}, u32[]{:S(2)}, u32[]{:S(2)}) collective-permute-start(bf16[32,4608]{1,0:T(8,128)(2,1)S(1)} %slice.8.refs_2_), channel_id=1, source_target_pairs={{4,8},{8,4},{5,9},{9,5},{6,10},{10,6},{7,11},{11,7},{20,24},{24,20... | collective-permute-start | bytes 884744 | tf_op jit(solution)/shard_map/ppermute | solution.py:43
  8.0 12.5 %collective-permute-start.7 = (bf16[32,3584]{1,0:T(8,128)(2,1)S(1)}, bf16[32,3584]{1,0:T(8,128)(2,1)S(1)}, u32[]{:S(2)}, u32[]{:S(2)}) collective-permute-start(bf16[32,3584]{1,0:T(8,128)(2,1)S(1)} %slice.9.refs_3_), channel_id=1, source_target_pairs={{0,4},{4,0},{8,12},{12,8},{1,5},{5,1},{9,13},{13,9},{2,6},{6,2},{1... | collective-permute-start | bytes 688136 | tf_op jit(solution)/shard_map/ppermute | solution.py:43
  14.6 5.8 %collective-permute-start.8 = (bf16[32,3584]{1,0:T(8,128)(2,1)S(1)}, bf16[32,3584]{1,0:T(8,128)(2,1)S(1)}, u32[]{:S(2)}, u32[]{:S(2)}) collective-permute-start(bf16[32,3584]{1,0:T(8,128)(2,1)S(1)} %slice.9.refs_3_), channel_id=1, source_target_pairs={{4,8},{8,4},{5,9},{9,5},{6,10},{10,6},{7,11},{11,7},{20,24},{24,20... | collective-permute-start | bytes 688136 | tf_op jit(solution)/shard_map/ppermute | solution.py:43
  15.3 12.4 %collective-permute-start.3 = (bf16[32,4608]{1,0:T(8,128)(2,1)S(1)}, bf16[32,4608]{1,0:T(8,128)(2,1)S(1)}, u32[]{:S(2)}, u32[]{:S(2)}) collective-permute-start(bf16[32,4608]{1,0:T(8,128)(2,1)S(1)} %collective-permute-done.2.refs_5_), channel_id=1, source_target_pairs={{0,4},{4,0},{8,12},{12,8},{1,5},{5,1},{9,13},{13,9},{2,6},{6,2},{1... | collective-permute-start | bytes 884744 | tf_op jit(solution)/shard_map/ppermute | solution.py:52
  19.8 7.9 %collective-permute-start.5 = (bf16[32,4608]{1,0:T(8,128)(2,1)S(1)}, bf16[32,4608]{1,0:T(8,128)(2,1)S(1)}, u32[]{:S(2)}, u32[]{:S(2)}) collective-permute-start(bf16[32,4608]{1,0:T(8,128)(2,1)S(1)} %collective-permute-done.1.refs_4_), channel_id=1, source_target_pairs={{4,8},{8,4},{5,9},{9,5},{6,10},{10,6},{7,11},{11,7},{20,24},{24,20... | collective-permute-start | bytes 884744 | tf_op jit(solution)/shard_map/ppermute | solution.py:54
  20.4 14.9 %collective-permute-start.9 = (bf16[32,3584]{1,0:T(8,128)(2,1)S(1)}, bf16[32,3584]{1,0:T(8,128)(2,1)S(1)}, u32[]{:S(2)}, u32[]{:S(2)}) collective-permute-start(bf16[32,3584]{1,0:T(8,128)(2,1)S(1)} %collective-permute-done.8.refs_7_), channel_id=1, source_target_pairs={{0,4},{4,0},{8,12},{12,8},{1,5},{5,1},{9,13},{13,9},{2,6},{6,2},{1... | collective-permute-start | bytes 688136 | tf_op jit(solution)/shard_map/ppermute | solution.py:52
  25.8 9.6 %collective-permute-start.10 = (bf16[32,3584]{1,0:T(8,128)(2,1)S(1)}, bf16[32,3584]{1,0:T(8,128)(2,1)S(1)}, u32[]{:S(2)}, u32[]{:S(2)}) collective-permute-start(bf16[32,3584]{1,0:T(8,128)(2,1)S(1)} %collective-permute-done.7.refs_5_), channel_id=1, source_target_pairs={{4,8},{8,4},{5,9},{9,5},{6,10},{10,6},{7,11},{11,7},{20,24},{24,20... | collective-permute-start | bytes 688136 | tf_op jit(solution)/shard_map/ppermute | solution.py:54
  27.7 14.0 %collective-permute-start.6 = (bf16[32,4608]{1,0:T(8,128)(2,1)S(1)}, bf16[32,4608]{1,0:T(8,128)(2,1)S(1)}, u32[]{:S(2)}, u32[]{:S(2)}) collective-permute-start(bf16[32,4608]{1,0:T(8,128)(2,1)S(1)} %collective-permute-done.5.refs_1_), channel_id=1, source_target_pairs={{0,4},{4,0},{8,12},{12,8},{1,5},{5,1},{9,13},{13,9},{2,6},{6,2},{1... | collective-permute-start | bytes 884744 | tf_op jit(solution)/shard_map/ppermute | solution.py:59
  35.4 6.3 %collective-permute-start.11 = (bf16[32,3584]{1,0:T(8,128)(2,1)S(1)}, bf16[32,3584]{1,0:T(8,128)(2,1)S(1)}, u32[]{:S(2)}, u32[]{:S(2)}) collective-permute-start(bf16[32,3584]{1,0:T(8,128)(2,1)S(1)} %collective-permute-done.10.refs_3_), channel_id=1, source_target_pairs={{0,4},{4,0},{8,12},{12,8},{1,5},{5,1},{9,13},{13,9},{2,6},{6,2},{1... | collective-permute-start | bytes 688136 | tf_op jit(solution)/shard_map/ppermute | solution.py:59
  41.7 3.4 %collective-permute-start.12 = (bf16[96,8192]{1,0:T(8,128)(2,1)S(1)}, bf16[96,8192]{1,0:T(8,128)(2,1)S(1)}, u32[]{:S(2)}, u32[]{:S(2)}) collective-permute-start(bf16[96,8192]{1,0:T(8,128)(2,1)S(1)} %collective-permute-done.refs_9_), channel_id=1, source_target_pairs={{0,1},{1,0},{2,3},{3,2},{4,5},{5,4},{6,7},{7,6},{8,9},{9,8},{10,11... | collective-permute-start | bytes 4718600 | tf_op jit(solution)/shard_map/ppermute | solution.py:20
  46.2 3.6 %collective-permute-start.14 = (f32[2,384]{1,0:T(2,128)S(1)}, f32[2,384]{1,0:T(2,128)S(1)}, u32[]{:S(2)}, u32[]{:S(2)}) collective-permute-start(f32[2,384]{1,0:T(2,128)S(1)} %get-tuple-element.66.refs_0_), channel_id=1, source_target_pairs={{0,2},{1,3},{2,0},{3,1},{4,6},{5,7},{6,4},{7,5},{8,10},{9,11},{10,... | collective-permute-start | bytes 9224 | tf_op jit(solution)/shard_map/ppermute | solution.py:20
  50.7 9.2 %collective-permute-start.16 = (bf16[32,4096]{1,0:T(8,128)(2,1)S(1)}, bf16[32,4096]{1,0:T(8,128)(2,1)S(1)}, u32[]{:S(2)}, u32[]{:S(2)}) collective-permute-start(bf16[32,4096]{1,0:T(8,128)(2,1)S(1)} %get-tuple-element.72), channel_id=1, source_target_pairs={{0,4},{4,0},{8,12},{12,8},{1,5},{5,1},{9,13},{13,9},{2,6},{6,2},{1... | collective-permute-start | bytes 786440 | tf_op jit(solution)/shard_map/ppermute | solution.py:94
  56.3 9.7 %collective-permute-start.17 = (bf16[32,4096]{1,0:T(8,128)(2,1)S(1)}, bf16[32,4096]{1,0:T(8,128)(2,1)S(1)}, u32[]{:S(2)}, u32[]{:S(2)}) collective-permute-start(bf16[32,4096]{1,0:T(8,128)(2,1)S(1)} %get-tuple-element.74), channel_id=1, source_target_pairs={{0,4},{4,0},{8,12},{12,8},{1,5},{5,1},{9,13},{13,9},{2,6},{6,2},{1... | collective-permute-start | bytes 786440 | tf_op jit(solution)/shard_map/ppermute | solution.py:94
  59.9 11.7 %collective-permute-start.24 = (bf16[32,4096]{1,0:T(8,128)(2,1)S(1)}, bf16[32,4096]{1,0:T(8,128)(2,1)S(1)}, u32[]{:S(2)}, u32[]{:S(2)}) collective-permute-start(bf16[32,4096]{1,0:T(8,128)(2,1)S(1)} %get-tuple-element.77), channel_id=1, source_target_pairs={{0,4},{4,0},{8,12},{12,8},{1,5},{5,1},{9,13},{13,9},{2,6},{6,2},{1... | collective-permute-start | bytes 786440 | tf_op jit(solution)/shard_map/ppermute | solution.py:98
  62.0 4.7 %collective-permute-start.22 = (bf16[32,4096]{1,0:T(8,128)(2,1)S(1)}, bf16[32,4096]{1,0:T(8,128)(2,1)S(1)}, u32[]{:S(2)}, u32[]{:S(2)}) collective-permute-start(bf16[32,4096]{1,0:T(8,128)(2,1)S(1)} %add_convert_fusion.2), channel_id=1, source_target_pairs={{4,8},{8,4},{5,9},{9,5},{6,10},{10,6},{7,11},{11,7},{20,24},{24,20... | collective-permute-start | bytes 786440 | tf_op jit(solution)/shard_map/ppermute | solution.py:101
  62.7 14.5 %collective-permute-start.20 = (bf16[32,4096]{1,0:T(8,128)(2,1)S(1)}, bf16[32,4096]{1,0:T(8,128)(2,1)S(1)}, u32[]{:S(2)}, u32[]{:S(2)}) collective-permute-start(bf16[32,4096]{1,0:T(8,128)(2,1)S(1)} %get-tuple-element.73), channel_id=1, source_target_pairs={{0,4},{4,0},{8,12},{12,8},{1,5},{5,1},{9,13},{13,9},{2,6},{6,2},{1... | collective-permute-start | bytes 786440 | tf_op jit(solution)/shard_map/ppermute | solution.py:98
  66.0 6.3 %collective-permute-start.18 = (bf16[32,4096]{1,0:T(8,128)(2,1)S(1)}, bf16[32,4096]{1,0:T(8,128)(2,1)S(1)}, u32[]{:S(2)}, u32[]{:S(2)}) collective-permute-start(bf16[32,4096]{1,0:T(8,128)(2,1)S(1)} %add_convert_fusion.5), channel_id=1, source_target_pairs={{4,8},{8,4},{5,9},{9,5},{6,10},{10,6},{7,11},{11,7},{20,24},{24,20... | collective-permute-start | bytes 786440 | tf_op jit(solution)/shard_map/ppermute | solution.py:101
  66.8 15.6 %collective-permute-start.23 = (bf16[32,4096]{1,0:T(8,128)(2,1)S(1)}, bf16[32,4096]{1,0:T(8,128)(2,1)S(1)}, u32[]{:S(2)}, u32[]{:S(2)}) collective-permute-start(bf16[32,4096]{1,0:T(8,128)(2,1)S(1)} %fusion.1), channel_id=1, source_target_pairs={{0,4},{4,0},{8,12},{12,8},{1,5},{5,1},{9,13},{13,9},{2,6},{6,2},{1... | collective-permute-start | bytes 786440 | tf_op jit(solution)/shard_map/ppermute | solution.py:104
  71.6 10.8 %collective-permute-start.25 = (bf16[32,4096]{1,0:T(8,128)(2,1)S(1)}, bf16[32,4096]{1,0:T(8,128)(2,1)S(1)}, u32[]{:S(2)}, u32[]{:S(2)}) collective-permute-start(bf16[32,4096]{1,0:T(8,128)(2,1)S(1)} %add_convert_fusion), channel_id=1, source_target_pairs={{4,8},{8,4},{5,9},{9,5},{6,10},{10,6},{7,11},{11,7},{20,24},{24,20... | collective-permute-start | bytes 786440 | tf_op jit(solution)/shard_map/ppermute | solution.py:102
  72.4 15.0 %collective-permute-start.19 = (bf16[32,4096]{1,0:T(8,128)(2,1)S(1)}, bf16[32,4096]{1,0:T(8,128)(2,1)S(1)}, u32[]{:S(2)}, u32[]{:S(2)}) collective-permute-start(bf16[32,4096]{1,0:T(8,128)(2,1)S(1)} %fusion), channel_id=1, source_target_pairs={{0,4},{4,0},{8,12},{12,8},{1,5},{5,1},{9,13},{13,9},{2,6},{6,2},{1... | collective-permute-start | bytes 786440 | tf_op jit(solution)/shard_map/ppermute | solution.py:104
  77.3 10.2 %collective-permute-start.21 = (bf16[32,4096]{1,0:T(8,128)(2,1)S(1)}, bf16[32,4096]{1,0:T(8,128)(2,1)S(1)}, u32[]{:S(2)}, u32[]{:S(2)}) collective-permute-start(bf16[32,4096]{1,0:T(8,128)(2,1)S(1)} %add_convert_fusion.3), channel_id=1, source_target_pairs={{4,8},{8,4},{5,9},{9,5},{6,10},{10,6},{7,11},{11,7},{20,24},{24,20... | collective-permute-start | bytes 786440 | tf_op jit(solution)/shard_map/ppermute | solution.py:102
  (7 other events, 24.4 us)

commit v21 on v20

--- a/solution.py
+++ b/solution.py
@@ -14,6 +14,7 @@
 ANY_SPEC = pl.BlockSpec(memory_space=pl.ANY)
 SIDES = [(0, 1), (1, 0), (2, 3), (3, 2)]
 MIDDLE = [(1, 2), (2, 1)]
+OUTWARD = [(1, 0), (2, 3)]
 
 
 def swap_bits(block, axis, bits):
@@ -56,7 +57,7 @@
             far, across_far, *early = lax.optimization_barrier((far, across_far, *early))
         else:
             far, across_far = lax.optimization_barrier((far, across_far))
-        end = lax.ppermute(across_far, "blk", SIDES)
+        end = lax.ppermute(across_far, "blk", OUTWARD)
         far_parts.append([far, across_far])
         end_parts.append([end, across])
     weighted, penalty, staged_near, noise = early
@@ -112,8 +113,12 @@
     copies, stop = [], out_ref.shape[1]
     for i, ref in enumerate(refs[:count]):
         start = stop - ref.shape[1]
-        copies.append(pltpu.make_async_copy(ref, out_ref.at[:, start:stop], sems.at[i]))
-        copies[-1].start()
+        for j, row in enumerate(range(0, ref.shape[0], 8)):
+            rows = slice(row, row + 8)
+            copies.append(
+                pltpu.make_async_copy(ref.at[rows], out_ref.at[rows, start:stop], sems.at[i, j])
+            )
+            copies[-1].start()
         stop = start
     for copy in copies:
         copy.wait()
@@ -126,7 +131,7 @@
         out_shape=jax.ShapeDtypeStruct((pieces[0].shape[0], width), pieces[0].dtype),
         in_specs=[VMEM_SPEC] * len(pieces),
         out_specs=ANY_SPEC,
-        scratch_shapes=[pltpu.SemaphoreType.DMA((len(pieces),))],
+        scratch_shapes=[pltpu.SemaphoreType.DMA((len(pieces), pieces[0].shape[0] // 8))],
         compiler_params=pltpu.CompilerParams(vmem_limit_bytes=SUMS_VMEM),
         name="beside",
     )(*pieces[::-1])

time: 89 us -> 90.1 us (1.012)
  waiting for transfers between devices: 24.4 us -> 27 us
  starting transfers between devices: 47.8 us -> 46.1 us
    ppermute x2, starting transfers between devices: 4.49 us -> 2.57 us  [staged_gather(): end = lax.ppermute(across_far, 'blk', OUTWARD)]
    ppermute x6, waiting for transfers between devices: 5.9 us -> 7.81 us  [swap_bits(): lax.ppermute(block, axis, [(i, i ^ bits) for i in range(lax.axis_size(axi...]
    ppermute x2, waiting for transfers between devices: 2.79 us -> 4.06 us  [staged_gather(): end = lax.ppermute(across_far, 'blk', OUTWARD)]
where the time goes in v21:
time: 90.1 us; the launch traced here: 89.6 us
  starting transfers between devices  46.1 us (51%)
  waiting for transfers between devices  27 us (30%)
  local copies, waits for them, and re-layouts  7.47 us (8%)
  Pallas kernels  7.38 us (8%)
  between operations  0.93 us (1%)
    ppermute x2, starting transfers between devices, pair_scatter(): from_side = lax.ppermute(near, axis, SIDES)  9.78 us
    ppermute x2, starting transfers between devices, staged_gather(): far = lax.ppermute(across, 'blk', SIDES)  9.77 us
    ppermute x2, waiting for transfers between devices, pair_scatter(): from_side = lax.ppermute(near, axis, SIDES)  8.74 us
    ppermute x6, waiting for transfers between devices, swap_bits(): lax.ppermute(block, axis, [(i, i ^ bits) for i in range(lax.axis_size(axi...  7.81 us
    ppermute x2, starting transfers between devices, staged_gather(): lax.ppermute(one, 'blk', SIDES)  6.09 us
    ppermute x2, starting transfers between devices, pair_scatter(): for_far_middle = [lax.ppermute(part, axis, SIDES) for part in second]  5.41 us
    ppermute x6, starting transfers between devices, swap_bits(): lax.ppermute(block, axis, [(i, i ^ bits) for i in range(lax.axis_size(axi...  5.01 us
    unnamed x10, local copies, waits for them, and re-layouts  4.95 us
  transfers between devices with their start and end apart: 26, of which 9 were waited for; matrix products, arithmetic and copies ran while one was open for 3% of the time, Pallas kernels for 5%

profile of v21, /device:TPU:0, one launch (start us, length us, event | category | flops | bytes accessed | tf_op | source)
XLA Modules:
  0.0 89.6 jit_solution(9673781797989812087)
XLA Ops:
  1.1 2.6 %collective-permute-start = (bf16[96,8192]{1,0:T(8,128)(2,1)}, bf16[96,8192]{1,0:T(8,128)(2,1)S(1)}, u32[]{:S(2)}, u32[]{:S(2)}) collective-permute-start(bf16[96,8192]{1,0:T(8,128)(2,1)} %refs_0_.1), channel_id=1, source_target_pairs={{0,2},{1,3},{2,0},{3,1},{4,6},{5,7},{6,4},{7,5},{8,10},{9,11},{10,... | collective-permute-start | bytes 4718600 | tf_op jit(solution)/shard_map/ppermute | solution.py:21
  4.7 1.6 %collective-permute-start.1 = (bf16[32,4608]{1,0:T(8,128)(2,1)S(1)}, bf16[32,4608]{1,0:T(8,128)(2,1)S(1)}, u32[]{:S(2)}, u32[]{:S(2)}) collective-permute-start(bf16[32,4608]{1,0:T(8,128)(2,1)S(1)} %slice.8.refs_2_), channel_id=1, source_target_pairs={{0,4},{4,0},{8,12},{12,8},{1,5},{5,1},{9,13},{13,9},{2,6},{6,2},{1... | collective-permute-start | bytes 884744 | tf_op jit(solution)/shard_map/ppermute | solution.py:44
  8.0 4.4 %collective-permute-start.7 = (bf16[32,3584]{1,0:T(8,128)(2,1)S(1)}, bf16[32,3584]{1,0:T(8,128)(2,1)S(1)}, u32[]{:S(2)}, u32[]{:S(2)}) collective-permute-start(bf16[32,3584]{1,0:T(8,128)(2,1)S(1)} %slice.9.refs_3_), channel_id=1, source_target_pairs={{0,4},{4,0},{8,12},{12,8},{1,5},{5,1},{9,13},{13,9},{2,6},{6,2},{1... | collective-permute-start | bytes 688136 | tf_op jit(solution)/shard_map/ppermute | solution.py:44
  12.4 2.2 %collective-permute-done.1.refs_4_ = bf16[32,4608]{1,0:T(8,128)(2,1)S(1)} collective-permute-done((bf16[32,4608]{1,0:T(8,128)(2,1)S(1)}, bf16[32,4608]{1,0:T(8,128)(2,1)S(1)}, u32[]{:S(2)}, u32[]{:S(2)}) %collective-permute-start.1) | collective-permute-done | bytes 294944 | tf_op jit(solution)/shard_map/ppermute | solution.py:44
  15.3 4.5 %collective-permute-start.3 = (bf16[32,4608]{1,0:T(8,128)(2,1)S(1)}, bf16[32,4608]{1,0:T(8,128)(2,1)S(1)}, u32[]{:S(2)}, u32[]{:S(2)}) collective-permute-start(bf16[32,4608]{1,0:T(8,128)(2,1)S(1)} %collective-permute-done.2.refs_5_), channel_id=1, source_target_pairs={{0,4},{4,0},{8,12},{12,8},{1,5},{5,1},{9,13},{13,9},{2,6},{6,2},{1... | collective-permute-start | bytes 884744 | tf_op jit(solution)/shard_map/ppermute | solution.py:53
  20.4 5.3 %collective-permute-start.9 = (bf16[32,3584]{1,0:T(8,128)(2,1)S(1)}, bf16[32,3584]{1,0:T(8,128)(2,1)S(1)}, u32[]{:S(2)}, u32[]{:S(2)}) collective-permute-start(bf16[32,3584]{1,0:T(8,128)(2,1)S(1)} %collective-permute-done.8.refs_7_), channel_id=1, source_target_pairs={{0,4},{4,0},{8,12},{12,8},{1,5},{5,1},{9,13},{13,9},{2,6},{6,2},{1... | collective-permute-start | bytes 688136 | tf_op jit(solution)/shard_map/ppermute | solution.py:53
  26.4 1.2 %collective-permute-done.3.refs_0_ = bf16[32,4608]{1,0:T(8,128)(2,1)S(1)} collective-permute-done((bf16[32,4608]{1,0:T(8,128)(2,1)S(1)}, bf16[32,4608]{1,0:T(8,128)(2,1)S(1)}, u32[]{:S(2)}, u32[]{:S(2)}) %collective-permute-start.3) | collective-permute-done | bytes 294944 | tf_op jit(solution)/shard_map/ppermute | solution.py:53
  27.7 1.3 %collective-permute-start.6 = (bf16[32,4608]{1,0:T(8,128)(2,1)S(1)}, bf16[32,4608]{1,0:T(8,128)(2,1)S(1)}, u32[]{:S(2)}, u32[]{:S(2)}) collective-permute-start(bf16[32,4608]{1,0:T(8,128)(2,1)S(1)} %collective-permute-done.5.refs_1_), channel_id=1, source_target_pairs={{4,0},{8,12},{5,1},{9,13},{6,2},{10,14},{7,3},{11,15},{20,16},{24,... | collective-permute-start | bytes 884744 | tf_op jit(solution)/shard_map/ppermute | solution.py:60
  29.0 1.4 %copy-done.2 = bf16[96,8192]{1,0:T(8,128)(2,1)S(1)} copy-done((bf16[96,8192]{1,0:T(8,128)(2,1)S(1)}, bf16[96,8192]{1,0:T(8,128)(2,1)}, u32[]{:S(2)}) %copy-start.2) | copy-done | bytes 1572888
  31.1 1.1 %stage.1 = (bf16[64,8192]{1,0:T(8,128)(2,1)S(1)}, f32[64,1]{1,0:T(8,128)S(1)}, bf16[192,8192]{1,0:T(8,128)(2,1)S(1)}, f32[1,8192]{1,0:T(1,128)S(1)}) custom-call(bf16[96,8192]{1,0:T(8,128)(2,1)S(1)} %copy-done.2, bf16[96,8192]{1,0:T(8,128)(2,1)S(1)} %collective-permute-done.4.refs_1_, bf16[32,4608]{1,0:T(8,128)(2,1)S(1)} %slice.8.refs_2_, ...), custom_call_target="tpu_custom_call" | custom-call | flops 4194304 | bytes 12000000 | tf_op jit(solution)/shard_map/stage/pallas_call | solution.py:253
  32.3 1.3 %collective-permute-start.11 = (bf16[32,3584]{1,0:T(8,128)(2,1)S(1)}, bf16[32,3584]{1,0:T(8,128)(2,1)S(1)}, u32[]{:S(2)}, u32[]{:S(2)}) collective-permute-start(bf16[32,3584]{1,0:T(8,128)(2,1)S(1)} %collective-permute-done.10.refs_3_), channel_id=1, source_target_pairs={{4,0},{8,12},{5,1},{9,13},{6,2},{10,14},{7,3},{11,15},{20,16},{24,... | collective-permute-start | bytes 688136 | tf_op jit(solution)/shard_map/ppermute | solution.py:60
  33.6 5.4 %collective-permute-done.refs_9_ = bf16[96,8192]{1,0:T(8,128)(2,1)S(1)} collective-permute-done((bf16[96,8192]{1,0:T(8,128)(2,1)}, bf16[96,8192]{1,0:T(8,128)(2,1)S(1)}, u32[]{:S(2)}, u32[]{:S(2)}) %collective-permute-start) | collective-permute-done | bytes 1572896 | tf_op jit(solution)/shard_map/ppermute | solution.py:21
  38.9 4.1 %collective-permute-done.11.refs_6_ = bf16[32,3584]{1,0:T(8,128)(2,1)S(1)} collective-permute-done((bf16[32,3584]{1,0:T(8,128)(2,1)S(1)}, bf16[32,3584]{1,0:T(8,128)(2,1)S(1)}, u32[]{:S(2)}, u32[]{:S(2)}) %collective-permute-start.11) | collective-permute-done | bytes 229408 | tf_op jit(solution)/shard_map/ppermute | solution.py:60
  43.0 2.8 %stage_rest.1 = (bf16[8192,128]{1,0:T(8,128)(2,1)S(1)}, f32[128,1]{1,0:T(8,128)S(1)}, bf16[384,8192]{1,0:T(8,128)(2,1)S(1)}, f32[384,128]{1,0:T(8,128)S(1)}) custom-call(bf16[32,4608]{1,0:T(8,128)(2,1)S(1)} %collective-permute-done.3.refs_0_, bf16[32,4608]{1,0:T(8,128)(2,1)S(1)} %collective-permute-done.5.refs_1_, ...), custom_call_target="tpu_custom_call" | custom-call | flops 8388608 | bytes 12000000 | tf_op jit(solution)/shard_map/stage_rest/pallas_call | solution.py:321
  48.0 1.2 %collective-permute-start.15 = (f32[2,384]{1,0:T(2,128)S(1)}, f32[2,384]{1,0:T(2,128)S(1)}, u32[]{:S(2)}, u32[]{:S(2)}) collective-permute-start(f32[2,384]{1,0:T(2,128)S(1)} %get-tuple-element.66.refs_0_), channel_id=1, source_target_pairs={{0,3},{1,2},{2,1},{3,0},{4,7},{5,6},{6,5},{7,4},{8,11},{9,10},{10,... | collective-permute-start | bytes 9224 | tf_op jit(solution)/shard_map/ppermute | solution.py:21
  49.2 1.9 %collective-permute-done.14.refs_2_ = f32[2,384]{1,0:T(2,128)S(1)} collective-permute-done((f32[2,384]{1,0:T(2,128)S(1)}, f32[2,384]{1,0:T(2,128)S(1)}, u32[]{:S(2)}, u32[]{:S(2)}) %collective-permute-start.14) | collective-permute-done | bytes 3104 | tf_op jit(solution)/shard_map/ppermute | solution.py:21
  52.0 2.8 %copy-done.1 = bf16[384,8192]{1,0:T(8,128)(2,1)S(1)} copy-done((bf16[384,8192]{1,0:T(8,128)(2,1)S(1)}, bf16[384,8192]{1,0:T(8,128)(2,1)}, u32[]{:S(2)}) %copy-start.1) | copy-done | bytes 6291480
  55.5 2.0 %collective-permute-start.17 = (bf16[32,4096]{1,0:T(8,128)(2,1)S(1)}, bf16[32,4096]{1,0:T(8,128)(2,1)S(1)}, u32[]{:S(2)}, u32[]{:S(2)}) collective-permute-start(bf16[32,4096]{1,0:T(8,128)(2,1)S(1)} %get-tuple-element.74), channel_id=1, source_target_pairs={{0,4},{4,0},{8,12},{12,8},{1,5},{5,1},{9,13},{13,9},{2,6},{6,2},{1... | collective-permute-start | bytes 786440 | tf_op jit(solution)/shard_map/ppermute | solution.py:95
  58.2 3.0 %collective-permute-done.16 = bf16[32,4096]{1,0:T(8,128)(2,1)S(1)} collective-permute-done((bf16[32,4096]{1,0:T(8,128)(2,1)S(1)}, bf16[32,4096]{1,0:T(8,128)(2,1)S(1)}, u32[]{:S(2)}, u32[]{:S(2)}) %collective-permute-start.16) | collective-permute-done | bytes 262176 | tf_op jit(solution)/shard_map/ppermute | solution.py:95
  61.9 5.4 %collective-permute-start.20 = (bf16[32,4096]{1,0:T(8,128)(2,1)S(1)}, bf16[32,4096]{1,0:T(8,128)(2,1)S(1)}, u32[]{:S(2)}, u32[]{:S(2)}) collective-permute-start(bf16[32,4096]{1,0:T(8,128)(2,1)S(1)} %get-tuple-element.73), channel_id=1, source_target_pairs={{0,4},{4,0},{8,12},{12,8},{1,5},{5,1},{9,13},{13,9},{2,6},{6,2},{1... | collective-permute-start | bytes 786440 | tf_op jit(solution)/shard_map/ppermute | solution.py:99
  68.2 5.0 %collective-permute-start.23 = (bf16[32,4096]{1,0:T(8,128)(2,1)S(1)}, bf16[32,4096]{1,0:T(8,128)(2,1)S(1)}, u32[]{:S(2)}, u32[]{:S(2)}) collective-permute-start(bf16[32,4096]{1,0:T(8,128)(2,1)S(1)} %fusion.1), channel_id=1, source_target_pairs={{0,4},{4,0},{8,12},{12,8},{1,5},{5,1},{9,13},{13,9},{2,6},{6,2},{1... | collective-permute-start | bytes 786440 | tf_op jit(solution)/shard_map/ppermute | solution.py:105
  74.0 4.8 %collective-permute-start.19 = (bf16[32,4096]{1,0:T(8,128)(2,1)S(1)}, bf16[32,4096]{1,0:T(8,128)(2,1)S(1)}, u32[]{:S(2)}, u32[]{:S(2)}) collective-permute-start(bf16[32,4096]{1,0:T(8,128)(2,1)S(1)} %fusion), channel_id=1, source_target_pairs={{0,4},{4,0},{8,12},{12,8},{1,5},{5,1},{9,13},{13,9},{2,6},{6,2},{1... | collective-permute-start | bytes 786440 | tf_op jit(solution)/shard_map/ppermute | solution.py:105
  79.6 4.1 %collective-permute-done.23 = bf16[32,4096]{1,0:T(8,128)(2,1)S(1)} collective-permute-done((bf16[32,4096]{1,0:T(8,128)(2,1)S(1)}, bf16[32,4096]{1,0:T(8,128)(2,1)S(1)}, u32[]{:S(2)}, u32[]{:S(2)}) %collective-permute-start.23) | collective-permute-done | bytes 262176 | tf_op jit(solution)/shard_map/ppermute | solution.py:105
  83.7 4.7 %collective-permute-done.19 = bf16[32,4096]{1,0:T(8,128)(2,1)S(1)} collective-permute-done((bf16[32,4096]{1,0:T(8,128)(2,1)S(1)}, bf16[32,4096]{1,0:T(8,128)(2,1)S(1)}, u32[]{:S(2)}, u32[]{:S(2)}) %collective-permute-start.19) | collective-permute-done | bytes 262176 | tf_op jit(solution)/shard_map/ppermute | solution.py:105
  (55 shorter events, 14.7 us)
Async XLA Ops:
  0.6 19.1 %collective-permute-start.4 = (bf16[96,8192]{1,0:T(8,128)(2,1)}, bf16[96,8192]{1,0:T(8,128)(2,1)S(1)}, u32[]{:S(2)}, u32[]{:S(2)}) collective-permute-start(bf16[96,8192]{1,0:T(8,128)(2,1)} %refs_0_.1), channel_id=1, source_target_pairs={{0,1},{1,0},{2,3},{3,2},{4,5},{5,4},{6,7},{7,6},{8,9},{9,8},{10,11... | collective-permute-start | bytes 4718600 | tf_op jit(solution)/shard_map/ppermute | solution.py:21
  1.1 37.8 %collective-permute-start = (bf16[96,8192]{1,0:T(8,128)(2,1)}, bf16[96,8192]{1,0:T(8,128)(2,1)S(1)}, u32[]{:S(2)}, u32[]{:S(2)}) collective-permute-start(bf16[96,8192]{1,0:T(8,128)(2,1)} %refs_0_.1), channel_id=1, source_target_pairs={{0,2},{1,3},{2,0},{3,1},{4,6},{5,7},{6,4},{7,5},{8,10},{9,11},{10,... | collective-permute-start | bytes 4718600 | tf_op jit(solution)/shard_map/ppermute | solution.py:21
  4.7 9.9 %collective-permute-start.1 = (bf16[32,4608]{1,0:T(8,128)(2,1)S(1)}, bf16[32,4608]{1,0:T(8,128)(2,1)S(1)}, u32[]{:S(2)}, u32[]{:S(2)}) collective-permute-start(bf16[32,4608]{1,0:T(8,128)(2,1)S(1)} %slice.8.refs_2_), channel_id=1, source_target_pairs={{0,4},{4,0},{8,12},{12,8},{1,5},{5,1},{9,13},{13,9},{2,6},{6,2},{1... | collective-permute-start | bytes 884744 | tf_op jit(solution)/shard_map/ppermute | solution.py:44
  6.3 8.9 %collective-permute-start.2 = (bf16[32,4608]{1,0:T(8,128)(2,1)S(1)}, bf16[32,4608]{1,0:T(8,128)(2,1)S(1)}, u32[]{:S(2)}, u32[]{:S(2)}) collective-permute-start(bf16[32,4608]{1,0:T(8,128)(2,1)S(1)} %slice.8.refs_2_), channel_id=1, source_target_pairs={{4,8},{8,4},{5,9},{9,5},{6,10},{10,6},{7,11},{11,7},{20,24},{24,20... | collective-permute-start | bytes 884744 | tf_op jit(solution)/shard_map/ppermute | solution.py:44
  8.0 12.5 %collective-permute-start.7 = (bf16[32,3584]{1,0:T(8,128)(2,1)S(1)}, bf16[32,3584]{1,0:T(8,128)(2,1)S(1)}, u32[]{:S(2)}, u32[]{:S(2)}) collective-permute-start(bf16[32,3584]{1,0:T(8,128)(2,1)S(1)} %slice.9.refs_3_), channel_id=1, source_target_pairs={{0,4},{4,0},{8,12},{12,8},{1,5},{5,1},{9,13},{13,9},{2,6},{6,2},{1... | collective-permute-start | bytes 688136 | tf_op jit(solution)/shard_map/ppermute | solution.py:44
  14.6 5.8 %collective-permute-start.8 = (bf16[32,3584]{1,0:T(8,128)(2,1)S(1)}, bf16[32,3584]{1,0:T(8,128)(2,1)S(1)}, u32[]{:S(2)}, u32[]{:S(2)}) collective-permute-start(bf16[32,3584]{1,0:T(8,128)(2,1)S(1)} %slice.9.refs_3_), channel_id=1, source_target_pairs={{4,8},{8,4},{5,9},{9,5},{6,10},{10,6},{7,11},{11,7},{20,24},{24,20... | collective-permute-start | bytes 688136 | tf_op jit(solution)/shard_map/ppermute | solution.py:44
  15.3 12.4 %collective-permute-start.3 = (bf16[32,4608]{1,0:T(8,128)(2,1)S(1)}, bf16[32,4608]{1,0:T(8,128)(2,1)S(1)}, u32[]{:S(2)}, u32[]{:S(2)}) collective-permute-start(bf16[32,4608]{1,0:T(8,128)(2,1)S(1)} %collective-permute-done.2.refs_5_), channel_id=1, source_target_pairs={{0,4},{4,0},{8,12},{12,8},{1,5},{5,1},{9,13},{13,9},{2,6},{6,2},{1... | collective-permute-start | bytes 884744 | tf_op jit(solution)/shard_map/ppermute | solution.py:53
  19.8 7.9 %collective-permute-start.5 = (bf16[32,4608]{1,0:T(8,128)(2,1)S(1)}, bf16[32,4608]{1,0:T(8,128)(2,1)S(1)}, u32[]{:S(2)}, u32[]{:S(2)}) collective-permute-start(bf16[32,4608]{1,0:T(8,128)(2,1)S(1)} %collective-permute-done.1.refs_4_), channel_id=1, source_target_pairs={{4,8},{8,4},{5,9},{9,5},{6,10},{10,6},{7,11},{11,7},{20,24},{24,20... | collective-permute-start | bytes 884744 | tf_op jit(solution)/shard_map/ppermute | solution.py:55
  20.4 11.8 %collective-permute-start.9 = (bf16[32,3584]{1,0:T(8,128)(2,1)S(1)}, bf16[32,3584]{1,0:T(8,128)(2,1)S(1)}, u32[]{:S(2)}, u32[]{:S(2)}) collective-permute-start(bf16[32,3584]{1,0:T(8,128)(2,1)S(1)} %collective-permute-done.8.refs_7_), channel_id=1, source_target_pairs={{0,4},{4,0},{8,12},{12,8},{1,5},{5,1},{9,13},{13,9},{2,6},{6,2},{1... | collective-permute-start | bytes 688136 | tf_op jit(solution)/shard_map/ppermute | solution.py:53
  25.8 6.5 %collective-permute-start.10 = (bf16[32,3584]{1,0:T(8,128)(2,1)S(1)}, bf16[32,3584]{1,0:T(8,128)(2,1)S(1)}, u32[]{:S(2)}, u32[]{:S(2)}) collective-permute-start(bf16[32,3584]{1,0:T(8,128)(2,1)S(1)} %collective-permute-done.7.refs_5_), channel_id=1, source_target_pairs={{4,8},{8,4},{5,9},{9,5},{6,10},{10,6},{7,11},{11,7},{20,24},{24,20... | collective-permute-start | bytes 688136 | tf_op jit(solution)/shard_map/ppermute | solution.py:55
  27.7 15.3 %collective-permute-start.6 = (bf16[32,4608]{1,0:T(8,128)(2,1)S(1)}, bf16[32,4608]{1,0:T(8,128)(2,1)S(1)}, u32[]{:S(2)}, u32[]{:S(2)}) collective-permute-start(bf16[32,4608]{1,0:T(8,128)(2,1)S(1)} %collective-permute-done.5.refs_1_), channel_id=1, source_target_pairs={{4,0},{8,12},{5,1},{9,13},{6,2},{10,14},{7,3},{11,15},{20,16},{24,... | collective-permute-start | bytes 884744 | tf_op jit(solution)/shard_map/ppermute | solution.py:60
  32.3 10.7 %collective-permute-start.11 = (bf16[32,3584]{1,0:T(8,128)(2,1)S(1)}, bf16[32,3584]{1,0:T(8,128)(2,1)S(1)}, u32[]{:S(2)}, u32[]{:S(2)}) collective-permute-start(bf16[32,3584]{1,0:T(8,128)(2,1)S(1)} %collective-permute-done.10.refs_3_), channel_id=1, source_target_pairs={{4,0},{8,12},{5,1},{9,13},{6,2},{10,14},{7,3},{11,15},{20,16},{24,... | collective-permute-start | bytes 688136 | tf_op jit(solution)/shard_map/ppermute | solution.py:60
  43.0 3.4 %collective-permute-start.12 = (bf16[96,8192]{1,0:T(8,128)(2,1)S(1)}, bf16[96,8192]{1,0:T(8,128)(2,1)S(1)}, u32[]{:S(2)}, u32[]{:S(2)}) collective-permute-start(bf16[96,8192]{1,0:T(8,128)(2,1)S(1)} %collective-permute-done.refs_9_), channel_id=1, source_target_pairs={{0,1},{1,0},{2,3},{3,2},{4,5},{5,4},{6,7},{7,6},{8,9},{9,8},{10,11... | collective-permute-start | bytes 4718600 | tf_op jit(solution)/shard_map/ppermute | solution.py:21
  47.5 3.6 %collective-permute-start.14 = (f32[2,384]{1,0:T(2,128)S(1)}, f32[2,384]{1,0:T(2,128)S(1)}, u32[]{:S(2)}, u32[]{:S(2)}) collective-permute-start(f32[2,384]{1,0:T(2,128)S(1)} %get-tuple-element.66.refs_0_), channel_id=1, source_target_pairs={{0,2},{1,3},{2,0},{3,1},{4,6},{5,7},{6,4},{7,5},{8,10},{9,11},{10,... | collective-permute-start | bytes 9224 | tf_op jit(solution)/shard_map/ppermute | solution.py:21
  51.9 9.2 %collective-permute-start.16 = (bf16[32,4096]{1,0:T(8,128)(2,1)S(1)}, bf16[32,4096]{1,0:T(8,128)(2,1)S(1)}, u32[]{:S(2)}, u32[]{:S(2)}) collective-permute-start(bf16[32,4096]{1,0:T(8,128)(2,1)S(1)} %get-tuple-element.72), channel_id=1, source_target_pairs={{0,4},{4,0},{8,12},{12,8},{1,5},{5,1},{9,13},{13,9},{2,6},{6,2},{1... | collective-permute-start | bytes 786440 | tf_op jit(solution)/shard_map/ppermute | solution.py:95
  55.5 11.8 %collective-permute-start.17 = (bf16[32,4096]{1,0:T(8,128)(2,1)S(1)}, bf16[32,4096]{1,0:T(8,128)(2,1)S(1)}, u32[]{:S(2)}, u32[]{:S(2)}) collective-permute-start(bf16[32,4096]{1,0:T(8,128)(2,1)S(1)} %get-tuple-element.74), channel_id=1, source_target_pairs={{0,4},{4,0},{8,12},{12,8},{1,5},{5,1},{9,13},{13,9},{2,6},{6,2},{1... | collective-permute-start | bytes 786440 | tf_op jit(solution)/shard_map/ppermute | solution.py:95
  61.2 12.0 %collective-permute-start.24 = (bf16[32,4096]{1,0:T(8,128)(2,1)S(1)}, bf16[32,4096]{1,0:T(8,128)(2,1)S(1)}, u32[]{:S(2)}, u32[]{:S(2)}) collective-permute-start(bf16[32,4096]{1,0:T(8,128)(2,1)S(1)} %get-tuple-element.77), channel_id=1, source_target_pairs={{0,4},{4,0},{8,12},{12,8},{1,5},{5,1},{9,13},{13,9},{2,6},{6,2},{1... | collective-permute-start | bytes 786440 | tf_op jit(solution)/shard_map/ppermute | solution.py:99
  61.2 6.8 %collective-permute-start.22 = (bf16[32,4096]{1,0:T(8,128)(2,1)S(1)}, bf16[32,4096]{1,0:T(8,128)(2,1)S(1)}, u32[]{:S(2)}, u32[]{:S(2)}) collective-permute-start(bf16[32,4096]{1,0:T(8,128)(2,1)S(1)} %add_convert_fusion.2), channel_id=1, source_target_pairs={{4,8},{8,4},{5,9},{9,5},{6,10},{10,6},{7,11},{11,7},{20,24},{24,20... | collective-permute-start | bytes 786440 | tf_op jit(solution)/shard_map/ppermute | solution.py:102
  61.9 16.9 %collective-permute-start.20 = (bf16[32,4096]{1,0:T(8,128)(2,1)S(1)}, bf16[32,4096]{1,0:T(8,128)(2,1)S(1)}, u32[]{:S(2)}, u32[]{:S(2)}) collective-permute-start(bf16[32,4096]{1,0:T(8,128)(2,1)S(1)} %get-tuple-element.73), channel_id=1, source_target_pairs={{0,4},{4,0},{8,12},{12,8},{1,5},{5,1},{9,13},{13,9},{2,6},{6,2},{1... | collective-permute-start | bytes 786440 | tf_op jit(solution)/shard_map/ppermute | solution.py:99
  67.4 6.6 %collective-permute-start.18 = (bf16[32,4096]{1,0:T(8,128)(2,1)S(1)}, bf16[32,4096]{1,0:T(8,128)(2,1)S(1)}, u32[]{:S(2)}, u32[]{:S(2)}) collective-permute-start(bf16[32,4096]{1,0:T(8,128)(2,1)S(1)} %add_convert_fusion.5), channel_id=1, source_target_pairs={{4,8},{8,4},{5,9},{9,5},{6,10},{10,6},{7,11},{11,7},{20,24},{24,20... | collective-permute-start | bytes 786440 | tf_op jit(solution)/shard_map/ppermute | solution.py:102
  68.2 15.5 %collective-permute-start.23 = (bf16[32,4096]{1,0:T(8,128)(2,1)S(1)}, bf16[32,4096]{1,0:T(8,128)(2,1)S(1)}, u32[]{:S(2)}, u32[]{:S(2)}) collective-permute-start(bf16[32,4096]{1,0:T(8,128)(2,1)S(1)} %fusion.1), channel_id=1, source_target_pairs={{0,4},{4,0},{8,12},{12,8},{1,5},{5,1},{9,13},{13,9},{2,6},{6,2},{1... | collective-permute-start | bytes 786440 | tf_op jit(solution)/shard_map/ppermute | solution.py:105
  73.3 10.4 %collective-permute-start.25 = (bf16[32,4096]{1,0:T(8,128)(2,1)S(1)}, bf16[32,4096]{1,0:T(8,128)(2,1)S(1)}, u32[]{:S(2)}, u32[]{:S(2)}) collective-permute-start(bf16[32,4096]{1,0:T(8,128)(2,1)S(1)} %add_convert_fusion), channel_id=1, source_target_pairs={{4,8},{8,4},{5,9},{9,5},{6,10},{10,6},{7,11},{11,7},{20,24},{24,20... | collective-permute-start | bytes 786440 | tf_op jit(solution)/shard_map/ppermute | solution.py:103
  74.0 14.4 %collective-permute-start.19 = (bf16[32,4096]{1,0:T(8,128)(2,1)S(1)}, bf16[32,4096]{1,0:T(8,128)(2,1)S(1)}, u32[]{:S(2)}, u32[]{:S(2)}) collective-permute-start(bf16[32,4096]{1,0:T(8,128)(2,1)S(1)} %fusion), channel_id=1, source_target_pairs={{0,4},{4,0},{8,12},{12,8},{1,5},{5,1},{9,13},{13,9},{2,6},{6,2},{1... | collective-permute-start | bytes 786440 | tf_op jit(solution)/shard_map/ppermute | solution.py:105
  78.9 9.5 %collective-permute-start.21 = (bf16[32,4096]{1,0:T(8,128)(2,1)S(1)}, bf16[32,4096]{1,0:T(8,128)(2,1)S(1)}, u32[]{:S(2)}, u32[]{:S(2)}) collective-permute-start(bf16[32,4096]{1,0:T(8,128)(2,1)S(1)} %add_convert_fusion.3), channel_id=1, source_target_pairs={{4,8},{8,4},{5,9},{9,5},{6,10},{10,6},{7,11},{11,7},{20,24},{24,20... | collective-permute-start | bytes 786440 | tf_op jit(solution)/shard_map/ppermute | solution.py:103
  (7 other events, 28.7 us)

commit v22 on v20

--- a/solution.py
+++ b/solution.py
@@ -14,6 +14,7 @@
 ANY_SPEC = pl.BlockSpec(memory_space=pl.ANY)
 SIDES = [(0, 1), (1, 0), (2, 3), (3, 2)]
 MIDDLE = [(1, 2), (2, 1)]
+OUTWARD = [(1, 0), (2, 3)]
 
 
 def swap_bits(block, axis, bits):
@@ -56,7 +57,7 @@
             far, across_far, *early = lax.optimization_barrier((far, across_far, *early))
         else:
             far, across_far = lax.optimization_barrier((far, across_far))
-        end = lax.ppermute(across_far, "blk", SIDES)
+        end = lax.ppermute(across_far, "blk", OUTWARD if last else SIDES)
         far_parts.append([far, across_far])
         end_parts.append([end, across])
     weighted, penalty, staged_near, noise = early

time: 89 us -> 90.4 us (1.016)
  starting transfers between devices: 47.8 us -> 49.3 us
    ppermute x2, waiting for transfers between devices: 2.79 us -> 4.39 us  [staged_gather(): end = lax.ppermute(across_far, 'blk', OUTWARD if last else SIDES)]
    ppermute x2, starting transfers between devices: 4.49 us -> 5.71 us  [staged_gather(): end = lax.ppermute(across_far, 'blk', OUTWARD if last else SIDES)]
    ppermute x6, waiting for transfers between devices: 5.9 us -> 4.68 us  [swap_bits(): lax.ppermute(block, axis, [(i, i ^ bits) for i in range(lax.axis_size(axi...]
where the time goes in v22:
time: 90.4 us; the launch traced here: 89.8 us
  starting transfers between devices  49.3 us (55%)
  waiting for transfers between devices  24.2 us (27%)
  local copies, waits for them, and re-layouts  7.47 us (8%)
  Pallas kernels  7.32 us (8%)
  between operations  0.92 us (1%)
    ppermute x2, starting transfers between devices, pair_scatter(): from_side = lax.ppermute(near, axis, SIDES)  9.79 us
    ppermute x2, starting transfers between devices, staged_gather(): far = lax.ppermute(across, 'blk', SIDES)  9.77 us
    ppermute x2, waiting for transfers between devices, pair_scatter(): from_side = lax.ppermute(near, axis, SIDES)  8.72 us
    ppermute x2, starting transfers between devices, staged_gather(): lax.ppermute(one, 'blk', SIDES)  6.09 us
    ppermute x2, starting transfers between devices, staged_gather(): end = lax.ppermute(across_far, 'blk', OUTWARD if last else SIDES)  5.71 us
    ppermute x2, starting transfers between devices, pair_scatter(): for_far_middle = [lax.ppermute(part, axis, SIDES) for part in second]  5.41 us
    ppermute x6, starting transfers between devices, swap_bits(): lax.ppermute(block, axis, [(i, i ^ bits) for i in range(lax.axis_size(axi...  5.01 us
    unnamed x10, local copies, waits for them, and re-layouts  4.95 us
  transfers between devices with their start and end apart: 26, of which 9 were waited for; matrix products, arithmetic and copies ran while one was open for 3% of the time, Pallas kernels for 5%

profile of v22, /device:TPU:0, one launch (start us, length us, event | category | flops | bytes accessed | tf_op | source)
XLA Modules:
  0.0 89.8 jit_solution(3489502076794904109)
XLA Ops:
  1.1 2.6 %collective-permute-start = (bf16[96,8192]{1,0:T(8,128)(2,1)}, bf16[96,8192]{1,0:T(8,128)(2,1)S(1)}, u32[]{:S(2)}, u32[]{:S(2)}) collective-permute-start(bf16[96,8192]{1,0:T(8,128)(2,1)} %refs_0_.1), channel_id=1, source_target_pairs={{0,2},{1,3},{2,0},{3,1},{4,6},{5,7},{6,4},{7,5},{8,10},{9,11},{10,... | collective-permute-start | bytes 4718600 | tf_op jit(solution)/shard_map/ppermute | solution.py:21
  4.7 1.6 %collective-permute-start.1 = (bf16[32,4608]{1,0:T(8,128)(2,1)S(1)}, bf16[32,4608]{1,0:T(8,128)(2,1)S(1)}, u32[]{:S(2)}, u32[]{:S(2)}) collective-permute-start(bf16[32,4608]{1,0:T(8,128)(2,1)S(1)} %slice.8.refs_2_), channel_id=1, source_target_pairs={{0,4},{4,0},{8,12},{12,8},{1,5},{5,1},{9,13},{13,9},{2,6},{6,2},{1... | collective-permute-start | bytes 884744 | tf_op jit(solution)/shard_map/ppermute | solution.py:44
  8.0 4.4 %collective-permute-start.7 = (bf16[32,3584]{1,0:T(8,128)(2,1)S(1)}, bf16[32,3584]{1,0:T(8,128)(2,1)S(1)}, u32[]{:S(2)}, u32[]{:S(2)}) collective-permute-start(bf16[32,3584]{1,0:T(8,128)(2,1)S(1)} %slice.9.refs_3_), channel_id=1, source_target_pairs={{0,4},{4,0},{8,12},{12,8},{1,5},{5,1},{9,13},{13,9},{2,6},{6,2},{1... | collective-permute-start | bytes 688136 | tf_op jit(solution)/shard_map/ppermute | solution.py:44
  12.4 2.2 %collective-permute-done.1.refs_4_ = bf16[32,4608]{1,0:T(8,128)(2,1)S(1)} collective-permute-done((bf16[32,4608]{1,0:T(8,128)(2,1)S(1)}, bf16[32,4608]{1,0:T(8,128)(2,1)S(1)}, u32[]{:S(2)}, u32[]{:S(2)}) %collective-permute-start.1) | collective-permute-done | bytes 294944 | tf_op jit(solution)/shard_map/ppermute | solution.py:44
  15.3 4.5 %collective-permute-start.3 = (bf16[32,4608]{1,0:T(8,128)(2,1)S(1)}, bf16[32,4608]{1,0:T(8,128)(2,1)S(1)}, u32[]{:S(2)}, u32[]{:S(2)}) collective-permute-start(bf16[32,4608]{1,0:T(8,128)(2,1)S(1)} %collective-permute-done.2.refs_5_), channel_id=1, source_target_pairs={{0,4},{4,0},{8,12},{12,8},{1,5},{5,1},{9,13},{13,9},{2,6},{6,2},{1... | collective-permute-start | bytes 884744 | tf_op jit(solution)/shard_map/ppermute | solution.py:53
  20.4 5.3 %collective-permute-start.9 = (bf16[32,3584]{1,0:T(8,128)(2,1)S(1)}, bf16[32,3584]{1,0:T(8,128)(2,1)S(1)}, u32[]{:S(2)}, u32[]{:S(2)}) collective-permute-start(bf16[32,3584]{1,0:T(8,128)(2,1)S(1)} %collective-permute-done.8.refs_7_), channel_id=1, source_target_pairs={{0,4},{4,0},{8,12},{12,8},{1,5},{5,1},{9,13},{13,9},{2,6},{6,2},{1... | collective-permute-start | bytes 688136 | tf_op jit(solution)/shard_map/ppermute | solution.py:53
  26.4 1.2 %collective-permute-done.3.refs_0_ = bf16[32,4608]{1,0:T(8,128)(2,1)S(1)} collective-permute-done((bf16[32,4608]{1,0:T(8,128)(2,1)S(1)}, bf16[32,4608]{1,0:T(8,128)(2,1)S(1)}, u32[]{:S(2)}, u32[]{:S(2)}) %collective-permute-start.3) | collective-permute-done | bytes 294944 | tf_op jit(solution)/shard_map/ppermute | solution.py:53
  27.7 4.4 %collective-permute-start.6 = (bf16[32,4608]{1,0:T(8,128)(2,1)S(1)}, bf16[32,4608]{1,0:T(8,128)(2,1)S(1)}, u32[]{:S(2)}, u32[]{:S(2)}) collective-permute-start(bf16[32,4608]{1,0:T(8,128)(2,1)S(1)} %collective-permute-done.5.refs_1_), channel_id=1, source_target_pairs={{0,4},{4,0},{8,12},{12,8},{1,5},{5,1},{9,13},{13,9},{2,6},{6,2},{1... | collective-permute-start | bytes 884744 | tf_op jit(solution)/shard_map/ppermute | solution.py:60
  32.1 1.4 %copy-done.2 = bf16[96,8192]{1,0:T(8,128)(2,1)S(1)} copy-done((bf16[96,8192]{1,0:T(8,128)(2,1)S(1)}, bf16[96,8192]{1,0:T(8,128)(2,1)}, u32[]{:S(2)}) %copy-start.2) | copy-done | bytes 1572888
  34.2 1.1 %stage.1 = (bf16[64,8192]{1,0:T(8,128)(2,1)S(1)}, f32[64,1]{1,0:T(8,128)S(1)}, bf16[192,8192]{1,0:T(8,128)(2,1)S(1)}, f32[1,8192]{1,0:T(1,128)S(1)}) custom-call(bf16[96,8192]{1,0:T(8,128)(2,1)S(1)} %copy-done.2, bf16[96,8192]{1,0:T(8,128)(2,1)S(1)} %collective-permute-done.4.refs_1_, bf16[32,4608]{1,0:T(8,128)(2,1)S(1)} %slice.8.refs_2_, ...), custom_call_target="tpu_custom_call" | custom-call | flops 4194304 | bytes 12000000 | tf_op jit(solution)/shard_map/stage/pallas_call | solution.py:249
  35.4 1.3 %collective-permute-start.11 = (bf16[32,3584]{1,0:T(8,128)(2,1)S(1)}, bf16[32,3584]{1,0:T(8,128)(2,1)S(1)}, u32[]{:S(2)}, u32[]{:S(2)}) collective-permute-start(bf16[32,3584]{1,0:T(8,128)(2,1)S(1)} %collective-permute-done.10.refs_3_), channel_id=1, source_target_pairs={{4,0},{8,12},{5,1},{9,13},{6,2},{10,14},{7,3},{11,15},{20,16},{24,... | collective-permute-start | bytes 688136 | tf_op jit(solution)/shard_map/ppermute | solution.py:60
  36.7 2.2 %collective-permute-done.refs_9_ = bf16[96,8192]{1,0:T(8,128)(2,1)S(1)} collective-permute-done((bf16[96,8192]{1,0:T(8,128)(2,1)}, bf16[96,8192]{1,0:T(8,128)(2,1)S(1)}, u32[]{:S(2)}, u32[]{:S(2)}) %collective-permute-start) | collective-permute-done | bytes 1572896 | tf_op jit(solution)/shard_map/ppermute | solution.py:21
  38.9 4.4 %collective-permute-done.11.refs_6_ = bf16[32,3584]{1,0:T(8,128)(2,1)S(1)} collective-permute-done((bf16[32,3584]{1,0:T(8,128)(2,1)S(1)}, bf16[32,3584]{1,0:T(8,128)(2,1)S(1)}, u32[]{:S(2)}, u32[]{:S(2)}) %collective-permute-start.11) | collective-permute-done | bytes 229408 | tf_op jit(solution)/shard_map/ppermute | solution.py:60
  43.3 2.8 %stage_rest.1 = (bf16[8192,128]{1,0:T(8,128)(2,1)S(1)}, f32[128,1]{1,0:T(8,128)S(1)}, bf16[384,8192]{1,0:T(8,128)(2,1)S(1)}, f32[384,128]{1,0:T(8,128)S(1)}) custom-call(bf16[32,4608]{1,0:T(8,128)(2,1)S(1)} %collective-permute-done.3.refs_0_, bf16[32,4608]{1,0:T(8,128)(2,1)S(1)} %collective-permute-done.5.refs_1_, ...), custom_call_target="tpu_custom_call" | custom-call | flops 8388608 | bytes 12000000 | tf_op jit(solution)/shard_map/stage_rest/pallas_call | solution.py:317
  48.4 1.2 %collective-permute-start.15 = (f32[2,384]{1,0:T(2,128)S(1)}, f32[2,384]{1,0:T(2,128)S(1)}, u32[]{:S(2)}, u32[]{:S(2)}) collective-permute-start(f32[2,384]{1,0:T(2,128)S(1)} %get-tuple-element.66.refs_0_), channel_id=1, source_target_pairs={{0,3},{1,2},{2,1},{3,0},{4,7},{5,6},{6,5},{7,4},{8,11},{9,10},{10,... | collective-permute-start | bytes 9224 | tf_op jit(solution)/shard_map/ppermute | solution.py:21
  49.5 1.9 %collective-permute-done.14.refs_2_ = f32[2,384]{1,0:T(2,128)S(1)} collective-permute-done((f32[2,384]{1,0:T(2,128)S(1)}, f32[2,384]{1,0:T(2,128)S(1)}, u32[]{:S(2)}, u32[]{:S(2)}) %collective-permute-start.14) | collective-permute-done | bytes 3104 | tf_op jit(solution)/shard_map/ppermute | solution.py:21
  52.4 2.8 %copy-done.1 = bf16[384,8192]{1,0:T(8,128)(2,1)S(1)} copy-done((bf16[384,8192]{1,0:T(8,128)(2,1)S(1)}, bf16[384,8192]{1,0:T(8,128)(2,1)}, u32[]{:S(2)}) %copy-start.1) | copy-done | bytes 6291480
  55.9 2.1 %collective-permute-start.17 = (bf16[32,4096]{1,0:T(8,128)(2,1)S(1)}, bf16[32,4096]{1,0:T(8,128)(2,1)S(1)}, u32[]{:S(2)}, u32[]{:S(2)}) collective-permute-start(bf16[32,4096]{1,0:T(8,128)(2,1)S(1)} %get-tuple-element.74), channel_id=1, source_target_pairs={{0,4},{4,0},{8,12},{12,8},{1,5},{5,1},{9,13},{13,9},{2,6},{6,2},{1... | collective-permute-start | bytes 786440 | tf_op jit(solution)/shard_map/ppermute | solution.py:95
  58.5 3.0 %collective-permute-done.16 = bf16[32,4096]{1,0:T(8,128)(2,1)S(1)} collective-permute-done((bf16[32,4096]{1,0:T(8,128)(2,1)S(1)}, bf16[32,4096]{1,0:T(8,128)(2,1)S(1)}, u32[]{:S(2)}, u32[]{:S(2)}) %collective-permute-start.16) | collective-permute-done | bytes 262176 | tf_op jit(solution)/shard_map/ppermute | solution.py:95
  62.2 5.4 %collective-permute-start.20 = (bf16[32,4096]{1,0:T(8,128)(2,1)S(1)}, bf16[32,4096]{1,0:T(8,128)(2,1)S(1)}, u32[]{:S(2)}, u32[]{:S(2)}) collective-permute-start(bf16[32,4096]{1,0:T(8,128)(2,1)S(1)} %get-tuple-element.73), channel_id=1, source_target_pairs={{0,4},{4,0},{8,12},{12,8},{1,5},{5,1},{9,13},{13,9},{2,6},{6,2},{1... | collective-permute-start | bytes 786440 | tf_op jit(solution)/shard_map/ppermute | solution.py:99
  68.5 5.0 %collective-permute-start.23 = (bf16[32,4096]{1,0:T(8,128)(2,1)S(1)}, bf16[32,4096]{1,0:T(8,128)(2,1)S(1)}, u32[]{:S(2)}, u32[]{:S(2)}) collective-permute-start(bf16[32,4096]{1,0:T(8,128)(2,1)S(1)} %fusion.1), channel_id=1, source_target_pairs={{0,4},{4,0},{8,12},{12,8},{1,5},{5,1},{9,13},{13,9},{2,6},{6,2},{1... | collective-permute-start | bytes 786440 | tf_op jit(solution)/shard_map/ppermute | solution.py:105
  74.4 4.8 %collective-permute-start.19 = (bf16[32,4096]{1,0:T(8,128)(2,1)S(1)}, bf16[32,4096]{1,0:T(8,128)(2,1)S(1)}, u32[]{:S(2)}, u32[]{:S(2)}) collective-permute-start(bf16[32,4096]{1,0:T(8,128)(2,1)S(1)} %fusion), channel_id=1, source_target_pairs={{0,4},{4,0},{8,12},{12,8},{1,5},{5,1},{9,13},{13,9},{2,6},{6,2},{1... | collective-permute-start | bytes 786440 | tf_op jit(solution)/shard_map/ppermute | solution.py:105
  79.9 4.1 %collective-permute-done.23 = bf16[32,4096]{1,0:T(8,128)(2,1)S(1)} collective-permute-done((bf16[32,4096]{1,0:T(8,128)(2,1)S(1)}, bf16[32,4096]{1,0:T(8,128)(2,1)S(1)}, u32[]{:S(2)}, u32[]{:S(2)}) %collective-permute-start.23) | collective-permute-done | bytes 262176 | tf_op jit(solution)/shard_map/ppermute | solution.py:105
  84.1 4.7 %collective-permute-done.19 = bf16[32,4096]{1,0:T(8,128)(2,1)S(1)} collective-permute-done((bf16[32,4096]{1,0:T(8,128)(2,1)S(1)}, bf16[32,4096]{1,0:T(8,128)(2,1)S(1)}, u32[]{:S(2)}, u32[]{:S(2)}) %collective-permute-start.19) | collective-permute-done | bytes 262176 | tf_op jit(solution)/shard_map/ppermute | solution.py:105
  (55 shorter events, 14.6 us)
Async XLA Ops:
  0.6 19.1 %collective-permute-start.4 = (bf16[96,8192]{1,0:T(8,128)(2,1)}, bf16[96,8192]{1,0:T(8,128)(2,1)S(1)}, u32[]{:S(2)}, u32[]{:S(2)}) collective-permute-start(bf16[96,8192]{1,0:T(8,128)(2,1)} %refs_0_.1), channel_id=1, source_target_pairs={{0,1},{1,0},{2,3},{3,2},{4,5},{5,4},{6,7},{7,6},{8,9},{9,8},{10,11... | collective-permute-start | bytes 4718600 | tf_op jit(solution)/shard_map/ppermute | solution.py:21
  1.1 37.8 %collective-permute-start = (bf16[96,8192]{1,0:T(8,128)(2,1)}, bf16[96,8192]{1,0:T(8,128)(2,1)S(1)}, u32[]{:S(2)}, u32[]{:S(2)}) collective-permute-start(bf16[96,8192]{1,0:T(8,128)(2,1)} %refs_0_.1), channel_id=1, source_target_pairs={{0,2},{1,3},{2,0},{3,1},{4,6},{5,7},{6,4},{7,5},{8,10},{9,11},{10,... | collective-permute-start | bytes 4718600 | tf_op jit(solution)/shard_map/ppermute | solution.py:21
  4.7 9.9 %collective-permute-start.1 = (bf16[32,4608]{1,0:T(8,128)(2,1)S(1)}, bf16[32,4608]{1,0:T(8,128)(2,1)S(1)}, u32[]{:S(2)}, u32[]{:S(2)}) collective-permute-start(bf16[32,4608]{1,0:T(8,128)(2,1)S(1)} %slice.8.refs_2_), channel_id=1, source_target_pairs={{0,4},{4,0},{8,12},{12,8},{1,5},{5,1},{9,13},{13,9},{2,6},{6,2},{1... | collective-permute-start | bytes 884744 | tf_op jit(solution)/shard_map/ppermute | solution.py:44
  6.3 8.9 %collective-permute-start.2 = (bf16[32,4608]{1,0:T(8,128)(2,1)S(1)}, bf16[32,4608]{1,0:T(8,128)(2,1)S(1)}, u32[]{:S(2)}, u32[]{:S(2)}) collective-permute-start(bf16[32,4608]{1,0:T(8,128)(2,1)S(1)} %slice.8.refs_2_), channel_id=1, source_target_pairs={{4,8},{8,4},{5,9},{9,5},{6,10},{10,6},{7,11},{11,7},{20,24},{24,20... | collective-permute-start | bytes 884744 | tf_op jit(solution)/shard_map/ppermute | solution.py:44
  8.0 12.5 %collective-permute-start.7 = (bf16[32,3584]{1,0:T(8,128)(2,1)S(1)}, bf16[32,3584]{1,0:T(8,128)(2,1)S(1)}, u32[]{:S(2)}, u32[]{:S(2)}) collective-permute-start(bf16[32,3584]{1,0:T(8,128)(2,1)S(1)} %slice.9.refs_3_), channel_id=1, source_target_pairs={{0,4},{4,0},{8,12},{12,8},{1,5},{5,1},{9,13},{13,9},{2,6},{6,2},{1... | collective-permute-start | bytes 688136 | tf_op jit(solution)/shard_map/ppermute | solution.py:44
  14.6 5.8 %collective-permute-start.8 = (bf16[32,3584]{1,0:T(8,128)(2,1)S(1)}, bf16[32,3584]{1,0:T(8,128)(2,1)S(1)}, u32[]{:S(2)}, u32[]{:S(2)}) collective-permute-start(bf16[32,3584]{1,0:T(8,128)(2,1)S(1)} %slice.9.refs_3_), channel_id=1, source_target_pairs={{4,8},{8,4},{5,9},{9,5},{6,10},{10,6},{7,11},{11,7},{20,24},{24,20... | collective-permute-start | bytes 688136 | tf_op jit(solution)/shard_map/ppermute | solution.py:44
  15.3 12.4 %collective-permute-start.3 = (bf16[32,4608]{1,0:T(8,128)(2,1)S(1)}, bf16[32,4608]{1,0:T(8,128)(2,1)S(1)}, u32[]{:S(2)}, u32[]{:S(2)}) collective-permute-start(bf16[32,4608]{1,0:T(8,128)(2,1)S(1)} %collective-permute-done.2.refs_5_), channel_id=1, source_target_pairs={{0,4},{4,0},{8,12},{12,8},{1,5},{5,1},{9,13},{13,9},{2,6},{6,2},{1... | collective-permute-start | bytes 884744 | tf_op jit(solution)/shard_map/ppermute | solution.py:53
  19.8 7.9 %collective-permute-start.5 = (bf16[32,4608]{1,0:T(8,128)(2,1)S(1)}, bf16[32,4608]{1,0:T(8,128)(2,1)S(1)}, u32[]{:S(2)}, u32[]{:S(2)}) collective-permute-start(bf16[32,4608]{1,0:T(8,128)(2,1)S(1)} %collective-permute-done.1.refs_4_), channel_id=1, source_target_pairs={{4,8},{8,4},{5,9},{9,5},{6,10},{10,6},{7,11},{11,7},{20,24},{24,20... | collective-permute-start | bytes 884744 | tf_op jit(solution)/shard_map/ppermute | solution.py:55
  20.4 14.9 %collective-permute-start.9 = (bf16[32,3584]{1,0:T(8,128)(2,1)S(1)}, bf16[32,3584]{1,0:T(8,128)(2,1)S(1)}, u32[]{:S(2)}, u32[]{:S(2)}) collective-permute-start(bf16[32,3584]{1,0:T(8,128)(2,1)S(1)} %collective-permute-done.8.refs_7_), channel_id=1, source_target_pairs={{0,4},{4,0},{8,12},{12,8},{1,5},{5,1},{9,13},{13,9},{2,6},{6,2},{1... | collective-permute-start | bytes 688136 | tf_op jit(solution)/shard_map/ppermute | solution.py:53
  25.8 9.6 %collective-permute-start.10 = (bf16[32,3584]{1,0:T(8,128)(2,1)S(1)}, bf16[32,3584]{1,0:T(8,128)(2,1)S(1)}, u32[]{:S(2)}, u32[]{:S(2)}) collective-permute-start(bf16[32,3584]{1,0:T(8,128)(2,1)S(1)} %collective-permute-done.7.refs_5_), channel_id=1, source_target_pairs={{4,8},{8,4},{5,9},{9,5},{6,10},{10,6},{7,11},{11,7},{20,24},{24,20... | collective-permute-start | bytes 688136 | tf_op jit(solution)/shard_map/ppermute | solution.py:55
  27.7 15.6 %collective-permute-start.6 = (bf16[32,4608]{1,0:T(8,128)(2,1)S(1)}, bf16[32,4608]{1,0:T(8,128)(2,1)S(1)}, u32[]{:S(2)}, u32[]{:S(2)}) collective-permute-start(bf16[32,4608]{1,0:T(8,128)(2,1)S(1)} %collective-permute-done.5.refs_1_), channel_id=1, source_target_pairs={{0,4},{4,0},{8,12},{12,8},{1,5},{5,1},{9,13},{13,9},{2,6},{6,2},{1... | collective-permute-start | bytes 884744 | tf_op jit(solution)/shard_map/ppermute | solution.py:60
  35.4 7.9 %collective-permute-start.11 = (bf16[32,3584]{1,0:T(8,128)(2,1)S(1)}, bf16[32,3584]{1,0:T(8,128)(2,1)S(1)}, u32[]{:S(2)}, u32[]{:S(2)}) collective-permute-start(bf16[32,3584]{1,0:T(8,128)(2,1)S(1)} %collective-permute-done.10.refs_3_), channel_id=1, source_target_pairs={{4,0},{8,12},{5,1},{9,13},{6,2},{10,14},{7,3},{11,15},{20,16},{24,... | collective-permute-start | bytes 688136 | tf_op jit(solution)/shard_map/ppermute | solution.py:60
  43.3 3.4 %collective-permute-start.12 = (bf16[96,8192]{1,0:T(8,128)(2,1)S(1)}, bf16[96,8192]{1,0:T(8,128)(2,1)S(1)}, u32[]{:S(2)}, u32[]{:S(2)}) collective-permute-start(bf16[96,8192]{1,0:T(8,128)(2,1)S(1)} %collective-permute-done.refs_9_), channel_id=1, source_target_pairs={{0,1},{1,0},{2,3},{3,2},{4,5},{5,4},{6,7},{7,6},{8,9},{9,8},{10,11... | collective-permute-start | bytes 4718600 | tf_op jit(solution)/shard_map/ppermute | solution.py:21
  47.8 3.6 %collective-permute-start.14 = (f32[2,384]{1,0:T(2,128)S(1)}, f32[2,384]{1,0:T(2,128)S(1)}, u32[]{:S(2)}, u32[]{:S(2)}) collective-permute-start(f32[2,384]{1,0:T(2,128)S(1)} %get-tuple-element.66.refs_0_), channel_id=1, source_target_pairs={{0,2},{1,3},{2,0},{3,1},{4,6},{5,7},{6,4},{7,5},{8,10},{9,11},{10,... | collective-permute-start | bytes 9224 | tf_op jit(solution)/shard_map/ppermute | solution.py:21
  52.3 9.2 %collective-permute-start.16 = (bf16[32,4096]{1,0:T(8,128)(2,1)S(1)}, bf16[32,4096]{1,0:T(8,128)(2,1)S(1)}, u32[]{:S(2)}, u32[]{:S(2)}) collective-permute-start(bf16[32,4096]{1,0:T(8,128)(2,1)S(1)} %get-tuple-element.72), channel_id=1, source_target_pairs={{0,4},{4,0},{8,12},{12,8},{1,5},{5,1},{9,13},{13,9},{2,6},{6,2},{1... | collective-permute-start | bytes 786440 | tf_op jit(solution)/shard_map/ppermute | solution.py:95
  55.9 11.8 %collective-permute-start.17 = (bf16[32,4096]{1,0:T(8,128)(2,1)S(1)}, bf16[32,4096]{1,0:T(8,128)(2,1)S(1)}, u32[]{:S(2)}, u32[]{:S(2)}) collective-permute-start(bf16[32,4096]{1,0:T(8,128)(2,1)S(1)} %get-tuple-element.74), channel_id=1, source_target_pairs={{0,4},{4,0},{8,12},{12,8},{1,5},{5,1},{9,13},{13,9},{2,6},{6,2},{1... | collective-permute-start | bytes 786440 | tf_op jit(solution)/shard_map/ppermute | solution.py:95
  61.5 12.0 %collective-permute-start.24 = (bf16[32,4096]{1,0:T(8,128)(2,1)S(1)}, bf16[32,4096]{1,0:T(8,128)(2,1)S(1)}, u32[]{:S(2)}, u32[]{:S(2)}) collective-permute-start(bf16[32,4096]{1,0:T(8,128)(2,1)S(1)} %get-tuple-element.77), channel_id=1, source_target_pairs={{0,4},{4,0},{8,12},{12,8},{1,5},{5,1},{9,13},{13,9},{2,6},{6,2},{1... | collective-permute-start | bytes 786440 | tf_op jit(solution)/shard_map/ppermute | solution.py:99
  61.6 6.9 %collective-permute-start.22 = (bf16[32,4096]{1,0:T(8,128)(2,1)S(1)}, bf16[32,4096]{1,0:T(8,128)(2,1)S(1)}, u32[]{:S(2)}, u32[]{:S(2)}) collective-permute-start(bf16[32,4096]{1,0:T(8,128)(2,1)S(1)} %add_convert_fusion.2), channel_id=1, source_target_pairs={{4,8},{8,4},{5,9},{9,5},{6,10},{10,6},{7,11},{11,7},{20,24},{24,20... | collective-permute-start | bytes 786440 | tf_op jit(solution)/shard_map/ppermute | solution.py:102
  62.2 16.9 %collective-permute-start.20 = (bf16[32,4096]{1,0:T(8,128)(2,1)S(1)}, bf16[32,4096]{1,0:T(8,128)(2,1)S(1)}, u32[]{:S(2)}, u32[]{:S(2)}) collective-permute-start(bf16[32,4096]{1,0:T(8,128)(2,1)S(1)} %get-tuple-element.73), channel_id=1, source_target_pairs={{0,4},{4,0},{8,12},{12,8},{1,5},{5,1},{9,13},{13,9},{2,6},{6,2},{1... | collective-permute-start | bytes 786440 | tf_op jit(solution)/shard_map/ppermute | solution.py:99
  67.7 6.6 %collective-permute-start.18 = (bf16[32,4096]{1,0:T(8,128)(2,1)S(1)}, bf16[32,4096]{1,0:T(8,128)(2,1)S(1)}, u32[]{:S(2)}, u32[]{:S(2)}) collective-permute-start(bf16[32,4096]{1,0:T(8,128)(2,1)S(1)} %add_convert_fusion.5), channel_id=1, source_target_pairs={{4,8},{8,4},{5,9},{9,5},{6,10},{10,6},{7,11},{11,7},{20,24},{24,20... | collective-permute-start | bytes 786440 | tf_op jit(solution)/shard_map/ppermute | solution.py:102
  68.5 15.4 %collective-permute-start.23 = (bf16[32,4096]{1,0:T(8,128)(2,1)S(1)}, bf16[32,4096]{1,0:T(8,128)(2,1)S(1)}, u32[]{:S(2)}, u32[]{:S(2)}) collective-permute-start(bf16[32,4096]{1,0:T(8,128)(2,1)S(1)} %fusion.1), channel_id=1, source_target_pairs={{0,4},{4,0},{8,12},{12,8},{1,5},{5,1},{9,13},{13,9},{2,6},{6,2},{1... | collective-permute-start | bytes 786440 | tf_op jit(solution)/shard_map/ppermute | solution.py:105
  73.6 10.4 %collective-permute-start.25 = (bf16[32,4096]{1,0:T(8,128)(2,1)S(1)}, bf16[32,4096]{1,0:T(8,128)(2,1)S(1)}, u32[]{:S(2)}, u32[]{:S(2)}) collective-permute-start(bf16[32,4096]{1,0:T(8,128)(2,1)S(1)} %add_convert_fusion), channel_id=1, source_target_pairs={{4,8},{8,4},{5,9},{9,5},{6,10},{10,6},{7,11},{11,7},{20,24},{24,20... | collective-permute-start | bytes 786440 | tf_op jit(solution)/shard_map/ppermute | solution.py:103
  74.4 14.4 %collective-permute-start.19 = (bf16[32,4096]{1,0:T(8,128)(2,1)S(1)}, bf16[32,4096]{1,0:T(8,128)(2,1)S(1)}, u32[]{:S(2)}, u32[]{:S(2)}) collective-permute-start(bf16[32,4096]{1,0:T(8,128)(2,1)S(1)} %fusion), channel_id=1, source_target_pairs={{0,4},{4,0},{8,12},{12,8},{1,5},{5,1},{9,13},{13,9},{2,6},{6,2},{1... | collective-permute-start | bytes 786440 | tf_op jit(solution)/shard_map/ppermute | solution.py:105
  79.2 9.5 %collective-permute-start.21 = (bf16[32,4096]{1,0:T(8,128)(2,1)S(1)}, bf16[32,4096]{1,0:T(8,128)(2,1)S(1)}, u32[]{:S(2)}, u32[]{:S(2)}) collective-permute-start(bf16[32,4096]{1,0:T(8,128)(2,1)S(1)} %add_convert_fusion.3), channel_id=1, source_target_pairs={{4,8},{8,4},{5,9},{9,5},{6,10},{10,6},{7,11},{11,7},{20,24},{24,20... | collective-permute-start | bytes 786440 | tf_op jit(solution)/shard_map/ppermute | solution.py:103
  (7 other events, 25.9 us)

commit v23 on v20

--- a/solution.py
+++ b/solution.py
@@ -48,20 +48,17 @@
         [[[one] for one in cuts], [[side] for side, _ in firsts]], near, noise
     )
     far_parts, end_parts = [], []
-    for last, (side, across) in enumerate(firsts):
+    for side, across in firsts:
         far = lax.ppermute(across, "blk", SIDES)
         side, *_ = lax.optimization_barrier((side, *near))
         across_far = lax.ppermute(side, "blk", MIDDLE)
-        if last:
-            far, across_far, *early = lax.optimization_barrier((far, across_far, *early))
-        else:
-            far, across_far = lax.optimization_barrier((far, across_far))
+        far, across_far = lax.optimization_barrier((far, across_far))
         end = lax.ppermute(across_far, "blk", SIDES)
         far_parts.append([far, across_far])
         end_parts.append([end, across])
     weighted, penalty, staged_near, noise = early
     ends = [parts[0] for parts in end_parts]
-    crossed, *_ = lax.optimization_barrier((crossed, *ends))
+    crossed, *_ = lax.optimization_barrier((crossed, *ends, *early))
     far = swap_gather(crossed, "reader", near_bits)
     staged = stage_rest([far_parts, end_parts], staged_near, crossed, weighted, penalty, noise)
     return staged, far[1:]

time: 89 us -> 89 us (level)
  starting transfers between devices: 47.8 us -> 51 us
  waiting for transfers between devices: 24.4 us -> 21.2 us
    ppermute x2, starting transfers between devices: 4.49 us -> 7.71 us  [staged_gather(): end = lax.ppermute(across_far, 'blk', SIDES)]
    ppermute x6, waiting for transfers between devices: 5.9 us -> 2.7 us  [swap_bits(): lax.ppermute(block, axis, [(i, i ^ bits) for i in range(lax.axis_size(axi...]
where the time goes in v23:
time: 89 us; the launch traced here: 88.5 us
  starting transfers between devices  51 us (57%)
  waiting for transfers between devices  21.2 us (24%)
  local copies, waits for them, and re-layouts  7.48 us (8%)
  Pallas kernels  7.34 us (8%)
    ppermute x2, starting transfers between devices, staged_gather(): far = lax.ppermute(across, 'blk', SIDES)  9.77 us
    ppermute x2, starting transfers between devices, pair_scatter(): from_side = lax.ppermute(near, axis, SIDES)  9.54 us
    ppermute x2, waiting for transfers between devices, pair_scatter(): from_side = lax.ppermute(near, axis, SIDES)  9.39 us
    ppermute x2, starting transfers between devices, staged_gather(): end = lax.ppermute(across_far, 'blk', SIDES)  7.71 us
    ppermute x2, starting transfers between devices, staged_gather(): lax.ppermute(one, 'blk', SIDES)  6.09 us
    ppermute x2, starting transfers between devices, pair_scatter(): for_far_middle = [lax.ppermute(part, axis, SIDES) for part in second]  5.32 us
    ppermute x6, starting transfers between devices, swap_bits(): lax.ppermute(block, axis, [(i, i ^ bits) for i in range(lax.axis_size(axi...  5.01 us
    unnamed x10, local copies, waits for them, and re-layouts  4.96 us
  transfers between devices with their start and end apart: 26, of which 9 were waited for; matrix products, arithmetic and copies ran while one was open for 3% of the time, Pallas kernels for 5%

profile of v23, /device:TPU:0, one launch (start us, length us, event | category | flops | bytes accessed | tf_op | source)
XLA Modules:
  0.0 88.5 jit_solution(13478192239722255620)
XLA Ops:
  1.1 2.6 %collective-permute-start = (bf16[96,8192]{1,0:T(8,128)(2,1)}, bf16[96,8192]{1,0:T(8,128)(2,1)S(1)}, u32[]{:S(2)}, u32[]{:S(2)}) collective-permute-start(bf16[96,8192]{1,0:T(8,128)(2,1)} %refs_0_.1), channel_id=1, source_target_pairs={{0,2},{1,3},{2,0},{3,1},{4,6},{5,7},{6,4},{7,5},{8,10},{9,11},{10,... | collective-permute-start | bytes 4718600 | tf_op jit(solution)/shard_map/ppermute | solution.py:20
  4.7 1.6 %collective-permute-start.1 = (bf16[32,4608]{1,0:T(8,128)(2,1)S(1)}, bf16[32,4608]{1,0:T(8,128)(2,1)S(1)}, u32[]{:S(2)}, u32[]{:S(2)}) collective-permute-start(bf16[32,4608]{1,0:T(8,128)(2,1)S(1)} %slice.8.refs_2_), channel_id=1, source_target_pairs={{0,4},{4,0},{8,12},{12,8},{1,5},{5,1},{9,13},{13,9},{2,6},{6,2},{1... | collective-permute-start | bytes 884744 | tf_op jit(solution)/shard_map/ppermute | solution.py:43
  8.0 4.4 %collective-permute-start.7 = (bf16[32,3584]{1,0:T(8,128)(2,1)S(1)}, bf16[32,3584]{1,0:T(8,128)(2,1)S(1)}, u32[]{:S(2)}, u32[]{:S(2)}) collective-permute-start(bf16[32,3584]{1,0:T(8,128)(2,1)S(1)} %slice.9.refs_3_), channel_id=1, source_target_pairs={{0,4},{4,0},{8,12},{12,8},{1,5},{5,1},{9,13},{13,9},{2,6},{6,2},{1... | collective-permute-start | bytes 688136 | tf_op jit(solution)/shard_map/ppermute | solution.py:43
  12.4 2.2 %collective-permute-done.1.refs_4_ = bf16[32,4608]{1,0:T(8,128)(2,1)S(1)} collective-permute-done((bf16[32,4608]{1,0:T(8,128)(2,1)S(1)}, bf16[32,4608]{1,0:T(8,128)(2,1)S(1)}, u32[]{:S(2)}, u32[]{:S(2)}) %collective-permute-start.1) | collective-permute-done | bytes 294944 | tf_op jit(solution)/shard_map/ppermute | solution.py:43
  15.3 4.5 %collective-permute-start.3 = (bf16[32,4608]{1,0:T(8,128)(2,1)S(1)}, bf16[32,4608]{1,0:T(8,128)(2,1)S(1)}, u32[]{:S(2)}, u32[]{:S(2)}) collective-permute-start(bf16[32,4608]{1,0:T(8,128)(2,1)S(1)} %collective-permute-done.2.refs_5_), channel_id=1, source_target_pairs={{0,4},{4,0},{8,12},{12,8},{1,5},{5,1},{9,13},{13,9},{2,6},{6,2},{1... | collective-permute-start | bytes 884744 | tf_op jit(solution)/shard_map/ppermute | solution.py:52
  20.4 5.3 %collective-permute-start.9 = (bf16[32,3584]{1,0:T(8,128)(2,1)S(1)}, bf16[32,3584]{1,0:T(8,128)(2,1)S(1)}, u32[]{:S(2)}, u32[]{:S(2)}) collective-permute-start(bf16[32,3584]{1,0:T(8,128)(2,1)S(1)} %collective-permute-done.8.refs_7_), channel_id=1, source_target_pairs={{0,4},{4,0},{8,12},{12,8},{1,5},{5,1},{9,13},{13,9},{2,6},{6,2},{1... | collective-permute-start | bytes 688136 | tf_op jit(solution)/shard_map/ppermute | solution.py:52
  26.4 1.2 %collective-permute-done.3.refs_0_ = bf16[32,4608]{1,0:T(8,128)(2,1)S(1)} collective-permute-done((bf16[32,4608]{1,0:T(8,128)(2,1)S(1)}, bf16[32,4608]{1,0:T(8,128)(2,1)S(1)}, u32[]{:S(2)}, u32[]{:S(2)}) %collective-permute-start.3) | collective-permute-done | bytes 294944 | tf_op jit(solution)/shard_map/ppermute | solution.py:52
  27.7 4.4 %collective-permute-start.6 = (bf16[32,4608]{1,0:T(8,128)(2,1)S(1)}, bf16[32,4608]{1,0:T(8,128)(2,1)S(1)}, u32[]{:S(2)}, u32[]{:S(2)}) collective-permute-start(bf16[32,4608]{1,0:T(8,128)(2,1)S(1)} %collective-permute-done.5.refs_1_), channel_id=1, source_target_pairs={{0,4},{4,0},{8,12},{12,8},{1,5},{5,1},{9,13},{13,9},{2,6},{6,2},{1... | collective-permute-start | bytes 884744 | tf_op jit(solution)/shard_map/ppermute | solution.py:56
  32.1 3.3 %collective-permute-start.11 = (bf16[32,3584]{1,0:T(8,128)(2,1)S(1)}, bf16[32,3584]{1,0:T(8,128)(2,1)S(1)}, u32[]{:S(2)}, u32[]{:S(2)}) collective-permute-start(bf16[32,3584]{1,0:T(8,128)(2,1)S(1)} %collective-permute-done.10.refs_3_), channel_id=1, source_target_pairs={{0,4},{4,0},{8,12},{12,8},{1,5},{5,1},{9,13},{13,9},{2,6},{6,2},{1... | collective-permute-start | bytes 688136 | tf_op jit(solution)/shard_map/ppermute | solution.py:56
  35.4 1.4 %copy-done.2 = bf16[96,8192]{1,0:T(8,128)(2,1)S(1)} copy-done((bf16[96,8192]{1,0:T(8,128)(2,1)S(1)}, bf16[96,8192]{1,0:T(8,128)(2,1)}, u32[]{:S(2)}) %copy-start.2) | copy-done | bytes 1572888
  37.5 1.1 %stage.1 = (bf16[64,8192]{1,0:T(8,128)(2,1)S(1)}, f32[64,1]{1,0:T(8,128)S(1)}, bf16[192,8192]{1,0:T(8,128)(2,1)S(1)}, f32[1,8192]{1,0:T(1,128)S(1)}) custom-call(bf16[96,8192]{1,0:T(8,128)(2,1)S(1)} %copy-done.2, bf16[96,8192]{1,0:T(8,128)(2,1)S(1)} %collective-permute-done.4.refs_1_, bf16[32,4608]{1,0:T(8,128)(2,1)S(1)} %slice.8.refs_2_, ...), custom_call_target="tpu_custom_call" | custom-call | flops 4194304 | bytes 12000000 | tf_op jit(solution)/shard_map/stage/pallas_call | solution.py:245
  38.9 2.8 %collective-permute-done.11.refs_6_ = bf16[32,3584]{1,0:T(8,128)(2,1)S(1)} collective-permute-done((bf16[32,3584]{1,0:T(8,128)(2,1)S(1)}, bf16[32,3584]{1,0:T(8,128)(2,1)S(1)}, u32[]{:S(2)}, u32[]{:S(2)}) %collective-permute-start.11) | collective-permute-done | bytes 229408 | tf_op jit(solution)/shard_map/ppermute | solution.py:56
  41.7 2.9 %stage_rest.1 = (bf16[8192,128]{1,0:T(8,128)(2,1)S(1)}, f32[128,1]{1,0:T(8,128)S(1)}, bf16[384,8192]{1,0:T(8,128)(2,1)S(1)}, f32[384,128]{1,0:T(8,128)S(1)}) custom-call(bf16[32,4608]{1,0:T(8,128)(2,1)S(1)} %collective-permute-done.3.refs_0_, bf16[32,4608]{1,0:T(8,128)(2,1)S(1)} %collective-permute-done.5.refs_1_, ...), custom_call_target="tpu_custom_call" | custom-call | flops 8388608 | bytes 12000000 | tf_op jit(solution)/shard_map/stage_rest/pallas_call | solution.py:313
  46.8 1.2 %collective-permute-start.15 = (f32[2,384]{1,0:T(2,128)S(1)}, f32[2,384]{1,0:T(2,128)S(1)}, u32[]{:S(2)}, u32[]{:S(2)}) collective-permute-start(f32[2,384]{1,0:T(2,128)S(1)} %get-tuple-element.58.refs_0_), channel_id=1, source_target_pairs={{0,3},{1,2},{2,1},{3,0},{4,7},{5,6},{6,5},{7,4},{8,11},{9,10},{10,... | collective-permute-start | bytes 9224 | tf_op jit(solution)/shard_map/ppermute | solution.py:20
  47.9 1.9 %collective-permute-done.14.refs_2_ = f32[2,384]{1,0:T(2,128)S(1)} collective-permute-done((f32[2,384]{1,0:T(2,128)S(1)}, f32[2,384]{1,0:T(2,128)S(1)}, u32[]{:S(2)}, u32[]{:S(2)}) %collective-permute-start.14) | collective-permute-done | bytes 3104 | tf_op jit(solution)/shard_map/ppermute | solution.py:20
  50.7 2.1 %collective-permute-start.16 = (bf16[32,4096]{1,0:T(8,128)(2,1)S(1)}, bf16[32,4096]{1,0:T(8,128)(2,1)S(1)}, u32[]{:S(2)}, u32[]{:S(2)}) collective-permute-start(bf16[32,4096]{1,0:T(8,128)(2,1)S(1)} %get-tuple-element.64), channel_id=1, source_target_pairs={{0,4},{4,0},{8,12},{12,8},{1,5},{5,1},{9,13},{13,9},{2,6},{6,2},{1... | collective-permute-start | bytes 786440 | tf_op jit(solution)/shard_map/ppermute | solution.py:91
  52.8 2.8 %copy-done.1 = bf16[384,8192]{1,0:T(8,128)(2,1)S(1)} copy-done((bf16[384,8192]{1,0:T(8,128)(2,1)S(1)}, bf16[384,8192]{1,0:T(8,128)(2,1)}, u32[]{:S(2)}) %copy-start.1) | copy-done | bytes 6291480
  57.0 2.9 %collective-permute-done.16 = bf16[32,4096]{1,0:T(8,128)(2,1)S(1)} collective-permute-done((bf16[32,4096]{1,0:T(8,128)(2,1)S(1)}, bf16[32,4096]{1,0:T(8,128)(2,1)S(1)}, u32[]{:S(2)}, u32[]{:S(2)}) %collective-permute-start.16) | collective-permute-done | bytes 262176 | tf_op jit(solution)/shard_map/ppermute | solution.py:91
  59.9 2.1 %collective-permute-start.24 = (bf16[32,4096]{1,0:T(8,128)(2,1)S(1)}, bf16[32,4096]{1,0:T(8,128)(2,1)S(1)}, u32[]{:S(2)}, u32[]{:S(2)}) collective-permute-start(bf16[32,4096]{1,0:T(8,128)(2,1)S(1)} %get-tuple-element.69), channel_id=1, source_target_pairs={{0,4},{4,0},{8,12},{12,8},{1,5},{5,1},{9,13},{13,9},{2,6},{6,2},{1... | collective-permute-start | bytes 786440 | tf_op jit(solution)/shard_map/ppermute | solution.py:95
  62.7 3.3 %collective-permute-start.20 = (bf16[32,4096]{1,0:T(8,128)(2,1)S(1)}, bf16[32,4096]{1,0:T(8,128)(2,1)S(1)}, u32[]{:S(2)}, u32[]{:S(2)}) collective-permute-start(bf16[32,4096]{1,0:T(8,128)(2,1)S(1)} %get-tuple-element.65), channel_id=1, source_target_pairs={{0,4},{4,0},{8,12},{12,8},{1,5},{5,1},{9,13},{13,9},{2,6},{6,2},{1... | collective-permute-start | bytes 786440 | tf_op jit(solution)/shard_map/ppermute | solution.py:95
  66.8 4.8 %collective-permute-start.23 = (bf16[32,4096]{1,0:T(8,128)(2,1)S(1)}, bf16[32,4096]{1,0:T(8,128)(2,1)S(1)}, u32[]{:S(2)}, u32[]{:S(2)}) collective-permute-start(bf16[32,4096]{1,0:T(8,128)(2,1)S(1)} %fusion.1), channel_id=1, source_target_pairs={{0,4},{4,0},{8,12},{12,8},{1,5},{5,1},{9,13},{13,9},{2,6},{6,2},{1... | collective-permute-start | bytes 786440 | tf_op jit(solution)/shard_map/ppermute | solution.py:101
  72.4 4.8 %collective-permute-start.19 = (bf16[32,4096]{1,0:T(8,128)(2,1)S(1)}, bf16[32,4096]{1,0:T(8,128)(2,1)S(1)}, u32[]{:S(2)}, u32[]{:S(2)}) collective-permute-start(bf16[32,4096]{1,0:T(8,128)(2,1)S(1)} %fusion), channel_id=1, source_target_pairs={{0,4},{4,0},{8,12},{12,8},{1,5},{5,1},{9,13},{13,9},{2,6},{6,2},{1... | collective-permute-start | bytes 786440 | tf_op jit(solution)/shard_map/ppermute | solution.py:101
  77.9 4.5 %collective-permute-done.23 = bf16[32,4096]{1,0:T(8,128)(2,1)S(1)} collective-permute-done((bf16[32,4096]{1,0:T(8,128)(2,1)S(1)}, bf16[32,4096]{1,0:T(8,128)(2,1)S(1)}, u32[]{:S(2)}, u32[]{:S(2)}) %collective-permute-start.23) | collective-permute-done | bytes 262176 | tf_op jit(solution)/shard_map/ppermute | solution.py:101
  82.5 4.9 %collective-permute-done.19 = bf16[32,4096]{1,0:T(8,128)(2,1)S(1)} collective-permute-done((bf16[32,4096]{1,0:T(8,128)(2,1)S(1)}, bf16[32,4096]{1,0:T(8,128)(2,1)S(1)}, u32[]{:S(2)}, u32[]{:S(2)}) %collective-permute-start.19) | collective-permute-done | bytes 262176 | tf_op jit(solution)/shard_map/ppermute | solution.py:101
  (55 shorter events, 14.9 us)
Async XLA Ops:
  0.6 19.1 %collective-permute-start.4 = (bf16[96,8192]{1,0:T(8,128)(2,1)}, bf16[96,8192]{1,0:T(8,128)(2,1)S(1)}, u32[]{:S(2)}, u32[]{:S(2)}) collective-permute-start(bf16[96,8192]{1,0:T(8,128)(2,1)} %refs_0_.1), channel_id=1, source_target_pairs={{0,1},{1,0},{2,3},{3,2},{4,5},{5,4},{6,7},{7,6},{8,9},{9,8},{10,11... | collective-permute-start | bytes 4718600 | tf_op jit(solution)/shard_map/ppermute | solution.py:20
  1.1 37.8 %collective-permute-start = (bf16[96,8192]{1,0:T(8,128)(2,1)}, bf16[96,8192]{1,0:T(8,128)(2,1)S(1)}, u32[]{:S(2)}, u32[]{:S(2)}) collective-permute-start(bf16[96,8192]{1,0:T(8,128)(2,1)} %refs_0_.1), channel_id=1, source_target_pairs={{0,2},{1,3},{2,0},{3,1},{4,6},{5,7},{6,4},{7,5},{8,10},{9,11},{10,... | collective-permute-start | bytes 4718600 | tf_op jit(solution)/shard_map/ppermute | solution.py:20
  4.7 9.9 %collective-permute-start.1 = (bf16[32,4608]{1,0:T(8,128)(2,1)S(1)}, bf16[32,4608]{1,0:T(8,128)(2,1)S(1)}, u32[]{:S(2)}, u32[]{:S(2)}) collective-permute-start(bf16[32,4608]{1,0:T(8,128)(2,1)S(1)} %slice.8.refs_2_), channel_id=1, source_target_pairs={{0,4},{4,0},{8,12},{12,8},{1,5},{5,1},{9,13},{13,9},{2,6},{6,2},{1... | collective-permute-start | bytes 884744 | tf_op jit(solution)/shard_map/ppermute | solution.py:43
  6.3 8.9 %collective-permute-start.2 = (bf16[32,4608]{1,0:T(8,128)(2,1)S(1)}, bf16[32,4608]{1,0:T(8,128)(2,1)S(1)}, u32[]{:S(2)}, u32[]{:S(2)}) collective-permute-start(bf16[32,4608]{1,0:T(8,128)(2,1)S(1)} %slice.8.refs_2_), channel_id=1, source_target_pairs={{4,8},{8,4},{5,9},{9,5},{6,10},{10,6},{7,11},{11,7},{20,24},{24,20... | collective-permute-start | bytes 884744 | tf_op jit(solution)/shard_map/ppermute | solution.py:43
  8.0 12.5 %collective-permute-start.7 = (bf16[32,3584]{1,0:T(8,128)(2,1)S(1)}, bf16[32,3584]{1,0:T(8,128)(2,1)S(1)}, u32[]{:S(2)}, u32[]{:S(2)}) collective-permute-start(bf16[32,3584]{1,0:T(8,128)(2,1)S(1)} %slice.9.refs_3_), channel_id=1, source_target_pairs={{0,4},{4,0},{8,12},{12,8},{1,5},{5,1},{9,13},{13,9},{2,6},{6,2},{1... | collective-permute-start | bytes 688136 | tf_op jit(solution)/shard_map/ppermute | solution.py:43
  14.6 5.8 %collective-permute-start.8 = (bf16[32,3584]{1,0:T(8,128)(2,1)S(1)}, bf16[32,3584]{1,0:T(8,128)(2,1)S(1)}, u32[]{:S(2)}, u32[]{:S(2)}) collective-permute-start(bf16[32,3584]{1,0:T(8,128)(2,1)S(1)} %slice.9.refs_3_), channel_id=1, source_target_pairs={{4,8},{8,4},{5,9},{9,5},{6,10},{10,6},{7,11},{11,7},{20,24},{24,20... | collective-permute-start | bytes 688136 | tf_op jit(solution)/shard_map/ppermute | solution.py:43
  15.3 12.4 %collective-permute-start.3 = (bf16[32,4608]{1,0:T(8,128)(2,1)S(1)}, bf16[32,4608]{1,0:T(8,128)(2,1)S(1)}, u32[]{:S(2)}, u32[]{:S(2)}) collective-permute-start(bf16[32,4608]{1,0:T(8,128)(2,1)S(1)} %collective-permute-done.2.refs_5_), channel_id=1, source_target_pairs={{0,4},{4,0},{8,12},{12,8},{1,5},{5,1},{9,13},{13,9},{2,6},{6,2},{1... | collective-permute-start | bytes 884744 | tf_op jit(solution)/shard_map/ppermute | solution.py:52
  19.8 7.9 %collective-permute-start.5 = (bf16[32,4608]{1,0:T(8,128)(2,1)S(1)}, bf16[32,4608]{1,0:T(8,128)(2,1)S(1)}, u32[]{:S(2)}, u32[]{:S(2)}) collective-permute-start(bf16[32,4608]{1,0:T(8,128)(2,1)S(1)} %collective-permute-done.1.refs_4_), channel_id=1, source_target_pairs={{4,8},{8,4},{5,9},{9,5},{6,10},{10,6},{7,11},{11,7},{20,24},{24,20... | collective-permute-start | bytes 884744 | tf_op jit(solution)/shard_map/ppermute | solution.py:54
  20.4 11.6 %collective-permute-start.9 = (bf16[32,3584]{1,0:T(8,128)(2,1)S(1)}, bf16[32,3584]{1,0:T(8,128)(2,1)S(1)}, u32[]{:S(2)}, u32[]{:S(2)}) collective-permute-start(bf16[32,3584]{1,0:T(8,128)(2,1)S(1)} %collective-permute-done.8.refs_7_), channel_id=1, source_target_pairs={{0,4},{4,0},{8,12},{12,8},{1,5},{5,1},{9,13},{13,9},{2,6},{6,2},{1... | collective-permute-start | bytes 688136 | tf_op jit(solution)/shard_map/ppermute | solution.py:52
  25.8 6.3 %collective-permute-start.10 = (bf16[32,3584]{1,0:T(8,128)(2,1)S(1)}, bf16[32,3584]{1,0:T(8,128)(2,1)S(1)}, u32[]{:S(2)}, u32[]{:S(2)}) collective-permute-start(bf16[32,3584]{1,0:T(8,128)(2,1)S(1)} %collective-permute-done.7.refs_5_), channel_id=1, source_target_pairs={{4,8},{8,4},{5,9},{9,5},{6,10},{10,6},{7,11},{11,7},{20,24},{24,20... | collective-permute-start | bytes 688136 | tf_op jit(solution)/shard_map/ppermute | solution.py:54
  27.7 14.0 %collective-permute-start.6 = (bf16[32,4608]{1,0:T(8,128)(2,1)S(1)}, bf16[32,4608]{1,0:T(8,128)(2,1)S(1)}, u32[]{:S(2)}, u32[]{:S(2)}) collective-permute-start(bf16[32,4608]{1,0:T(8,128)(2,1)S(1)} %collective-permute-done.5.refs_1_), channel_id=1, source_target_pairs={{0,4},{4,0},{8,12},{12,8},{1,5},{5,1},{9,13},{13,9},{2,6},{6,2},{1... | collective-permute-start | bytes 884744 | tf_op jit(solution)/shard_map/ppermute | solution.py:56
  32.1 9.6 %collective-permute-start.11 = (bf16[32,3584]{1,0:T(8,128)(2,1)S(1)}, bf16[32,3584]{1,0:T(8,128)(2,1)S(1)}, u32[]{:S(2)}, u32[]{:S(2)}) collective-permute-start(bf16[32,3584]{1,0:T(8,128)(2,1)S(1)} %collective-permute-done.10.refs_3_), channel_id=1, source_target_pairs={{0,4},{4,0},{8,12},{12,8},{1,5},{5,1},{9,13},{13,9},{2,6},{6,2},{1... | collective-permute-start | bytes 688136 | tf_op jit(solution)/shard_map/ppermute | solution.py:56
  41.7 3.4 %collective-permute-start.12 = (bf16[96,8192]{1,0:T(8,128)(2,1)S(1)}, bf16[96,8192]{1,0:T(8,128)(2,1)S(1)}, u32[]{:S(2)}, u32[]{:S(2)}) collective-permute-start(bf16[96,8192]{1,0:T(8,128)(2,1)S(1)} %collective-permute-done.refs_9_), channel_id=1, source_target_pairs={{0,1},{1,0},{2,3},{3,2},{4,5},{5,4},{6,7},{7,6},{8,9},{9,8},{10,11... | collective-permute-start | bytes 4718600 | tf_op jit(solution)/shard_map/ppermute | solution.py:20
  46.2 3.6 %collective-permute-start.14 = (f32[2,384]{1,0:T(2,128)S(1)}, f32[2,384]{1,0:T(2,128)S(1)}, u32[]{:S(2)}, u32[]{:S(2)}) collective-permute-start(f32[2,384]{1,0:T(2,128)S(1)} %get-tuple-element.58.refs_0_), channel_id=1, source_target_pairs={{0,2},{1,3},{2,0},{3,1},{4,6},{5,7},{6,4},{7,5},{8,10},{9,11},{10,... | collective-permute-start | bytes 9224 | tf_op jit(solution)/shard_map/ppermute | solution.py:20
  50.7 9.2 %collective-permute-start.16 = (bf16[32,4096]{1,0:T(8,128)(2,1)S(1)}, bf16[32,4096]{1,0:T(8,128)(2,1)S(1)}, u32[]{:S(2)}, u32[]{:S(2)}) collective-permute-start(bf16[32,4096]{1,0:T(8,128)(2,1)S(1)} %get-tuple-element.64), channel_id=1, source_target_pairs={{0,4},{4,0},{8,12},{12,8},{1,5},{5,1},{9,13},{13,9},{2,6},{6,2},{1... | collective-permute-start | bytes 786440 | tf_op jit(solution)/shard_map/ppermute | solution.py:91
  56.3 9.7 %collective-permute-start.17 = (bf16[32,4096]{1,0:T(8,128)(2,1)S(1)}, bf16[32,4096]{1,0:T(8,128)(2,1)S(1)}, u32[]{:S(2)}, u32[]{:S(2)}) collective-permute-start(bf16[32,4096]{1,0:T(8,128)(2,1)S(1)} %get-tuple-element.66), channel_id=1, source_target_pairs={{0,4},{4,0},{8,12},{12,8},{1,5},{5,1},{9,13},{13,9},{2,6},{6,2},{1... | collective-permute-start | bytes 786440 | tf_op jit(solution)/shard_map/ppermute | solution.py:91
  59.9 11.7 %collective-permute-start.24 = (bf16[32,4096]{1,0:T(8,128)(2,1)S(1)}, bf16[32,4096]{1,0:T(8,128)(2,1)S(1)}, u32[]{:S(2)}, u32[]{:S(2)}) collective-permute-start(bf16[32,4096]{1,0:T(8,128)(2,1)S(1)} %get-tuple-element.69), channel_id=1, source_target_pairs={{0,4},{4,0},{8,12},{12,8},{1,5},{5,1},{9,13},{13,9},{2,6},{6,2},{1... | collective-permute-start | bytes 786440 | tf_op jit(solution)/shard_map/ppermute | solution.py:95
  62.0 4.7 %collective-permute-start.22 = (bf16[32,4096]{1,0:T(8,128)(2,1)S(1)}, bf16[32,4096]{1,0:T(8,128)(2,1)S(1)}, u32[]{:S(2)}, u32[]{:S(2)}) collective-permute-start(bf16[32,4096]{1,0:T(8,128)(2,1)S(1)} %add_convert_fusion.2), channel_id=1, source_target_pairs={{4,8},{8,4},{5,9},{9,5},{6,10},{10,6},{7,11},{11,7},{20,24},{24,20... | collective-permute-start | bytes 786440 | tf_op jit(solution)/shard_map/ppermute | solution.py:98
  62.7 14.5 %collective-permute-start.20 = (bf16[32,4096]{1,0:T(8,128)(2,1)S(1)}, bf16[32,4096]{1,0:T(8,128)(2,1)S(1)}, u32[]{:S(2)}, u32[]{:S(2)}) collective-permute-start(bf16[32,4096]{1,0:T(8,128)(2,1)S(1)} %get-tuple-element.65), channel_id=1, source_target_pairs={{0,4},{4,0},{8,12},{12,8},{1,5},{5,1},{9,13},{13,9},{2,6},{6,2},{1... | collective-permute-start | bytes 786440 | tf_op jit(solution)/shard_map/ppermute | solution.py:95
  66.0 6.3 %collective-permute-start.18 = (bf16[32,4096]{1,0:T(8,128)(2,1)S(1)}, bf16[32,4096]{1,0:T(8,128)(2,1)S(1)}, u32[]{:S(2)}, u32[]{:S(2)}) collective-permute-start(bf16[32,4096]{1,0:T(8,128)(2,1)S(1)} %add_convert_fusion.5), channel_id=1, source_target_pairs={{4,8},{8,4},{5,9},{9,5},{6,10},{10,6},{7,11},{11,7},{20,24},{24,20... | collective-permute-start | bytes 786440 | tf_op jit(solution)/shard_map/ppermute | solution.py:98
  66.8 15.6 %collective-permute-start.23 = (bf16[32,4096]{1,0:T(8,128)(2,1)S(1)}, bf16[32,4096]{1,0:T(8,128)(2,1)S(1)}, u32[]{:S(2)}, u32[]{:S(2)}) collective-permute-start(bf16[32,4096]{1,0:T(8,128)(2,1)S(1)} %fusion.1), channel_id=1, source_target_pairs={{0,4},{4,0},{8,12},{12,8},{1,5},{5,1},{9,13},{13,9},{2,6},{6,2},{1... | collective-permute-start | bytes 786440 | tf_op jit(solution)/shard_map/ppermute | solution.py:101
  71.6 10.8 %collective-permute-start.25 = (bf16[32,4096]{1,0:T(8,128)(2,1)S(1)}, bf16[32,4096]{1,0:T(8,128)(2,1)S(1)}, u32[]{:S(2)}, u32[]{:S(2)}) collective-permute-start(bf16[32,4096]{1,0:T(8,128)(2,1)S(1)} %add_convert_fusion), channel_id=1, source_target_pairs={{4,8},{8,4},{5,9},{9,5},{6,10},{10,6},{7,11},{11,7},{20,24},{24,20... | collective-permute-start | bytes 786440 | tf_op jit(solution)/shard_map/ppermute | solution.py:99
  72.4 15.0 %collective-permute-start.19 = (bf16[32,4096]{1,0:T(8,128)(2,1)S(1)}, bf16[32,4096]{1,0:T(8,128)(2,1)S(1)}, u32[]{:S(2)}, u32[]{:S(2)}) collective-permute-start(bf16[32,4096]{1,0:T(8,128)(2,1)S(1)} %fusion), channel_id=1, source_target_pairs={{0,4},{4,0},{8,12},{12,8},{1,5},{5,1},{9,13},{13,9},{2,6},{6,2},{1... | collective-permute-start | bytes 786440 | tf_op jit(solution)/shard_map/ppermute | solution.py:101
  77.3 10.2 %collective-permute-start.21 = (bf16[32,4096]{1,0:T(8,128)(2,1)S(1)}, bf16[32,4096]{1,0:T(8,128)(2,1)S(1)}, u32[]{:S(2)}, u32[]{:S(2)}) collective-permute-start(bf16[32,4096]{1,0:T(8,128)(2,1)S(1)} %add_convert_fusion.3), channel_id=1, source_target_pairs={{4,8},{8,4},{5,9},{9,5},{6,10},{10,6},{7,11},{11,7},{20,24},{24,20... | collective-permute-start | bytes 786440 | tf_op jit(solution)/shard_map/ppermute | solution.py:99
  (7 other events, 18.0 us)

commit v24 on v23

--- a/solution.py
+++ b/solution.py
@@ -147,12 +147,6 @@
     if size > 1:
         total = total + up.astype(jnp.float32) + down.astype(jnp.float32)
     return total
-
-
-def column_lse(scores):
-    peak = jnp.max(scores, axis=0, keepdims=True)
-    total = jnp.sum(jnp.exp(scores - peak), axis=0, keepdims=True)
-    return peak + jnp.log(total)
 
 
 def at_end():
@@ -336,10 +330,12 @@
 
 def write_packet(packet_ref, scores, route_ref):
     top, rows = route_ref.shape
-    packet_ref[0:1, :] = column_lse(scores)
-    packet_ref[1:2, :] = jnp.zeros((1, packet_ref.shape[1]), jnp.float32)
+    peak = jnp.max(scores, axis=0, keepdims=True)
+    packet_ref[0:1, :] = peak
+    packet_ref[1:2, :] = jnp.sum(jnp.exp(scores - peak), axis=0, keepdims=True)
+    packet_ref[2:3, :] = jnp.zeros((1, packet_ref.shape[1]), jnp.float32)
     for t in range(top):
-        packet_ref[1:2, t * rows : (t + 1) * rows] = route_ref[t : t + 1, :].astype(jnp.float32)
+        packet_ref[2:3, t * rows : (t + 1) * rows] = route_ref[t : t + 1, :].astype(jnp.float32)
 
 
 def score_kernel(readers, finish, *refs):
@@ -375,7 +371,7 @@
         partial(score_kernel, slots // rows, finish),
         out_shape=(
             jax.ShapeDtypeStruct((refs, slots), jnp.float32),
-            jax.ShapeDtypeStruct((2, slots), jnp.float32),
+            jax.ShapeDtypeStruct((3, slots), jnp.float32),
             jax.ShapeDtypeStruct((slots, width), jnp.bfloat16),
         ),
         in_specs=[VMEM_SPEC] * (len(far) + 5),
@@ -402,7 +398,7 @@
 def make_packet(scores, routes):
     return pl.pallas_call(
         packet_kernel,
-        out_shape=jax.ShapeDtypeStruct((2, scores.shape[1]), jnp.float32),
+        out_shape=jax.ShapeDtypeStruct((3, scores.shape[1]), jnp.float32),
         name="packet",
     )(scores, routes)
 
@@ -411,7 +407,7 @@
     reader = lax.axis_index("reader")
     readers = len(packets)
     for t in range(route_ref.shape[0]):
-        routes = [ref[1:2, t * rows : (t + 1) * rows] for ref in packets]
+        routes = [ref[2:3, t * rows : (t + 1) * rows] for ref in packets]
         bit = 1
         while bit < readers:
             flip = (reader & bit) > 0
@@ -445,9 +441,9 @@
     highest = kept[0]
     for value in kept[1:]:
         highest = jnp.maximum(highest, value)
-    spread = jnp.exp(kept[0] - highest)
-    for value in kept[1:]:
-        spread = spread + jnp.exp(value - highest)
+    spread = packets[0][1:2, :] * jnp.exp(kept[0] - highest)
+    for packet, value in zip(packets[1:], kept[1:]):
+        spread = spread + packet[1:2, :] * jnp.exp(value - highest)
     norm = highest + jnp.log(spread)
     norm_ref[...] = norm
     exponent = jnp.where(mine, score_ref[...] - norm, -jnp.inf)

time: 89 us -> 89.1 us (level)
  no operation moved by 1% of the time
where the time goes in v24:
time: 89.1 us; the launch traced here: 88.6 us
  starting transfers between devices  51 us (57%)
  waiting for transfers between devices  21.3 us (24%)
  local copies, waits for them, and re-layouts  7.48 us (8%)
  Pallas kernels  7.36 us (8%)
    ppermute x2, starting transfers between devices, staged_gather(): far = lax.ppermute(across, 'blk', SIDES)  9.77 us
    ppermute x2, starting transfers between devices, pair_scatter(): from_side = lax.ppermute(near, axis, SIDES)  9.54 us
    ppermute x2, waiting for transfers between devices, pair_scatter(): from_side = lax.ppermute(near, axis, SIDES)  9.38 us
    ppermute x2, starting transfers between devices, staged_gather(): end = lax.ppermute(across_far, 'blk', SIDES)  7.71 us
    ppermute x2, starting transfers between devices, staged_gather(): lax.ppermute(one, 'blk', SIDES)  6.09 us
    ppermute x2, starting transfers between devices, pair_scatter(): for_far_middle = [lax.ppermute(part, axis, SIDES) for part in second]  5.31 us
    ppermute x6, starting transfers between devices, swap_bits(): lax.ppermute(block, axis, [(i, i ^ bits) for i in range(lax.axis_size(axi...  5.01 us
    unnamed x10, local copies, waits for them, and re-layouts  4.96 us
  transfers between devices with their start and end apart: 26, of which 9 were waited for; matrix products, arithmetic and copies ran while one was open for 3% of the time, Pallas kernels for 5%

profile of v24, /device:TPU:0, one launch (start us, length us, event | category | flops | bytes accessed | tf_op | source)
XLA Modules:
  0.0 88.6 jit_solution(6360707253654217636)
XLA Ops:
  1.1 2.6 %collective-permute-start = (bf16[96,8192]{1,0:T(8,128)(2,1)}, bf16[96,8192]{1,0:T(8,128)(2,1)S(1)}, u32[]{:S(2)}, u32[]{:S(2)}) collective-permute-start(bf16[96,8192]{1,0:T(8,128)(2,1)} %refs_0_.1), channel_id=1, source_target_pairs={{0,2},{1,3},{2,0},{3,1},{4,6},{5,7},{6,4},{7,5},{8,10},{9,11},{10,... | collective-permute-start | bytes 4718600 | tf_op jit(solution)/shard_map/ppermute | solution.py:20
  4.7 1.6 %collective-permute-start.1 = (bf16[32,4608]{1,0:T(8,128)(2,1)S(1)}, bf16[32,4608]{1,0:T(8,128)(2,1)S(1)}, u32[]{:S(2)}, u32[]{:S(2)}) collective-permute-start(bf16[32,4608]{1,0:T(8,128)(2,1)S(1)} %slice.8.refs_2_), channel_id=1, source_target_pairs={{0,4},{4,0},{8,12},{12,8},{1,5},{5,1},{9,13},{13,9},{2,6},{6,2},{1... | collective-permute-start | bytes 884744 | tf_op jit(solution)/shard_map/ppermute | solution.py:43
  8.0 4.4 %collective-permute-start.7 = (bf16[32,3584]{1,0:T(8,128)(2,1)S(1)}, bf16[32,3584]{1,0:T(8,128)(2,1)S(1)}, u32[]{:S(2)}, u32[]{:S(2)}) collective-permute-start(bf16[32,3584]{1,0:T(8,128)(2,1)S(1)} %slice.9.refs_3_), channel_id=1, source_target_pairs={{0,4},{4,0},{8,12},{12,8},{1,5},{5,1},{9,13},{13,9},{2,6},{6,2},{1... | collective-permute-start | bytes 688136 | tf_op jit(solution)/shard_map/ppermute | solution.py:43
  12.4 2.2 %collective-permute-done.1.refs_4_ = bf16[32,4608]{1,0:T(8,128)(2,1)S(1)} collective-permute-done((bf16[32,4608]{1,0:T(8,128)(2,1)S(1)}, bf16[32,4608]{1,0:T(8,128)(2,1)S(1)}, u32[]{:S(2)}, u32[]{:S(2)}) %collective-permute-start.1) | collective-permute-done | bytes 294944 | tf_op jit(solution)/shard_map/ppermute | solution.py:43
  15.3 4.5 %collective-permute-start.3 = (bf16[32,4608]{1,0:T(8,128)(2,1)S(1)}, bf16[32,4608]{1,0:T(8,128)(2,1)S(1)}, u32[]{:S(2)}, u32[]{:S(2)}) collective-permute-start(bf16[32,4608]{1,0:T(8,128)(2,1)S(1)} %collective-permute-done.2.refs_5_), channel_id=1, source_target_pairs={{0,4},{4,0},{8,12},{12,8},{1,5},{5,1},{9,13},{13,9},{2,6},{6,2},{1... | collective-permute-start | bytes 884744 | tf_op jit(solution)/shard_map/ppermute | solution.py:52
  20.4 5.3 %collective-permute-start.9 = (bf16[32,3584]{1,0:T(8,128)(2,1)S(1)}, bf16[32,3584]{1,0:T(8,128)(2,1)S(1)}, u32[]{:S(2)}, u32[]{:S(2)}) collective-permute-start(bf16[32,3584]{1,0:T(8,128)(2,1)S(1)} %collective-permute-done.8.refs_7_), channel_id=1, source_target_pairs={{0,4},{4,0},{8,12},{12,8},{1,5},{5,1},{9,13},{13,9},{2,6},{6,2},{1... | collective-permute-start | bytes 688136 | tf_op jit(solution)/shard_map/ppermute | solution.py:52
  26.4 1.2 %collective-permute-done.3.refs_0_ = bf16[32,4608]{1,0:T(8,128)(2,1)S(1)} collective-permute-done((bf16[32,4608]{1,0:T(8,128)(2,1)S(1)}, bf16[32,4608]{1,0:T(8,128)(2,1)S(1)}, u32[]{:S(2)}, u32[]{:S(2)}) %collective-permute-start.3) | collective-permute-done | bytes 294944 | tf_op jit(solution)/shard_map/ppermute | solution.py:52
  27.7 4.4 %collective-permute-start.6 = (bf16[32,4608]{1,0:T(8,128)(2,1)S(1)}, bf16[32,4608]{1,0:T(8,128)(2,1)S(1)}, u32[]{:S(2)}, u32[]{:S(2)}) collective-permute-start(bf16[32,4608]{1,0:T(8,128)(2,1)S(1)} %collective-permute-done.5.refs_1_), channel_id=1, source_target_pairs={{0,4},{4,0},{8,12},{12,8},{1,5},{5,1},{9,13},{13,9},{2,6},{6,2},{1... | collective-permute-start | bytes 884744 | tf_op jit(solution)/shard_map/ppermute | solution.py:56
  32.1 3.3 %collective-permute-start.11 = (bf16[32,3584]{1,0:T(8,128)(2,1)S(1)}, bf16[32,3584]{1,0:T(8,128)(2,1)S(1)}, u32[]{:S(2)}, u32[]{:S(2)}) collective-permute-start(bf16[32,3584]{1,0:T(8,128)(2,1)S(1)} %collective-permute-done.10.refs_3_), channel_id=1, source_target_pairs={{0,4},{4,0},{8,12},{12,8},{1,5},{5,1},{9,13},{13,9},{2,6},{6,2},{1... | collective-permute-start | bytes 688136 | tf_op jit(solution)/shard_map/ppermute | solution.py:56
  35.4 1.4 %copy-done.2 = bf16[96,8192]{1,0:T(8,128)(2,1)S(1)} copy-done((bf16[96,8192]{1,0:T(8,128)(2,1)S(1)}, bf16[96,8192]{1,0:T(8,128)(2,1)}, u32[]{:S(2)}) %copy-start.2) | copy-done | bytes 1572888
  37.5 1.1 %stage.1 = (bf16[64,8192]{1,0:T(8,128)(2,1)S(1)}, f32[64,1]{1,0:T(8,128)S(1)}, bf16[192,8192]{1,0:T(8,128)(2,1)S(1)}, f32[1,8192]{1,0:T(1,128)S(1)}) custom-call(bf16[96,8192]{1,0:T(8,128)(2,1)S(1)} %copy-done.2, bf16[96,8192]{1,0:T(8,128)(2,1)S(1)} %collective-permute-done.4.refs_1_, bf16[32,4608]{1,0:T(8,128)(2,1)S(1)} %slice.8.refs_2_, ...), custom_call_target="tpu_custom_call" | custom-call | flops 4194304 | bytes 12000000 | tf_op jit(solution)/shard_map/stage/pallas_call | solution.py:239
  38.9 2.8 %collective-permute-done.11.refs_6_ = bf16[32,3584]{1,0:T(8,128)(2,1)S(1)} collective-permute-done((bf16[32,3584]{1,0:T(8,128)(2,1)S(1)}, bf16[32,3584]{1,0:T(8,128)(2,1)S(1)}, u32[]{:S(2)}, u32[]{:S(2)}) %collective-permute-start.11) | collective-permute-done | bytes 229408 | tf_op jit(solution)/shard_map/ppermute | solution.py:56
  41.7 2.9 %stage_rest.1 = (bf16[8192,128]{1,0:T(8,128)(2,1)S(1)}, f32[128,1]{1,0:T(8,128)S(1)}, bf16[384,8192]{1,0:T(8,128)(2,1)S(1)}, f32[384,128]{1,0:T(8,128)S(1)}) custom-call(bf16[32,4608]{1,0:T(8,128)(2,1)S(1)} %collective-permute-done.3.refs_0_, bf16[32,4608]{1,0:T(8,128)(2,1)S(1)} %collective-permute-done.5.refs_1_, ...), custom_call_target="tpu_custom_call" | custom-call | flops 8388608 | bytes 12000000 | tf_op jit(solution)/shard_map/stage_rest/pallas_call | solution.py:307
  46.8 1.2 %collective-permute-start.15 = (f32[3,384]{1,0:T(4,128)S(1)}, f32[3,384]{1,0:T(4,128)S(1)}, u32[]{:S(2)}, u32[]{:S(2)}) collective-permute-start(f32[3,384]{1,0:T(4,128)S(1)} %get-tuple-element.58.refs_0_), channel_id=1, source_target_pairs={{0,3},{1,2},{2,1},{3,0},{4,7},{5,6},{6,5},{7,4},{8,11},{9,10},{10,... | collective-permute-start | bytes 13832 | tf_op jit(solution)/shard_map/ppermute | solution.py:20
  47.9 1.9 %collective-permute-done.14.refs_2_ = f32[3,384]{1,0:T(4,128)S(1)} collective-permute-done((f32[3,384]{1,0:T(4,128)S(1)}, f32[3,384]{1,0:T(4,128)S(1)}, u32[]{:S(2)}, u32[]{:S(2)}) %collective-permute-start.14) | collective-permute-done | bytes 4640 | tf_op jit(solution)/shard_map/ppermute | solution.py:20
  50.8 2.1 %collective-permute-start.16 = (bf16[32,4096]{1,0:T(8,128)(2,1)S(1)}, bf16[32,4096]{1,0:T(8,128)(2,1)S(1)}, u32[]{:S(2)}, u32[]{:S(2)}) collective-permute-start(bf16[32,4096]{1,0:T(8,128)(2,1)S(1)} %get-tuple-element.64), channel_id=1, source_target_pairs={{0,4},{4,0},{8,12},{12,8},{1,5},{5,1},{9,13},{13,9},{2,6},{6,2},{1... | collective-permute-start | bytes 786440 | tf_op jit(solution)/shard_map/ppermute | solution.py:91
  52.8 2.8 %copy-done.1 = bf16[384,8192]{1,0:T(8,128)(2,1)S(1)} copy-done((bf16[384,8192]{1,0:T(8,128)(2,1)S(1)}, bf16[384,8192]{1,0:T(8,128)(2,1)}, u32[]{:S(2)}) %copy-start.1) | copy-done | bytes 6291480
  57.0 2.9 %collective-permute-done.16 = bf16[32,4096]{1,0:T(8,128)(2,1)S(1)} collective-permute-done((bf16[32,4096]{1,0:T(8,128)(2,1)S(1)}, bf16[32,4096]{1,0:T(8,128)(2,1)S(1)}, u32[]{:S(2)}, u32[]{:S(2)}) %collective-permute-start.16) | collective-permute-done | bytes 262176 | tf_op jit(solution)/shard_map/ppermute | solution.py:91
  59.9 2.0 %collective-permute-start.24 = (bf16[32,4096]{1,0:T(8,128)(2,1)S(1)}, bf16[32,4096]{1,0:T(8,128)(2,1)S(1)}, u32[]{:S(2)}, u32[]{:S(2)}) collective-permute-start(bf16[32,4096]{1,0:T(8,128)(2,1)S(1)} %get-tuple-element.69), channel_id=1, source_target_pairs={{0,4},{4,0},{8,12},{12,8},{1,5},{5,1},{9,13},{13,9},{2,6},{6,2},{1... | collective-permute-start | bytes 786440 | tf_op jit(solution)/shard_map/ppermute | solution.py:95
  62.7 3.3 %collective-permute-start.20 = (bf16[32,4096]{1,0:T(8,128)(2,1)S(1)}, bf16[32,4096]{1,0:T(8,128)(2,1)S(1)}, u32[]{:S(2)}, u32[]{:S(2)}) collective-permute-start(bf16[32,4096]{1,0:T(8,128)(2,1)S(1)} %get-tuple-element.65), channel_id=1, source_target_pairs={{0,4},{4,0},{8,12},{12,8},{1,5},{5,1},{9,13},{13,9},{2,6},{6,2},{1... | collective-permute-start | bytes 786440 | tf_op jit(solution)/shard_map/ppermute | solution.py:95
  66.9 4.8 %collective-permute-start.23 = (bf16[32,4096]{1,0:T(8,128)(2,1)S(1)}, bf16[32,4096]{1,0:T(8,128)(2,1)S(1)}, u32[]{:S(2)}, u32[]{:S(2)}) collective-permute-start(bf16[32,4096]{1,0:T(8,128)(2,1)S(1)} %fusion.1), channel_id=1, source_target_pairs={{0,4},{4,0},{8,12},{12,8},{1,5},{5,1},{9,13},{13,9},{2,6},{6,2},{1... | collective-permute-start | bytes 786440 | tf_op jit(solution)/shard_map/ppermute | solution.py:101
  72.5 4.8 %collective-permute-start.19 = (bf16[32,4096]{1,0:T(8,128)(2,1)S(1)}, bf16[32,4096]{1,0:T(8,128)(2,1)S(1)}, u32[]{:S(2)}, u32[]{:S(2)}) collective-permute-start(bf16[32,4096]{1,0:T(8,128)(2,1)S(1)} %fusion), channel_id=1, source_target_pairs={{0,4},{4,0},{8,12},{12,8},{1,5},{5,1},{9,13},{13,9},{2,6},{6,2},{1... | collective-permute-start | bytes 786440 | tf_op jit(solution)/shard_map/ppermute | solution.py:101
  78.0 4.5 %collective-permute-done.23 = bf16[32,4096]{1,0:T(8,128)(2,1)S(1)} collective-permute-done((bf16[32,4096]{1,0:T(8,128)(2,1)S(1)}, bf16[32,4096]{1,0:T(8,128)(2,1)S(1)}, u32[]{:S(2)}, u32[]{:S(2)}) %collective-permute-start.23) | collective-permute-done | bytes 262176 | tf_op jit(solution)/shard_map/ppermute | solution.py:101
  82.6 4.9 %collective-permute-done.19 = bf16[32,4096]{1,0:T(8,128)(2,1)S(1)} collective-permute-done((bf16[32,4096]{1,0:T(8,128)(2,1)S(1)}, bf16[32,4096]{1,0:T(8,128)(2,1)S(1)}, u32[]{:S(2)}, u32[]{:S(2)}) %collective-permute-start.19) | collective-permute-done | bytes 262176 | tf_op jit(solution)/shard_map/ppermute | solution.py:101
  (55 shorter events, 14.9 us)
Async XLA Ops:
  0.6 19.1 %collective-permute-start.4 = (bf16[96,8192]{1,0:T(8,128)(2,1)}, bf16[96,8192]{1,0:T(8,128)(2,1)S(1)}, u32[]{:S(2)}, u32[]{:S(2)}) collective-permute-start(bf16[96,8192]{1,0:T(8,128)(2,1)} %refs_0_.1), channel_id=1, source_target_pairs={{0,1},{1,0},{2,3},{3,2},{4,5},{5,4},{6,7},{7,6},{8,9},{9,8},{10,11... | collective-permute-start | bytes 4718600 | tf_op jit(solution)/shard_map/ppermute | solution.py:20
  1.1 37.8 %collective-permute-start = (bf16[96,8192]{1,0:T(8,128)(2,1)}, bf16[96,8192]{1,0:T(8,128)(2,1)S(1)}, u32[]{:S(2)}, u32[]{:S(2)}) collective-permute-start(bf16[96,8192]{1,0:T(8,128)(2,1)} %refs_0_.1), channel_id=1, source_target_pairs={{0,2},{1,3},{2,0},{3,1},{4,6},{5,7},{6,4},{7,5},{8,10},{9,11},{10,... | collective-permute-start | bytes 4718600 | tf_op jit(solution)/shard_map/ppermute | solution.py:20
  4.7 9.9 %collective-permute-start.1 = (bf16[32,4608]{1,0:T(8,128)(2,1)S(1)}, bf16[32,4608]{1,0:T(8,128)(2,1)S(1)}, u32[]{:S(2)}, u32[]{:S(2)}) collective-permute-start(bf16[32,4608]{1,0:T(8,128)(2,1)S(1)} %slice.8.refs_2_), channel_id=1, source_target_pairs={{0,4},{4,0},{8,12},{12,8},{1,5},{5,1},{9,13},{13,9},{2,6},{6,2},{1... | collective-permute-start | bytes 884744 | tf_op jit(solution)/shard_map/ppermute | solution.py:43
  6.3 8.9 %collective-permute-start.2 = (bf16[32,4608]{1,0:T(8,128)(2,1)S(1)}, bf16[32,4608]{1,0:T(8,128)(2,1)S(1)}, u32[]{:S(2)}, u32[]{:S(2)}) collective-permute-start(bf16[32,4608]{1,0:T(8,128)(2,1)S(1)} %slice.8.refs_2_), channel_id=1, source_target_pairs={{4,8},{8,4},{5,9},{9,5},{6,10},{10,6},{7,11},{11,7},{20,24},{24,20... | collective-permute-start | bytes 884744 | tf_op jit(solution)/shard_map/ppermute | solution.py:43
  8.0 12.5 %collective-permute-start.7 = (bf16[32,3584]{1,0:T(8,128)(2,1)S(1)}, bf16[32,3584]{1,0:T(8,128)(2,1)S(1)}, u32[]{:S(2)}, u32[]{:S(2)}) collective-permute-start(bf16[32,3584]{1,0:T(8,128)(2,1)S(1)} %slice.9.refs_3_), channel_id=1, source_target_pairs={{0,4},{4,0},{8,12},{12,8},{1,5},{5,1},{9,13},{13,9},{2,6},{6,2},{1... | collective-permute-start | bytes 688136 | tf_op jit(solution)/shard_map/ppermute | solution.py:43
  14.6 5.8 %collective-permute-start.8 = (bf16[32,3584]{1,0:T(8,128)(2,1)S(1)}, bf16[32,3584]{1,0:T(8,128)(2,1)S(1)}, u32[]{:S(2)}, u32[]{:S(2)}) collective-permute-start(bf16[32,3584]{1,0:T(8,128)(2,1)S(1)} %slice.9.refs_3_), channel_id=1, source_target_pairs={{4,8},{8,4},{5,9},{9,5},{6,10},{10,6},{7,11},{11,7},{20,24},{24,20... | collective-permute-start | bytes 688136 | tf_op jit(solution)/shard_map/ppermute | solution.py:43
  15.3 12.4 %collective-permute-start.3 = (bf16[32,4608]{1,0:T(8,128)(2,1)S(1)}, bf16[32,4608]{1,0:T(8,128)(2,1)S(1)}, u32[]{:S(2)}, u32[]{:S(2)}) collective-permute-start(bf16[32,4608]{1,0:T(8,128)(2,1)S(1)} %collective-permute-done.2.refs_5_), channel_id=1, source_target_pairs={{0,4},{4,0},{8,12},{12,8},{1,5},{5,1},{9,13},{13,9},{2,6},{6,2},{1... | collective-permute-start | bytes 884744 | tf_op jit(solution)/shard_map/ppermute | solution.py:52
  19.8 7.9 %collective-permute-start.5 = (bf16[32,4608]{1,0:T(8,128)(2,1)S(1)}, bf16[32,4608]{1,0:T(8,128)(2,1)S(1)}, u32[]{:S(2)}, u32[]{:S(2)}) collective-permute-start(bf16[32,4608]{1,0:T(8,128)(2,1)S(1)} %collective-permute-done.1.refs_4_), channel_id=1, source_target_pairs={{4,8},{8,4},{5,9},{9,5},{6,10},{10,6},{7,11},{11,7},{20,24},{24,20... | collective-permute-start | bytes 884744 | tf_op jit(solution)/shard_map/ppermute | solution.py:54
  20.4 11.6 %collective-permute-start.9 = (bf16[32,3584]{1,0:T(8,128)(2,1)S(1)}, bf16[32,3584]{1,0:T(8,128)(2,1)S(1)}, u32[]{:S(2)}, u32[]{:S(2)}) collective-permute-start(bf16[32,3584]{1,0:T(8,128)(2,1)S(1)} %collective-permute-done.8.refs_7_), channel_id=1, source_target_pairs={{0,4},{4,0},{8,12},{12,8},{1,5},{5,1},{9,13},{13,9},{2,6},{6,2},{1... | collective-permute-start | bytes 688136 | tf_op jit(solution)/shard_map/ppermute | solution.py:52
  25.8 6.3 %collective-permute-start.10 = (bf16[32,3584]{1,0:T(8,128)(2,1)S(1)}, bf16[32,3584]{1,0:T(8,128)(2,1)S(1)}, u32[]{:S(2)}, u32[]{:S(2)}) collective-permute-start(bf16[32,3584]{1,0:T(8,128)(2,1)S(1)} %collective-permute-done.7.refs_5_), channel_id=1, source_target_pairs={{4,8},{8,4},{5,9},{9,5},{6,10},{10,6},{7,11},{11,7},{20,24},{24,20... | collective-permute-start | bytes 688136 | tf_op jit(solution)/shard_map/ppermute | solution.py:54
  27.7 14.0 %collective-permute-start.6 = (bf16[32,4608]{1,0:T(8,128)(2,1)S(1)}, bf16[32,4608]{1,0:T(8,128)(2,1)S(1)}, u32[]{:S(2)}, u32[]{:S(2)}) collective-permute-start(bf16[32,4608]{1,0:T(8,128)(2,1)S(1)} %collective-permute-done.5.refs_1_), channel_id=1, source_target_pairs={{0,4},{4,0},{8,12},{12,8},{1,5},{5,1},{9,13},{13,9},{2,6},{6,2},{1... | collective-permute-start | bytes 884744 | tf_op jit(solution)/shard_map/ppermute | solution.py:56
  32.1 9.6 %collective-permute-start.11 = (bf16[32,3584]{1,0:T(8,128)(2,1)S(1)}, bf16[32,3584]{1,0:T(8,128)(2,1)S(1)}, u32[]{:S(2)}, u32[]{:S(2)}) collective-permute-start(bf16[32,3584]{1,0:T(8,128)(2,1)S(1)} %collective-permute-done.10.refs_3_), channel_id=1, source_target_pairs={{0,4},{4,0},{8,12},{12,8},{1,5},{5,1},{9,13},{13,9},{2,6},{6,2},{1... | collective-permute-start | bytes 688136 | tf_op jit(solution)/shard_map/ppermute | solution.py:56
  41.7 3.4 %collective-permute-start.12 = (bf16[96,8192]{1,0:T(8,128)(2,1)S(1)}, bf16[96,8192]{1,0:T(8,128)(2,1)S(1)}, u32[]{:S(2)}, u32[]{:S(2)}) collective-permute-start(bf16[96,8192]{1,0:T(8,128)(2,1)S(1)} %collective-permute-done.refs_9_), channel_id=1, source_target_pairs={{0,1},{1,0},{2,3},{3,2},{4,5},{5,4},{6,7},{7,6},{8,9},{9,8},{10,11... | collective-permute-start | bytes 4718600 | tf_op jit(solution)/shard_map/ppermute | solution.py:20
  46.2 3.7 %collective-permute-start.14 = (f32[3,384]{1,0:T(4,128)S(1)}, f32[3,384]{1,0:T(4,128)S(1)}, u32[]{:S(2)}, u32[]{:S(2)}) collective-permute-start(f32[3,384]{1,0:T(4,128)S(1)} %get-tuple-element.58.refs_0_), channel_id=1, source_target_pairs={{0,2},{1,3},{2,0},{3,1},{4,6},{5,7},{6,4},{7,5},{8,10},{9,11},{10,... | collective-permute-start | bytes 13832 | tf_op jit(solution)/shard_map/ppermute | solution.py:20
  50.8 9.2 %collective-permute-start.16 = (bf16[32,4096]{1,0:T(8,128)(2,1)S(1)}, bf16[32,4096]{1,0:T(8,128)(2,1)S(1)}, u32[]{:S(2)}, u32[]{:S(2)}) collective-permute-start(bf16[32,4096]{1,0:T(8,128)(2,1)S(1)} %get-tuple-element.64), channel_id=1, source_target_pairs={{0,4},{4,0},{8,12},{12,8},{1,5},{5,1},{9,13},{13,9},{2,6},{6,2},{1... | collective-permute-start | bytes 786440 | tf_op jit(solution)/shard_map/ppermute | solution.py:91
  56.3 9.7 %collective-permute-start.17 = (bf16[32,4096]{1,0:T(8,128)(2,1)S(1)}, bf16[32,4096]{1,0:T(8,128)(2,1)S(1)}, u32[]{:S(2)}, u32[]{:S(2)}) collective-permute-start(bf16[32,4096]{1,0:T(8,128)(2,1)S(1)} %get-tuple-element.66), channel_id=1, source_target_pairs={{0,4},{4,0},{8,12},{12,8},{1,5},{5,1},{9,13},{13,9},{2,6},{6,2},{1... | collective-permute-start | bytes 786440 | tf_op jit(solution)/shard_map/ppermute | solution.py:91
  59.9 11.7 %collective-permute-start.24 = (bf16[32,4096]{1,0:T(8,128)(2,1)S(1)}, bf16[32,4096]{1,0:T(8,128)(2,1)S(1)}, u32[]{:S(2)}, u32[]{:S(2)}) collective-permute-start(bf16[32,4096]{1,0:T(8,128)(2,1)S(1)} %get-tuple-element.69), channel_id=1, source_target_pairs={{0,4},{4,0},{8,12},{12,8},{1,5},{5,1},{9,13},{13,9},{2,6},{6,2},{1... | collective-permute-start | bytes 786440 | tf_op jit(solution)/shard_map/ppermute | solution.py:95
  62.0 4.7 %collective-permute-start.22 = (bf16[32,4096]{1,0:T(8,128)(2,1)S(1)}, bf16[32,4096]{1,0:T(8,128)(2,1)S(1)}, u32[]{:S(2)}, u32[]{:S(2)}) collective-permute-start(bf16[32,4096]{1,0:T(8,128)(2,1)S(1)} %add_convert_fusion.2), channel_id=1, source_target_pairs={{4,8},{8,4},{5,9},{9,5},{6,10},{10,6},{7,11},{11,7},{20,24},{24,20... | collective-permute-start | bytes 786440 | tf_op jit(solution)/shard_map/ppermute | solution.py:98
  62.7 14.5 %collective-permute-start.20 = (bf16[32,4096]{1,0:T(8,128)(2,1)S(1)}, bf16[32,4096]{1,0:T(8,128)(2,1)S(1)}, u32[]{:S(2)}, u32[]{:S(2)}) collective-permute-start(bf16[32,4096]{1,0:T(8,128)(2,1)S(1)} %get-tuple-element.65), channel_id=1, source_target_pairs={{0,4},{4,0},{8,12},{12,8},{1,5},{5,1},{9,13},{13,9},{2,6},{6,2},{1... | collective-permute-start | bytes 786440 | tf_op jit(solution)/shard_map/ppermute | solution.py:95
  66.1 6.3 %collective-permute-start.18 = (bf16[32,4096]{1,0:T(8,128)(2,1)S(1)}, bf16[32,4096]{1,0:T(8,128)(2,1)S(1)}, u32[]{:S(2)}, u32[]{:S(2)}) collective-permute-start(bf16[32,4096]{1,0:T(8,128)(2,1)S(1)} %add_convert_fusion.5), channel_id=1, source_target_pairs={{4,8},{8,4},{5,9},{9,5},{6,10},{10,6},{7,11},{11,7},{20,24},{24,20... | collective-permute-start | bytes 786440 | tf_op jit(solution)/shard_map/ppermute | solution.py:98
  66.9 15.6 %collective-permute-start.23 = (bf16[32,4096]{1,0:T(8,128)(2,1)S(1)}, bf16[32,4096]{1,0:T(8,128)(2,1)S(1)}, u32[]{:S(2)}, u32[]{:S(2)}) collective-permute-start(bf16[32,4096]{1,0:T(8,128)(2,1)S(1)} %fusion.1), channel_id=1, source_target_pairs={{0,4},{4,0},{8,12},{12,8},{1,5},{5,1},{9,13},{13,9},{2,6},{6,2},{1... | collective-permute-start | bytes 786440 | tf_op jit(solution)/shard_map/ppermute | solution.py:101
  71.7 10.8 %collective-permute-start.25 = (bf16[32,4096]{1,0:T(8,128)(2,1)S(1)}, bf16[32,4096]{1,0:T(8,128)(2,1)S(1)}, u32[]{:S(2)}, u32[]{:S(2)}) collective-permute-start(bf16[32,4096]{1,0:T(8,128)(2,1)S(1)} %add_convert_fusion), channel_id=1, source_target_pairs={{4,8},{8,4},{5,9},{9,5},{6,10},{10,6},{7,11},{11,7},{20,24},{24,20... | collective-permute-start | bytes 786440 | tf_op jit(solution)/shard_map/ppermute | solution.py:99
  72.5 15.0 %collective-permute-start.19 = (bf16[32,4096]{1,0:T(8,128)(2,1)S(1)}, bf16[32,4096]{1,0:T(8,128)(2,1)S(1)}, u32[]{:S(2)}, u32[]{:S(2)}) collective-permute-start(bf16[32,4096]{1,0:T(8,128)(2,1)S(1)} %fusion), channel_id=1, source_target_pairs={{0,4},{4,0},{8,12},{12,8},{1,5},{5,1},{9,13},{13,9},{2,6},{6,2},{1... | collective-permute-start | bytes 786440 | tf_op jit(solution)/shard_map/ppermute | solution.py:101
  77.3 10.2 %collective-permute-start.21 = (bf16[32,4096]{1,0:T(8,128)(2,1)S(1)}, bf16[32,4096]{1,0:T(8,128)(2,1)S(1)}, u32[]{:S(2)}, u32[]{:S(2)}) collective-permute-start(bf16[32,4096]{1,0:T(8,128)(2,1)S(1)} %add_convert_fusion.3), channel_id=1, source_target_pairs={{4,8},{8,4},{5,9},{9,5},{6,10},{10,6},{7,11},{11,7},{20,24},{24,20... | collective-permute-start | bytes 786440 | tf_op jit(solution)/shard_map/ppermute | solution.py:99
  (7 other events, 18.2 us)

commit v25 on v24

--- a/solution.py
+++ b/solution.py
@@ -104,29 +104,35 @@
     return beside(totals)
 
 
-def beside_kernel(count, *refs):
-    out_ref, sems = refs[count:]
-    copies, stop = [], out_ref.shape[1]
-    for i, ref in enumerate(refs[:count]):
-        start = stop - ref.shape[1]
-        copies.append(pltpu.make_async_copy(ref, out_ref.at[:, start:stop], sems.at[i]))
-        copies[-1].start()
-        stop = start
-    for copy in copies:
-        copy.wait()
+def put_kernel(start, piece_ref, *refs):
+    out_ref, sem = refs[-2:]
+    width = piece_ref.shape[1]
+    copy = pltpu.make_async_copy(piece_ref, out_ref.at[:, start : start + width], sem)
+    copy.start()
+    copy.wait()
+
+
+def put(piece, start, width, out=None):
+    operands = [piece] if out is None else [piece, out]
+    return pl.pallas_call(
+        partial(put_kernel, start),
+        out_shape=jax.ShapeDtypeStruct((piece.shape[0], width), piece.dtype),
+        in_specs=[VMEM_SPEC, ANY_SPEC][: len(operands)],
+        out_specs=ANY_SPEC,
+        scratch_shapes=[pltpu.SemaphoreType.DMA],
+        input_output_aliases={} if out is None else {1: 0},
+        compiler_params=pltpu.CompilerParams(vmem_limit_bytes=SUMS_VMEM),
+        name="put",
+    )(*operands)
 
 
 def beside(pieces):
     width = sum(piece.shape[1] for piece in pieces)
-    return pl.pallas_call(
-        partial(beside_kernel, len(pieces)),
-        out_shape=jax.ShapeDtypeStruct((pieces[0].shape[0], width), pieces[0].dtype),
-        in_specs=[VMEM_SPEC] * len(pieces),
-        out_specs=ANY_SPEC,
-        scratch_shapes=[pltpu.SemaphoreType.DMA((len(pieces),))],
-        compiler_params=pltpu.CompilerParams(vmem_limit_bytes=SUMS_VMEM),
-        name="beside",
-    )(*pieces[::-1])
+    out, start = None, 0
+    for piece in pieces:
+        out = put(piece, start, width, out)
+        start += piece.shape[1]
+    return out
 
 
 def line_scatter(pieces, axis):

time: 89.1 us -> 88.9 us (level)
  transfers between devices with their start and end apart: 26 -> 26, of which waited for: 9 -> 9; matrix products, arithmetic and copies ran while one was open for 3% -> 3% of each run, Pallas kernels for 5% -> 6%
where the time goes in v25:
time: 88.9 us; the launch traced here: 88.4 us
  starting transfers between devices  51 us (57%)
  waiting for transfers between devices  20.5 us (23%)
  Pallas kernels  7.98 us (9%)
  local copies, waits for them, and re-layouts  7.48 us (8%)
    ppermute x2, starting transfers between devices, staged_gather(): far = lax.ppermute(across, 'blk', SIDES)  9.77 us
    ppermute x2, starting transfers between devices, pair_scatter(): from_side = lax.ppermute(near, axis, SIDES)  9.54 us
    ppermute x2, waiting for transfers between devices, pair_scatter(): from_side = lax.ppermute(near, axis, SIDES)  8.57 us
    ppermute x2, starting transfers between devices, staged_gather(): end = lax.ppermute(across_far, 'blk', SIDES)  7.71 us
    ppermute x2, starting transfers between devices, staged_gather(): lax.ppermute(one, 'blk', SIDES)  6.09 us
    ppermute x2, starting transfers between devices, pair_scatter(): for_far_middle = [lax.ppermute(part, axis, SIDES) for part in second]  5.31 us
    ppermute x6, starting transfers between devices, swap_bits(): lax.ppermute(block, axis, [(i, i ^ bits) for i in range(lax.axis_size(axi...  5.01 us
    unnamed x10, local copies, waits for them, and re-layouts  4.96 us
  transfers between devices with their start and end apart: 26, of which 9 were waited for; matrix products, arithmetic and copies ran while one was open for 3% of the time, Pallas kernels for 6%

profile of v25, /device:TPU:0, one launch (start us, length us, event | category | flops | bytes accessed | tf_op | source)
XLA Modules:
  0.0 88.4 jit_solution(13639567938911602573)
XLA Ops:
  1.1 2.6 %collective-permute-start = (bf16[96,8192]{1,0:T(8,128)(2,1)}, bf16[96,8192]{1,0:T(8,128)(2,1)S(1)}, u32[]{:S(2)}, u32[]{:S(2)}) collective-permute-start(bf16[96,8192]{1,0:T(8,128)(2,1)} %refs_0_.1), channel_id=1, source_target_pairs={{0,2},{1,3},{2,0},{3,1},{4,6},{5,7},{6,4},{7,5},{8,10},{9,11},{10,... | collective-permute-start | bytes 4718600 | tf_op jit(solution)/shard_map/ppermute | solution.py:20
  4.7 1.6 %collective-permute-start.1 = (bf16[32,4608]{1,0:T(8,128)(2,1)S(1)}, bf16[32,4608]{1,0:T(8,128)(2,1)S(1)}, u32[]{:S(2)}, u32[]{:S(2)}) collective-permute-start(bf16[32,4608]{1,0:T(8,128)(2,1)S(1)} %slice.8.refs_2_), channel_id=1, source_target_pairs={{0,4},{4,0},{8,12},{12,8},{1,5},{5,1},{9,13},{13,9},{2,6},{6,2},{1... | collective-permute-start | bytes 884744 | tf_op jit(solution)/shard_map/ppermute | solution.py:43
  8.0 4.4 %collective-permute-start.7 = (bf16[32,3584]{1,0:T(8,128)(2,1)S(1)}, bf16[32,3584]{1,0:T(8,128)(2,1)S(1)}, u32[]{:S(2)}, u32[]{:S(2)}) collective-permute-start(bf16[32,3584]{1,0:T(8,128)(2,1)S(1)} %slice.9.refs_3_), channel_id=1, source_target_pairs={{0,4},{4,0},{8,12},{12,8},{1,5},{5,1},{9,13},{13,9},{2,6},{6,2},{1... | collective-permute-start | bytes 688136 | tf_op jit(solution)/shard_map/ppermute | solution.py:43
  12.4 2.2 %collective-permute-done.1.refs_4_ = bf16[32,4608]{1,0:T(8,128)(2,1)S(1)} collective-permute-done((bf16[32,4608]{1,0:T(8,128)(2,1)S(1)}, bf16[32,4608]{1,0:T(8,128)(2,1)S(1)}, u32[]{:S(2)}, u32[]{:S(2)}) %collective-permute-start.1) | collective-permute-done | bytes 294944 | tf_op jit(solution)/shard_map/ppermute | solution.py:43
  15.3 4.5 %collective-permute-start.3 = (bf16[32,4608]{1,0:T(8,128)(2,1)S(1)}, bf16[32,4608]{1,0:T(8,128)(2,1)S(1)}, u32[]{:S(2)}, u32[]{:S(2)}) collective-permute-start(bf16[32,4608]{1,0:T(8,128)(2,1)S(1)} %collective-permute-done.2.refs_5_), channel_id=1, source_target_pairs={{0,4},{4,0},{8,12},{12,8},{1,5},{5,1},{9,13},{13,9},{2,6},{6,2},{1... | collective-permute-start | bytes 884744 | tf_op jit(solution)/shard_map/ppermute | solution.py:52
  20.4 5.3 %collective-permute-start.9 = (bf16[32,3584]{1,0:T(8,128)(2,1)S(1)}, bf16[32,3584]{1,0:T(8,128)(2,1)S(1)}, u32[]{:S(2)}, u32[]{:S(2)}) collective-permute-start(bf16[32,3584]{1,0:T(8,128)(2,1)S(1)} %collective-permute-done.8.refs_7_), channel_id=1, source_target_pairs={{0,4},{4,0},{8,12},{12,8},{1,5},{5,1},{9,13},{13,9},{2,6},{6,2},{1... | collective-permute-start | bytes 688136 | tf_op jit(solution)/shard_map/ppermute | solution.py:52
  26.4 1.2 %collective-permute-done.3.refs_0_ = bf16[32,4608]{1,0:T(8,128)(2,1)S(1)} collective-permute-done((bf16[32,4608]{1,0:T(8,128)(2,1)S(1)}, bf16[32,4608]{1,0:T(8,128)(2,1)S(1)}, u32[]{:S(2)}, u32[]{:S(2)}) %collective-permute-start.3) | collective-permute-done | bytes 294944 | tf_op jit(solution)/shard_map/ppermute | solution.py:52
  27.7 4.4 %collective-permute-start.6 = (bf16[32,4608]{1,0:T(8,128)(2,1)S(1)}, bf16[32,4608]{1,0:T(8,128)(2,1)S(1)}, u32[]{:S(2)}, u32[]{:S(2)}) collective-permute-start(bf16[32,4608]{1,0:T(8,128)(2,1)S(1)} %collective-permute-done.5.refs_1_), channel_id=1, source_target_pairs={{0,4},{4,0},{8,12},{12,8},{1,5},{5,1},{9,13},{13,9},{2,6},{6,2},{1... | collective-permute-start | bytes 884744 | tf_op jit(solution)/shard_map/ppermute | solution.py:56
  32.1 3.3 %collective-permute-start.11 = (bf16[32,3584]{1,0:T(8,128)(2,1)S(1)}, bf16[32,3584]{1,0:T(8,128)(2,1)S(1)}, u32[]{:S(2)}, u32[]{:S(2)}) collective-permute-start(bf16[32,3584]{1,0:T(8,128)(2,1)S(1)} %collective-permute-done.10.refs_3_), channel_id=1, source_target_pairs={{0,4},{4,0},{8,12},{12,8},{1,5},{5,1},{9,13},{13,9},{2,6},{6,2},{1... | collective-permute-start | bytes 688136 | tf_op jit(solution)/shard_map/ppermute | solution.py:56
  35.4 1.4 %copy-done.2 = bf16[96,8192]{1,0:T(8,128)(2,1)S(1)} copy-done((bf16[96,8192]{1,0:T(8,128)(2,1)S(1)}, bf16[96,8192]{1,0:T(8,128)(2,1)}, u32[]{:S(2)}) %copy-start.2) | copy-done | bytes 1572888
  37.5 1.1 %stage.1 = (bf16[64,8192]{1,0:T(8,128)(2,1)S(1)}, f32[64,1]{1,0:T(8,128)S(1)}, bf16[192,8192]{1,0:T(8,128)(2,1)S(1)}, f32[1,8192]{1,0:T(1,128)S(1)}) custom-call(bf16[96,8192]{1,0:T(8,128)(2,1)S(1)} %copy-done.2, bf16[96,8192]{1,0:T(8,128)(2,1)S(1)} %collective-permute-done.4.refs_1_, bf16[32,4608]{1,0:T(8,128)(2,1)S(1)} %slice.8.refs_2_, ...), custom_call_target="tpu_custom_call" | custom-call | flops 4194304 | bytes 12000000 | tf_op jit(solution)/shard_map/stage/pallas_call | solution.py:245
  38.9 2.8 %collective-permute-done.11.refs_6_ = bf16[32,3584]{1,0:T(8,128)(2,1)S(1)} collective-permute-done((bf16[32,3584]{1,0:T(8,128)(2,1)S(1)}, bf16[32,3584]{1,0:T(8,128)(2,1)S(1)}, u32[]{:S(2)}, u32[]{:S(2)}) %collective-permute-start.11) | collective-permute-done | bytes 229408 | tf_op jit(solution)/shard_map/ppermute | solution.py:56
  41.7 2.9 %stage_rest.1 = (bf16[8192,128]{1,0:T(8,128)(2,1)S(1)}, f32[128,1]{1,0:T(8,128)S(1)}, bf16[384,8192]{1,0:T(8,128)(2,1)S(1)}, f32[384,128]{1,0:T(8,128)S(1)}) custom-call(bf16[32,4608]{1,0:T(8,128)(2,1)S(1)} %collective-permute-done.3.refs_0_, bf16[32,4608]{1,0:T(8,128)(2,1)S(1)} %collective-permute-done.5.refs_1_, ...), custom_call_target="tpu_custom_call" | custom-call | flops 8388608 | bytes 12000000 | tf_op jit(solution)/shard_map/stage_rest/pallas_call | solution.py:313
  46.8 1.2 %collective-permute-start.15 = (f32[3,384]{1,0:T(4,128)S(1)}, f32[3,384]{1,0:T(4,128)S(1)}, u32[]{:S(2)}, u32[]{:S(2)}) collective-permute-start(f32[3,384]{1,0:T(4,128)S(1)} %get-tuple-element.58.refs_0_), channel_id=1, source_target_pairs={{0,3},{1,2},{2,1},{3,0},{4,7},{5,6},{6,5},{7,4},{8,11},{9,10},{10,... | collective-permute-start | bytes 13832 | tf_op jit(solution)/shard_map/ppermute | solution.py:20
  47.9 1.9 %collective-permute-done.14.refs_2_ = f32[3,384]{1,0:T(4,128)S(1)} collective-permute-done((f32[3,384]{1,0:T(4,128)S(1)}, f32[3,384]{1,0:T(4,128)S(1)}, u32[]{:S(2)}, u32[]{:S(2)}) %collective-permute-start.14) | collective-permute-done | bytes 4640 | tf_op jit(solution)/shard_map/ppermute | solution.py:20
  50.8 2.1 %collective-permute-start.16 = (bf16[32,4096]{1,0:T(8,128)(2,1)S(1)}, bf16[32,4096]{1,0:T(8,128)(2,1)S(1)}, u32[]{:S(2)}, u32[]{:S(2)}) collective-permute-start(bf16[32,4096]{1,0:T(8,128)(2,1)S(1)} %get-tuple-element.64), channel_id=1, source_target_pairs={{0,4},{4,0},{8,12},{12,8},{1,5},{5,1},{9,13},{13,9},{2,6},{6,2},{1... | collective-permute-start | bytes 786440 | tf_op jit(solution)/shard_map/ppermute | solution.py:91
  52.8 2.8 %copy-done.1 = bf16[384,8192]{1,0:T(8,128)(2,1)S(1)} copy-done((bf16[384,8192]{1,0:T(8,128)(2,1)S(1)}, bf16[384,8192]{1,0:T(8,128)(2,1)}, u32[]{:S(2)}) %copy-start.1) | copy-done | bytes 6291480
  57.0 2.9 %collective-permute-done.16 = bf16[32,4096]{1,0:T(8,128)(2,1)S(1)} collective-permute-done((bf16[32,4096]{1,0:T(8,128)(2,1)S(1)}, bf16[32,4096]{1,0:T(8,128)(2,1)S(1)}, u32[]{:S(2)}, u32[]{:S(2)}) %collective-permute-start.16) | collective-permute-done | bytes 262176 | tf_op jit(solution)/shard_map/ppermute | solution.py:91
  59.9 2.0 %collective-permute-start.24 = (bf16[32,4096]{1,0:T(8,128)(2,1)S(1)}, bf16[32,4096]{1,0:T(8,128)(2,1)S(1)}, u32[]{:S(2)}, u32[]{:S(2)}) collective-permute-start(bf16[32,4096]{1,0:T(8,128)(2,1)S(1)} %get-tuple-element.69), channel_id=1, source_target_pairs={{0,4},{4,0},{8,12},{12,8},{1,5},{5,1},{9,13},{13,9},{2,6},{6,2},{1... | collective-permute-start | bytes 786440 | tf_op jit(solution)/shard_map/ppermute | solution.py:95
  62.7 3.3 %collective-permute-start.20 = (bf16[32,4096]{1,0:T(8,128)(2,1)S(1)}, bf16[32,4096]{1,0:T(8,128)(2,1)S(1)}, u32[]{:S(2)}, u32[]{:S(2)}) collective-permute-start(bf16[32,4096]{1,0:T(8,128)(2,1)S(1)} %get-tuple-element.65), channel_id=1, source_target_pairs={{0,4},{4,0},{8,12},{12,8},{1,5},{5,1},{9,13},{13,9},{2,6},{6,2},{1... | collective-permute-start | bytes 786440 | tf_op jit(solution)/shard_map/ppermute | solution.py:95
  66.9 4.8 %collective-permute-start.23 = (bf16[32,4096]{1,0:T(8,128)(2,1)S(1)}, bf16[32,4096]{1,0:T(8,128)(2,1)S(1)}, u32[]{:S(2)}, u32[]{:S(2)}) collective-permute-start(bf16[32,4096]{1,0:T(8,128)(2,1)S(1)} %fusion.1), channel_id=1, source_target_pairs={{0,4},{4,0},{8,12},{12,8},{1,5},{5,1},{9,13},{13,9},{2,6},{6,2},{1... | collective-permute-start | bytes 786440 | tf_op jit(solution)/shard_map/ppermute | solution.py:101
  72.5 4.8 %collective-permute-start.19 = (bf16[32,4096]{1,0:T(8,128)(2,1)S(1)}, bf16[32,4096]{1,0:T(8,128)(2,1)S(1)}, u32[]{:S(2)}, u32[]{:S(2)}) collective-permute-start(bf16[32,4096]{1,0:T(8,128)(2,1)S(1)} %fusion), channel_id=1, source_target_pairs={{0,4},{4,0},{8,12},{12,8},{1,5},{5,1},{9,13},{13,9},{2,6},{6,2},{1... | collective-permute-start | bytes 786440 | tf_op jit(solution)/shard_map/ppermute | solution.py:101
  78.0 4.5 %collective-permute-done.23 = bf16[32,4096]{1,0:T(8,128)(2,1)S(1)} collective-permute-done((bf16[32,4096]{1,0:T(8,128)(2,1)S(1)}, bf16[32,4096]{1,0:T(8,128)(2,1)S(1)}, u32[]{:S(2)}, u32[]{:S(2)}) %collective-permute-start.23) | collective-permute-done | bytes 262176 | tf_op jit(solution)/shard_map/ppermute | solution.py:101
  83.4 4.1 %collective-permute-done.19 = bf16[32,4096]{1,0:T(8,128)(2,1)S(1)} collective-permute-done((bf16[32,4096]{1,0:T(8,128)(2,1)S(1)}, bf16[32,4096]{1,0:T(8,128)(2,1)S(1)}, u32[]{:S(2)}, u32[]{:S(2)}) %collective-permute-start.19) | collective-permute-done | bytes 262176 | tf_op jit(solution)/shard_map/ppermute | solution.py:101
  (56 shorter events, 15.5 us)
Async XLA Ops:
  0.6 19.1 %collective-permute-start.4 = (bf16[96,8192]{1,0:T(8,128)(2,1)}, bf16[96,8192]{1,0:T(8,128)(2,1)S(1)}, u32[]{:S(2)}, u32[]{:S(2)}) collective-permute-start(bf16[96,8192]{1,0:T(8,128)(2,1)} %refs_0_.1), channel_id=1, source_target_pairs={{0,1},{1,0},{2,3},{3,2},{4,5},{5,4},{6,7},{7,6},{8,9},{9,8},{10,11... | collective-permute-start | bytes 4718600 | tf_op jit(solution)/shard_map/ppermute | solution.py:20
  1.1 37.8 %collective-permute-start = (bf16[96,8192]{1,0:T(8,128)(2,1)}, bf16[96,8192]{1,0:T(8,128)(2,1)S(1)}, u32[]{:S(2)}, u32[]{:S(2)}) collective-permute-start(bf16[96,8192]{1,0:T(8,128)(2,1)} %refs_0_.1), channel_id=1, source_target_pairs={{0,2},{1,3},{2,0},{3,1},{4,6},{5,7},{6,4},{7,5},{8,10},{9,11},{10,... | collective-permute-start | bytes 4718600 | tf_op jit(solution)/shard_map/ppermute | solution.py:20
  4.7 9.9 %collective-permute-start.1 = (bf16[32,4608]{1,0:T(8,128)(2,1)S(1)}, bf16[32,4608]{1,0:T(8,128)(2,1)S(1)}, u32[]{:S(2)}, u32[]{:S(2)}) collective-permute-start(bf16[32,4608]{1,0:T(8,128)(2,1)S(1)} %slice.8.refs_2_), channel_id=1, source_target_pairs={{0,4},{4,0},{8,12},{12,8},{1,5},{5,1},{9,13},{13,9},{2,6},{6,2},{1... | collective-permute-start | bytes 884744 | tf_op jit(solution)/shard_map/ppermute | solution.py:43
  6.3 8.9 %collective-permute-start.2 = (bf16[32,4608]{1,0:T(8,128)(2,1)S(1)}, bf16[32,4608]{1,0:T(8,128)(2,1)S(1)}, u32[]{:S(2)}, u32[]{:S(2)}) collective-permute-start(bf16[32,4608]{1,0:T(8,128)(2,1)S(1)} %slice.8.refs_2_), channel_id=1, source_target_pairs={{4,8},{8,4},{5,9},{9,5},{6,10},{10,6},{7,11},{11,7},{20,24},{24,20... | collective-permute-start | bytes 884744 | tf_op jit(solution)/shard_map/ppermute | solution.py:43
  8.0 12.5 %collective-permute-start.7 = (bf16[32,3584]{1,0:T(8,128)(2,1)S(1)}, bf16[32,3584]{1,0:T(8,128)(2,1)S(1)}, u32[]{:S(2)}, u32[]{:S(2)}) collective-permute-start(bf16[32,3584]{1,0:T(8,128)(2,1)S(1)} %slice.9.refs_3_), channel_id=1, source_target_pairs={{0,4},{4,0},{8,12},{12,8},{1,5},{5,1},{9,13},{13,9},{2,6},{6,2},{1... | collective-permute-start | bytes 688136 | tf_op jit(solution)/shard_map/ppermute | solution.py:43
  14.6 5.8 %collective-permute-start.8 = (bf16[32,3584]{1,0:T(8,128)(2,1)S(1)}, bf16[32,3584]{1,0:T(8,128)(2,1)S(1)}, u32[]{:S(2)}, u32[]{:S(2)}) collective-permute-start(bf16[32,3584]{1,0:T(8,128)(2,1)S(1)} %slice.9.refs_3_), channel_id=1, source_target_pairs={{4,8},{8,4},{5,9},{9,5},{6,10},{10,6},{7,11},{11,7},{20,24},{24,20... | collective-permute-start | bytes 688136 | tf_op jit(solution)/shard_map/ppermute | solution.py:43
  15.3 12.4 %collective-permute-start.3 = (bf16[32,4608]{1,0:T(8,128)(2,1)S(1)}, bf16[32,4608]{1,0:T(8,128)(2,1)S(1)}, u32[]{:S(2)}, u32[]{:S(2)}) collective-permute-start(bf16[32,4608]{1,0:T(8,128)(2,1)S(1)} %collective-permute-done.2.refs_5_), channel_id=1, source_target_pairs={{0,4},{4,0},{8,12},{12,8},{1,5},{5,1},{9,13},{13,9},{2,6},{6,2},{1... | collective-permute-start | bytes 884744 | tf_op jit(solution)/shard_map/ppermute | solution.py:52
  19.8 7.9 %collective-permute-start.5 = (bf16[32,4608]{1,0:T(8,128)(2,1)S(1)}, bf16[32,4608]{1,0:T(8,128)(2,1)S(1)}, u32[]{:S(2)}, u32[]{:S(2)}) collective-permute-start(bf16[32,4608]{1,0:T(8,128)(2,1)S(1)} %collective-permute-done.1.refs_4_), channel_id=1, source_target_pairs={{4,8},{8,4},{5,9},{9,5},{6,10},{10,6},{7,11},{11,7},{20,24},{24,20... | collective-permute-start | bytes 884744 | tf_op jit(solution)/shard_map/ppermute | solution.py:54
  20.4 11.6 %collective-permute-start.9 = (bf16[32,3584]{1,0:T(8,128)(2,1)S(1)}, bf16[32,3584]{1,0:T(8,128)(2,1)S(1)}, u32[]{:S(2)}, u32[]{:S(2)}) collective-permute-start(bf16[32,3584]{1,0:T(8,128)(2,1)S(1)} %collective-permute-done.8.refs_7_), channel_id=1, source_target_pairs={{0,4},{4,0},{8,12},{12,8},{1,5},{5,1},{9,13},{13,9},{2,6},{6,2},{1... | collective-permute-start | bytes 688136 | tf_op jit(solution)/shard_map/ppermute | solution.py:52
  25.8 6.3 %collective-permute-start.10 = (bf16[32,3584]{1,0:T(8,128)(2,1)S(1)}, bf16[32,3584]{1,0:T(8,128)(2,1)S(1)}, u32[]{:S(2)}, u32[]{:S(2)}) collective-permute-start(bf16[32,3584]{1,0:T(8,128)(2,1)S(1)} %collective-permute-done.7.refs_5_), channel_id=1, source_target_pairs={{4,8},{8,4},{5,9},{9,5},{6,10},{10,6},{7,11},{11,7},{20,24},{24,20... | collective-permute-start | bytes 688136 | tf_op jit(solution)/shard_map/ppermute | solution.py:54
  27.7 14.0 %collective-permute-start.6 = (bf16[32,4608]{1,0:T(8,128)(2,1)S(1)}, bf16[32,4608]{1,0:T(8,128)(2,1)S(1)}, u32[]{:S(2)}, u32[]{:S(2)}) collective-permute-start(bf16[32,4608]{1,0:T(8,128)(2,1)S(1)} %collective-permute-done.5.refs_1_), channel_id=1, source_target_pairs={{0,4},{4,0},{8,12},{12,8},{1,5},{5,1},{9,13},{13,9},{2,6},{6,2},{1... | collective-permute-start | bytes 884744 | tf_op jit(solution)/shard_map/ppermute | solution.py:56
  32.1 9.6 %collective-permute-start.11 = (bf16[32,3584]{1,0:T(8,128)(2,1)S(1)}, bf16[32,3584]{1,0:T(8,128)(2,1)S(1)}, u32[]{:S(2)}, u32[]{:S(2)}) collective-permute-start(bf16[32,3584]{1,0:T(8,128)(2,1)S(1)} %collective-permute-done.10.refs_3_), channel_id=1, source_target_pairs={{0,4},{4,0},{8,12},{12,8},{1,5},{5,1},{9,13},{13,9},{2,6},{6,2},{1... | collective-permute-start | bytes 688136 | tf_op jit(solution)/shard_map/ppermute | solution.py:56
  41.7 3.4 %collective-permute-start.12 = (bf16[96,8192]{1,0:T(8,128)(2,1)S(1)}, bf16[96,8192]{1,0:T(8,128)(2,1)S(1)}, u32[]{:S(2)}, u32[]{:S(2)}) collective-permute-start(bf16[96,8192]{1,0:T(8,128)(2,1)S(1)} %collective-permute-done.refs_9_), channel_id=1, source_target_pairs={{0,1},{1,0},{2,3},{3,2},{4,5},{5,4},{6,7},{7,6},{8,9},{9,8},{10,11... | collective-permute-start | bytes 4718600 | tf_op jit(solution)/shard_map/ppermute | solution.py:20
  46.2 3.7 %collective-permute-start.14 = (f32[3,384]{1,0:T(4,128)S(1)}, f32[3,384]{1,0:T(4,128)S(1)}, u32[]{:S(2)}, u32[]{:S(2)}) collective-permute-start(f32[3,384]{1,0:T(4,128)S(1)} %get-tuple-element.58.refs_0_), channel_id=1, source_target_pairs={{0,2},{1,3},{2,0},{3,1},{4,6},{5,7},{6,4},{7,5},{8,10},{9,11},{10,... | collective-permute-start | bytes 13832 | tf_op jit(solution)/shard_map/ppermute | solution.py:20
  50.8 9.2 %collective-permute-start.16 = (bf16[32,4096]{1,0:T(8,128)(2,1)S(1)}, bf16[32,4096]{1,0:T(8,128)(2,1)S(1)}, u32[]{:S(2)}, u32[]{:S(2)}) collective-permute-start(bf16[32,4096]{1,0:T(8,128)(2,1)S(1)} %get-tuple-element.64), channel_id=1, source_target_pairs={{0,4},{4,0},{8,12},{12,8},{1,5},{5,1},{9,13},{13,9},{2,6},{6,2},{1... | collective-permute-start | bytes 786440 | tf_op jit(solution)/shard_map/ppermute | solution.py:91
  56.3 9.7 %collective-permute-start.17 = (bf16[32,4096]{1,0:T(8,128)(2,1)S(1)}, bf16[32,4096]{1,0:T(8,128)(2,1)S(1)}, u32[]{:S(2)}, u32[]{:S(2)}) collective-permute-start(bf16[32,4096]{1,0:T(8,128)(2,1)S(1)} %get-tuple-element.66), channel_id=1, source_target_pairs={{0,4},{4,0},{8,12},{12,8},{1,5},{5,1},{9,13},{13,9},{2,6},{6,2},{1... | collective-permute-start | bytes 786440 | tf_op jit(solution)/shard_map/ppermute | solution.py:91
  59.9 11.7 %collective-permute-start.24 = (bf16[32,4096]{1,0:T(8,128)(2,1)S(1)}, bf16[32,4096]{1,0:T(8,128)(2,1)S(1)}, u32[]{:S(2)}, u32[]{:S(2)}) collective-permute-start(bf16[32,4096]{1,0:T(8,128)(2,1)S(1)} %get-tuple-element.69), channel_id=1, source_target_pairs={{0,4},{4,0},{8,12},{12,8},{1,5},{5,1},{9,13},{13,9},{2,6},{6,2},{1... | collective-permute-start | bytes 786440 | tf_op jit(solution)/shard_map/ppermute | solution.py:95
  62.0 4.7 %collective-permute-start.22 = (bf16[32,4096]{1,0:T(8,128)(2,1)S(1)}, bf16[32,4096]{1,0:T(8,128)(2,1)S(1)}, u32[]{:S(2)}, u32[]{:S(2)}) collective-permute-start(bf16[32,4096]{1,0:T(8,128)(2,1)S(1)} %add_convert_fusion.2), channel_id=1, source_target_pairs={{4,8},{8,4},{5,9},{9,5},{6,10},{10,6},{7,11},{11,7},{20,24},{24,20... | collective-permute-start | bytes 786440 | tf_op jit(solution)/shard_map/ppermute | solution.py:98
  62.7 14.5 %collective-permute-start.20 = (bf16[32,4096]{1,0:T(8,128)(2,1)S(1)}, bf16[32,4096]{1,0:T(8,128)(2,1)S(1)}, u32[]{:S(2)}, u32[]{:S(2)}) collective-permute-start(bf16[32,4096]{1,0:T(8,128)(2,1)S(1)} %get-tuple-element.65), channel_id=1, source_target_pairs={{0,4},{4,0},{8,12},{12,8},{1,5},{5,1},{9,13},{13,9},{2,6},{6,2},{1... | collective-permute-start | bytes 786440 | tf_op jit(solution)/shard_map/ppermute | solution.py:95
  66.1 6.3 %collective-permute-start.18 = (bf16[32,4096]{1,0:T(8,128)(2,1)S(1)}, bf16[32,4096]{1,0:T(8,128)(2,1)S(1)}, u32[]{:S(2)}, u32[]{:S(2)}) collective-permute-start(bf16[32,4096]{1,0:T(8,128)(2,1)S(1)} %add_convert_fusion.5), channel_id=1, source_target_pairs={{4,8},{8,4},{5,9},{9,5},{6,10},{10,6},{7,11},{11,7},{20,24},{24,20... | collective-permute-start | bytes 786440 | tf_op jit(solution)/shard_map/ppermute | solution.py:98
  66.9 15.6 %collective-permute-start.23 = (bf16[32,4096]{1,0:T(8,128)(2,1)S(1)}, bf16[32,4096]{1,0:T(8,128)(2,1)S(1)}, u32[]{:S(2)}, u32[]{:S(2)}) collective-permute-start(bf16[32,4096]{1,0:T(8,128)(2,1)S(1)} %fusion.1), channel_id=1, source_target_pairs={{0,4},{4,0},{8,12},{12,8},{1,5},{5,1},{9,13},{13,9},{2,6},{6,2},{1... | collective-permute-start | bytes 786440 | tf_op jit(solution)/shard_map/ppermute | solution.py:101
  71.7 10.8 %collective-permute-start.25 = (bf16[32,4096]{1,0:T(8,128)(2,1)S(1)}, bf16[32,4096]{1,0:T(8,128)(2,1)S(1)}, u32[]{:S(2)}, u32[]{:S(2)}) collective-permute-start(bf16[32,4096]{1,0:T(8,128)(2,1)S(1)} %add_convert_fusion), channel_id=1, source_target_pairs={{4,8},{8,4},{5,9},{9,5},{6,10},{10,6},{7,11},{11,7},{20,24},{24,20... | collective-permute-start | bytes 786440 | tf_op jit(solution)/shard_map/ppermute | solution.py:99
  72.5 15.0 %collective-permute-start.19 = (bf16[32,4096]{1,0:T(8,128)(2,1)S(1)}, bf16[32,4096]{1,0:T(8,128)(2,1)S(1)}, u32[]{:S(2)}, u32[]{:S(2)}) collective-permute-start(bf16[32,4096]{1,0:T(8,128)(2,1)S(1)} %fusion), channel_id=1, source_target_pairs={{0,4},{4,0},{8,12},{12,8},{1,5},{5,1},{9,13},{13,9},{2,6},{6,2},{1... | collective-permute-start | bytes 786440 | tf_op jit(solution)/shard_map/ppermute | solution.py:101
  77.3 10.2 %collective-permute-start.21 = (bf16[32,4096]{1,0:T(8,128)(2,1)S(1)}, bf16[32,4096]{1,0:T(8,128)(2,1)S(1)}, u32[]{:S(2)}, u32[]{:S(2)}) collective-permute-start(bf16[32,4096]{1,0:T(8,128)(2,1)S(1)} %add_convert_fusion.3), channel_id=1, source_target_pairs={{4,8},{8,4},{5,9},{9,5},{6,10},{10,6},{7,11},{11,7},{20,24},{24,20... | collective-permute-start | bytes 786440 | tf_op jit(solution)/shard_map/ppermute | solution.py:99
  (7 other events, 18.2 us)

commit v26 on v25

--- a/solution.py
+++ b/solution.py
@@ -34,7 +34,7 @@
 
 
 def staged_gather(block, images, noise, near_bits, far_bit):
-    cut = block.shape[1] // 16 * 9
+    cut = block.shape[1] // 32 * 17
     cuts = [block[:, :cut], block[:, cut:]]
     crossed = swap_bits(images, "reader", far_bit)
     near = swap_gather(images, "reader", near_bits)

time: 88.9 us -> 89 us (level)
  starting transfers between devices: 51 us -> 52.6 us
  waiting for transfers between devices: 20.5 us -> 18.9 us
    ppermute x2, waiting for transfers between devices: 1.23 us -> 0.01 us  [staged_gather(): far = lax.ppermute(across, 'blk', SIDES)]
    ppermute x2, starting transfers between devices: 7.71 us -> 8.63 us  [staged_gather(): end = lax.ppermute(across_far, 'blk', SIDES)]
  transfers between devices with their start and end apart: 26 -> 26, of which waited for: 9 -> 8; matrix products, arithmetic and copies ran while one was open for 3% -> 3% of each run, Pallas kernels for 6% -> 6%
where the time goes in v26:
time: 89 us; the launch traced here: 88.5 us
  starting transfers between devices  52.6 us (59%)
  waiting for transfers between devices  18.9 us (21%)
  Pallas kernels  7.97 us (9%)
  local copies, waits for them, and re-layouts  7.48 us (8%)
    ppermute x2, starting transfers between devices, staged_gather(): far = lax.ppermute(across, 'blk', SIDES)  10.6 us
    ppermute x2, starting transfers between devices, pair_scatter(): from_side = lax.ppermute(near, axis, SIDES)  9.43 us
    ppermute x2, waiting for transfers between devices, pair_scatter(): from_side = lax.ppermute(near, axis, SIDES)  8.73 us
    ppermute x2, starting transfers between devices, staged_gather(): end = lax.ppermute(across_far, 'blk', SIDES)  8.63 us
    ppermute x2, starting transfers between devices, staged_gather(): lax.ppermute(one, 'blk', SIDES)  6.09 us
    ppermute x2, starting transfers between devices, pair_scatter(): for_far_middle = [lax.ppermute(part, axis, SIDES) for part in second]  5.27 us
    ppermute x6, starting transfers between devices, swap_bits(): lax.ppermute(block, axis, [(i, i ^ bits) for i in range(lax.axis_size(axi...  5.01 us
    unnamed x10, local copies, waits for them, and re-layouts  4.96 us
  transfers between devices with their start and end apart: 26, of which 8 were waited for; matrix products, arithmetic and copies ran while one was open for 3% of the time, Pallas kernels for 6%

profile of v26, /device:TPU:0, one launch (start us, length us, event | category | flops | bytes accessed | tf_op | source)
XLA Modules:
  0.0 88.5 jit_solution(14282950932117390656)
XLA Ops:
  1.1 2.6 %collective-permute-start = (bf16[96,8192]{1,0:T(8,128)(2,1)}, bf16[96,8192]{1,0:T(8,128)(2,1)S(1)}, u32[]{:S(2)}, u32[]{:S(2)}) collective-permute-start(bf16[96,8192]{1,0:T(8,128)(2,1)} %refs_0_.1), channel_id=1, source_target_pairs={{0,2},{1,3},{2,0},{3,1},{4,6},{5,7},{6,4},{7,5},{8,10},{9,11},{10,... | collective-permute-start | bytes 4718600 | tf_op jit(solution)/shard_map/ppermute | solution.py:20
  3.7 1.0 %slice.8.refs_2_ = bf16[32,4352]{1,0:T(8,128)(2,1)S(1)} slice(bf16[32,8192]{1,0:T(8,128)(2,1)} %bitcast.9), slice={[0:32], [0:4352]} | slice | bytes 557056 | tf_op jit(solution)/shard_map/slice | solution.py:38
  4.7 1.6 %collective-permute-start.1 = (bf16[32,4352]{1,0:T(8,128)(2,1)S(1)}, bf16[32,4352]{1,0:T(8,128)(2,1)S(1)}, u32[]{:S(2)}, u32[]{:S(2)}) collective-permute-start(bf16[32,4352]{1,0:T(8,128)(2,1)S(1)} %slice.8.refs_2_), channel_id=1, source_target_pairs={{0,4},{4,0},{8,12},{12,8},{1,5},{5,1},{9,13},{13,9},{2,6},{6,2},{1... | collective-permute-start | bytes 835592 | tf_op jit(solution)/shard_map/ppermute | solution.py:43
  8.0 4.4 %collective-permute-start.7 = (bf16[32,3840]{1,0:T(8,128)(2,1)S(1)}, bf16[32,3840]{1,0:T(8,128)(2,1)S(1)}, u32[]{:S(2)}, u32[]{:S(2)}) collective-permute-start(bf16[32,3840]{1,0:T(8,128)(2,1)S(1)} %slice.9.refs_3_), channel_id=1, source_target_pairs={{0,4},{4,0},{8,12},{12,8},{1,5},{5,1},{9,13},{13,9},{2,6},{6,2},{1... | collective-permute-start | bytes 737288 | tf_op jit(solution)/shard_map/ppermute | solution.py:43
  12.4 1.6 %collective-permute-done.1.refs_4_ = bf16[32,4352]{1,0:T(8,128)(2,1)S(1)} collective-permute-done((bf16[32,4352]{1,0:T(8,128)(2,1)S(1)}, bf16[32,4352]{1,0:T(8,128)(2,1)S(1)}, u32[]{:S(2)}, u32[]{:S(2)}) %collective-permute-start.1) | collective-permute-done | bytes 278560 | tf_op jit(solution)/shard_map/ppermute | solution.py:43
  14.7 4.7 %collective-permute-start.3 = (bf16[32,4352]{1,0:T(8,128)(2,1)S(1)}, bf16[32,4352]{1,0:T(8,128)(2,1)S(1)}, u32[]{:S(2)}, u32[]{:S(2)}) collective-permute-start(bf16[32,4352]{1,0:T(8,128)(2,1)S(1)} %collective-permute-done.2.refs_5_), channel_id=1, source_target_pairs={{0,4},{4,0},{8,12},{12,8},{1,5},{5,1},{9,13},{13,9},{2,6},{6,2},{1... | collective-permute-start | bytes 835592 | tf_op jit(solution)/shard_map/ppermute | solution.py:52
  20.1 6.0 %collective-permute-start.9 = (bf16[32,3840]{1,0:T(8,128)(2,1)S(1)}, bf16[32,3840]{1,0:T(8,128)(2,1)S(1)}, u32[]{:S(2)}, u32[]{:S(2)}) collective-permute-start(bf16[32,3840]{1,0:T(8,128)(2,1)S(1)} %collective-permute-done.8.refs_7_), channel_id=1, source_target_pairs={{0,4},{4,0},{8,12},{12,8},{1,5},{5,1},{9,13},{13,9},{2,6},{6,2},{1... | collective-permute-start | bytes 737288 | tf_op jit(solution)/shard_map/ppermute | solution.py:52
  26.7 5.3 %collective-permute-start.6 = (bf16[32,4352]{1,0:T(8,128)(2,1)S(1)}, bf16[32,4352]{1,0:T(8,128)(2,1)S(1)}, u32[]{:S(2)}, u32[]{:S(2)}) collective-permute-start(bf16[32,4352]{1,0:T(8,128)(2,1)S(1)} %collective-permute-done.5.refs_1_), channel_id=1, source_target_pairs={{0,4},{4,0},{8,12},{12,8},{1,5},{5,1},{9,13},{13,9},{2,6},{6,2},{1... | collective-permute-start | bytes 835592 | tf_op jit(solution)/shard_map/ppermute | solution.py:56
  32.0 3.4 %collective-permute-start.11 = (bf16[32,3840]{1,0:T(8,128)(2,1)S(1)}, bf16[32,3840]{1,0:T(8,128)(2,1)S(1)}, u32[]{:S(2)}, u32[]{:S(2)}) collective-permute-start(bf16[32,3840]{1,0:T(8,128)(2,1)S(1)} %collective-permute-done.10.refs_3_), channel_id=1, source_target_pairs={{0,4},{4,0},{8,12},{12,8},{1,5},{5,1},{9,13},{13,9},{2,6},{6,2},{1... | collective-permute-start | bytes 737288 | tf_op jit(solution)/shard_map/ppermute | solution.py:56
  35.4 1.4 %copy-done.2 = bf16[96,8192]{1,0:T(8,128)(2,1)S(1)} copy-done((bf16[96,8192]{1,0:T(8,128)(2,1)S(1)}, bf16[96,8192]{1,0:T(8,128)(2,1)}, u32[]{:S(2)}) %copy-start.2) | copy-done | bytes 1572888
  37.5 1.1 %stage.1 = (bf16[64,8192]{1,0:T(8,128)(2,1)S(1)}, f32[64,1]{1,0:T(8,128)S(1)}, bf16[192,8192]{1,0:T(8,128)(2,1)S(1)}, f32[1,8192]{1,0:T(1,128)S(1)}) custom-call(bf16[96,8192]{1,0:T(8,128)(2,1)S(1)} %copy-done.2, bf16[96,8192]{1,0:T(8,128)(2,1)S(1)} %collective-permute-done.4.refs_1_, bf16[32,4352]{1,0:T(8,128)(2,1)S(1)} %slice.8.refs_2_, ...), custom_call_target="tpu_custom_call" | custom-call | flops 4194304 | bytes 12000000 | tf_op jit(solution)/shard_map/stage/pallas_call | solution.py:245
  38.9 2.9 %collective-permute-done.11.refs_6_ = bf16[32,3840]{1,0:T(8,128)(2,1)S(1)} collective-permute-done((bf16[32,3840]{1,0:T(8,128)(2,1)S(1)}, bf16[32,3840]{1,0:T(8,128)(2,1)S(1)}, u32[]{:S(2)}, u32[]{:S(2)}) %collective-permute-start.11) | collective-permute-done | bytes 245792 | tf_op jit(solution)/shard_map/ppermute | solution.py:56
  41.8 2.9 %stage_rest.1 = (bf16[8192,128]{1,0:T(8,128)(2,1)S(1)}, f32[128,1]{1,0:T(8,128)S(1)}, bf16[384,8192]{1,0:T(8,128)(2,1)S(1)}, f32[384,128]{1,0:T(8,128)S(1)}) custom-call(bf16[32,4352]{1,0:T(8,128)(2,1)S(1)} %collective-permute-done.3.refs_0_, bf16[32,4352]{1,0:T(8,128)(2,1)S(1)} %collective-permute-done.5.refs_1_, ...), custom_call_target="tpu_custom_call" | custom-call | flops 8388608 | bytes 12000000 | tf_op jit(solution)/shard_map/stage_rest/pallas_call | solution.py:313
  46.9 1.2 %collective-permute-start.15 = (f32[3,384]{1,0:T(4,128)S(1)}, f32[3,384]{1,0:T(4,128)S(1)}, u32[]{:S(2)}, u32[]{:S(2)}) collective-permute-start(f32[3,384]{1,0:T(4,128)S(1)} %get-tuple-element.58.refs_0_), channel_id=1, source_target_pairs={{0,3},{1,2},{2,1},{3,0},{4,7},{5,6},{6,5},{7,4},{8,11},{9,10},{10,... | collective-permute-start | bytes 13832 | tf_op jit(solution)/shard_map/ppermute | solution.py:20
  48.0 1.9 %collective-permute-done.14.refs_2_ = f32[3,384]{1,0:T(4,128)S(1)} collective-permute-done((f32[3,384]{1,0:T(4,128)S(1)}, f32[3,384]{1,0:T(4,128)S(1)}, u32[]{:S(2)}, u32[]{:S(2)}) %collective-permute-start.14) | collective-permute-done | bytes 4640 | tf_op jit(solution)/shard_map/ppermute | solution.py:20
  50.8 2.1 %collective-permute-start.16 = (bf16[32,4096]{1,0:T(8,128)(2,1)S(1)}, bf16[32,4096]{1,0:T(8,128)(2,1)S(1)}, u32[]{:S(2)}, u32[]{:S(2)}) collective-permute-start(bf16[32,4096]{1,0:T(8,128)(2,1)S(1)} %get-tuple-element.64), channel_id=1, source_target_pairs={{0,4},{4,0},{8,12},{12,8},{1,5},{5,1},{9,13},{13,9},{2,6},{6,2},{1... | collective-permute-start | bytes 786440 | tf_op jit(solution)/shard_map/ppermute | solution.py:91
  52.9 2.8 %copy-done.1 = bf16[384,8192]{1,0:T(8,128)(2,1)S(1)} copy-done((bf16[384,8192]{1,0:T(8,128)(2,1)S(1)}, bf16[384,8192]{1,0:T(8,128)(2,1)}, u32[]{:S(2)}) %copy-start.1) | copy-done | bytes 6291480
  57.1 2.9 %collective-permute-done.16 = bf16[32,4096]{1,0:T(8,128)(2,1)S(1)} collective-permute-done((bf16[32,4096]{1,0:T(8,128)(2,1)S(1)}, bf16[32,4096]{1,0:T(8,128)(2,1)S(1)}, u32[]{:S(2)}, u32[]{:S(2)}) %collective-permute-start.16) | collective-permute-done | bytes 262176 | tf_op jit(solution)/shard_map/ppermute | solution.py:91
  60.0 2.1 %collective-permute-start.24 = (bf16[32,4096]{1,0:T(8,128)(2,1)S(1)}, bf16[32,4096]{1,0:T(8,128)(2,1)S(1)}, u32[]{:S(2)}, u32[]{:S(2)}) collective-permute-start(bf16[32,4096]{1,0:T(8,128)(2,1)S(1)} %get-tuple-element.69), channel_id=1, source_target_pairs={{0,4},{4,0},{8,12},{12,8},{1,5},{5,1},{9,13},{13,9},{2,6},{6,2},{1... | collective-permute-start | bytes 786440 | tf_op jit(solution)/shard_map/ppermute | solution.py:95
  62.8 3.2 %collective-permute-start.20 = (bf16[32,4096]{1,0:T(8,128)(2,1)S(1)}, bf16[32,4096]{1,0:T(8,128)(2,1)S(1)}, u32[]{:S(2)}, u32[]{:S(2)}) collective-permute-start(bf16[32,4096]{1,0:T(8,128)(2,1)S(1)} %get-tuple-element.65), channel_id=1, source_target_pairs={{0,4},{4,0},{8,12},{12,8},{1,5},{5,1},{9,13},{13,9},{2,6},{6,2},{1... | collective-permute-start | bytes 786440 | tf_op jit(solution)/shard_map/ppermute | solution.py:95
  66.9 4.7 %collective-permute-start.23 = (bf16[32,4096]{1,0:T(8,128)(2,1)S(1)}, bf16[32,4096]{1,0:T(8,128)(2,1)S(1)}, u32[]{:S(2)}, u32[]{:S(2)}) collective-permute-start(bf16[32,4096]{1,0:T(8,128)(2,1)S(1)} %fusion.1), channel_id=1, source_target_pairs={{0,4},{4,0},{8,12},{12,8},{1,5},{5,1},{9,13},{13,9},{2,6},{6,2},{1... | collective-permute-start | bytes 786440 | tf_op jit(solution)/shard_map/ppermute | solution.py:101
  72.4 4.8 %collective-permute-start.19 = (bf16[32,4096]{1,0:T(8,128)(2,1)S(1)}, bf16[32,4096]{1,0:T(8,128)(2,1)S(1)}, u32[]{:S(2)}, u32[]{:S(2)}) collective-permute-start(bf16[32,4096]{1,0:T(8,128)(2,1)S(1)} %fusion), channel_id=1, source_target_pairs={{0,4},{4,0},{8,12},{12,8},{1,5},{5,1},{9,13},{13,9},{2,6},{6,2},{1... | collective-permute-start | bytes 786440 | tf_op jit(solution)/shard_map/ppermute | solution.py:101
  77.9 4.6 %collective-permute-done.23 = bf16[32,4096]{1,0:T(8,128)(2,1)S(1)} collective-permute-done((bf16[32,4096]{1,0:T(8,128)(2,1)S(1)}, bf16[32,4096]{1,0:T(8,128)(2,1)S(1)}, u32[]{:S(2)}, u32[]{:S(2)}) %collective-permute-start.23) | collective-permute-done | bytes 262176 | tf_op jit(solution)/shard_map/ppermute | solution.py:101
  83.5 4.1 %collective-permute-done.19 = bf16[32,4096]{1,0:T(8,128)(2,1)S(1)} collective-permute-done((bf16[32,4096]{1,0:T(8,128)(2,1)S(1)}, bf16[32,4096]{1,0:T(8,128)(2,1)S(1)}, u32[]{:S(2)}, u32[]{:S(2)}) %collective-permute-start.19) | collective-permute-done | bytes 262176 | tf_op jit(solution)/shard_map/ppermute | solution.py:101
  (56 shorter events, 14.6 us)
Async XLA Ops:
  0.6 18.8 %collective-permute-start.4 = (bf16[96,8192]{1,0:T(8,128)(2,1)}, bf16[96,8192]{1,0:T(8,128)(2,1)S(1)}, u32[]{:S(2)}, u32[]{:S(2)}) collective-permute-start(bf16[96,8192]{1,0:T(8,128)(2,1)} %refs_0_.1), channel_id=1, source_target_pairs={{0,1},{1,0},{2,3},{3,2},{4,5},{5,4},{6,7},{7,6},{8,9},{9,8},{10,11... | collective-permute-start | bytes 4718600 | tf_op jit(solution)/shard_map/ppermute | solution.py:20
  1.1 37.8 %collective-permute-start = (bf16[96,8192]{1,0:T(8,128)(2,1)}, bf16[96,8192]{1,0:T(8,128)(2,1)S(1)}, u32[]{:S(2)}, u32[]{:S(2)}) collective-permute-start(bf16[96,8192]{1,0:T(8,128)(2,1)} %refs_0_.1), channel_id=1, source_target_pairs={{0,2},{1,3},{2,0},{3,1},{4,6},{5,7},{6,4},{7,5},{8,10},{9,11},{10,... | collective-permute-start | bytes 4718600 | tf_op jit(solution)/shard_map/ppermute | solution.py:20
  4.7 9.3 %collective-permute-start.1 = (bf16[32,4352]{1,0:T(8,128)(2,1)S(1)}, bf16[32,4352]{1,0:T(8,128)(2,1)S(1)}, u32[]{:S(2)}, u32[]{:S(2)}) collective-permute-start(bf16[32,4352]{1,0:T(8,128)(2,1)S(1)} %slice.8.refs_2_), channel_id=1, source_target_pairs={{0,4},{4,0},{8,12},{12,8},{1,5},{5,1},{9,13},{13,9},{2,6},{6,2},{1... | collective-permute-start | bytes 835592 | tf_op jit(solution)/shard_map/ppermute | solution.py:43
  6.3 8.4 %collective-permute-start.2 = (bf16[32,4352]{1,0:T(8,128)(2,1)S(1)}, bf16[32,4352]{1,0:T(8,128)(2,1)S(1)}, u32[]{:S(2)}, u32[]{:S(2)}) collective-permute-start(bf16[32,4352]{1,0:T(8,128)(2,1)S(1)} %slice.8.refs_2_), channel_id=1, source_target_pairs={{4,8},{8,4},{5,9},{9,5},{6,10},{10,6},{7,11},{11,7},{20,24},{24,20... | collective-permute-start | bytes 835592 | tf_op jit(solution)/shard_map/ppermute | solution.py:43
  8.0 12.1 %collective-permute-start.7 = (bf16[32,3840]{1,0:T(8,128)(2,1)S(1)}, bf16[32,3840]{1,0:T(8,128)(2,1)S(1)}, u32[]{:S(2)}, u32[]{:S(2)}) collective-permute-start(bf16[32,3840]{1,0:T(8,128)(2,1)S(1)} %slice.9.refs_3_), channel_id=1, source_target_pairs={{0,4},{4,0},{8,12},{12,8},{1,5},{5,1},{9,13},{13,9},{2,6},{6,2},{1... | collective-permute-start | bytes 737288 | tf_op jit(solution)/shard_map/ppermute | solution.py:43
  14.0 6.1 %collective-permute-start.8 = (bf16[32,3840]{1,0:T(8,128)(2,1)S(1)}, bf16[32,3840]{1,0:T(8,128)(2,1)S(1)}, u32[]{:S(2)}, u32[]{:S(2)}) collective-permute-start(bf16[32,3840]{1,0:T(8,128)(2,1)S(1)} %slice.9.refs_3_), channel_id=1, source_target_pairs={{4,8},{8,4},{5,9},{9,5},{6,10},{10,6},{7,11},{11,7},{20,24},{24,20... | collective-permute-start | bytes 737288 | tf_op jit(solution)/shard_map/ppermute | solution.py:43
  14.7 12.0 %collective-permute-start.3 = (bf16[32,4352]{1,0:T(8,128)(2,1)S(1)}, bf16[32,4352]{1,0:T(8,128)(2,1)S(1)}, u32[]{:S(2)}, u32[]{:S(2)}) collective-permute-start(bf16[32,4352]{1,0:T(8,128)(2,1)S(1)} %collective-permute-done.2.refs_5_), channel_id=1, source_target_pairs={{0,4},{4,0},{8,12},{12,8},{1,5},{5,1},{9,13},{13,9},{2,6},{6,2},{1... | collective-permute-start | bytes 835592 | tf_op jit(solution)/shard_map/ppermute | solution.py:52
  19.4 7.3 %collective-permute-start.5 = (bf16[32,4352]{1,0:T(8,128)(2,1)S(1)}, bf16[32,4352]{1,0:T(8,128)(2,1)S(1)}, u32[]{:S(2)}, u32[]{:S(2)}) collective-permute-start(bf16[32,4352]{1,0:T(8,128)(2,1)S(1)} %collective-permute-done.1.refs_4_), channel_id=1, source_target_pairs={{4,8},{8,4},{5,9},{9,5},{6,10},{10,6},{7,11},{11,7},{20,24},{24,20... | collective-permute-start | bytes 835592 | tf_op jit(solution)/shard_map/ppermute | solution.py:54
  20.1 11.9 %collective-permute-start.9 = (bf16[32,3840]{1,0:T(8,128)(2,1)S(1)}, bf16[32,3840]{1,0:T(8,128)(2,1)S(1)}, u32[]{:S(2)}, u32[]{:S(2)}) collective-permute-start(bf16[32,3840]{1,0:T(8,128)(2,1)S(1)} %collective-permute-done.8.refs_7_), channel_id=1, source_target_pairs={{0,4},{4,0},{8,12},{12,8},{1,5},{5,1},{9,13},{13,9},{2,6},{6,2},{1... | collective-permute-start | bytes 737288 | tf_op jit(solution)/shard_map/ppermute | solution.py:52
  26.0 6.0 %collective-permute-start.10 = (bf16[32,3840]{1,0:T(8,128)(2,1)S(1)}, bf16[32,3840]{1,0:T(8,128)(2,1)S(1)}, u32[]{:S(2)}, u32[]{:S(2)}) collective-permute-start(bf16[32,3840]{1,0:T(8,128)(2,1)S(1)} %collective-permute-done.7.refs_5_), channel_id=1, source_target_pairs={{4,8},{8,4},{5,9},{9,5},{6,10},{10,6},{7,11},{11,7},{20,24},{24,20... | collective-permute-start | bytes 737288 | tf_op jit(solution)/shard_map/ppermute | solution.py:54
  26.7 15.1 %collective-permute-start.6 = (bf16[32,4352]{1,0:T(8,128)(2,1)S(1)}, bf16[32,4352]{1,0:T(8,128)(2,1)S(1)}, u32[]{:S(2)}, u32[]{:S(2)}) collective-permute-start(bf16[32,4352]{1,0:T(8,128)(2,1)S(1)} %collective-permute-done.5.refs_1_), channel_id=1, source_target_pairs={{0,4},{4,0},{8,12},{12,8},{1,5},{5,1},{9,13},{13,9},{2,6},{6,2},{1... | collective-permute-start | bytes 835592 | tf_op jit(solution)/shard_map/ppermute | solution.py:56
  32.0 9.8 %collective-permute-start.11 = (bf16[32,3840]{1,0:T(8,128)(2,1)S(1)}, bf16[32,3840]{1,0:T(8,128)(2,1)S(1)}, u32[]{:S(2)}, u32[]{:S(2)}) collective-permute-start(bf16[32,3840]{1,0:T(8,128)(2,1)S(1)} %collective-permute-done.10.refs_3_), channel_id=1, source_target_pairs={{0,4},{4,0},{8,12},{12,8},{1,5},{5,1},{9,13},{13,9},{2,6},{6,2},{1... | collective-permute-start | bytes 737288 | tf_op jit(solution)/shard_map/ppermute | solution.py:56
  41.8 3.4 %collective-permute-start.12 = (bf16[96,8192]{1,0:T(8,128)(2,1)S(1)}, bf16[96,8192]{1,0:T(8,128)(2,1)S(1)}, u32[]{:S(2)}, u32[]{:S(2)}) collective-permute-start(bf16[96,8192]{1,0:T(8,128)(2,1)S(1)} %collective-permute-done.refs_9_), channel_id=1, source_target_pairs={{0,1},{1,0},{2,3},{3,2},{4,5},{5,4},{6,7},{7,6},{8,9},{9,8},{10,11... | collective-permute-start | bytes 4718600 | tf_op jit(solution)/shard_map/ppermute | solution.py:20
  46.3 3.7 %collective-permute-start.14 = (f32[3,384]{1,0:T(4,128)S(1)}, f32[3,384]{1,0:T(4,128)S(1)}, u32[]{:S(2)}, u32[]{:S(2)}) collective-permute-start(f32[3,384]{1,0:T(4,128)S(1)} %get-tuple-element.58.refs_0_), channel_id=1, source_target_pairs={{0,2},{1,3},{2,0},{3,1},{4,6},{5,7},{6,4},{7,5},{8,10},{9,11},{10,... | collective-permute-start | bytes 13832 | tf_op jit(solution)/shard_map/ppermute | solution.py:20
  50.8 9.2 %collective-permute-start.16 = (bf16[32,4096]{1,0:T(8,128)(2,1)S(1)}, bf16[32,4096]{1,0:T(8,128)(2,1)S(1)}, u32[]{:S(2)}, u32[]{:S(2)}) collective-permute-start(bf16[32,4096]{1,0:T(8,128)(2,1)S(1)} %get-tuple-element.64), channel_id=1, source_target_pairs={{0,4},{4,0},{8,12},{12,8},{1,5},{5,1},{9,13},{13,9},{2,6},{6,2},{1... | collective-permute-start | bytes 786440 | tf_op jit(solution)/shard_map/ppermute | solution.py:91
  56.4 9.6 %collective-permute-start.17 = (bf16[32,4096]{1,0:T(8,128)(2,1)S(1)}, bf16[32,4096]{1,0:T(8,128)(2,1)S(1)}, u32[]{:S(2)}, u32[]{:S(2)}) collective-permute-start(bf16[32,4096]{1,0:T(8,128)(2,1)S(1)} %get-tuple-element.66), channel_id=1, source_target_pairs={{0,4},{4,0},{8,12},{12,8},{1,5},{5,1},{9,13},{13,9},{2,6},{6,2},{1... | collective-permute-start | bytes 786440 | tf_op jit(solution)/shard_map/ppermute | solution.py:91
  60.0 11.5 %collective-permute-start.24 = (bf16[32,4096]{1,0:T(8,128)(2,1)S(1)}, bf16[32,4096]{1,0:T(8,128)(2,1)S(1)}, u32[]{:S(2)}, u32[]{:S(2)}) collective-permute-start(bf16[32,4096]{1,0:T(8,128)(2,1)S(1)} %get-tuple-element.69), channel_id=1, source_target_pairs={{0,4},{4,0},{8,12},{12,8},{1,5},{5,1},{9,13},{13,9},{2,6},{6,2},{1... | collective-permute-start | bytes 786440 | tf_op jit(solution)/shard_map/ppermute | solution.py:95
  62.2 4.7 %collective-permute-start.22 = (bf16[32,4096]{1,0:T(8,128)(2,1)S(1)}, bf16[32,4096]{1,0:T(8,128)(2,1)S(1)}, u32[]{:S(2)}, u32[]{:S(2)}) collective-permute-start(bf16[32,4096]{1,0:T(8,128)(2,1)S(1)} %add_convert_fusion.2), channel_id=1, source_target_pairs={{4,8},{8,4},{5,9},{9,5},{6,10},{10,6},{7,11},{11,7},{20,24},{24,20... | collective-permute-start | bytes 786440 | tf_op jit(solution)/shard_map/ppermute | solution.py:98
  62.8 14.4 %collective-permute-start.20 = (bf16[32,4096]{1,0:T(8,128)(2,1)S(1)}, bf16[32,4096]{1,0:T(8,128)(2,1)S(1)}, u32[]{:S(2)}, u32[]{:S(2)}) collective-permute-start(bf16[32,4096]{1,0:T(8,128)(2,1)S(1)} %get-tuple-element.65), channel_id=1, source_target_pairs={{0,4},{4,0},{8,12},{12,8},{1,5},{5,1},{9,13},{13,9},{2,6},{6,2},{1... | collective-permute-start | bytes 786440 | tf_op jit(solution)/shard_map/ppermute | solution.py:95
  66.1 6.2 %collective-permute-start.18 = (bf16[32,4096]{1,0:T(8,128)(2,1)S(1)}, bf16[32,4096]{1,0:T(8,128)(2,1)S(1)}, u32[]{:S(2)}, u32[]{:S(2)}) collective-permute-start(bf16[32,4096]{1,0:T(8,128)(2,1)S(1)} %add_convert_fusion.5), channel_id=1, source_target_pairs={{4,8},{8,4},{5,9},{9,5},{6,10},{10,6},{7,11},{11,7},{20,24},{24,20... | collective-permute-start | bytes 786440 | tf_op jit(solution)/shard_map/ppermute | solution.py:98
  66.9 15.7 %collective-permute-start.23 = (bf16[32,4096]{1,0:T(8,128)(2,1)S(1)}, bf16[32,4096]{1,0:T(8,128)(2,1)S(1)}, u32[]{:S(2)}, u32[]{:S(2)}) collective-permute-start(bf16[32,4096]{1,0:T(8,128)(2,1)S(1)} %fusion.1), channel_id=1, source_target_pairs={{0,4},{4,0},{8,12},{12,8},{1,5},{5,1},{9,13},{13,9},{2,6},{6,2},{1... | collective-permute-start | bytes 786440 | tf_op jit(solution)/shard_map/ppermute | solution.py:101
  71.6 10.9 %collective-permute-start.25 = (bf16[32,4096]{1,0:T(8,128)(2,1)S(1)}, bf16[32,4096]{1,0:T(8,128)(2,1)S(1)}, u32[]{:S(2)}, u32[]{:S(2)}) collective-permute-start(bf16[32,4096]{1,0:T(8,128)(2,1)S(1)} %add_convert_fusion), channel_id=1, source_target_pairs={{4,8},{8,4},{5,9},{9,5},{6,10},{10,6},{7,11},{11,7},{20,24},{24,20... | collective-permute-start | bytes 786440 | tf_op jit(solution)/shard_map/ppermute | solution.py:99
  72.4 15.2 %collective-permute-start.19 = (bf16[32,4096]{1,0:T(8,128)(2,1)S(1)}, bf16[32,4096]{1,0:T(8,128)(2,1)S(1)}, u32[]{:S(2)}, u32[]{:S(2)}) collective-permute-start(bf16[32,4096]{1,0:T(8,128)(2,1)S(1)} %fusion), channel_id=1, source_target_pairs={{0,4},{4,0},{8,12},{12,8},{1,5},{5,1},{9,13},{13,9},{2,6},{6,2},{1... | collective-permute-start | bytes 786440 | tf_op jit(solution)/shard_map/ppermute | solution.py:101
  77.3 10.3 %collective-permute-start.21 = (bf16[32,4096]{1,0:T(8,128)(2,1)S(1)}, bf16[32,4096]{1,0:T(8,128)(2,1)S(1)}, u32[]{:S(2)}, u32[]{:S(2)}) collective-permute-start(bf16[32,4096]{1,0:T(8,128)(2,1)S(1)} %add_convert_fusion.3), channel_id=1, source_target_pairs={{4,8},{8,4},{5,9},{9,5},{6,10},{10,6},{7,11},{11,7},{20,24},{24,20... | collective-permute-start | bytes 786440 | tf_op jit(solution)/shard_map/ppermute | solution.py:99
  (7 other events, 18.1 us)

commit v27 on v25

--- a/solution.py
+++ b/solution.py
@@ -38,12 +38,8 @@
     cuts = [block[:, :cut], block[:, cut:]]
     crossed = swap_bits(images, "reader", far_bit)
     near = swap_gather(images, "reader", near_bits)
-    firsts = [
-        lax.optimization_barrier(
-            (lax.ppermute(one, "blk", SIDES), lax.ppermute(one, "blk", MIDDLE))
-        )
-        for one in cuts
-    ]
+    firsts = [(lax.ppermute(one, "blk", SIDES), lax.ppermute(one, "blk", MIDDLE)) for one in cuts]
+    firsts[0] = lax.optimization_barrier(firsts[0])
     early = stage(
         [[[one] for one in cuts], [[side] for side, _ in firsts]], near, noise
     )

time: 88.9 us -> 90.2 us (1.015)
  waiting for transfers between devices: 20.5 us -> 29.4 us
  starting transfers between devices: 51 us -> 43.4 us
    ppermute x2, waiting for transfers between devices: 1.23 us -> 6.42 us  [staged_gather(): far = lax.ppermute(across, 'blk', SIDES)]
    ppermute x2, starting transfers between devices: 7.71 us -> 3.97 us  [staged_gather(): end = lax.ppermute(across_far, 'blk', SIDES)]
    ppermute x2, waiting for transfers between devices: 2.19 us -> 5.18 us  [staged_gather(): lax.ppermute(one, 'blk', SIDES)]
    ppermute x2, starting transfers between devices: 6.09 us -> 3.22 us  [staged_gather(): lax.ppermute(one, 'blk', SIDES)]
    ppermute x2, starting transfers between devices: 9.77 us -> 8.02 us  [staged_gather(): far = lax.ppermute(across, 'blk', SIDES)]
    ppermute x2, waiting for transfers between devices: 2.79 us -> 4.25 us  [staged_gather(): end = lax.ppermute(across_far, 'blk', SIDES)]
    ppermute x2, waiting for transfers between devices: 8.57 us -> 7.51 us  [pair_scatter(): from_side = lax.ppermute(near, axis, SIDES)]
  transfers between devices with their start and end apart: 26 -> 26, of which waited for: 9 -> 11; matrix products, arithmetic and copies ran while one was open for 3% -> 3% of each run, Pallas kernels for 6% -> 6%
where the time goes in v27:
time: 90.2 us; the launch traced here: 89.7 us
  starting transfers between devices  43.4 us (48%)
  waiting for transfers between devices  29.4 us (33%)
  Pallas kernels  7.96 us (9%)
  local copies, waits for them, and re-layouts  7.48 us (8%)
    ppermute x2, starting transfers between devices, pair_scatter(): from_side = lax.ppermute(near, axis, SIDES)  9.67 us
    ppermute x2, starting transfers between devices, staged_gather(): far = lax.ppermute(across, 'blk', SIDES)  8.02 us
    ppermute x2, waiting for transfers between devices, pair_scatter(): from_side = lax.ppermute(near, axis, SIDES)  7.51 us
    ppermute x2, waiting for transfers between devices, staged_gather(): far = lax.ppermute(across, 'blk', SIDES)  6.42 us
    ppermute x2, starting transfers between devices, pair_scatter(): for_far_middle = [lax.ppermute(part, axis, SIDES) for part in second]  5.94 us
    ppermute x2, waiting for transfers between devices, staged_gather(): lax.ppermute(one, 'blk', SIDES)  5.18 us
    ppermute x6, starting transfers between devices, swap_bits(): lax.ppermute(block, axis, [(i, i ^ bits) for i in range(lax.axis_size(axi...  5.01 us
    unnamed x10, local copies, waits for them, and re-layouts  4.96 us
  transfers between devices with their start and end apart: 26, of which 11 were waited for; matrix products, arithmetic and copies ran while one was open for 3% of the time, Pallas kernels for 6%

profile of v27, /device:TPU:0, one launch (start us, length us, event | category | flops | bytes accessed | tf_op | source)
XLA Modules:
  0.0 89.7 jit_solution(14541416501043856393)
XLA Ops:
  1.1 2.6 %collective-permute-start = (bf16[96,8192]{1,0:T(8,128)(2,1)}, bf16[96,8192]{1,0:T(8,128)(2,1)S(1)}, u32[]{:S(2)}, u32[]{:S(2)}) collective-permute-start(bf16[96,8192]{1,0:T(8,128)(2,1)} %refs_0_.1), channel_id=1, source_target_pairs={{0,2},{1,3},{2,0},{3,1},{4,6},{5,7},{6,4},{7,5},{8,10},{9,11},{10,... | collective-permute-start | bytes 4718600 | tf_op jit(solution)/shard_map/ppermute | solution.py:20
  4.7 1.6 %collective-permute-start.1 = (bf16[32,4608]{1,0:T(8,128)(2,1)S(1)}, bf16[32,4608]{1,0:T(8,128)(2,1)S(1)}, u32[]{:S(2)}, u32[]{:S(2)}) collective-permute-start(bf16[32,4608]{1,0:T(8,128)(2,1)S(1)} %slice.8.refs_2_), channel_id=1, source_target_pairs={{0,4},{4,0},{8,12},{12,8},{1,5},{5,1},{9,13},{13,9},{2,6},{6,2},{1... | collective-permute-start | bytes 884744 | tf_op jit(solution)/shard_map/ppermute | solution.py:41
  8.7 5.2 %collective-permute-done.1.refs_4_ = bf16[32,4608]{1,0:T(8,128)(2,1)S(1)} collective-permute-done((bf16[32,4608]{1,0:T(8,128)(2,1)S(1)}, bf16[32,4608]{1,0:T(8,128)(2,1)S(1)}, u32[]{:S(2)}, u32[]{:S(2)}) %collective-permute-start.1) | collective-permute-done | bytes 294944 | tf_op jit(solution)/shard_map/ppermute | solution.py:41
  13.8 1.6 %collective-permute-start.9 = (bf16[32,3584]{1,0:T(8,128)(2,1)S(1)}, bf16[32,3584]{1,0:T(8,128)(2,1)S(1)}, u32[]{:S(2)}, u32[]{:S(2)}) collective-permute-start(bf16[32,3584]{1,0:T(8,128)(2,1)S(1)} %slice.9.refs_3_), channel_id=1, source_target_pairs={{0,4},{4,0},{8,12},{12,8},{1,5},{5,1},{9,13},{13,9},{2,6},{6,2},{1... | collective-permute-start | bytes 688136 | tf_op jit(solution)/shard_map/ppermute | solution.py:41
  15.4 3.8 %collective-permute-start.3 = (bf16[32,4608]{1,0:T(8,128)(2,1)S(1)}, bf16[32,4608]{1,0:T(8,128)(2,1)S(1)}, u32[]{:S(2)}, u32[]{:S(2)}) collective-permute-start(bf16[32,4608]{1,0:T(8,128)(2,1)S(1)} %collective-permute-done.2.refs_5_), channel_id=1, source_target_pairs={{0,4},{4,0},{8,12},{12,8},{1,5},{5,1},{9,13},{13,9},{2,6},{6,2},{1... | collective-permute-start | bytes 884744 | tf_op jit(solution)/shard_map/ppermute | solution.py:48
  19.9 4.2 %collective-permute-start.8 = (bf16[32,3584]{1,0:T(8,128)(2,1)S(1)}, bf16[32,3584]{1,0:T(8,128)(2,1)S(1)}, u32[]{:S(2)}, u32[]{:S(2)}) collective-permute-start(bf16[32,3584]{1,0:T(8,128)(2,1)S(1)} %collective-permute-done.7.refs_7_), channel_id=1, source_target_pairs={{0,4},{4,0},{8,12},{12,8},{1,5},{5,1},{9,13},{13,9},{2,6},{6,2},{1... | collective-permute-start | bytes 688136 | tf_op jit(solution)/shard_map/ppermute | solution.py:48
  24.8 3.9 %collective-permute-done.3.refs_0_ = bf16[32,4608]{1,0:T(8,128)(2,1)S(1)} collective-permute-done((bf16[32,4608]{1,0:T(8,128)(2,1)S(1)}, bf16[32,4608]{1,0:T(8,128)(2,1)S(1)}, u32[]{:S(2)}, u32[]{:S(2)}) %collective-permute-start.3) | collective-permute-done | bytes 294944 | tf_op jit(solution)/shard_map/ppermute | solution.py:48
  28.7 2.4 %collective-permute-start.6 = (bf16[32,4608]{1,0:T(8,128)(2,1)S(1)}, bf16[32,4608]{1,0:T(8,128)(2,1)S(1)}, u32[]{:S(2)}, u32[]{:S(2)}) collective-permute-start(bf16[32,4608]{1,0:T(8,128)(2,1)S(1)} %collective-permute-done.5.refs_1_), channel_id=1, source_target_pairs={{0,4},{4,0},{8,12},{12,8},{1,5},{5,1},{9,13},{13,9},{2,6},{6,2},{1... | collective-permute-start | bytes 884744 | tf_op jit(solution)/shard_map/ppermute | solution.py:52
  31.1 2.5 %collective-permute-done.8.refs_2_ = bf16[32,3584]{1,0:T(8,128)(2,1)S(1)} collective-permute-done((bf16[32,3584]{1,0:T(8,128)(2,1)S(1)}, bf16[32,3584]{1,0:T(8,128)(2,1)S(1)}, u32[]{:S(2)}, u32[]{:S(2)}) %collective-permute-start.8) | collective-permute-done | bytes 229408 | tf_op jit(solution)/shard_map/ppermute | solution.py:48
  33.6 1.6 %collective-permute-start.11 = (bf16[32,3584]{1,0:T(8,128)(2,1)S(1)}, bf16[32,3584]{1,0:T(8,128)(2,1)S(1)}, u32[]{:S(2)}, u32[]{:S(2)}) collective-permute-start(bf16[32,3584]{1,0:T(8,128)(2,1)S(1)} %collective-permute-done.10.refs_3_), channel_id=1, source_target_pairs={{0,4},{4,0},{8,12},{12,8},{1,5},{5,1},{9,13},{13,9},{2,6},{6,2},{1... | collective-permute-start | bytes 688136 | tf_op jit(solution)/shard_map/ppermute | solution.py:52
  35.2 1.4 %copy-done.2 = bf16[96,8192]{1,0:T(8,128)(2,1)S(1)} copy-done((bf16[96,8192]{1,0:T(8,128)(2,1)S(1)}, bf16[96,8192]{1,0:T(8,128)(2,1)}, u32[]{:S(2)}) %copy-start.2) | copy-done | bytes 1572888
  37.4 1.1 %stage.1 = (bf16[64,8192]{1,0:T(8,128)(2,1)S(1)}, f32[64,1]{1,0:T(8,128)S(1)}, bf16[192,8192]{1,0:T(8,128)(2,1)S(1)}, f32[1,8192]{1,0:T(1,128)S(1)}) custom-call(bf16[96,8192]{1,0:T(8,128)(2,1)S(1)} %copy-done.2, bf16[96,8192]{1,0:T(8,128)(2,1)S(1)} %collective-permute-done.4.refs_1_, bf16[32,4608]{1,0:T(8,128)(2,1)S(1)} %slice.8.refs_2_, ...), custom_call_target="tpu_custom_call" | custom-call | flops 4194304 | bytes 12000000 | tf_op jit(solution)/shard_map/stage/pallas_call | solution.py:241
  38.9 4.2 %collective-permute-done.11.refs_6_ = bf16[32,3584]{1,0:T(8,128)(2,1)S(1)} collective-permute-done((bf16[32,3584]{1,0:T(8,128)(2,1)S(1)}, bf16[32,3584]{1,0:T(8,128)(2,1)S(1)}, u32[]{:S(2)}, u32[]{:S(2)}) %collective-permute-start.11) | collective-permute-done | bytes 229408 | tf_op jit(solution)/shard_map/ppermute | solution.py:52
  43.2 2.9 %stage_rest.1 = (bf16[8192,128]{1,0:T(8,128)(2,1)S(1)}, f32[128,1]{1,0:T(8,128)S(1)}, bf16[384,8192]{1,0:T(8,128)(2,1)S(1)}, f32[384,128]{1,0:T(8,128)S(1)}) custom-call(bf16[32,4608]{1,0:T(8,128)(2,1)S(1)} %collective-permute-done.3.refs_0_, bf16[32,4608]{1,0:T(8,128)(2,1)S(1)} %collective-permute-done.5.refs_1_, ...), custom_call_target="tpu_custom_call" | custom-call | flops 8388608 | bytes 12000000 | tf_op jit(solution)/shard_map/stage_rest/pallas_call | solution.py:309
  49.4 1.9 %collective-permute-done.14.refs_2_ = f32[3,384]{1,0:T(4,128)S(1)} collective-permute-done((f32[3,384]{1,0:T(4,128)S(1)}, f32[3,384]{1,0:T(4,128)S(1)}, u32[]{:S(2)}, u32[]{:S(2)}) %collective-permute-start.14) | collective-permute-done | bytes 4640 | tf_op jit(solution)/shard_map/ppermute | solution.py:20
  52.3 1.6 %collective-permute-start.16 = (bf16[32,4096]{1,0:T(8,128)(2,1)S(1)}, bf16[32,4096]{1,0:T(8,128)(2,1)S(1)}, u32[]{:S(2)}, u32[]{:S(2)}) collective-permute-start(bf16[32,4096]{1,0:T(8,128)(2,1)S(1)} %get-tuple-element.60), channel_id=1, source_target_pairs={{0,4},{4,0},{8,12},{12,8},{1,5},{5,1},{9,13},{13,9},{2,6},{6,2},{1... | collective-permute-start | bytes 786440 | tf_op jit(solution)/shard_map/ppermute | solution.py:87
  53.8 2.8 %copy-done.1 = bf16[384,8192]{1,0:T(8,128)(2,1)S(1)} copy-done((bf16[384,8192]{1,0:T(8,128)(2,1)S(1)}, bf16[384,8192]{1,0:T(8,128)(2,1)}, u32[]{:S(2)}) %copy-start.1) | copy-done | bytes 6291480
  58.5 3.0 %collective-permute-done.16 = bf16[32,4096]{1,0:T(8,128)(2,1)S(1)} collective-permute-done((bf16[32,4096]{1,0:T(8,128)(2,1)S(1)}, bf16[32,4096]{1,0:T(8,128)(2,1)S(1)}, u32[]{:S(2)}, u32[]{:S(2)}) %collective-permute-start.16) | collective-permute-done | bytes 262176 | tf_op jit(solution)/shard_map/ppermute | solution.py:87
  61.5 1.5 %collective-permute-start.24 = (bf16[32,4096]{1,0:T(8,128)(2,1)S(1)}, bf16[32,4096]{1,0:T(8,128)(2,1)S(1)}, u32[]{:S(2)}, u32[]{:S(2)}) collective-permute-start(bf16[32,4096]{1,0:T(8,128)(2,1)S(1)} %get-tuple-element.65), channel_id=1, source_target_pairs={{0,4},{4,0},{8,12},{12,8},{1,5},{5,1},{9,13},{13,9},{2,6},{6,2},{1... | collective-permute-start | bytes 786440 | tf_op jit(solution)/shard_map/ppermute | solution.py:91
  63.7 4.4 %collective-permute-start.20 = (bf16[32,4096]{1,0:T(8,128)(2,1)S(1)}, bf16[32,4096]{1,0:T(8,128)(2,1)S(1)}, u32[]{:S(2)}, u32[]{:S(2)}) collective-permute-start(bf16[32,4096]{1,0:T(8,128)(2,1)S(1)} %get-tuple-element.61), channel_id=1, source_target_pairs={{0,4},{4,0},{8,12},{12,8},{1,5},{5,1},{9,13},{13,9},{2,6},{6,2},{1... | collective-permute-start | bytes 786440 | tf_op jit(solution)/shard_map/ppermute | solution.py:91
  69.0 4.9 %collective-permute-start.23 = (bf16[32,4096]{1,0:T(8,128)(2,1)S(1)}, bf16[32,4096]{1,0:T(8,128)(2,1)S(1)}, u32[]{:S(2)}, u32[]{:S(2)}) collective-permute-start(bf16[32,4096]{1,0:T(8,128)(2,1)S(1)} %fusion.1), channel_id=1, source_target_pairs={{0,4},{4,0},{8,12},{12,8},{1,5},{5,1},{9,13},{13,9},{2,6},{6,2},{1... | collective-permute-start | bytes 786440 | tf_op jit(solution)/shard_map/ppermute | solution.py:97
  74.8 4.8 %collective-permute-start.19 = (bf16[32,4096]{1,0:T(8,128)(2,1)S(1)}, bf16[32,4096]{1,0:T(8,128)(2,1)S(1)}, u32[]{:S(2)}, u32[]{:S(2)}) collective-permute-start(bf16[32,4096]{1,0:T(8,128)(2,1)S(1)} %fusion), channel_id=1, source_target_pairs={{0,4},{4,0},{8,12},{12,8},{1,5},{5,1},{9,13},{13,9},{2,6},{6,2},{1... | collective-permute-start | bytes 786440 | tf_op jit(solution)/shard_map/ppermute | solution.py:97
  80.3 3.6 %collective-permute-done.23 = bf16[32,4096]{1,0:T(8,128)(2,1)S(1)} collective-permute-done((bf16[32,4096]{1,0:T(8,128)(2,1)S(1)}, bf16[32,4096]{1,0:T(8,128)(2,1)S(1)}, u32[]{:S(2)}, u32[]{:S(2)}) %collective-permute-start.23) | collective-permute-done | bytes 262176 | tf_op jit(solution)/shard_map/ppermute | solution.py:97
  84.9 3.9 %collective-permute-done.19 = bf16[32,4096]{1,0:T(8,128)(2,1)S(1)} collective-permute-done((bf16[32,4096]{1,0:T(8,128)(2,1)S(1)}, bf16[32,4096]{1,0:T(8,128)(2,1)S(1)}, u32[]{:S(2)}, u32[]{:S(2)}) %collective-permute-start.19) | collective-permute-done | bytes 262176 | tf_op jit(solution)/shard_map/ppermute | solution.py:97
  (56 shorter events, 17.5 us)
Async XLA Ops:
  0.6 18.6 %collective-permute-start.4 = (bf16[96,8192]{1,0:T(8,128)(2,1)}, bf16[96,8192]{1,0:T(8,128)(2,1)S(1)}, u32[]{:S(2)}, u32[]{:S(2)}) collective-permute-start(bf16[96,8192]{1,0:T(8,128)(2,1)} %refs_0_.1), channel_id=1, source_target_pairs={{0,1},{1,0},{2,3},{3,2},{4,5},{5,4},{6,7},{7,6},{8,9},{9,8},{10,11... | collective-permute-start | bytes 4718600 | tf_op jit(solution)/shard_map/ppermute | solution.py:20
  1.1 37.8 %collective-permute-start = (bf16[96,8192]{1,0:T(8,128)(2,1)}, bf16[96,8192]{1,0:T(8,128)(2,1)S(1)}, u32[]{:S(2)}, u32[]{:S(2)}) collective-permute-start(bf16[96,8192]{1,0:T(8,128)(2,1)} %refs_0_.1), channel_id=1, source_target_pairs={{0,2},{1,3},{2,0},{3,1},{4,6},{5,7},{6,4},{7,5},{8,10},{9,11},{10,... | collective-permute-start | bytes 4718600 | tf_op jit(solution)/shard_map/ppermute | solution.py:20
  4.7 9.1 %collective-permute-start.1 = (bf16[32,4608]{1,0:T(8,128)(2,1)S(1)}, bf16[32,4608]{1,0:T(8,128)(2,1)S(1)}, u32[]{:S(2)}, u32[]{:S(2)}) collective-permute-start(bf16[32,4608]{1,0:T(8,128)(2,1)S(1)} %slice.8.refs_2_), channel_id=1, source_target_pairs={{0,4},{4,0},{8,12},{12,8},{1,5},{5,1},{9,13},{13,9},{2,6},{6,2},{1... | collective-permute-start | bytes 884744 | tf_op jit(solution)/shard_map/ppermute | solution.py:41
  6.3 9.1 %collective-permute-start.2 = (bf16[32,4608]{1,0:T(8,128)(2,1)S(1)}, bf16[32,4608]{1,0:T(8,128)(2,1)S(1)}, u32[]{:S(2)}, u32[]{:S(2)}) collective-permute-start(bf16[32,4608]{1,0:T(8,128)(2,1)S(1)} %slice.8.refs_2_), channel_id=1, source_target_pairs={{4,8},{8,4},{5,9},{9,5},{6,10},{10,6},{7,11},{11,7},{20,24},{24,20... | collective-permute-start | bytes 884744 | tf_op jit(solution)/shard_map/ppermute | solution.py:41
  8.0 11.9 %collective-permute-start.7 = (bf16[32,3584]{1,0:T(8,128)(2,1)S(1)}, bf16[32,3584]{1,0:T(8,128)(2,1)S(1)}, u32[]{:S(2)}, u32[]{:S(2)}) collective-permute-start(bf16[32,3584]{1,0:T(8,128)(2,1)S(1)} %slice.9.refs_3_), channel_id=1, source_target_pairs={{4,8},{8,4},{5,9},{9,5},{6,10},{10,6},{7,11},{11,7},{20,24},{24,20... | collective-permute-start | bytes 688136 | tf_op jit(solution)/shard_map/ppermute | solution.py:41
  13.8 10.3 %collective-permute-start.9 = (bf16[32,3584]{1,0:T(8,128)(2,1)S(1)}, bf16[32,3584]{1,0:T(8,128)(2,1)S(1)}, u32[]{:S(2)}, u32[]{:S(2)}) collective-permute-start(bf16[32,3584]{1,0:T(8,128)(2,1)S(1)} %slice.9.refs_3_), channel_id=1, source_target_pairs={{0,4},{4,0},{8,12},{12,8},{1,5},{5,1},{9,13},{13,9},{2,6},{6,2},{1... | collective-permute-start | bytes 688136 | tf_op jit(solution)/shard_map/ppermute | solution.py:41
  15.4 13.3 %collective-permute-start.3 = (bf16[32,4608]{1,0:T(8,128)(2,1)S(1)}, bf16[32,4608]{1,0:T(8,128)(2,1)S(1)}, u32[]{:S(2)}, u32[]{:S(2)}) collective-permute-start(bf16[32,4608]{1,0:T(8,128)(2,1)S(1)} %collective-permute-done.2.refs_5_), channel_id=1, source_target_pairs={{0,4},{4,0},{8,12},{12,8},{1,5},{5,1},{9,13},{13,9},{2,6},{6,2},{1... | collective-permute-start | bytes 884744 | tf_op jit(solution)/shard_map/ppermute | solution.py:48
  19.2 9.5 %collective-permute-start.5 = (bf16[32,4608]{1,0:T(8,128)(2,1)S(1)}, bf16[32,4608]{1,0:T(8,128)(2,1)S(1)}, u32[]{:S(2)}, u32[]{:S(2)}) collective-permute-start(bf16[32,4608]{1,0:T(8,128)(2,1)S(1)} %collective-permute-done.1.refs_4_), channel_id=1, source_target_pairs={{4,8},{8,4},{5,9},{9,5},{6,10},{10,6},{7,11},{11,7},{20,24},{24,20... | collective-permute-start | bytes 884744 | tf_op jit(solution)/shard_map/ppermute | solution.py:50
  19.9 13.7 %collective-permute-start.8 = (bf16[32,3584]{1,0:T(8,128)(2,1)S(1)}, bf16[32,3584]{1,0:T(8,128)(2,1)S(1)}, u32[]{:S(2)}, u32[]{:S(2)}) collective-permute-start(bf16[32,3584]{1,0:T(8,128)(2,1)S(1)} %collective-permute-done.7.refs_7_), channel_id=1, source_target_pairs={{0,4},{4,0},{8,12},{12,8},{1,5},{5,1},{9,13},{13,9},{2,6},{6,2},{1... | collective-permute-start | bytes 688136 | tf_op jit(solution)/shard_map/ppermute | solution.py:48
  24.1 9.5 %collective-permute-start.10 = (bf16[32,3584]{1,0:T(8,128)(2,1)S(1)}, bf16[32,3584]{1,0:T(8,128)(2,1)S(1)}, u32[]{:S(2)}, u32[]{:S(2)}) collective-permute-start(bf16[32,3584]{1,0:T(8,128)(2,1)S(1)} %collective-permute-done.9.refs_5_), channel_id=1, source_target_pairs={{4,8},{8,4},{5,9},{9,5},{6,10},{10,6},{7,11},{11,7},{20,24},{24,20... | collective-permute-start | bytes 688136 | tf_op jit(solution)/shard_map/ppermute | solution.py:50
  28.7 14.5 %collective-permute-start.6 = (bf16[32,4608]{1,0:T(8,128)(2,1)S(1)}, bf16[32,4608]{1,0:T(8,128)(2,1)S(1)}, u32[]{:S(2)}, u32[]{:S(2)}) collective-permute-start(bf16[32,4608]{1,0:T(8,128)(2,1)S(1)} %collective-permute-done.5.refs_1_), channel_id=1, source_target_pairs={{0,4},{4,0},{8,12},{12,8},{1,5},{5,1},{9,13},{13,9},{2,6},{6,2},{1... | collective-permute-start | bytes 884744 | tf_op jit(solution)/shard_map/ppermute | solution.py:52
  33.6 9.5 %collective-permute-start.11 = (bf16[32,3584]{1,0:T(8,128)(2,1)S(1)}, bf16[32,3584]{1,0:T(8,128)(2,1)S(1)}, u32[]{:S(2)}, u32[]{:S(2)}) collective-permute-start(bf16[32,3584]{1,0:T(8,128)(2,1)S(1)} %collective-permute-done.10.refs_3_), channel_id=1, source_target_pairs={{0,4},{4,0},{8,12},{12,8},{1,5},{5,1},{9,13},{13,9},{2,6},{6,2},{1... | collective-permute-start | bytes 688136 | tf_op jit(solution)/shard_map/ppermute | solution.py:52
  43.2 3.4 %collective-permute-start.12 = (bf16[96,8192]{1,0:T(8,128)(2,1)S(1)}, bf16[96,8192]{1,0:T(8,128)(2,1)S(1)}, u32[]{:S(2)}, u32[]{:S(2)}) collective-permute-start(bf16[96,8192]{1,0:T(8,128)(2,1)S(1)} %collective-permute-done.refs_9_), channel_id=1, source_target_pairs={{0,1},{1,0},{2,3},{3,2},{4,5},{5,4},{6,7},{7,6},{8,9},{9,8},{10,11... | collective-permute-start | bytes 4718600 | tf_op jit(solution)/shard_map/ppermute | solution.py:20
  47.7 3.6 %collective-permute-start.14 = (f32[3,384]{1,0:T(4,128)S(1)}, f32[3,384]{1,0:T(4,128)S(1)}, u32[]{:S(2)}, u32[]{:S(2)}) collective-permute-start(f32[3,384]{1,0:T(4,128)S(1)} %get-tuple-element.54.refs_0_), channel_id=1, source_target_pairs={{0,2},{1,3},{2,0},{3,1},{4,6},{5,7},{6,4},{7,5},{8,10},{9,11},{10,... | collective-permute-start | bytes 13832 | tf_op jit(solution)/shard_map/ppermute | solution.py:20
  52.3 9.2 %collective-permute-start.16 = (bf16[32,4096]{1,0:T(8,128)(2,1)S(1)}, bf16[32,4096]{1,0:T(8,128)(2,1)S(1)}, u32[]{:S(2)}, u32[]{:S(2)}) collective-permute-start(bf16[32,4096]{1,0:T(8,128)(2,1)S(1)} %get-tuple-element.60), channel_id=1, source_target_pairs={{0,4},{4,0},{8,12},{12,8},{1,5},{5,1},{9,13},{13,9},{2,6},{6,2},{1... | collective-permute-start | bytes 786440 | tf_op jit(solution)/shard_map/ppermute | solution.py:87
  57.3 10.9 %collective-permute-start.17 = (bf16[32,4096]{1,0:T(8,128)(2,1)S(1)}, bf16[32,4096]{1,0:T(8,128)(2,1)S(1)}, u32[]{:S(2)}, u32[]{:S(2)}) collective-permute-start(bf16[32,4096]{1,0:T(8,128)(2,1)S(1)} %get-tuple-element.62), channel_id=1, source_target_pairs={{0,4},{4,0},{8,12},{12,8},{1,5},{5,1},{9,13},{13,9},{2,6},{6,2},{1... | collective-permute-start | bytes 786440 | tf_op jit(solution)/shard_map/ppermute | solution.py:87
  61.5 12.5 %collective-permute-start.24 = (bf16[32,4096]{1,0:T(8,128)(2,1)S(1)}, bf16[32,4096]{1,0:T(8,128)(2,1)S(1)}, u32[]{:S(2)}, u32[]{:S(2)}) collective-permute-start(bf16[32,4096]{1,0:T(8,128)(2,1)S(1)} %get-tuple-element.65), channel_id=1, source_target_pairs={{0,4},{4,0},{8,12},{12,8},{1,5},{5,1},{9,13},{13,9},{2,6},{6,2},{1... | collective-permute-start | bytes 786440 | tf_op jit(solution)/shard_map/ppermute | solution.py:91
  63.1 5.9 %collective-permute-start.22 = (bf16[32,4096]{1,0:T(8,128)(2,1)S(1)}, bf16[32,4096]{1,0:T(8,128)(2,1)S(1)}, u32[]{:S(2)}, u32[]{:S(2)}) collective-permute-start(bf16[32,4096]{1,0:T(8,128)(2,1)S(1)} %add_convert_fusion.2), channel_id=1, source_target_pairs={{4,8},{8,4},{5,9},{9,5},{6,10},{10,6},{7,11},{11,7},{20,24},{24,20... | collective-permute-start | bytes 786440 | tf_op jit(solution)/shard_map/ppermute | solution.py:94
  63.7 15.8 %collective-permute-start.20 = (bf16[32,4096]{1,0:T(8,128)(2,1)S(1)}, bf16[32,4096]{1,0:T(8,128)(2,1)S(1)}, u32[]{:S(2)}, u32[]{:S(2)}) collective-permute-start(bf16[32,4096]{1,0:T(8,128)(2,1)S(1)} %get-tuple-element.61), channel_id=1, source_target_pairs={{0,4},{4,0},{8,12},{12,8},{1,5},{5,1},{9,13},{13,9},{2,6},{6,2},{1... | collective-permute-start | bytes 786440 | tf_op jit(solution)/shard_map/ppermute | solution.py:91
  68.3 6.5 %collective-permute-start.18 = (bf16[32,4096]{1,0:T(8,128)(2,1)S(1)}, bf16[32,4096]{1,0:T(8,128)(2,1)S(1)}, u32[]{:S(2)}, u32[]{:S(2)}) collective-permute-start(bf16[32,4096]{1,0:T(8,128)(2,1)S(1)} %add_convert_fusion.5), channel_id=1, source_target_pairs={{4,8},{8,4},{5,9},{9,5},{6,10},{10,6},{7,11},{11,7},{20,24},{24,20... | collective-permute-start | bytes 786440 | tf_op jit(solution)/shard_map/ppermute | solution.py:94
  69.0 14.9 %collective-permute-start.23 = (bf16[32,4096]{1,0:T(8,128)(2,1)S(1)}, bf16[32,4096]{1,0:T(8,128)(2,1)S(1)}, u32[]{:S(2)}, u32[]{:S(2)}) collective-permute-start(bf16[32,4096]{1,0:T(8,128)(2,1)S(1)} %fusion.1), channel_id=1, source_target_pairs={{0,4},{4,0},{8,12},{12,8},{1,5},{5,1},{9,13},{13,9},{2,6},{6,2},{1... | collective-permute-start | bytes 786440 | tf_op jit(solution)/shard_map/ppermute | solution.py:97
  74.0 9.9 %collective-permute-start.25 = (bf16[32,4096]{1,0:T(8,128)(2,1)S(1)}, bf16[32,4096]{1,0:T(8,128)(2,1)S(1)}, u32[]{:S(2)}, u32[]{:S(2)}) collective-permute-start(bf16[32,4096]{1,0:T(8,128)(2,1)S(1)} %add_convert_fusion), channel_id=1, source_target_pairs={{4,8},{8,4},{5,9},{9,5},{6,10},{10,6},{7,11},{11,7},{20,24},{24,20... | collective-permute-start | bytes 786440 | tf_op jit(solution)/shard_map/ppermute | solution.py:95
  74.8 14.0 %collective-permute-start.19 = (bf16[32,4096]{1,0:T(8,128)(2,1)S(1)}, bf16[32,4096]{1,0:T(8,128)(2,1)S(1)}, u32[]{:S(2)}, u32[]{:S(2)}) collective-permute-start(bf16[32,4096]{1,0:T(8,128)(2,1)S(1)} %fusion), channel_id=1, source_target_pairs={{0,4},{4,0},{8,12},{12,8},{1,5},{5,1},{9,13},{13,9},{2,6},{6,2},{1... | collective-permute-start | bytes 786440 | tf_op jit(solution)/shard_map/ppermute | solution.py:97
  79.6 9.1 %collective-permute-start.21 = (bf16[32,4096]{1,0:T(8,128)(2,1)S(1)}, bf16[32,4096]{1,0:T(8,128)(2,1)S(1)}, u32[]{:S(2)}, u32[]{:S(2)}) collective-permute-start(bf16[32,4096]{1,0:T(8,128)(2,1)S(1)} %add_convert_fusion.3), channel_id=1, source_target_pairs={{4,8},{8,4},{5,9},{9,5},{6,10},{10,6},{7,11},{11,7},{20,24},{24,20... | collective-permute-start | bytes 786440 | tf_op jit(solution)/shard_map/ppermute | solution.py:95
  (7 other events, 18.2 us)

commit v28 on v25

--- a/solution.py
+++ b/solution.py
@@ -8,7 +8,7 @@
 from jax.sharding import PartitionSpec as P
 
 SCORE_VMEM = 20 * 1024 * 1024
-SUMS_VMEM = 12 * 1024 * 1024
+SUMS_VMEM = 9 * 1024 * 1024
 STEP = 1024
 VMEM_SPEC = pl.BlockSpec(memory_space=pltpu.VMEM)
 ANY_SPEC = pl.BlockSpec(memory_space=pl.ANY)

time: 88.9 us -> 88.9 us (level)
  no operation moved by 1% of the time
where the time goes in v28:
time: 88.9 us; the launch traced here: 88.4 us
  starting transfers between devices  51 us (57%)
  waiting for transfers between devices  20.5 us (23%)
  Pallas kernels  7.98 us (9%)
  local copies, waits for them, and re-layouts  7.48 us (8%)
    ppermute x2, starting transfers between devices, staged_gather(): far = lax.ppermute(across, 'blk', SIDES)  9.77 us
    ppermute x2, starting transfers between devices, pair_scatter(): from_side = lax.ppermute(near, axis, SIDES)  9.54 us
    ppermute x2, waiting for transfers between devices, pair_scatter(): from_side = lax.ppermute(near, axis, SIDES)  8.57 us
    ppermute x2, starting transfers between devices, staged_gather(): end = lax.ppermute(across_far, 'blk', SIDES)  7.71 us
    ppermute x2, starting transfers between devices, staged_gather(): lax.ppermute(one, 'blk', SIDES)  6.09 us
    ppermute x2, starting transfers between devices, pair_scatter(): for_far_middle = [lax.ppermute(part, axis, SIDES) for part in second]  5.31 us
    ppermute x6, starting transfers between devices, swap_bits(): lax.ppermute(block, axis, [(i, i ^ bits) for i in range(lax.axis_size(axi...  5.01 us
    unnamed x10, local copies, waits for them, and re-layouts  4.96 us
  transfers between devices with their start and end apart: 26, of which 9 were waited for; matrix products, arithmetic and copies ran while one was open for 3% of the time, Pallas kernels for 6%

profile of v28, /device:TPU:0, one launch (start us, length us, event | category | flops | bytes accessed | tf_op | source)
XLA Modules:
  0.0 88.4 jit_solution(13559878614564090312)
XLA Ops:
  1.1 2.6 %collective-permute-start = (bf16[96,8192]{1,0:T(8,128)(2,1)}, bf16[96,8192]{1,0:T(8,128)(2,1)S(1)}, u32[]{:S(2)}, u32[]{:S(2)}) collective-permute-start(bf16[96,8192]{1,0:T(8,128)(2,1)} %refs_0_.1), channel_id=1, source_target_pairs={{0,2},{1,3},{2,0},{3,1},{4,6},{5,7},{6,4},{7,5},{8,10},{9,11},{10,... | collective-permute-start | bytes 4718600 | tf_op jit(solution)/shard_map/ppermute | solution.py:20
  4.7 1.6 %collective-permute-start.1 = (bf16[32,4608]{1,0:T(8,128)(2,1)S(1)}, bf16[32,4608]{1,0:T(8,128)(2,1)S(1)}, u32[]{:S(2)}, u32[]{:S(2)}) collective-permute-start(bf16[32,4608]{1,0:T(8,128)(2,1)S(1)} %slice.8.refs_2_), channel_id=1, source_target_pairs={{0,4},{4,0},{8,12},{12,8},{1,5},{5,1},{9,13},{13,9},{2,6},{6,2},{1... | collective-permute-start | bytes 884744 | tf_op jit(solution)/shard_map/ppermute | solution.py:43
  8.0 4.4 %collective-permute-start.7 = (bf16[32,3584]{1,0:T(8,128)(2,1)S(1)}, bf16[32,3584]{1,0:T(8,128)(2,1)S(1)}, u32[]{:S(2)}, u32[]{:S(2)}) collective-permute-start(bf16[32,3584]{1,0:T(8,128)(2,1)S(1)} %slice.9.refs_3_), channel_id=1, source_target_pairs={{0,4},{4,0},{8,12},{12,8},{1,5},{5,1},{9,13},{13,9},{2,6},{6,2},{1... | collective-permute-start | bytes 688136 | tf_op jit(solution)/shard_map/ppermute | solution.py:43
  12.4 2.2 %collective-permute-done.1.refs_4_ = bf16[32,4608]{1,0:T(8,128)(2,1)S(1)} collective-permute-done((bf16[32,4608]{1,0:T(8,128)(2,1)S(1)}, bf16[32,4608]{1,0:T(8,128)(2,1)S(1)}, u32[]{:S(2)}, u32[]{:S(2)}) %collective-permute-start.1) | collective-permute-done | bytes 294944 | tf_op jit(solution)/shard_map/ppermute | solution.py:43
  15.3 4.5 %collective-permute-start.3 = (bf16[32,4608]{1,0:T(8,128)(2,1)S(1)}, bf16[32,4608]{1,0:T(8,128)(2,1)S(1)}, u32[]{:S(2)}, u32[]{:S(2)}) collective-permute-start(bf16[32,4608]{1,0:T(8,128)(2,1)S(1)} %collective-permute-done.2.refs_5_), channel_id=1, source_target_pairs={{0,4},{4,0},{8,12},{12,8},{1,5},{5,1},{9,13},{13,9},{2,6},{6,2},{1... | collective-permute-start | bytes 884744 | tf_op jit(solution)/shard_map/ppermute | solution.py:52
  20.4 5.3 %collective-permute-start.9 = (bf16[32,3584]{1,0:T(8,128)(2,1)S(1)}, bf16[32,3584]{1,0:T(8,128)(2,1)S(1)}, u32[]{:S(2)}, u32[]{:S(2)}) collective-permute-start(bf16[32,3584]{1,0:T(8,128)(2,1)S(1)} %collective-permute-done.8.refs_7_), channel_id=1, source_target_pairs={{0,4},{4,0},{8,12},{12,8},{1,5},{5,1},{9,13},{13,9},{2,6},{6,2},{1... | collective-permute-start | bytes 688136 | tf_op jit(solution)/shard_map/ppermute | solution.py:52
  26.4 1.2 %collective-permute-done.3.refs_0_ = bf16[32,4608]{1,0:T(8,128)(2,1)S(1)} collective-permute-done((bf16[32,4608]{1,0:T(8,128)(2,1)S(1)}, bf16[32,4608]{1,0:T(8,128)(2,1)S(1)}, u32[]{:S(2)}, u32[]{:S(2)}) %collective-permute-start.3) | collective-permute-done | bytes 294944 | tf_op jit(solution)/shard_map/ppermute | solution.py:52
  27.7 4.4 %collective-permute-start.6 = (bf16[32,4608]{1,0:T(8,128)(2,1)S(1)}, bf16[32,4608]{1,0:T(8,128)(2,1)S(1)}, u32[]{:S(2)}, u32[]{:S(2)}) collective-permute-start(bf16[32,4608]{1,0:T(8,128)(2,1)S(1)} %collective-permute-done.5.refs_1_), channel_id=1, source_target_pairs={{0,4},{4,0},{8,12},{12,8},{1,5},{5,1},{9,13},{13,9},{2,6},{6,2},{1... | collective-permute-start | bytes 884744 | tf_op jit(solution)/shard_map/ppermute | solution.py:56
  32.1 3.3 %collective-permute-start.11 = (bf16[32,3584]{1,0:T(8,128)(2,1)S(1)}, bf16[32,3584]{1,0:T(8,128)(2,1)S(1)}, u32[]{:S(2)}, u32[]{:S(2)}) collective-permute-start(bf16[32,3584]{1,0:T(8,128)(2,1)S(1)} %collective-permute-done.10.refs_3_), channel_id=1, source_target_pairs={{0,4},{4,0},{8,12},{12,8},{1,5},{5,1},{9,13},{13,9},{2,6},{6,2},{1... | collective-permute-start | bytes 688136 | tf_op jit(solution)/shard_map/ppermute | solution.py:56
  35.4 1.4 %copy-done.2 = bf16[96,8192]{1,0:T(8,128)(2,1)S(1)} copy-done((bf16[96,8192]{1,0:T(8,128)(2,1)S(1)}, bf16[96,8192]{1,0:T(8,128)(2,1)}, u32[]{:S(2)}) %copy-start.2) | copy-done | bytes 1572888
  37.5 1.1 %stage.1 = (bf16[64,8192]{1,0:T(8,128)(2,1)S(1)}, f32[64,1]{1,0:T(8,128)S(1)}, bf16[192,8192]{1,0:T(8,128)(2,1)S(1)}, f32[1,8192]{1,0:T(1,128)S(1)}) custom-call(bf16[96,8192]{1,0:T(8,128)(2,1)S(1)} %copy-done.2, bf16[96,8192]{1,0:T(8,128)(2,1)S(1)} %collective-permute-done.4.refs_1_, bf16[32,4608]{1,0:T(8,128)(2,1)S(1)} %slice.8.refs_2_, ...), custom_call_target="tpu_custom_call" | custom-call | flops 4194304 | bytes 12000000 | tf_op jit(solution)/shard_map/stage/pallas_call | solution.py:245
  38.9 2.8 %collective-permute-done.11.refs_6_ = bf16[32,3584]{1,0:T(8,128)(2,1)S(1)} collective-permute-done((bf16[32,3584]{1,0:T(8,128)(2,1)S(1)}, bf16[32,3584]{1,0:T(8,128)(2,1)S(1)}, u32[]{:S(2)}, u32[]{:S(2)}) %collective-permute-start.11) | collective-permute-done | bytes 229408 | tf_op jit(solution)/shard_map/ppermute | solution.py:56
  41.7 2.9 %stage_rest.1 = (bf16[8192,128]{1,0:T(8,128)(2,1)S(1)}, f32[128,1]{1,0:T(8,128)S(1)}, bf16[384,8192]{1,0:T(8,128)(2,1)S(1)}, f32[384,128]{1,0:T(8,128)S(1)}) custom-call(bf16[32,4608]{1,0:T(8,128)(2,1)S(1)} %collective-permute-done.3.refs_0_, bf16[32,4608]{1,0:T(8,128)(2,1)S(1)} %collective-permute-done.5.refs_1_, ...), custom_call_target="tpu_custom_call" | custom-call | flops 8388608 | bytes 12000000 | tf_op jit(solution)/shard_map/stage_rest/pallas_call | solution.py:313
  46.8 1.2 %collective-permute-start.15 = (f32[3,384]{1,0:T(4,128)S(1)}, f32[3,384]{1,0:T(4,128)S(1)}, u32[]{:S(2)}, u32[]{:S(2)}) collective-permute-start(f32[3,384]{1,0:T(4,128)S(1)} %get-tuple-element.58.refs_0_), channel_id=1, source_target_pairs={{0,3},{1,2},{2,1},{3,0},{4,7},{5,6},{6,5},{7,4},{8,11},{9,10},{10,... | collective-permute-start | bytes 13832 | tf_op jit(solution)/shard_map/ppermute | solution.py:20
  47.9 1.9 %collective-permute-done.14.refs_2_ = f32[3,384]{1,0:T(4,128)S(1)} collective-permute-done((f32[3,384]{1,0:T(4,128)S(1)}, f32[3,384]{1,0:T(4,128)S(1)}, u32[]{:S(2)}, u32[]{:S(2)}) %collective-permute-start.14) | collective-permute-done | bytes 4640 | tf_op jit(solution)/shard_map/ppermute | solution.py:20
  50.8 2.1 %collective-permute-start.16 = (bf16[32,4096]{1,0:T(8,128)(2,1)S(1)}, bf16[32,4096]{1,0:T(8,128)(2,1)S(1)}, u32[]{:S(2)}, u32[]{:S(2)}) collective-permute-start(bf16[32,4096]{1,0:T(8,128)(2,1)S(1)} %get-tuple-element.64), channel_id=1, source_target_pairs={{0,4},{4,0},{8,12},{12,8},{1,5},{5,1},{9,13},{13,9},{2,6},{6,2},{1... | collective-permute-start | bytes 786440 | tf_op jit(solution)/shard_map/ppermute | solution.py:91
  52.8 2.8 %copy-done.1 = bf16[384,8192]{1,0:T(8,128)(2,1)S(1)} copy-done((bf16[384,8192]{1,0:T(8,128)(2,1)S(1)}, bf16[384,8192]{1,0:T(8,128)(2,1)}, u32[]{:S(2)}) %copy-start.1) | copy-done | bytes 6291480
  57.0 2.9 %collective-permute-done.16 = bf16[32,4096]{1,0:T(8,128)(2,1)S(1)} collective-permute-done((bf16[32,4096]{1,0:T(8,128)(2,1)S(1)}, bf16[32,4096]{1,0:T(8,128)(2,1)S(1)}, u32[]{:S(2)}, u32[]{:S(2)}) %collective-permute-start.16) | collective-permute-done | bytes 262176 | tf_op jit(solution)/shard_map/ppermute | solution.py:91
  59.9 2.0 %collective-permute-start.24 = (bf16[32,4096]{1,0:T(8,128)(2,1)S(1)}, bf16[32,4096]{1,0:T(8,128)(2,1)S(1)}, u32[]{:S(2)}, u32[]{:S(2)}) collective-permute-start(bf16[32,4096]{1,0:T(8,128)(2,1)S(1)} %get-tuple-element.69), channel_id=1, source_target_pairs={{0,4},{4,0},{8,12},{12,8},{1,5},{5,1},{9,13},{13,9},{2,6},{6,2},{1... | collective-permute-start | bytes 786440 | tf_op jit(solution)/shard_map/ppermute | solution.py:95
  62.7 3.3 %collective-permute-start.20 = (bf16[32,4096]{1,0:T(8,128)(2,1)S(1)}, bf16[32,4096]{1,0:T(8,128)(2,1)S(1)}, u32[]{:S(2)}, u32[]{:S(2)}) collective-permute-start(bf16[32,4096]{1,0:T(8,128)(2,1)S(1)} %get-tuple-element.65), channel_id=1, source_target_pairs={{0,4},{4,0},{8,12},{12,8},{1,5},{5,1},{9,13},{13,9},{2,6},{6,2},{1... | collective-permute-start | bytes 786440 | tf_op jit(solution)/shard_map/ppermute | solution.py:95
  66.9 4.8 %collective-permute-start.23 = (bf16[32,4096]{1,0:T(8,128)(2,1)S(1)}, bf16[32,4096]{1,0:T(8,128)(2,1)S(1)}, u32[]{:S(2)}, u32[]{:S(2)}) collective-permute-start(bf16[32,4096]{1,0:T(8,128)(2,1)S(1)} %fusion.1), channel_id=1, source_target_pairs={{0,4},{4,0},{8,12},{12,8},{1,5},{5,1},{9,13},{13,9},{2,6},{6,2},{1... | collective-permute-start | bytes 786440 | tf_op jit(solution)/shard_map/ppermute | solution.py:101
  72.5 4.8 %collective-permute-start.19 = (bf16[32,4096]{1,0:T(8,128)(2,1)S(1)}, bf16[32,4096]{1,0:T(8,128)(2,1)S(1)}, u32[]{:S(2)}, u32[]{:S(2)}) collective-permute-start(bf16[32,4096]{1,0:T(8,128)(2,1)S(1)} %fusion), channel_id=1, source_target_pairs={{0,4},{4,0},{8,12},{12,8},{1,5},{5,1},{9,13},{13,9},{2,6},{6,2},{1... | collective-permute-start | bytes 786440 | tf_op jit(solution)/shard_map/ppermute | solution.py:101
  78.0 4.5 %collective-permute-done.23 = bf16[32,4096]{1,0:T(8,128)(2,1)S(1)} collective-permute-done((bf16[32,4096]{1,0:T(8,128)(2,1)S(1)}, bf16[32,4096]{1,0:T(8,128)(2,1)S(1)}, u32[]{:S(2)}, u32[]{:S(2)}) %collective-permute-start.23) | collective-permute-done | bytes 262176 | tf_op jit(solution)/shard_map/ppermute | solution.py:101
  83.4 4.1 %collective-permute-done.19 = bf16[32,4096]{1,0:T(8,128)(2,1)S(1)} collective-permute-done((bf16[32,4096]{1,0:T(8,128)(2,1)S(1)}, bf16[32,4096]{1,0:T(8,128)(2,1)S(1)}, u32[]{:S(2)}, u32[]{:S(2)}) %collective-permute-start.19) | collective-permute-done | bytes 262176 | tf_op jit(solution)/shard_map/ppermute | solution.py:101
  (56 shorter events, 15.5 us)
Async XLA Ops:
  0.6 19.1 %collective-permute-start.4 = (bf16[96,8192]{1,0:T(8,128)(2,1)}, bf16[96,8192]{1,0:T(8,128)(2,1)S(1)}, u32[]{:S(2)}, u32[]{:S(2)}) collective-permute-start(bf16[96,8192]{1,0:T(8,128)(2,1)} %refs_0_.1), channel_id=1, source_target_pairs={{0,1},{1,0},{2,3},{3,2},{4,5},{5,4},{6,7},{7,6},{8,9},{9,8},{10,11... | collective-permute-start | bytes 4718600 | tf_op jit(solution)/shard_map/ppermute | solution.py:20
  1.1 37.8 %collective-permute-start = (bf16[96,8192]{1,0:T(8,128)(2,1)}, bf16[96,8192]{1,0:T(8,128)(2,1)S(1)}, u32[]{:S(2)}, u32[]{:S(2)}) collective-permute-start(bf16[96,8192]{1,0:T(8,128)(2,1)} %refs_0_.1), channel_id=1, source_target_pairs={{0,2},{1,3},{2,0},{3,1},{4,6},{5,7},{6,4},{7,5},{8,10},{9,11},{10,... | collective-permute-start | bytes 4718600 | tf_op jit(solution)/shard_map/ppermute | solution.py:20
  4.7 9.9 %collective-permute-start.1 = (bf16[32,4608]{1,0:T(8,128)(2,1)S(1)}, bf16[32,4608]{1,0:T(8,128)(2,1)S(1)}, u32[]{:S(2)}, u32[]{:S(2)}) collective-permute-start(bf16[32,4608]{1,0:T(8,128)(2,1)S(1)} %slice.8.refs_2_), channel_id=1, source_target_pairs={{0,4},{4,0},{8,12},{12,8},{1,5},{5,1},{9,13},{13,9},{2,6},{6,2},{1... | collective-permute-start | bytes 884744 | tf_op jit(solution)/shard_map/ppermute | solution.py:43
  6.3 8.9 %collective-permute-start.2 = (bf16[32,4608]{1,0:T(8,128)(2,1)S(1)}, bf16[32,4608]{1,0:T(8,128)(2,1)S(1)}, u32[]{:S(2)}, u32[]{:S(2)}) collective-permute-start(bf16[32,4608]{1,0:T(8,128)(2,1)S(1)} %slice.8.refs_2_), channel_id=1, source_target_pairs={{4,8},{8,4},{5,9},{9,5},{6,10},{10,6},{7,11},{11,7},{20,24},{24,20... | collective-permute-start | bytes 884744 | tf_op jit(solution)/shard_map/ppermute | solution.py:43
  8.0 12.5 %collective-permute-start.7 = (bf16[32,3584]{1,0:T(8,128)(2,1)S(1)}, bf16[32,3584]{1,0:T(8,128)(2,1)S(1)}, u32[]{:S(2)}, u32[]{:S(2)}) collective-permute-start(bf16[32,3584]{1,0:T(8,128)(2,1)S(1)} %slice.9.refs_3_), channel_id=1, source_target_pairs={{0,4},{4,0},{8,12},{12,8},{1,5},{5,1},{9,13},{13,9},{2,6},{6,2},{1... | collective-permute-start | bytes 688136 | tf_op jit(solution)/shard_map/ppermute | solution.py:43
  14.6 5.8 %collective-permute-start.8 = (bf16[32,3584]{1,0:T(8,128)(2,1)S(1)}, bf16[32,3584]{1,0:T(8,128)(2,1)S(1)}, u32[]{:S(2)}, u32[]{:S(2)}) collective-permute-start(bf16[32,3584]{1,0:T(8,128)(2,1)S(1)} %slice.9.refs_3_), channel_id=1, source_target_pairs={{4,8},{8,4},{5,9},{9,5},{6,10},{10,6},{7,11},{11,7},{20,24},{24,20... | collective-permute-start | bytes 688136 | tf_op jit(solution)/shard_map/ppermute | solution.py:43
  15.3 12.4 %collective-permute-start.3 = (bf16[32,4608]{1,0:T(8,128)(2,1)S(1)}, bf16[32,4608]{1,0:T(8,128)(2,1)S(1)}, u32[]{:S(2)}, u32[]{:S(2)}) collective-permute-start(bf16[32,4608]{1,0:T(8,128)(2,1)S(1)} %collective-permute-done.2.refs_5_), channel_id=1, source_target_pairs={{0,4},{4,0},{8,12},{12,8},{1,5},{5,1},{9,13},{13,9},{2,6},{6,2},{1... | collective-permute-start | bytes 884744 | tf_op jit(solution)/shard_map/ppermute | solution.py:52
  19.8 7.9 %collective-permute-start.5 = (bf16[32,4608]{1,0:T(8,128)(2,1)S(1)}, bf16[32,4608]{1,0:T(8,128)(2,1)S(1)}, u32[]{:S(2)}, u32[]{:S(2)}) collective-permute-start(bf16[32,4608]{1,0:T(8,128)(2,1)S(1)} %collective-permute-done.1.refs_4_), channel_id=1, source_target_pairs={{4,8},{8,4},{5,9},{9,5},{6,10},{10,6},{7,11},{11,7},{20,24},{24,20... | collective-permute-start | bytes 884744 | tf_op jit(solution)/shard_map/ppermute | solution.py:54
  20.4 11.6 %collective-permute-start.9 = (bf16[32,3584]{1,0:T(8,128)(2,1)S(1)}, bf16[32,3584]{1,0:T(8,128)(2,1)S(1)}, u32[]{:S(2)}, u32[]{:S(2)}) collective-permute-start(bf16[32,3584]{1,0:T(8,128)(2,1)S(1)} %collective-permute-done.8.refs_7_), channel_id=1, source_target_pairs={{0,4},{4,0},{8,12},{12,8},{1,5},{5,1},{9,13},{13,9},{2,6},{6,2},{1... | collective-permute-start | bytes 688136 | tf_op jit(solution)/shard_map/ppermute | solution.py:52
  25.8 6.3 %collective-permute-start.10 = (bf16[32,3584]{1,0:T(8,128)(2,1)S(1)}, bf16[32,3584]{1,0:T(8,128)(2,1)S(1)}, u32[]{:S(2)}, u32[]{:S(2)}) collective-permute-start(bf16[32,3584]{1,0:T(8,128)(2,1)S(1)} %collective-permute-done.7.refs_5_), channel_id=1, source_target_pairs={{4,8},{8,4},{5,9},{9,5},{6,10},{10,6},{7,11},{11,7},{20,24},{24,20... | collective-permute-start | bytes 688136 | tf_op jit(solution)/shard_map/ppermute | solution.py:54
  27.7 14.0 %collective-permute-start.6 = (bf16[32,4608]{1,0:T(8,128)(2,1)S(1)}, bf16[32,4608]{1,0:T(8,128)(2,1)S(1)}, u32[]{:S(2)}, u32[]{:S(2)}) collective-permute-start(bf16[32,4608]{1,0:T(8,128)(2,1)S(1)} %collective-permute-done.5.refs_1_), channel_id=1, source_target_pairs={{0,4},{4,0},{8,12},{12,8},{1,5},{5,1},{9,13},{13,9},{2,6},{6,2},{1... | collective-permute-start | bytes 884744 | tf_op jit(solution)/shard_map/ppermute | solution.py:56
  32.1 9.6 %collective-permute-start.11 = (bf16[32,3584]{1,0:T(8,128)(2,1)S(1)}, bf16[32,3584]{1,0:T(8,128)(2,1)S(1)}, u32[]{:S(2)}, u32[]{:S(2)}) collective-permute-start(bf16[32,3584]{1,0:T(8,128)(2,1)S(1)} %collective-permute-done.10.refs_3_), channel_id=1, source_target_pairs={{0,4},{4,0},{8,12},{12,8},{1,5},{5,1},{9,13},{13,9},{2,6},{6,2},{1... | collective-permute-start | bytes 688136 | tf_op jit(solution)/shard_map/ppermute | solution.py:56
  41.7 3.4 %collective-permute-start.12 = (bf16[96,8192]{1,0:T(8,128)(2,1)S(1)}, bf16[96,8192]{1,0:T(8,128)(2,1)S(1)}, u32[]{:S(2)}, u32[]{:S(2)}) collective-permute-start(bf16[96,8192]{1,0:T(8,128)(2,1)S(1)} %collective-permute-done.refs_9_), channel_id=1, source_target_pairs={{0,1},{1,0},{2,3},{3,2},{4,5},{5,4},{6,7},{7,6},{8,9},{9,8},{10,11... | collective-permute-start | bytes 4718600 | tf_op jit(solution)/shard_map/ppermute | solution.py:20
  46.2 3.7 %collective-permute-start.14 = (f32[3,384]{1,0:T(4,128)S(1)}, f32[3,384]{1,0:T(4,128)S(1)}, u32[]{:S(2)}, u32[]{:S(2)}) collective-permute-start(f32[3,384]{1,0:T(4,128)S(1)} %get-tuple-element.58.refs_0_), channel_id=1, source_target_pairs={{0,2},{1,3},{2,0},{3,1},{4,6},{5,7},{6,4},{7,5},{8,10},{9,11},{10,... | collective-permute-start | bytes 13832 | tf_op jit(solution)/shard_map/ppermute | solution.py:20
  50.8 9.2 %collective-permute-start.16 = (bf16[32,4096]{1,0:T(8,128)(2,1)S(1)}, bf16[32,4096]{1,0:T(8,128)(2,1)S(1)}, u32[]{:S(2)}, u32[]{:S(2)}) collective-permute-start(bf16[32,4096]{1,0:T(8,128)(2,1)S(1)} %get-tuple-element.64), channel_id=1, source_target_pairs={{0,4},{4,0},{8,12},{12,8},{1,5},{5,1},{9,13},{13,9},{2,6},{6,2},{1... | collective-permute-start | bytes 786440 | tf_op jit(solution)/shard_map/ppermute | solution.py:91
  56.3 9.7 %collective-permute-start.17 = (bf16[32,4096]{1,0:T(8,128)(2,1)S(1)}, bf16[32,4096]{1,0:T(8,128)(2,1)S(1)}, u32[]{:S(2)}, u32[]{:S(2)}) collective-permute-start(bf16[32,4096]{1,0:T(8,128)(2,1)S(1)} %get-tuple-element.66), channel_id=1, source_target_pairs={{0,4},{4,0},{8,12},{12,8},{1,5},{5,1},{9,13},{13,9},{2,6},{6,2},{1... | collective-permute-start | bytes 786440 | tf_op jit(solution)/shard_map/ppermute | solution.py:91
  59.9 11.7 %collective-permute-start.24 = (bf16[32,4096]{1,0:T(8,128)(2,1)S(1)}, bf16[32,4096]{1,0:T(8,128)(2,1)S(1)}, u32[]{:S(2)}, u32[]{:S(2)}) collective-permute-start(bf16[32,4096]{1,0:T(8,128)(2,1)S(1)} %get-tuple-element.69), channel_id=1, source_target_pairs={{0,4},{4,0},{8,12},{12,8},{1,5},{5,1},{9,13},{13,9},{2,6},{6,2},{1... | collective-permute-start | bytes 786440 | tf_op jit(solution)/shard_map/ppermute | solution.py:95
  62.0 4.7 %collective-permute-start.22 = (bf16[32,4096]{1,0:T(8,128)(2,1)S(1)}, bf16[32,4096]{1,0:T(8,128)(2,1)S(1)}, u32[]{:S(2)}, u32[]{:S(2)}) collective-permute-start(bf16[32,4096]{1,0:T(8,128)(2,1)S(1)} %add_convert_fusion.2), channel_id=1, source_target_pairs={{4,8},{8,4},{5,9},{9,5},{6,10},{10,6},{7,11},{11,7},{20,24},{24,20... | collective-permute-start | bytes 786440 | tf_op jit(solution)/shard_map/ppermute | solution.py:98
  62.7 14.5 %collective-permute-start.20 = (bf16[32,4096]{1,0:T(8,128)(2,1)S(1)}, bf16[32,4096]{1,0:T(8,128)(2,1)S(1)}, u32[]{:S(2)}, u32[]{:S(2)}) collective-permute-start(bf16[32,4096]{1,0:T(8,128)(2,1)S(1)} %get-tuple-element.65), channel_id=1, source_target_pairs={{0,4},{4,0},{8,12},{12,8},{1,5},{5,1},{9,13},{13,9},{2,6},{6,2},{1... | collective-permute-start | bytes 786440 | tf_op jit(solution)/shard_map/ppermute | solution.py:95
  66.1 6.3 %collective-permute-start.18 = (bf16[32,4096]{1,0:T(8,128)(2,1)S(1)}, bf16[32,4096]{1,0:T(8,128)(2,1)S(1)}, u32[]{:S(2)}, u32[]{:S(2)}) collective-permute-start(bf16[32,4096]{1,0:T(8,128)(2,1)S(1)} %add_convert_fusion.5), channel_id=1, source_target_pairs={{4,8},{8,4},{5,9},{9,5},{6,10},{10,6},{7,11},{11,7},{20,24},{24,20... | collective-permute-start | bytes 786440 | tf_op jit(solution)/shard_map/ppermute | solution.py:98
  66.9 15.6 %collective-permute-start.23 = (bf16[32,4096]{1,0:T(8,128)(2,1)S(1)}, bf16[32,4096]{1,0:T(8,128)(2,1)S(1)}, u32[]{:S(2)}, u32[]{:S(2)}) collective-permute-start(bf16[32,4096]{1,0:T(8,128)(2,1)S(1)} %fusion.1), channel_id=1, source_target_pairs={{0,4},{4,0},{8,12},{12,8},{1,5},{5,1},{9,13},{13,9},{2,6},{6,2},{1... | collective-permute-start | bytes 786440 | tf_op jit(solution)/shard_map/ppermute | solution.py:101
  71.7 10.8 %collective-permute-start.25 = (bf16[32,4096]{1,0:T(8,128)(2,1)S(1)}, bf16[32,4096]{1,0:T(8,128)(2,1)S(1)}, u32[]{:S(2)}, u32[]{:S(2)}) collective-permute-start(bf16[32,4096]{1,0:T(8,128)(2,1)S(1)} %add_convert_fusion), channel_id=1, source_target_pairs={{4,8},{8,4},{5,9},{9,5},{6,10},{10,6},{7,11},{11,7},{20,24},{24,20... | collective-permute-start | bytes 786440 | tf_op jit(solution)/shard_map/ppermute | solution.py:99
  72.5 15.0 %collective-permute-start.19 = (bf16[32,4096]{1,0:T(8,128)(2,1)S(1)}, bf16[32,4096]{1,0:T(8,128)(2,1)S(1)}, u32[]{:S(2)}, u32[]{:S(2)}) collective-permute-start(bf16[32,4096]{1,0:T(8,128)(2,1)S(1)} %fusion), channel_id=1, source_target_pairs={{0,4},{4,0},{8,12},{12,8},{1,5},{5,1},{9,13},{13,9},{2,6},{6,2},{1... | collective-permute-start | bytes 786440 | tf_op jit(solution)/shard_map/ppermute | solution.py:101
  77.3 10.2 %collective-permute-start.21 = (bf16[32,4096]{1,0:T(8,128)(2,1)S(1)}, bf16[32,4096]{1,0:T(8,128)(2,1)S(1)}, u32[]{:S(2)}, u32[]{:S(2)}) collective-permute-start(bf16[32,4096]{1,0:T(8,128)(2,1)S(1)} %add_convert_fusion.3), channel_id=1, source_target_pairs={{4,8},{8,4},{5,9},{9,5},{6,10},{10,6},{7,11},{11,7},{20,24},{24,20... | collective-permute-start | bytes 786440 | tf_op jit(solution)/shard_map/ppermute | solution.py:99
  (7 other events, 18.2 us)
